TPU v7x, 32 devices: a whole 2x2x4 slice. The times are simulated.
32 devices in a mesh: rep: 2 (over y), node: 4 (over x, core), local: 4 (over z).
Axes of the slice: x: 2, y: 2, z: 4, core: 2. Of those that a mesh axis runs over, the one named last changes fastest.
Arguments:
- tokens: bfloat16 [256, 7168], P(('rep', 'node', 'local')), parts along dimension 0, may hold values from -6 to 6
- group_ids: int32 [256, 4], P(('rep', 'node', 'local')), parts along dimension 0, may hold values from 0 to 3, as said below
- route_weights: bfloat16 [256, 4], P(('rep', 'node', 'local')), parts along dimension 0, may hold values from 0.049804688 to 0.59765625
- gate_experts: bfloat16 [4, 7168, 2048], P('node', None, 'local'), may hold values from -0.0625 to 0.0625
- up_experts: bfloat16 [4, 7168, 2048], P('node', None, 'local'), may hold values from -0.0625 to 0.0625
- down_experts: bfloat16 [4, 2048, 7168], P('node', 'local'), may hold values from -0.125 to 0.125
- gate_shared: bfloat16 [7168, 2048], P(None, 'local'), may hold values from -0.0625 to 0.0625
- up_shared: bfloat16 [7168, 2048], P(None, 'local'), may hold values from -0.0625 to 0.0625
- down_shared: bfloat16 [2048, 7168], P('local'), may hold values from -0.125 to 0.125
Outputs:
- layer_out: bfloat16 [256, 7168], P(('rep', 'node', 'local')), parts along dimension 0
There are 2 independent parts, one for each index of `rep`. A program takes and returns all parts, laid end to end along the dimension named above; an argument that names none is the same for every part. Nothing has to cross between parts.
Inputs may be any that keep to these rules, and one draw needn't show every extreme that they name: `group_ids`: each row names 4 different groups. Of the 8 rows of one device, each group is named by exactly 8 rows.
All inputs are finite; a program needn't handle non-finite values.
Results may differ from a plain program's by a relative error of at most 0.01.
Values may be sent and summed in bfloat16 or wider, within the bound.
No kernel may reach another device: no remote copies, remote signals or barrier semaphores. Data moves between devices by JAX's collectives and lax.ppermute only.
A program may use at most 128 MiB of HBM per device.

v0:
```python
import jax
import jax.numpy as jnp
from jax import lax
from jax.sharding import PartitionSpec as P


def swiglu_rows(row_block, gate_weight, up_weight):
    gate_value = jnp.dot(row_block, gate_weight, preferred_element_type=jnp.float32)
    up_value = jnp.dot(row_block, up_weight, preferred_element_type=jnp.float32)
    return (jax.nn.silu(gate_value) * up_value).astype(jnp.bfloat16)


def per_device(
    tokens,
    group_ids,
    route_weights,
    gate_experts,
    up_experts,
    down_experts,
    gate_shared,
    up_shared,
    down_shared,
):
    row_count, model_width = tokens.shape
    top_groups = group_ids.shape[1]
    node_count = lax.axis_size("node")
    local_count = lax.axis_size("local")
    group_rows = row_count * top_groups // node_count
    slot_total = node_count * group_rows
    gate_slice = gate_experts[0]
    up_slice = up_experts[0]
    down_slice = down_experts[0]
    shared_act = swiglu_rows(
        lax.all_gather(tokens, "local", axis=0, tiled=True), gate_shared, up_shared
    )
    shared = lax.psum_scatter(
        jnp.dot(shared_act, down_shared, preferred_element_type=jnp.float32).astype(jnp.bfloat16),
        "local",
        scatter_dimension=0,
        tiled=True,
    ).astype(jnp.float32)
    group_range = jnp.arange(node_count, dtype=jnp.int32)
    chosen = jnp.any(group_ids[:, :, None] == group_range[None, None, :], axis=1).astype(jnp.int32)
    row_order = jnp.cumsum(chosen, axis=0) - chosen
    slot_table = group_range[None, :] * group_rows + row_order
    pick_slot = jnp.take_along_axis(slot_table, group_ids, axis=1)
    row_source = (
        jnp.zeros((slot_total,), jnp.int32)
        .at[pick_slot.reshape(-1)]
        .set(jnp.repeat(jnp.arange(row_count, dtype=jnp.int32), top_groups))
    )
    first_rows = tokens[row_source].reshape(node_count, group_rows, model_width)
    outgoing = jnp.broadcast_to(
        first_rows[:, None], (node_count, local_count, group_rows, model_width)
    ).reshape(node_count * local_count, group_rows, model_width)
    received = lax.all_to_all(outgoing, ("node", "local"), split_axis=0, concat_axis=0, tiled=True)
    block_shape = received.shape
    flat_rows = received.reshape(-1, block_shape[-1])
    activation = swiglu_rows(flat_rows, gate_slice, up_slice)
    answered = jnp.dot(activation, down_slice, preferred_element_type=jnp.float32).astype(
        jnp.bfloat16
    )
    returned = lax.all_to_all(
        answered.reshape(block_shape), ("node", "local"), split_axis=0, concat_axis=0, tiled=True
    )
    expert_sum = jnp.sum(
        returned.reshape(node_count, local_count, group_rows, model_width).astype(jnp.float32),
        axis=1,
    )
    picked = expert_sum.reshape(slot_total, model_width)[pick_slot]
    routed = jnp.sum(picked * route_weights.astype(jnp.float32)[:, :, None], axis=1)
    return (routed + shared).astype(jnp.bfloat16)


def solution(mesh):
    in_specs = (
        P(("rep", "node", "local"), None),
        P(("rep", "node", "local"), None),
        P(("rep", "node", "local"), None),
        P("node", None, "local"),
        P("node", None, "local"),
        P("node", "local", None),
        P(None, "local"),
        P(None, "local"),
        P("local", None),
    )
    out_specs = P(("rep", "node", "local"), None)
    return jax.shard_map(
        per_device, mesh=mesh, in_specs=in_specs, out_specs=out_specs, check_vma=False
    )
```

profile of v0, /device:TPU:0, one launch (start us, length us, event | category | flops | bytes accessed | tf_op | source)
XLA Modules:
  0.0 175.7 jit_solution(15180240975914130915)
XLA Ops:
  6.5 0.7 fusion.35
  7.2 0.8 copy.24
  8.0 0.1 copy.27
  8.1 0.1 copy.28
  8.2 0.1 copy.29
  8.3 0.1 reshape.94
  8.4 0.7 gather_fusion.2
  9.1 0.1 reshape.97
  9.2 0.1 select_n.43
  9.3 0.1 reshape.104
  9.3 0.7 scatter_custom_fusion
  10.1 2.2 %gather_fusion = bf16[32,7168]{1,0:T(8,128)(2,1)S(1)} fusion(bf16[8,7168]{1,0:T(8,128)(2,1)} %param.9, s32[1024]{0:T(1024)S(1)} %pad_clamp_fusion.1), kind=kCustom, calls=%fused_computation | custom fusion | bytes 917632 | tf_op jit(solution)/shard_map/gather | solution.py:52
  12.2 0.2 broadcast_in_dim.27
  12.4 51.0 %all_to_all.10 = bf16[16,8,7168]{2,1,0:T(8,128)(2,1)S(1)} all-to-all(bf16[16,8,7168]{2,1,0:T(8,128)(2,1)S(1)} %bitcast.46), channel_id=1, replica_groups=mesh['rep'=2,'node'=4,'local'=4] {'node','local'}, dimensions={0} | all-to-all | bytes 3670016 | tf_op jit(solution)/shard_map/all_to_all | solution.py:56
  63.4 4.2 %fusion.4 = f32[128,512]{1,0:T(8,128)S(1)} fusion(bf16[1,7168,512]{2,1,0:T(8,128)(2,1)} %param.12, bf16[16,8,7168]{2,1,0:T(8,128)(2,1)S(1)} %all_to_all.10), kind=kOutput, calls=%fused_computation.10 | convolution fusion | flops 939524096 | bytes 9437184 | tf_op jit(solution)/shard_map/dot_general | solution.py:8
  67.6 0.0 copy-start
  67.6 8.7 %fusion = bf16[16,8,7168]{2,1,0:T(8,128)(2,1)} fusion(bf16[1,512,7168]{2,1,0:T(8,128)(2,1)} %param.14, bf16[1,7168,512]{2,1,0:T(8,128)(2,1)} %param.13, bf16[16,8,7168]{2,1,0:T(8,128)(2,1)S(1)} %all_to_all.10, f32[128,512]{1,0:T(8,128)S(1)} %fusion.4), kind=kOutput, calls=%fused_computation.5 | convolution fusion | flops 1880358912 | bytes 18612224 | tf_op jit(solution)/shard_map/dot_general | solution.py:60
  76.3 3.7 %all-to-all-start.1 = ((bf16[16,8,7168]{2,1,0:T(8,128)(2,1)}), bf16[16,8,7168]{2,1,0:T(8,128)(2,1)S(1)}, u32[]{:S(2)}, u32[]{:S(2)}) async-start(bf16[16,8,7168]{2,1,0:T(8,128)(2,1)} %fusion), calls=%async_computation.1 | async-start | bytes 3670016 | tf_op jit(solution)/shard_map/all_to_all | solution.py:63
  80.0 0.0 reduce-scatter.2.cloned.1.call-start
  80.0 0.0 copy-done
  80.1 52.3 %all_gather.3 = bf16[32,7168]{1,0:T(8,128)(2,1)S(1)} all-gather(bf16[8,7168]{1,0:T(8,128)(2,1)S(1)} %copy-done), channel_id=1, replica_groups=mesh['rep'=2,'node'=4,'local'=4] {'local'}, dimensions={0}, use_global_device_ids=true | all-gather | bytes 573440 | tf_op jit(solution)/shard_map/all_gather | solution.py:34
  132.3 4.4 %fusion.41 = f32[32,512]{1,0:T(8,128)S(1)} fusion(bf16[32,7168]{1,0:T(8,128)(2,1)S(1)} %all_gather.3, bf16[7168,512]{1,0:T(8,128)(2,1)} %param.15), kind=kOutput, calls=%fused_computation.51 | convolution fusion | flops 234881024 | bytes 7864320 | tf_op jit(solution)/shard_map/dot_general | solution.py:8
  136.8 0.0 copy-start.1
  136.8 8.7 %convolution_convert_fusion.1 = bf16[32,7168]{1,0:T(8,128)(2,1)} fusion(bf16[512,7168]{1,0:T(8,128)(2,1)} %param.17, bf16[32,7168]{1,0:T(8,128)(2,1)S(1)} %all_gather.3, bf16[7168,512]{1,0:T(8,128)(2,1)} %param.16, f32[32,512]{1,0:T(8,128)S(1)} %fusion.41), kind=kOutput, calls=%fused_computation.6 | convolution fusion | flops 470089728 | bytes 15663104 | tf_op jit(solution)/shard_map/dot_general | solution.py:37
  145.5 0.0 reduce-scatter.2.cloned.1.call-update
  145.5 0.1 reshape.88
  145.6 0.0 copy-done.1
  145.6 0.1 copy.30
  145.7 0.0 all-to-all-done.1
  145.7 0.3 convert_reduce_fusion
  145.9 0.9 gather_fusion.1
  146.8 0.3 reshape.87
  147.1 0.6 multiply_reduce_fusion
  147.7 19.6 %reduce-scatter.2.cloned.1.call-done = bf16[8,7168]{1,0:T(8,128)(2,1)} async-done(((bf16[32,7168]{1,0:T(8,128)(2,1)}), bf16[8,7168]{1,0:T(8,128)(2,1)}) %reduce-scatter.2.cloned.1.call-update) | async-done | bytes 114704 | tf_op jit(solution)/shard_map/reduce_scatter | solution.py:36
  167.3 1.6 add_convert_fusion
  (12 shorter events, 0.1 us)
Async XLA Ops:
  67.6 12.5 %copy-start = (bf16[8,7168]{1,0:T(8,128)(2,1)S(1)}, bf16[8,7168]{1,0:T(8,128)(2,1)}, u32[]{:S(2)}) copy-start(bf16[8,7168]{1,0:T(8,128)(2,1)} %param.9) | copy-start | bytes 344068
  76.3 69.4 %all-to-all-start.1 = ((bf16[16,8,7168]{2,1,0:T(8,128)(2,1)}), bf16[16,8,7168]{2,1,0:T(8,128)(2,1)S(1)}, u32[]{:S(2)}, u32[]{:S(2)}) async-start(bf16[16,8,7168]{2,1,0:T(8,128)(2,1)} %fusion), calls=%async_computation.1 | async-start | bytes 3670016 | tf_op jit(solution)/shard_map/all_to_all | solution.py:63
  80.0 87.3 %reduce-scatter.2.cloned.1.call-start = ((), (), s32[]{:S(2)}) async-start(), calls=%async_computation.3 | async-start | bytes 573440 | tf_op jit(solution)/shard_map/reduce_scatter | solution.py:36
  136.8 8.8 %copy-start.1 = (bf16[8,4]{0,1:T(4,128)(2,1)S(1)}, bf16[8,4]{0,1:T(4,128)(2,1)}, u32[]{:S(2)}) copy-start(bf16[8,4]{0,1:T(4,128)(2,1)} %param.11) | copy-start | bytes 196
Sparse Core Ops, SparseCore 0:
  145.6 21.6 reduce-scatter.1
where the time goes:
time: 176 us
  blocking collectives  103 us (59%)
  matrix products  26 us (15%)
  waiting for transfers between devices  19.6 us (11%)
  between operations  13.5 us (8%)
  local copies, waits for them, and re-layouts  6.33 us (4%)
  starting transfers between devices  3.75 us (2%)
  other arithmetic  3.24 us (2%)
    all_gather x1, blocking collectives, per_device(): lax.all_gather(tokens, 'local', axis=0, tiled=True)  52.3 us
    all_to_all x1, blocking collectives, per_device(): lax.all_to_all(outgoing, ('node', 'local'), split_axis=0, concat_axis=0,...  51 us
    reduce_scatter x1, waiting for transfers between devices, per_device(): lax.psum_scatter(jnp.dot(shared_act, down_shared, preferred_element_type=...  19.6 us
    dot_general x1, matrix products, per_device(): jnp.dot(shared_act, down_shared, preferred_element_type=jnp.float32)  8.68 us
    dot_general x1, matrix products, per_device(): jnp.dot(activation, down_slice, preferred_element_type=jnp.float32)  8.67 us
    dot_general x2, matrix products, swiglu_rows(): jnp.dot(row_block, gate_weight, preferred_element_type=jnp.float32)  8.62 us
    all_to_all x1, starting transfers between devices, per_device(): lax.all_to_all(answered.reshape(block_shape), ('node', 'local'), split_ax...  3.71 us
  transfers between devices with their start and end apart: 2, of which 1 were waited for; matrix products, arithmetic and copies ran while one was open for 9% of the time, Pallas kernels for 0%

commit v1 on v0

v1 whole, which is shorter than its diff:
```python
import functools

import jax
import jax.numpy as jnp
from jax import lax
from jax.experimental import pallas as pl
from jax.experimental.pallas import tpu as pltpu
from jax.sharding import PartitionSpec as P

LANES = 128
ROW_BLOCK = 128
F32 = jnp.float32
BF16 = jnp.bfloat16


def pack_kernel(tokens_ref, groups_ref, weights_ref, out_ref):
    rows, width = tokens_ref.shape
    out_ref[:, :width] = tokens_ref[...]
    lane = lax.broadcasted_iota(jnp.int32, (rows, LANES), 1)
    dense = jnp.zeros((rows, LANES), F32)
    for k in range(groups_ref.shape[1]):
        dense += jnp.where(
            lane == groups_ref[:, k : k + 1], weights_ref[:, k : k + 1].astype(F32), 0.0
        )
    out_ref[:, width:] = dense.astype(BF16)


def pack_rows(tokens, group_ids, route_weights):
    rows, width = tokens.shape
    return pl.pallas_call(
        pack_kernel,
        out_shape=jax.ShapeDtypeStruct((rows, width + LANES), BF16),
        name="pack_rows",
    )(tokens, group_ids, route_weights)


def expert_kernel(
    share, place_ref, x_ref, gate_ref, up_ref, down_ref, sgate_ref, sup_ref, sdown_ref,
    out_ref, sgu, sd, acc, act, sems,
):
    width = down_ref.shape[1]
    hidden = gate_ref.shape[1]
    rows = x_ref.shape[0]
    step = 512
    node = place_ref[0]
    column = pl.multiple_of((node // share) * LANES, LANES)
    copies = [
        pltpu.make_async_copy(sgate_ref.at[:, pl.ds(column, LANES)], sgu.at[:, pl.ds(0, LANES)], sems.at[0]),
        pltpu.make_async_copy(sup_ref.at[:, pl.ds(column, LANES)], sgu.at[:, pl.ds(LANES, LANES)], sems.at[1]),
        pltpu.make_async_copy(sdown_ref.at[pl.ds(column, LANES), :], sd, sems.at[2]),
    ]

    @pl.when(pl.program_id(0) == 0)
    def _():
        for copy in copies:
            copy.start()

    acc[...] = jnp.zeros_like(acc)

    def first(i, carry):
        at = pl.multiple_of(i * step, step)
        x = x_ref[:, pl.ds(at, step)]
        acc[:, :hidden] += jnp.dot(x, gate_ref[pl.ds(at, step), :], preferred_element_type=F32)
        acc[:, hidden : 2 * hidden] += jnp.dot(x, up_ref[pl.ds(at, step), :], preferred_element_type=F32)
        return carry

    lax.fori_loop(0, width // step, first, 0)

    @pl.when(pl.program_id(0) == 0)
    def _():
        for copy in copies:
            copy.wait()

    def second(i, carry):
        at = pl.multiple_of(i * step, step)
        acc[:, 2 * hidden :] += jnp.dot(
            x_ref[:, pl.ds(at, step)], sgu[pl.ds(at, step), :], preferred_element_type=F32
        )
        return carry

    lax.fori_loop(0, width // step, second, 0)

    lane = lax.broadcasted_iota(jnp.int32, (rows, LANES), 1)
    weight = jnp.sum(
        jnp.where(lane == node, x_ref[:, pl.ds(width, LANES)].astype(F32), 0.0), axis=1, keepdims=True
    )
    gate = acc[:, :hidden]
    act[:, :hidden] = (gate / (1.0 + jnp.exp(-gate)) * acc[:, hidden : 2 * hidden] * weight).astype(BF16)
    gate = acc[:, 2 * hidden : 2 * hidden + LANES]
    shared = gate / (1.0 + jnp.exp(-gate)) * acc[:, 2 * hidden + LANES :]
    if share > 1:
        shared = jnp.where(lane // (LANES // share) == node % share, shared, 0.0)
    act[:, hidden:] = shared.astype(BF16)

    def third(i, carry):
        at = pl.multiple_of(i * step, step)
        total = jnp.dot(act[:, :hidden], down_ref[:, pl.ds(at, step)], preferred_element_type=F32)
        total += jnp.dot(act[:, hidden:], sd[:, pl.ds(at, step)], preferred_element_type=F32)
        out_ref[:, pl.ds(at, step)] = total.astype(BF16)
        return carry

    lax.fori_loop(0, width // step, third, 0)


def expert_rows(place, x, gate, up, down, sgate, sup, sdown, node_count):
    rows, packed = x.shape
    hidden, width = down.shape
    share = max(1, LANES * node_count // sgate.shape[1])
    block = min(rows, ROW_BLOCK)
    vmem = pl.BlockSpec(memory_space=pltpu.VMEM)
    hbm = pl.BlockSpec(memory_space=pl.ANY)
    if rows == block:
        x_spec, out_spec = vmem, vmem
    else:
        x_spec = pl.BlockSpec((block, packed), lambda i: (i, 0))
        out_spec = pl.BlockSpec((block, width), lambda i: (i, 0))
    gate, up, down = (pltpu.with_memory_space_constraint(w, pltpu.VMEM) for w in (gate, up, down))
    return pl.pallas_call(
        functools.partial(expert_kernel, share),
        grid=(rows // block,),
        in_specs=[pl.BlockSpec(memory_space=pltpu.SMEM), x_spec, vmem, vmem, vmem, hbm, hbm, hbm],
        out_specs=out_spec,
        out_shape=jax.ShapeDtypeStruct((rows, width), BF16),
        scratch_shapes=[
            pltpu.VMEM((width, 2 * LANES), BF16),
            pltpu.VMEM((LANES, width), BF16),
            pltpu.VMEM((block, 2 * hidden + 2 * LANES), F32),
            pltpu.VMEM((block, hidden + LANES), BF16),
            pltpu.SemaphoreType.DMA((3,)),
        ],
        compiler_params=pltpu.CompilerParams(vmem_limit_bytes=24 << 20),
        name="expert_rows",
    )(place, x, gate, up, down, sgate, sup, sdown)


def add_rows(*terms):
    total = terms[0].astype(F32)
    for term in terms[1:]:
        total = total + term.astype(F32)
    return total.astype(BF16)


def per_device(
    tokens,
    group_ids,
    route_weights,
    gate_experts,
    up_experts,
    down_experts,
    gate_shared,
    up_shared,
    down_shared,
):
    rows, width = tokens.shape
    node_count = lax.axis_size("node")
    local_count = lax.axis_size("local")
    x_count = node_count // 2
    small = node_count % 2 == 0 and x_count * local_count <= 8
    place = lax.axis_index("node").reshape(1)
    packed = pack_rows(tokens, group_ids, route_weights)

    def shift_local(value, k):
        return lax.ppermute(value, "local", [(i, (i + k) % local_count) for i in range(local_count)])

    def shift_x(value, k):
        return lax.ppermute(
            value, "node", [(i, (i + 2 * k) % node_count) for i in range(node_count)]
        )

    def swap_core(value):
        return lax.ppermute(value, "node", [(i, i ^ 1) for i in range(node_count)])

    if small:
        blocks = [packed] + [shift_local(packed, k) for k in range(1, local_count)]
        blocks = blocks + [shift_x(b, j) for j in range(1, x_count) for b in blocks]
        blocks = blocks + [swap_core(b) for b in blocks]
        x = jnp.concatenate(blocks, axis=0)
    else:
        x = lax.all_gather(packed, ("node", "local"), axis=0, tiled=True)
    part = expert_rows(
        place, x, gate_experts[0], up_experts[0], down_experts[0],
        gate_shared, up_shared, down_shared, node_count,
    )
    if not small:
        return lax.psum_scatter(part, ("node", "local"), scatter_dimension=0, tiled=True)
    half = x_count * local_count * rows
    part = add_rows(part[:half], swap_core(part[half:]))
    span = local_count * rows
    part = add_rows(
        part[:span],
        *(shift_x(part[j * span : (j + 1) * span], -j) for j in range(1, x_count)),
    )
    return add_rows(
        part[:rows],
        *(shift_local(part[k * rows : (k + 1) * rows], -k) for k in range(1, local_count)),
    )


def solution(mesh):
    in_specs = (
        P(("rep", "node", "local"), None),
        P(("rep", "node", "local"), None),
        P(("rep", "node", "local"), None),
        P("node", None, "local"),
        P("node", None, "local"),
        P("node", "local", None),
        P(None, "local"),
        P(None, "local"),
        P("local", None),
    )
    out_specs = P(("rep", "node", "local"), None)
    return jax.shard_map(
        per_device, mesh=mesh, in_specs=in_specs, out_specs=out_specs, check_vma=False
    )
```

time: 176 us -> 77.9 us (0.44)
  blocking collectives: 103 us -> 0 us
  matrix products: 26 us -> 0 us
  starting transfers between devices: 3.75 us -> 20.4 us
  between operations: 13.5 us -> 0.15 us
  Pallas kernels: 0 us -> 12.5 us
  waiting for transfers between devices: 19.6 us -> 30.4 us
  local copies, waits for them, and re-layouts: 6.33 us -> 13.2 us
  other arithmetic: 3.24 us -> 1.03 us
    all_gather x1 -> x0, blocking collectives: 52.3 us -> none  [per_device(): lax.all_gather(tokens, 'local', axis=0, tiled=True)]
    all_to_all x1 -> x0, blocking collectives: 51 us -> none  [per_device(): lax.all_to_all(outgoing, ('node', 'local'), split_axis=0, concat_axis=0,...]
    ppermute x0 -> x20, waiting for transfers between devices: none -> 30.4 us  [the longest x5 15.9 us: shift_x(): lax.ppermute(value, 'node', [(i, (i + 2 * k) % node_count) for i in range...]
    dot_general x4 -> x0, matrix products: 26 us -> none  [the longest x1 8.68 us: per_device(): jnp.dot(shared_act, down_shared, preferred_element_type=jnp.float32)]
    ppermute x0 -> x20, starting transfers between devices: none -> 20.4 us  [the longest x6 11.2 us: shift_local(): lax.ppermute(value, 'local', [(i, (i + k) % local_count) for i in range(l...]
    reduce_scatter x1 -> x0, waiting for transfers between devices: 19.6 us -> none  [per_device(): lax.psum_scatter(jnp.dot(shared_act, down_shared, preferred_element_type=...]
    pallas_call x0 -> x2, Pallas kernels: none -> 12.5 us  [the longest x1 10.8 us: expert_rows(): pl.pallas_call(functools.partial(expert_kernel, share), grid=(rows // blo...]
    unnamed x5 -> x23, local copies, waits for them, and re-layouts: 0.77 us -> 13.1 us
  transfers between devices with their start and end apart: 2 -> 20, of which waited for: 1 -> 10; matrix products, arithmetic and copies ran while one was open for 9% -> 1% of each run, Pallas kernels for 0% -> 0%
where the time goes in v1:
time: 77.9 us; the launch traced here: 77.6 us
  waiting for transfers between devices  30.4 us (39%)
  starting transfers between devices  20.4 us (26%)
  local copies, waits for them, and re-layouts  13.2 us (17%)
  Pallas kernels  12.5 us (16%)
  other arithmetic  1.03 us (1%)
    ppermute x5, waiting for transfers between devices, shift_x(): lax.ppermute(value, 'node', [(i, (i + 2 * k) % node_count) for i in range...  15.9 us
    unnamed x23, local copies, waits for them, and re-layouts  13.1 us
    ppermute x6, waiting for transfers between devices, shift_local(): lax.ppermute(value, 'local', [(i, (i + k) % local_count) for i in range(l...  11.5 us
    ppermute x6, starting transfers between devices, shift_local(): lax.ppermute(value, 'local', [(i, (i + k) % local_count) for i in range(l...  11.2 us
    pallas_call x1, Pallas kernels, expert_rows(): pl.pallas_call(functools.partial(expert_kernel, share), grid=(rows // blo...  10.8 us
    ppermute x5, starting transfers between devices, shift_x(): lax.ppermute(value, 'node', [(i, (i + 2 * k) % node_count) for i in range...  6.91 us
    ppermute x9, waiting for transfers between devices, swap_core(): return lax.ppermute(value, 'node', [(i, i ^ 1) for i in range(node_count)])  2.98 us
    ppermute x9, starting transfers between devices, swap_core(): return lax.ppermute(value, 'node', [(i, i ^ 1) for i in range(node_count)])  2.28 us
  transfers between devices with their start and end apart: 20, of which 10 were waited for; matrix products, arithmetic and copies ran while one was open for 1% of the time, Pallas kernels for 0%

profile of v1, /device:TPU:0, one launch (start us, length us, event | category | flops | bytes accessed | tf_op | source)
XLA Modules:
  0.0 77.6 jit_solution(9244259179428553747)
XLA Ops:
  0.0 1.3 %copy.10.groups_ref = s32[8,4]{1,0:T(8,128)} copy(s32[8,4]{0,1:T(4,128)} %param.10) | data formatting | bytes 256 | tf_op args[1]
  1.3 1.4 %copy.11.weights_ref = bf16[8,4]{1,0:T(8,128)(2,1)} copy(bf16[8,4]{0,1:T(4,128)(2,1)} %param.11) | data formatting | bytes 128 | tf_op args[2]
  2.7 1.6 %pack_rows.1 = bf16[8,7296]{1,0:T(8,128)(2,1)} custom-call(bf16[8,7168]{1,0:T(8,128)(2,1)} %tokens_ref.1, s32[8,4]{1,0:T(8,128)} %copy.10.groups_ref, bf16[8,4]{1,0:T(8,128)(2,1)} %copy.11.weights_ref), custom_call_target="tpu_custom_call" | custom-call | tf_op jit(solution)/shard_map/pack_rows/pallas_call | solution.py:30
  4.3 3.0 %collective-permute-start = (bf16[8,7296]{1,0:T(8,128)(2,1)}, bf16[8,7296]{1,0:T(8,128)(2,1)S(1)}, u32[]{:S(2)}, u32[]{:S(2)}) collective-permute-start(bf16[8,7296]{1,0:T(8,128)(2,1)} %pack_rows.1), channel_id=1, source_target_pairs={{0,1},{1,2},{2,3},{3,0},{4,5},{5,6},{6,7},{7,4},{8,9},{9,10},{10,1... | collective-permute-start | bytes 350216 | tf_op jit(solution)/shard_map/ppermute | solution.py:163
  7.4 2.6 %collective-permute-start.1 = (bf16[8,7296]{1,0:T(8,128)(2,1)}, bf16[8,7296]{1,0:T(8,128)(2,1)S(1)}, u32[]{:S(2)}, u32[]{:S(2)}) collective-permute-start(bf16[8,7296]{1,0:T(8,128)(2,1)} %pack_rows.1), channel_id=1, source_target_pairs={{0,2},{1,3},{2,0},{3,1},{4,6},{5,7},{6,4},{7,5},{8,10},{9,11},{10,... | collective-permute-start | bytes 350216 | tf_op jit(solution)/shard_map/ppermute | solution.py:163
  10.0 1.3 %collective-permute-start.2 = (bf16[8,7296]{1,0:T(8,128)(2,1)}, bf16[8,7296]{1,0:T(8,128)(2,1)S(1)}, u32[]{:S(2)}, u32[]{:S(2)}) collective-permute-start(bf16[8,7296]{1,0:T(8,128)(2,1)} %pack_rows.1), channel_id=1, source_target_pairs={{0,3},{1,0},{2,1},{3,2},{4,7},{5,4},{6,5},{7,6},{8,11},{9,8},{10,9... | collective-permute-start | bytes 350216 | tf_op jit(solution)/shard_map/ppermute | solution.py:163
  11.3 1.5 %collective-permute-start.3 = (bf16[8,7296]{1,0:T(8,128)(2,1)}, bf16[8,7296]{1,0:T(8,128)(2,1)S(1)}, u32[]{:S(2)}, u32[]{:S(2)}) collective-permute-start(bf16[8,7296]{1,0:T(8,128)(2,1)} %pack_rows.1), channel_id=1, source_target_pairs={{0,8},{4,12},{8,0},{12,4},{1,9},{5,13},{9,1},{13,5},{2,10},{6,14},... | collective-permute-start | bytes 350216 | tf_op jit(solution)/shard_map/ppermute | solution.py:166
  12.8 0.0 collective-permute-start.7
  12.8 0.9 %constant_dynamic-update-slice_fusion.15 = bf16[128,7296]{1,0:T(8,128)(2,1)S(1)} fusion(bf16[8,7296]{1,0:T(8,128)(2,1)} %pack_rows.1), kind=kLoop, calls=%fused_computation.18 | loop fusion | bytes 233472
  13.7 0.0 collective-permute-done
  13.7 1.7 %collective-permute-start.4 = (bf16[8,7296]{1,0:T(8,128)(2,1)S(1)}, bf16[8,7296]{1,0:T(8,128)(2,1)S(1)}, u32[]{:S(2)}, u32[]{:S(2)}) collective-permute-start(bf16[8,7296]{1,0:T(8,128)(2,1)S(1)} %collective-permute-done), channel_id=1, source_target_pairs={{0,8},{4,12},{8,0},{12,4},{1,9},{5,13},{9,1},{13,5},{2,10},{6,14},... | collective-permute-start | bytes 350216 | tf_op jit(solution)/shard_map/ppermute | solution.py:166
  15.5 2.4 %collective-permute-done.1 = bf16[8,7296]{1,0:T(8,128)(2,1)S(1)} collective-permute-done((bf16[8,7296]{1,0:T(8,128)(2,1)}, bf16[8,7296]{1,0:T(8,128)(2,1)S(1)}, u32[]{:S(2)}, u32[]{:S(2)}) %collective-permute-start.1) | collective-permute-done | bytes 116768 | tf_op jit(solution)/shard_map/ppermute | solution.py:163
  17.9 1.5 %collective-permute-start.5 = (bf16[8,7296]{1,0:T(8,128)(2,1)S(1)}, bf16[8,7296]{1,0:T(8,128)(2,1)S(1)}, u32[]{:S(2)}, u32[]{:S(2)}) collective-permute-start(bf16[8,7296]{1,0:T(8,128)(2,1)S(1)} %collective-permute-done.1), channel_id=1, source_target_pairs={{0,8},{4,12},{8,0},{12,4},{1,9},{5,13},{9,1},{13,5},{2,10},{6,14},... | collective-permute-start | bytes 350216 | tf_op jit(solution)/shard_map/ppermute | solution.py:166
  19.4 0.0 collective-permute-done.2
  19.4 0.6 collective-permute-start.6
  20.0 0.0 collective-permute-done.3
  20.0 0.1 collective-permute-start.8
  20.1 0.6 collective-permute-start.9
  20.7 3.2 %collective-permute-done.5 = bf16[8,7296]{1,0:T(8,128)(2,1)S(1)} collective-permute-done((bf16[8,7296]{1,0:T(8,128)(2,1)S(1)}, bf16[8,7296]{1,0:T(8,128)(2,1)S(1)}, u32[]{:S(2)}, u32[]{:S(2)}) %collective-permute-start.5) | collective-permute-done | bytes 116768 | tf_op jit(solution)/shard_map/ppermute | solution.py:166
  24.0 0.0 collective-permute-start.10
  24.0 1.4 %collective-permute-done.6 = bf16[8,7296]{1,0:T(8,128)(2,1)S(1)} collective-permute-done((bf16[8,7296]{1,0:T(8,128)(2,1)S(1)}, bf16[8,7296]{1,0:T(8,128)(2,1)S(1)}, u32[]{:S(2)}, u32[]{:S(2)}) %collective-permute-start.6) | collective-permute-done | bytes 116768 | tf_op jit(solution)/shard_map/ppermute | solution.py:166
  25.4 0.0 collective-permute-start.11
  25.4 0.6 collective-permute-start.12
  26.0 0.1 collective-permute-start.13
  26.1 0.0 collective-permute-done.9
  26.1 0.6 collective-permute-start.14
  26.7 0.0 collective-permute-done.10
  26.8 0.2 collective-permute-done.12
  27.0 0.4 collective-permute-done.13
  27.4 0.2 collective-permute-done.14
  27.7 3.1 %copy-done = bf16[1,7168,512]{2,1,0:T(8,128)(2,1)S(1)} copy-done((bf16[1,7168,512]{2,1,0:T(8,128)(2,1)S(1)}, bf16[1,7168,512]{2,1,0:T(8,128)(2,1)}, u32[]{:S(2)}) %copy-start) | copy-done | bytes 7340056
  30.8 3.1 %copy-done.1 = bf16[1,7168,512]{2,1,0:T(8,128)(2,1)S(1)} copy-done((bf16[1,7168,512]{2,1,0:T(8,128)(2,1)S(1)}, bf16[1,7168,512]{2,1,0:T(8,128)(2,1)}, u32[]{:S(2)}) %copy-start.1) | copy-done | bytes 7340056
  33.9 3.1 %copy-done.2 = bf16[1,512,7168]{2,1,0:T(8,128)(2,1)S(1)} copy-done((bf16[1,512,7168]{2,1,0:T(8,128)(2,1)S(1)}, bf16[1,512,7168]{2,1,0:T(8,128)(2,1)}, u32[]{:S(2)}) %copy-start.2) | copy-done | bytes 7340056
  36.9 10.8 %expert_rows.1 = bf16[128,7168]{1,0:T(8,128)(2,1)S(1)} custom-call(s32[1]{0:T(128)} %bitcast.place_ref, bf16[128,7296]{1,0:T(8,128)(2,1)S(1)} %constant_dynamic-update-slice_fusion.x_ref, bf16[7168,512]{1,0:T(8,128)(2,1)S(1)} %bitcast.4, bf16[7168,512]{1,0:T(8,128)(2,1)S(1)} %bitcast.5, bf16[512,7168]{1,0:T(8,128)(2,1)S(1)} %bitcast.6, ...), custom_call_target="tpu_custom_call" | custom-call | tf_op jit(solution)/shard_map/expert_rows/pallas_call | solution.py:118
  47.8 0.1 slice.33
  47.9 0.4 collective-permute-start.15
  48.3 2.1 %collective-permute-done.15 = bf16[64,7168]{1,0:T(8,128)(2,1)S(1)} collective-permute-done((bf16[64,7168]{1,0:T(8,128)(2,1)S(1)}, bf16[64,7168]{1,0:T(8,128)(2,1)S(1)}, u32[]{:S(2)}, u32[]{:S(2)}) %collective-permute-start.15) | collective-permute-done | bytes 917536 | tf_op jit(solution)/shard_map/ppermute | solution.py:171
  50.4 0.2 add_convert_fusion
  50.6 1.6 %collective-permute-start.16 = (bf16[32,7168]{1,0:T(8,128)(2,1)S(1)}, bf16[32,7168]{1,0:T(8,128)(2,1)S(1)}, u32[]{:S(2)}, u32[]{:S(2)}) collective-permute-start(bf16[32,7168]{1,0:T(8,128)(2,1)S(1)} %slice.35), channel_id=1, source_target_pairs={{0,8},{4,12},{8,0},{12,4},{1,9},{5,13},{9,1},{13,5},{2,10},{6,14},... | collective-permute-start | bytes 1376264 | tf_op jit(solution)/shard_map/ppermute | solution.py:166
  52.3 11.2 %collective-permute-done.16 = bf16[32,7168]{1,0:T(8,128)(2,1)S(1)} collective-permute-done((bf16[32,7168]{1,0:T(8,128)(2,1)S(1)}, bf16[32,7168]{1,0:T(8,128)(2,1)S(1)}, u32[]{:S(2)}, u32[]{:S(2)}) %collective-permute-start.16) | collective-permute-done | bytes 458784 | tf_op jit(solution)/shard_map/ppermute | solution.py:166
  63.5 0.1 add_convert_fusion.1
  63.6 3.2 %collective-permute-start.17 = (bf16[8,7168]{1,0:T(8,128)(2,1)S(1)}, bf16[8,7168]{1,0:T(8,128)(2,1)S(1)}, u32[]{:S(2)}, u32[]{:S(2)}) collective-permute-start(bf16[8,7168]{1,0:T(8,128)(2,1)S(1)} %get-tuple-element.5), channel_id=1, source_target_pairs={{0,3},{1,0},{2,1},{3,2},{4,7},{5,4},{6,5},{7,6},{8,11},{9,8},{10,9... | collective-permute-start | bytes 344072 | tf_op jit(solution)/shard_map/ppermute | solution.py:163
  66.8 0.0 collective-permute-start.18
  66.8 1.1 %collective-permute-start.19 = (bf16[8,7168]{1,0:T(8,128)(2,1)S(1)}, bf16[8,7168]{1,0:T(8,128)(2,1)S(1)}, u32[]{:S(2)}, u32[]{:S(2)}) collective-permute-start(bf16[8,7168]{1,0:T(8,128)(2,1)S(1)} %get-tuple-element.6), channel_id=1, source_target_pairs={{0,1},{1,2},{2,3},{3,0},{4,5},{5,6},{6,7},{7,4},{8,9},{9,10},{10,1... | collective-permute-start | bytes 344072 | tf_op jit(solution)/shard_map/ppermute | solution.py:163
  67.9 2.5 %collective-permute-done.17 = bf16[8,7168]{1,0:T(8,128)(2,1)S(1)} collective-permute-done((bf16[8,7168]{1,0:T(8,128)(2,1)S(1)}, bf16[8,7168]{1,0:T(8,128)(2,1)S(1)}, u32[]{:S(2)}, u32[]{:S(2)}) %collective-permute-start.17) | collective-permute-done | bytes 114720 | tf_op jit(solution)/shard_map/ppermute | solution.py:163
  70.4 6.5 %collective-permute-done.18 = bf16[8,7168]{1,0:T(8,128)(2,1)S(1)} collective-permute-done((bf16[8,7168]{1,0:T(8,128)(2,1)S(1)}, bf16[8,7168]{1,0:T(8,128)(2,1)S(1)}, u32[]{:S(2)}, u32[]{:S(2)}) %collective-permute-start.18) | collective-permute-done | bytes 114720 | tf_op jit(solution)/shard_map/ppermute | solution.py:163
  76.9 0.0 collective-permute-done.19
  76.9 0.7 add_convert_fusion.2
  (24 shorter events, 0.3 us)
Async XLA Ops:
  4.3 9.4 %collective-permute-start = (bf16[8,7296]{1,0:T(8,128)(2,1)}, bf16[8,7296]{1,0:T(8,128)(2,1)S(1)}, u32[]{:S(2)}, u32[]{:S(2)}) collective-permute-start(bf16[8,7296]{1,0:T(8,128)(2,1)} %pack_rows.1), channel_id=1, source_target_pairs={{0,1},{1,2},{2,3},{3,0},{4,5},{5,6},{6,7},{7,4},{8,9},{9,10},{10,1... | collective-permute-start | bytes 350216 | tf_op jit(solution)/shard_map/ppermute | solution.py:163
  7.4 10.5 %collective-permute-start.1 = (bf16[8,7296]{1,0:T(8,128)(2,1)}, bf16[8,7296]{1,0:T(8,128)(2,1)S(1)}, u32[]{:S(2)}, u32[]{:S(2)}) collective-permute-start(bf16[8,7296]{1,0:T(8,128)(2,1)} %pack_rows.1), channel_id=1, source_target_pairs={{0,2},{1,3},{2,0},{3,1},{4,6},{5,7},{6,4},{7,5},{8,10},{9,11},{10,... | collective-permute-start | bytes 350216 | tf_op jit(solution)/shard_map/ppermute | solution.py:163
  10.0 9.5 %collective-permute-start.2 = (bf16[8,7296]{1,0:T(8,128)(2,1)}, bf16[8,7296]{1,0:T(8,128)(2,1)S(1)}, u32[]{:S(2)}, u32[]{:S(2)}) collective-permute-start(bf16[8,7296]{1,0:T(8,128)(2,1)} %pack_rows.1), channel_id=1, source_target_pairs={{0,3},{1,0},{2,1},{3,2},{4,7},{5,4},{6,5},{7,6},{8,11},{9,8},{10,9... | collective-permute-start | bytes 350216 | tf_op jit(solution)/shard_map/ppermute | solution.py:163
  11.3 8.7 %collective-permute-start.3 = (bf16[8,7296]{1,0:T(8,128)(2,1)}, bf16[8,7296]{1,0:T(8,128)(2,1)S(1)}, u32[]{:S(2)}, u32[]{:S(2)}) collective-permute-start(bf16[8,7296]{1,0:T(8,128)(2,1)} %pack_rows.1), channel_id=1, source_target_pairs={{0,8},{4,12},{8,0},{12,4},{1,9},{5,13},{9,1},{13,5},{2,10},{6,14},... | collective-permute-start | bytes 350216 | tf_op jit(solution)/shard_map/ppermute | solution.py:166
  12.8 12.6 %collective-permute-start.7 = (bf16[8,7296]{1,0:T(8,128)(2,1)}, bf16[8,7296]{1,0:T(8,128)(2,1)S(1)}, u32[]{:S(2)}, u32[]{:S(2)}) collective-permute-start(bf16[8,7296]{1,0:T(8,128)(2,1)} %pack_rows.1), channel_id=1, source_target_pairs={{0,4},{4,0},{8,12},{12,8},{1,5},{5,1},{9,13},{13,9},{2,6},{6,2},{1... | collective-permute-start | bytes 350216 | tf_op jit(solution)/shard_map/ppermute | solution.py:171
  13.7 6.4 %collective-permute-start.4 = (bf16[8,7296]{1,0:T(8,128)(2,1)S(1)}, bf16[8,7296]{1,0:T(8,128)(2,1)S(1)}, u32[]{:S(2)}, u32[]{:S(2)}) collective-permute-start(bf16[8,7296]{1,0:T(8,128)(2,1)S(1)} %collective-permute-done), channel_id=1, source_target_pairs={{0,8},{4,12},{8,0},{12,4},{1,9},{5,13},{9,1},{13,5},{2,10},{6,14},... | collective-permute-start | bytes 350216 | tf_op jit(solution)/shard_map/ppermute | solution.py:166
  17.9 6.1 %collective-permute-start.5 = (bf16[8,7296]{1,0:T(8,128)(2,1)S(1)}, bf16[8,7296]{1,0:T(8,128)(2,1)S(1)}, u32[]{:S(2)}, u32[]{:S(2)}) collective-permute-start(bf16[8,7296]{1,0:T(8,128)(2,1)S(1)} %collective-permute-done.1), channel_id=1, source_target_pairs={{0,8},{4,12},{8,0},{12,4},{1,9},{5,13},{9,1},{13,5},{2,10},{6,14},... | collective-permute-start | bytes 350216 | tf_op jit(solution)/shard_map/ppermute | solution.py:166
  19.4 6.0 %collective-permute-start.6 = (bf16[8,7296]{1,0:T(8,128)(2,1)S(1)}, bf16[8,7296]{1,0:T(8,128)(2,1)S(1)}, u32[]{:S(2)}, u32[]{:S(2)}) collective-permute-start(bf16[8,7296]{1,0:T(8,128)(2,1)S(1)} %collective-permute-done.2), channel_id=1, source_target_pairs={{0,8},{4,12},{8,0},{12,4},{1,9},{5,13},{9,1},{13,5},{2,10},{6,14},... | collective-permute-start | bytes 350216 | tf_op jit(solution)/shard_map/ppermute | solution.py:166
  20.0 6.0 %collective-permute-start.8 = (bf16[8,7296]{1,0:T(8,128)(2,1)S(1)}, bf16[8,7296]{1,0:T(8,128)(2,1)S(1)}, u32[]{:S(2)}, u32[]{:S(2)}) collective-permute-start(bf16[8,7296]{1,0:T(8,128)(2,1)S(1)} %collective-permute-done), channel_id=1, source_target_pairs={{0,4},{4,0},{8,12},{12,8},{1,5},{5,1},{9,13},{13,9},{2,6},{6,2},{1... | collective-permute-start | bytes 350216 | tf_op jit(solution)/shard_map/ppermute | solution.py:171
  20.1 6.0 %collective-permute-start.9 = (bf16[8,7296]{1,0:T(8,128)(2,1)S(1)}, bf16[8,7296]{1,0:T(8,128)(2,1)S(1)}, u32[]{:S(2)}, u32[]{:S(2)}) collective-permute-start(bf16[8,7296]{1,0:T(8,128)(2,1)S(1)} %collective-permute-done.1), channel_id=1, source_target_pairs={{0,4},{4,0},{8,12},{12,8},{1,5},{5,1},{9,13},{13,9},{2,6},{6,2},{1... | collective-permute-start | bytes 350216 | tf_op jit(solution)/shard_map/ppermute | solution.py:171
  24.0 2.8 %collective-permute-start.10 = (bf16[8,7296]{1,0:T(8,128)(2,1)S(1)}, bf16[8,7296]{1,0:T(8,128)(2,1)S(1)}, u32[]{:S(2)}, u32[]{:S(2)}) collective-permute-start(bf16[8,7296]{1,0:T(8,128)(2,1)S(1)} %collective-permute-done.2), channel_id=1, source_target_pairs={{0,4},{4,0},{8,12},{12,8},{1,5},{5,1},{9,13},{13,9},{2,6},{6,2},{1... | collective-permute-start | bytes 350216 | tf_op jit(solution)/shard_map/ppermute | solution.py:171
  25.4 1.3 %collective-permute-start.11 = (bf16[8,7296]{1,0:T(8,128)(2,1)S(1)}, bf16[8,7296]{1,0:T(8,128)(2,1)S(1)}, u32[]{:S(2)}, u32[]{:S(2)}) collective-permute-start(bf16[8,7296]{1,0:T(8,128)(2,1)S(1)} %collective-permute-done.3), channel_id=1, source_target_pairs={{0,4},{4,0},{8,12},{12,8},{1,5},{5,1},{9,13},{13,9},{2,6},{6,2},{1... | collective-permute-start | bytes 350216 | tf_op jit(solution)/shard_map/ppermute | solution.py:171
  25.4 1.5 %collective-permute-start.12 = (bf16[8,7296]{1,0:T(8,128)(2,1)S(1)}, bf16[8,7296]{1,0:T(8,128)(2,1)S(1)}, u32[]{:S(2)}, u32[]{:S(2)}) collective-permute-start(bf16[8,7296]{1,0:T(8,128)(2,1)S(1)} %collective-permute-done.4), channel_id=1, source_target_pairs={{0,4},{4,0},{8,12},{12,8},{1,5},{5,1},{9,13},{13,9},{2,6},{6,2},{1... | collective-permute-start | bytes 350216 | tf_op jit(solution)/shard_map/ppermute | solution.py:171
  26.0 1.4 %collective-permute-start.13 = (bf16[8,7296]{1,0:T(8,128)(2,1)S(1)}, bf16[8,7296]{1,0:T(8,128)(2,1)S(1)}, u32[]{:S(2)}, u32[]{:S(2)}) collective-permute-start(bf16[8,7296]{1,0:T(8,128)(2,1)S(1)} %collective-permute-done.5), channel_id=1, source_target_pairs={{0,4},{4,0},{8,12},{12,8},{1,5},{5,1},{9,13},{13,9},{2,6},{6,2},{1... | collective-permute-start | bytes 350216 | tf_op jit(solution)/shard_map/ppermute | solution.py:171
  26.1 1.5 %collective-permute-start.14 = (bf16[8,7296]{1,0:T(8,128)(2,1)S(1)}, bf16[8,7296]{1,0:T(8,128)(2,1)S(1)}, u32[]{:S(2)}, u32[]{:S(2)}) collective-permute-start(bf16[8,7296]{1,0:T(8,128)(2,1)S(1)} %collective-permute-done.6), channel_id=1, source_target_pairs={{0,4},{4,0},{8,12},{12,8},{1,5},{5,1},{9,13},{13,9},{2,6},{6,2},{1... | collective-permute-start | bytes 350216 | tf_op jit(solution)/shard_map/ppermute | solution.py:171
  27.7 3.1 %copy-start = (bf16[1,7168,512]{2,1,0:T(8,128)(2,1)S(1)}, bf16[1,7168,512]{2,1,0:T(8,128)(2,1)}, u32[]{:S(2)}) copy-start(bf16[1,7168,512]{2,1,0:T(8,128)(2,1)} %param.12) | copy-start | bytes 22020100
  30.8 3.1 %copy-start.1 = (bf16[1,7168,512]{2,1,0:T(8,128)(2,1)S(1)}, bf16[1,7168,512]{2,1,0:T(8,128)(2,1)}, u32[]{:S(2)}) copy-start(bf16[1,7168,512]{2,1,0:T(8,128)(2,1)} %param.13) | copy-start | bytes 22020100
  33.9 3.1 %copy-start.2 = (bf16[1,512,7168]{2,1,0:T(8,128)(2,1)S(1)}, bf16[1,512,7168]{2,1,0:T(8,128)(2,1)}, u32[]{:S(2)}) copy-start(bf16[1,512,7168]{2,1,0:T(8,128)(2,1)} %param.14) | copy-start | bytes 22020100
  47.9 2.5 %collective-permute-start.15 = (bf16[64,7168]{1,0:T(8,128)(2,1)S(1)}, bf16[64,7168]{1,0:T(8,128)(2,1)S(1)}, u32[]{:S(2)}, u32[]{:S(2)}) collective-permute-start(bf16[64,7168]{1,0:T(8,128)(2,1)S(1)} %slice.33), channel_id=1, source_target_pairs={{0,4},{4,0},{8,12},{12,8},{1,5},{5,1},{9,13},{13,9},{2,6},{6,2},{1... | collective-permute-start | bytes 2752520 | tf_op jit(solution)/shard_map/ppermute | solution.py:171
  50.6 12.9 %collective-permute-start.16 = (bf16[32,7168]{1,0:T(8,128)(2,1)S(1)}, bf16[32,7168]{1,0:T(8,128)(2,1)S(1)}, u32[]{:S(2)}, u32[]{:S(2)}) collective-permute-start(bf16[32,7168]{1,0:T(8,128)(2,1)S(1)} %slice.35), channel_id=1, source_target_pairs={{0,8},{4,12},{8,0},{12,4},{1,9},{5,13},{9,1},{13,5},{2,10},{6,14},... | collective-permute-start | bytes 1376264 | tf_op jit(solution)/shard_map/ppermute | solution.py:166
  63.6 6.8 %collective-permute-start.17 = (bf16[8,7168]{1,0:T(8,128)(2,1)S(1)}, bf16[8,7168]{1,0:T(8,128)(2,1)S(1)}, u32[]{:S(2)}, u32[]{:S(2)}) collective-permute-start(bf16[8,7168]{1,0:T(8,128)(2,1)S(1)} %get-tuple-element.5), channel_id=1, source_target_pairs={{0,3},{1,0},{2,1},{3,2},{4,7},{5,4},{6,5},{7,6},{8,11},{9,8},{10,9... | collective-permute-start | bytes 344072 | tf_op jit(solution)/shard_map/ppermute | solution.py:163
  66.8 10.1 %collective-permute-start.18 = (bf16[8,7168]{1,0:T(8,128)(2,1)S(1)}, bf16[8,7168]{1,0:T(8,128)(2,1)S(1)}, u32[]{:S(2)}, u32[]{:S(2)}) collective-permute-start(bf16[8,7168]{1,0:T(8,128)(2,1)S(1)} %get-tuple-element.7), channel_id=1, source_target_pairs={{0,2},{1,3},{2,0},{3,1},{4,6},{5,7},{6,4},{7,5},{8,10},{9,11},{10,... | collective-permute-start | bytes 344072 | tf_op jit(solution)/shard_map/ppermute | solution.py:163
  66.8 10.1 %collective-permute-start.19 = (bf16[8,7168]{1,0:T(8,128)(2,1)S(1)}, bf16[8,7168]{1,0:T(8,128)(2,1)S(1)}, u32[]{:S(2)}, u32[]{:S(2)}) collective-permute-start(bf16[8,7168]{1,0:T(8,128)(2,1)S(1)} %get-tuple-element.6), channel_id=1, source_target_pairs={{0,1},{1,2},{2,3},{3,0},{4,5},{5,6},{6,7},{7,4},{8,9},{9,10},{10,1... | collective-permute-start | bytes 344072 | tf_op jit(solution)/shard_map/ppermute | solution.py:163

commit v2 on v0

v2 whole, which is shorter than its diff:
```python
import functools

import jax
import jax.numpy as jnp
from jax import lax
from jax.experimental import pallas as pl
from jax.experimental.pallas import tpu as pltpu
from jax.sharding import PartitionSpec as P

LANES = 128
ROW_BLOCK = 128
F32 = jnp.float32
BF16 = jnp.bfloat16
VMEM_SPEC = pl.BlockSpec(memory_space=pltpu.VMEM)
SMEM_SPEC = pl.BlockSpec(memory_space=pltpu.SMEM)
ANY_SPEC = pl.BlockSpec(memory_space=pl.ANY)


def pack_kernel(tokens_ref, groups_ref, weights_ref, out_ref):
    rows, width = tokens_ref.shape
    out_ref[:, :width] = tokens_ref[...]
    groups = groups_ref[...].T
    weights = weights_ref[...].astype(F32).T
    lane = lax.broadcasted_iota(jnp.int32, (rows, LANES), 1)
    dense = jnp.zeros((rows, LANES), F32)
    for k in range(groups.shape[1]):
        dense += jnp.where(lane == groups[:, k : k + 1], weights[:, k : k + 1], 0.0)
    out_ref[:, width:] = dense.astype(BF16)


def pack_rows(tokens, group_ids, route_weights):
    rows, width = tokens.shape
    return pl.pallas_call(
        pack_kernel,
        out_shape=jax.ShapeDtypeStruct((rows, width + LANES), BF16),
        name="pack_rows",
    )(tokens, group_ids.T, route_weights.T)


def in_hbm(value):
    return pltpu.with_memory_space_constraint(value, pltpu.HBM)


def run_copies(copies):
    for copy in copies:
        copy.start()
    for copy in copies:
        copy.wait()


def load_first_kernel(share, place_ref, after_ref, gate_ref, up_ref, sgate_ref, sup_ref, out_ref, sems):
    del after_ref
    width, hidden = gate_ref.shape
    column = pl.multiple_of((place_ref[0] // share) * LANES, LANES)
    parts = 4
    piece = width // parts
    copies = []
    for i in range(parts):
        at = pl.ds(i * piece, piece)
        for source, lower, size in (
            (gate_ref.at[at, :], 0, hidden),
            (up_ref.at[at, :], hidden, hidden),
            (sgate_ref.at[at, pl.ds(column, LANES)], 2 * hidden, LANES),
            (sup_ref.at[at, pl.ds(column, LANES)], 2 * hidden + LANES, LANES),
        ):
            copies.append(
                pltpu.make_async_copy(source, out_ref.at[at, pl.ds(lower, size)], sems.at[len(copies)])
            )
    run_copies(copies)


def load_first(place, after, gate, up, sgate, sup, share):
    width, hidden = gate.shape
    shape = (width, 2 * hidden + 2 * LANES)
    gate, up, sgate, sup = (in_hbm(w) for w in (gate, up, sgate, sup))
    return pl.pallas_call(
        functools.partial(load_first_kernel, share),
        in_specs=[SMEM_SPEC] + [ANY_SPEC] * 5,
        out_specs=VMEM_SPEC,
        out_shape=pltpu.VMEM(shape, BF16),
        scratch_shapes=[pltpu.SemaphoreType.DMA((16,))],
        cost_estimate=pl.CostEstimate(flops=0, bytes_accessed=4 * shape[0] * shape[1], transcendentals=0),
        compiler_params=pltpu.CompilerParams(vmem_limit_bytes=1 << 20),
        name="load_first",
    )(place, after, gate, up, sgate, sup)


def load_second_kernel(share, place_ref, after_ref, down_ref, sdown_ref, out_ref, sems):
    del after_ref
    hidden, width = down_ref.shape
    column = pl.multiple_of((place_ref[0] // share) * LANES, LANES)
    copies = []
    for i in range(0, hidden, LANES):
        copies.append(
            pltpu.make_async_copy(down_ref.at[pl.ds(i, LANES), :], out_ref.at[pl.ds(i, LANES), :], sems.at[len(copies)])
        )
    copies.append(
        pltpu.make_async_copy(sdown_ref.at[pl.ds(column, LANES), :], out_ref.at[pl.ds(hidden, LANES), :], sems.at[len(copies)])
    )
    run_copies(copies)


def load_second(place, after, down, sdown, share):
    hidden, width = down.shape
    shape = (hidden + LANES, width)
    down, sdown = in_hbm(down), in_hbm(sdown)
    return pl.pallas_call(
        functools.partial(load_second_kernel, share),
        in_specs=[SMEM_SPEC] + [ANY_SPEC] * 3,
        out_specs=VMEM_SPEC,
        out_shape=pltpu.VMEM(shape, BF16),
        scratch_shapes=[pltpu.SemaphoreType.DMA((hidden // LANES + 1,))],
        cost_estimate=pl.CostEstimate(flops=0, bytes_accessed=4 * shape[0] * shape[1], transcendentals=0),
        compiler_params=pltpu.CompilerParams(vmem_limit_bytes=1 << 20),
        name="load_second",
    )(place, after, down, sdown)


def expert_kernel(share, place_ref, x_ref, first_ref, second_ref, out_ref, act):
    total_hidden, width = second_ref.shape
    hidden = total_hidden - LANES
    rows = x_ref.shape[0]
    node = place_ref[0]
    lane = lax.broadcasted_iota(jnp.int32, (rows, LANES), 1)
    weight = jnp.sum(
        jnp.where(lane == node, x_ref[:, width:].astype(F32), 0.0), axis=1, keepdims=True
    )
    tile = 2 * LANES
    x = x_ref[:, :width]

    def silu(v):
        return v / (1.0 + jnp.exp(-v))

    for at in range(0, hidden, tile):
        gate = jnp.dot(x, first_ref[:, at : at + tile], preferred_element_type=F32)
        up = jnp.dot(x, first_ref[:, hidden + at : hidden + at + tile], preferred_element_type=F32)
        act[:, at : at + tile] = (silu(gate) * up * weight).astype(BF16)
    both = jnp.dot(x, first_ref[:, 2 * hidden :], preferred_element_type=F32)
    shared = silu(both[:, :LANES]) * both[:, LANES:]
    if share > 1:
        shared = jnp.where(lane // (LANES // share) == node % share, shared, 0.0)
    act[:, hidden:] = shared.astype(BF16)

    step = 1024

    def third(i, carry):
        at = pl.multiple_of(i * step, step)
        total = jnp.dot(act[...], second_ref[:, pl.ds(at, step)], preferred_element_type=F32)
        out_ref[:, pl.ds(at, step)] = total.astype(BF16)
        return carry

    lax.fori_loop(0, width // step, third, 0)


def expert_rows(place, x, first, second, share):
    rows, packed = x.shape
    width = second.shape[1]
    block = min(rows, ROW_BLOCK)
    if rows == block:
        x_spec, out_spec = VMEM_SPEC, VMEM_SPEC
    else:
        x_spec = pl.BlockSpec((block, packed), lambda i: (i, 0))
        out_spec = pl.BlockSpec((block, width), lambda i: (i, 0))
    return pl.pallas_call(
        functools.partial(expert_kernel, share),
        grid=(rows // block,),
        in_specs=[SMEM_SPEC, x_spec, VMEM_SPEC, VMEM_SPEC],
        out_specs=out_spec,
        out_shape=jax.ShapeDtypeStruct((rows, width), BF16),
        scratch_shapes=[pltpu.VMEM((block, second.shape[0]), BF16)],
        compiler_params=pltpu.CompilerParams(vmem_limit_bytes=20 << 20),
        name="expert_rows",
    )(place, x, first, second)


def f32_sum(*terms):
    return functools.reduce(lambda a, b: a + b, (t.astype(F32) for t in terms))


def per_device(
    tokens,
    group_ids,
    route_weights,
    gate_experts,
    up_experts,
    down_experts,
    gate_shared,
    up_shared,
    down_shared,
):
    rows, width = tokens.shape
    node_count = lax.axis_size("node")
    local_count = lax.axis_size("local")
    share = max(1, LANES * node_count // gate_shared.shape[1])
    place = lax.axis_index("node").reshape(1)
    packed = pack_rows(tokens, group_ids, route_weights)

    if node_count != 4 or local_count != 4:
        first = load_first(place, packed, gate_experts[0], up_experts[0], gate_shared, up_shared, share)
        second = load_second(place, packed, down_experts[0], down_shared, share)
        x = lax.all_gather(packed, ("node", "local"), axis=0, tiled=True)
        part = expert_rows(place, x, first, second, share)
        return lax.psum_scatter(part, ("node", "local"), scatter_dimension=0, tiled=True)

    def swap(value, axis, bit):
        return lax.ppermute(value, axis, [(i, i ^ bit) for i in range(4)])

    def swap_z2(value):
        return swap(value, "local", 2)

    def swap_z1(value):
        return swap(value, "local", 1)

    def swap_x(value):
        return swap(value, "node", 2)

    def swap_core(value):
        return swap(value, "node", 1)

    cut = width // 2
    two = 2 * rows
    got = swap_z2(packed)
    first = load_first(place, packed, gate_experts[0], up_experts[0], gate_shared, up_shared, share)
    got, first = lax.optimization_barrier((got, first))
    rows_1 = jnp.concatenate([packed, got], axis=0)
    a1, b1 = rows_1[:, :cut], rows_1[:, cut:]
    a2 = jnp.concatenate([a1, swap_z1(a1)], axis=0)
    b2 = jnp.concatenate([b1, swap_x(b1)], axis=0)
    a_got = swap_x(a2)
    b3 = swap_z1(b2)
    second = load_second(place, a2, down_experts[0], down_shared, share)
    a_got, b3, second = lax.optimization_barrier((a_got, b3, second))
    a3 = jnp.concatenate([a2, a_got], axis=0)
    b3 = jnp.concatenate([b2[:two], b3[:two], b2[two:], b3[two:]], axis=0)
    rows_3 = jnp.concatenate([a3, b3], axis=1)
    x = jnp.concatenate([rows_3, swap_core(rows_3)], axis=0)

    part = expert_rows(place, x, first, second, share)

    half = 8 * rows
    mine, other = part[:half], swap_core(part[half:])
    four = 4 * rows
    a_send = f32_sum(mine[four:, :cut], other[four:, :cut]).astype(BF16)
    b_mine, b_other = mine[:, cut:], other[:, cut:]

    def odd(value):
        return jnp.concatenate([value[two:four], value[four + two :]], axis=0)

    def even(value):
        return jnp.concatenate([value[:two], value[four : four + two]], axis=0)

    b_send = f32_sum(odd(b_mine), odd(b_other)).astype(BF16)
    a_got = swap_x(a_send)
    b_got = swap_z1(b_send)
    a_sum = f32_sum(mine[:four, :cut], other[:four, :cut], a_got)
    b_sum = f32_sum(even(b_mine), even(b_other), b_got)
    a_got = swap_z1(a_sum[two:].astype(BF16))
    b_got = swap_x(b_sum[two:].astype(BF16))
    a_sum = f32_sum(a_sum[:two], a_got)
    b_sum = f32_sum(b_sum[:two], b_got)
    total = jnp.concatenate([a_sum, b_sum], axis=1)
    got = swap_z2(total[rows:].astype(BF16))
    return f32_sum(total[:rows], got).astype(BF16)


def solution(mesh):
    in_specs = (
        P(("rep", "node", "local"), None),
        P(("rep", "node", "local"), None),
        P(("rep", "node", "local"), None),
        P("node", None, "local"),
        P("node", None, "local"),
        P("node", "local", None),
        P(None, "local"),
        P(None, "local"),
        P("local", None),
    )
    out_specs = P(("rep", "node", "local"), None)
    return jax.shard_map(
        per_device, mesh=mesh, in_specs=in_specs, out_specs=out_specs, check_vma=False
    )
```

time: 176 us -> 60.3 us (0.34)
  blocking collectives: 103 us -> 0 us
  matrix products: 26 us -> 0 us
  Pallas kernels: 0 us -> 17.1 us
  between operations: 13.5 us -> 0.15 us
  starting transfers between devices: 3.75 us -> 15.2 us
  local copies, waits for them, and re-layouts: 6.33 us -> 1.1 us
  waiting for transfers between devices: 19.6 us -> 24 us
    all_gather x1 -> x0, blocking collectives: 52.3 us -> none  [per_device(): lax.all_gather(tokens, 'local', axis=0, tiled=True)]
    all_to_all x1 -> x0, blocking collectives: 51 us -> none  [per_device(): lax.all_to_all(outgoing, ('node', 'local'), split_axis=0, concat_axis=0,...]
    dot_general x4 -> x0, matrix products: 26 us -> none  [the longest x1 8.68 us: per_device(): jnp.dot(shared_act, down_shared, preferred_element_type=jnp.float32)]
    ppermute x0 -> x12, waiting for transfers between devices: none -> 24 us  [swap(): return lax.ppermute(value, axis, [(i, i ^ bit) for i in range(4)])]
    reduce_scatter x1 -> x0, waiting for transfers between devices: 19.6 us -> none  [per_device(): lax.psum_scatter(jnp.dot(shared_act, down_shared, preferred_element_type=...]
    pallas_call x0 -> x4, Pallas kernels: none -> 17.1 us  [the longest x1 6.46 us: load_first(): pl.pallas_call(functools.partial(load_first_kernel, share), in_specs=[SME...]
    ppermute x0 -> x12, starting transfers between devices: none -> 15.2 us  [swap(): return lax.ppermute(value, axis, [(i, i ^ bit) for i in range(4)])]
    gather x8 -> x0, local copies, waits for them, and re-layouts: 4.29 us -> none  [the longest x1 2.16 us: per_device(): first_rows = tokens[row_source].reshape(node_count, group_rows, model_width)]
  transfers between devices with their start and end apart: 2 -> 12, of which waited for: 1 -> 9; matrix products, arithmetic and copies ran while one was open for 9% -> 1% of each run, Pallas kernels for 0% -> 17%
where the time goes in v2:
time: 60.3 us; the launch traced here: 60.2 us
  waiting for transfers between devices  24 us (40%)
  Pallas kernels  17.1 us (28%)
  starting transfers between devices  15.2 us (25%)
  other arithmetic  2.51 us (4%)
  local copies, waits for them, and re-layouts  1.1 us (2%)
    ppermute x12, waiting for transfers between devices, swap(): return lax.ppermute(value, axis, [(i, i ^ bit) for i in range(4)])  24 us
    ppermute x12, starting transfers between devices, swap(): return lax.ppermute(value, axis, [(i, i ^ bit) for i in range(4)])  15.2 us
    pallas_call x1, Pallas kernels, load_first(): pl.pallas_call(functools.partial(load_first_kernel, share), in_specs=[SME...  6.46 us
    pallas_call x1, Pallas kernels, expert_rows(): pl.pallas_call(functools.partial(expert_kernel, share), grid=(rows // blo...  5.22 us
    pallas_call x1, Pallas kernels, load_second(): pl.pallas_call(functools.partial(load_second_kernel, share), in_specs=[SM...  3.72 us
    pallas_call x1, Pallas kernels, pack_rows(): pl.pallas_call(pack_kernel, out_shape=jax.ShapeDtypeStruct((rows, width +...  1.73 us
    concatenate x1, other arithmetic, per_device(): x = jnp.concatenate([rows_3, swap_core(rows_3)], axis=0)  1.37 us
  transfers between devices with their start and end apart: 12, of which 9 were waited for; matrix products, arithmetic and copies ran while one was open for 1% of the time, Pallas kernels for 17%

profile of v2, /device:TPU:0, one launch (start us, length us, event | category | flops | bytes accessed | tf_op | source)
XLA Modules:
  0.0 60.2 jit_solution(16624240879088796335)
XLA Ops:
  0.0 1.7 %pack_rows.1.after_ref = bf16[8,7296]{1,0:T(8,128)(2,1)} custom-call(bf16[8,7168]{1,0:T(8,128)(2,1)} %tokens_ref.1, s32[4,8]{1,0:T(4,128)} %bitcast.9, bf16[4,8]{1,0:T(4,128)(2,1)} %bitcast.10), custom_call_target="tpu_custom_call" | custom-call | tf_op jit(solution)/shard_map/pack_rows/pallas_call | solution.py:33
  1.7 4.0 %collective-permute-start = (bf16[8,7296]{1,0:T(8,128)(2,1)}, bf16[8,7296]{1,0:T(8,128)(2,1)S(1)}, u32[]{:S(2)}, u32[]{:S(2)}) collective-permute-start(bf16[8,7296]{1,0:T(8,128)(2,1)} %pack_rows.1.after_ref), channel_id=1, source_target_pairs={{0,2},{1,3},{2,0},{3,1},{4,6},{5,7},{6,4},{7,5},{8,10},{9,11},{10,... | collective-permute-start | bytes 350216 | tf_op jit(solution)/shard_map/ppermute | solution.py:206
  5.8 0.0 copy-start
  5.8 0.9 %copy-done = bf16[8,7296]{1,0:T(8,128)(2,1)S(1)} copy-done((bf16[8,7296]{1,0:T(8,128)(2,1)S(1)}, bf16[8,7296]{1,0:T(8,128)(2,1)}, u32[]{:S(2)}) %copy-start) | copy-done | bytes 116760
  6.7 0.0 copy-start.1
  6.7 6.5 %load_first.1.first_ref = bf16[7168,1280]{1,0:T(8,128)(2,1)S(1)} custom-call(s32[1]{0:T(128)} %bitcast.place_ref, bf16[8,7296]{1,0:T(8,128)(2,1)S(1)} %copy-done, bf16[7168,512]{1,0:T(8,128)(2,1)} %bitcast.6, bf16[7168,512]{1,0:T(8,128)(2,1)} %bitcast.7, bf16[7168,512]{1,0:T(8,128)(2,1)} %sgate_ref.1, bf16[7168,512]{1,0:T(8,128)(2,1)} %sup_ref.1), custom_call_target="tpu_custom_call" | custom-call | bytes 36700160 | tf_op jit(solution)/shard_map/load_first/pallas_call | solution.py:76
  13.2 0.0 collective-permute-done
  13.2 0.0 copy-done.1
  13.2 1.6 %collective-permute-start.3 = (bf16[16,3712]{1,0:T(8,128)(2,1)S(1)}, bf16[16,3712]{1,0:T(8,128)(2,1)S(1)}, u32[]{:S(2)}, u32[]{:S(2)}) collective-permute-start(bf16[16,3712]{1,0:T(8,128)(2,1)S(1)} %pad_maximum_fusion.4), channel_id=1, source_target_pairs={{0,8},{4,12},{8,0},{12,4},{1,9},{5,13},{9,1},{13,5},{2,10},{6,14},... | collective-permute-start | bytes 356360 | tf_op jit(solution)/shard_map/ppermute | solution.py:206
  14.8 1.6 %collective-permute-start.1 = (bf16[16,3584]{1,0:T(8,128)(2,1)S(1)}, bf16[16,3584]{1,0:T(8,128)(2,1)S(1)}, u32[]{:S(2)}, u32[]{:S(2)}) collective-permute-start(bf16[16,3584]{1,0:T(8,128)(2,1)S(1)} %pad_maximum_fusion.5), channel_id=1, source_target_pairs={{0,1},{1,0},{2,3},{3,2},{4,5},{5,4},{6,7},{7,6},{8,9},{9,8},{10,11... | collective-permute-start | bytes 344072 | tf_op jit(solution)/shard_map/ppermute | solution.py:206
  16.4 1.7 %collective-permute-done.3 = bf16[16,3712]{1,0:T(8,128)(2,1)S(1)} collective-permute-done((bf16[16,3712]{1,0:T(8,128)(2,1)S(1)}, bf16[16,3712]{1,0:T(8,128)(2,1)S(1)}, u32[]{:S(2)}, u32[]{:S(2)}) %collective-permute-start.3) | collective-permute-done | bytes 118816 | tf_op jit(solution)/shard_map/ppermute | solution.py:206
  18.1 1.6 %collective-permute-start.4 = (bf16[32,3712]{1,0:T(8,128)(2,1)S(1)}, bf16[32,3712]{1,0:T(8,128)(2,1)S(1)}, u32[]{:S(2)}, u32[]{:S(2)}) collective-permute-start(bf16[32,3712]{1,0:T(8,128)(2,1)S(1)} %pad_maximum_fusion.1), channel_id=1, source_target_pairs={{0,1},{1,0},{2,3},{3,2},{4,5},{5,4},{6,7},{7,6},{8,9},{9,8},{10,11... | collective-permute-start | bytes 712712 | tf_op jit(solution)/shard_map/ppermute | solution.py:206
  19.8 0.3 collective-permute-done.1
  20.1 1.2 %collective-permute-start.2 = (bf16[32,3584]{1,0:T(8,128)(2,1)S(1)}, bf16[32,3584]{1,0:T(8,128)(2,1)S(1)}, u32[]{:S(2)}, u32[]{:S(2)}) collective-permute-start(bf16[32,3584]{1,0:T(8,128)(2,1)S(1)} %pad_maximum_fusion.3.after_ref), channel_id=1, source_target_pairs={{0,8},{4,12},{8,0},{12,4},{1,9},{5,13},{9,1},{13,5},{2,10},{6,14},... | collective-permute-start | bytes 688136 | tf_op jit(solution)/shard_map/ppermute | solution.py:206
  21.4 3.7 %load_second.1.second_ref = bf16[640,7168]{1,0:T(8,128)(2,1)S(1)} custom-call(s32[1]{0:T(128)} %bitcast.place_ref, bf16[32,3584]{1,0:T(8,128)(2,1)S(1)} %pad_maximum_fusion.3.after_ref, bf16[512,7168]{1,0:T(8,128)(2,1)} %bitcast.8, bf16[512,7168]{1,0:T(8,128)(2,1)} %sdown_ref.1), custom_call_target="tpu_custom_call" | custom-call | bytes 18350080 | tf_op jit(solution)/shard_map/load_second/pallas_call | solution.py:107
  25.1 1.1 %collective-permute-done.2 = bf16[32,3584]{1,0:T(8,128)(2,1)S(1)} collective-permute-done((bf16[32,3584]{1,0:T(8,128)(2,1)S(1)}, bf16[32,3584]{1,0:T(8,128)(2,1)S(1)}, u32[]{:S(2)}, u32[]{:S(2)}) %collective-permute-start.2) | collective-permute-done | bytes 229408 | tf_op jit(solution)/shard_map/ppermute | solution.py:206
  26.2 0.0 collective-permute-done.4
  26.2 0.1 maximum_maximum_fusion
  26.3 0.1 collective-permute-start.5
  26.4 2.5 %collective-permute-done.5 = bf16[64,7296]{1,0:T(8,128)(2,1)S(1)} collective-permute-done((bf16[64,7296]{1,0:T(8,128)(2,1)S(1)}, bf16[64,7296]{1,0:T(8,128)(2,1)S(1)}, u32[]{:S(2)}, u32[]{:S(2)}) %collective-permute-start.5) | collective-permute-done | bytes 933920 | tf_op jit(solution)/shard_map/ppermute | solution.py:206
  28.9 1.4 %pad_maximum_fusion.x_ref = bf16[128,7296]{1,0:T(8,128)(2,1)S(1)} fusion(bf16[64,7296]{1,0:T(8,128)(2,1)S(1)} %collective-permute-done.5, bf16[16,3712]{1,0:T(8,128)(2,1)S(1)} %get-tuple-element.24, bf16[16,3712]{1,0:T(8,128)(2,1)S(1)} %collective-permute-done.3, bf16[16,3712]{1,0:T(8,128)(2,1)S(1)} %get-tuple-element.23, ...), kind=kLoop, calls=%fused_computation | loop fusion | flops 14942208 | bytes 3735552 | tf_op jit(solution)/shard_map/concatenate | solution.py:236
  30.3 5.2 %expert_rows.1 = bf16[128,7168]{1,0:T(8,128)(2,1)S(1)} custom-call(s32[1]{0:T(128)} %bitcast.place_ref, bf16[128,7296]{1,0:T(8,128)(2,1)S(1)} %pad_maximum_fusion.x_ref, bf16[7168,1280]{1,0:T(8,128)(2,1)S(1)} %load_first.1.first_ref, bf16[640,7168]{1,0:T(8,128)(2,1)S(1)} %load_second.1.second_ref), custom_call_target="tpu_custom_call" | custom-call | tf_op jit(solution)/shard_map/expert_rows/pallas_call | solution.py:164
  35.5 0.1 slice.110
  35.6 0.2 collective-permute-start.6
  35.8 2.3 %collective-permute-done.6 = bf16[64,7168]{1,0:T(8,128)(2,1)S(1)} collective-permute-done((bf16[64,7168]{1,0:T(8,128)(2,1)S(1)}, bf16[64,7168]{1,0:T(8,128)(2,1)S(1)}, u32[]{:S(2)}, u32[]{:S(2)}) %collective-permute-start.6) | collective-permute-done | bytes 917536 | tf_op jit(solution)/shard_map/ppermute | solution.py:206
  38.1 0.1 add_convert_fusion.1
  38.1 1.2 %collective-permute-start.7 = (bf16[32,3584]{1,0:T(8,128)(2,1)S(1)}, bf16[32,3584]{1,0:T(8,128)(2,1)S(1)}, u32[]{:S(2)}, u32[]{:S(2)}) collective-permute-start(bf16[32,3584]{1,0:T(8,128)(2,1)S(1)} %add_convert_fusion.1), channel_id=1, source_target_pairs={{0,8},{4,12},{8,0},{12,4},{1,9},{5,13},{9,1},{13,5},{2,10},{6,14},... | collective-permute-start | bytes 688136 | tf_op jit(solution)/shard_map/ppermute | solution.py:206
  39.4 0.1 add_convert_fusion
  39.5 0.5 collective-permute-start.9
  40.0 5.8 %collective-permute-done.7 = bf16[32,3584]{1,0:T(8,128)(2,1)S(1)} collective-permute-done((bf16[32,3584]{1,0:T(8,128)(2,1)S(1)}, bf16[32,3584]{1,0:T(8,128)(2,1)S(1)}, u32[]{:S(2)}, u32[]{:S(2)}) %collective-permute-start.7) | collective-permute-done | bytes 229408 | tf_op jit(solution)/shard_map/ppermute | solution.py:206
  45.9 0.1 convert_add_fusion.1
  46.0 1.6 %collective-permute-start.8 = (bf16[16,3584]{1,0:T(8,128)(2,1)S(1)}, bf16[16,3584]{1,0:T(8,128)(2,1)S(1)}, u32[]{:S(2)}, u32[]{:S(2)}) collective-permute-start(bf16[16,3584]{1,0:T(8,128)(2,1)S(1)} %slice.147), channel_id=1, source_target_pairs={{0,1},{1,0},{2,3},{3,2},{4,5},{5,4},{6,7},{7,6},{8,9},{9,8},{10,11... | collective-permute-start | bytes 344072 | tf_op jit(solution)/shard_map/ppermute | solution.py:206
  47.6 0.0 collective-permute-done.9
  47.6 0.1 convert_add_fusion
  47.7 0.4 collective-permute-start.10
  48.1 2.8 %collective-permute-done.8 = bf16[16,3584]{1,0:T(8,128)(2,1)S(1)} collective-permute-done((bf16[16,3584]{1,0:T(8,128)(2,1)S(1)}, bf16[16,3584]{1,0:T(8,128)(2,1)S(1)}, u32[]{:S(2)}, u32[]{:S(2)}) %collective-permute-start.8) | collective-permute-done | bytes 114720 | tf_op jit(solution)/shard_map/ppermute | solution.py:206
  50.8 1.7 %collective-permute-done.10 = bf16[16,3584]{1,0:T(8,128)(2,1)S(1)} collective-permute-done((bf16[16,3584]{1,0:T(8,128)(2,1)S(1)}, bf16[16,3584]{1,0:T(8,128)(2,1)S(1)}, u32[]{:S(2)}, u32[]{:S(2)}) %collective-permute-start.10) | collective-permute-done | bytes 114720 | tf_op jit(solution)/shard_map/ppermute | solution.py:206
  52.6 1.1 %collective-permute-start.11 = (bf16[8,7168]{1,0:T(8,128)(2,1)S(1)}, bf16[8,7168]{1,0:T(8,128)(2,1)S(1)}, u32[]{:S(2)}, u32[]{:S(2)}) collective-permute-start(bf16[8,7168]{1,0:T(8,128)(2,1)S(1)} %fusion.3), channel_id=1, source_target_pairs={{0,2},{1,3},{2,0},{3,1},{4,6},{5,7},{6,4},{7,5},{8,10},{9,11},{10,... | collective-permute-start | bytes 344072 | tf_op jit(solution)/shard_map/ppermute | solution.py:206
  53.7 5.8 %collective-permute-done.11 = bf16[8,7168]{1,0:T(8,128)(2,1)S(1)} collective-permute-done((bf16[8,7168]{1,0:T(8,128)(2,1)S(1)}, bf16[8,7168]{1,0:T(8,128)(2,1)S(1)}, u32[]{:S(2)}, u32[]{:S(2)}) %collective-permute-start.11) | collective-permute-done | bytes 114720 | tf_op jit(solution)/shard_map/ppermute | solution.py:206
  59.5 0.7 %fusion.2 = bf16[8,7168]{1,0:T(8,128)(2,1)} fusion(f32[16,3584]{1,0:T(8,128)S(1)} %slice_add_fusion.1, f32[16,3584]{1,0:T(8,128)S(1)} %slice_add_fusion, bf16[8,7168]{1,0:T(8,128)(2,1)S(1)} %collective-permute-done.11), kind=kLoop, calls=%fused_computation.11 | loop fusion | flops 229376 | bytes 688128 | tf_op jit(solution)/shard_map/convert_element_type | solution.py:263
  (12 shorter events, 0.2 us)
Async XLA Ops:
  1.7 11.4 %collective-permute-start = (bf16[8,7296]{1,0:T(8,128)(2,1)}, bf16[8,7296]{1,0:T(8,128)(2,1)S(1)}, u32[]{:S(2)}, u32[]{:S(2)}) collective-permute-start(bf16[8,7296]{1,0:T(8,128)(2,1)} %pack_rows.1.after_ref), channel_id=1, source_target_pairs={{0,2},{1,3},{2,0},{3,1},{4,6},{5,7},{6,4},{7,5},{8,10},{9,11},{10,... | collective-permute-start | bytes 350216 | tf_op jit(solution)/shard_map/ppermute | solution.py:206
  5.8 0.9 %copy-start = (bf16[8,7296]{1,0:T(8,128)(2,1)S(1)}, bf16[8,7296]{1,0:T(8,128)(2,1)}, u32[]{:S(2)}) copy-start(bf16[8,7296]{1,0:T(8,128)(2,1)} %pack_rows.1.after_ref) | copy-start | bytes 350212
  6.7 6.5 %copy-start.1 = (bf16[8,7296]{1,0:T(8,128)(2,1)S(1)}, bf16[8,7296]{1,0:T(8,128)(2,1)}, u32[]{:S(2)}) copy-start(bf16[8,7296]{1,0:T(8,128)(2,1)} %pack_rows.1.after_ref) | copy-start | bytes 350212
  13.2 4.9 %collective-permute-start.3 = (bf16[16,3712]{1,0:T(8,128)(2,1)S(1)}, bf16[16,3712]{1,0:T(8,128)(2,1)S(1)}, u32[]{:S(2)}, u32[]{:S(2)}) collective-permute-start(bf16[16,3712]{1,0:T(8,128)(2,1)S(1)} %pad_maximum_fusion.4), channel_id=1, source_target_pairs={{0,8},{4,12},{8,0},{12,4},{1,9},{5,13},{9,1},{13,5},{2,10},{6,14},... | collective-permute-start | bytes 356360 | tf_op jit(solution)/shard_map/ppermute | solution.py:206
  14.8 5.3 %collective-permute-start.1 = (bf16[16,3584]{1,0:T(8,128)(2,1)S(1)}, bf16[16,3584]{1,0:T(8,128)(2,1)S(1)}, u32[]{:S(2)}, u32[]{:S(2)}) collective-permute-start(bf16[16,3584]{1,0:T(8,128)(2,1)S(1)} %pad_maximum_fusion.5), channel_id=1, source_target_pairs={{0,1},{1,0},{2,3},{3,2},{4,5},{5,4},{6,7},{7,6},{8,9},{9,8},{10,11... | collective-permute-start | bytes 344072 | tf_op jit(solution)/shard_map/ppermute | solution.py:206
  18.1 8.1 %collective-permute-start.4 = (bf16[32,3712]{1,0:T(8,128)(2,1)S(1)}, bf16[32,3712]{1,0:T(8,128)(2,1)S(1)}, u32[]{:S(2)}, u32[]{:S(2)}) collective-permute-start(bf16[32,3712]{1,0:T(8,128)(2,1)S(1)} %pad_maximum_fusion.1), channel_id=1, source_target_pairs={{0,1},{1,0},{2,3},{3,2},{4,5},{5,4},{6,7},{7,6},{8,9},{9,8},{10,11... | collective-permute-start | bytes 712712 | tf_op jit(solution)/shard_map/ppermute | solution.py:206
  20.1 6.1 %collective-permute-start.2 = (bf16[32,3584]{1,0:T(8,128)(2,1)S(1)}, bf16[32,3584]{1,0:T(8,128)(2,1)S(1)}, u32[]{:S(2)}, u32[]{:S(2)}) collective-permute-start(bf16[32,3584]{1,0:T(8,128)(2,1)S(1)} %pad_maximum_fusion.3.after_ref), channel_id=1, source_target_pairs={{0,8},{4,12},{8,0},{12,4},{1,9},{5,13},{9,1},{13,5},{2,10},{6,14},... | collective-permute-start | bytes 688136 | tf_op jit(solution)/shard_map/ppermute | solution.py:206
  26.3 2.6 %collective-permute-start.5 = (bf16[64,7296]{1,0:T(8,128)(2,1)S(1)}, bf16[64,7296]{1,0:T(8,128)(2,1)S(1)}, u32[]{:S(2)}, u32[]{:S(2)}) collective-permute-start(bf16[64,7296]{1,0:T(8,128)(2,1)S(1)} %maximum_maximum_fusion), channel_id=1, source_target_pairs={{0,4},{4,0},{8,12},{12,8},{1,5},{5,1},{9,13},{13,9},{2,6},{6,2},{1... | collective-permute-start | bytes 2801672 | tf_op jit(solution)/shard_map/ppermute | solution.py:206
  35.6 2.5 %collective-permute-start.6 = (bf16[64,7168]{1,0:T(8,128)(2,1)S(1)}, bf16[64,7168]{1,0:T(8,128)(2,1)S(1)}, u32[]{:S(2)}, u32[]{:S(2)}) collective-permute-start(bf16[64,7168]{1,0:T(8,128)(2,1)S(1)} %slice.110), channel_id=1, source_target_pairs={{0,4},{4,0},{8,12},{12,8},{1,5},{5,1},{9,13},{13,9},{2,6},{6,2},{1... | collective-permute-start | bytes 2752520 | tf_op jit(solution)/shard_map/ppermute | solution.py:206
  38.1 7.7 %collective-permute-start.7 = (bf16[32,3584]{1,0:T(8,128)(2,1)S(1)}, bf16[32,3584]{1,0:T(8,128)(2,1)S(1)}, u32[]{:S(2)}, u32[]{:S(2)}) collective-permute-start(bf16[32,3584]{1,0:T(8,128)(2,1)S(1)} %add_convert_fusion.1), channel_id=1, source_target_pairs={{0,8},{4,12},{8,0},{12,4},{1,9},{5,13},{9,1},{13,5},{2,10},{6,14},... | collective-permute-start | bytes 688136 | tf_op jit(solution)/shard_map/ppermute | solution.py:206
  39.5 8.1 %collective-permute-start.9 = (bf16[32,3584]{1,0:T(8,128)(2,1)S(1)}, bf16[32,3584]{1,0:T(8,128)(2,1)S(1)}, u32[]{:S(2)}, u32[]{:S(2)}) collective-permute-start(bf16[32,3584]{1,0:T(8,128)(2,1)S(1)} %add_convert_fusion), channel_id=1, source_target_pairs={{0,1},{1,0},{2,3},{3,2},{4,5},{5,4},{6,7},{7,6},{8,9},{9,8},{10,11... | collective-permute-start | bytes 688136 | tf_op jit(solution)/shard_map/ppermute | solution.py:206
  46.0 4.9 %collective-permute-start.8 = (bf16[16,3584]{1,0:T(8,128)(2,1)S(1)}, bf16[16,3584]{1,0:T(8,128)(2,1)S(1)}, u32[]{:S(2)}, u32[]{:S(2)}) collective-permute-start(bf16[16,3584]{1,0:T(8,128)(2,1)S(1)} %slice.147), channel_id=1, source_target_pairs={{0,1},{1,0},{2,3},{3,2},{4,5},{5,4},{6,7},{7,6},{8,9},{9,8},{10,11... | collective-permute-start | bytes 344072 | tf_op jit(solution)/shard_map/ppermute | solution.py:206
  47.7 4.9 %collective-permute-start.10 = (bf16[16,3584]{1,0:T(8,128)(2,1)S(1)}, bf16[16,3584]{1,0:T(8,128)(2,1)S(1)}, u32[]{:S(2)}, u32[]{:S(2)}) collective-permute-start(bf16[16,3584]{1,0:T(8,128)(2,1)S(1)} %slice.146), channel_id=1, source_target_pairs={{0,8},{4,12},{8,0},{12,4},{1,9},{5,13},{9,1},{13,5},{2,10},{6,14},... | collective-permute-start | bytes 344072 | tf_op jit(solution)/shard_map/ppermute | solution.py:206
  52.6 6.9 %collective-permute-start.11 = (bf16[8,7168]{1,0:T(8,128)(2,1)S(1)}, bf16[8,7168]{1,0:T(8,128)(2,1)S(1)}, u32[]{:S(2)}, u32[]{:S(2)}) collective-permute-start(bf16[8,7168]{1,0:T(8,128)(2,1)S(1)} %fusion.3), channel_id=1, source_target_pairs={{0,2},{1,3},{2,0},{3,1},{4,6},{5,7},{6,4},{7,5},{8,10},{9,11},{10,... | collective-permute-start | bytes 344072 | tf_op jit(solution)/shard_map/ppermute | solution.py:206

commit v3 on v0

v3 whole, which is shorter than its diff:
```python
import functools

import jax
import jax.numpy as jnp
from jax import lax
from jax.experimental import pallas as pl
from jax.experimental.pallas import tpu as pltpu
from jax.sharding import PartitionSpec as P

LANES = 128
ROW_BLOCK = 128
F32 = jnp.float32
BF16 = jnp.bfloat16
VMEM_SPEC = pl.BlockSpec(memory_space=pltpu.VMEM)
SMEM_SPEC = pl.BlockSpec(memory_space=pltpu.SMEM)
ANY_SPEC = pl.BlockSpec(memory_space=pl.ANY)


def in_hbm(value):
    return pltpu.with_memory_space_constraint(value, pltpu.HBM)


def run_copies(copies):
    for copy in copies:
        copy.start()
    for copy in copies:
        copy.wait()


def after(value, *done):
    return lax.optimization_barrier((value, *done))[0]


def shared_column(place_ref, share):
    return pl.multiple_of((place_ref[0] // share) * LANES, LANES)


def load_gate_kernel(
    share, place_ref, groups_ref, weights_ref, gate_ref, sgate_ref, sup_ref, out_ref, dense_ref, sems
):
    width, hidden = gate_ref.shape
    column = shared_column(place_ref, share)
    parts = 4
    piece = width // parts
    copies = []
    for i in range(parts):
        at = pl.ds(i * piece, piece)
        for source, lower, size in (
            (gate_ref.at[at, :], 0, hidden),
            (sgate_ref.at[at, pl.ds(column, LANES)], hidden, LANES),
            (sup_ref.at[at, pl.ds(column, LANES)], hidden + LANES, LANES),
        ):
            copies.append(
                pltpu.make_async_copy(source, out_ref.at[at, pl.ds(lower, size)], sems.at[len(copies)])
            )
    for copy in copies:
        copy.start()
    groups = groups_ref[...].T
    weights = weights_ref[...].astype(F32).T
    lane = lax.broadcasted_iota(jnp.int32, dense_ref.shape, 1)
    dense = jnp.zeros(dense_ref.shape, F32)
    for k in range(groups.shape[1]):
        dense += jnp.where(lane == groups[:, k : k + 1], weights[:, k : k + 1], 0.0)
    dense_ref[...] = dense.astype(BF16)
    for copy in copies:
        copy.wait()


def load_gate(place, group_ids, route_weights, gate, sgate, sup, share):
    width, hidden = gate.shape
    shape = (width, hidden + 2 * LANES)
    return pl.pallas_call(
        functools.partial(load_gate_kernel, share),
        in_specs=[SMEM_SPEC] + [VMEM_SPEC] * 2 + [ANY_SPEC] * 3,
        out_specs=[VMEM_SPEC] * 2,
        out_shape=[pltpu.VMEM(shape, BF16), pltpu.VMEM((group_ids.shape[0], LANES), BF16)],
        scratch_shapes=[pltpu.SemaphoreType.DMA((12,))],
        cost_estimate=pl.CostEstimate(flops=0, bytes_accessed=4 * shape[0] * shape[1], transcendentals=0),
        compiler_params=pltpu.CompilerParams(vmem_limit_bytes=1 << 20),
        name="load_gate",
    )(place, group_ids.T, route_weights.T, in_hbm(gate), in_hbm(sgate), in_hbm(sup))


def load_up_kernel(up_ref, out_ref, sems):
    width = up_ref.shape[0]
    parts = 8
    piece = width // parts
    run_copies(
        [
            pltpu.make_async_copy(
                up_ref.at[pl.ds(i * piece, piece), :], out_ref.at[pl.ds(i * piece, piece), :], sems.at[i]
            )
            for i in range(parts)
        ]
    )


def load_up(up):
    width, hidden = up.shape
    return pl.pallas_call(
        load_up_kernel,
        in_specs=[ANY_SPEC],
        out_specs=VMEM_SPEC,
        out_shape=pltpu.VMEM((width, hidden), BF16),
        scratch_shapes=[pltpu.SemaphoreType.DMA((8,))],
        cost_estimate=pl.CostEstimate(flops=0, bytes_accessed=4 * width * hidden, transcendentals=0),
        compiler_params=pltpu.CompilerParams(vmem_limit_bytes=1 << 20),
        name="load_up",
    )(in_hbm(up))


def silu(v):
    return v / (1.0 + jnp.exp(-v))


def activate(share, node, x, first_ref, up_ref, weight, act):
    width, hidden = up_ref.shape
    tile = min(2 * LANES, hidden)
    for at in range(0, hidden, tile):
        gate = jnp.dot(x, first_ref[:, at : at + tile], preferred_element_type=F32)
        up = jnp.dot(x, up_ref[:, at : at + tile], preferred_element_type=F32)
        act[:, at : at + tile] = (silu(gate) * up * weight).astype(BF16)
    both = jnp.dot(x, first_ref[:, hidden:], preferred_element_type=F32)
    shared = silu(both[:, :LANES]) * both[:, LANES:]
    if share > 1:
        lane = lax.broadcasted_iota(jnp.int32, shared.shape, 1)
        shared = jnp.where(lane // (LANES // share) == node % share, shared, 0.0)
    act[:, hidden:] = shared.astype(BF16)


def row_weight(node, dense):
    lane = lax.broadcasted_iota(jnp.int32, dense.shape, 1)
    return jnp.sum(jnp.where(lane == node, dense.astype(F32), 0.0), axis=1, keepdims=True)


def down_copies(share, place_ref, down_ref, sdown_ref, second, sems):
    hidden, width = down_ref.shape
    column = shared_column(place_ref, share)
    parts = 4
    piece = width // parts
    copies = []
    for i in range(parts):
        at = pl.ds(i * piece, piece)
        copies.append(
            pltpu.make_async_copy(down_ref.at[:, at], second.at[pl.ds(0, hidden), at], sems.at[2 * i])
        )
        copies.append(
            pltpu.make_async_copy(
                sdown_ref.at[pl.ds(column, LANES), at], second.at[pl.ds(hidden, LANES), at], sems.at[2 * i + 1]
            )
        )
    return copies


def split_kernel(
    share, place_ref, a0_ref, b0_ref, a1_ref, b1_ref, first_ref, up_ref, down_ref, sdown_ref,
    own_a_ref, own_b_ref, other_a_ref, other_b_ref, x, act, second, sems,
):
    copies = down_copies(share, place_ref, down_ref, sdown_ref, second, sems)
    for copy in copies:
        copy.start()
    width = up_ref.shape[0]
    half, cut = a0_ref.shape
    quarter = half // 4
    order = (0, 2, 1, 3)
    for c, (a_ref, b_ref) in enumerate(((a0_ref, b0_ref), (a1_ref, b1_ref))):
        x[c * half : (c + 1) * half, :cut] = a_ref[...]
        for i, j in enumerate(order):
            x[c * half + i * quarter : c * half + (i + 1) * quarter, cut:] = b_ref[
                j * quarter : (j + 1) * quarter, :
            ]
    node = place_ref[0]
    weight = row_weight(node, x[:, width:])
    activate(share, node, x[:, :width], first_ref, up_ref, weight, act)
    parts = 4
    piece = width // parts
    for i in range(parts):
        copies[2 * i].wait()
        copies[2 * i + 1].wait()
        total = jnp.dot(
            act[...], second[:, i * piece : (i + 1) * piece], preferred_element_type=F32
        ).astype(BF16)
        if i < parts // 2:
            at = slice(i * piece, (i + 1) * piece)
            own_a_ref[:, at] = total[:half]
            other_a_ref[:, at] = total[half:]
        else:
            at = slice(i * piece - cut, (i + 1) * piece - cut)
            for k, j in enumerate(order):
                to = slice(k * quarter, (k + 1) * quarter)
                own_b_ref[to, at] = total[j * quarter : (j + 1) * quarter]
                other_b_ref[to, at] = total[half + j * quarter : half + (j + 1) * quarter]


def split_rows(place, pieces, first, up, down, sdown, share):
    half, cut = pieces[0].shape
    hidden, width = down.shape
    out = jax.ShapeDtypeStruct((half, cut), BF16)
    return pl.pallas_call(
        functools.partial(split_kernel, share),
        in_specs=[SMEM_SPEC] + [VMEM_SPEC] * 6 + [ANY_SPEC] * 2,
        out_specs=[VMEM_SPEC] * 4,
        out_shape=[out] * 4,
        scratch_shapes=[
            pltpu.VMEM((2 * half, width + LANES), BF16),
            pltpu.VMEM((2 * half, hidden + LANES), BF16),
            pltpu.VMEM((hidden + LANES, width), BF16),
            pltpu.SemaphoreType.DMA((8,)),
        ],
        compiler_params=pltpu.CompilerParams(vmem_limit_bytes=28 << 20),
        name="split_rows",
    )(place, *pieces, first, up, in_hbm(down), in_hbm(sdown))


def block_kernel(share, place_ref, x_ref, first_ref, up_ref, down_ref, sdown_ref, out_ref, act, second, sems):
    copies = down_copies(share, place_ref, down_ref, sdown_ref, second, sems)

    @pl.when(pl.program_id(0) == 0)
    def _():
        run_copies(copies)

    width = up_ref.shape[0]
    node = place_ref[0]
    weight = row_weight(node, x_ref[:, width:])
    activate(share, node, x_ref[:, :width], first_ref, up_ref, weight, act)
    parts = 4
    piece = width // parts
    for i in range(parts):
        at = slice(i * piece, (i + 1) * piece)
        out_ref[:, at] = jnp.dot(act[...], second[:, at], preferred_element_type=F32).astype(BF16)


def block_rows(place, x, first, up, down, sdown, share):
    rows, packed = x.shape
    hidden, width = down.shape
    block = min(rows, ROW_BLOCK)
    return pl.pallas_call(
        functools.partial(block_kernel, share),
        grid=(rows // block,),
        in_specs=[SMEM_SPEC, pl.BlockSpec((block, packed), lambda i: (i, 0))] + [VMEM_SPEC] * 2 + [ANY_SPEC] * 2,
        out_specs=pl.BlockSpec((block, width), lambda i: (i, 0)),
        out_shape=jax.ShapeDtypeStruct((rows, width), BF16),
        scratch_shapes=[
            pltpu.VMEM((block, hidden + LANES), BF16),
            pltpu.VMEM((hidden + LANES, width), BF16),
            pltpu.SemaphoreType.DMA((8,)),
        ],
        compiler_params=pltpu.CompilerParams(vmem_limit_bytes=28 << 20),
        name="block_rows",
    )(place, x, first, up, in_hbm(down), in_hbm(sdown))


def f32_sum(*terms):
    return functools.reduce(lambda a, b: a + b, (t.astype(F32) for t in terms))


def swap(value, axis, bit):
    return lax.ppermute(value, axis, [(i, i ^ bit) for i in range(4)])


swap_z2 = functools.partial(swap, axis="local", bit=2)
swap_z1 = functools.partial(swap, axis="local", bit=1)
swap_x = functools.partial(swap, axis="node", bit=2)
swap_core = functools.partial(swap, axis="node", bit=1)


def stack(*values):
    return jnp.concatenate(values, axis=0)


def per_device(
    tokens,
    group_ids,
    route_weights,
    gate_experts,
    up_experts,
    down_experts,
    gate_shared,
    up_shared,
    down_shared,
):
    rows, width = tokens.shape
    node_count = lax.axis_size("node")
    local_count = lax.axis_size("local")
    share = max(1, LANES * node_count // gate_shared.shape[1])
    place = lax.axis_index("node").reshape(1)
    gate, up, down = gate_experts[0], up_experts[0], down_experts[0]
    first, dense = load_gate(place, group_ids, route_weights, gate, gate_shared, up_shared, share)

    if node_count != 4 or local_count != 4:
        up = load_up(up)
        x = lax.all_gather(
            jnp.concatenate([tokens, dense], axis=1), ("node", "local"), axis=0, tiled=True
        )
        part = block_rows(place, x, first, up, down, down_shared, share)
        return lax.psum_scatter(part, ("node", "local"), scatter_dimension=0, tiled=True)

    cut = width // 2
    got_dense = swap_z2(dense)
    got, first = lax.optimization_barrier((swap_z2(tokens), first))
    a = stack(tokens[:, :cut], got[:, :cut])
    b = jnp.concatenate(
        [stack(tokens[:, cut:], got[:, cut:]), stack(dense, got_dense)], axis=1
    )
    b = stack(b, swap_x(b))
    a = stack(a, swap_z1(a))
    b_got = swap_z1(b)
    a_got = swap_x(a)
    up = load_up(after(up, a, b))
    a_got, b_got, up = lax.optimization_barrier((a_got, b_got, up))
    a = stack(a, a_got)
    b = stack(b, b_got)
    pieces = (a, b, swap_core(a), swap_core(b))

    own_a, own_b, other_a, other_b = split_rows(place, pieces, first, up, down, down_shared, share)

    def scatter(own, other, swap_first, swap_second):
        got = swap_core(other)
        send = f32_sum(own[4 * rows :], got[4 * rows :]).astype(BF16)
        total = f32_sum(own[: 4 * rows], got[: 4 * rows], swap_first(send))
        total = f32_sum(total[: 2 * rows], swap_second(total[2 * rows :].astype(BF16)))
        return f32_sum(total[:rows], swap_z2(total[rows:].astype(BF16))).astype(BF16)

    a = scatter(own_a, other_a, swap_x, swap_z1)
    b = scatter(own_b, other_b, swap_z1, swap_x)
    return jnp.concatenate([a, b], axis=1)


def solution(mesh):
    in_specs = (
        P(("rep", "node", "local"), None),
        P(("rep", "node", "local"), None),
        P(("rep", "node", "local"), None),
        P("node", None, "local"),
        P("node", None, "local"),
        P("node", "local", None),
        P(None, "local"),
        P(None, "local"),
        P("local", None),
    )
    out_specs = P(("rep", "node", "local"), None)
    return jax.shard_map(
        per_device, mesh=mesh, in_specs=in_specs, out_specs=out_specs, check_vma=False
    )
```

time: 176 us -> 59.8 us (0.34)
  blocking collectives: 103 us -> 0 us
  matrix products: 26 us -> 0 us
  Pallas kernels: 0 us -> 13.5 us
  between operations: 13.5 us -> 0.17 us
  starting transfers between devices: 3.75 us -> 16.7 us
  waiting for transfers between devices: 19.6 us -> 26.8 us
  local copies, waits for them, and re-layouts: 6.33 us -> 1.43 us
  other arithmetic: 3.24 us -> 1.13 us
    all_gather x1 -> x0, blocking collectives: 52.3 us -> none  [per_device(): lax.all_gather(tokens, 'local', axis=0, tiled=True)]
    all_to_all x1 -> x0, blocking collectives: 51 us -> none  [per_device(): lax.all_to_all(outgoing, ('node', 'local'), split_axis=0, concat_axis=0,...]
    ppermute x0 -> x16, waiting for transfers between devices: none -> 26.8 us  [swap(): return lax.ppermute(value, axis, [(i, i ^ bit) for i in range(4)])]
    dot_general x4 -> x0, matrix products: 26 us -> none  [the longest x1 8.68 us: per_device(): jnp.dot(shared_act, down_shared, preferred_element_type=jnp.float32)]
    reduce_scatter x1 -> x0, waiting for transfers between devices: 19.6 us -> none  [per_device(): lax.psum_scatter(jnp.dot(shared_act, down_shared, preferred_element_type=...]
    ppermute x0 -> x16, starting transfers between devices: none -> 16.7 us  [swap(): return lax.ppermute(value, axis, [(i, i ^ bit) for i in range(4)])]
    pallas_call x0 -> x3, Pallas kernels: none -> 13.5 us  [the longest x1 5.95 us: split_rows(): pl.pallas_call(functools.partial(split_kernel, share), in_specs=[SMEM_SPE...]
    gather x8 -> x0, local copies, waits for them, and re-layouts: 4.29 us -> none  [the longest x1 2.16 us: per_device(): first_rows = tokens[row_source].reshape(node_count, group_rows, model_width)]
  transfers between devices with their start and end apart: 2 -> 16, of which waited for: 1 -> 11; matrix products, arithmetic and copies ran while one was open for 9% -> 1% of each run, Pallas kernels for 0% -> 13%
where the time goes in v3:
time: 59.8 us; the launch traced here: 59.7 us
  waiting for transfers between devices  26.8 us (45%)
  starting transfers between devices  16.7 us (28%)
  Pallas kernels  13.5 us (23%)
  local copies, waits for them, and re-layouts  1.43 us (2%)
  other arithmetic  1.13 us (2%)
    ppermute x16, waiting for transfers between devices, swap(): return lax.ppermute(value, axis, [(i, i ^ bit) for i in range(4)])  26.8 us
    ppermute x16, starting transfers between devices, swap(): return lax.ppermute(value, axis, [(i, i ^ bit) for i in range(4)])  16.7 us
    pallas_call x1, Pallas kernels, split_rows(): pl.pallas_call(functools.partial(split_kernel, share), in_specs=[SMEM_SPE...  5.95 us
    pallas_call x1, Pallas kernels, load_gate(): pl.pallas_call(functools.partial(load_gate_kernel, share), in_specs=[SMEM...  4.35 us
    pallas_call x1, Pallas kernels, load_up(): pl.pallas_call(load_up_kernel, in_specs=[ANY_SPEC], out_specs=VMEM_SPEC,...  3.17 us
    unnamed x6, local copies, waits for them, and re-layouts  1.36 us
  transfers between devices with their start and end apart: 16, of which 11 were waited for; matrix products, arithmetic and copies ran while one was open for 1% of the time, Pallas kernels for 13%

profile of v3, /device:TPU:0, one launch (start us, length us, event | category | flops | bytes accessed | tf_op | source)
XLA Modules:
  0.0 59.7 jit_solution(13932093300108523490)
XLA Ops:
  0.0 4.0 %collective-permute-start = (bf16[8,7168]{1,0:T(8,128)(2,1)}, bf16[8,7168]{1,0:T(8,128)(2,1)S(1)}, u32[]{:S(2)}, u32[]{:S(2)}) collective-permute-start(bf16[8,7168]{1,0:T(8,128)(2,1)} %param.9), channel_id=1, source_target_pairs={{0,2},{1,3},{2,0},{3,1},{4,6},{5,7},{6,4},{7,5},{8,10},{9,11},{10,... | collective-permute-start | bytes 344072 | tf_op jit(solution)/shard_map/ppermute | solution.py:258
  4.0 0.0 copy-start
  4.0 0.7 %copy-done = s32[8,4]{0,1:T(4,128)S(1)} copy-done((s32[8,4]{0,1:T(4,128)S(1)}, s32[8,4]{0,1:T(4,128)}, u32[]{:S(2)}) %copy-start) | copy-done | bytes 152
  4.7 0.0 copy-start.1
  4.7 0.7 %copy-done.1 = bf16[8,4]{0,1:T(4,128)(2,1)S(1)} copy-done((bf16[8,4]{0,1:T(4,128)(2,1)S(1)}, bf16[8,4]{0,1:T(4,128)(2,1)}, u32[]{:S(2)}) %copy-start.1) | copy-done | bytes 88
  5.4 0.0 copy-start.2
  5.4 4.3 %load_gate.1 = (bf16[7168,768]{1,0:T(8,128)(2,1)S(1)}, bf16[8,128]{1,0:T(8,128)(2,1)S(1)}) custom-call(s32[1]{0:T(128)} %bitcast.place_ref, s32[4,8]{1,0:T(4,128)S(1)} %bitcast.6, bf16[4,8]{1,0:T(4,128)(2,1)S(1)} %bitcast.7, bf16[7168,512]{1,0:T(8,128)(2,1)} %bitcast.9, bf16[7168,512]{1,0:T(8,128)(2,1)} %sgate_ref.1, bf16[7168,512]{1,0:T(8,128)(2,1)} %sup_ref.1), custom_call_target="tpu_custom_call" | custom-call | bytes 22020096 | tf_op jit(solution)/shard_map/load_gate/pallas_call | solution.py:72
  9.8 0.1 collective-permute-start.3
  9.8 0.0 copy-done.2
  9.9 0.0 collective-permute-done
  9.9 4.4 %collective-permute-done.3 = bf16[8,128]{1,0:T(8,128)(2,1)S(1)} collective-permute-done((bf16[8,128]{1,0:T(8,128)(2,1)S(1)}, bf16[8,128]{1,0:T(8,128)(2,1)S(1)}, u32[]{:S(2)}, u32[]{:S(2)}) %collective-permute-start.3) | collective-permute-done | bytes 2080 | tf_op jit(solution)/shard_map/ppermute | solution.py:258
  14.3 1.6 %collective-permute-start.4 = (bf16[16,3712]{1,0:T(8,128)(2,1)S(1)}, bf16[16,3712]{1,0:T(8,128)(2,1)S(1)}, u32[]{:S(2)}, u32[]{:S(2)}) collective-permute-start(bf16[16,3712]{1,0:T(8,128)(2,1)S(1)} %maximum_maximum_fusion), channel_id=1, source_target_pairs={{0,8},{4,12},{8,0},{12,4},{1,9},{5,13},{9,1},{13,5},{2,10},{6,14},... | collective-permute-start | bytes 356360 | tf_op jit(solution)/shard_map/ppermute | solution.py:258
  15.9 1.6 %collective-permute-start.1 = (bf16[16,3584]{1,0:T(8,128)(2,1)S(1)}, bf16[16,3584]{1,0:T(8,128)(2,1)S(1)}, u32[]{:S(2)}, u32[]{:S(2)}) collective-permute-start(bf16[16,3584]{1,0:T(8,128)(2,1)S(1)} %pad_maximum_fusion.4), channel_id=1, source_target_pairs={{0,1},{1,0},{2,3},{3,2},{4,5},{5,4},{6,7},{7,6},{8,9},{9,8},{10,11... | collective-permute-start | bytes 344072 | tf_op jit(solution)/shard_map/ppermute | solution.py:258
  17.5 1.7 %collective-permute-done.4 = bf16[16,3712]{1,0:T(8,128)(2,1)S(1)} collective-permute-done((bf16[16,3712]{1,0:T(8,128)(2,1)S(1)}, bf16[16,3712]{1,0:T(8,128)(2,1)S(1)}, u32[]{:S(2)}, u32[]{:S(2)}) %collective-permute-start.4) | collective-permute-done | bytes 118816 | tf_op jit(solution)/shard_map/ppermute | solution.py:258
  19.2 1.6 %collective-permute-start.5 = (bf16[32,3712]{1,0:T(8,128)(2,1)S(1)}, bf16[32,3712]{1,0:T(8,128)(2,1)S(1)}, u32[]{:S(2)}, u32[]{:S(2)}) collective-permute-start(bf16[32,3712]{1,0:T(8,128)(2,1)S(1)} %pad_maximum_fusion.2), channel_id=1, source_target_pairs={{0,1},{1,0},{2,3},{3,2},{4,5},{5,4},{6,7},{7,6},{8,9},{9,8},{10,11... | collective-permute-start | bytes 712712 | tf_op jit(solution)/shard_map/ppermute | solution.py:258
  20.9 1.0 %collective-permute-done.1 = bf16[16,3584]{1,0:T(8,128)(2,1)S(1)} collective-permute-done((bf16[16,3584]{1,0:T(8,128)(2,1)S(1)}, bf16[16,3584]{1,0:T(8,128)(2,1)S(1)}, u32[]{:S(2)}, u32[]{:S(2)}) %collective-permute-start.1) | collective-permute-done | bytes 114720 | tf_op jit(solution)/shard_map/ppermute | solution.py:258
  21.9 0.6 collective-permute-start.2
  22.5 3.2 %load_up.1.up_ref = bf16[7168,512]{1,0:T(8,128)(2,1)S(1)} custom-call(bf16[7168,512]{1,0:T(8,128)(2,1)} %bitcast.8), custom_call_target="tpu_custom_call" | custom-call | bytes 14680064 | tf_op jit(solution)/shard_map/load_up/pallas_call | solution.py:100
  25.6 2.3 %collective-permute-done.2 = bf16[32,3584]{1,0:T(8,128)(2,1)S(1)} collective-permute-done((bf16[32,3584]{1,0:T(8,128)(2,1)S(1)}, bf16[32,3584]{1,0:T(8,128)(2,1)S(1)}, u32[]{:S(2)}, u32[]{:S(2)}) %collective-permute-start.2) | collective-permute-done | bytes 229408 | tf_op jit(solution)/shard_map/ppermute | solution.py:258
  28.0 0.0 collective-permute-done.5
  28.0 0.1 collective-permute-start.7
  28.2 0.6 collective-permute-start.6
  28.7 1.9 %collective-permute-done.6.a1_ref = bf16[64,3584]{1,0:T(8,128)(2,1)S(1)} collective-permute-done((bf16[64,3584]{1,0:T(8,128)(2,1)S(1)}, bf16[64,3584]{1,0:T(8,128)(2,1)S(1)}, u32[]{:S(2)}, u32[]{:S(2)}) %collective-permute-start.6) | collective-permute-done | bytes 458784 | tf_op jit(solution)/shard_map/ppermute | solution.py:258
  30.6 0.0 collective-permute-done.7.b1_ref
  30.6 5.9 %split_rows.1 = (bf16[64,3584]{1,0:T(8,128)(2,1)S(1)}, bf16[64,3584]{1,0:T(8,128)(2,1)S(1)}, bf16[64,3584]{1,0:T(8,128)(2,1)S(1)}, bf16[64,3584]{1,0:T(8,128)(2,1)S(1)}) custom-call(s32[1]{0:T(128)} %bitcast.place_ref, bf16[64,3584]{1,0:T(8,128)(2,1)S(1)} %pad_maximum_fusion.1.a0_ref, bf16[64,3712]{1,0:T(8,128)(2,1)S(1)} %pad_maximum_fusion.b0_ref, ...), custom_call_target="tpu_custom_call" | custom-call | tf_op jit(solution)/shard_map/split_rows/pallas_call | solution.py:199
  36.6 0.2 collective-permute-start.8
  36.8 0.4 collective-permute-start.12
  37.1 1.3 %collective-permute-done.8 = bf16[64,3584]{1,0:T(8,128)(2,1)S(1)} collective-permute-done((bf16[64,3584]{1,0:T(8,128)(2,1)S(1)}, bf16[64,3584]{1,0:T(8,128)(2,1)S(1)}, u32[]{:S(2)}, u32[]{:S(2)}) %collective-permute-start.8) | collective-permute-done | bytes 458784 | tf_op jit(solution)/shard_map/ppermute | solution.py:258
  38.4 0.1 add_convert_fusion.1
  38.5 0.6 collective-permute-start.9
  39.1 0.0 collective-permute-done.12
  39.1 0.1 add_convert_fusion
  39.2 1.6 %collective-permute-start.13 = (bf16[32,3584]{1,0:T(8,128)(2,1)S(1)}, bf16[32,3584]{1,0:T(8,128)(2,1)S(1)}, u32[]{:S(2)}, u32[]{:S(2)}) collective-permute-start(bf16[32,3584]{1,0:T(8,128)(2,1)S(1)} %add_convert_fusion), channel_id=1, source_target_pairs={{0,1},{1,0},{2,3},{3,2},{4,5},{5,4},{6,7},{7,6},{8,9},{9,8},{10,11... | collective-permute-start | bytes 688136 | tf_op jit(solution)/shard_map/ppermute | solution.py:258
  40.8 5.4 %collective-permute-done.9 = bf16[32,3584]{1,0:T(8,128)(2,1)S(1)} collective-permute-done((bf16[32,3584]{1,0:T(8,128)(2,1)S(1)}, bf16[32,3584]{1,0:T(8,128)(2,1)S(1)}, u32[]{:S(2)}, u32[]{:S(2)}) %collective-permute-start.9) | collective-permute-done | bytes 229408 | tf_op jit(solution)/shard_map/ppermute | solution.py:258
  46.2 0.1 convert_add_fusion.1
  46.3 1.6 %collective-permute-start.10 = (bf16[16,3584]{1,0:T(8,128)(2,1)S(1)}, bf16[16,3584]{1,0:T(8,128)(2,1)S(1)}, u32[]{:S(2)}, u32[]{:S(2)}) collective-permute-start(bf16[16,3584]{1,0:T(8,128)(2,1)S(1)} %slice.117), channel_id=1, source_target_pairs={{0,1},{1,0},{2,3},{3,2},{4,5},{5,4},{6,7},{7,6},{8,9},{9,8},{10,11... | collective-permute-start | bytes 344072 | tf_op jit(solution)/shard_map/ppermute | solution.py:258
  48.0 0.0 collective-permute-done.13
  48.0 0.1 convert_add_fusion
  48.1 0.4 collective-permute-start.14
  48.4 2.8 %collective-permute-done.10 = bf16[16,3584]{1,0:T(8,128)(2,1)S(1)} collective-permute-done((bf16[16,3584]{1,0:T(8,128)(2,1)S(1)}, bf16[16,3584]{1,0:T(8,128)(2,1)S(1)}, u32[]{:S(2)}, u32[]{:S(2)}) %collective-permute-start.10) | collective-permute-done | bytes 114720 | tf_op jit(solution)/shard_map/ppermute | solution.py:258
  51.2 0.4 collective-permute-start.11
  51.6 1.3 %collective-permute-done.14 = bf16[16,3584]{1,0:T(8,128)(2,1)S(1)} collective-permute-done((bf16[16,3584]{1,0:T(8,128)(2,1)S(1)}, bf16[16,3584]{1,0:T(8,128)(2,1)S(1)}, u32[]{:S(2)}, u32[]{:S(2)}) %collective-permute-start.14) | collective-permute-done | bytes 114720 | tf_op jit(solution)/shard_map/ppermute | solution.py:258
  53.0 1.4 %collective-permute-start.15 = (bf16[8,3584]{1,0:T(8,128)(2,1)S(1)}, bf16[8,3584]{1,0:T(8,128)(2,1)S(1)}, u32[]{:S(2)}, u32[]{:S(2)}) collective-permute-start(bf16[8,3584]{1,0:T(8,128)(2,1)S(1)} %slice.118), channel_id=1, source_target_pairs={{0,2},{1,3},{2,0},{3,1},{4,6},{5,7},{6,4},{7,5},{8,10},{9,11},{10,... | collective-permute-start | bytes 172040 | tf_op jit(solution)/shard_map/ppermute | solution.py:258
  54.3 2.2 %collective-permute-done.11 = bf16[8,3584]{1,0:T(8,128)(2,1)S(1)} collective-permute-done((bf16[8,3584]{1,0:T(8,128)(2,1)S(1)}, bf16[8,3584]{1,0:T(8,128)(2,1)S(1)}, u32[]{:S(2)}, u32[]{:S(2)}) %collective-permute-start.11) | collective-permute-done | bytes 57376 | tf_op jit(solution)/shard_map/ppermute | solution.py:258
  56.6 2.4 %collective-permute-done.15 = bf16[8,3584]{1,0:T(8,128)(2,1)S(1)} collective-permute-done((bf16[8,3584]{1,0:T(8,128)(2,1)S(1)}, bf16[8,3584]{1,0:T(8,128)(2,1)S(1)}, u32[]{:S(2)}, u32[]{:S(2)}) %collective-permute-start.15) | collective-permute-done | bytes 57376 | tf_op jit(solution)/shard_map/ppermute | solution.py:258
  59.0 0.7 %pad_maximum_fusion.5 = bf16[8,7168]{1,0:T(8,128)(2,1)} fusion(bf16[8,3584]{1,0:T(8,128)(2,1)S(1)} %fusion, bf16[8,3584]{1,0:T(8,128)(2,1)S(1)} %fusion.1), kind=kLoop, calls=%fused_computation.20 | loop fusion | flops 229376 | bytes 229376 | tf_op jit(solution)/shard_map/concatenate | solution.py:326
  (16 shorter events, 0.3 us)
Async XLA Ops:
  0.0 9.9 %collective-permute-start = (bf16[8,7168]{1,0:T(8,128)(2,1)}, bf16[8,7168]{1,0:T(8,128)(2,1)S(1)}, u32[]{:S(2)}, u32[]{:S(2)}) collective-permute-start(bf16[8,7168]{1,0:T(8,128)(2,1)} %param.9), channel_id=1, source_target_pairs={{0,2},{1,3},{2,0},{3,1},{4,6},{5,7},{6,4},{7,5},{8,10},{9,11},{10,... | collective-permute-start | bytes 344072 | tf_op jit(solution)/shard_map/ppermute | solution.py:258
  4.0 0.7 %copy-start = (s32[8,4]{0,1:T(4,128)S(1)}, s32[8,4]{0,1:T(4,128)}, u32[]{:S(2)}) copy-start(s32[8,4]{0,1:T(4,128)} %param.10) | copy-start | bytes 388
  4.7 0.7 %copy-start.1 = (bf16[8,4]{0,1:T(4,128)(2,1)S(1)}, bf16[8,4]{0,1:T(4,128)(2,1)}, u32[]{:S(2)}) copy-start(bf16[8,4]{0,1:T(4,128)(2,1)} %param.11) | copy-start | bytes 196
  5.4 4.4 %copy-start.2 = (bf16[8,7168]{1,0:T(8,128)(2,1)S(1)}, bf16[8,7168]{1,0:T(8,128)(2,1)}, u32[]{:S(2)}) copy-start(bf16[8,7168]{1,0:T(8,128)(2,1)} %param.9) | copy-start | bytes 344068
  9.8 4.5 %collective-permute-start.3 = (bf16[8,128]{1,0:T(8,128)(2,1)S(1)}, bf16[8,128]{1,0:T(8,128)(2,1)S(1)}, u32[]{:S(2)}, u32[]{:S(2)}) collective-permute-start(bf16[8,128]{1,0:T(8,128)(2,1)S(1)} %get-tuple-element.19), channel_id=1, source_target_pairs={{0,2},{1,3},{2,0},{3,1},{4,6},{5,7},{6,4},{7,5},{8,10},{9,11},{10,... | collective-permute-start | bytes 6152 | tf_op jit(solution)/shard_map/ppermute | solution.py:258
  14.3 4.9 %collective-permute-start.4 = (bf16[16,3712]{1,0:T(8,128)(2,1)S(1)}, bf16[16,3712]{1,0:T(8,128)(2,1)S(1)}, u32[]{:S(2)}, u32[]{:S(2)}) collective-permute-start(bf16[16,3712]{1,0:T(8,128)(2,1)S(1)} %maximum_maximum_fusion), channel_id=1, source_target_pairs={{0,8},{4,12},{8,0},{12,4},{1,9},{5,13},{9,1},{13,5},{2,10},{6,14},... | collective-permute-start | bytes 356360 | tf_op jit(solution)/shard_map/ppermute | solution.py:258
  15.9 6.0 %collective-permute-start.1 = (bf16[16,3584]{1,0:T(8,128)(2,1)S(1)}, bf16[16,3584]{1,0:T(8,128)(2,1)S(1)}, u32[]{:S(2)}, u32[]{:S(2)}) collective-permute-start(bf16[16,3584]{1,0:T(8,128)(2,1)S(1)} %pad_maximum_fusion.4), channel_id=1, source_target_pairs={{0,1},{1,0},{2,3},{3,2},{4,5},{5,4},{6,7},{7,6},{8,9},{9,8},{10,11... | collective-permute-start | bytes 344072 | tf_op jit(solution)/shard_map/ppermute | solution.py:258
  19.2 8.7 %collective-permute-start.5 = (bf16[32,3712]{1,0:T(8,128)(2,1)S(1)}, bf16[32,3712]{1,0:T(8,128)(2,1)S(1)}, u32[]{:S(2)}, u32[]{:S(2)}) collective-permute-start(bf16[32,3712]{1,0:T(8,128)(2,1)S(1)} %pad_maximum_fusion.2), channel_id=1, source_target_pairs={{0,1},{1,0},{2,3},{3,2},{4,5},{5,4},{6,7},{7,6},{8,9},{9,8},{10,11... | collective-permute-start | bytes 712712 | tf_op jit(solution)/shard_map/ppermute | solution.py:258
  21.9 6.1 %collective-permute-start.2 = (bf16[32,3584]{1,0:T(8,128)(2,1)S(1)}, bf16[32,3584]{1,0:T(8,128)(2,1)S(1)}, u32[]{:S(2)}, u32[]{:S(2)}) collective-permute-start(bf16[32,3584]{1,0:T(8,128)(2,1)S(1)} %pad_maximum_fusion.3), channel_id=1, source_target_pairs={{0,8},{4,12},{8,0},{12,4},{1,9},{5,13},{9,1},{13,5},{2,10},{6,14},... | collective-permute-start | bytes 688136 | tf_op jit(solution)/shard_map/ppermute | solution.py:258
  28.0 2.6 %collective-permute-start.7 = (bf16[64,3712]{1,0:T(8,128)(2,1)S(1)}, bf16[64,3712]{1,0:T(8,128)(2,1)S(1)}, u32[]{:S(2)}, u32[]{:S(2)}) collective-permute-start(bf16[64,3712]{1,0:T(8,128)(2,1)S(1)} %pad_maximum_fusion.b0_ref), channel_id=1, source_target_pairs={{0,4},{4,0},{8,12},{12,8},{1,5},{5,1},{9,13},{13,9},{2,6},{6,2},{1... | collective-permute-start | bytes 1425416 | tf_op jit(solution)/shard_map/ppermute | solution.py:258
  28.2 2.4 %collective-permute-start.6 = (bf16[64,3584]{1,0:T(8,128)(2,1)S(1)}, bf16[64,3584]{1,0:T(8,128)(2,1)S(1)}, u32[]{:S(2)}, u32[]{:S(2)}) collective-permute-start(bf16[64,3584]{1,0:T(8,128)(2,1)S(1)} %pad_maximum_fusion.1.a0_ref), channel_id=1, source_target_pairs={{0,4},{4,0},{8,12},{12,8},{1,5},{5,1},{9,13},{13,9},{2,6},{6,2},{1... | collective-permute-start | bytes 1376264 | tf_op jit(solution)/shard_map/ppermute | solution.py:258
  36.6 1.9 %collective-permute-start.8 = (bf16[64,3584]{1,0:T(8,128)(2,1)S(1)}, bf16[64,3584]{1,0:T(8,128)(2,1)S(1)}, u32[]{:S(2)}, u32[]{:S(2)}) collective-permute-start(bf16[64,3584]{1,0:T(8,128)(2,1)S(1)} %get-tuple-element.26), channel_id=1, source_target_pairs={{0,4},{4,0},{8,12},{12,8},{1,5},{5,1},{9,13},{13,9},{2,6},{6,2},{1... | collective-permute-start | bytes 1376264 | tf_op jit(solution)/shard_map/ppermute | solution.py:258
  36.8 2.3 %collective-permute-start.12 = (bf16[64,3584]{1,0:T(8,128)(2,1)S(1)}, bf16[64,3584]{1,0:T(8,128)(2,1)S(1)}, u32[]{:S(2)}, u32[]{:S(2)}) collective-permute-start(bf16[64,3584]{1,0:T(8,128)(2,1)S(1)} %get-tuple-element.28), channel_id=1, source_target_pairs={{0,4},{4,0},{8,12},{12,8},{1,5},{5,1},{9,13},{13,9},{2,6},{6,2},{1... | collective-permute-start | bytes 1376264 | tf_op jit(solution)/shard_map/ppermute | solution.py:258
  38.5 7.7 %collective-permute-start.9 = (bf16[32,3584]{1,0:T(8,128)(2,1)S(1)}, bf16[32,3584]{1,0:T(8,128)(2,1)S(1)}, u32[]{:S(2)}, u32[]{:S(2)}) collective-permute-start(bf16[32,3584]{1,0:T(8,128)(2,1)S(1)} %add_convert_fusion.1), channel_id=1, source_target_pairs={{0,8},{4,12},{8,0},{12,4},{1,9},{5,13},{9,1},{13,5},{2,10},{6,14},... | collective-permute-start | bytes 688136 | tf_op jit(solution)/shard_map/ppermute | solution.py:258
  39.2 8.8 %collective-permute-start.13 = (bf16[32,3584]{1,0:T(8,128)(2,1)S(1)}, bf16[32,3584]{1,0:T(8,128)(2,1)S(1)}, u32[]{:S(2)}, u32[]{:S(2)}) collective-permute-start(bf16[32,3584]{1,0:T(8,128)(2,1)S(1)} %add_convert_fusion), channel_id=1, source_target_pairs={{0,1},{1,0},{2,3},{3,2},{4,5},{5,4},{6,7},{7,6},{8,9},{9,8},{10,11... | collective-permute-start | bytes 688136 | tf_op jit(solution)/shard_map/ppermute | solution.py:258
  46.3 4.9 %collective-permute-start.10 = (bf16[16,3584]{1,0:T(8,128)(2,1)S(1)}, bf16[16,3584]{1,0:T(8,128)(2,1)S(1)}, u32[]{:S(2)}, u32[]{:S(2)}) collective-permute-start(bf16[16,3584]{1,0:T(8,128)(2,1)S(1)} %slice.117), channel_id=1, source_target_pairs={{0,1},{1,0},{2,3},{3,2},{4,5},{5,4},{6,7},{7,6},{8,9},{9,8},{10,11... | collective-permute-start | bytes 344072 | tf_op jit(solution)/shard_map/ppermute | solution.py:258
  48.1 4.9 %collective-permute-start.14 = (bf16[16,3584]{1,0:T(8,128)(2,1)S(1)}, bf16[16,3584]{1,0:T(8,128)(2,1)S(1)}, u32[]{:S(2)}, u32[]{:S(2)}) collective-permute-start(bf16[16,3584]{1,0:T(8,128)(2,1)S(1)} %slice.116), channel_id=1, source_target_pairs={{0,8},{4,12},{8,0},{12,4},{1,9},{5,13},{9,1},{13,5},{2,10},{6,14},... | collective-permute-start | bytes 344072 | tf_op jit(solution)/shard_map/ppermute | solution.py:258
  51.2 5.3 %collective-permute-start.11 = (bf16[8,3584]{1,0:T(8,128)(2,1)S(1)}, bf16[8,3584]{1,0:T(8,128)(2,1)S(1)}, u32[]{:S(2)}, u32[]{:S(2)}) collective-permute-start(bf16[8,3584]{1,0:T(8,128)(2,1)S(1)} %slice.119), channel_id=1, source_target_pairs={{0,2},{1,3},{2,0},{3,1},{4,6},{5,7},{6,4},{7,5},{8,10},{9,11},{10,... | collective-permute-start | bytes 172040 | tf_op jit(solution)/shard_map/ppermute | solution.py:258
  53.0 6.0 %collective-permute-start.15 = (bf16[8,3584]{1,0:T(8,128)(2,1)S(1)}, bf16[8,3584]{1,0:T(8,128)(2,1)S(1)}, u32[]{:S(2)}, u32[]{:S(2)}) collective-permute-start(bf16[8,3584]{1,0:T(8,128)(2,1)S(1)} %slice.118), channel_id=1, source_target_pairs={{0,2},{1,3},{2,0},{3,1},{4,6},{5,7},{6,4},{7,5},{8,10},{9,11},{10,... | collective-permute-start | bytes 172040 | tf_op jit(solution)/shard_map/ppermute | solution.py:258

commit v4 on v3

--- a/solution.py
+++ b/solution.py
@@ -35,9 +35,25 @@
     return pl.multiple_of((place_ref[0] // share) * LANES, LANES)
 
 
-def load_gate_kernel(
-    share, place_ref, groups_ref, weights_ref, gate_ref, sgate_ref, sup_ref, out_ref, dense_ref, sems
-):
+def dense_kernel(groups_ref, weights_ref, out_ref):
+    groups = groups_ref[...].T
+    weights = weights_ref[...].astype(F32).T
+    lane = lax.broadcasted_iota(jnp.int32, out_ref.shape, 1)
+    dense = jnp.zeros(out_ref.shape, F32)
+    for k in range(groups.shape[1]):
+        dense += jnp.where(lane == groups[:, k : k + 1], weights[:, k : k + 1], 0.0)
+    out_ref[...] = dense.astype(BF16)
+
+
+def dense_weights(group_ids, route_weights):
+    return pl.pallas_call(
+        dense_kernel,
+        out_shape=jax.ShapeDtypeStruct((group_ids.shape[0], LANES), BF16),
+        name="dense_weights",
+    )(group_ids.T, route_weights.T)
+
+
+def load_gate_kernel(share, place_ref, gate_ref, sgate_ref, sup_ref, out_ref, sems):
     width, hidden = gate_ref.shape
     column = shared_column(place_ref, share)
     parts = 4
@@ -53,32 +69,22 @@
             copies.append(
                 pltpu.make_async_copy(source, out_ref.at[at, pl.ds(lower, size)], sems.at[len(copies)])
             )
-    for copy in copies:
-        copy.start()
-    groups = groups_ref[...].T
-    weights = weights_ref[...].astype(F32).T
-    lane = lax.broadcasted_iota(jnp.int32, dense_ref.shape, 1)
-    dense = jnp.zeros(dense_ref.shape, F32)
-    for k in range(groups.shape[1]):
-        dense += jnp.where(lane == groups[:, k : k + 1], weights[:, k : k + 1], 0.0)
-    dense_ref[...] = dense.astype(BF16)
-    for copy in copies:
-        copy.wait()
-
-
-def load_gate(place, group_ids, route_weights, gate, sgate, sup, share):
+    run_copies(copies)
+
+
+def load_gate(place, gate, sgate, sup, share):
     width, hidden = gate.shape
     shape = (width, hidden + 2 * LANES)
     return pl.pallas_call(
         functools.partial(load_gate_kernel, share),
-        in_specs=[SMEM_SPEC] + [VMEM_SPEC] * 2 + [ANY_SPEC] * 3,
-        out_specs=[VMEM_SPEC] * 2,
-        out_shape=[pltpu.VMEM(shape, BF16), pltpu.VMEM((group_ids.shape[0], LANES), BF16)],
+        in_specs=[SMEM_SPEC] + [ANY_SPEC] * 3,
+        out_specs=VMEM_SPEC,
+        out_shape=pltpu.VMEM(shape, BF16),
         scratch_shapes=[pltpu.SemaphoreType.DMA((12,))],
         cost_estimate=pl.CostEstimate(flops=0, bytes_accessed=4 * shape[0] * shape[1], transcendentals=0),
         compiler_params=pltpu.CompilerParams(vmem_limit_bytes=1 << 20),
         name="load_gate",
-    )(place, group_ids.T, route_weights.T, in_hbm(gate), in_hbm(sgate), in_hbm(sup))
+    )(place, in_hbm(gate), in_hbm(sgate), in_hbm(sup))
 
 
 def load_up_kernel(up_ref, out_ref, sems):
@@ -152,6 +158,18 @@
     return copies
 
 
+def regroup(value, outer, inner):
+    rows = value.shape[0] // (outer * inner)
+    return jnp.concatenate(
+        [
+            value[(o * inner + i) * rows : (o * inner + i + 1) * rows]
+            for i in range(inner)
+            for o in range(outer)
+        ],
+        axis=0,
+    )
+
+
 def split_kernel(
     share, place_ref, a0_ref, b0_ref, a1_ref, b1_ref, first_ref, up_ref, down_ref, sdown_ref,
     own_a_ref, own_b_ref, other_a_ref, other_b_ref, x, act, second, sems,
@@ -161,46 +179,42 @@
         copy.start()
     width = up_ref.shape[0]
     half, cut = a0_ref.shape
-    quarter = half // 4
-    order = (0, 2, 1, 3)
     for c, (a_ref, b_ref) in enumerate(((a0_ref, b0_ref), (a1_ref, b1_ref))):
-        x[c * half : (c + 1) * half, :cut] = a_ref[...]
-        for i, j in enumerate(order):
-            x[c * half + i * quarter : c * half + (i + 1) * quarter, cut:] = b_ref[
-                j * quarter : (j + 1) * quarter, :
-            ]
+        rows = slice(c * half, (c + 1) * half)
+        x[rows, :cut] = a_ref[...]
+        x[rows, cut:] = regroup(b_ref[...].astype(F32), 4, 2).astype(BF16)
     node = place_ref[0]
     weight = row_weight(node, x[:, width:])
     activate(share, node, x[:, :width], first_ref, up_ref, weight, act)
-    parts = 4
-    piece = width // parts
+    parts = len(copies) // 2
+    piece = width // parts
+    cut = own_a_ref.shape[1]
     for i in range(parts):
         copies[2 * i].wait()
         copies[2 * i + 1].wait()
-        total = jnp.dot(
-            act[...], second[:, i * piece : (i + 1) * piece], preferred_element_type=F32
-        ).astype(BF16)
-        if i < parts // 2:
-            at = slice(i * piece, (i + 1) * piece)
-            own_a_ref[:, at] = total[:half]
-            other_a_ref[:, at] = total[half:]
-        else:
-            at = slice(i * piece - cut, (i + 1) * piece - cut)
-            for k, j in enumerate(order):
-                to = slice(k * quarter, (k + 1) * quarter)
-                own_b_ref[to, at] = total[j * quarter : (j + 1) * quarter]
-                other_b_ref[to, at] = total[half + j * quarter : half + (j + 1) * quarter]
-
-
-def split_rows(place, pieces, first, up, down, sdown, share):
-    half, cut = pieces[0].shape
+        lower, upper = i * piece, (i + 1) * piece
+        for at, to in ((lower, min(upper, cut)), (max(lower, cut), upper)):
+            if at >= to:
+                continue
+            total = jnp.dot(act[...], second[:, at:to], preferred_element_type=F32)
+            if to <= cut:
+                own_a_ref[:, at:to] = total[:half].astype(BF16)
+                other_a_ref[:, at:to] = total[half:].astype(BF16)
+            else:
+                own_b_ref[:, at - cut : to - cut] = regroup(total[:half], 2, 4).astype(BF16)
+                other_b_ref[:, at - cut : to - cut] = regroup(total[half:], 2, 4).astype(BF16)
+
+
+def split_rows(place, pieces, first, up, down, sdown, cut, share):
+    half = pieces[0].shape[0]
     hidden, width = down.shape
-    out = jax.ShapeDtypeStruct((half, cut), BF16)
+    out_a = jax.ShapeDtypeStruct((half, cut), BF16)
+    out_b = jax.ShapeDtypeStruct((half, width - cut), BF16)
     return pl.pallas_call(
         functools.partial(split_kernel, share),
         in_specs=[SMEM_SPEC] + [VMEM_SPEC] * 6 + [ANY_SPEC] * 2,
         out_specs=[VMEM_SPEC] * 4,
-        out_shape=[out] * 4,
+        out_shape=[out_a, out_b] * 2,
         scratch_shapes=[
             pltpu.VMEM((2 * half, width + LANES), BF16),
             pltpu.VMEM((2 * half, hidden + LANES), BF16),
@@ -258,10 +272,12 @@
     return lax.ppermute(value, axis, [(i, i ^ bit) for i in range(4)])
 
 
-swap_z2 = functools.partial(swap, axis="local", bit=2)
-swap_z1 = functools.partial(swap, axis="local", bit=1)
 swap_x = functools.partial(swap, axis="node", bit=2)
 swap_core = functools.partial(swap, axis="node", bit=1)
+
+
+def swap_z(value, k):
+    return swap(value, "local", k)
 
 
 def stack(*values):
@@ -285,9 +301,10 @@
     share = max(1, LANES * node_count // gate_shared.shape[1])
     place = lax.axis_index("node").reshape(1)
     gate, up, down = gate_experts[0], up_experts[0], down_experts[0]
-    first, dense = load_gate(place, group_ids, route_weights, gate, gate_shared, up_shared, share)
+    dense = dense_weights(group_ids, route_weights)
 
     if node_count != 4 or local_count != 4:
+        first = load_gate(place, gate, gate_shared, up_shared, share)
         up = load_up(up)
         x = lax.all_gather(
             jnp.concatenate([tokens, dense], axis=1), ("node", "local"), axis=0, tiled=True
@@ -295,35 +312,42 @@
         part = block_rows(place, x, first, up, down, down_shared, share)
         return lax.psum_scatter(part, ("node", "local"), scatter_dimension=0, tiled=True)
 
-    cut = width // 2
-    got_dense = swap_z2(dense)
-    got, first = lax.optimization_barrier((swap_z2(tokens), first))
-    a = stack(tokens[:, :cut], got[:, :cut])
+    steps = (3, 2, 1)
+    cut = width * 39 // 56 // LANES * LANES
+    across = swap_x(tokens)
+    a = tokens[:, :cut]
+    got = {k: swap_z(a, k) for k in steps}
+    dense_across = swap_x(dense)
+    first = load_gate(after(place, dense), gate, gate_shared, up_shared, share)
+    across, dense_across, got, first = lax.optimization_barrier((across, dense_across, got, first))
+    far = stack(got[1], got[2], got[3])
     b = jnp.concatenate(
-        [stack(tokens[:, cut:], got[:, cut:]), stack(dense, got_dense)], axis=1
-    )
-    b = stack(b, swap_x(b))
-    a = stack(a, swap_z1(a))
-    b_got = swap_z1(b)
-    a_got = swap_x(a)
-    up = load_up(after(up, a, b))
-    a_got, b_got, up = lax.optimization_barrier((a_got, b_got, up))
-    a = stack(a, a_got)
-    b = stack(b, b_got)
+        [stack(tokens[:, cut:], across[:, cut:]), stack(dense, dense_across)], axis=1
+    )
+    b_got = {k: swap_z(b, k) for k in steps}
+    far_across = swap_x(far)
+    up = load_up(after(up, far, b))
+    far_across, b_got, up = lax.optimization_barrier((far_across, b_got, up))
+    a = stack(a, far, across[:, :cut], far_across)
+    b = stack(b, b_got[1], b_got[2], b_got[3])
     pieces = (a, b, swap_core(a), swap_core(b))
 
-    own_a, own_b, other_a, other_b = split_rows(place, pieces, first, up, down, down_shared, share)
-
-    def scatter(own, other, swap_first, swap_second):
-        got = swap_core(other)
-        send = f32_sum(own[4 * rows :], got[4 * rows :]).astype(BF16)
-        total = f32_sum(own[: 4 * rows], got[: 4 * rows], swap_first(send))
-        total = f32_sum(total[: 2 * rows], swap_second(total[2 * rows :].astype(BF16)))
-        return f32_sum(total[:rows], swap_z2(total[rows:].astype(BF16))).astype(BF16)
-
-    a = scatter(own_a, other_a, swap_x, swap_z1)
-    b = scatter(own_b, other_b, swap_z1, swap_x)
-    return jnp.concatenate([a, b], axis=1)
+    cut = width * 36 // 56 // LANES * LANES
+    own_a, own_b, other_a, other_b = split_rows(place, pieces, first, up, down, down_shared, cut, share)
+
+    four, two = 4 * rows, 2 * rows
+    a_got = swap_core(other_a)
+    b_got = swap_core(other_b)
+    a_sum = f32_sum(own_a[:four], a_got[:four], swap_x(f32_sum(own_a[four:], a_got[four:]).astype(BF16)))
+    b_sum = f32_sum(own_b[:two], b_got[:two])
+    for k in steps:
+        at = slice(k * two, (k + 1) * two)
+        b_sum = f32_sum(b_sum, swap_z(f32_sum(own_b[at], b_got[at]).astype(BF16), k))
+    a = a_sum[:rows]
+    for k in steps:
+        a = f32_sum(a, swap_z(a_sum[k * rows : (k + 1) * rows].astype(BF16), k))
+    b = f32_sum(b_sum[:rows], swap_x(b_sum[rows:].astype(BF16)))
+    return jnp.concatenate([a.astype(BF16), b.astype(BF16)], axis=1)
 
 
 def solution(mesh):

time: 59.8 us -> 59.8 us (level)
  waiting for transfers between devices: 26.8 us -> 14.5 us
  starting transfers between devices: 16.7 us -> 27.3 us
  Pallas kernels: 13.5 us -> 14.7 us
    ppermute x16 -> x21, waiting for transfers between devices: 26.8 us -> 14.5 us  [swap(): return lax.ppermute(value, axis, [(i, i ^ bit) for i in range(4)])]
    ppermute x16 -> x21, starting transfers between devices: 16.7 us -> 27.3 us  [swap(): return lax.ppermute(value, axis, [(i, i ^ bit) for i in range(4)])]
    pallas_call x0 -> x1, Pallas kernels: none -> 1.43 us  [dense_weights(): pl.pallas_call(dense_kernel, out_shape=jax.ShapeDtypeStruct((group_ids.sh...]
    unnamed x6 -> x5, local copies, waits for them, and re-layouts: 1.36 us -> 0.05 us
    slice x5 -> x4, local copies, waits for them, and re-layouts: 0.06 us -> 0.96 us  [the longest x1 0.93 us: per_device(): a = tokens[:, :cut]]
    slice x1, local copies, waits for them, and re-layouts: 0.01 us -> 0.77 us  [per_device(): tokens[:, cut:]]
  transfers between devices with their start and end apart: 16 -> 21, of which waited for: 11 -> 9; matrix products, arithmetic and copies ran while one was open for 1% -> 4% of each run, Pallas kernels for 13% -> 15%
where the time goes in v4:
time: 59.8 us; the launch traced here: 59.6 us
  starting transfers between devices  27.3 us (46%)
  Pallas kernels  14.7 us (25%)
  waiting for transfers between devices  14.5 us (24%)
  local copies, waits for them, and re-layouts  1.82 us (3%)
  other arithmetic  1.03 us (2%)
    ppermute x21, starting transfers between devices, swap(): return lax.ppermute(value, axis, [(i, i ^ bit) for i in range(4)])  27.3 us
    ppermute x21, waiting for transfers between devices, swap(): return lax.ppermute(value, axis, [(i, i ^ bit) for i in range(4)])  14.5 us
    pallas_call x1, Pallas kernels, split_rows(): pl.pallas_call(functools.partial(split_kernel, share), in_specs=[SMEM_SPE...  5.83 us
    pallas_call x1, Pallas kernels, load_gate(): pl.pallas_call(functools.partial(load_gate_kernel, share), in_specs=[SMEM...  4.32 us
    pallas_call x1, Pallas kernels, load_up(): pl.pallas_call(load_up_kernel, in_specs=[ANY_SPEC], out_specs=VMEM_SPEC,...  3.17 us
    pallas_call x1, Pallas kernels, dense_weights(): pl.pallas_call(dense_kernel, out_shape=jax.ShapeDtypeStruct((group_ids.sh...  1.43 us
  transfers between devices with their start and end apart: 21, of which 9 were waited for; matrix products, arithmetic and copies ran while one was open for 4% of the time, Pallas kernels for 15%

profile of v4, /device:TPU:0, one launch (start us, length us, event | category | flops | bytes accessed | tf_op | source)
XLA Modules:
  0.0 59.6 jit_solution(12599424927493318559)
XLA Ops:
  0.0 2.9 %collective-permute-start = (bf16[8,7168]{1,0:T(8,128)(2,1)}, bf16[8,7168]{1,0:T(8,128)(2,1)S(1)}, u32[]{:S(2)}, u32[]{:S(2)}) collective-permute-start(bf16[8,7168]{1,0:T(8,128)(2,1)} %param.9), channel_id=1, source_target_pairs={{0,8},{4,12},{8,0},{12,4},{1,9},{5,13},{9,1},{13,5},{2,10},{6,14},... | collective-permute-start | bytes 344072 | tf_op jit(solution)/shard_map/ppermute | solution.py:272
  2.9 0.9 %fusion.6 = (bf16[8,4992]{1,0:T(8,128)(2,1)S(1)}, bf16[64,4992]{1,0:T(8,128)(2,1)S(1)}) fusion(bf16[8,7168]{1,0:T(8,128)(2,1)} %param.9), kind=kLoop, calls=%fused_computation.27 | loop fusion | bytes 239616 | tf_op jit(solution)/shard_map/slice | solution.py:318
  3.9 3.7 %collective-permute-start.4 = (bf16[8,4992]{1,0:T(8,128)(2,1)S(1)}, bf16[8,4992]{1,0:T(8,128)(2,1)S(1)}, u32[]{:S(2)}, u32[]{:S(2)}) collective-permute-start(bf16[8,4992]{1,0:T(8,128)(2,1)S(1)} %get-tuple-element.47), channel_id=1, source_target_pairs={{0,3},{1,2},{2,1},{3,0},{4,7},{5,6},{6,5},{7,4},{8,11},{9,10},{10,... | collective-permute-start | bytes 239624 | tf_op jit(solution)/shard_map/ppermute | solution.py:272
  7.5 0.0 collective-permute-start.3
  7.5 0.8 %collective-permute-start.2 = (bf16[8,4992]{1,0:T(8,128)(2,1)S(1)}, bf16[8,4992]{1,0:T(8,128)(2,1)S(1)}, u32[]{:S(2)}, u32[]{:S(2)}) collective-permute-start(bf16[8,4992]{1,0:T(8,128)(2,1)S(1)} %get-tuple-element.47), channel_id=1, source_target_pairs={{0,1},{1,0},{2,3},{3,2},{4,5},{5,4},{6,7},{7,6},{8,9},{9,8},{10,11... | collective-permute-start | bytes 239624 | tf_op jit(solution)/shard_map/ppermute | solution.py:272
  8.3 1.4 %dense_weights.1 = bf16[8,128]{1,0:T(8,128)(2,1)} custom-call(s32[4,8]{1,0:T(4,128)} %bitcast.9, bf16[4,8]{1,0:T(4,128)(2,1)} %bitcast.10), custom_call_target="tpu_custom_call" | custom-call | tf_op jit(solution)/shard_map/dense_weights/pallas_call | solution.py:49
  9.8 0.4 collective-permute-start.1
  10.1 0.8 %slice.72 = bf16[8,2176]{1,0:T(8,128)(2,1)S(1)} slice(bf16[8,7168]{1,0:T(8,128)(2,1)} %param.9), slice={[0:8], [4992:7168]} | slice | bytes 69632 | tf_op jit(solution)/shard_map/slice | solution.py:325
  10.9 4.3 %load_gate.1.first_ref = bf16[7168,768]{1,0:T(8,128)(2,1)S(1)} custom-call(s32[1]{0:T(128)} %bitcast.place_ref, bf16[7168,512]{1,0:T(8,128)(2,1)} %bitcast.7, bf16[7168,512]{1,0:T(8,128)(2,1)} %sgate_ref.1, bf16[7168,512]{1,0:T(8,128)(2,1)} %sup_ref.1), custom_call_target="tpu_custom_call" | custom-call | bytes 22020096 | tf_op jit(solution)/shard_map/load_gate/pallas_call | solution.py:78
  15.2 0.0 collective-permute-done.1
  15.3 0.0 collective-permute-done.4
  15.3 0.0 collective-permute-done.3
  15.3 0.0 collective-permute-done.2
  15.3 0.0 collective-permute-done
  15.3 3.8 %collective-permute-start.8 = (bf16[16,2304]{1,0:T(8,128)(2,1)S(1)}, bf16[16,2304]{1,0:T(8,128)(2,1)S(1)}, u32[]{:S(2)}, u32[]{:S(2)}) collective-permute-start(bf16[16,2304]{1,0:T(8,128)(2,1)S(1)} %maximum_maximum_fusion), channel_id=1, source_target_pairs={{0,3},{1,2},{2,1},{3,0},{4,7},{5,6},{6,5},{7,4},{8,11},{9,10},{10,... | collective-permute-start | bytes 221192 | tf_op jit(solution)/shard_map/ppermute | solution.py:272
  19.1 0.0 collective-permute-start.7
  19.2 0.6 %collective-permute-start.6 = (bf16[16,2304]{1,0:T(8,128)(2,1)S(1)}, bf16[16,2304]{1,0:T(8,128)(2,1)S(1)}, u32[]{:S(2)}, u32[]{:S(2)}) collective-permute-start(bf16[16,2304]{1,0:T(8,128)(2,1)S(1)} %maximum_maximum_fusion), channel_id=1, source_target_pairs={{0,1},{1,0},{2,3},{3,2},{4,5},{5,4},{6,7},{7,6},{8,9},{9,8},{10,11... | collective-permute-start | bytes 221192 | tf_op jit(solution)/shard_map/ppermute | solution.py:272
  19.9 1.7 %collective-permute-start.5 = (bf16[24,4992]{1,0:T(8,128)(2,1)S(1)}, bf16[24,4992]{1,0:T(8,128)(2,1)S(1)}, u32[]{:S(2)}, u32[]{:S(2)}) collective-permute-start(bf16[24,4992]{1,0:T(8,128)(2,1)S(1)} %get-tuple-element.49), channel_id=1, source_target_pairs={{0,8},{4,12},{8,0},{12,4},{1,9},{5,13},{9,1},{13,5},{2,10},{6,14},... | collective-permute-start | bytes 718856 | tf_op jit(solution)/shard_map/ppermute | solution.py:272
  21.6 3.2 %load_up.1.up_ref = bf16[7168,512]{1,0:T(8,128)(2,1)S(1)} custom-call(bf16[7168,512]{1,0:T(8,128)(2,1)} %bitcast.6), custom_call_target="tpu_custom_call" | custom-call | bytes 14680064 | tf_op jit(solution)/shard_map/load_up/pallas_call | solution.py:106
  24.7 0.0 collective-permute-done.8
  24.8 0.0 collective-permute-done.7
  24.8 0.0 collective-permute-done.6
  24.8 1.3 %collective-permute-done.5 = bf16[24,4992]{1,0:T(8,128)(2,1)S(1)} collective-permute-done((bf16[24,4992]{1,0:T(8,128)(2,1)S(1)}, bf16[24,4992]{1,0:T(8,128)(2,1)S(1)}, u32[]{:S(2)}, u32[]{:S(2)}) %collective-permute-start.5) | collective-permute-done | bytes 239648 | tf_op jit(solution)/shard_map/ppermute | solution.py:272
  26.1 0.1 collective-permute-start.9
  26.2 0.6 collective-permute-start.10
  26.7 1.9 %collective-permute-done.10.b1_ref = bf16[64,2304]{1,0:T(8,128)(2,1)S(1)} collective-permute-done((bf16[64,2304]{1,0:T(8,128)(2,1)S(1)}, bf16[64,2304]{1,0:T(8,128)(2,1)S(1)}, u32[]{:S(2)}, u32[]{:S(2)}) %collective-permute-start.10) | collective-permute-done | bytes 294944 | tf_op jit(solution)/shard_map/ppermute | solution.py:272
  28.6 0.0 collective-permute-done.9.a1_ref
  28.6 5.8 %split_rows.1 = (bf16[64,4608]{1,0:T(8,128)(2,1)S(1)}, bf16[64,2560]{1,0:T(8,128)(2,1)S(1)}, bf16[64,4608]{1,0:T(8,128)(2,1)S(1)}, bf16[64,2560]{1,0:T(8,128)(2,1)S(1)}) custom-call(s32[1]{0:T(128)} %bitcast.place_ref, bf16[64,4992]{1,0:T(8,128)(2,1)S(1)} %constant_dynamic-update-slice_fusion.3.a0_ref, bf16[64,2304]{1,0:T(8,128)(2,1)S(1)} %pad_maximum_fusion.b0_ref, ...), custom_call_target="tpu_custom_call" | custom-call | tf_op jit(solution)/shard_map/split_rows/pallas_call | solution.py:213
  34.5 0.2 collective-permute-start.16
  34.7 0.4 collective-permute-start.11
  35.0 1.1 %collective-permute-done.16 = bf16[64,2560]{1,0:T(8,128)(2,1)S(1)} collective-permute-done((bf16[64,2560]{1,0:T(8,128)(2,1)S(1)}, bf16[64,2560]{1,0:T(8,128)(2,1)S(1)}, u32[]{:S(2)}, u32[]{:S(2)}) %collective-permute-start.16) | collective-permute-done | bytes 327712 | tf_op jit(solution)/shard_map/ppermute | solution.py:272
  36.2 0.1 add_convert_fusion.3
  36.2 3.8 %collective-permute-start.17 = (bf16[16,2560]{1,0:T(8,128)(2,1)S(1)}, bf16[16,2560]{1,0:T(8,128)(2,1)S(1)}, u32[]{:S(2)}, u32[]{:S(2)}) collective-permute-start(bf16[16,2560]{1,0:T(8,128)(2,1)S(1)} %get-tuple-element.41), channel_id=1, source_target_pairs={{0,3},{1,2},{2,1},{3,0},{4,7},{5,6},{6,5},{7,4},{8,11},{9,10},{10,... | collective-permute-start | bytes 245768 | tf_op jit(solution)/shard_map/ppermute | solution.py:272
  40.0 0.6 %collective-permute-start.18 = (bf16[16,2560]{1,0:T(8,128)(2,1)S(1)}, bf16[16,2560]{1,0:T(8,128)(2,1)S(1)}, u32[]{:S(2)}, u32[]{:S(2)}) collective-permute-start(bf16[16,2560]{1,0:T(8,128)(2,1)S(1)} %get-tuple-element.43), channel_id=1, source_target_pairs={{0,2},{1,3},{2,0},{3,1},{4,6},{5,7},{6,4},{7,5},{8,10},{9,11},{10,... | collective-permute-start | bytes 245768 | tf_op jit(solution)/shard_map/ppermute | solution.py:272
  40.7 0.1 add_convert_fusion
  40.8 1.7 %collective-permute-start.12 = (bf16[32,4608]{1,0:T(8,128)(2,1)S(1)}, bf16[32,4608]{1,0:T(8,128)(2,1)S(1)}, u32[]{:S(2)}, u32[]{:S(2)}) collective-permute-start(bf16[32,4608]{1,0:T(8,128)(2,1)S(1)} %add_convert_fusion), channel_id=1, source_target_pairs={{0,8},{4,12},{8,0},{12,4},{1,9},{5,13},{9,1},{13,5},{2,10},{6,14},... | collective-permute-start | bytes 884744 | tf_op jit(solution)/shard_map/ppermute | solution.py:272
  42.5 0.9 %collective-permute-done.17 = bf16[16,2560]{1,0:T(8,128)(2,1)S(1)} collective-permute-done((bf16[16,2560]{1,0:T(8,128)(2,1)S(1)}, bf16[16,2560]{1,0:T(8,128)(2,1)S(1)}, u32[]{:S(2)}, u32[]{:S(2)}) %collective-permute-start.17) | collective-permute-done | bytes 81952 | tf_op jit(solution)/shard_map/ppermute | solution.py:272
  43.4 2.8 %collective-permute-done.19 = bf16[16,2560]{1,0:T(8,128)(2,1)S(1)} collective-permute-done((bf16[16,2560]{1,0:T(8,128)(2,1)S(1)}, bf16[16,2560]{1,0:T(8,128)(2,1)S(1)}, u32[]{:S(2)}, u32[]{:S(2)}) %collective-permute-start.19) | collective-permute-done | bytes 81952 | tf_op jit(solution)/shard_map/ppermute | solution.py:272
  46.2 1.0 %collective-permute-done.18 = bf16[16,2560]{1,0:T(8,128)(2,1)S(1)} collective-permute-done((bf16[16,2560]{1,0:T(8,128)(2,1)S(1)}, bf16[16,2560]{1,0:T(8,128)(2,1)S(1)}, u32[]{:S(2)}, u32[]{:S(2)}) %collective-permute-start.18) | collective-permute-done | bytes 81952 | tf_op jit(solution)/shard_map/ppermute | solution.py:272
  47.1 0.1 convert_add_fusion.1
  47.2 1.6 %collective-permute-start.20 = (bf16[8,2560]{1,0:T(8,128)(2,1)S(1)}, bf16[8,2560]{1,0:T(8,128)(2,1)S(1)}, u32[]{:S(2)}, u32[]{:S(2)}) collective-permute-start(bf16[8,2560]{1,0:T(8,128)(2,1)S(1)} %slice.129), channel_id=1, source_target_pairs={{0,8},{4,12},{8,0},{12,4},{1,9},{5,13},{9,1},{13,5},{2,10},{6,14},... | collective-permute-start | bytes 122888 | tf_op jit(solution)/shard_map/ppermute | solution.py:272
  48.8 1.0 %collective-permute-done.12 = bf16[32,4608]{1,0:T(8,128)(2,1)S(1)} collective-permute-done((bf16[32,4608]{1,0:T(8,128)(2,1)S(1)}, bf16[32,4608]{1,0:T(8,128)(2,1)S(1)}, u32[]{:S(2)}, u32[]{:S(2)}) %collective-permute-start.12) | collective-permute-done | bytes 294944 | tf_op jit(solution)/shard_map/ppermute | solution.py:272
  49.8 0.1 fusion.4
  49.9 3.5 %collective-permute-start.13 = (bf16[8,4608]{1,0:T(8,128)(2,1)S(1)}, bf16[8,4608]{1,0:T(8,128)(2,1)S(1)}, u32[]{:S(2)}, u32[]{:S(2)}) collective-permute-start(bf16[8,4608]{1,0:T(8,128)(2,1)S(1)} %get-tuple-element.44), channel_id=1, source_target_pairs={{0,3},{1,2},{2,1},{3,0},{4,7},{5,6},{6,5},{7,4},{8,11},{9,10},{10,... | collective-permute-start | bytes 221192 | tf_op jit(solution)/shard_map/ppermute | solution.py:272
  53.4 0.9 %collective-permute-start.14 = (bf16[8,4608]{1,0:T(8,128)(2,1)S(1)}, bf16[8,4608]{1,0:T(8,128)(2,1)S(1)}, u32[]{:S(2)}, u32[]{:S(2)}) collective-permute-start(bf16[8,4608]{1,0:T(8,128)(2,1)S(1)} %get-tuple-element.46), channel_id=1, source_target_pairs={{0,2},{1,3},{2,0},{3,1},{4,6},{5,7},{6,4},{7,5},{8,10},{9,11},{10,... | collective-permute-start | bytes 221192 | tf_op jit(solution)/shard_map/ppermute | solution.py:272
  54.4 2.3 %collective-permute-done.13 = bf16[8,4608]{1,0:T(8,128)(2,1)S(1)} collective-permute-done((bf16[8,4608]{1,0:T(8,128)(2,1)S(1)}, bf16[8,4608]{1,0:T(8,128)(2,1)S(1)}, u32[]{:S(2)}, u32[]{:S(2)}) %collective-permute-start.13) | collective-permute-done | bytes 73760 | tf_op jit(solution)/shard_map/ppermute | solution.py:272
  56.7 2.2 %collective-permute-done.15 = bf16[8,4608]{1,0:T(8,128)(2,1)S(1)} collective-permute-done((bf16[8,4608]{1,0:T(8,128)(2,1)S(1)}, bf16[8,4608]{1,0:T(8,128)(2,1)S(1)}, u32[]{:S(2)}, u32[]{:S(2)}) %collective-permute-start.15) | collective-permute-done | bytes 73760 | tf_op jit(solution)/shard_map/ppermute | solution.py:272
  58.9 0.7 %pad_maximum_fusion.1 = bf16[8,7168]{1,0:T(8,128)(2,1)} fusion(bf16[8,2560]{1,0:T(8,128)(2,1)S(1)} %fusion.3, bf16[8,4608]{1,0:T(8,128)(2,1)S(1)} %fusion.2), kind=kLoop, calls=%fused_computation.11 | loop fusion | flops 229376 | bytes 229376 | tf_op jit(solution)/shard_map/concatenate | solution.py:350
  (19 shorter events, 0.2 us)
Async XLA Ops:
  0.0 15.3 %collective-permute-start = (bf16[8,7168]{1,0:T(8,128)(2,1)}, bf16[8,7168]{1,0:T(8,128)(2,1)S(1)}, u32[]{:S(2)}, u32[]{:S(2)}) collective-permute-start(bf16[8,7168]{1,0:T(8,128)(2,1)} %param.9), channel_id=1, source_target_pairs={{0,8},{4,12},{8,0},{12,4},{1,9},{5,13},{9,1},{13,5},{2,10},{6,14},... | collective-permute-start | bytes 344072 | tf_op jit(solution)/shard_map/ppermute | solution.py:272
  3.9 11.4 %collective-permute-start.4 = (bf16[8,4992]{1,0:T(8,128)(2,1)S(1)}, bf16[8,4992]{1,0:T(8,128)(2,1)S(1)}, u32[]{:S(2)}, u32[]{:S(2)}) collective-permute-start(bf16[8,4992]{1,0:T(8,128)(2,1)S(1)} %get-tuple-element.47), channel_id=1, source_target_pairs={{0,3},{1,2},{2,1},{3,0},{4,7},{5,6},{6,5},{7,4},{8,11},{9,10},{10,... | collective-permute-start | bytes 239624 | tf_op jit(solution)/shard_map/ppermute | solution.py:272
  7.5 7.7 %collective-permute-start.3 = (bf16[8,4992]{1,0:T(8,128)(2,1)S(1)}, bf16[8,4992]{1,0:T(8,128)(2,1)S(1)}, u32[]{:S(2)}, u32[]{:S(2)}) collective-permute-start(bf16[8,4992]{1,0:T(8,128)(2,1)S(1)} %get-tuple-element.47), channel_id=1, source_target_pairs={{0,2},{1,3},{2,0},{3,1},{4,6},{5,7},{6,4},{7,5},{8,10},{9,11},{10,... | collective-permute-start | bytes 239624 | tf_op jit(solution)/shard_map/ppermute | solution.py:272
  7.5 7.7 %collective-permute-start.2 = (bf16[8,4992]{1,0:T(8,128)(2,1)S(1)}, bf16[8,4992]{1,0:T(8,128)(2,1)S(1)}, u32[]{:S(2)}, u32[]{:S(2)}) collective-permute-start(bf16[8,4992]{1,0:T(8,128)(2,1)S(1)} %get-tuple-element.47), channel_id=1, source_target_pairs={{0,1},{1,0},{2,3},{3,2},{4,5},{5,4},{6,7},{7,6},{8,9},{9,8},{10,11... | collective-permute-start | bytes 239624 | tf_op jit(solution)/shard_map/ppermute | solution.py:272
  9.8 5.5 %collective-permute-start.1 = (bf16[8,128]{1,0:T(8,128)(2,1)}, bf16[8,128]{1,0:T(8,128)(2,1)S(1)}, u32[]{:S(2)}, u32[]{:S(2)}) collective-permute-start(bf16[8,128]{1,0:T(8,128)(2,1)} %dense_weights.1), channel_id=1, source_target_pairs={{0,8},{4,12},{8,0},{12,4},{1,9},{5,13},{9,1},{13,5},{2,10},{6,14},... | collective-permute-start | bytes 6152 | tf_op jit(solution)/shard_map/ppermute | solution.py:272
  10.9 4.4 %copy-start = (bf16[8,128]{1,0:T(8,128)(2,1)S(1)}, bf16[8,128]{1,0:T(8,128)(2,1)}, u32[]{:S(2)}) copy-start(bf16[8,128]{1,0:T(8,128)(2,1)} %dense_weights.1) | copy-start | bytes 6148
  15.3 9.4 %collective-permute-start.8 = (bf16[16,2304]{1,0:T(8,128)(2,1)S(1)}, bf16[16,2304]{1,0:T(8,128)(2,1)S(1)}, u32[]{:S(2)}, u32[]{:S(2)}) collective-permute-start(bf16[16,2304]{1,0:T(8,128)(2,1)S(1)} %maximum_maximum_fusion), channel_id=1, source_target_pairs={{0,3},{1,2},{2,1},{3,0},{4,7},{5,6},{6,5},{7,4},{8,11},{9,10},{10,... | collective-permute-start | bytes 221192 | tf_op jit(solution)/shard_map/ppermute | solution.py:272
  19.1 5.6 %collective-permute-start.7 = (bf16[16,2304]{1,0:T(8,128)(2,1)S(1)}, bf16[16,2304]{1,0:T(8,128)(2,1)S(1)}, u32[]{:S(2)}, u32[]{:S(2)}) collective-permute-start(bf16[16,2304]{1,0:T(8,128)(2,1)S(1)} %maximum_maximum_fusion), channel_id=1, source_target_pairs={{0,2},{1,3},{2,0},{3,1},{4,6},{5,7},{6,4},{7,5},{8,10},{9,11},{10,... | collective-permute-start | bytes 221192 | tf_op jit(solution)/shard_map/ppermute | solution.py:272
  19.2 5.6 %collective-permute-start.6 = (bf16[16,2304]{1,0:T(8,128)(2,1)S(1)}, bf16[16,2304]{1,0:T(8,128)(2,1)S(1)}, u32[]{:S(2)}, u32[]{:S(2)}) collective-permute-start(bf16[16,2304]{1,0:T(8,128)(2,1)S(1)} %maximum_maximum_fusion), channel_id=1, source_target_pairs={{0,1},{1,0},{2,3},{3,2},{4,5},{5,4},{6,7},{7,6},{8,9},{9,8},{10,11... | collective-permute-start | bytes 221192 | tf_op jit(solution)/shard_map/ppermute | solution.py:272
  19.9 6.2 %collective-permute-start.5 = (bf16[24,4992]{1,0:T(8,128)(2,1)S(1)}, bf16[24,4992]{1,0:T(8,128)(2,1)S(1)}, u32[]{:S(2)}, u32[]{:S(2)}) collective-permute-start(bf16[24,4992]{1,0:T(8,128)(2,1)S(1)} %get-tuple-element.49), channel_id=1, source_target_pairs={{0,8},{4,12},{8,0},{12,4},{1,9},{5,13},{9,1},{13,5},{2,10},{6,14},... | collective-permute-start | bytes 718856 | tf_op jit(solution)/shard_map/ppermute | solution.py:272
  26.1 2.6 %collective-permute-start.9 = (bf16[64,4992]{1,0:T(8,128)(2,1)S(1)}, bf16[64,4992]{1,0:T(8,128)(2,1)S(1)}, u32[]{:S(2)}, u32[]{:S(2)}) collective-permute-start(bf16[64,4992]{1,0:T(8,128)(2,1)S(1)} %constant_dynamic-update-slice_fusion.3.a0_ref), channel_id=1, source_target_pairs={{0,4},{4,0},{8,12},{12,8},{1,5},{5,1},{9,13},{13,9},{2,6},{6,2},{1... | collective-permute-start | bytes 1916936 | tf_op jit(solution)/shard_map/ppermute | solution.py:272
  26.2 2.5 %collective-permute-start.10 = (bf16[64,2304]{1,0:T(8,128)(2,1)S(1)}, bf16[64,2304]{1,0:T(8,128)(2,1)S(1)}, u32[]{:S(2)}, u32[]{:S(2)}) collective-permute-start(bf16[64,2304]{1,0:T(8,128)(2,1)S(1)} %pad_maximum_fusion.b0_ref), channel_id=1, source_target_pairs={{0,4},{4,0},{8,12},{12,8},{1,5},{5,1},{9,13},{13,9},{2,6},{6,2},{1... | collective-permute-start | bytes 884744 | tf_op jit(solution)/shard_map/ppermute | solution.py:272
  34.5 1.7 %collective-permute-start.16 = (bf16[64,2560]{1,0:T(8,128)(2,1)S(1)}, bf16[64,2560]{1,0:T(8,128)(2,1)S(1)}, u32[]{:S(2)}, u32[]{:S(2)}) collective-permute-start(bf16[64,2560]{1,0:T(8,128)(2,1)S(1)} %get-tuple-element.38), channel_id=1, source_target_pairs={{0,4},{4,0},{8,12},{12,8},{1,5},{5,1},{9,13},{13,9},{2,6},{6,2},{1... | collective-permute-start | bytes 983048 | tf_op jit(solution)/shard_map/ppermute | solution.py:272
  34.7 6.0 %collective-permute-start.11 = (bf16[64,4608]{1,0:T(8,128)(2,1)S(1)}, bf16[64,4608]{1,0:T(8,128)(2,1)S(1)}, u32[]{:S(2)}, u32[]{:S(2)}) collective-permute-start(bf16[64,4608]{1,0:T(8,128)(2,1)S(1)} %get-tuple-element.36), channel_id=1, source_target_pairs={{0,4},{4,0},{8,12},{12,8},{1,5},{5,1},{9,13},{13,9},{2,6},{6,2},{1... | collective-permute-start | bytes 1769480 | tf_op jit(solution)/shard_map/ppermute | solution.py:272
  36.2 7.2 %collective-permute-start.17 = (bf16[16,2560]{1,0:T(8,128)(2,1)S(1)}, bf16[16,2560]{1,0:T(8,128)(2,1)S(1)}, u32[]{:S(2)}, u32[]{:S(2)}) collective-permute-start(bf16[16,2560]{1,0:T(8,128)(2,1)S(1)} %get-tuple-element.41), channel_id=1, source_target_pairs={{0,3},{1,2},{2,1},{3,0},{4,7},{5,6},{6,5},{7,4},{8,11},{9,10},{10,... | collective-permute-start | bytes 245768 | tf_op jit(solution)/shard_map/ppermute | solution.py:272
  40.0 6.1 %collective-permute-start.19 = (bf16[16,2560]{1,0:T(8,128)(2,1)S(1)}, bf16[16,2560]{1,0:T(8,128)(2,1)S(1)}, u32[]{:S(2)}, u32[]{:S(2)}) collective-permute-start(bf16[16,2560]{1,0:T(8,128)(2,1)S(1)} %get-tuple-element.42), channel_id=1, source_target_pairs={{0,1},{1,0},{2,3},{3,2},{4,5},{5,4},{6,7},{7,6},{8,9},{9,8},{10,11... | collective-permute-start | bytes 245768 | tf_op jit(solution)/shard_map/ppermute | solution.py:272
  40.0 7.1 %collective-permute-start.18 = (bf16[16,2560]{1,0:T(8,128)(2,1)S(1)}, bf16[16,2560]{1,0:T(8,128)(2,1)S(1)}, u32[]{:S(2)}, u32[]{:S(2)}) collective-permute-start(bf16[16,2560]{1,0:T(8,128)(2,1)S(1)} %get-tuple-element.43), channel_id=1, source_target_pairs={{0,2},{1,3},{2,0},{3,1},{4,6},{5,7},{6,4},{7,5},{8,10},{9,11},{10,... | collective-permute-start | bytes 245768 | tf_op jit(solution)/shard_map/ppermute | solution.py:272
  40.8 9.0 %collective-permute-start.12 = (bf16[32,4608]{1,0:T(8,128)(2,1)S(1)}, bf16[32,4608]{1,0:T(8,128)(2,1)S(1)}, u32[]{:S(2)}, u32[]{:S(2)}) collective-permute-start(bf16[32,4608]{1,0:T(8,128)(2,1)S(1)} %add_convert_fusion), channel_id=1, source_target_pairs={{0,8},{4,12},{8,0},{12,4},{1,9},{5,13},{9,1},{13,5},{2,10},{6,14},... | collective-permute-start | bytes 884744 | tf_op jit(solution)/shard_map/ppermute | solution.py:272
  47.2 7.1 %collective-permute-start.20 = (bf16[8,2560]{1,0:T(8,128)(2,1)S(1)}, bf16[8,2560]{1,0:T(8,128)(2,1)S(1)}, u32[]{:S(2)}, u32[]{:S(2)}) collective-permute-start(bf16[8,2560]{1,0:T(8,128)(2,1)S(1)} %slice.129), channel_id=1, source_target_pairs={{0,8},{4,12},{8,0},{12,4},{1,9},{5,13},{9,1},{13,5},{2,10},{6,14},... | collective-permute-start | bytes 122888 | tf_op jit(solution)/shard_map/ppermute | solution.py:272
  49.9 6.8 %collective-permute-start.13 = (bf16[8,4608]{1,0:T(8,128)(2,1)S(1)}, bf16[8,4608]{1,0:T(8,128)(2,1)S(1)}, u32[]{:S(2)}, u32[]{:S(2)}) collective-permute-start(bf16[8,4608]{1,0:T(8,128)(2,1)S(1)} %get-tuple-element.44), channel_id=1, source_target_pairs={{0,3},{1,2},{2,1},{3,0},{4,7},{5,6},{6,5},{7,4},{8,11},{9,10},{10,... | collective-permute-start | bytes 221192 | tf_op jit(solution)/shard_map/ppermute | solution.py:272
  53.4 5.4 %collective-permute-start.15 = (bf16[8,4608]{1,0:T(8,128)(2,1)S(1)}, bf16[8,4608]{1,0:T(8,128)(2,1)S(1)}, u32[]{:S(2)}, u32[]{:S(2)}) collective-permute-start(bf16[8,4608]{1,0:T(8,128)(2,1)S(1)} %get-tuple-element.45), channel_id=1, source_target_pairs={{0,1},{1,0},{2,3},{3,2},{4,5},{5,4},{6,7},{7,6},{8,9},{9,8},{10,11... | collective-permute-start | bytes 221192 | tf_op jit(solution)/shard_map/ppermute | solution.py:272
  53.4 5.4 %collective-permute-start.14 = (bf16[8,4608]{1,0:T(8,128)(2,1)S(1)}, bf16[8,4608]{1,0:T(8,128)(2,1)S(1)}, u32[]{:S(2)}, u32[]{:S(2)}) collective-permute-start(bf16[8,4608]{1,0:T(8,128)(2,1)S(1)} %get-tuple-element.46), channel_id=1, source_target_pairs={{0,2},{1,3},{2,0},{3,1},{4,6},{5,7},{6,4},{7,5},{8,10},{9,11},{10,... | collective-permute-start | bytes 221192 | tf_op jit(solution)/shard_map/ppermute | solution.py:272

commit v5 on v0

v5 whole, which is shorter than its diff:
```python
import functools

import jax
import jax.numpy as jnp
from jax import lax
from jax.experimental import pallas as pl
from jax.experimental.pallas import tpu as pltpu
from jax.sharding import PartitionSpec as P

LANES = 128
ROW_BLOCK = 128
F32 = jnp.float32
BF16 = jnp.bfloat16
VMEM_SPEC = pl.BlockSpec(memory_space=pltpu.VMEM)
SMEM_SPEC = pl.BlockSpec(memory_space=pltpu.SMEM)
ANY_SPEC = pl.BlockSpec(memory_space=pl.ANY)


def in_hbm(value):
    return pltpu.with_memory_space_constraint(value, pltpu.HBM)


def run_copies(copies):
    for copy in copies:
        copy.start()
    for copy in copies:
        copy.wait()


def after(value, *done):
    return lax.optimization_barrier((value, *done))[0]


def pack_kernel(tokens_ref, groups_ref, weights_ref, packed_ref, tail_ref):
    rows, width = tokens_ref.shape
    packed_ref[:, :width] = tokens_ref[...]
    tail_ref[...] = tokens_ref[:, width - tail_ref.shape[1] :]
    groups = groups_ref[...].T
    weights = weights_ref[...].astype(F32).T
    lane = lax.broadcasted_iota(jnp.int32, (rows, LANES), 1)
    dense = jnp.zeros((rows, LANES), F32)
    for k in range(groups.shape[1]):
        dense += jnp.where(lane == groups[:, k : k + 1], weights[:, k : k + 1], 0.0)
    packed_ref[:, width:] = dense.astype(BF16)


def pack_rows(tokens, group_ids, route_weights, tail):
    rows, width = tokens.shape
    return pl.pallas_call(
        pack_kernel,
        out_specs=[VMEM_SPEC] * 2,
        out_shape=[pltpu.VMEM((rows, width + LANES), BF16), pltpu.VMEM((rows, tail), BF16)],
        name="pack_rows",
    )(tokens, group_ids.T, route_weights.T)


def load_kernel(weight_ref, out_ref, sems):
    parts = sems.shape[0]
    piece = weight_ref.shape[0] // parts
    run_copies(
        [
            pltpu.make_async_copy(
                weight_ref.at[pl.ds(i * piece, piece), :], out_ref.at[pl.ds(i * piece, piece), :], sems.at[i]
            )
            for i in range(parts)
        ]
    )


def load_weight(weight):
    return pl.pallas_call(
        load_kernel,
        in_specs=[ANY_SPEC],
        out_specs=VMEM_SPEC,
        out_shape=pltpu.VMEM(weight.shape, BF16),
        scratch_shapes=[pltpu.SemaphoreType.DMA((8,))],
        cost_estimate=pl.CostEstimate(flops=0, bytes_accessed=4 * weight.size, transcendentals=0),
        compiler_params=pltpu.CompilerParams(vmem_limit_bytes=1 << 20),
        name="load_weight",
    )(in_hbm(weight))


def silu(v):
    return v / (1.0 + jnp.exp(-v))


def activate(share, node, x, gate_ref, up_ref, weight, act):
    width, hidden = up_ref.shape
    tile = min(2 * LANES, hidden)
    for at in range(0, hidden, tile):
        gate = jnp.dot(x, gate_ref[:, at : at + tile], preferred_element_type=F32)
        up = jnp.dot(x, up_ref[:, at : at + tile], preferred_element_type=F32)
        act[:, at : at + tile] = (silu(gate) * up * weight).astype(BF16)


def activate_shared(share, node, x, first_shared, act):
    both = jnp.dot(x, first_shared[...], preferred_element_type=F32)
    shared = silu(both[:, :LANES]) * both[:, LANES:]
    if share > 1:
        lane = lax.broadcasted_iota(jnp.int32, shared.shape, 1)
        shared = jnp.where(lane // (LANES // share) == node % share, shared, 0.0)
    act[:, act.shape[1] - LANES :] = shared.astype(BF16)


def row_weight(node, dense):
    lane = lax.broadcasted_iota(jnp.int32, dense.shape, 1)
    return jnp.sum(jnp.where(lane == node, dense.astype(F32), 0.0), axis=1, keepdims=True)


DOWN_PARTS = 4


def weight_copies(share, place_ref, sgate_ref, sup_ref, down_ref, sdown_ref, first_shared, second, sems):
    hidden, width = down_ref.shape
    column = pl.multiple_of((place_ref[0] // share) * LANES, LANES)
    own = pl.ds(column, LANES)
    pairs = [
        (sgate_ref.at[:, own], first_shared.at[:, pl.ds(0, LANES)]),
        (sup_ref.at[:, own], first_shared.at[:, pl.ds(LANES, LANES)]),
    ]
    piece = width // DOWN_PARTS
    for i in range(DOWN_PARTS):
        at = pl.ds(i * piece, piece)
        pairs.append((down_ref.at[:, at], second.at[pl.ds(0, hidden), at]))
        pairs.append((sdown_ref.at[own, at], second.at[pl.ds(hidden, LANES), at]))
    return [pltpu.make_async_copy(a, b, sems.at[i]) for i, (a, b) in enumerate(pairs)]


def weight_scratch(hidden, width):
    return [
        pltpu.VMEM((width, 2 * LANES), BF16),
        pltpu.VMEM((hidden + LANES, width), BF16),
        pltpu.SemaphoreType.DMA((2 + 2 * DOWN_PARTS,)),
    ]


def split_kernel(
    share, place_ref, b0_ref, a0_ref, b1_ref, a1_ref, gate_ref, up_ref, sgate_ref, sup_ref, down_ref, sdown_ref,
    own_b_ref, own_a_ref, other_b_ref, other_a_ref, x, act, first_shared, second, sems,
):
    copies = weight_copies(
        share, place_ref, sgate_ref, sup_ref, down_ref, sdown_ref, first_shared, second, sems
    )
    for copy in copies:
        copy.start()
    width = up_ref.shape[0]
    half = a0_ref.shape[0]
    cut = width - a0_ref.shape[1]
    group, eighth = half // 4, half // 8
    for c, (b_ref, a_ref) in enumerate(((b0_ref, a0_ref), (b1_ref, a1_ref))):
        a = a_ref[...].astype(F32)
        for k in range(4):
            rows = pl.ds(pl.multiple_of(c * half + (place_ref[1] ^ k) * group, group), group)
            pair = [a[x_at * 4 * eighth + k * eighth :][:eighth] for x_at in range(2)]
            x[rows, cut:width] = jnp.concatenate(pair, axis=0).astype(BF16)
            x[rows, :cut] = b_ref[k * group : (k + 1) * group, :cut]
            x[rows, width:] = b_ref[k * group : (k + 1) * group, cut:]
    node = place_ref[0]
    weight = row_weight(node, x[:, width:])
    activate(share, node, x[:, :width], gate_ref, up_ref, weight, act)
    copies[0].wait()
    copies[1].wait()
    activate_shared(share, node, x[:, :width], first_shared, act)
    piece = width // DOWN_PARTS
    cut = own_b_ref.shape[1]
    for i in range(DOWN_PARTS):
        copies[2 + 2 * i].wait()
        copies[3 + 2 * i].wait()
        lower, upper = i * piece, (i + 1) * piece
        for at, to in ((lower, min(upper, cut)), (max(lower, cut), upper)):
            if at >= to:
                continue
            total = jnp.dot(act[...], second[:, at:to], preferred_element_type=F32)
            if to <= cut:
                own_b_ref[:, at:to] = total[:half].astype(BF16)
                other_b_ref[:, at:to] = total[half:].astype(BF16)
            else:
                own_a_ref[:, at - cut : to - cut] = total[:half].astype(BF16)
                other_a_ref[:, at - cut : to - cut] = total[half:].astype(BF16)


def split_rows(place, pieces, gate, up, sgate, sup, down, sdown, cut, share):
    half = pieces[0].shape[0]
    hidden, width = down.shape
    out_b = jax.ShapeDtypeStruct((half, cut), BF16)
    out_a = jax.ShapeDtypeStruct((half, width - cut), BF16)
    return pl.pallas_call(
        functools.partial(split_kernel, share),
        in_specs=[SMEM_SPEC] + [VMEM_SPEC] * 6 + [ANY_SPEC] * 4,
        out_specs=[VMEM_SPEC] * 4,
        out_shape=[out_b, out_a] * 2,
        scratch_shapes=[
            pltpu.VMEM((2 * half, width + LANES), BF16),
            pltpu.VMEM((2 * half, hidden + LANES), BF16),
        ]
        + weight_scratch(hidden, width),
        compiler_params=pltpu.CompilerParams(vmem_limit_bytes=30 << 20),
        name="split_rows",
    )(place, *pieces, gate, up, *(in_hbm(w) for w in (sgate, sup, down, sdown)))


def block_kernel(
    share, place_ref, x_ref, gate_ref, up_ref, sgate_ref, sup_ref, down_ref, sdown_ref,
    out_ref, act, first_shared, second, sems,
):
    copies = weight_copies(
        share, place_ref, sgate_ref, sup_ref, down_ref, sdown_ref, first_shared, second, sems
    )

    @pl.when(pl.program_id(0) == 0)
    def _():
        run_copies(copies)

    width = up_ref.shape[0]
    node = place_ref[0]
    weight = row_weight(node, x_ref[:, width:])
    x = x_ref[:, :width]
    activate(share, node, x, gate_ref, up_ref, weight, act)
    activate_shared(share, node, x, first_shared, act)
    piece = width // DOWN_PARTS
    for i in range(DOWN_PARTS):
        at = slice(i * piece, (i + 1) * piece)
        out_ref[:, at] = jnp.dot(act[...], second[:, at], preferred_element_type=F32).astype(BF16)


def block_rows(place, x, gate, up, sgate, sup, down, sdown, share):
    rows, packed = x.shape
    hidden, width = down.shape
    block = min(rows, ROW_BLOCK)
    return pl.pallas_call(
        functools.partial(block_kernel, share),
        grid=(rows // block,),
        in_specs=[SMEM_SPEC, pl.BlockSpec((block, packed), lambda i: (i, 0))] + [VMEM_SPEC] * 2 + [ANY_SPEC] * 4,
        out_specs=pl.BlockSpec((block, width), lambda i: (i, 0)),
        out_shape=jax.ShapeDtypeStruct((rows, width), BF16),
        scratch_shapes=[pltpu.VMEM((block, hidden + LANES), BF16)] + weight_scratch(hidden, width),
        compiler_params=pltpu.CompilerParams(vmem_limit_bytes=30 << 20),
        name="block_rows",
    )(place, x, gate, up, *(in_hbm(w) for w in (sgate, sup, down, sdown)))


def f32_sum(*terms):
    return functools.reduce(lambda a, b: a + b, (t.astype(F32) for t in terms))


def swap(value, axis, bit):
    return lax.ppermute(value, axis, [(i, i ^ bit) for i in range(4)])


swap_x = functools.partial(swap, axis="node", bit=2)
swap_core = functools.partial(swap, axis="node", bit=1)


def swap_z(value, k):
    return swap(value, "local", k)


def stack(*values):
    return jnp.concatenate(values, axis=0)


def per_device(
    tokens,
    group_ids,
    route_weights,
    gate_experts,
    up_experts,
    down_experts,
    gate_shared,
    up_shared,
    down_shared,
):
    rows, width = tokens.shape
    node_count = lax.axis_size("node")
    local_count = lax.axis_size("local")
    share = max(1, LANES * node_count // gate_shared.shape[1])
    place = jnp.stack([lax.axis_index("node"), lax.axis_index("local")])
    gate, up, down = gate_experts[0], up_experts[0], down_experts[0]
    rest = (gate_shared, up_shared, down, down_shared)
    cut = width * 17 // 56 // LANES * LANES
    packed, a = pack_rows(tokens, group_ids, route_weights, width - cut)

    if node_count != 4 or local_count != 4:
        x = lax.all_gather(packed, ("node", "local"), axis=0, tiled=True)
        part = block_rows(place, x, load_weight(gate), load_weight(up), *rest, share)
        return lax.psum_scatter(part, ("node", "local"), scatter_dimension=0, tiled=True)

    steps = (3, 2, 1)
    across = swap_x(packed)
    got = {k: swap_z(a, k) for k in steps}
    gate = load_weight(after(gate, a))
    got[1], gate = lax.optimization_barrier((got[1], gate))
    near_across = swap_x(got[1])
    across, got[2], got[3], gate = lax.optimization_barrier((across, got[2], got[3], gate))
    b = stack(packed, across)
    b = jnp.concatenate([b[:, :cut], b[:, width:]], axis=1)
    b_got = {k: swap_z(b, k) for k in steps}
    far = stack(got[2], got[3])
    far_across = swap_x(far)
    up = load_weight(after(up, far, b))
    b_got, far_across, up = lax.optimization_barrier((b_got, far_across, up))
    a = stack(a, got[1], far, across[:, cut:width], near_across, far_across)
    b = stack(b, b_got[1], b_got[2], b_got[3])
    pieces = (b, a, swap_core(b), swap_core(a))

    cut = width * 20 // 56 // LANES * LANES
    own_b, own_a, other_b, other_a = split_rows(place, pieces, gate, up, *rest, cut, share)

    def by_place(value):
        return value.reshape(4, 2, rows, -1)

    def exchange(value):
        return f32_sum(*lax.all_to_all(value.astype(BF16), "local", 0, 0))

    b_got = swap_core(other_b)
    a_got = swap_core(other_a)
    b_got = after(b_got, a_got)
    own_a, a_got = by_place(own_a), by_place(a_got)
    a_cross = swap_x(f32_sum(own_a[:, 1], a_got[:, 1]).astype(BF16))
    b_sum = exchange(by_place(f32_sum(own_b, b_got)))
    b = f32_sum(b_sum[0], swap_x(b_sum[1].astype(BF16)))
    a = exchange(f32_sum(own_a[:, 0], a_got[:, 0], a_cross))
    return jnp.concatenate([b.astype(BF16), a.astype(BF16)], axis=1)


def solution(mesh):
    in_specs = (
        P(("rep", "node", "local"), None),
        P(("rep", "node", "local"), None),
        P(("rep", "node", "local"), None),
        P("node", None, "local"),
        P("node", None, "local"),
        P("node", "local", None),
        P(None, "local"),
        P(None, "local"),
        P("local", None),
    )
    out_specs = P(("rep", "node", "local"), None)
    return jax.shard_map(
        per_device, mesh=mesh, in_specs=in_specs, out_specs=out_specs, check_vma=False
    )
```

time: 176 us -> 75.9 us (0.43)
  blocking collectives: 103 us -> 0 us
  matrix products: 26 us -> 0 us
  starting transfers between devices: 3.75 us -> 23.8 us
  Pallas kernels: 0 us -> 16 us
  between operations: 13.5 us -> 0.21 us
  local copies, waits for them, and re-layouts: 6.33 us -> 12.3 us
    all_gather x1 -> x0, blocking collectives: 52.3 us -> none  [per_device(): lax.all_gather(tokens, 'local', axis=0, tiled=True)]
    all_to_all x1 -> x0, blocking collectives: 51 us -> none  [per_device(): lax.all_to_all(outgoing, ('node', 'local'), split_axis=0, concat_axis=0,...]
    dot_general x4 -> x0, matrix products: 26 us -> none  [the longest x1 8.68 us: per_device(): jnp.dot(shared_act, down_shared, preferred_element_type=jnp.float32)]
    reduce_scatter x1 -> x0, waiting for transfers between devices: 19.6 us -> none  [per_device(): lax.psum_scatter(jnp.dot(shared_act, down_shared, preferred_element_type=...]
    all_to_all x1 -> x2, waiting for transfers between devices: 0.01 us -> 16.9 us  [exchange(): return f32_sum(*lax.all_to_all(value.astype(BF16), 'local', 0, 0))]
    ppermute x0 -> x15, starting transfers between devices: none -> 16.1 us  [swap(): return lax.ppermute(value, axis, [(i, i ^ bit) for i in range(4)])]
    pallas_call x0 -> x4, Pallas kernels: none -> 16 us  [the longest x1 8.58 us: split_rows(): pl.pallas_call(functools.partial(split_kernel, share), in_specs=[SMEM_SPE...]
    unnamed x5 -> x15, local copies, waits for them, and re-layouts: 0.77 us -> 12.2 us
  transfers between devices with their start and end apart: 2 -> 17, of which waited for: 1 -> 4; matrix products, arithmetic and copies ran while one was open for 9% -> 2% of each run, Pallas kernels for 0% -> 8%
where the time goes in v5:
time: 75.9 us; the launch traced here: 75.5 us
  starting transfers between devices  23.8 us (31%)
  waiting for transfers between devices  20.7 us (27%)
  Pallas kernels  16 us (21%)
  local copies, waits for them, and re-layouts  12.3 us (16%)
  other arithmetic  2.56 us (3%)
    all_to_all x2, waiting for transfers between devices, exchange(): return f32_sum(*lax.all_to_all(value.astype(BF16), 'local', 0, 0))  16.9 us
    ppermute x15, starting transfers between devices, swap(): return lax.ppermute(value, axis, [(i, i ^ bit) for i in range(4)])  16.1 us
    unnamed x15, local copies, waits for them, and re-layouts  12.2 us
    pallas_call x1, Pallas kernels, split_rows(): pl.pallas_call(functools.partial(split_kernel, share), in_specs=[SMEM_SPE...  8.58 us
    all_to_all x2, starting transfers between devices, exchange(): return f32_sum(*lax.all_to_all(value.astype(BF16), 'local', 0, 0))  7.64 us
    pallas_call x2, Pallas kernels, load_weight(): pl.pallas_call(load_kernel, in_specs=[ANY_SPEC], out_specs=VMEM_SPEC, out...  6.34 us
    ppermute x15, waiting for transfers between devices, swap(): return lax.ppermute(value, axis, [(i, i ^ bit) for i in range(4)])  3.82 us
    convert_element_type x2, other arithmetic, exchange(): return f32_sum(*lax.all_to_all(value.astype(BF16), 'local', 0, 0))  1.63 us
  transfers between devices with their start and end apart: 17, of which 4 were waited for; matrix products, arithmetic and copies ran while one was open for 2% of the time, Pallas kernels for 8%

profile of v5, /device:TPU:0, one launch (start us, length us, event | category | flops | bytes accessed | tf_op | source)
XLA Modules:
  0.0 75.5 jit_solution(17938580814326856660)
XLA Ops:
  0.0 1.1 %pack_rows.1 = (bf16[8,7296]{1,0:T(8,128)(2,1)S(1)}, bf16[8,4992]{1,0:T(8,128)(2,1)S(1)}) custom-call(bf16[8,7168]{1,0:T(8,128)(2,1)} %tokens_ref.1, s32[4,8]{1,0:T(4,128)} %bitcast.49, bf16[4,8]{1,0:T(4,128)(2,1)} %bitcast.50), custom_call_target="tpu_custom_call" | custom-call | tf_op jit(solution)/shard_map/pack_rows/pallas_call | solution.py:49
  1.1 3.1 %collective-permute-start.3 = (bf16[8,4992]{1,0:T(8,128)(2,1)S(1)}, bf16[8,4992]{1,0:T(8,128)(2,1)S(1)}, u32[]{:S(2)}, u32[]{:S(2)}) collective-permute-start(bf16[8,4992]{1,0:T(8,128)(2,1)S(1)} %get-tuple-element.26), channel_id=1, source_target_pairs={{0,1},{1,0},{2,3},{3,2},{4,5},{5,4},{6,7},{7,6},{8,9},{9,8},{10,11... | collective-permute-start | bytes 239624 | tf_op jit(solution)/shard_map/ppermute | solution.py:247
  4.2 2.5 %collective-permute-start.2 = (bf16[8,4992]{1,0:T(8,128)(2,1)S(1)}, bf16[8,4992]{1,0:T(8,128)(2,1)S(1)}, u32[]{:S(2)}, u32[]{:S(2)}) collective-permute-start(bf16[8,4992]{1,0:T(8,128)(2,1)S(1)} %get-tuple-element.26), channel_id=1, source_target_pairs={{0,3},{1,2},{2,1},{3,0},{4,7},{5,6},{6,5},{7,4},{8,11},{9,10},{10,... | collective-permute-start | bytes 239624 | tf_op jit(solution)/shard_map/ppermute | solution.py:247
  6.6 0.1 collective-permute-start.1
  6.8 1.5 %collective-permute-start = (bf16[8,7296]{1,0:T(8,128)(2,1)S(1)}, bf16[8,7296]{1,0:T(8,128)(2,1)S(1)}, u32[]{:S(2)}, u32[]{:S(2)}) collective-permute-start(bf16[8,7296]{1,0:T(8,128)(2,1)S(1)} %get-tuple-element.25), channel_id=1, source_target_pairs={{0,8},{4,12},{8,0},{12,4},{1,9},{5,13},{9,1},{13,5},{2,10},{6,14},... | collective-permute-start | bytes 350216 | tf_op jit(solution)/shard_map/ppermute | solution.py:247
  8.3 3.2 %load_weight.2.gate_ref = bf16[7168,512]{1,0:T(8,128)(2,1)S(1)} custom-call(bf16[7168,512]{1,0:T(8,128)(2,1)} %bitcast.44), custom_call_target="tpu_custom_call" | custom-call | bytes 14680064 | tf_op jit(solution)/shard_map/load_weight/pallas_call | solution.py:71
  11.5 0.0 copy-start
  11.5 2.9 %copy-done = bf16[7168,512]{1,0:T(8,128)(2,1)} copy-done((bf16[7168,512]{1,0:T(8,128)(2,1)}, bf16[7168,512]{1,0:T(8,128)(2,1)S(1)}, u32[]{:S(2)}) %copy-start) | copy-done | bytes 7340056
  14.4 0.0 collective-permute-done.3
  14.4 0.5 collective-permute-start.8
  15.0 0.0 collective-permute-done.2
  15.0 0.0 collective-permute-done.1
  15.0 0.0 collective-permute-done
  15.0 3.0 %collective-permute-start.6 = (bf16[16,2304]{1,0:T(8,128)(2,1)S(1)}, bf16[16,2304]{1,0:T(8,128)(2,1)S(1)}, u32[]{:S(2)}, u32[]{:S(2)}) collective-permute-start(bf16[16,2304]{1,0:T(8,128)(2,1)S(1)} %pad_maximum_fusion.2), channel_id=1, source_target_pairs={{0,3},{1,2},{2,1},{3,0},{4,7},{5,6},{6,5},{7,4},{8,11},{9,10},{10,... | collective-permute-start | bytes 221192 | tf_op jit(solution)/shard_map/ppermute | solution.py:247
  18.0 0.3 collective-permute-start.5
  18.4 1.1 %collective-permute-start.4 = (bf16[16,2304]{1,0:T(8,128)(2,1)S(1)}, bf16[16,2304]{1,0:T(8,128)(2,1)S(1)}, u32[]{:S(2)}, u32[]{:S(2)}) collective-permute-start(bf16[16,2304]{1,0:T(8,128)(2,1)S(1)} %pad_maximum_fusion.2), channel_id=1, source_target_pairs={{0,1},{1,0},{2,3},{3,2},{4,5},{5,4},{6,7},{7,6},{8,9},{9,8},{10,11... | collective-permute-start | bytes 221192 | tf_op jit(solution)/shard_map/ppermute | solution.py:247
  19.6 1.6 %collective-permute-start.7 = (bf16[16,4992]{1,0:T(8,128)(2,1)S(1)}, bf16[16,4992]{1,0:T(8,128)(2,1)S(1)}, u32[]{:S(2)}, u32[]{:S(2)}) collective-permute-start(bf16[16,4992]{1,0:T(8,128)(2,1)S(1)} %get-tuple-element.46), channel_id=1, source_target_pairs={{0,8},{4,12},{8,0},{12,4},{1,9},{5,13},{9,1},{13,5},{2,10},{6,14},... | collective-permute-start | bytes 479240 | tf_op jit(solution)/shard_map/ppermute | solution.py:247
  21.1 3.2 %load_weight.3.up_ref = bf16[7168,512]{1,0:T(8,128)(2,1)S(1)} custom-call(bf16[7168,512]{1,0:T(8,128)(2,1)} %bitcast.45), custom_call_target="tpu_custom_call" | custom-call | bytes 14680064 | tf_op jit(solution)/shard_map/load_weight/pallas_call | solution.py:71
  24.3 3.0 %copy-done.2 = bf16[7168,512]{1,0:T(8,128)(2,1)} copy-done((bf16[7168,512]{1,0:T(8,128)(2,1)}, bf16[7168,512]{1,0:T(8,128)(2,1)S(1)}, u32[]{:S(2)}) %copy-start.2) | copy-done | bytes 7340056
  27.3 0.0 collective-permute-done.8
  27.3 0.0 collective-permute-done.6
  27.3 0.0 collective-permute-done.5
  27.3 0.0 collective-permute-done.4
  27.3 0.0 collective-permute-done.7
  27.4 0.1 collective-permute-start.10
  27.5 0.6 collective-permute-start.9
  28.0 0.1 pad_add_fusion.place_ref
  28.1 1.8 %collective-permute-done.9.b1_ref = bf16[64,2304]{1,0:T(8,128)(2,1)S(1)} collective-permute-done((bf16[64,2304]{1,0:T(8,128)(2,1)S(1)}, bf16[64,2304]{1,0:T(8,128)(2,1)S(1)}, u32[]{:S(2)}, u32[]{:S(2)}) %collective-permute-start.9) | collective-permute-done | bytes 294944 | tf_op jit(solution)/shard_map/ppermute | solution.py:247
  29.9 0.0 collective-permute-done.10.a1_ref
  29.9 3.1 %copy-done.1 = bf16[7168,512]{1,0:T(8,128)(2,1)S(1)} copy-done((bf16[7168,512]{1,0:T(8,128)(2,1)S(1)}, bf16[7168,512]{1,0:T(8,128)(2,1)}, u32[]{:S(2)}) %copy-start.1) | copy-done | bytes 7340056
  33.0 3.1 %copy-done.3 = bf16[7168,512]{1,0:T(8,128)(2,1)S(1)} copy-done((bf16[7168,512]{1,0:T(8,128)(2,1)S(1)}, bf16[7168,512]{1,0:T(8,128)(2,1)}, u32[]{:S(2)}) %copy-start.3) | copy-done | bytes 7340056
  36.1 8.6 %split_rows.1 = (bf16[64,2560]{1,0:T(8,128)(2,1)S(1)}, bf16[64,4608]{1,0:T(8,128)(2,1)S(1)}, bf16[64,2560]{1,0:T(8,128)(2,1)S(1)}, bf16[64,4608]{1,0:T(8,128)(2,1)S(1)}) custom-call(s32[2]{0:T(128)S(1)} %pad_add_fusion.place_ref, bf16[64,2304]{1,0:T(8,128)(2,1)S(1)} %pad_maximum_fusion.b0_ref, ...), custom_call_target="tpu_custom_call" | custom-call | tf_op jit(solution)/shard_map/split_rows/pallas_call | solution.py:187
  44.7 0.2 collective-permute-start.12
  44.9 0.4 collective-permute-start.11
  45.3 2.0 %collective-permute-done.11 = bf16[64,2560]{1,0:T(8,128)(2,1)S(1)} collective-permute-done((bf16[64,2560]{1,0:T(8,128)(2,1)S(1)}, bf16[64,2560]{1,0:T(8,128)(2,1)S(1)}, u32[]{:S(2)}, u32[]{:S(2)}) %collective-permute-start.11) | collective-permute-done | bytes 327712 | tf_op jit(solution)/shard_map/ppermute | solution.py:247
  47.2 0.0 collective-permute-done.12
  47.2 0.8 %add_convert_fusion = bf16[64,2560]{1,0:T(8,128)(2,1)} fusion(bf16[64,2560]{1,0:T(8,128)(2,1)S(1)} %collective-permute-done.11, bf16[64,2560]{1,0:T(8,128)(2,1)S(1)} %get-tuple-element.40), kind=kLoop, calls=%fused_computation | loop fusion | flops 655360 | bytes 983040 | tf_op jit(solution)/shard_map/convert_element_type | solution.py:313
  48.1 4.2 %all-to-all-start = ((bf16[4,2,8,2560]{3,2,1,0:T(8,128)(2,1)}), bf16[4,2,8,2560]{3,2,1,0:T(8,128)(2,1)S(1)}, u32[]{:S(2)}, u32[]{:S(2)}) async-start(bf16[4,2,8,2560]{3,2,1,0:T(8,128)(2,1)} %bitcast.7), calls=%async_computation | async-start | bytes 655360 | tf_op jit(solution)/shard_map/all_to_all | solution.py:313
  52.3 0.1 fusion.1
  52.3 0.6 collective-permute-start.14
  52.9 10.0 %all-to-all-done = bf16[4,2,8,2560]{3,2,1,0:T(8,128)(2,1)S(1)} async-done(((bf16[4,2,8,2560]{3,2,1,0:T(8,128)(2,1)}), bf16[4,2,8,2560]{3,2,1,0:T(8,128)(2,1)S(1)}, u32[]{:S(2)}, u32[]{:S(2)}) %all-to-all-start) | async-done | bytes 327712 | tf_op jit(solution)/shard_map/all_to_all | solution.py:313
  62.9 0.6 collective-permute-start.13
  63.5 0.0 collective-permute-done.14
  63.5 0.8 %fusion = bf16[4,8,4608]{2,1,0:T(8,128)(2,1)} fusion(bf16[4,8,4608]{2,1,0:T(8,128)(2,1)S(1)} %collective-permute-done.14, bf16[4,2,8,4608]{3,2,1,0:T(8,128)(2,1)S(1)} %bitcast.48, bf16[4,2,8,4608]{3,2,1,0:T(8,128)(2,1)S(1)} %bitcast.43), kind=kLoop, calls=%fused_computation.2 | loop fusion | flops 884736 | bytes 1179648 | tf_op jit(solution)/shard_map/convert_element_type | solution.py:313
  64.4 3.5 %all-to-all-start.1 = ((bf16[4,8,4608]{2,1,0:T(8,128)(2,1)}), bf16[4,8,4608]{2,1,0:T(8,128)(2,1)S(1)}, u32[]{:S(2)}, u32[]{:S(2)}) async-start(bf16[4,8,4608]{2,1,0:T(8,128)(2,1)} %fusion), calls=%async_computation.1 | async-start | bytes 589824 | tf_op jit(solution)/shard_map/all_to_all | solution.py:313
  67.8 0.0 collective-permute-done.13
  67.8 7.0 %all-to-all-done.1 = bf16[4,8,4608]{2,1,0:T(8,128)(2,1)S(1)} async-done(((bf16[4,8,4608]{2,1,0:T(8,128)(2,1)}), bf16[4,8,4608]{2,1,0:T(8,128)(2,1)S(1)}, u32[]{:S(2)}, u32[]{:S(2)}) %all-to-all-start.1) | async-done | bytes 294944 | tf_op jit(solution)/shard_map/all_to_all | solution.py:313
  74.9 0.7 pad_maximum_fusion.1
  (20 shorter events, 0.3 us)
Async XLA Ops:
  1.1 13.3 %collective-permute-start.3 = (bf16[8,4992]{1,0:T(8,128)(2,1)S(1)}, bf16[8,4992]{1,0:T(8,128)(2,1)S(1)}, u32[]{:S(2)}, u32[]{:S(2)}) collective-permute-start(bf16[8,4992]{1,0:T(8,128)(2,1)S(1)} %get-tuple-element.26), channel_id=1, source_target_pairs={{0,1},{1,0},{2,3},{3,2},{4,5},{5,4},{6,7},{7,6},{8,9},{9,8},{10,11... | collective-permute-start | bytes 239624 | tf_op jit(solution)/shard_map/ppermute | solution.py:247
  4.2 10.8 %collective-permute-start.2 = (bf16[8,4992]{1,0:T(8,128)(2,1)S(1)}, bf16[8,4992]{1,0:T(8,128)(2,1)S(1)}, u32[]{:S(2)}, u32[]{:S(2)}) collective-permute-start(bf16[8,4992]{1,0:T(8,128)(2,1)S(1)} %get-tuple-element.26), channel_id=1, source_target_pairs={{0,3},{1,2},{2,1},{3,0},{4,7},{5,6},{6,5},{7,4},{8,11},{9,10},{10,... | collective-permute-start | bytes 239624 | tf_op jit(solution)/shard_map/ppermute | solution.py:247
  6.6 8.3 %collective-permute-start.1 = (bf16[8,4992]{1,0:T(8,128)(2,1)S(1)}, bf16[8,4992]{1,0:T(8,128)(2,1)S(1)}, u32[]{:S(2)}, u32[]{:S(2)}) collective-permute-start(bf16[8,4992]{1,0:T(8,128)(2,1)S(1)} %get-tuple-element.26), channel_id=1, source_target_pairs={{0,2},{1,3},{2,0},{3,1},{4,6},{5,7},{6,4},{7,5},{8,10},{9,11},{10,... | collective-permute-start | bytes 239624 | tf_op jit(solution)/shard_map/ppermute | solution.py:247
  6.8 8.2 %collective-permute-start = (bf16[8,7296]{1,0:T(8,128)(2,1)S(1)}, bf16[8,7296]{1,0:T(8,128)(2,1)S(1)}, u32[]{:S(2)}, u32[]{:S(2)}) collective-permute-start(bf16[8,7296]{1,0:T(8,128)(2,1)S(1)} %get-tuple-element.25), channel_id=1, source_target_pairs={{0,8},{4,12},{8,0},{12,4},{1,9},{5,13},{9,1},{13,5},{2,10},{6,14},... | collective-permute-start | bytes 350216 | tf_op jit(solution)/shard_map/ppermute | solution.py:247
  11.5 2.9 %copy-start = (bf16[7168,512]{1,0:T(8,128)(2,1)}, bf16[7168,512]{1,0:T(8,128)(2,1)S(1)}, u32[]{:S(2)}) copy-start(bf16[7168,512]{1,0:T(8,128)(2,1)S(1)} %load_weight.2.gate_ref) | copy-start | bytes 22020100
  14.4 12.9 %collective-permute-start.8 = (bf16[8,4992]{1,0:T(8,128)(2,1)S(1)}, bf16[8,4992]{1,0:T(8,128)(2,1)S(1)}, u32[]{:S(2)}, u32[]{:S(2)}) collective-permute-start(bf16[8,4992]{1,0:T(8,128)(2,1)S(1)} %collective-permute-done.3), channel_id=1, source_target_pairs={{0,8},{4,12},{8,0},{12,4},{1,9},{5,13},{9,1},{13,5},{2,10},{6,14},... | collective-permute-start | bytes 239624 | tf_op jit(solution)/shard_map/ppermute | solution.py:247
  15.0 12.3 %collective-permute-start.6 = (bf16[16,2304]{1,0:T(8,128)(2,1)S(1)}, bf16[16,2304]{1,0:T(8,128)(2,1)S(1)}, u32[]{:S(2)}, u32[]{:S(2)}) collective-permute-start(bf16[16,2304]{1,0:T(8,128)(2,1)S(1)} %pad_maximum_fusion.2), channel_id=1, source_target_pairs={{0,3},{1,2},{2,1},{3,0},{4,7},{5,6},{6,5},{7,4},{8,11},{9,10},{10,... | collective-permute-start | bytes 221192 | tf_op jit(solution)/shard_map/ppermute | solution.py:247
  18.0 9.3 %collective-permute-start.5 = (bf16[16,2304]{1,0:T(8,128)(2,1)S(1)}, bf16[16,2304]{1,0:T(8,128)(2,1)S(1)}, u32[]{:S(2)}, u32[]{:S(2)}) collective-permute-start(bf16[16,2304]{1,0:T(8,128)(2,1)S(1)} %pad_maximum_fusion.2), channel_id=1, source_target_pairs={{0,2},{1,3},{2,0},{3,1},{4,6},{5,7},{6,4},{7,5},{8,10},{9,11},{10,... | collective-permute-start | bytes 221192 | tf_op jit(solution)/shard_map/ppermute | solution.py:247
  18.4 9.0 %collective-permute-start.4 = (bf16[16,2304]{1,0:T(8,128)(2,1)S(1)}, bf16[16,2304]{1,0:T(8,128)(2,1)S(1)}, u32[]{:S(2)}, u32[]{:S(2)}) collective-permute-start(bf16[16,2304]{1,0:T(8,128)(2,1)S(1)} %pad_maximum_fusion.2), channel_id=1, source_target_pairs={{0,1},{1,0},{2,3},{3,2},{4,5},{5,4},{6,7},{7,6},{8,9},{9,8},{10,11... | collective-permute-start | bytes 221192 | tf_op jit(solution)/shard_map/ppermute | solution.py:247
  19.6 7.8 %collective-permute-start.7 = (bf16[16,4992]{1,0:T(8,128)(2,1)S(1)}, bf16[16,4992]{1,0:T(8,128)(2,1)S(1)}, u32[]{:S(2)}, u32[]{:S(2)}) collective-permute-start(bf16[16,4992]{1,0:T(8,128)(2,1)S(1)} %get-tuple-element.46), channel_id=1, source_target_pairs={{0,8},{4,12},{8,0},{12,4},{1,9},{5,13},{9,1},{13,5},{2,10},{6,14},... | collective-permute-start | bytes 479240 | tf_op jit(solution)/shard_map/ppermute | solution.py:247
  24.3 3.0 %copy-start.2 = (bf16[7168,512]{1,0:T(8,128)(2,1)}, bf16[7168,512]{1,0:T(8,128)(2,1)S(1)}, u32[]{:S(2)}) copy-start(bf16[7168,512]{1,0:T(8,128)(2,1)S(1)} %load_weight.3.up_ref) | copy-start | bytes 22020100
  27.4 2.6 %collective-permute-start.10 = (bf16[64,4992]{1,0:T(8,128)(2,1)S(1)}, bf16[64,4992]{1,0:T(8,128)(2,1)S(1)}, u32[]{:S(2)}, u32[]{:S(2)}) collective-permute-start(bf16[64,4992]{1,0:T(8,128)(2,1)S(1)} %constant_dynamic-update-slice_fusion.4.a0_ref), channel_id=1, source_target_pairs={{0,4},{4,0},{8,12},{12,8},{1,5},{5,1},{9,13},{13,9},{2,6},{6,2},{1... | collective-permute-start | bytes 1916936 | tf_op jit(solution)/shard_map/ppermute | solution.py:247
  27.5 2.5 %collective-permute-start.9 = (bf16[64,2304]{1,0:T(8,128)(2,1)S(1)}, bf16[64,2304]{1,0:T(8,128)(2,1)S(1)}, u32[]{:S(2)}, u32[]{:S(2)}) collective-permute-start(bf16[64,2304]{1,0:T(8,128)(2,1)S(1)} %pad_maximum_fusion.b0_ref), channel_id=1, source_target_pairs={{0,4},{4,0},{8,12},{12,8},{1,5},{5,1},{9,13},{13,9},{2,6},{6,2},{1... | collective-permute-start | bytes 884744 | tf_op jit(solution)/shard_map/ppermute | solution.py:247
  29.9 3.1 %copy-start.1 = (bf16[7168,512]{1,0:T(8,128)(2,1)S(1)}, bf16[7168,512]{1,0:T(8,128)(2,1)}, u32[]{:S(2)}) copy-start(bf16[7168,512]{1,0:T(8,128)(2,1)} %copy-done) | copy-start | bytes 22020100
  33.0 3.1 %copy-start.3 = (bf16[7168,512]{1,0:T(8,128)(2,1)S(1)}, bf16[7168,512]{1,0:T(8,128)(2,1)}, u32[]{:S(2)}) copy-start(bf16[7168,512]{1,0:T(8,128)(2,1)} %copy-done.2) | copy-start | bytes 22020100
  44.7 2.5 %collective-permute-start.12 = (bf16[64,4608]{1,0:T(8,128)(2,1)S(1)}, bf16[64,4608]{1,0:T(8,128)(2,1)S(1)}, u32[]{:S(2)}, u32[]{:S(2)}) collective-permute-start(bf16[64,4608]{1,0:T(8,128)(2,1)S(1)} %get-tuple-element.42), channel_id=1, source_target_pairs={{0,4},{4,0},{8,12},{12,8},{1,5},{5,1},{9,13},{13,9},{2,6},{6,2},{1... | collective-permute-start | bytes 1769480 | tf_op jit(solution)/shard_map/ppermute | solution.py:247
  44.9 2.3 %collective-permute-start.11 = (bf16[64,2560]{1,0:T(8,128)(2,1)S(1)}, bf16[64,2560]{1,0:T(8,128)(2,1)S(1)}, u32[]{:S(2)}, u32[]{:S(2)}) collective-permute-start(bf16[64,2560]{1,0:T(8,128)(2,1)S(1)} %get-tuple-element.41), channel_id=1, source_target_pairs={{0,4},{4,0},{8,12},{12,8},{1,5},{5,1},{9,13},{13,9},{2,6},{6,2},{1... | collective-permute-start | bytes 983048 | tf_op jit(solution)/shard_map/ppermute | solution.py:247
  48.1 14.8 %all-to-all-start = ((bf16[4,2,8,2560]{3,2,1,0:T(8,128)(2,1)}), bf16[4,2,8,2560]{3,2,1,0:T(8,128)(2,1)S(1)}, u32[]{:S(2)}, u32[]{:S(2)}) async-start(bf16[4,2,8,2560]{3,2,1,0:T(8,128)(2,1)} %bitcast.7), calls=%async_computation | async-start | bytes 655360 | tf_op jit(solution)/shard_map/all_to_all | solution.py:313
  52.3 11.2 %collective-permute-start.14 = (bf16[4,8,4608]{2,1,0:T(8,128)(2,1)S(1)}, bf16[4,8,4608]{2,1,0:T(8,128)(2,1)S(1)}, u32[]{:S(2)}, u32[]{:S(2)}) collective-permute-start(bf16[4,8,4608]{2,1,0:T(8,128)(2,1)S(1)} %fusion.1), channel_id=1, source_target_pairs={{0,8},{4,12},{8,0},{12,4},{1,9},{5,13},{9,1},{13,5},{2,10},{6,14},... | collective-permute-start | bytes 884744 | tf_op jit(solution)/shard_map/ppermute | solution.py:247
  62.9 4.9 %collective-permute-start.13 = (bf16[8,2560]{1,0:T(8,128)(2,1)S(1)}, bf16[8,2560]{1,0:T(8,128)(2,1)S(1)}, u32[]{:S(2)}, u32[]{:S(2)}) collective-permute-start(bf16[8,2560]{1,0:T(8,128)(2,1)S(1)} %fusion.5), channel_id=1, source_target_pairs={{0,8},{4,12},{8,0},{12,4},{1,9},{5,13},{9,1},{13,5},{2,10},{6,14},... | collective-permute-start | bytes 122888 | tf_op jit(solution)/shard_map/ppermute | solution.py:247
  64.4 10.5 %all-to-all-start.1 = ((bf16[4,8,4608]{2,1,0:T(8,128)(2,1)}), bf16[4,8,4608]{2,1,0:T(8,128)(2,1)S(1)}, u32[]{:S(2)}, u32[]{:S(2)}) async-start(bf16[4,8,4608]{2,1,0:T(8,128)(2,1)} %fusion), calls=%async_computation.1 | async-start | bytes 589824 | tf_op jit(solution)/shard_map/all_to_all | solution.py:313

commit v6 on v4

--- a/solution.py
+++ b/solution.py
@@ -31,31 +31,32 @@
     return lax.optimization_barrier((value, *done))[0]
 
 
-def shared_column(place_ref, share):
-    return pl.multiple_of((place_ref[0] // share) * LANES, LANES)
-
-
-def dense_kernel(groups_ref, weights_ref, out_ref):
+def pack_kernel(tokens_ref, groups_ref, weights_ref, packed_ref, tail_ref):
+    rows, width = tokens_ref.shape
+    packed_ref[:, :width] = tokens_ref[...]
+    tail_ref[...] = tokens_ref[:, width - tail_ref.shape[1] :]
     groups = groups_ref[...].T
     weights = weights_ref[...].astype(F32).T
-    lane = lax.broadcasted_iota(jnp.int32, out_ref.shape, 1)
-    dense = jnp.zeros(out_ref.shape, F32)
+    lane = lax.broadcasted_iota(jnp.int32, (rows, LANES), 1)
+    dense = jnp.zeros((rows, LANES), F32)
     for k in range(groups.shape[1]):
         dense += jnp.where(lane == groups[:, k : k + 1], weights[:, k : k + 1], 0.0)
-    out_ref[...] = dense.astype(BF16)
-
-
-def dense_weights(group_ids, route_weights):
-    return pl.pallas_call(
-        dense_kernel,
-        out_shape=jax.ShapeDtypeStruct((group_ids.shape[0], LANES), BF16),
-        name="dense_weights",
-    )(group_ids.T, route_weights.T)
+    packed_ref[:, width:] = dense.astype(BF16)
+
+
+def pack_rows(tokens, group_ids, route_weights, tail):
+    rows, width = tokens.shape
+    return pl.pallas_call(
+        pack_kernel,
+        out_specs=[VMEM_SPEC] * 2,
+        out_shape=[pltpu.VMEM((rows, width + LANES), BF16), pltpu.VMEM((rows, tail), BF16)],
+        name="pack_rows",
+    )(tokens, group_ids.T, route_weights.T)
 
 
 def load_gate_kernel(share, place_ref, gate_ref, sgate_ref, sup_ref, out_ref, sems):
     width, hidden = gate_ref.shape
-    column = shared_column(place_ref, share)
+    column = pl.multiple_of((place_ref[0] // share) * LANES, LANES)
     parts = 4
     piece = width // parts
     copies = []
@@ -139,13 +140,15 @@
     return jnp.sum(jnp.where(lane == node, dense.astype(F32), 0.0), axis=1, keepdims=True)
 
 
+DOWN_PARTS = 4
+
+
 def down_copies(share, place_ref, down_ref, sdown_ref, second, sems):
     hidden, width = down_ref.shape
-    column = shared_column(place_ref, share)
-    parts = 4
-    piece = width // parts
+    column = pl.multiple_of((place_ref[0] // share) * LANES, LANES)
+    piece = width // DOWN_PARTS
     copies = []
-    for i in range(parts):
+    for i in range(DOWN_PARTS):
         at = pl.ds(i * piece, piece)
         copies.append(
             pltpu.make_async_copy(down_ref.at[:, at], second.at[pl.ds(0, hidden), at], sems.at[2 * i])
@@ -158,6 +161,14 @@
     return copies
 
 
+def down_scratch(rows, hidden, width):
+    return [
+        pltpu.VMEM((rows, hidden + LANES), BF16),
+        pltpu.VMEM((hidden + LANES, width), BF16),
+        pltpu.SemaphoreType.DMA((2 * DOWN_PARTS,)),
+    ]
+
+
 def regroup(value, outer, inner):
     rows = value.shape[0] // (outer * inner)
     return jnp.concatenate(
@@ -171,25 +182,27 @@
 
 
 def split_kernel(
-    share, place_ref, a0_ref, b0_ref, a1_ref, b1_ref, first_ref, up_ref, down_ref, sdown_ref,
-    own_a_ref, own_b_ref, other_a_ref, other_b_ref, x, act, second, sems,
+    share, place_ref, b0_ref, a0_ref, b1_ref, a1_ref, first_ref, up_ref, down_ref, sdown_ref,
+    own_b_ref, own_a_ref, other_b_ref, other_a_ref, x, act, second, sems,
 ):
     copies = down_copies(share, place_ref, down_ref, sdown_ref, second, sems)
     for copy in copies:
         copy.start()
     width = up_ref.shape[0]
-    half, cut = a0_ref.shape
-    for c, (a_ref, b_ref) in enumerate(((a0_ref, b0_ref), (a1_ref, b1_ref))):
+    half = a0_ref.shape[0]
+    cut = width - a0_ref.shape[1]
+    for c, (b_ref, a_ref) in enumerate(((b0_ref, a0_ref), (b1_ref, a1_ref))):
         rows = slice(c * half, (c + 1) * half)
-        x[rows, :cut] = a_ref[...]
-        x[rows, cut:] = regroup(b_ref[...].astype(F32), 4, 2).astype(BF16)
+        b = regroup(b_ref[...].astype(F32), 4, 2).astype(BF16)
+        x[rows, :cut] = b[:, :cut]
+        x[rows, cut:width] = a_ref[...]
+        x[rows, width:] = b[:, cut:]
     node = place_ref[0]
     weight = row_weight(node, x[:, width:])
     activate(share, node, x[:, :width], first_ref, up_ref, weight, act)
-    parts = len(copies) // 2
-    piece = width // parts
-    cut = own_a_ref.shape[1]
-    for i in range(parts):
+    piece = width // DOWN_PARTS
+    cut = own_b_ref.shape[1]
+    for i in range(DOWN_PARTS):
         copies[2 * i].wait()
         copies[2 * i + 1].wait()
         lower, upper = i * piece, (i + 1) * piece
@@ -198,29 +211,24 @@
                 continue
             total = jnp.dot(act[...], second[:, at:to], preferred_element_type=F32)
             if to <= cut:
-                own_a_ref[:, at:to] = total[:half].astype(BF16)
-                other_a_ref[:, at:to] = total[half:].astype(BF16)
+                own_b_ref[:, at:to] = regroup(total[:half], 2, 4).astype(BF16)
+                other_b_ref[:, at:to] = regroup(total[half:], 2, 4).astype(BF16)
             else:
-                own_b_ref[:, at - cut : to - cut] = regroup(total[:half], 2, 4).astype(BF16)
-                other_b_ref[:, at - cut : to - cut] = regroup(total[half:], 2, 4).astype(BF16)
+                own_a_ref[:, at - cut : to - cut] = total[:half].astype(BF16)
+                other_a_ref[:, at - cut : to - cut] = total[half:].astype(BF16)
 
 
 def split_rows(place, pieces, first, up, down, sdown, cut, share):
     half = pieces[0].shape[0]
     hidden, width = down.shape
-    out_a = jax.ShapeDtypeStruct((half, cut), BF16)
-    out_b = jax.ShapeDtypeStruct((half, width - cut), BF16)
+    out_b = jax.ShapeDtypeStruct((half, cut), BF16)
+    out_a = jax.ShapeDtypeStruct((half, width - cut), BF16)
     return pl.pallas_call(
         functools.partial(split_kernel, share),
         in_specs=[SMEM_SPEC] + [VMEM_SPEC] * 6 + [ANY_SPEC] * 2,
         out_specs=[VMEM_SPEC] * 4,
-        out_shape=[out_a, out_b] * 2,
-        scratch_shapes=[
-            pltpu.VMEM((2 * half, width + LANES), BF16),
-            pltpu.VMEM((2 * half, hidden + LANES), BF16),
-            pltpu.VMEM((hidden + LANES, width), BF16),
-            pltpu.SemaphoreType.DMA((8,)),
-        ],
+        out_shape=[out_b, out_a] * 2,
+        scratch_shapes=[pltpu.VMEM((2 * half, width + LANES), BF16)] + down_scratch(2 * half, hidden, width),
         compiler_params=pltpu.CompilerParams(vmem_limit_bytes=28 << 20),
         name="split_rows",
     )(place, *pieces, first, up, in_hbm(down), in_hbm(sdown))
@@ -237,9 +245,8 @@
     node = place_ref[0]
     weight = row_weight(node, x_ref[:, width:])
     activate(share, node, x_ref[:, :width], first_ref, up_ref, weight, act)
-    parts = 4
-    piece = width // parts
-    for i in range(parts):
+    piece = width // DOWN_PARTS
+    for i in range(DOWN_PARTS):
         at = slice(i * piece, (i + 1) * piece)
         out_ref[:, at] = jnp.dot(act[...], second[:, at], preferred_element_type=F32).astype(BF16)
 
@@ -254,11 +261,7 @@
         in_specs=[SMEM_SPEC, pl.BlockSpec((block, packed), lambda i: (i, 0))] + [VMEM_SPEC] * 2 + [ANY_SPEC] * 2,
         out_specs=pl.BlockSpec((block, width), lambda i: (i, 0)),
         out_shape=jax.ShapeDtypeStruct((rows, width), BF16),
-        scratch_shapes=[
-            pltpu.VMEM((block, hidden + LANES), BF16),
-            pltpu.VMEM((hidden + LANES, width), BF16),
-            pltpu.SemaphoreType.DMA((8,)),
-        ],
+        scratch_shapes=down_scratch(block, hidden, width),
         compiler_params=pltpu.CompilerParams(vmem_limit_bytes=28 << 20),
         name="block_rows",
     )(place, x, first, up, in_hbm(down), in_hbm(sdown))
@@ -301,53 +304,52 @@
     share = max(1, LANES * node_count // gate_shared.shape[1])
     place = lax.axis_index("node").reshape(1)
     gate, up, down = gate_experts[0], up_experts[0], down_experts[0]
-    dense = dense_weights(group_ids, route_weights)
+    cut = width * 17 // 56 // LANES * LANES
+    packed, a = pack_rows(tokens, group_ids, route_weights, width - cut)
 
     if node_count != 4 or local_count != 4:
+        x = lax.all_gather(packed, ("node", "local"), axis=0, tiled=True)
         first = load_gate(place, gate, gate_shared, up_shared, share)
-        up = load_up(up)
-        x = lax.all_gather(
-            jnp.concatenate([tokens, dense], axis=1), ("node", "local"), axis=0, tiled=True
-        )
-        part = block_rows(place, x, first, up, down, down_shared, share)
+        part = block_rows(place, x, first, load_up(up), down, down_shared, share)
         return lax.psum_scatter(part, ("node", "local"), scatter_dimension=0, tiled=True)
 
-    steps = (3, 2, 1)
-    cut = width * 39 // 56 // LANES * LANES
-    across = swap_x(tokens)
-    a = tokens[:, :cut]
+    steps = (1, 2, 3)
+    across = swap_x(packed)
     got = {k: swap_z(a, k) for k in steps}
-    dense_across = swap_x(dense)
-    first = load_gate(after(place, dense), gate, gate_shared, up_shared, share)
-    across, dense_across, got, first = lax.optimization_barrier((across, dense_across, got, first))
-    far = stack(got[1], got[2], got[3])
-    b = jnp.concatenate(
-        [stack(tokens[:, cut:], across[:, cut:]), stack(dense, dense_across)], axis=1
-    )
+    first = load_gate(after(place, a), gate, gate_shared, up_shared, share)
+    got[1], first = lax.optimization_barrier((got[1], first))
+    far = {1: swap_x(got[1])}
+    got[2] = after(got[2], got[1])
+    far[2] = swap_x(got[2])
+    got[3] = after(got[3], got[2])
+    far[3] = swap_x(got[3])
+    b = stack(packed, across)
+    b = jnp.concatenate([b[:, :cut], b[:, width:]], axis=1)
+    b = after(b, got[3])
     b_got = {k: swap_z(b, k) for k in steps}
-    far_across = swap_x(far)
-    up = load_up(after(up, far, b))
-    far_across, b_got, up = lax.optimization_barrier((far_across, b_got, up))
-    a = stack(a, far, across[:, :cut], far_across)
+    up = load_up(after(up, got[3], b))
+    far, b_got, up = lax.optimization_barrier((far, b_got, up))
+    a = stack(a, got[1], got[2], got[3], across[:, cut:width], far[1], far[2], far[3])
     b = stack(b, b_got[1], b_got[2], b_got[3])
-    pieces = (a, b, swap_core(a), swap_core(b))
-
-    cut = width * 36 // 56 // LANES * LANES
-    own_a, own_b, other_a, other_b = split_rows(place, pieces, first, up, down, down_shared, cut, share)
+    pieces = (b, a, swap_core(b), swap_core(a))
+
+    cut = width * 20 // 56 // LANES * LANES
+    own_b, own_a, other_b, other_a = split_rows(place, pieces, first, up, down, down_shared, cut, share)
 
     four, two = 4 * rows, 2 * rows
     a_got = swap_core(other_a)
-    b_got = swap_core(other_b)
-    a_sum = f32_sum(own_a[:four], a_got[:four], swap_x(f32_sum(own_a[four:], a_got[four:]).astype(BF16)))
-    b_sum = f32_sum(own_b[:two], b_got[:two])
-    for k in steps:
-        at = slice(k * two, (k + 1) * two)
-        b_sum = f32_sum(b_sum, swap_z(f32_sum(own_b[at], b_got[at]).astype(BF16), k))
-    a = a_sum[:rows]
-    for k in steps:
-        a = f32_sum(a, swap_z(a_sum[k * rows : (k + 1) * rows].astype(BF16), k))
+    a_cross = swap_x(f32_sum(own_a[four:], a_got[four:]).astype(BF16))
+    b_got = swap_core(after(other_b, a_got))
+    b_far = [
+        swap_z(f32_sum(own_b[k * two : (k + 1) * two], b_got[k * two : (k + 1) * two]).astype(BF16), k)
+        for k in steps
+    ]
+    a_cross, b_far = lax.optimization_barrier((a_cross, b_far))
+    a_sum = f32_sum(own_a[:four], a_got[:four], a_cross)
+    a = f32_sum(a_sum[:rows], *(swap_z(a_sum[k * rows : (k + 1) * rows].astype(BF16), k) for k in steps))
+    b_sum = f32_sum(own_b[:two], b_got[:two], *b_far)
     b = f32_sum(b_sum[:rows], swap_x(b_sum[rows:].astype(BF16)))
-    return jnp.concatenate([a.astype(BF16), b.astype(BF16)], axis=1)
+    return jnp.concatenate([b.astype(BF16), a.astype(BF16)], axis=1)
 
 
 def solution(mesh):

time: 59.8 us -> 60 us (level)
  waiting for transfers between devices: 14.5 us -> 17.5 us
  local copies, waits for them, and re-layouts: 1.82 us -> 0.18 us
  starting transfers between devices: 27.3 us -> 26.4 us
    ppermute x21 -> x22, waiting for transfers between devices: 14.5 us -> 17.5 us  [swap(): return lax.ppermute(value, axis, [(i, i ^ bit) for i in range(4)])]
    slice x4 -> x3, local copies, waits for them, and re-layouts: 1.72 us -> 0.03 us  [the longest x1 0.02 us: per_device(): a_sum[k * rows:(k + 1) * rows].astype(BF16)]
    ppermute x21 -> x22, starting transfers between devices: 27.3 us -> 26.4 us  [swap(): return lax.ppermute(value, axis, [(i, i ^ bit) for i in range(4)])]
  transfers between devices with their start and end apart: 21 -> 22, of which waited for: 9 -> 9; matrix products, arithmetic and copies ran while one was open for 4% -> 1% of each run, Pallas kernels for 15% -> 12%
where the time goes in v6:
time: 60 us; the launch traced here: 59.9 us
  starting transfers between devices  26.4 us (44%)
  waiting for transfers between devices  17.5 us (29%)
  Pallas kernels  14.6 us (24%)
  other arithmetic  1 us (2%)
    ppermute x22, starting transfers between devices, swap(): return lax.ppermute(value, axis, [(i, i ^ bit) for i in range(4)])  26.4 us
    ppermute x22, waiting for transfers between devices, swap(): return lax.ppermute(value, axis, [(i, i ^ bit) for i in range(4)])  17.5 us
    pallas_call x1, Pallas kernels, split_rows(): pl.pallas_call(functools.partial(split_kernel, share), in_specs=[SMEM_SPE...  6.07 us
    pallas_call x1, Pallas kernels, load_gate(): pl.pallas_call(functools.partial(load_gate_kernel, share), in_specs=[SMEM...  4.32 us
    pallas_call x1, Pallas kernels, load_up(): pl.pallas_call(load_up_kernel, in_specs=[ANY_SPEC], out_specs=VMEM_SPEC,...  3.17 us
  transfers between devices with their start and end apart: 22, of which 9 were waited for; matrix products, arithmetic and copies ran while one was open for 1% of the time, Pallas kernels for 12%

profile of v6, /device:TPU:0, one launch (start us, length us, event | category | flops | bytes accessed | tf_op | source)
XLA Modules:
  0.0 59.9 jit_solution(1804563047969320801)
XLA Ops:
  0.0 1.1 %pack_rows.1 = (bf16[8,7296]{1,0:T(8,128)(2,1)S(1)}, bf16[8,4992]{1,0:T(8,128)(2,1)S(1)}) custom-call(bf16[8,7168]{1,0:T(8,128)(2,1)} %tokens_ref.1, s32[4,8]{1,0:T(4,128)} %bitcast.9, bf16[4,8]{1,0:T(4,128)(2,1)} %bitcast.10), custom_call_target="tpu_custom_call" | custom-call | tf_op jit(solution)/shard_map/pack_rows/pallas_call | solution.py:49
  1.1 3.1 %collective-permute-start.3 = (bf16[8,4992]{1,0:T(8,128)(2,1)S(1)}, bf16[8,4992]{1,0:T(8,128)(2,1)S(1)}, u32[]{:S(2)}, u32[]{:S(2)}) collective-permute-start(bf16[8,4992]{1,0:T(8,128)(2,1)S(1)} %get-tuple-element.31), channel_id=1, source_target_pairs={{0,1},{1,0},{2,3},{3,2},{4,5},{5,4},{6,7},{7,6},{8,9},{9,8},{10,11... | collective-permute-start | bytes 239624 | tf_op jit(solution)/shard_map/ppermute | solution.py:275
  4.2 2.6 %collective-permute-start.2 = (bf16[8,4992]{1,0:T(8,128)(2,1)S(1)}, bf16[8,4992]{1,0:T(8,128)(2,1)S(1)}, u32[]{:S(2)}, u32[]{:S(2)}) collective-permute-start(bf16[8,4992]{1,0:T(8,128)(2,1)S(1)} %get-tuple-element.31), channel_id=1, source_target_pairs={{0,2},{1,3},{2,0},{3,1},{4,6},{5,7},{6,4},{7,5},{8,10},{9,11},{10,... | collective-permute-start | bytes 239624 | tf_op jit(solution)/shard_map/ppermute | solution.py:275
  6.8 0.0 collective-permute-start.1
  6.8 1.7 %collective-permute-start = (bf16[8,7296]{1,0:T(8,128)(2,1)S(1)}, bf16[8,7296]{1,0:T(8,128)(2,1)S(1)}, u32[]{:S(2)}, u32[]{:S(2)}) collective-permute-start(bf16[8,7296]{1,0:T(8,128)(2,1)S(1)} %get-tuple-element.30), channel_id=1, source_target_pairs={{0,8},{4,12},{8,0},{12,4},{1,9},{5,13},{9,1},{13,5},{2,10},{6,14},... | collective-permute-start | bytes 350216 | tf_op jit(solution)/shard_map/ppermute | solution.py:275
  8.5 4.3 %load_gate.1.first_ref = bf16[7168,768]{1,0:T(8,128)(2,1)S(1)} custom-call(s32[1]{0:T(128)} %bitcast.place_ref, bf16[7168,512]{1,0:T(8,128)(2,1)} %bitcast.7, bf16[7168,512]{1,0:T(8,128)(2,1)} %sgate_ref.1, bf16[7168,512]{1,0:T(8,128)(2,1)} %sup_ref.1), custom_call_target="tpu_custom_call" | custom-call | bytes 22020096 | tf_op jit(solution)/shard_map/load_gate/pallas_call | solution.py:79
  12.8 0.0 collective-permute-done.3
  12.8 0.4 collective-permute-start.4
  13.2 0.0 collective-permute-done.2
  13.2 1.8 %collective-permute-start.5 = (bf16[8,4992]{1,0:T(8,128)(2,1)S(1)}, bf16[8,4992]{1,0:T(8,128)(2,1)S(1)}, u32[]{:S(2)}, u32[]{:S(2)}) collective-permute-start(bf16[8,4992]{1,0:T(8,128)(2,1)S(1)} %collective-permute-done.2), channel_id=1, source_target_pairs={{0,8},{4,12},{8,0},{12,4},{1,9},{5,13},{9,1},{13,5},{2,10},{6,14},... | collective-permute-start | bytes 239624 | tf_op jit(solution)/shard_map/ppermute | solution.py:275
  15.0 0.0 collective-permute-done.1
  15.0 0.4 collective-permute-start.6
  15.4 0.0 collective-permute-done
  15.5 3.9 %collective-permute-start.9 = (bf16[16,2304]{1,0:T(8,128)(2,1)S(1)}, bf16[16,2304]{1,0:T(8,128)(2,1)S(1)}, u32[]{:S(2)}, u32[]{:S(2)}) collective-permute-start(bf16[16,2304]{1,0:T(8,128)(2,1)S(1)} %pad_maximum_fusion.1), channel_id=1, source_target_pairs={{0,3},{1,2},{2,1},{3,0},{4,7},{5,6},{6,5},{7,4},{8,11},{9,10},{10,... | collective-permute-start | bytes 221192 | tf_op jit(solution)/shard_map/ppermute | solution.py:275
  19.4 0.0 collective-permute-start.8
  19.4 0.1 collective-permute-done.6
  19.5 0.7 %collective-permute-start.7 = (bf16[16,2304]{1,0:T(8,128)(2,1)S(1)}, bf16[16,2304]{1,0:T(8,128)(2,1)S(1)}, u32[]{:S(2)}, u32[]{:S(2)}) collective-permute-start(bf16[16,2304]{1,0:T(8,128)(2,1)S(1)} %pad_maximum_fusion.1), channel_id=1, source_target_pairs={{0,1},{1,0},{2,3},{3,2},{4,5},{5,4},{6,7},{7,6},{8,9},{9,8},{10,11... | collective-permute-start | bytes 221192 | tf_op jit(solution)/shard_map/ppermute | solution.py:275
  20.2 3.2 %load_up.1.up_ref = bf16[7168,512]{1,0:T(8,128)(2,1)S(1)} custom-call(bf16[7168,512]{1,0:T(8,128)(2,1)} %bitcast.6), custom_call_target="tpu_custom_call" | custom-call | bytes 14680064 | tf_op jit(solution)/shard_map/load_up/pallas_call | solution.py:107
  23.4 0.0 collective-permute-done.4
  23.4 1.3 %collective-permute-done.8 = bf16[16,2304]{1,0:T(8,128)(2,1)S(1)} collective-permute-done((bf16[16,2304]{1,0:T(8,128)(2,1)S(1)}, bf16[16,2304]{1,0:T(8,128)(2,1)S(1)}, u32[]{:S(2)}, u32[]{:S(2)}) %collective-permute-start.8) | collective-permute-done | bytes 73760 | tf_op jit(solution)/shard_map/ppermute | solution.py:275
  24.7 0.1 collective-permute-start.11
  24.8 0.5 collective-permute-start.10
  25.4 1.9 %collective-permute-done.10.b1_ref = bf16[64,2304]{1,0:T(8,128)(2,1)S(1)} collective-permute-done((bf16[64,2304]{1,0:T(8,128)(2,1)S(1)}, bf16[64,2304]{1,0:T(8,128)(2,1)S(1)}, u32[]{:S(2)}, u32[]{:S(2)}) %collective-permute-start.10) | collective-permute-done | bytes 294944 | tf_op jit(solution)/shard_map/ppermute | solution.py:275
  27.3 0.0 collective-permute-done.11.a1_ref
  27.3 6.1 %split_rows.1 = (bf16[64,2560]{1,0:T(8,128)(2,1)S(1)}, bf16[64,4608]{1,0:T(8,128)(2,1)S(1)}, bf16[64,2560]{1,0:T(8,128)(2,1)S(1)}, bf16[64,4608]{1,0:T(8,128)(2,1)S(1)}) custom-call(s32[1]{0:T(128)} %bitcast.place_ref, bf16[64,2304]{1,0:T(8,128)(2,1)S(1)} %constant_dynamic-update-slice_fusion.2.b0_ref, ...), custom_call_target="tpu_custom_call" | custom-call | tf_op jit(solution)/shard_map/split_rows/pallas_call | solution.py:226
  33.3 0.2 collective-permute-start.12
  33.5 1.9 %collective-permute-done.12 = bf16[64,4608]{1,0:T(8,128)(2,1)S(1)} collective-permute-done((bf16[64,4608]{1,0:T(8,128)(2,1)S(1)}, bf16[64,4608]{1,0:T(8,128)(2,1)S(1)}, u32[]{:S(2)}, u32[]{:S(2)}) %collective-permute-start.12) | collective-permute-done | bytes 589856 | tf_op jit(solution)/shard_map/ppermute | solution.py:275
  35.4 0.1 collective-permute-start.13
  35.6 0.1 add_convert_fusion
  35.6 1.5 %collective-permute-start.14 = (bf16[32,4608]{1,0:T(8,128)(2,1)S(1)}, bf16[32,4608]{1,0:T(8,128)(2,1)S(1)}, u32[]{:S(2)}, u32[]{:S(2)}) collective-permute-start(bf16[32,4608]{1,0:T(8,128)(2,1)S(1)} %add_convert_fusion), channel_id=1, source_target_pairs={{0,8},{4,12},{8,0},{12,4},{1,9},{5,13},{9,1},{13,5},{2,10},{6,14},... | collective-permute-start | bytes 884744 | tf_op jit(solution)/shard_map/ppermute | solution.py:275
  37.2 0.1 add_convert_fusion.1
  37.2 2.7 %collective-permute-start.17 = (bf16[16,2560]{1,0:T(8,128)(2,1)S(1)}, bf16[16,2560]{1,0:T(8,128)(2,1)S(1)}, u32[]{:S(2)}, u32[]{:S(2)}) collective-permute-start(bf16[16,2560]{1,0:T(8,128)(2,1)S(1)} %get-tuple-element.57), channel_id=1, source_target_pairs={{0,3},{1,2},{2,1},{3,0},{4,7},{5,6},{6,5},{7,4},{8,11},{9,10},{10,... | collective-permute-start | bytes 245768 | tf_op jit(solution)/shard_map/ppermute | solution.py:275
  40.0 0.0 collective-permute-start.16
  40.0 1.7 %collective-permute-start.15 = (bf16[16,2560]{1,0:T(8,128)(2,1)S(1)}, bf16[16,2560]{1,0:T(8,128)(2,1)S(1)}, u32[]{:S(2)}, u32[]{:S(2)}) collective-permute-start(bf16[16,2560]{1,0:T(8,128)(2,1)S(1)} %get-tuple-element.59), channel_id=1, source_target_pairs={{0,1},{1,0},{2,3},{3,2},{4,5},{5,4},{6,7},{7,6},{8,9},{9,8},{10,11... | collective-permute-start | bytes 245768 | tf_op jit(solution)/shard_map/ppermute | solution.py:275
  41.7 3.3 %collective-permute-done.14 = bf16[32,4608]{1,0:T(8,128)(2,1)S(1)} collective-permute-done((bf16[32,4608]{1,0:T(8,128)(2,1)S(1)}, bf16[32,4608]{1,0:T(8,128)(2,1)S(1)}, u32[]{:S(2)}, u32[]{:S(2)}) %collective-permute-start.14) | collective-permute-done | bytes 294944 | tf_op jit(solution)/shard_map/ppermute | solution.py:275
  45.0 0.0 collective-permute-done.17
  45.0 2.5 %collective-permute-done.16 = bf16[16,2560]{1,0:T(8,128)(2,1)S(1)} collective-permute-done((bf16[16,2560]{1,0:T(8,128)(2,1)S(1)}, bf16[16,2560]{1,0:T(8,128)(2,1)S(1)}, u32[]{:S(2)}, u32[]{:S(2)}) %collective-permute-start.16) | collective-permute-done | bytes 81952 | tf_op jit(solution)/shard_map/ppermute | solution.py:275
  47.4 0.0 collective-permute-done.15
  47.4 0.1 convert_add_fusion.1
  47.5 1.4 %collective-permute-start.18 = (bf16[8,2560]{1,0:T(8,128)(2,1)S(1)}, bf16[8,2560]{1,0:T(8,128)(2,1)S(1)}, u32[]{:S(2)}, u32[]{:S(2)}) collective-permute-start(bf16[8,2560]{1,0:T(8,128)(2,1)S(1)} %slice.127), channel_id=1, source_target_pairs={{0,8},{4,12},{8,0},{12,4},{1,9},{5,13},{9,1},{13,5},{2,10},{6,14},... | collective-permute-start | bytes 122888 | tf_op jit(solution)/shard_map/ppermute | solution.py:275
  48.9 0.1 fusion.4
  49.0 0.4 collective-permute-start.19
  49.5 2.3 %collective-permute-start.21 = (bf16[8,4608]{1,0:T(8,128)(2,1)S(1)}, bf16[8,4608]{1,0:T(8,128)(2,1)S(1)}, u32[]{:S(2)}, u32[]{:S(2)}) collective-permute-start(bf16[8,4608]{1,0:T(8,128)(2,1)S(1)} %get-tuple-element.61), channel_id=1, source_target_pairs={{0,3},{1,2},{2,1},{3,0},{4,7},{5,6},{6,5},{7,4},{8,11},{9,10},{10,... | collective-permute-start | bytes 221192 | tf_op jit(solution)/shard_map/ppermute | solution.py:275
  51.8 0.8 %collective-permute-start.20 = (bf16[8,4608]{1,0:T(8,128)(2,1)S(1)}, bf16[8,4608]{1,0:T(8,128)(2,1)S(1)}, u32[]{:S(2)}, u32[]{:S(2)}) collective-permute-start(bf16[8,4608]{1,0:T(8,128)(2,1)S(1)} %get-tuple-element.62), channel_id=1, source_target_pairs={{0,2},{1,3},{2,0},{3,1},{4,6},{5,7},{6,4},{7,5},{8,10},{9,11},{10,... | collective-permute-start | bytes 221192 | tf_op jit(solution)/shard_map/ppermute | solution.py:275
  52.6 1.1 %collective-permute-done.19 = bf16[8,4608]{1,0:T(8,128)(2,1)S(1)} collective-permute-done((bf16[8,4608]{1,0:T(8,128)(2,1)S(1)}, bf16[8,4608]{1,0:T(8,128)(2,1)S(1)}, u32[]{:S(2)}, u32[]{:S(2)}) %collective-permute-start.19) | collective-permute-done | bytes 73760 | tf_op jit(solution)/shard_map/ppermute | solution.py:275
  53.7 2.7 %collective-permute-done.21 = bf16[8,4608]{1,0:T(8,128)(2,1)S(1)} collective-permute-done((bf16[8,4608]{1,0:T(8,128)(2,1)S(1)}, bf16[8,4608]{1,0:T(8,128)(2,1)S(1)}, u32[]{:S(2)}, u32[]{:S(2)}) %collective-permute-start.21) | collective-permute-done | bytes 73760 | tf_op jit(solution)/shard_map/ppermute | solution.py:275
  56.4 2.8 %collective-permute-done.20 = bf16[8,4608]{1,0:T(8,128)(2,1)S(1)} collective-permute-done((bf16[8,4608]{1,0:T(8,128)(2,1)S(1)}, bf16[8,4608]{1,0:T(8,128)(2,1)S(1)}, u32[]{:S(2)}, u32[]{:S(2)}) %collective-permute-start.20) | collective-permute-done | bytes 73760 | tf_op jit(solution)/shard_map/ppermute | solution.py:275
  59.2 0.7 %pad_maximum_fusion = bf16[8,7168]{1,0:T(8,128)(2,1)} fusion(bf16[8,4608]{1,0:T(8,128)(2,1)S(1)} %fusion.2, bf16[8,2560]{1,0:T(8,128)(2,1)S(1)} %fusion.3), kind=kLoop, calls=%fused_computation.10 | loop fusion | flops 229376 | bytes 229376 | tf_op jit(solution)/shard_map/concatenate | solution.py:352
  (26 shorter events, 0.3 us)
Async XLA Ops:
  1.1 11.8 %collective-permute-start.3 = (bf16[8,4992]{1,0:T(8,128)(2,1)S(1)}, bf16[8,4992]{1,0:T(8,128)(2,1)S(1)}, u32[]{:S(2)}, u32[]{:S(2)}) collective-permute-start(bf16[8,4992]{1,0:T(8,128)(2,1)S(1)} %get-tuple-element.31), channel_id=1, source_target_pairs={{0,1},{1,0},{2,3},{3,2},{4,5},{5,4},{6,7},{7,6},{8,9},{9,8},{10,11... | collective-permute-start | bytes 239624 | tf_op jit(solution)/shard_map/ppermute | solution.py:275
  4.2 9.1 %collective-permute-start.2 = (bf16[8,4992]{1,0:T(8,128)(2,1)S(1)}, bf16[8,4992]{1,0:T(8,128)(2,1)S(1)}, u32[]{:S(2)}, u32[]{:S(2)}) collective-permute-start(bf16[8,4992]{1,0:T(8,128)(2,1)S(1)} %get-tuple-element.31), channel_id=1, source_target_pairs={{0,2},{1,3},{2,0},{3,1},{4,6},{5,7},{6,4},{7,5},{8,10},{9,11},{10,... | collective-permute-start | bytes 239624 | tf_op jit(solution)/shard_map/ppermute | solution.py:275
  6.8 8.3 %collective-permute-start.1 = (bf16[8,4992]{1,0:T(8,128)(2,1)S(1)}, bf16[8,4992]{1,0:T(8,128)(2,1)S(1)}, u32[]{:S(2)}, u32[]{:S(2)}) collective-permute-start(bf16[8,4992]{1,0:T(8,128)(2,1)S(1)} %get-tuple-element.31), channel_id=1, source_target_pairs={{0,3},{1,2},{2,1},{3,0},{4,7},{5,6},{6,5},{7,4},{8,11},{9,10},{10,... | collective-permute-start | bytes 239624 | tf_op jit(solution)/shard_map/ppermute | solution.py:275
  6.8 8.7 %collective-permute-start = (bf16[8,7296]{1,0:T(8,128)(2,1)S(1)}, bf16[8,7296]{1,0:T(8,128)(2,1)S(1)}, u32[]{:S(2)}, u32[]{:S(2)}) collective-permute-start(bf16[8,7296]{1,0:T(8,128)(2,1)S(1)} %get-tuple-element.30), channel_id=1, source_target_pairs={{0,8},{4,12},{8,0},{12,4},{1,9},{5,13},{9,1},{13,5},{2,10},{6,14},... | collective-permute-start | bytes 350216 | tf_op jit(solution)/shard_map/ppermute | solution.py:275
  12.8 10.5 %collective-permute-start.4 = (bf16[8,4992]{1,0:T(8,128)(2,1)S(1)}, bf16[8,4992]{1,0:T(8,128)(2,1)S(1)}, u32[]{:S(2)}, u32[]{:S(2)}) collective-permute-start(bf16[8,4992]{1,0:T(8,128)(2,1)S(1)} %collective-permute-done.3), channel_id=1, source_target_pairs={{0,8},{4,12},{8,0},{12,4},{1,9},{5,13},{9,1},{13,5},{2,10},{6,14},... | collective-permute-start | bytes 239624 | tf_op jit(solution)/shard_map/ppermute | solution.py:275
  13.2 10.1 %collective-permute-start.5 = (bf16[8,4992]{1,0:T(8,128)(2,1)S(1)}, bf16[8,4992]{1,0:T(8,128)(2,1)S(1)}, u32[]{:S(2)}, u32[]{:S(2)}) collective-permute-start(bf16[8,4992]{1,0:T(8,128)(2,1)S(1)} %collective-permute-done.2), channel_id=1, source_target_pairs={{0,8},{4,12},{8,0},{12,4},{1,9},{5,13},{9,1},{13,5},{2,10},{6,14},... | collective-permute-start | bytes 239624 | tf_op jit(solution)/shard_map/ppermute | solution.py:275
  15.0 4.5 %collective-permute-start.6 = (bf16[8,4992]{1,0:T(8,128)(2,1)S(1)}, bf16[8,4992]{1,0:T(8,128)(2,1)S(1)}, u32[]{:S(2)}, u32[]{:S(2)}) collective-permute-start(bf16[8,4992]{1,0:T(8,128)(2,1)S(1)} %collective-permute-done.1), channel_id=1, source_target_pairs={{0,8},{4,12},{8,0},{12,4},{1,9},{5,13},{9,1},{13,5},{2,10},{6,14},... | collective-permute-start | bytes 239624 | tf_op jit(solution)/shard_map/ppermute | solution.py:275
  15.5 7.9 %collective-permute-start.9 = (bf16[16,2304]{1,0:T(8,128)(2,1)S(1)}, bf16[16,2304]{1,0:T(8,128)(2,1)S(1)}, u32[]{:S(2)}, u32[]{:S(2)}) collective-permute-start(bf16[16,2304]{1,0:T(8,128)(2,1)S(1)} %pad_maximum_fusion.1), channel_id=1, source_target_pairs={{0,3},{1,2},{2,1},{3,0},{4,7},{5,6},{6,5},{7,4},{8,11},{9,10},{10,... | collective-permute-start | bytes 221192 | tf_op jit(solution)/shard_map/ppermute | solution.py:275
  19.4 5.3 %collective-permute-start.8 = (bf16[16,2304]{1,0:T(8,128)(2,1)S(1)}, bf16[16,2304]{1,0:T(8,128)(2,1)S(1)}, u32[]{:S(2)}, u32[]{:S(2)}) collective-permute-start(bf16[16,2304]{1,0:T(8,128)(2,1)S(1)} %pad_maximum_fusion.1), channel_id=1, source_target_pairs={{0,2},{1,3},{2,0},{3,1},{4,6},{5,7},{6,4},{7,5},{8,10},{9,11},{10,... | collective-permute-start | bytes 221192 | tf_op jit(solution)/shard_map/ppermute | solution.py:275
  19.5 5.1 %collective-permute-start.7 = (bf16[16,2304]{1,0:T(8,128)(2,1)S(1)}, bf16[16,2304]{1,0:T(8,128)(2,1)S(1)}, u32[]{:S(2)}, u32[]{:S(2)}) collective-permute-start(bf16[16,2304]{1,0:T(8,128)(2,1)S(1)} %pad_maximum_fusion.1), channel_id=1, source_target_pairs={{0,1},{1,0},{2,3},{3,2},{4,5},{5,4},{6,7},{7,6},{8,9},{9,8},{10,11... | collective-permute-start | bytes 221192 | tf_op jit(solution)/shard_map/ppermute | solution.py:275
  24.7 2.6 %collective-permute-start.11 = (bf16[64,4992]{1,0:T(8,128)(2,1)S(1)}, bf16[64,4992]{1,0:T(8,128)(2,1)S(1)}, u32[]{:S(2)}, u32[]{:S(2)}) collective-permute-start(bf16[64,4992]{1,0:T(8,128)(2,1)S(1)} %constant_dynamic-update-slice_fusion.6.a0_ref), channel_id=1, source_target_pairs={{0,4},{4,0},{8,12},{12,8},{1,5},{5,1},{9,13},{13,9},{2,6},{6,2},{1... | collective-permute-start | bytes 1916936 | tf_op jit(solution)/shard_map/ppermute | solution.py:275
  24.8 2.4 %collective-permute-start.10 = (bf16[64,2304]{1,0:T(8,128)(2,1)S(1)}, bf16[64,2304]{1,0:T(8,128)(2,1)S(1)}, u32[]{:S(2)}, u32[]{:S(2)}) collective-permute-start(bf16[64,2304]{1,0:T(8,128)(2,1)S(1)} %constant_dynamic-update-slice_fusion.2.b0_ref), channel_id=1, source_target_pairs={{0,4},{4,0},{8,12},{12,8},{1,5},{5,1},{9,13},{13,9},{2,6},{6,2},{1... | collective-permute-start | bytes 884744 | tf_op jit(solution)/shard_map/ppermute | solution.py:275
  33.3 2.1 %collective-permute-start.12 = (bf16[64,4608]{1,0:T(8,128)(2,1)S(1)}, bf16[64,4608]{1,0:T(8,128)(2,1)S(1)}, u32[]{:S(2)}, u32[]{:S(2)}) collective-permute-start(bf16[64,4608]{1,0:T(8,128)(2,1)S(1)} %get-tuple-element.48), channel_id=1, source_target_pairs={{0,4},{4,0},{8,12},{12,8},{1,5},{5,1},{9,13},{13,9},{2,6},{6,2},{1... | collective-permute-start | bytes 1769480 | tf_op jit(solution)/shard_map/ppermute | solution.py:275
  35.4 1.8 %collective-permute-start.13 = (bf16[64,2560]{1,0:T(8,128)(2,1)S(1)}, bf16[64,2560]{1,0:T(8,128)(2,1)S(1)}, u32[]{:S(2)}, u32[]{:S(2)}) collective-permute-start(bf16[64,2560]{1,0:T(8,128)(2,1)S(1)} %get-tuple-element.49), channel_id=1, source_target_pairs={{0,4},{4,0},{8,12},{12,8},{1,5},{5,1},{9,13},{13,9},{2,6},{6,2},{1... | collective-permute-start | bytes 983048 | tf_op jit(solution)/shard_map/ppermute | solution.py:275
  35.6 9.4 %collective-permute-start.14 = (bf16[32,4608]{1,0:T(8,128)(2,1)S(1)}, bf16[32,4608]{1,0:T(8,128)(2,1)S(1)}, u32[]{:S(2)}, u32[]{:S(2)}) collective-permute-start(bf16[32,4608]{1,0:T(8,128)(2,1)S(1)} %add_convert_fusion), channel_id=1, source_target_pairs={{0,8},{4,12},{8,0},{12,4},{1,9},{5,13},{9,1},{13,5},{2,10},{6,14},... | collective-permute-start | bytes 884744 | tf_op jit(solution)/shard_map/ppermute | solution.py:275
  37.2 7.8 %collective-permute-start.17 = (bf16[16,2560]{1,0:T(8,128)(2,1)S(1)}, bf16[16,2560]{1,0:T(8,128)(2,1)S(1)}, u32[]{:S(2)}, u32[]{:S(2)}) collective-permute-start(bf16[16,2560]{1,0:T(8,128)(2,1)S(1)} %get-tuple-element.57), channel_id=1, source_target_pairs={{0,3},{1,2},{2,1},{3,0},{4,7},{5,6},{6,5},{7,4},{8,11},{9,10},{10,... | collective-permute-start | bytes 245768 | tf_op jit(solution)/shard_map/ppermute | solution.py:275
  40.0 7.5 %collective-permute-start.16 = (bf16[16,2560]{1,0:T(8,128)(2,1)S(1)}, bf16[16,2560]{1,0:T(8,128)(2,1)S(1)}, u32[]{:S(2)}, u32[]{:S(2)}) collective-permute-start(bf16[16,2560]{1,0:T(8,128)(2,1)S(1)} %get-tuple-element.58), channel_id=1, source_target_pairs={{0,2},{1,3},{2,0},{3,1},{4,6},{5,7},{6,4},{7,5},{8,10},{9,11},{10,... | collective-permute-start | bytes 245768 | tf_op jit(solution)/shard_map/ppermute | solution.py:275
  40.0 7.5 %collective-permute-start.15 = (bf16[16,2560]{1,0:T(8,128)(2,1)S(1)}, bf16[16,2560]{1,0:T(8,128)(2,1)S(1)}, u32[]{:S(2)}, u32[]{:S(2)}) collective-permute-start(bf16[16,2560]{1,0:T(8,128)(2,1)S(1)} %get-tuple-element.59), channel_id=1, source_target_pairs={{0,1},{1,0},{2,3},{3,2},{4,5},{5,4},{6,7},{7,6},{8,9},{9,8},{10,11... | collective-permute-start | bytes 245768 | tf_op jit(solution)/shard_map/ppermute | solution.py:275
  47.5 5.1 %collective-permute-start.18 = (bf16[8,2560]{1,0:T(8,128)(2,1)S(1)}, bf16[8,2560]{1,0:T(8,128)(2,1)S(1)}, u32[]{:S(2)}, u32[]{:S(2)}) collective-permute-start(bf16[8,2560]{1,0:T(8,128)(2,1)S(1)} %slice.127), channel_id=1, source_target_pairs={{0,8},{4,12},{8,0},{12,4},{1,9},{5,13},{9,1},{13,5},{2,10},{6,14},... | collective-permute-start | bytes 122888 | tf_op jit(solution)/shard_map/ppermute | solution.py:275
  49.0 4.6 %collective-permute-start.19 = (bf16[8,4608]{1,0:T(8,128)(2,1)S(1)}, bf16[8,4608]{1,0:T(8,128)(2,1)S(1)}, u32[]{:S(2)}, u32[]{:S(2)}) collective-permute-start(bf16[8,4608]{1,0:T(8,128)(2,1)S(1)} %get-tuple-element.60), channel_id=1, source_target_pairs={{0,1},{1,0},{2,3},{3,2},{4,5},{5,4},{6,7},{7,6},{8,9},{9,8},{10,11... | collective-permute-start | bytes 221192 | tf_op jit(solution)/shard_map/ppermute | solution.py:275
  49.5 6.9 %collective-permute-start.21 = (bf16[8,4608]{1,0:T(8,128)(2,1)S(1)}, bf16[8,4608]{1,0:T(8,128)(2,1)S(1)}, u32[]{:S(2)}, u32[]{:S(2)}) collective-permute-start(bf16[8,4608]{1,0:T(8,128)(2,1)S(1)} %get-tuple-element.61), channel_id=1, source_target_pairs={{0,3},{1,2},{2,1},{3,0},{4,7},{5,6},{6,5},{7,4},{8,11},{9,10},{10,... | collective-permute-start | bytes 221192 | tf_op jit(solution)/shard_map/ppermute | solution.py:275
  51.8 7.4 %collective-permute-start.20 = (bf16[8,4608]{1,0:T(8,128)(2,1)S(1)}, bf16[8,4608]{1,0:T(8,128)(2,1)S(1)}, u32[]{:S(2)}, u32[]{:S(2)}) collective-permute-start(bf16[8,4608]{1,0:T(8,128)(2,1)S(1)} %get-tuple-element.62), channel_id=1, source_target_pairs={{0,2},{1,3},{2,0},{3,1},{4,6},{5,7},{6,4},{7,5},{8,10},{9,11},{10,... | collective-permute-start | bytes 221192 | tf_op jit(solution)/shard_map/ppermute | solution.py:275

commit v7 on v6

--- a/solution.py
+++ b/solution.py
@@ -31,10 +31,9 @@
     return lax.optimization_barrier((value, *done))[0]
 
 
-def pack_kernel(tokens_ref, groups_ref, weights_ref, packed_ref, tail_ref):
+def pack_kernel(tokens_ref, groups_ref, weights_ref, packed_ref):
     rows, width = tokens_ref.shape
     packed_ref[:, :width] = tokens_ref[...]
-    tail_ref[...] = tokens_ref[:, width - tail_ref.shape[1] :]
     groups = groups_ref[...].T
     weights = weights_ref[...].astype(F32).T
     lane = lax.broadcasted_iota(jnp.int32, (rows, LANES), 1)
@@ -44,12 +43,12 @@
     packed_ref[:, width:] = dense.astype(BF16)
 
 
-def pack_rows(tokens, group_ids, route_weights, tail):
+def pack_rows(tokens, group_ids, route_weights):
     rows, width = tokens.shape
     return pl.pallas_call(
         pack_kernel,
-        out_specs=[VMEM_SPEC] * 2,
-        out_shape=[pltpu.VMEM((rows, width + LANES), BF16), pltpu.VMEM((rows, tail), BF16)],
+        out_specs=VMEM_SPEC,
+        out_shape=pltpu.VMEM((rows, width + LANES), BF16),
         name="pack_rows",
     )(tokens, group_ids.T, route_weights.T)
 
@@ -169,69 +168,43 @@
     ]
 
 
-def regroup(value, outer, inner):
-    rows = value.shape[0] // (outer * inner)
-    return jnp.concatenate(
-        [
-            value[(o * inner + i) * rows : (o * inner + i + 1) * rows]
-            for i in range(inner)
-            for o in range(outer)
-        ],
-        axis=0,
-    )
-
-
-def split_kernel(
-    share, place_ref, b0_ref, a0_ref, b1_ref, a1_ref, first_ref, up_ref, down_ref, sdown_ref,
-    own_b_ref, own_a_ref, other_b_ref, other_a_ref, x, act, second, sems,
+def pair_kernel(
+    share, place_ref, own_ref, other_ref, first_ref, up_ref, down_ref, sdown_ref,
+    own_out_ref, other_out_ref, x, act, second, sems,
 ):
     copies = down_copies(share, place_ref, down_ref, sdown_ref, second, sems)
     for copy in copies:
         copy.start()
     width = up_ref.shape[0]
-    half = a0_ref.shape[0]
-    cut = width - a0_ref.shape[1]
-    for c, (b_ref, a_ref) in enumerate(((b0_ref, a0_ref), (b1_ref, a1_ref))):
-        rows = slice(c * half, (c + 1) * half)
-        b = regroup(b_ref[...].astype(F32), 4, 2).astype(BF16)
-        x[rows, :cut] = b[:, :cut]
-        x[rows, cut:width] = a_ref[...]
-        x[rows, width:] = b[:, cut:]
+    half = own_ref.shape[0]
+    x[:half, :] = own_ref[...]
+    x[half:, :] = other_ref[...]
     node = place_ref[0]
     weight = row_weight(node, x[:, width:])
     activate(share, node, x[:, :width], first_ref, up_ref, weight, act)
     piece = width // DOWN_PARTS
-    cut = own_b_ref.shape[1]
     for i in range(DOWN_PARTS):
         copies[2 * i].wait()
         copies[2 * i + 1].wait()
-        lower, upper = i * piece, (i + 1) * piece
-        for at, to in ((lower, min(upper, cut)), (max(lower, cut), upper)):
-            if at >= to:
-                continue
-            total = jnp.dot(act[...], second[:, at:to], preferred_element_type=F32)
-            if to <= cut:
-                own_b_ref[:, at:to] = regroup(total[:half], 2, 4).astype(BF16)
-                other_b_ref[:, at:to] = regroup(total[half:], 2, 4).astype(BF16)
-            else:
-                own_a_ref[:, at - cut : to - cut] = total[:half].astype(BF16)
-                other_a_ref[:, at - cut : to - cut] = total[half:].astype(BF16)
-
-
-def split_rows(place, pieces, first, up, down, sdown, cut, share):
-    half = pieces[0].shape[0]
+        at = slice(i * piece, (i + 1) * piece)
+        total = jnp.dot(act[...], second[:, at], preferred_element_type=F32).astype(BF16)
+        own_out_ref[:, at] = total[:half]
+        other_out_ref[:, at] = total[half:]
+
+
+def pair_rows(place, own, other, first, up, down, sdown, share):
+    half = own.shape[0]
     hidden, width = down.shape
-    out_b = jax.ShapeDtypeStruct((half, cut), BF16)
-    out_a = jax.ShapeDtypeStruct((half, width - cut), BF16)
-    return pl.pallas_call(
-        functools.partial(split_kernel, share),
-        in_specs=[SMEM_SPEC] + [VMEM_SPEC] * 6 + [ANY_SPEC] * 2,
-        out_specs=[VMEM_SPEC] * 4,
-        out_shape=[out_b, out_a] * 2,
+    out = jax.ShapeDtypeStruct((half, width), BF16)
+    return pl.pallas_call(
+        functools.partial(pair_kernel, share),
+        in_specs=[SMEM_SPEC] + [VMEM_SPEC] * 4 + [ANY_SPEC] * 2,
+        out_specs=[VMEM_SPEC] * 2,
+        out_shape=[out] * 2,
         scratch_shapes=[pltpu.VMEM((2 * half, width + LANES), BF16)] + down_scratch(2 * half, hidden, width),
         compiler_params=pltpu.CompilerParams(vmem_limit_bytes=28 << 20),
-        name="split_rows",
-    )(place, *pieces, first, up, in_hbm(down), in_hbm(sdown))
+        name="pair_rows",
+    )(place, own, other, first, up, in_hbm(down), in_hbm(sdown))
 
 
 def block_kernel(share, place_ref, x_ref, first_ref, up_ref, down_ref, sdown_ref, out_ref, act, second, sems):
@@ -271,16 +244,17 @@
     return functools.reduce(lambda a, b: a + b, (t.astype(F32) for t in terms))
 
 
-def swap(value, axis, bit):
-    return lax.ppermute(value, axis, [(i, i ^ bit) for i in range(4)])
-
-
-swap_x = functools.partial(swap, axis="node", bit=2)
-swap_core = functools.partial(swap, axis="node", bit=1)
-
-
-def swap_z(value, k):
-    return swap(value, "local", k)
+def flipped(value, even, odd):
+    pairs = []
+    for node in range(4):
+        for local in range(4):
+            node_bits, local_bits = odd if node % 2 else even
+            pairs.append((node * 4 + local, (node ^ node_bits) * 4 + (local ^ local_bits)))
+    return lax.ppermute(value, ("node", "local"), pairs)
+
+
+X, Z1, Z2, CORE = (2, 0), (0, 1), (0, 2), (1, 0)
+PHASES = ((Z2, X), (Z1, Z2), (X, Z1))
 
 
 def stack(*values):
@@ -304,8 +278,7 @@
     share = max(1, LANES * node_count // gate_shared.shape[1])
     place = lax.axis_index("node").reshape(1)
     gate, up, down = gate_experts[0], up_experts[0], down_experts[0]
-    cut = width * 17 // 56 // LANES * LANES
-    packed, a = pack_rows(tokens, group_ids, route_weights, width - cut)
+    packed = pack_rows(tokens, group_ids, route_weights)
 
     if node_count != 4 or local_count != 4:
         x = lax.all_gather(packed, ("node", "local"), axis=0, tiled=True)
@@ -313,43 +286,25 @@
         part = block_rows(place, x, first, load_up(up), down, down_shared, share)
         return lax.psum_scatter(part, ("node", "local"), scatter_dimension=0, tiled=True)
 
-    steps = (1, 2, 3)
-    across = swap_x(packed)
-    got = {k: swap_z(a, k) for k in steps}
-    first = load_gate(after(place, a), gate, gate_shared, up_shared, share)
-    got[1], first = lax.optimization_barrier((got[1], first))
-    far = {1: swap_x(got[1])}
-    got[2] = after(got[2], got[1])
-    far[2] = swap_x(got[2])
-    got[3] = after(got[3], got[2])
-    far[3] = swap_x(got[3])
-    b = stack(packed, across)
-    b = jnp.concatenate([b[:, :cut], b[:, width:]], axis=1)
-    b = after(b, got[3])
-    b_got = {k: swap_z(b, k) for k in steps}
-    up = load_up(after(up, got[3], b))
-    far, b_got, up = lax.optimization_barrier((far, b_got, up))
-    a = stack(a, got[1], got[2], got[3], across[:, cut:width], far[1], far[2], far[3])
-    b = stack(b, b_got[1], b_got[2], b_got[3])
-    pieces = (b, a, swap_core(b), swap_core(a))
-
-    cut = width * 20 // 56 // LANES * LANES
-    own_b, own_a, other_b, other_a = split_rows(place, pieces, first, up, down, down_shared, cut, share)
-
-    four, two = 4 * rows, 2 * rows
-    a_got = swap_core(other_a)
-    a_cross = swap_x(f32_sum(own_a[four:], a_got[four:]).astype(BF16))
-    b_got = swap_core(after(other_b, a_got))
-    b_far = [
-        swap_z(f32_sum(own_b[k * two : (k + 1) * two], b_got[k * two : (k + 1) * two]).astype(BF16), k)
-        for k in steps
-    ]
-    a_cross, b_far = lax.optimization_barrier((a_cross, b_far))
-    a_sum = f32_sum(own_a[:four], a_got[:four], a_cross)
-    a = f32_sum(a_sum[:rows], *(swap_z(a_sum[k * rows : (k + 1) * rows].astype(BF16), k) for k in steps))
-    b_sum = f32_sum(own_b[:two], b_got[:two], *b_far)
-    b = f32_sum(b_sum[:rows], swap_x(b_sum[rows:].astype(BF16)))
-    return jnp.concatenate([b.astype(BF16), a.astype(BF16)], axis=1)
+    own = stack(packed, flipped(packed, *PHASES[0]))
+    got = flipped(own, *PHASES[1])
+    first = load_gate(after(place, own), gate, gate_shared, up_shared, share)
+    got, first = lax.optimization_barrier((got, first))
+    own = stack(own, got)
+    got = flipped(own, *PHASES[2])
+    up = load_up(after(up, own))
+    got, up = lax.optimization_barrier((got, up))
+    own = stack(own, got)
+    other = flipped(own, CORE, CORE)
+
+    own, other = pair_rows(place, own, other, first, up, down, down_shared, share)
+
+    total = [own, flipped(other, CORE, CORE)]
+    for phase in reversed(PHASES):
+        half = total[0].shape[0] // 2
+        sent = f32_sum(*(t[half:] for t in total)).astype(BF16)
+        total = [f32_sum(*(t[:half] for t in total)), flipped(sent, *phase)]
+    return f32_sum(*total).astype(BF16)
 
 
 def solution(mesh):

time: 60 us -> 59.8 us (level)
  starting transfers between devices: 26.4 us -> 14.4 us
  waiting for transfers between devices: 17.5 us -> 29.4 us
    ppermute x22 -> x8, starting transfers between devices: 26.4 us -> 14.4 us  [flipped(): return lax.ppermute(value, ('node', 'local'), pairs)]
    ppermute x22 -> x8, waiting for transfers between devices: 17.5 us -> 29.4 us  [flipped(): return lax.ppermute(value, ('node', 'local'), pairs)]
    convert_element_type x4, other arithmetic: 0.18 us -> 0.98 us  [the longest x1 0.69 us: per_device(): return f32_sum(*total).astype(BF16)]
  transfers between devices with their start and end apart: 22 -> 8, of which waited for: 9 -> 8; matrix products, arithmetic and copies ran while one was open for 1% -> 0% of each run, Pallas kernels for 12% -> 13%
where the time goes in v7:
time: 59.8 us; the launch traced here: 59.6 us
  waiting for transfers between devices  29.4 us (49%)
  Pallas kernels  14.6 us (24%)
  starting transfers between devices  14.4 us (24%)
  other arithmetic  1.15 us (2%)
    ppermute x8, waiting for transfers between devices, flipped(): return lax.ppermute(value, ('node', 'local'), pairs)  29.4 us
    ppermute x8, starting transfers between devices, flipped(): return lax.ppermute(value, ('node', 'local'), pairs)  14.4 us
    pallas_call x1, Pallas kernels, pair_rows(): pl.pallas_call(functools.partial(pair_kernel, share), in_specs=[SMEM_SPEC...  6.04 us
    pallas_call x1, Pallas kernels, load_gate(): pl.pallas_call(functools.partial(load_gate_kernel, share), in_specs=[SMEM...  4.31 us
    pallas_call x1, Pallas kernels, load_up(): pl.pallas_call(load_up_kernel, in_specs=[ANY_SPEC], out_specs=VMEM_SPEC,...  3.17 us
  transfers between devices with their start and end apart: 8, of which 8 were waited for; matrix products, arithmetic and copies ran while one was open for 0% of the time, Pallas kernels for 13%

profile of v7, /device:TPU:0, one launch (start us, length us, event | category | flops | bytes accessed | tf_op | source)
XLA Modules:
  0.0 59.6 jit_solution(10055364893596714749)
XLA Ops:
  0.0 1.1 %pack_rows.1 = bf16[8,7296]{1,0:T(8,128)(2,1)S(1)} custom-call(bf16[8,7168]{1,0:T(8,128)(2,1)} %tokens_ref.1, s32[4,8]{1,0:T(4,128)} %bitcast.9, bf16[4,8]{1,0:T(4,128)(2,1)} %bitcast.10), custom_call_target="tpu_custom_call" | custom-call | tf_op jit(solution)/shard_map/pack_rows/pallas_call | solution.py:48
  1.1 4.1 %collective-permute-start = (bf16[8,7296]{1,0:T(8,128)(2,1)S(1)}, bf16[8,7296]{1,0:T(8,128)(2,1)S(1)}, u32[]{:S(2)}, u32[]{:S(2)}) collective-permute-start(bf16[8,7296]{1,0:T(8,128)(2,1)S(1)} %pack_rows.1), channel_id=1, source_target_pairs={{0,2},{1,3},{2,0},{3,1},{4,12},{5,13},{6,14},{7,15},{8,10},{9,11},... | collective-permute-start | bytes 350216 | tf_op jit(solution)/shard_map/ppermute | solution.py:253
  5.2 2.8 %collective-permute-done = bf16[8,7296]{1,0:T(8,128)(2,1)S(1)} collective-permute-done((bf16[8,7296]{1,0:T(8,128)(2,1)S(1)}, bf16[8,7296]{1,0:T(8,128)(2,1)S(1)}, u32[]{:S(2)}, u32[]{:S(2)}) %collective-permute-start) | collective-permute-done | bytes 116768 | tf_op jit(solution)/shard_map/ppermute | solution.py:253
  8.0 2.3 %collective-permute-start.1 = (bf16[16,7296]{1,0:T(8,128)(2,1)S(1)}, bf16[16,7296]{1,0:T(8,128)(2,1)S(1)}, u32[]{:S(2)}, u32[]{:S(2)}) collective-permute-start(bf16[16,7296]{1,0:T(8,128)(2,1)S(1)} %pad_maximum_fusion.2), channel_id=1, source_target_pairs={{0,1},{1,0},{2,3},{3,2},{4,6},{5,7},{6,4},{7,5},{8,9},{9,8},{10,11... | collective-permute-start | bytes 700424 | tf_op jit(solution)/shard_map/ppermute | solution.py:253
  10.3 4.3 %load_gate.1.first_ref = bf16[7168,768]{1,0:T(8,128)(2,1)S(1)} custom-call(s32[1]{0:T(128)} %bitcast.place_ref, bf16[7168,512]{1,0:T(8,128)(2,1)} %bitcast.7, bf16[7168,512]{1,0:T(8,128)(2,1)} %sgate_ref.1, bf16[7168,512]{1,0:T(8,128)(2,1)} %sup_ref.1), custom_call_target="tpu_custom_call" | custom-call | bytes 22020096 | tf_op jit(solution)/shard_map/load_gate/pallas_call | solution.py:78
  14.6 1.1 %collective-permute-done.1 = bf16[16,7296]{1,0:T(8,128)(2,1)S(1)} collective-permute-done((bf16[16,7296]{1,0:T(8,128)(2,1)S(1)}, bf16[16,7296]{1,0:T(8,128)(2,1)S(1)}, u32[]{:S(2)}, u32[]{:S(2)}) %collective-permute-start.1) | collective-permute-done | bytes 233504 | tf_op jit(solution)/shard_map/ppermute | solution.py:253
  15.7 3.0 %collective-permute-start.2 = (bf16[32,7296]{1,0:T(8,128)(2,1)S(1)}, bf16[32,7296]{1,0:T(8,128)(2,1)S(1)}, u32[]{:S(2)}, u32[]{:S(2)}) collective-permute-start(bf16[32,7296]{1,0:T(8,128)(2,1)S(1)} %pad_maximum_fusion.1), channel_id=1, source_target_pairs={{0,8},{1,9},{2,10},{3,11},{4,5},{5,4},{6,7},{7,6},{8,0},{9,1},{10,... | collective-permute-start | bytes 1400840 | tf_op jit(solution)/shard_map/ppermute | solution.py:253
  18.7 3.2 %load_up.1.up_ref = bf16[7168,512]{1,0:T(8,128)(2,1)S(1)} custom-call(bf16[7168,512]{1,0:T(8,128)(2,1)} %bitcast.6), custom_call_target="tpu_custom_call" | custom-call | bytes 14680064 | tf_op jit(solution)/shard_map/load_up/pallas_call | solution.py:106
  21.9 3.4 %collective-permute-done.2 = bf16[32,7296]{1,0:T(8,128)(2,1)S(1)} collective-permute-done((bf16[32,7296]{1,0:T(8,128)(2,1)S(1)}, bf16[32,7296]{1,0:T(8,128)(2,1)S(1)}, u32[]{:S(2)}, u32[]{:S(2)}) %collective-permute-start.2) | collective-permute-done | bytes 466976 | tf_op jit(solution)/shard_map/ppermute | solution.py:253
  25.2 0.1 pad_maximum_fusion.own_ref
  25.3 0.1 collective-permute-start.3
  25.4 2.5 %collective-permute-done.3.other_ref = bf16[64,7296]{1,0:T(8,128)(2,1)S(1)} collective-permute-done((bf16[64,7296]{1,0:T(8,128)(2,1)S(1)}, bf16[64,7296]{1,0:T(8,128)(2,1)S(1)}, u32[]{:S(2)}, u32[]{:S(2)}) %collective-permute-start.3) | collective-permute-done | bytes 933920 | tf_op jit(solution)/shard_map/ppermute | solution.py:253
  27.9 6.0 %pair_rows.1 = (bf16[64,7168]{1,0:T(8,128)(2,1)S(1)}, bf16[64,7168]{1,0:T(8,128)(2,1)S(1)}) custom-call(s32[1]{0:T(128)} %bitcast.place_ref, bf16[64,7296]{1,0:T(8,128)(2,1)S(1)} %pad_maximum_fusion.own_ref, bf16[64,7296]{1,0:T(8,128)(2,1)S(1)} %collective-permute-done.3.other_ref, bf16[7168,768]{1,0:T(8,128)(2,1)S(1)} %load_gate.1.first_ref, ...), custom_call_target="tpu_custom_call" | custom-call | tf_op jit(solution)/shard_map/pair_rows/pallas_call | solution.py:199
  33.9 0.2 collective-permute-start.4
  34.1 2.3 %collective-permute-done.4 = bf16[64,7168]{1,0:T(8,128)(2,1)S(1)} collective-permute-done((bf16[64,7168]{1,0:T(8,128)(2,1)S(1)}, bf16[64,7168]{1,0:T(8,128)(2,1)S(1)}, u32[]{:S(2)}, u32[]{:S(2)}) %collective-permute-start.4) | collective-permute-done | bytes 917536 | tf_op jit(solution)/shard_map/ppermute | solution.py:253
  36.5 0.2 add_convert_fusion
  36.7 2.1 %collective-permute-start.5 = (bf16[32,7168]{1,0:T(8,128)(2,1)S(1)}, bf16[32,7168]{1,0:T(8,128)(2,1)S(1)}, u32[]{:S(2)}, u32[]{:S(2)}) collective-permute-start(bf16[32,7168]{1,0:T(8,128)(2,1)S(1)} %get-tuple-element.21), channel_id=1, source_target_pairs={{0,8},{1,9},{2,10},{3,11},{4,5},{5,4},{6,7},{7,6},{8,0},{9,1},{10,... | collective-permute-start | bytes 1376264 | tf_op jit(solution)/shard_map/ppermute | solution.py:253
  38.8 6.5 %collective-permute-done.5 = bf16[32,7168]{1,0:T(8,128)(2,1)S(1)} collective-permute-done((bf16[32,7168]{1,0:T(8,128)(2,1)S(1)}, bf16[32,7168]{1,0:T(8,128)(2,1)S(1)}, u32[]{:S(2)}, u32[]{:S(2)}) %collective-permute-start.5) | collective-permute-done | bytes 458784 | tf_op jit(solution)/shard_map/ppermute | solution.py:253
  45.2 0.1 fusion
  45.3 0.1 collective-permute-start.6
  45.4 7.8 %collective-permute-done.6 = bf16[16,7168]{1,0:T(8,128)(2,1)S(1)} collective-permute-done((bf16[16,7168]{1,0:T(8,128)(2,1)S(1)}, bf16[16,7168]{1,0:T(8,128)(2,1)S(1)}, u32[]{:S(2)}, u32[]{:S(2)}) %collective-permute-start.6) | collective-permute-done | bytes 229408 | tf_op jit(solution)/shard_map/ppermute | solution.py:253
  53.2 2.6 %collective-permute-start.7 = (bf16[8,7168]{1,0:T(8,128)(2,1)S(1)}, bf16[8,7168]{1,0:T(8,128)(2,1)S(1)}, u32[]{:S(2)}, u32[]{:S(2)}) collective-permute-start(bf16[8,7168]{1,0:T(8,128)(2,1)S(1)} %fusion.1), channel_id=1, source_target_pairs={{0,2},{1,3},{2,0},{3,1},{4,12},{5,13},{6,14},{7,15},{8,10},{9,11},... | collective-permute-start | bytes 344072 | tf_op jit(solution)/shard_map/ppermute | solution.py:253
  55.8 3.2 %collective-permute-done.7 = bf16[8,7168]{1,0:T(8,128)(2,1)S(1)} collective-permute-done((bf16[8,7168]{1,0:T(8,128)(2,1)S(1)}, bf16[8,7168]{1,0:T(8,128)(2,1)S(1)}, u32[]{:S(2)}, u32[]{:S(2)}) %collective-permute-start.7) | collective-permute-done | bytes 114720 | tf_op jit(solution)/shard_map/ppermute | solution.py:253
  58.9 0.7 %fusion.3 = bf16[8,7168]{1,0:T(8,128)(2,1)} fusion(f32[16,7168]{1,0:T(8,128)S(1)} %get-tuple-element.24, bf16[8,7168]{1,0:T(8,128)(2,1)S(1)} %collective-permute-done.7, bf16[16,7168]{1,0:T(8,128)(2,1)S(1)} %collective-permute-done.6), kind=kLoop, calls=%fused_computation.12 | loop fusion | flops 286720 | bytes 573440 | tf_op jit(solution)/shard_map/convert_element_type | solution.py:307
  (3 shorter events, 0.1 us)
Async XLA Ops:
  1.1 6.9 %collective-permute-start = (bf16[8,7296]{1,0:T(8,128)(2,1)S(1)}, bf16[8,7296]{1,0:T(8,128)(2,1)S(1)}, u32[]{:S(2)}, u32[]{:S(2)}) collective-permute-start(bf16[8,7296]{1,0:T(8,128)(2,1)S(1)} %pack_rows.1), channel_id=1, source_target_pairs={{0,2},{1,3},{2,0},{3,1},{4,12},{5,13},{6,14},{7,15},{8,10},{9,11},... | collective-permute-start | bytes 350216 | tf_op jit(solution)/shard_map/ppermute | solution.py:253
  8.0 7.7 %collective-permute-start.1 = (bf16[16,7296]{1,0:T(8,128)(2,1)S(1)}, bf16[16,7296]{1,0:T(8,128)(2,1)S(1)}, u32[]{:S(2)}, u32[]{:S(2)}) collective-permute-start(bf16[16,7296]{1,0:T(8,128)(2,1)S(1)} %pad_maximum_fusion.2), channel_id=1, source_target_pairs={{0,1},{1,0},{2,3},{3,2},{4,6},{5,7},{6,4},{7,5},{8,9},{9,8},{10,11... | collective-permute-start | bytes 700424 | tf_op jit(solution)/shard_map/ppermute | solution.py:253
  15.7 9.5 %collective-permute-start.2 = (bf16[32,7296]{1,0:T(8,128)(2,1)S(1)}, bf16[32,7296]{1,0:T(8,128)(2,1)S(1)}, u32[]{:S(2)}, u32[]{:S(2)}) collective-permute-start(bf16[32,7296]{1,0:T(8,128)(2,1)S(1)} %pad_maximum_fusion.1), channel_id=1, source_target_pairs={{0,8},{1,9},{2,10},{3,11},{4,5},{5,4},{6,7},{7,6},{8,0},{9,1},{10,... | collective-permute-start | bytes 1400840 | tf_op jit(solution)/shard_map/ppermute | solution.py:253
  25.3 2.6 %collective-permute-start.3 = (bf16[64,7296]{1,0:T(8,128)(2,1)S(1)}, bf16[64,7296]{1,0:T(8,128)(2,1)S(1)}, u32[]{:S(2)}, u32[]{:S(2)}) collective-permute-start(bf16[64,7296]{1,0:T(8,128)(2,1)S(1)} %pad_maximum_fusion.own_ref), channel_id=1, source_target_pairs={{0,4},{1,5},{2,6},{3,7},{4,0},{5,1},{6,2},{7,3},{8,12},{9,13},{10,... | collective-permute-start | bytes 2801672 | tf_op jit(solution)/shard_map/ppermute | solution.py:253
  33.9 2.5 %collective-permute-start.4 = (bf16[64,7168]{1,0:T(8,128)(2,1)S(1)}, bf16[64,7168]{1,0:T(8,128)(2,1)S(1)}, u32[]{:S(2)}, u32[]{:S(2)}) collective-permute-start(bf16[64,7168]{1,0:T(8,128)(2,1)S(1)} %get-tuple-element.20), channel_id=1, source_target_pairs={{0,4},{1,5},{2,6},{3,7},{4,0},{5,1},{6,2},{7,3},{8,12},{9,13},{10,... | collective-permute-start | bytes 2752520 | tf_op jit(solution)/shard_map/ppermute | solution.py:253
  36.7 8.5 %collective-permute-start.5 = (bf16[32,7168]{1,0:T(8,128)(2,1)S(1)}, bf16[32,7168]{1,0:T(8,128)(2,1)S(1)}, u32[]{:S(2)}, u32[]{:S(2)}) collective-permute-start(bf16[32,7168]{1,0:T(8,128)(2,1)S(1)} %get-tuple-element.21), channel_id=1, source_target_pairs={{0,8},{1,9},{2,10},{3,11},{4,5},{5,4},{6,7},{7,6},{8,0},{9,1},{10,... | collective-permute-start | bytes 1376264 | tf_op jit(solution)/shard_map/ppermute | solution.py:253
  45.3 7.8 %collective-permute-start.6 = (bf16[16,7168]{1,0:T(8,128)(2,1)S(1)}, bf16[16,7168]{1,0:T(8,128)(2,1)S(1)}, u32[]{:S(2)}, u32[]{:S(2)}) collective-permute-start(bf16[16,7168]{1,0:T(8,128)(2,1)S(1)} %get-tuple-element.23), channel_id=1, source_target_pairs={{0,1},{1,0},{2,3},{3,2},{4,6},{5,7},{6,4},{7,5},{8,9},{9,8},{10,11... | collective-permute-start | bytes 688136 | tf_op jit(solution)/shard_map/ppermute | solution.py:253
  53.2 5.8 %collective-permute-start.7 = (bf16[8,7168]{1,0:T(8,128)(2,1)S(1)}, bf16[8,7168]{1,0:T(8,128)(2,1)S(1)}, u32[]{:S(2)}, u32[]{:S(2)}) collective-permute-start(bf16[8,7168]{1,0:T(8,128)(2,1)S(1)} %fusion.1), channel_id=1, source_target_pairs={{0,2},{1,3},{2,0},{3,1},{4,12},{5,13},{6,14},{7,15},{8,10},{9,11},... | collective-permute-start | bytes 344072 | tf_op jit(solution)/shard_map/ppermute | solution.py:253

commit v8 on v7

v8 whole, which is shorter than its diff:
```python
import functools

import jax
import jax.numpy as jnp
from jax import lax
from jax.experimental import pallas as pl
from jax.experimental.pallas import tpu as pltpu
from jax.sharding import PartitionSpec as P

LANES = 128
ROW_BLOCK = 128
F32 = jnp.float32
BF16 = jnp.bfloat16
VMEM_SPEC = pl.BlockSpec(memory_space=pltpu.VMEM)
SMEM_SPEC = pl.BlockSpec(memory_space=pltpu.SMEM)
ANY_SPEC = pl.BlockSpec(memory_space=pl.ANY)


def in_hbm(value):
    return pltpu.with_memory_space_constraint(value, pltpu.HBM)


def run_copies(copies):
    for copy in copies:
        copy.start()
    for copy in copies:
        copy.wait()


def after(value, *done):
    return lax.optimization_barrier((value, *done))[0]


def pack_kernel(tokens_ref, groups_ref, weights_ref, packed_ref):
    rows, width = tokens_ref.shape
    packed_ref[:, :width] = tokens_ref[...]
    groups = groups_ref[...].T
    weights = weights_ref[...].astype(F32).T
    lane = lax.broadcasted_iota(jnp.int32, (rows, LANES), 1)
    dense = jnp.zeros((rows, LANES), F32)
    for k in range(groups.shape[1]):
        dense += jnp.where(lane == groups[:, k : k + 1], weights[:, k : k + 1], 0.0)
    packed_ref[:, width:] = dense.astype(BF16)


def pack_rows(tokens, group_ids, route_weights):
    rows, width = tokens.shape
    return pl.pallas_call(
        pack_kernel,
        out_specs=VMEM_SPEC,
        out_shape=pltpu.VMEM((rows, width + LANES), BF16),
        name="pack_rows",
    )(tokens, group_ids.T, route_weights.T)


def load_gate_kernel(share, place_ref, gate_ref, sgate_ref, sup_ref, out_ref, sems):
    width, hidden = gate_ref.shape
    column = pl.multiple_of((place_ref[0] // share) * LANES, LANES)
    parts = 4
    piece = width // parts
    copies = []
    for i in range(parts):
        at = pl.ds(i * piece, piece)
        for source, lower, size in (
            (gate_ref.at[at, :], 0, hidden),
            (sgate_ref.at[at, pl.ds(column, LANES)], hidden, LANES),
            (sup_ref.at[at, pl.ds(column, LANES)], hidden + LANES, LANES),
        ):
            copies.append(
                pltpu.make_async_copy(source, out_ref.at[at, pl.ds(lower, size)], sems.at[len(copies)])
            )
    run_copies(copies)


def load_gate(place, gate, sgate, sup, share):
    width, hidden = gate.shape
    shape = (width, hidden + 2 * LANES)
    return pl.pallas_call(
        functools.partial(load_gate_kernel, share),
        in_specs=[SMEM_SPEC] + [ANY_SPEC] * 3,
        out_specs=VMEM_SPEC,
        out_shape=pltpu.VMEM(shape, BF16),
        scratch_shapes=[pltpu.SemaphoreType.DMA((12,))],
        cost_estimate=pl.CostEstimate(flops=0, bytes_accessed=4 * shape[0] * shape[1], transcendentals=0),
        compiler_params=pltpu.CompilerParams(vmem_limit_bytes=1 << 20),
        name="load_gate",
    )(place, in_hbm(gate), in_hbm(sgate), in_hbm(sup))


def silu(v):
    return v / (1.0 + jnp.exp(-v))


def row_weight(node, dense):
    lane = lax.broadcasted_iota(jnp.int32, dense.shape, 1)
    return jnp.sum(jnp.where(lane == node, dense.astype(F32), 0.0), axis=1, keepdims=True)


DOWN_PARTS = 4
IN_FLIGHT = 3


def up_tile(hidden):
    return min(2 * LANES, hidden)


def stream_scratch(rows, hidden, width):
    copies = hidden // up_tile(hidden) + 2 * DOWN_PARTS
    return [
        pltpu.VMEM((rows, hidden), F32),
        pltpu.VMEM((rows, hidden + LANES), BF16),
        pltpu.VMEM((width, hidden), BF16),
        pltpu.VMEM((hidden + LANES, width), BF16),
        pltpu.SemaphoreType.DMA((copies,)),
    ]


def stream_copies(share, place_ref, up_ref, down_ref, sdown_ref, up, second, sems):
    width, hidden = up_ref.shape
    column = pl.multiple_of((place_ref[0] // share) * LANES, LANES)
    tile, piece = up_tile(hidden), width // DOWN_PARTS
    groups = [[(up_ref.at[:, pl.ds(at, tile)], up.at[:, pl.ds(at, tile)])] for at in range(0, hidden, tile)]
    for i in range(DOWN_PARTS):
        at = pl.ds(i * piece, piece)
        groups.append(
            [
                (down_ref.at[:, at], second.at[pl.ds(0, hidden), at]),
                (sdown_ref.at[pl.ds(column, LANES), at], second.at[pl.ds(hidden, LANES), at]),
            ]
        )
    count = iter(range(sems.shape[0]))
    return [[pltpu.make_async_copy(a, b, sems.at[next(count)]) for a, b in group] for group in groups]


def start_group(groups, i):
    if i < len(groups):
        for copy in groups[i]:
            copy.start()


def wait_group(groups, i):
    for copy in groups[i]:
        copy.wait()


def ffn(share, place_ref, x, first_ref, take, gate, act, up, second, store):
    width, hidden = up.shape
    node = place_ref[0]
    rows = x[:, :width]
    tile, piece = up_tile(hidden), width // DOWN_PARTS
    for at in range(0, hidden, tile):
        gate[:, at : at + tile] = jnp.dot(rows, first_ref[:, at : at + tile], preferred_element_type=F32)
    both = jnp.dot(rows, first_ref[:, hidden:], preferred_element_type=F32)
    shared = silu(both[:, :LANES]) * both[:, LANES:]
    if share > 1:
        lane = lax.broadcasted_iota(jnp.int32, shared.shape, 1)
        shared = jnp.where(lane // (LANES // share) == node % share, shared, 0.0)
    act[:, hidden:] = shared.astype(BF16)
    weight = row_weight(node, x[:, width:])
    tiles = hidden // tile
    for i in range(tiles):
        at = slice(i * tile, (i + 1) * tile)
        take(i)
        value = jnp.dot(rows, up[:, at], preferred_element_type=F32)
        act[:, at] = (silu(gate[:, at]) * value * weight).astype(BF16)
    for i in range(DOWN_PARTS):
        at = slice(i * piece, (i + 1) * piece)
        take(tiles + i)
        store(at, jnp.dot(act[...], second[:, at], preferred_element_type=F32).astype(BF16))


def pair_kernel(
    share, place_ref, own0_ref, own1_ref, other0_ref, other1_ref, first_ref, up_ref, down_ref, sdown_ref,
    own0_out_ref, own1_out_ref, other0_out_ref, other1_out_ref, x, gate, act, up, second, sems,
):
    groups = stream_copies(share, place_ref, up_ref, down_ref, sdown_ref, up, second, sems)
    for i in range(IN_FLIGHT):
        start_group(groups, i)
    half, cut = own0_ref.shape
    x[:half, :cut] = own0_ref[...]
    x[:half, cut:] = own1_ref[...]
    x[half:, :cut] = other0_ref[...]
    x[half:, cut:] = other1_ref[...]

    def take(i):
        wait_group(groups, i)
        start_group(groups, i + IN_FLIGHT)

    def store(at, total):
        own, other = (own0_out_ref, other0_out_ref) if at.stop <= cut else (own1_out_ref, other1_out_ref)
        at = slice(at.start % cut, at.start % cut + at.stop - at.start)
        own[:, at] = total[:half]
        other[:, at] = total[half:]

    ffn(share, place_ref, x, first_ref, take, gate, act, up, second, store)


def pair_rows(place, pieces, first, up, down, sdown, share):
    half, cut = pieces[0].shape
    hidden, width = down.shape
    out = jax.ShapeDtypeStruct((half, cut), BF16)
    return pl.pallas_call(
        functools.partial(pair_kernel, share),
        in_specs=[SMEM_SPEC] + [VMEM_SPEC] * 5 + [ANY_SPEC] * 3,
        out_specs=[VMEM_SPEC] * 4,
        out_shape=[out] * 4,
        scratch_shapes=[pltpu.VMEM((2 * half, width + LANES), BF16)] + stream_scratch(2 * half, hidden, width),
        compiler_params=pltpu.CompilerParams(vmem_limit_bytes=26 << 20),
        name="pair_rows",
    )(place, *pieces, first, in_hbm(up), in_hbm(down), in_hbm(sdown))


def block_kernel(
    share, place_ref, x_ref, first_ref, up_ref, down_ref, sdown_ref, out_ref, gate, act, up, second, sems
):
    groups = stream_copies(share, place_ref, up_ref, down_ref, sdown_ref, up, second, sems)

    @pl.when(pl.program_id(0) == 0)
    def _():
        for i in range(len(groups)):
            start_group(groups, i)
        for i in range(len(groups)):
            wait_group(groups, i)

    def store(at, total):
        out_ref[:, at] = total

    ffn(share, place_ref, x_ref, first_ref, lambda i: None, gate, act, up, second, store)


def block_rows(place, x, first, up, down, sdown, share):
    rows, packed = x.shape
    hidden, width = down.shape
    block = min(rows, ROW_BLOCK)
    return pl.pallas_call(
        functools.partial(block_kernel, share),
        grid=(rows // block,),
        in_specs=[SMEM_SPEC, pl.BlockSpec((block, packed), lambda i: (i, 0)), VMEM_SPEC] + [ANY_SPEC] * 3,
        out_specs=pl.BlockSpec((block, width), lambda i: (i, 0)),
        out_shape=jax.ShapeDtypeStruct((rows, width), BF16),
        scratch_shapes=stream_scratch(block, hidden, width),
        compiler_params=pltpu.CompilerParams(vmem_limit_bytes=26 << 20),
        name="block_rows",
    )(place, x, first, in_hbm(up), in_hbm(down), in_hbm(sdown))


def f32_sum(*terms):
    return functools.reduce(lambda a, b: a + b, (t.astype(F32) for t in terms))


def flipped(value, even, odd):
    pairs = []
    for node in range(4):
        for local in range(4):
            node_bits, local_bits = odd if node % 2 else even
            pairs.append((node * 4 + local, (node ^ node_bits) * 4 + (local ^ local_bits)))
    return lax.ppermute(value, ("node", "local"), pairs)


X, Z1, Z2, CORE = (2, 0), (0, 1), (0, 2), (1, 0)
PHASES = ((Z2, X), (Z1, Z2), (X, Z1))


def stack(*values):
    return jnp.concatenate(values, axis=0)


def per_device(
    tokens,
    group_ids,
    route_weights,
    gate_experts,
    up_experts,
    down_experts,
    gate_shared,
    up_shared,
    down_shared,
):
    rows, width = tokens.shape
    node_count = lax.axis_size("node")
    local_count = lax.axis_size("local")
    share = max(1, LANES * node_count // gate_shared.shape[1])
    place = lax.axis_index("node").reshape(1)
    gate, up, down = gate_experts[0], up_experts[0], down_experts[0]
    packed = pack_rows(tokens, group_ids, route_weights)

    if node_count != 4 or local_count != 4:
        x = lax.all_gather(packed, ("node", "local"), axis=0, tiled=True)
        first = load_gate(place, gate, gate_shared, up_shared, share)
        part = block_rows(place, x, first, up, down, down_shared, share)
        return lax.psum_scatter(part, ("node", "local"), scatter_dimension=0, tiled=True)

    cut = width // 2
    own = [packed[:, :cut], packed[:, cut:]]
    for phase in PHASES[:2]:
        own = [stack(part, flipped(part, *phase)) for part in own]
    got = [flipped(part, *PHASES[2]) for part in own]
    first = load_gate(after(place, *own), gate, gate_shared, up_shared, share)
    got, first = lax.optimization_barrier((got, first))
    own = [stack(part, add) for part, add in zip(own, got)]
    other = [flipped(part, CORE, CORE) for part in own]

    outs = pair_rows(place, own + other, first, up, down, down_shared, share)

    done = []
    for own, other in zip(outs[:2], outs[2:]):
        total = [own, flipped(other, CORE, CORE)]
        for phase in reversed(PHASES):
            half = total[0].shape[0] // 2
            sent = f32_sum(*(t[half:] for t in total)).astype(BF16)
            total = [f32_sum(*(t[:half] for t in total)), flipped(sent, *phase)]
        done.append(f32_sum(*total).astype(BF16))
    return jnp.concatenate(done, axis=1)


def solution(mesh):
    in_specs = (
        P(("rep", "node", "local"), None),
        P(("rep", "node", "local"), None),
        P(("rep", "node", "local"), None),
        P("node", None, "local"),
        P("node", None, "local"),
        P("node", "local", None),
        P(None, "local"),
        P(None, "local"),
        P("local", None),
    )
    out_specs = P(("rep", "node", "local"), None)
    return jax.shard_map(
        per_device, mesh=mesh, in_specs=in_specs, out_specs=out_specs, check_vma=False
    )
```

time: 59.8 us -> 60.6 us (1.013)
  waiting for transfers between devices: 29.4 us -> 30.7 us
    pallas_call x1 -> x0, Pallas kernels: 3.17 us -> none  [load_up(): pl.pallas_call(load_up_kernel, in_specs=[ANY_SPEC], out_specs=VMEM_SPEC,...]
    pallas_call x1, Pallas kernels: 6.04 us -> 8.98 us  [pair_rows(): pl.pallas_call(functools.partial(pair_kernel, share), in_specs=[SMEM_SPEC...]
    ppermute x8 -> x16, waiting for transfers between devices: 29.4 us -> 30.7 us  [flipped(): return lax.ppermute(value, ('node', 'local'), pairs)]
    concatenate x0 -> x1, other arithmetic: none -> 0.65 us  [per_device(): return jnp.concatenate(done, axis=1)]
    convert_element_type x1 -> x2, other arithmetic: 0.69 us -> 0.05 us  [per_device(): done.append(f32_sum(*total).astype(BF16))]
    ppermute x8 -> x16, starting transfers between devices: 14.4 us -> 14 us  [flipped(): return lax.ppermute(value, ('node', 'local'), pairs)]
  transfers between devices with their start and end apart: 8 -> 16, of which waited for: 8 -> 12; matrix products, arithmetic and copies ran while one was open for 0% -> 1% of each run, Pallas kernels for 13% -> 7%
where the time goes in v8:
time: 60.6 us; the launch traced here: 60.4 us
  waiting for transfers between devices  30.7 us (51%)
  Pallas kernels  14.4 us (24%)
  starting transfers between devices  14 us (23%)
  other arithmetic  1.15 us (2%)
    ppermute x16, waiting for transfers between devices, flipped(): return lax.ppermute(value, ('node', 'local'), pairs)  30.7 us
    ppermute x16, starting transfers between devices, flipped(): return lax.ppermute(value, ('node', 'local'), pairs)  14 us
    pallas_call x1, Pallas kernels, pair_rows(): pl.pallas_call(functools.partial(pair_kernel, share), in_specs=[SMEM_SPEC...  8.98 us
    pallas_call x1, Pallas kernels, load_gate(): pl.pallas_call(functools.partial(load_gate_kernel, share), in_specs=[SMEM...  4.31 us
  transfers between devices with their start and end apart: 16, of which 12 were waited for; matrix products, arithmetic and copies ran while one was open for 1% of the time, Pallas kernels for 7%

profile of v8, /device:TPU:0, one launch (start us, length us, event | category | flops | bytes accessed | tf_op | source)
XLA Modules:
  0.0 60.4 jit_solution(9130948015056523428)
XLA Ops:
  0.0 1.1 %pack_rows.1 = bf16[8,7296]{1,0:T(8,128)(2,1)S(1)} custom-call(bf16[8,7168]{1,0:T(8,128)(2,1)} %tokens_ref.1, s32[4,8]{1,0:T(4,128)} %bitcast.9, bf16[4,8]{1,0:T(4,128)(2,1)} %bitcast.10), custom_call_target="tpu_custom_call" | custom-call | tf_op jit(solution)/shard_map/pack_rows/pallas_call | solution.py:48
  1.1 4.1 %collective-permute-start.3 = (bf16[8,3712]{1,0:T(8,128)(2,1)S(1)}, bf16[8,3712]{1,0:T(8,128)(2,1)S(1)}, u32[]{:S(2)}, u32[]{:S(2)}) collective-permute-start(bf16[8,3712]{1,0:T(8,128)(2,1)S(1)} %slice.105), channel_id=1, source_target_pairs={{0,2},{1,3},{2,0},{3,1},{4,12},{5,13},{6,14},{7,15},{8,10},{9,11},... | collective-permute-start | bytes 178184 | tf_op jit(solution)/shard_map/ppermute | solution.py:257
  5.2 0.1 collective-permute-start
  5.3 2.1 %collective-permute-done.3 = bf16[8,3712]{1,0:T(8,128)(2,1)S(1)} collective-permute-done((bf16[8,3712]{1,0:T(8,128)(2,1)S(1)}, bf16[8,3712]{1,0:T(8,128)(2,1)S(1)}, u32[]{:S(2)}, u32[]{:S(2)}) %collective-permute-start.3) | collective-permute-done | bytes 59424 | tf_op jit(solution)/shard_map/ppermute | solution.py:257
  7.4 2.3 %collective-permute-start.4 = (bf16[16,3712]{1,0:T(8,128)(2,1)S(1)}, bf16[16,3712]{1,0:T(8,128)(2,1)S(1)}, u32[]{:S(2)}, u32[]{:S(2)}) collective-permute-start(bf16[16,3712]{1,0:T(8,128)(2,1)S(1)} %pad_maximum_fusion.4), channel_id=1, source_target_pairs={{0,1},{1,0},{2,3},{3,2},{4,6},{5,7},{6,4},{7,5},{8,9},{9,8},{10,11... | collective-permute-start | bytes 356360 | tf_op jit(solution)/shard_map/ppermute | solution.py:257
  9.7 4.2 %collective-permute-done = bf16[8,3584]{1,0:T(8,128)(2,1)S(1)} collective-permute-done((bf16[8,3584]{1,0:T(8,128)(2,1)S(1)}, bf16[8,3584]{1,0:T(8,128)(2,1)S(1)}, u32[]{:S(2)}, u32[]{:S(2)}) %collective-permute-start) | collective-permute-done | bytes 57376 | tf_op jit(solution)/shard_map/ppermute | solution.py:257
  14.0 0.1 collective-permute-start.1
  14.0 0.0 collective-permute-done.4
  14.1 1.6 %collective-permute-start.5 = (bf16[32,3712]{1,0:T(8,128)(2,1)S(1)}, bf16[32,3712]{1,0:T(8,128)(2,1)S(1)}, u32[]{:S(2)}, u32[]{:S(2)}) collective-permute-start(bf16[32,3712]{1,0:T(8,128)(2,1)S(1)} %pad_maximum_fusion.2), channel_id=1, source_target_pairs={{0,8},{1,9},{2,10},{3,11},{4,5},{5,4},{6,7},{7,6},{8,0},{9,1},{10,... | collective-permute-start | bytes 712712 | tf_op jit(solution)/shard_map/ppermute | solution.py:257
  15.6 4.4 %collective-permute-done.1 = bf16[16,3584]{1,0:T(8,128)(2,1)S(1)} collective-permute-done((bf16[16,3584]{1,0:T(8,128)(2,1)S(1)}, bf16[16,3584]{1,0:T(8,128)(2,1)S(1)}, u32[]{:S(2)}, u32[]{:S(2)}) %collective-permute-start.1) | collective-permute-done | bytes 114720 | tf_op jit(solution)/shard_map/ppermute | solution.py:257
  20.0 1.6 %collective-permute-start.2 = (bf16[32,3584]{1,0:T(8,128)(2,1)S(1)}, bf16[32,3584]{1,0:T(8,128)(2,1)S(1)}, u32[]{:S(2)}, u32[]{:S(2)}) collective-permute-start(bf16[32,3584]{1,0:T(8,128)(2,1)S(1)} %pad_maximum_fusion.3), channel_id=1, source_target_pairs={{0,8},{1,9},{2,10},{3,11},{4,5},{5,4},{6,7},{7,6},{8,0},{9,1},{10,... | collective-permute-start | bytes 688136 | tf_op jit(solution)/shard_map/ppermute | solution.py:257
  21.6 4.3 %load_gate.1.first_ref = bf16[7168,768]{1,0:T(8,128)(2,1)S(1)} custom-call(s32[1]{0:T(128)} %bitcast.place_ref, bf16[7168,512]{1,0:T(8,128)(2,1)} %bitcast.6, bf16[7168,512]{1,0:T(8,128)(2,1)} %sgate_ref.1, bf16[7168,512]{1,0:T(8,128)(2,1)} %sup_ref.1), custom_call_target="tpu_custom_call" | custom-call | bytes 22020096 | tf_op jit(solution)/shard_map/load_gate/pallas_call | solution.py:78
  25.9 0.2 collective-permute-done.2
  26.1 0.0 collective-permute-done.5
  26.2 0.1 collective-permute-start.7
  26.3 0.6 collective-permute-start.6
  26.9 1.9 %collective-permute-done.6.other0_ref = bf16[64,3584]{1,0:T(8,128)(2,1)S(1)} collective-permute-done((bf16[64,3584]{1,0:T(8,128)(2,1)S(1)}, bf16[64,3584]{1,0:T(8,128)(2,1)S(1)}, u32[]{:S(2)}, u32[]{:S(2)}) %collective-permute-start.6) | collective-permute-done | bytes 458784 | tf_op jit(solution)/shard_map/ppermute | solution.py:257
  28.7 0.0 collective-permute-done.7.other1_ref
  28.7 9.0 %pair_rows.1 = (bf16[64,3584]{1,0:T(8,128)(2,1)S(1)}, bf16[64,3584]{1,0:T(8,128)(2,1)S(1)}, bf16[64,3584]{1,0:T(8,128)(2,1)S(1)}, bf16[64,3584]{1,0:T(8,128)(2,1)S(1)}) custom-call(s32[1]{0:T(128)} %bitcast.place_ref, bf16[64,3584]{1,0:T(8,128)(2,1)S(1)} %pad_maximum_fusion.1.own0_ref, bf16[64,3712]{1,0:T(8,128)(2,1)S(1)} %pad_maximum_fusion.own1_ref, ...), custom_call_target="tpu_custom_call" | custom-call | tf_op jit(solution)/shard_map/pair_rows/pallas_call | solution.py:202
  37.7 0.2 collective-permute-start.8
  37.9 0.4 collective-permute-start.12
  38.3 1.3 %collective-permute-done.8 = bf16[64,3584]{1,0:T(8,128)(2,1)S(1)} collective-permute-done((bf16[64,3584]{1,0:T(8,128)(2,1)S(1)}, bf16[64,3584]{1,0:T(8,128)(2,1)S(1)}, u32[]{:S(2)}, u32[]{:S(2)}) %collective-permute-start.8) | collective-permute-done | bytes 458784 | tf_op jit(solution)/shard_map/ppermute | solution.py:257
  39.6 0.1 add_convert_fusion.1
  39.7 1.6 %collective-permute-start.9 = (bf16[32,3584]{1,0:T(8,128)(2,1)S(1)}, bf16[32,3584]{1,0:T(8,128)(2,1)S(1)}, u32[]{:S(2)}, u32[]{:S(2)}) collective-permute-start(bf16[32,3584]{1,0:T(8,128)(2,1)S(1)} %get-tuple-element.21), channel_id=1, source_target_pairs={{0,8},{1,9},{2,10},{3,11},{4,5},{5,4},{6,7},{7,6},{8,0},{9,1},{10,... | collective-permute-start | bytes 688136 | tf_op jit(solution)/shard_map/ppermute | solution.py:257
  41.3 0.0 collective-permute-done.12
  41.3 0.1 add_convert_fusion
  41.4 0.6 collective-permute-start.13
  42.0 3.8 %collective-permute-done.9 = bf16[32,3584]{1,0:T(8,128)(2,1)S(1)} collective-permute-done((bf16[32,3584]{1,0:T(8,128)(2,1)S(1)}, bf16[32,3584]{1,0:T(8,128)(2,1)S(1)}, u32[]{:S(2)}, u32[]{:S(2)}) %collective-permute-start.9) | collective-permute-done | bytes 229408 | tf_op jit(solution)/shard_map/ppermute | solution.py:257
  45.8 0.1 collective-permute-start.10
  45.9 2.3 %collective-permute-done.13 = bf16[32,3584]{1,0:T(8,128)(2,1)S(1)} collective-permute-done((bf16[32,3584]{1,0:T(8,128)(2,1)S(1)}, bf16[32,3584]{1,0:T(8,128)(2,1)S(1)}, u32[]{:S(2)}, u32[]{:S(2)}) %collective-permute-start.13) | collective-permute-done | bytes 229408 | tf_op jit(solution)/shard_map/ppermute | solution.py:257
  48.3 0.1 fusion
  48.3 0.1 collective-permute-start.14
  48.4 3.5 %collective-permute-done.10 = bf16[16,3584]{1,0:T(8,128)(2,1)S(1)} collective-permute-done((bf16[16,3584]{1,0:T(8,128)(2,1)S(1)}, bf16[16,3584]{1,0:T(8,128)(2,1)S(1)}, u32[]{:S(2)}, u32[]{:S(2)}) %collective-permute-start.10) | collective-permute-done | bytes 114720 | tf_op jit(solution)/shard_map/ppermute | solution.py:257
  51.9 0.1 collective-permute-start.11
  52.1 2.3 %collective-permute-done.14 = bf16[16,3584]{1,0:T(8,128)(2,1)S(1)} collective-permute-done((bf16[16,3584]{1,0:T(8,128)(2,1)S(1)}, bf16[16,3584]{1,0:T(8,128)(2,1)S(1)}, u32[]{:S(2)}, u32[]{:S(2)}) %collective-permute-start.14) | collective-permute-done | bytes 114720 | tf_op jit(solution)/shard_map/ppermute | solution.py:257
  54.3 0.7 %collective-permute-start.15 = (bf16[8,3584]{1,0:T(8,128)(2,1)S(1)}, bf16[8,3584]{1,0:T(8,128)(2,1)S(1)}, u32[]{:S(2)}, u32[]{:S(2)}) collective-permute-start(bf16[8,3584]{1,0:T(8,128)(2,1)S(1)} %fusion.2), channel_id=1, source_target_pairs={{0,2},{1,3},{2,0},{3,1},{4,12},{5,13},{6,14},{7,15},{8,10},{9,11},... | collective-permute-start | bytes 172040 | tf_op jit(solution)/shard_map/ppermute | solution.py:257
  55.0 2.1 %collective-permute-done.11 = bf16[8,3584]{1,0:T(8,128)(2,1)S(1)} collective-permute-done((bf16[8,3584]{1,0:T(8,128)(2,1)S(1)}, bf16[8,3584]{1,0:T(8,128)(2,1)S(1)}, u32[]{:S(2)}, u32[]{:S(2)}) %collective-permute-start.11) | collective-permute-done | bytes 57376 | tf_op jit(solution)/shard_map/ppermute | solution.py:257
  57.1 2.6 %collective-permute-done.15 = bf16[8,3584]{1,0:T(8,128)(2,1)S(1)} collective-permute-done((bf16[8,3584]{1,0:T(8,128)(2,1)S(1)}, bf16[8,3584]{1,0:T(8,128)(2,1)S(1)}, u32[]{:S(2)}, u32[]{:S(2)}) %collective-permute-start.15) | collective-permute-done | bytes 57376 | tf_op jit(solution)/shard_map/ppermute | solution.py:257
  59.8 0.7 %pad_maximum_fusion.6 = bf16[8,7168]{1,0:T(8,128)(2,1)} fusion(bf16[8,3584]{1,0:T(8,128)(2,1)S(1)} %fusion.4, bf16[8,3584]{1,0:T(8,128)(2,1)S(1)} %fusion.7), kind=kLoop, calls=%fused_computation.26 | loop fusion | flops 229376 | bytes 229376 | tf_op jit(solution)/shard_map/concatenate | solution.py:313
  (13 shorter events, 0.3 us)
Async XLA Ops:
  1.1 6.3 %collective-permute-start.3 = (bf16[8,3712]{1,0:T(8,128)(2,1)S(1)}, bf16[8,3712]{1,0:T(8,128)(2,1)S(1)}, u32[]{:S(2)}, u32[]{:S(2)}) collective-permute-start(bf16[8,3712]{1,0:T(8,128)(2,1)S(1)} %slice.105), channel_id=1, source_target_pairs={{0,2},{1,3},{2,0},{3,1},{4,12},{5,13},{6,14},{7,15},{8,10},{9,11},... | collective-permute-start | bytes 178184 | tf_op jit(solution)/shard_map/ppermute | solution.py:257
  5.2 8.8 %collective-permute-start = (bf16[8,3584]{1,0:T(8,128)(2,1)S(1)}, bf16[8,3584]{1,0:T(8,128)(2,1)S(1)}, u32[]{:S(2)}, u32[]{:S(2)}) collective-permute-start(bf16[8,3584]{1,0:T(8,128)(2,1)S(1)} %slice.104), channel_id=1, source_target_pairs={{0,2},{1,3},{2,0},{3,1},{4,12},{5,13},{6,14},{7,15},{8,10},{9,11},... | collective-permute-start | bytes 172040 | tf_op jit(solution)/shard_map/ppermute | solution.py:257
  7.4 6.7 %collective-permute-start.4 = (bf16[16,3712]{1,0:T(8,128)(2,1)S(1)}, bf16[16,3712]{1,0:T(8,128)(2,1)S(1)}, u32[]{:S(2)}, u32[]{:S(2)}) collective-permute-start(bf16[16,3712]{1,0:T(8,128)(2,1)S(1)} %pad_maximum_fusion.4), channel_id=1, source_target_pairs={{0,1},{1,0},{2,3},{3,2},{4,6},{5,7},{6,4},{7,5},{8,9},{9,8},{10,11... | collective-permute-start | bytes 356360 | tf_op jit(solution)/shard_map/ppermute | solution.py:257
  14.0 6.1 %collective-permute-start.1 = (bf16[16,3584]{1,0:T(8,128)(2,1)S(1)}, bf16[16,3584]{1,0:T(8,128)(2,1)S(1)}, u32[]{:S(2)}, u32[]{:S(2)}) collective-permute-start(bf16[16,3584]{1,0:T(8,128)(2,1)S(1)} %pad_maximum_fusion.5), channel_id=1, source_target_pairs={{0,1},{1,0},{2,3},{3,2},{4,6},{5,7},{6,4},{7,5},{8,9},{9,8},{10,11... | collective-permute-start | bytes 344072 | tf_op jit(solution)/shard_map/ppermute | solution.py:257
  14.1 12.1 %collective-permute-start.5 = (bf16[32,3712]{1,0:T(8,128)(2,1)S(1)}, bf16[32,3712]{1,0:T(8,128)(2,1)S(1)}, u32[]{:S(2)}, u32[]{:S(2)}) collective-permute-start(bf16[32,3712]{1,0:T(8,128)(2,1)S(1)} %pad_maximum_fusion.2), channel_id=1, source_target_pairs={{0,8},{1,9},{2,10},{3,11},{4,5},{5,4},{6,7},{7,6},{8,0},{9,1},{10,... | collective-permute-start | bytes 712712 | tf_op jit(solution)/shard_map/ppermute | solution.py:257
  20.0 6.1 %collective-permute-start.2 = (bf16[32,3584]{1,0:T(8,128)(2,1)S(1)}, bf16[32,3584]{1,0:T(8,128)(2,1)S(1)}, u32[]{:S(2)}, u32[]{:S(2)}) collective-permute-start(bf16[32,3584]{1,0:T(8,128)(2,1)S(1)} %pad_maximum_fusion.3), channel_id=1, source_target_pairs={{0,8},{1,9},{2,10},{3,11},{4,5},{5,4},{6,7},{7,6},{8,0},{9,1},{10,... | collective-permute-start | bytes 688136 | tf_op jit(solution)/shard_map/ppermute | solution.py:257
  26.2 2.6 %collective-permute-start.7 = (bf16[64,3712]{1,0:T(8,128)(2,1)S(1)}, bf16[64,3712]{1,0:T(8,128)(2,1)S(1)}, u32[]{:S(2)}, u32[]{:S(2)}) collective-permute-start(bf16[64,3712]{1,0:T(8,128)(2,1)S(1)} %pad_maximum_fusion.own1_ref), channel_id=1, source_target_pairs={{0,4},{1,5},{2,6},{3,7},{4,0},{5,1},{6,2},{7,3},{8,12},{9,13},{10,... | collective-permute-start | bytes 1425416 | tf_op jit(solution)/shard_map/ppermute | solution.py:257
  26.3 2.4 %collective-permute-start.6 = (bf16[64,3584]{1,0:T(8,128)(2,1)S(1)}, bf16[64,3584]{1,0:T(8,128)(2,1)S(1)}, u32[]{:S(2)}, u32[]{:S(2)}) collective-permute-start(bf16[64,3584]{1,0:T(8,128)(2,1)S(1)} %pad_maximum_fusion.1.own0_ref), channel_id=1, source_target_pairs={{0,4},{1,5},{2,6},{3,7},{4,0},{5,1},{6,2},{7,3},{8,12},{9,13},{10,... | collective-permute-start | bytes 1376264 | tf_op jit(solution)/shard_map/ppermute | solution.py:257
  37.7 1.9 %collective-permute-start.8 = (bf16[64,3584]{1,0:T(8,128)(2,1)S(1)}, bf16[64,3584]{1,0:T(8,128)(2,1)S(1)}, u32[]{:S(2)}, u32[]{:S(2)}) collective-permute-start(bf16[64,3584]{1,0:T(8,128)(2,1)S(1)} %get-tuple-element.18), channel_id=1, source_target_pairs={{0,4},{1,5},{2,6},{3,7},{4,0},{5,1},{6,2},{7,3},{8,12},{9,13},{10,... | collective-permute-start | bytes 1376264 | tf_op jit(solution)/shard_map/ppermute | solution.py:257
  37.9 3.4 %collective-permute-start.12 = (bf16[64,3584]{1,0:T(8,128)(2,1)S(1)}, bf16[64,3584]{1,0:T(8,128)(2,1)S(1)}, u32[]{:S(2)}, u32[]{:S(2)}) collective-permute-start(bf16[64,3584]{1,0:T(8,128)(2,1)S(1)} %get-tuple-element.20), channel_id=1, source_target_pairs={{0,4},{1,5},{2,6},{3,7},{4,0},{5,1},{6,2},{7,3},{8,12},{9,13},{10,... | collective-permute-start | bytes 1376264 | tf_op jit(solution)/shard_map/ppermute | solution.py:257
  39.7 6.1 %collective-permute-start.9 = (bf16[32,3584]{1,0:T(8,128)(2,1)S(1)}, bf16[32,3584]{1,0:T(8,128)(2,1)S(1)}, u32[]{:S(2)}, u32[]{:S(2)}) collective-permute-start(bf16[32,3584]{1,0:T(8,128)(2,1)S(1)} %get-tuple-element.21), channel_id=1, source_target_pairs={{0,8},{1,9},{2,10},{3,11},{4,5},{5,4},{6,7},{7,6},{8,0},{9,1},{10,... | collective-permute-start | bytes 688136 | tf_op jit(solution)/shard_map/ppermute | solution.py:257
  41.4 6.9 %collective-permute-start.13 = (bf16[32,3584]{1,0:T(8,128)(2,1)S(1)}, bf16[32,3584]{1,0:T(8,128)(2,1)S(1)}, u32[]{:S(2)}, u32[]{:S(2)}) collective-permute-start(bf16[32,3584]{1,0:T(8,128)(2,1)S(1)} %get-tuple-element.23), channel_id=1, source_target_pairs={{0,8},{1,9},{2,10},{3,11},{4,5},{5,4},{6,7},{7,6},{8,0},{9,1},{10,... | collective-permute-start | bytes 688136 | tf_op jit(solution)/shard_map/ppermute | solution.py:257
  45.8 6.1 %collective-permute-start.10 = (bf16[16,3584]{1,0:T(8,128)(2,1)S(1)}, bf16[16,3584]{1,0:T(8,128)(2,1)S(1)}, u32[]{:S(2)}, u32[]{:S(2)}) collective-permute-start(bf16[16,3584]{1,0:T(8,128)(2,1)S(1)} %get-tuple-element.25), channel_id=1, source_target_pairs={{0,1},{1,0},{2,3},{3,2},{4,6},{5,7},{6,4},{7,5},{8,9},{9,8},{10,11... | collective-permute-start | bytes 344072 | tf_op jit(solution)/shard_map/ppermute | solution.py:257
  48.3 6.0 %collective-permute-start.14 = (bf16[16,3584]{1,0:T(8,128)(2,1)S(1)}, bf16[16,3584]{1,0:T(8,128)(2,1)S(1)}, u32[]{:S(2)}, u32[]{:S(2)}) collective-permute-start(bf16[16,3584]{1,0:T(8,128)(2,1)S(1)} %get-tuple-element.27), channel_id=1, source_target_pairs={{0,1},{1,0},{2,3},{3,2},{4,6},{5,7},{6,4},{7,5},{8,9},{9,8},{10,11... | collective-permute-start | bytes 344072 | tf_op jit(solution)/shard_map/ppermute | solution.py:257
  51.9 5.1 %collective-permute-start.11 = (bf16[8,3584]{1,0:T(8,128)(2,1)S(1)}, bf16[8,3584]{1,0:T(8,128)(2,1)S(1)}, u32[]{:S(2)}, u32[]{:S(2)}) collective-permute-start(bf16[8,3584]{1,0:T(8,128)(2,1)S(1)} %fusion.5), channel_id=1, source_target_pairs={{0,2},{1,3},{2,0},{3,1},{4,12},{5,13},{6,14},{7,15},{8,10},{9,11},... | collective-permute-start | bytes 172040 | tf_op jit(solution)/shard_map/ppermute | solution.py:257
  54.3 5.4 %collective-permute-start.15 = (bf16[8,3584]{1,0:T(8,128)(2,1)S(1)}, bf16[8,3584]{1,0:T(8,128)(2,1)S(1)}, u32[]{:S(2)}, u32[]{:S(2)}) collective-permute-start(bf16[8,3584]{1,0:T(8,128)(2,1)S(1)} %fusion.2), channel_id=1, source_target_pairs={{0,2},{1,3},{2,0},{3,1},{4,12},{5,13},{6,14},{7,15},{8,10},{9,11},... | collective-permute-start | bytes 172040 | tf_op jit(solution)/shard_map/ppermute | solution.py:257

commit v9 on v8

--- a/solution.py
+++ b/solution.py
@@ -87,6 +87,34 @@
     )(place, in_hbm(gate), in_hbm(sgate), in_hbm(sup))
 
 
+def load_up_kernel(up_ref, out_ref, sems):
+    width = up_ref.shape[0]
+    parts = 8
+    piece = width // parts
+    run_copies(
+        [
+            pltpu.make_async_copy(
+                up_ref.at[pl.ds(i * piece, piece), :], out_ref.at[pl.ds(i * piece, piece), :], sems.at[i]
+            )
+            for i in range(parts)
+        ]
+    )
+
+
+def load_up(up):
+    width, hidden = up.shape
+    return pl.pallas_call(
+        load_up_kernel,
+        in_specs=[ANY_SPEC],
+        out_specs=VMEM_SPEC,
+        out_shape=pltpu.VMEM((width, hidden), BF16),
+        scratch_shapes=[pltpu.SemaphoreType.DMA((8,))],
+        cost_estimate=pl.CostEstimate(flops=0, bytes_accessed=4 * width * hidden, transcendentals=0),
+        compiler_params=pltpu.CompilerParams(vmem_limit_bytes=1 << 20),
+        name="load_up",
+    )(in_hbm(up))
+
+
 def silu(v):
     return v / (1.0 + jnp.exp(-v))
 
@@ -97,45 +125,39 @@
 
 
 DOWN_PARTS = 4
-IN_FLIGHT = 3
-
-
-def up_tile(hidden):
-    return min(2 * LANES, hidden)
-
-
-def stream_scratch(rows, hidden, width):
-    copies = hidden // up_tile(hidden) + 2 * DOWN_PARTS
+
+
+def down_scratch(rows, hidden, width):
     return [
-        pltpu.VMEM((rows, hidden), F32),
         pltpu.VMEM((rows, hidden + LANES), BF16),
-        pltpu.VMEM((width, hidden), BF16),
         pltpu.VMEM((hidden + LANES, width), BF16),
-        pltpu.SemaphoreType.DMA((copies,)),
+        pltpu.SemaphoreType.DMA((2 * DOWN_PARTS,)),
     ]
 
 
-def stream_copies(share, place_ref, up_ref, down_ref, sdown_ref, up, second, sems):
-    width, hidden = up_ref.shape
+def down_copies(share, place_ref, down_ref, sdown_ref, second, sems):
+    hidden, width = down_ref.shape
     column = pl.multiple_of((place_ref[0] // share) * LANES, LANES)
-    tile, piece = up_tile(hidden), width // DOWN_PARTS
-    groups = [[(up_ref.at[:, pl.ds(at, tile)], up.at[:, pl.ds(at, tile)])] for at in range(0, hidden, tile)]
+    piece = width // DOWN_PARTS
+    groups = []
     for i in range(DOWN_PARTS):
         at = pl.ds(i * piece, piece)
         groups.append(
             [
-                (down_ref.at[:, at], second.at[pl.ds(0, hidden), at]),
-                (sdown_ref.at[pl.ds(column, LANES), at], second.at[pl.ds(hidden, LANES), at]),
+                pltpu.make_async_copy(down_ref.at[:, at], second.at[pl.ds(0, hidden), at], sems.at[2 * i]),
+                pltpu.make_async_copy(
+                    sdown_ref.at[pl.ds(column, LANES), at],
+                    second.at[pl.ds(hidden, LANES), at],
+                    sems.at[2 * i + 1],
+                ),
             ]
         )
-    count = iter(range(sems.shape[0]))
-    return [[pltpu.make_async_copy(a, b, sems.at[next(count)]) for a, b in group] for group in groups]
+    return groups
 
 
 def start_group(groups, i):
-    if i < len(groups):
-        for copy in groups[i]:
-            copy.start()
+    for copy in groups[i]:
+        copy.start()
 
 
 def wait_group(groups, i):
@@ -143,56 +165,69 @@
         copy.wait()
 
 
-def ffn(share, place_ref, x, first_ref, take, gate, act, up, second, store):
-    width, hidden = up.shape
+def ffn(share, place_ref, x, first_ref, up_ref, act, second, take, store):
+    width, hidden = up_ref.shape
     node = place_ref[0]
     rows = x[:, :width]
-    tile, piece = up_tile(hidden), width // DOWN_PARTS
+    weight = row_weight(node, x[:, width:])
+    tile, piece = min(2 * LANES, hidden), width // DOWN_PARTS
     for at in range(0, hidden, tile):
-        gate[:, at : at + tile] = jnp.dot(rows, first_ref[:, at : at + tile], preferred_element_type=F32)
+        gate = jnp.dot(rows, first_ref[:, at : at + tile], preferred_element_type=F32)
+        up = jnp.dot(rows, up_ref[:, at : at + tile], preferred_element_type=F32)
+        act[:, at : at + tile] = (silu(gate) * up * weight).astype(BF16)
     both = jnp.dot(rows, first_ref[:, hidden:], preferred_element_type=F32)
     shared = silu(both[:, :LANES]) * both[:, LANES:]
     if share > 1:
         lane = lax.broadcasted_iota(jnp.int32, shared.shape, 1)
         shared = jnp.where(lane // (LANES // share) == node % share, shared, 0.0)
     act[:, hidden:] = shared.astype(BF16)
-    weight = row_weight(node, x[:, width:])
-    tiles = hidden // tile
-    for i in range(tiles):
-        at = slice(i * tile, (i + 1) * tile)
-        take(i)
-        value = jnp.dot(rows, up[:, at], preferred_element_type=F32)
-        act[:, at] = (silu(gate[:, at]) * value * weight).astype(BF16)
     for i in range(DOWN_PARTS):
         at = slice(i * piece, (i + 1) * piece)
-        take(tiles + i)
-        store(at, jnp.dot(act[...], second[:, at], preferred_element_type=F32).astype(BF16))
+        take(i)
+        store(at, jnp.dot(act[...], second[:, at], preferred_element_type=F32))
+
+
+def regroup(value, outer, inner):
+    rows = value.shape[0] // (outer * inner)
+    return jnp.concatenate(
+        [
+            value[(o * inner + i) * rows : (o * inner + i + 1) * rows]
+            for i in range(inner)
+            for o in range(outer)
+        ],
+        axis=0,
+    )
+
+
+def reorder(value, turn):
+    value = value.astype(F32)
+    return jnp.where(turn == 1, regroup(value, 2, 4), regroup(value, 4, 2)).astype(BF16)
 
 
 def pair_kernel(
     share, place_ref, own0_ref, own1_ref, other0_ref, other1_ref, first_ref, up_ref, down_ref, sdown_ref,
-    own0_out_ref, own1_out_ref, other0_out_ref, other1_out_ref, x, gate, act, up, second, sems,
+    own0_out_ref, own1_out_ref, other0_out_ref, other1_out_ref, x, act, second, sems,
 ):
-    groups = stream_copies(share, place_ref, up_ref, down_ref, sdown_ref, up, second, sems)
-    for i in range(IN_FLIGHT):
+    groups = down_copies(share, place_ref, down_ref, sdown_ref, second, sems)
+    for i in range(DOWN_PARTS):
         start_group(groups, i)
     half, cut = own0_ref.shape
     x[:half, :cut] = own0_ref[...]
-    x[:half, cut:] = own1_ref[...]
+    odd = place_ref[0] % 2
+    x[:half, cut:] = reorder(own1_ref[...], odd)
     x[half:, :cut] = other0_ref[...]
-    x[half:, cut:] = other1_ref[...]
-
-    def take(i):
-        wait_group(groups, i)
-        start_group(groups, i + IN_FLIGHT)
+    x[half:, cut:] = reorder(other1_ref[...], 1 - odd)
 
     def store(at, total):
-        own, other = (own0_out_ref, other0_out_ref) if at.stop <= cut else (own1_out_ref, other1_out_ref)
-        at = slice(at.start % cut, at.start % cut + at.stop - at.start)
-        own[:, at] = total[:half]
-        other[:, at] = total[half:]
-
-    ffn(share, place_ref, x, first_ref, take, gate, act, up, second, store)
+        if at.stop <= cut:
+            own0_out_ref[:, at] = total[:half].astype(BF16)
+            other0_out_ref[:, at] = total[half:].astype(BF16)
+        else:
+            at = slice(at.start - cut, at.stop - cut)
+            own1_out_ref[:, at] = reorder(total[:half], 1 - odd)
+            other1_out_ref[:, at] = reorder(total[half:], odd)
+
+    ffn(share, place_ref, x, first_ref, up_ref, act, second, functools.partial(wait_group, groups), store)
 
 
 def pair_rows(place, pieces, first, up, down, sdown, share):
@@ -201,31 +236,31 @@
     out = jax.ShapeDtypeStruct((half, cut), BF16)
     return pl.pallas_call(
         functools.partial(pair_kernel, share),
-        in_specs=[SMEM_SPEC] + [VMEM_SPEC] * 5 + [ANY_SPEC] * 3,
+        in_specs=[SMEM_SPEC] + [VMEM_SPEC] * 6 + [ANY_SPEC] * 2,
         out_specs=[VMEM_SPEC] * 4,
         out_shape=[out] * 4,
-        scratch_shapes=[pltpu.VMEM((2 * half, width + LANES), BF16)] + stream_scratch(2 * half, hidden, width),
-        compiler_params=pltpu.CompilerParams(vmem_limit_bytes=26 << 20),
+        scratch_shapes=[pltpu.VMEM((2 * half, width + LANES), BF16)] + down_scratch(2 * half, hidden, width),
+        compiler_params=pltpu.CompilerParams(vmem_limit_bytes=24 << 20),
         name="pair_rows",
-    )(place, *pieces, first, in_hbm(up), in_hbm(down), in_hbm(sdown))
+    )(place, *pieces, first, up, in_hbm(down), in_hbm(sdown))
 
 
 def block_kernel(
-    share, place_ref, x_ref, first_ref, up_ref, down_ref, sdown_ref, out_ref, gate, act, up, second, sems
+    share, place_ref, x_ref, first_ref, up_ref, down_ref, sdown_ref, out_ref, act, second, sems
 ):
-    groups = stream_copies(share, place_ref, up_ref, down_ref, sdown_ref, up, second, sems)
+    groups = down_copies(share, place_ref, down_ref, sdown_ref, second, sems)
 
     @pl.when(pl.program_id(0) == 0)
     def _():
-        for i in range(len(groups)):
+        for i in range(DOWN_PARTS):
             start_group(groups, i)
-        for i in range(len(groups)):
+        for i in range(DOWN_PARTS):
             wait_group(groups, i)
 
     def store(at, total):
-        out_ref[:, at] = total
-
-    ffn(share, place_ref, x_ref, first_ref, lambda i: None, gate, act, up, second, store)
+        out_ref[:, at] = total.astype(BF16)
+
+    ffn(share, place_ref, x_ref, first_ref, up_ref, act, second, lambda i: None, store)
 
 
 def block_rows(place, x, first, up, down, sdown, share):
@@ -235,13 +270,13 @@
     return pl.pallas_call(
         functools.partial(block_kernel, share),
         grid=(rows // block,),
-        in_specs=[SMEM_SPEC, pl.BlockSpec((block, packed), lambda i: (i, 0)), VMEM_SPEC] + [ANY_SPEC] * 3,
+        in_specs=[SMEM_SPEC, pl.BlockSpec((block, packed), lambda i: (i, 0))] + [VMEM_SPEC] * 2 + [ANY_SPEC] * 2,
         out_specs=pl.BlockSpec((block, width), lambda i: (i, 0)),
         out_shape=jax.ShapeDtypeStruct((rows, width), BF16),
-        scratch_shapes=stream_scratch(block, hidden, width),
-        compiler_params=pltpu.CompilerParams(vmem_limit_bytes=26 << 20),
+        scratch_shapes=down_scratch(block, hidden, width),
+        compiler_params=pltpu.CompilerParams(vmem_limit_bytes=24 << 20),
         name="block_rows",
-    )(place, x, first, in_hbm(up), in_hbm(down), in_hbm(sdown))
+    )(place, x, first, up, in_hbm(down), in_hbm(sdown))
 
 
 def f32_sum(*terms):
@@ -287,30 +322,37 @@
     if node_count != 4 or local_count != 4:
         x = lax.all_gather(packed, ("node", "local"), axis=0, tiled=True)
         first = load_gate(place, gate, gate_shared, up_shared, share)
-        part = block_rows(place, x, first, up, down, down_shared, share)
+        part = block_rows(place, x, first, load_up(up), down, down_shared, share)
         return lax.psum_scatter(part, ("node", "local"), scatter_dimension=0, tiled=True)
 
     cut = width // 2
     own = [packed[:, :cut], packed[:, cut:]]
-    for phase in PHASES[:2]:
-        own = [stack(part, flipped(part, *phase)) for part in own]
-    got = [flipped(part, *PHASES[2]) for part in own]
-    first = load_gate(after(place, *own), gate, gate_shared, up_shared, share)
-    got, first = lax.optimization_barrier((got, first))
-    own = [stack(part, add) for part, add in zip(own, got)]
+    loads = (
+        lambda *ready: None,
+        lambda *ready: load_up(after(up, *ready)),
+        lambda *ready: load_gate(after(place, *ready), gate, gate_shared, up_shared, share),
+    )
+    loaded = []
+    for phase, load in zip(PHASES, loads):
+        got = [flipped(part, *pairs) for part, pairs in zip(own, (phase, phase[::-1]))]
+        weights = load(*own)
+        if weights is not None:
+            got, weights = lax.optimization_barrier((got, weights))
+            loaded.append(weights)
+        own = [stack(part, add) for part, add in zip(own, got)]
+    up, first = loaded
     other = [flipped(part, CORE, CORE) for part in own]
 
     outs = pair_rows(place, own + other, first, up, down, down_shared, share)
 
-    done = []
-    for own, other in zip(outs[:2], outs[2:]):
-        total = [own, flipped(other, CORE, CORE)]
-        for phase in reversed(PHASES):
+    totals = [[own, flipped(other, CORE, CORE)] for own, other in zip(outs[:2], outs[2:])]
+    for phase in reversed(PHASES):
+        for i, pairs in enumerate((phase, phase[::-1])):
+            total = totals[i]
             half = total[0].shape[0] // 2
             sent = f32_sum(*(t[half:] for t in total)).astype(BF16)
-            total = [f32_sum(*(t[:half] for t in total)), flipped(sent, *phase)]
-        done.append(f32_sum(*total).astype(BF16))
-    return jnp.concatenate(done, axis=1)
+            totals[i] = [f32_sum(*(t[:half] for t in total)), flipped(sent, *pairs)]
+    return jnp.concatenate([f32_sum(*total).astype(BF16) for total in totals], axis=1)
 
 
 def solution(mesh):

time: 60.6 us -> 60.9 us (level)
  waiting for transfers between devices: 30.7 us -> 17.5 us
  starting transfers between devices: 14 us -> 21.1 us
  other arithmetic: 1.15 us -> 4.43 us
  local copies, waits for them, and re-layouts: 0.01 us -> 2.96 us
    ppermute x16, waiting for transfers between devices: 30.7 us -> 17.5 us  [flipped(): return lax.ppermute(value, ('node', 'local'), pairs)]
    ppermute x16, starting transfers between devices: 14 us -> 21.1 us  [flipped(): return lax.ppermute(value, ('node', 'local'), pairs)]
    concatenate x6, other arithmetic: 0.14 us -> 3.43 us  [stack(): return jnp.concatenate(values, axis=0)]
    pallas_call x0 -> x1, Pallas kernels: none -> 3.17 us  [load_up(): pl.pallas_call(load_up_kernel, in_specs=[ANY_SPEC], out_specs=VMEM_SPEC,...]
    pallas_call x1, Pallas kernels: 8.98 us -> 5.94 us  [pair_rows(): pl.pallas_call(functools.partial(pair_kernel, share), in_specs=[SMEM_SPEC...]
    unnamed x0 -> x10, local copies, waits for them, and re-layouts: none -> 2.95 us
  transfers between devices with their start and end apart: 16 -> 16, of which waited for: 12 -> 7; matrix products, arithmetic and copies ran while one was open for 1% -> 3% of each run, Pallas kernels for 7% -> 13%
where the time goes in v9:
time: 60.9 us; the launch traced here: 60.7 us
  starting transfers between devices  21.1 us (35%)
  waiting for transfers between devices  17.5 us (29%)
  Pallas kernels  14.6 us (24%)
  other arithmetic  4.43 us (7%)
  local copies, waits for them, and re-layouts  2.96 us (5%)
    ppermute x16, starting transfers between devices, flipped(): return lax.ppermute(value, ('node', 'local'), pairs)  21.1 us
    ppermute x16, waiting for transfers between devices, flipped(): return lax.ppermute(value, ('node', 'local'), pairs)  17.5 us
    pallas_call x1, Pallas kernels, pair_rows(): pl.pallas_call(functools.partial(pair_kernel, share), in_specs=[SMEM_SPEC...  5.94 us
    pallas_call x1, Pallas kernels, load_gate(): pl.pallas_call(functools.partial(load_gate_kernel, share), in_specs=[SMEM...  4.46 us
    concatenate x6, other arithmetic, stack(): return jnp.concatenate(values, axis=0)  3.43 us
    pallas_call x1, Pallas kernels, load_up(): pl.pallas_call(load_up_kernel, in_specs=[ANY_SPEC], out_specs=VMEM_SPEC,...  3.17 us
    unnamed x10, local copies, waits for them, and re-layouts  2.95 us
  transfers between devices with their start and end apart: 16, of which 7 were waited for; matrix products, arithmetic and copies ran while one was open for 3% of the time, Pallas kernels for 13%

profile of v9, /device:TPU:0, one launch (start us, length us, event | category | flops | bytes accessed | tf_op | source)
XLA Modules:
  0.0 60.7 jit_solution(2439911674283824520)
XLA Ops:
  0.0 1.1 %pack_rows.1 = bf16[8,7296]{1,0:T(8,128)(2,1)S(1)} custom-call(bf16[8,7168]{1,0:T(8,128)(2,1)} %tokens_ref.1, s32[4,8]{1,0:T(4,128)} %bitcast.11, bf16[4,8]{1,0:T(4,128)(2,1)} %bitcast.12), custom_call_target="tpu_custom_call" | custom-call | tf_op jit(solution)/shard_map/pack_rows/pallas_call | solution.py:48
  1.1 3.0 %collective-permute-start.2 = (bf16[8,3712]{1,0:T(8,128)(2,1)S(1)}, bf16[8,3712]{1,0:T(8,128)(2,1)S(1)}, u32[]{:S(2)}, u32[]{:S(2)}) collective-permute-start(bf16[8,3712]{1,0:T(8,128)(2,1)S(1)} %slice.105), channel_id=1, source_target_pairs={{0,8},{1,9},{2,10},{3,11},{4,6},{5,7},{6,4},{7,5},{8,0},{9,1},{10,... | collective-permute-start | bytes 178184 | tf_op jit(solution)/shard_map/ppermute | solution.py:292
  4.1 2.6 %collective-permute-start = (bf16[8,3584]{1,0:T(8,128)(2,1)S(1)}, bf16[8,3584]{1,0:T(8,128)(2,1)S(1)}, u32[]{:S(2)}, u32[]{:S(2)}) collective-permute-start(bf16[8,3584]{1,0:T(8,128)(2,1)S(1)} %slice.104), channel_id=1, source_target_pairs={{0,2},{1,3},{2,0},{3,1},{4,12},{5,13},{6,14},{7,15},{8,10},{9,11},... | collective-permute-start | bytes 172040 | tf_op jit(solution)/shard_map/ppermute | solution.py:292
  6.7 0.0 collective-permute-done.2
  6.7 2.8 %collective-permute-start.3 = (bf16[16,3712]{1,0:T(8,128)(2,1)S(1)}, bf16[16,3712]{1,0:T(8,128)(2,1)S(1)}, u32[]{:S(2)}, u32[]{:S(2)}) collective-permute-start(bf16[16,3712]{1,0:T(8,128)(2,1)S(1)} %pad_maximum_fusion.4), channel_id=1, source_target_pairs={{0,2},{1,3},{2,0},{3,1},{4,5},{5,4},{6,7},{7,6},{8,10},{9,11},{10,... | collective-permute-start | bytes 356360 | tf_op jit(solution)/shard_map/ppermute | solution.py:292
  9.5 0.0 collective-permute-done
  9.5 1.6 %collective-permute-start.1 = (bf16[16,3584]{1,0:T(8,128)(2,1)S(1)}, bf16[16,3584]{1,0:T(8,128)(2,1)S(1)}, u32[]{:S(2)}, u32[]{:S(2)}) collective-permute-start(bf16[16,3584]{1,0:T(8,128)(2,1)S(1)} %pad_maximum_fusion.5), channel_id=1, source_target_pairs={{0,1},{1,0},{2,3},{3,2},{4,6},{5,7},{6,4},{7,5},{8,9},{9,8},{10,11... | collective-permute-start | bytes 344072 | tf_op jit(solution)/shard_map/ppermute | solution.py:292
  11.1 3.2 %load_up.1.up_ref = bf16[7168,512]{1,0:T(8,128)(2,1)S(1)} custom-call(bf16[7168,512]{1,0:T(8,128)(2,1)} %bitcast.8), custom_call_target="tpu_custom_call" | custom-call | bytes 14680064 | tf_op jit(solution)/shard_map/load_up/pallas_call | solution.py:106
  14.3 0.0 copy-start
  14.3 2.9 %copy-done = bf16[7168,512]{1,0:T(8,128)(2,1)} copy-done((bf16[7168,512]{1,0:T(8,128)(2,1)}, bf16[7168,512]{1,0:T(8,128)(2,1)S(1)}, u32[]{:S(2)}) %copy-start) | copy-done | bytes 7340056
  17.2 0.0 collective-permute-done.1
  17.2 0.0 collective-permute-done.3
  17.3 0.7 %pad_maximum_fusion.2 = bf16[32,3712]{1,0:T(8,128)(2,1)} fusion(bf16[16,3712]{1,0:T(8,128)(2,1)S(1)} %collective-permute-done.3, bf16[8,3712]{1,0:T(8,128)(2,1)S(1)} %collective-permute-done.2, bf16[8,3712]{1,0:T(8,128)(2,1)S(1)} %slice.105), kind=kLoop, calls=%fused_computation.6 | loop fusion | flops 712704 | bytes 475136 | tf_op jit(solution)/shard_map/concatenate | solution.py:300
  18.0 0.4 collective-permute-start.5
  18.4 0.0 copy-done.1
  18.4 0.7 %pad_maximum_fusion.3 = bf16[32,3584]{1,0:T(8,128)(2,1)} fusion(bf16[16,3584]{1,0:T(8,128)(2,1)S(1)} %collective-permute-done.1, bf16[8,3584]{1,0:T(8,128)(2,1)S(1)} %collective-permute-done, bf16[8,3584]{1,0:T(8,128)(2,1)S(1)} %slice.104), kind=kLoop, calls=%fused_computation.13 | loop fusion | flops 688128 | bytes 458752 | tf_op jit(solution)/shard_map/concatenate | solution.py:300
  19.2 1.5 %collective-permute-start.4 = (bf16[32,3584]{1,0:T(8,128)(2,1)}, bf16[32,3584]{1,0:T(8,128)(2,1)}, u32[]{:S(2)}, u32[]{:S(2)}) collective-permute-start(bf16[32,3584]{1,0:T(8,128)(2,1)} %pad_maximum_fusion.3), channel_id=1, source_target_pairs={{0,8},{1,9},{2,10},{3,11},{4,5},{5,4},{6,7},{7,6},{8,0},{9,1},{10,... | collective-permute-start | bytes 688136 | tf_op jit(solution)/shard_map/ppermute | solution.py:292
  20.7 4.5 %load_gate.1.first_ref = bf16[7168,768]{1,0:T(8,128)(2,1)S(1)} custom-call(s32[1]{0:T(128)} %bitcast.place_ref, bf16[7168,512]{1,0:T(8,128)(2,1)} %bitcast.9, bf16[7168,512]{1,0:T(8,128)(2,1)} %sgate_ref.1, bf16[7168,512]{1,0:T(8,128)(2,1)} %sup_ref.1), custom_call_target="tpu_custom_call" | custom-call | bytes 22020096 | tf_op jit(solution)/shard_map/load_gate/pallas_call | solution.py:78
  25.1 0.3 collective-permute-done.4
  25.5 1.0 %collective-permute-done.5 = bf16[32,3712]{1,0:T(8,128)(2,1)} collective-permute-done((bf16[32,3712]{1,0:T(8,128)(2,1)}, bf16[32,3712]{1,0:T(8,128)(2,1)}, u32[]{:S(2)}, u32[]{:S(2)}) %collective-permute-start.5) | collective-permute-done | bytes 237600 | tf_op jit(solution)/shard_map/ppermute | solution.py:292
  26.5 1.0 %pad_maximum_fusion.own1_ref = bf16[64,3712]{1,0:T(8,128)(2,1)S(1)} fusion(bf16[32,3712]{1,0:T(8,128)(2,1)} %collective-permute-done.5, bf16[16,3712]{1,0:T(8,128)(2,1)S(1)} %collective-permute-done.3, bf16[8,3712]{1,0:T(8,128)(2,1)S(1)} %collective-permute-done.2, bf16[8,3712]{1,0:T(8,128)(2,1)S(1)} %slice.105), kind=kLoop, calls=%fused_computation | loop fusion | flops 1900544 | bytes 950272 | tf_op jit(solution)/shard_map/concatenate | solution.py:300
  27.5 0.3 collective-permute-start.7
  27.7 0.0 copy-done.2
  27.7 1.0 %pad_maximum_fusion.1.own0_ref = bf16[64,3584]{1,0:T(8,128)(2,1)S(1)} fusion(bf16[32,3584]{1,0:T(8,128)(2,1)} %collective-permute-done.4, bf16[16,3584]{1,0:T(8,128)(2,1)S(1)} %copy-done.2, bf16[8,3584]{1,0:T(8,128)(2,1)S(1)} %collective-permute-done, bf16[8,3584]{1,0:T(8,128)(2,1)S(1)} %slice.104), kind=kLoop, calls=%fused_computation.1 | loop fusion | flops 1835008 | bytes 917504 | tf_op jit(solution)/shard_map/concatenate | solution.py:300
  28.7 0.4 collective-permute-start.6
  29.1 1.5 %collective-permute-done.6.other0_ref = bf16[64,3584]{1,0:T(8,128)(2,1)S(1)} collective-permute-done((bf16[64,3584]{1,0:T(8,128)(2,1)S(1)}, bf16[64,3584]{1,0:T(8,128)(2,1)S(1)}, u32[]{:S(2)}, u32[]{:S(2)}) %collective-permute-start.6) | collective-permute-done | bytes 458784 | tf_op jit(solution)/shard_map/ppermute | solution.py:292
  30.6 0.0 collective-permute-done.7.other1_ref
  30.6 0.0 slice-done.1
  30.6 5.9 %pair_rows.1 = (bf16[64,3584]{1,0:T(8,128)(2,1)S(1)}, bf16[64,3584]{1,0:T(8,128)(2,1)S(1)}, bf16[64,3584]{1,0:T(8,128)(2,1)S(1)}, bf16[64,3584]{1,0:T(8,128)(2,1)S(1)}) custom-call(s32[1]{0:T(128)} %bitcast.place_ref, bf16[64,3584]{1,0:T(8,128)(2,1)S(1)} %pad_maximum_fusion.1.own0_ref, bf16[64,3712]{1,0:T(8,128)(2,1)S(1)} %pad_maximum_fusion.own1_ref, ...), custom_call_target="tpu_custom_call" | custom-call | tf_op jit(solution)/shard_map/pair_rows/pallas_call | solution.py:237
  36.6 0.4 collective-permute-start.8
  37.0 0.2 collective-permute-start.12
  37.1 1.3 %collective-permute-done.8 = bf16[64,3584]{1,0:T(8,128)(2,1)S(1)} collective-permute-done((bf16[64,3584]{1,0:T(8,128)(2,1)S(1)}, bf16[64,3584]{1,0:T(8,128)(2,1)S(1)}, u32[]{:S(2)}, u32[]{:S(2)}) %collective-permute-start.8) | collective-permute-done | bytes 458784 | tf_op jit(solution)/shard_map/ppermute | solution.py:292
  38.4 0.1 add_convert_fusion.1
  38.5 1.4 %collective-permute-start.9 = (bf16[32,3584]{1,0:T(8,128)(2,1)S(1)}, bf16[32,3584]{1,0:T(8,128)(2,1)S(1)}, u32[]{:S(2)}, u32[]{:S(2)}) collective-permute-start(bf16[32,3584]{1,0:T(8,128)(2,1)S(1)} %get-tuple-element.29), channel_id=1, source_target_pairs={{0,8},{1,9},{2,10},{3,11},{4,5},{5,4},{6,7},{7,6},{8,0},{9,1},{10,... | collective-permute-start | bytes 688136 | tf_op jit(solution)/shard_map/ppermute | solution.py:292
  40.0 0.0 collective-permute-done.12
  40.0 0.1 add_convert_fusion
  40.1 0.7 %collective-permute-start.13 = (bf16[32,3584]{1,0:T(8,128)(2,1)S(1)}, bf16[32,3584]{1,0:T(8,128)(2,1)S(1)}, u32[]{:S(2)}, u32[]{:S(2)}) collective-permute-start(bf16[32,3584]{1,0:T(8,128)(2,1)S(1)} %get-tuple-element.31), channel_id=1, source_target_pairs={{0,1},{1,0},{2,3},{3,2},{4,12},{5,13},{6,14},{7,15},{8,9},{9,8},{1... | collective-permute-start | bytes 688136 | tf_op jit(solution)/shard_map/ppermute | solution.py:292
  40.8 6.3 %collective-permute-done.9 = bf16[32,3584]{1,0:T(8,128)(2,1)S(1)} collective-permute-done((bf16[32,3584]{1,0:T(8,128)(2,1)S(1)}, bf16[32,3584]{1,0:T(8,128)(2,1)S(1)}, u32[]{:S(2)}, u32[]{:S(2)}) %collective-permute-start.9) | collective-permute-done | bytes 229408 | tf_op jit(solution)/shard_map/ppermute | solution.py:292
  47.1 0.1 collective-permute-start.10
  47.2 0.0 collective-permute-done.13
  47.3 3.3 %collective-permute-start.14 = (bf16[16,3584]{1,0:T(8,128)(2,1)S(1)}, bf16[16,3584]{1,0:T(8,128)(2,1)S(1)}, u32[]{:S(2)}, u32[]{:S(2)}) collective-permute-start(bf16[16,3584]{1,0:T(8,128)(2,1)S(1)} %get-tuple-element.35), channel_id=1, source_target_pairs={{0,2},{1,3},{2,0},{3,1},{4,5},{5,4},{6,7},{7,6},{8,10},{9,11},{10,... | collective-permute-start | bytes 344072 | tf_op jit(solution)/shard_map/ppermute | solution.py:292
  50.6 3.1 %collective-permute-done.10 = bf16[16,3584]{1,0:T(8,128)(2,1)S(1)} collective-permute-done((bf16[16,3584]{1,0:T(8,128)(2,1)S(1)}, bf16[16,3584]{1,0:T(8,128)(2,1)S(1)}, u32[]{:S(2)}, u32[]{:S(2)}) %collective-permute-start.10) | collective-permute-done | bytes 114720 | tf_op jit(solution)/shard_map/ppermute | solution.py:292
  53.6 1.9 %collective-permute-start.11 = (bf16[8,3584]{1,0:T(8,128)(2,1)S(1)}, bf16[8,3584]{1,0:T(8,128)(2,1)S(1)}, u32[]{:S(2)}, u32[]{:S(2)}) collective-permute-start(bf16[8,3584]{1,0:T(8,128)(2,1)S(1)} %fusion.5), channel_id=1, source_target_pairs={{0,2},{1,3},{2,0},{3,1},{4,12},{5,13},{6,14},{7,15},{8,10},{9,11},... | collective-permute-start | bytes 172040 | tf_op jit(solution)/shard_map/ppermute | solution.py:292
  55.5 0.0 collective-permute-done.14
  55.6 0.5 collective-permute-start.15
  56.0 4.0 %collective-permute-done.11 = bf16[8,3584]{1,0:T(8,128)(2,1)S(1)} collective-permute-done((bf16[8,3584]{1,0:T(8,128)(2,1)S(1)}, bf16[8,3584]{1,0:T(8,128)(2,1)S(1)}, u32[]{:S(2)}, u32[]{:S(2)}) %collective-permute-start.11) | collective-permute-done | bytes 57376 | tf_op jit(solution)/shard_map/ppermute | solution.py:292
  60.0 0.0 collective-permute-done.15
  60.1 0.7 %pad_maximum_fusion.6 = bf16[8,7168]{1,0:T(8,128)(2,1)} fusion(bf16[8,3584]{1,0:T(8,128)(2,1)S(1)} %fusion.4, bf16[8,3584]{1,0:T(8,128)(2,1)S(1)} %fusion.7), kind=kLoop, calls=%fused_computation.26 | loop fusion | flops 229376 | bytes 229376 | tf_op jit(solution)/shard_map/concatenate | solution.py:355
  (16 shorter events, 0.2 us)
Async XLA Ops:
  1.1 5.6 %collective-permute-start.2 = (bf16[8,3712]{1,0:T(8,128)(2,1)S(1)}, bf16[8,3712]{1,0:T(8,128)(2,1)S(1)}, u32[]{:S(2)}, u32[]{:S(2)}) collective-permute-start(bf16[8,3712]{1,0:T(8,128)(2,1)S(1)} %slice.105), channel_id=1, source_target_pairs={{0,8},{1,9},{2,10},{3,11},{4,6},{5,7},{6,4},{7,5},{8,0},{9,1},{10,... | collective-permute-start | bytes 178184 | tf_op jit(solution)/shard_map/ppermute | solution.py:292
  4.1 5.4 %collective-permute-start = (bf16[8,3584]{1,0:T(8,128)(2,1)S(1)}, bf16[8,3584]{1,0:T(8,128)(2,1)S(1)}, u32[]{:S(2)}, u32[]{:S(2)}) collective-permute-start(bf16[8,3584]{1,0:T(8,128)(2,1)S(1)} %slice.104), channel_id=1, source_target_pairs={{0,2},{1,3},{2,0},{3,1},{4,12},{5,13},{6,14},{7,15},{8,10},{9,11},... | collective-permute-start | bytes 172040 | tf_op jit(solution)/shard_map/ppermute | solution.py:292
  6.7 10.5 %collective-permute-start.3 = (bf16[16,3712]{1,0:T(8,128)(2,1)S(1)}, bf16[16,3712]{1,0:T(8,128)(2,1)S(1)}, u32[]{:S(2)}, u32[]{:S(2)}) collective-permute-start(bf16[16,3712]{1,0:T(8,128)(2,1)S(1)} %pad_maximum_fusion.4), channel_id=1, source_target_pairs={{0,2},{1,3},{2,0},{3,1},{4,5},{5,4},{6,7},{7,6},{8,10},{9,11},{10,... | collective-permute-start | bytes 356360 | tf_op jit(solution)/shard_map/ppermute | solution.py:292
  9.5 7.8 %collective-permute-start.1 = (bf16[16,3584]{1,0:T(8,128)(2,1)S(1)}, bf16[16,3584]{1,0:T(8,128)(2,1)S(1)}, u32[]{:S(2)}, u32[]{:S(2)}) collective-permute-start(bf16[16,3584]{1,0:T(8,128)(2,1)S(1)} %pad_maximum_fusion.5), channel_id=1, source_target_pairs={{0,1},{1,0},{2,3},{3,2},{4,6},{5,7},{6,4},{7,5},{8,9},{9,8},{10,11... | collective-permute-start | bytes 344072 | tf_op jit(solution)/shard_map/ppermute | solution.py:292
  14.3 2.9 %copy-start = (bf16[7168,512]{1,0:T(8,128)(2,1)}, bf16[7168,512]{1,0:T(8,128)(2,1)S(1)}, u32[]{:S(2)}) copy-start(bf16[7168,512]{1,0:T(8,128)(2,1)S(1)} %load_up.1.up_ref) | copy-start | bytes 22020100
  17.2 1.2 %copy-start.1 = (bf16[16,3584]{1,0:T(8,128)(2,1)}, bf16[16,3584]{1,0:T(8,128)(2,1)S(1)}, u32[]{:S(2)}) copy-start(bf16[16,3584]{1,0:T(8,128)(2,1)S(1)} %collective-permute-done.1) | copy-start | bytes 344068
  18.0 8.5 %collective-permute-start.5 = (bf16[32,3712]{1,0:T(8,128)(2,1)}, bf16[32,3712]{1,0:T(8,128)(2,1)}, u32[]{:S(2)}, u32[]{:S(2)}) collective-permute-start(bf16[32,3712]{1,0:T(8,128)(2,1)} %pad_maximum_fusion.2), channel_id=1, source_target_pairs={{0,1},{1,0},{2,3},{3,2},{4,12},{5,13},{6,14},{7,15},{8,9},{9,8},{1... | collective-permute-start | bytes 712712 | tf_op jit(solution)/shard_map/ppermute | solution.py:292
  18.4 12.2 %slice-start = ((s8[7340032]{0:T(1024)(128)(4,1)}), s8[3145728]{0:T(1024)(128)(4,1)S(1)}, s32[]{:S(2)}) async-start(s8[7340032]{0:T(1024)(128)(4,1)} %bitcast.6), calls=%async_computation | async-start | bytes 6291456
  19.2 6.3 %collective-permute-start.4 = (bf16[32,3584]{1,0:T(8,128)(2,1)}, bf16[32,3584]{1,0:T(8,128)(2,1)}, u32[]{:S(2)}, u32[]{:S(2)}) collective-permute-start(bf16[32,3584]{1,0:T(8,128)(2,1)} %pad_maximum_fusion.3), channel_id=1, source_target_pairs={{0,8},{1,9},{2,10},{3,11},{4,5},{5,4},{6,7},{7,6},{8,0},{9,1},{10,... | collective-permute-start | bytes 688136 | tf_op jit(solution)/shard_map/ppermute | solution.py:292
  20.7 7.1 %copy-start.2 = (bf16[16,3584]{1,0:T(8,128)(2,1)S(1)}, bf16[16,3584]{1,0:T(8,128)(2,1)}, u32[]{:S(2)}) copy-start(bf16[16,3584]{1,0:T(8,128)(2,1)} %copy-done.1) | copy-start | bytes 344068
  20.7 9.9 %slice-start.1 = ((s8[7340032]{0:T(1024)(128)(4,1)}), s8[4194304]{0:T(1024)(128)(4,1)S(1)}, s32[]{:S(2)}) async-start(s8[7340032]{0:T(1024)(128)(4,1)} %bitcast.6), calls=%async_computation.1 | async-start | bytes 8388608
  27.5 3.1 %collective-permute-start.7 = (bf16[64,3712]{1,0:T(8,128)(2,1)S(1)}, bf16[64,3712]{1,0:T(8,128)(2,1)S(1)}, u32[]{:S(2)}, u32[]{:S(2)}) collective-permute-start(bf16[64,3712]{1,0:T(8,128)(2,1)S(1)} %pad_maximum_fusion.own1_ref), channel_id=1, source_target_pairs={{0,4},{1,5},{2,6},{3,7},{4,0},{5,1},{6,2},{7,3},{8,12},{9,13},{10,... | collective-permute-start | bytes 1425416 | tf_op jit(solution)/shard_map/ppermute | solution.py:292
  28.7 1.9 %collective-permute-start.6 = (bf16[64,3584]{1,0:T(8,128)(2,1)S(1)}, bf16[64,3584]{1,0:T(8,128)(2,1)S(1)}, u32[]{:S(2)}, u32[]{:S(2)}) collective-permute-start(bf16[64,3584]{1,0:T(8,128)(2,1)S(1)} %pad_maximum_fusion.1.own0_ref), channel_id=1, source_target_pairs={{0,4},{1,5},{2,6},{3,7},{4,0},{5,1},{6,2},{7,3},{8,12},{9,13},{10,... | collective-permute-start | bytes 1376264 | tf_op jit(solution)/shard_map/ppermute | solution.py:292
  36.6 1.9 %collective-permute-start.8 = (bf16[64,3584]{1,0:T(8,128)(2,1)S(1)}, bf16[64,3584]{1,0:T(8,128)(2,1)S(1)}, u32[]{:S(2)}, u32[]{:S(2)}) collective-permute-start(bf16[64,3584]{1,0:T(8,128)(2,1)S(1)} %get-tuple-element.26), channel_id=1, source_target_pairs={{0,4},{1,5},{2,6},{3,7},{4,0},{5,1},{6,2},{7,3},{8,12},{9,13},{10,... | collective-permute-start | bytes 1376264 | tf_op jit(solution)/shard_map/ppermute | solution.py:292
  37.0 3.0 %collective-permute-start.12 = (bf16[64,3584]{1,0:T(8,128)(2,1)S(1)}, bf16[64,3584]{1,0:T(8,128)(2,1)S(1)}, u32[]{:S(2)}, u32[]{:S(2)}) collective-permute-start(bf16[64,3584]{1,0:T(8,128)(2,1)S(1)} %get-tuple-element.28), channel_id=1, source_target_pairs={{0,4},{1,5},{2,6},{3,7},{4,0},{5,1},{6,2},{7,3},{8,12},{9,13},{10,... | collective-permute-start | bytes 1376264 | tf_op jit(solution)/shard_map/ppermute | solution.py:292
  38.5 8.5 %collective-permute-start.9 = (bf16[32,3584]{1,0:T(8,128)(2,1)S(1)}, bf16[32,3584]{1,0:T(8,128)(2,1)S(1)}, u32[]{:S(2)}, u32[]{:S(2)}) collective-permute-start(bf16[32,3584]{1,0:T(8,128)(2,1)S(1)} %get-tuple-element.29), channel_id=1, source_target_pairs={{0,8},{1,9},{2,10},{3,11},{4,5},{5,4},{6,7},{7,6},{8,0},{9,1},{10,... | collective-permute-start | bytes 688136 | tf_op jit(solution)/shard_map/ppermute | solution.py:292
  40.1 7.1 %collective-permute-start.13 = (bf16[32,3584]{1,0:T(8,128)(2,1)S(1)}, bf16[32,3584]{1,0:T(8,128)(2,1)S(1)}, u32[]{:S(2)}, u32[]{:S(2)}) collective-permute-start(bf16[32,3584]{1,0:T(8,128)(2,1)S(1)} %get-tuple-element.31), channel_id=1, source_target_pairs={{0,1},{1,0},{2,3},{3,2},{4,12},{5,13},{6,14},{7,15},{8,9},{9,8},{1... | collective-permute-start | bytes 688136 | tf_op jit(solution)/shard_map/ppermute | solution.py:292
  47.1 6.5 %collective-permute-start.10 = (bf16[16,3584]{1,0:T(8,128)(2,1)S(1)}, bf16[16,3584]{1,0:T(8,128)(2,1)S(1)}, u32[]{:S(2)}, u32[]{:S(2)}) collective-permute-start(bf16[16,3584]{1,0:T(8,128)(2,1)S(1)} %get-tuple-element.33), channel_id=1, source_target_pairs={{0,1},{1,0},{2,3},{3,2},{4,6},{5,7},{6,4},{7,5},{8,9},{9,8},{10,11... | collective-permute-start | bytes 344072 | tf_op jit(solution)/shard_map/ppermute | solution.py:292
  47.3 8.3 %collective-permute-start.14 = (bf16[16,3584]{1,0:T(8,128)(2,1)S(1)}, bf16[16,3584]{1,0:T(8,128)(2,1)S(1)}, u32[]{:S(2)}, u32[]{:S(2)}) collective-permute-start(bf16[16,3584]{1,0:T(8,128)(2,1)S(1)} %get-tuple-element.35), channel_id=1, source_target_pairs={{0,2},{1,3},{2,0},{3,1},{4,5},{5,4},{6,7},{7,6},{8,10},{9,11},{10,... | collective-permute-start | bytes 344072 | tf_op jit(solution)/shard_map/ppermute | solution.py:292
  53.6 6.4 %collective-permute-start.11 = (bf16[8,3584]{1,0:T(8,128)(2,1)S(1)}, bf16[8,3584]{1,0:T(8,128)(2,1)S(1)}, u32[]{:S(2)}, u32[]{:S(2)}) collective-permute-start(bf16[8,3584]{1,0:T(8,128)(2,1)S(1)} %fusion.5), channel_id=1, source_target_pairs={{0,2},{1,3},{2,0},{3,1},{4,12},{5,13},{6,14},{7,15},{8,10},{9,11},... | collective-permute-start | bytes 172040 | tf_op jit(solution)/shard_map/ppermute | solution.py:292
  55.6 4.5 %collective-permute-start.15 = (bf16[8,3584]{1,0:T(8,128)(2,1)S(1)}, bf16[8,3584]{1,0:T(8,128)(2,1)S(1)}, u32[]{:S(2)}, u32[]{:S(2)}) collective-permute-start(bf16[8,3584]{1,0:T(8,128)(2,1)S(1)} %fusion.2), channel_id=1, source_target_pairs={{0,8},{1,9},{2,10},{3,11},{4,6},{5,7},{6,4},{7,5},{8,0},{9,1},{10,... | collective-permute-start | bytes 172040 | tf_op jit(solution)/shard_map/ppermute | solution.py:292

commit v10 on v9

--- a/solution.py
+++ b/solution.py
@@ -329,8 +329,8 @@
     own = [packed[:, :cut], packed[:, cut:]]
     loads = (
         lambda *ready: None,
+        lambda *ready: load_gate(after(place, *ready), gate, gate_shared, up_shared, share),
         lambda *ready: load_up(after(up, *ready)),
-        lambda *ready: load_gate(after(place, *ready), gate, gate_shared, up_shared, share),
     )
     loaded = []
     for phase, load in zip(PHASES, loads):
@@ -340,7 +340,7 @@
             got, weights = lax.optimization_barrier((got, weights))
             loaded.append(weights)
         own = [stack(part, add) for part, add in zip(own, got)]
-    up, first = loaded
+    first, up = loaded
     other = [flipped(part, CORE, CORE) for part in own]
 
     outs = pair_rows(place, own + other, first, up, down, down_shared, share)

time: 60.9 us -> 57 us (0.936)
  starting transfers between devices: 21.1 us -> 24.6 us
  other arithmetic: 4.43 us -> 1.15 us
  local copies, waits for them, and re-layouts: 2.96 us -> 0.01 us
  waiting for transfers between devices: 17.5 us -> 16.5 us
    ppermute x16, starting transfers between devices: 21.1 us -> 24.6 us  [flipped(): return lax.ppermute(value, ('node', 'local'), pairs)]
    concatenate x6, other arithmetic: 3.43 us -> 0.14 us  [stack(): return jnp.concatenate(values, axis=0)]
    unnamed x10 -> x0, local copies, waits for them, and re-layouts: 2.95 us -> none
    ppermute x16, waiting for transfers between devices: 17.5 us -> 16.5 us  [flipped(): return lax.ppermute(value, ('node', 'local'), pairs)]
  transfers between devices with their start and end apart: 16 -> 16, of which waited for: 7 -> 9; matrix products, arithmetic and copies ran while one was open for 3% -> 1% of each run, Pallas kernels for 13% -> 13%
where the time goes in v10:
time: 57 us; the launch traced here: 56.9 us
  starting transfers between devices  24.6 us (43%)
  waiting for transfers between devices  16.5 us (29%)
  Pallas kernels  14.5 us (25%)
  other arithmetic  1.15 us (2%)
    ppermute x16, starting transfers between devices, flipped(): return lax.ppermute(value, ('node', 'local'), pairs)  24.6 us
    ppermute x16, waiting for transfers between devices, flipped(): return lax.ppermute(value, ('node', 'local'), pairs)  16.5 us
    pallas_call x1, Pallas kernels, pair_rows(): pl.pallas_call(functools.partial(pair_kernel, share), in_specs=[SMEM_SPEC...  5.95 us
    pallas_call x1, Pallas kernels, load_gate(): pl.pallas_call(functools.partial(load_gate_kernel, share), in_specs=[SMEM...  4.31 us
    pallas_call x1, Pallas kernels, load_up(): pl.pallas_call(load_up_kernel, in_specs=[ANY_SPEC], out_specs=VMEM_SPEC,...  3.17 us
  transfers between devices with their start and end apart: 16, of which 9 were waited for; matrix products, arithmetic and copies ran while one was open for 1% of the time, Pallas kernels for 13%

profile of v10, /device:TPU:0, one launch (start us, length us, event | category | flops | bytes accessed | tf_op | source)
XLA Modules:
  0.0 56.9 jit_solution(2128483931273346899)
XLA Ops:
  0.0 1.1 %pack_rows.1 = bf16[8,7296]{1,0:T(8,128)(2,1)S(1)} custom-call(bf16[8,7168]{1,0:T(8,128)(2,1)} %tokens_ref.1, s32[4,8]{1,0:T(4,128)} %bitcast.9, bf16[4,8]{1,0:T(4,128)(2,1)} %bitcast.10), custom_call_target="tpu_custom_call" | custom-call | tf_op jit(solution)/shard_map/pack_rows/pallas_call | solution.py:48
  1.1 3.0 %collective-permute-start.2 = (bf16[8,3712]{1,0:T(8,128)(2,1)S(1)}, bf16[8,3712]{1,0:T(8,128)(2,1)S(1)}, u32[]{:S(2)}, u32[]{:S(2)}) collective-permute-start(bf16[8,3712]{1,0:T(8,128)(2,1)S(1)} %slice.105), channel_id=1, source_target_pairs={{0,8},{1,9},{2,10},{3,11},{4,6},{5,7},{6,4},{7,5},{8,0},{9,1},{10,... | collective-permute-start | bytes 178184 | tf_op jit(solution)/shard_map/ppermute | solution.py:292
  4.1 2.6 %collective-permute-start = (bf16[8,3584]{1,0:T(8,128)(2,1)S(1)}, bf16[8,3584]{1,0:T(8,128)(2,1)S(1)}, u32[]{:S(2)}, u32[]{:S(2)}) collective-permute-start(bf16[8,3584]{1,0:T(8,128)(2,1)S(1)} %slice.104), channel_id=1, source_target_pairs={{0,2},{1,3},{2,0},{3,1},{4,12},{5,13},{6,14},{7,15},{8,10},{9,11},... | collective-permute-start | bytes 172040 | tf_op jit(solution)/shard_map/ppermute | solution.py:292
  6.7 0.0 collective-permute-done.2
  6.7 2.8 %collective-permute-start.3 = (bf16[16,3712]{1,0:T(8,128)(2,1)S(1)}, bf16[16,3712]{1,0:T(8,128)(2,1)S(1)}, u32[]{:S(2)}, u32[]{:S(2)}) collective-permute-start(bf16[16,3712]{1,0:T(8,128)(2,1)S(1)} %pad_maximum_fusion.4), channel_id=1, source_target_pairs={{0,2},{1,3},{2,0},{3,1},{4,5},{5,4},{6,7},{7,6},{8,10},{9,11},{10,... | collective-permute-start | bytes 356360 | tf_op jit(solution)/shard_map/ppermute | solution.py:292
  9.5 0.0 collective-permute-done
  9.5 1.6 %collective-permute-start.1 = (bf16[16,3584]{1,0:T(8,128)(2,1)S(1)}, bf16[16,3584]{1,0:T(8,128)(2,1)S(1)}, u32[]{:S(2)}, u32[]{:S(2)}) collective-permute-start(bf16[16,3584]{1,0:T(8,128)(2,1)S(1)} %pad_maximum_fusion.5), channel_id=1, source_target_pairs={{0,1},{1,0},{2,3},{3,2},{4,6},{5,7},{6,4},{7,5},{8,9},{9,8},{10,11... | collective-permute-start | bytes 344072 | tf_op jit(solution)/shard_map/ppermute | solution.py:292
  11.1 4.3 %load_gate.1.first_ref = bf16[7168,768]{1,0:T(8,128)(2,1)S(1)} custom-call(s32[1]{0:T(128)} %bitcast.place_ref, bf16[7168,512]{1,0:T(8,128)(2,1)} %bitcast.7, bf16[7168,512]{1,0:T(8,128)(2,1)} %sgate_ref.1, bf16[7168,512]{1,0:T(8,128)(2,1)} %sup_ref.1), custom_call_target="tpu_custom_call" | custom-call | bytes 22020096 | tf_op jit(solution)/shard_map/load_gate/pallas_call | solution.py:78
  15.4 0.0 collective-permute-done.1
  15.5 0.3 collective-permute-done.3
  15.8 1.1 %collective-permute-start.5 = (bf16[32,3712]{1,0:T(8,128)(2,1)S(1)}, bf16[32,3712]{1,0:T(8,128)(2,1)S(1)}, u32[]{:S(2)}, u32[]{:S(2)}) collective-permute-start(bf16[32,3712]{1,0:T(8,128)(2,1)S(1)} %pad_maximum_fusion.2), channel_id=1, source_target_pairs={{0,1},{1,0},{2,3},{3,2},{4,12},{5,13},{6,14},{7,15},{8,9},{9,8},{1... | collective-permute-start | bytes 712712 | tf_op jit(solution)/shard_map/ppermute | solution.py:292
  16.9 1.6 %collective-permute-start.4 = (bf16[32,3584]{1,0:T(8,128)(2,1)S(1)}, bf16[32,3584]{1,0:T(8,128)(2,1)S(1)}, u32[]{:S(2)}, u32[]{:S(2)}) collective-permute-start(bf16[32,3584]{1,0:T(8,128)(2,1)S(1)} %pad_maximum_fusion.3), channel_id=1, source_target_pairs={{0,8},{1,9},{2,10},{3,11},{4,5},{5,4},{6,7},{7,6},{8,0},{9,1},{10,... | collective-permute-start | bytes 688136 | tf_op jit(solution)/shard_map/ppermute | solution.py:292
  18.5 3.2 %load_up.1.up_ref = bf16[7168,512]{1,0:T(8,128)(2,1)S(1)} custom-call(bf16[7168,512]{1,0:T(8,128)(2,1)} %bitcast.6), custom_call_target="tpu_custom_call" | custom-call | bytes 14680064 | tf_op jit(solution)/shard_map/load_up/pallas_call | solution.py:106
  21.7 2.1 %collective-permute-done.4 = bf16[32,3584]{1,0:T(8,128)(2,1)S(1)} collective-permute-done((bf16[32,3584]{1,0:T(8,128)(2,1)S(1)}, bf16[32,3584]{1,0:T(8,128)(2,1)S(1)}, u32[]{:S(2)}, u32[]{:S(2)}) %collective-permute-start.4) | collective-permute-done | bytes 229408 | tf_op jit(solution)/shard_map/ppermute | solution.py:292
  23.7 0.1 collective-permute-done.5
  23.8 0.5 collective-permute-start.7
  24.4 0.1 collective-permute-start.6
  24.5 1.9 %collective-permute-done.6.other0_ref = bf16[64,3584]{1,0:T(8,128)(2,1)S(1)} collective-permute-done((bf16[64,3584]{1,0:T(8,128)(2,1)S(1)}, bf16[64,3584]{1,0:T(8,128)(2,1)S(1)}, u32[]{:S(2)}, u32[]{:S(2)}) %collective-permute-start.6) | collective-permute-done | bytes 458784 | tf_op jit(solution)/shard_map/ppermute | solution.py:292
  26.5 0.0 collective-permute-done.7.other1_ref
  26.5 5.9 %pair_rows.1 = (bf16[64,3584]{1,0:T(8,128)(2,1)S(1)}, bf16[64,3584]{1,0:T(8,128)(2,1)S(1)}, bf16[64,3584]{1,0:T(8,128)(2,1)S(1)}, bf16[64,3584]{1,0:T(8,128)(2,1)S(1)}) custom-call(s32[1]{0:T(128)} %bitcast.place_ref, bf16[64,3584]{1,0:T(8,128)(2,1)S(1)} %pad_maximum_fusion.1.own0_ref, bf16[64,3712]{1,0:T(8,128)(2,1)S(1)} %pad_maximum_fusion.own1_ref, ...), custom_call_target="tpu_custom_call" | custom-call | tf_op jit(solution)/shard_map/pair_rows/pallas_call | solution.py:237
  32.4 0.4 collective-permute-start.8
  32.9 0.1 collective-permute-start.12
  33.0 1.3 %collective-permute-done.8 = bf16[64,3584]{1,0:T(8,128)(2,1)S(1)} collective-permute-done((bf16[64,3584]{1,0:T(8,128)(2,1)S(1)}, bf16[64,3584]{1,0:T(8,128)(2,1)S(1)}, u32[]{:S(2)}, u32[]{:S(2)}) %collective-permute-start.8) | collective-permute-done | bytes 458784 | tf_op jit(solution)/shard_map/ppermute | solution.py:292
  34.3 0.1 add_convert_fusion.1
  34.4 1.8 %collective-permute-start.9 = (bf16[32,3584]{1,0:T(8,128)(2,1)S(1)}, bf16[32,3584]{1,0:T(8,128)(2,1)S(1)}, u32[]{:S(2)}, u32[]{:S(2)}) collective-permute-start(bf16[32,3584]{1,0:T(8,128)(2,1)S(1)} %get-tuple-element.29), channel_id=1, source_target_pairs={{0,8},{1,9},{2,10},{3,11},{4,5},{5,4},{6,7},{7,6},{8,0},{9,1},{10,... | collective-permute-start | bytes 688136 | tf_op jit(solution)/shard_map/ppermute | solution.py:292
  36.2 0.0 collective-permute-done.12
  36.2 0.1 add_convert_fusion
  36.3 0.4 collective-permute-start.13
  36.7 5.7 %collective-permute-done.9 = bf16[32,3584]{1,0:T(8,128)(2,1)S(1)} collective-permute-done((bf16[32,3584]{1,0:T(8,128)(2,1)S(1)}, bf16[32,3584]{1,0:T(8,128)(2,1)S(1)}, u32[]{:S(2)}, u32[]{:S(2)}) %collective-permute-start.9) | collective-permute-done | bytes 229408 | tf_op jit(solution)/shard_map/ppermute | solution.py:292
  42.4 2.0 %collective-permute-start.10 = (bf16[16,3584]{1,0:T(8,128)(2,1)S(1)}, bf16[16,3584]{1,0:T(8,128)(2,1)S(1)}, u32[]{:S(2)}, u32[]{:S(2)}) collective-permute-start(bf16[16,3584]{1,0:T(8,128)(2,1)S(1)} %get-tuple-element.33), channel_id=1, source_target_pairs={{0,1},{1,0},{2,3},{3,2},{4,6},{5,7},{6,4},{7,5},{8,9},{9,8},{10,11... | collective-permute-start | bytes 344072 | tf_op jit(solution)/shard_map/ppermute | solution.py:292
  44.5 0.0 collective-permute-done.13
  44.5 0.1 fusion
  44.5 2.7 %collective-permute-start.14 = (bf16[16,3584]{1,0:T(8,128)(2,1)S(1)}, bf16[16,3584]{1,0:T(8,128)(2,1)S(1)}, u32[]{:S(2)}, u32[]{:S(2)}) collective-permute-start(bf16[16,3584]{1,0:T(8,128)(2,1)S(1)} %get-tuple-element.35), channel_id=1, source_target_pairs={{0,2},{1,3},{2,0},{3,1},{4,5},{5,4},{6,7},{7,6},{8,10},{9,11},{10,... | collective-permute-start | bytes 344072 | tf_op jit(solution)/shard_map/ppermute | solution.py:292
  47.2 1.0 %collective-permute-done.10 = bf16[16,3584]{1,0:T(8,128)(2,1)S(1)} collective-permute-done((bf16[16,3584]{1,0:T(8,128)(2,1)S(1)}, bf16[16,3584]{1,0:T(8,128)(2,1)S(1)}, u32[]{:S(2)}, u32[]{:S(2)}) %collective-permute-start.10) | collective-permute-done | bytes 114720 | tf_op jit(solution)/shard_map/ppermute | solution.py:292
  48.2 3.7 %collective-permute-start.11 = (bf16[8,3584]{1,0:T(8,128)(2,1)S(1)}, bf16[8,3584]{1,0:T(8,128)(2,1)S(1)}, u32[]{:S(2)}, u32[]{:S(2)}) collective-permute-start(bf16[8,3584]{1,0:T(8,128)(2,1)S(1)} %fusion.5), channel_id=1, source_target_pairs={{0,2},{1,3},{2,0},{3,1},{4,12},{5,13},{6,14},{7,15},{8,10},{9,11},... | collective-permute-start | bytes 172040 | tf_op jit(solution)/shard_map/ppermute | solution.py:292
  51.9 0.0 collective-permute-done.14
  52.0 0.1 collective-permute-start.15
  52.0 2.1 %collective-permute-done.11 = bf16[8,3584]{1,0:T(8,128)(2,1)S(1)} collective-permute-done((bf16[8,3584]{1,0:T(8,128)(2,1)S(1)}, bf16[8,3584]{1,0:T(8,128)(2,1)S(1)}, u32[]{:S(2)}, u32[]{:S(2)}) %collective-permute-start.11) | collective-permute-done | bytes 57376 | tf_op jit(solution)/shard_map/ppermute | solution.py:292
  54.1 2.1 %collective-permute-done.15 = bf16[8,3584]{1,0:T(8,128)(2,1)S(1)} collective-permute-done((bf16[8,3584]{1,0:T(8,128)(2,1)S(1)}, bf16[8,3584]{1,0:T(8,128)(2,1)S(1)}, u32[]{:S(2)}, u32[]{:S(2)}) %collective-permute-start.15) | collective-permute-done | bytes 57376 | tf_op jit(solution)/shard_map/ppermute | solution.py:292
  56.2 0.7 %pad_maximum_fusion.6 = bf16[8,7168]{1,0:T(8,128)(2,1)} fusion(bf16[8,3584]{1,0:T(8,128)(2,1)S(1)} %fusion.4, bf16[8,3584]{1,0:T(8,128)(2,1)S(1)} %fusion.7), kind=kLoop, calls=%fused_computation.26 | loop fusion | flops 229376 | bytes 229376 | tf_op jit(solution)/shard_map/concatenate | solution.py:355
  (13 shorter events, 0.3 us)
Async XLA Ops:
  1.1 5.6 %collective-permute-start.2 = (bf16[8,3712]{1,0:T(8,128)(2,1)S(1)}, bf16[8,3712]{1,0:T(8,128)(2,1)S(1)}, u32[]{:S(2)}, u32[]{:S(2)}) collective-permute-start(bf16[8,3712]{1,0:T(8,128)(2,1)S(1)} %slice.105), channel_id=1, source_target_pairs={{0,8},{1,9},{2,10},{3,11},{4,6},{5,7},{6,4},{7,5},{8,0},{9,1},{10,... | collective-permute-start | bytes 178184 | tf_op jit(solution)/shard_map/ppermute | solution.py:292
  4.1 5.4 %collective-permute-start = (bf16[8,3584]{1,0:T(8,128)(2,1)S(1)}, bf16[8,3584]{1,0:T(8,128)(2,1)S(1)}, u32[]{:S(2)}, u32[]{:S(2)}) collective-permute-start(bf16[8,3584]{1,0:T(8,128)(2,1)S(1)} %slice.104), channel_id=1, source_target_pairs={{0,2},{1,3},{2,0},{3,1},{4,12},{5,13},{6,14},{7,15},{8,10},{9,11},... | collective-permute-start | bytes 172040 | tf_op jit(solution)/shard_map/ppermute | solution.py:292
  6.7 9.1 %collective-permute-start.3 = (bf16[16,3712]{1,0:T(8,128)(2,1)S(1)}, bf16[16,3712]{1,0:T(8,128)(2,1)S(1)}, u32[]{:S(2)}, u32[]{:S(2)}) collective-permute-start(bf16[16,3712]{1,0:T(8,128)(2,1)S(1)} %pad_maximum_fusion.4), channel_id=1, source_target_pairs={{0,2},{1,3},{2,0},{3,1},{4,5},{5,4},{6,7},{7,6},{8,10},{9,11},{10,... | collective-permute-start | bytes 356360 | tf_op jit(solution)/shard_map/ppermute | solution.py:292
  9.5 6.0 %collective-permute-start.1 = (bf16[16,3584]{1,0:T(8,128)(2,1)S(1)}, bf16[16,3584]{1,0:T(8,128)(2,1)S(1)}, u32[]{:S(2)}, u32[]{:S(2)}) collective-permute-start(bf16[16,3584]{1,0:T(8,128)(2,1)S(1)} %pad_maximum_fusion.5), channel_id=1, source_target_pairs={{0,1},{1,0},{2,3},{3,2},{4,6},{5,7},{6,4},{7,5},{8,9},{9,8},{10,11... | collective-permute-start | bytes 344072 | tf_op jit(solution)/shard_map/ppermute | solution.py:292
  15.8 8.0 %collective-permute-start.5 = (bf16[32,3712]{1,0:T(8,128)(2,1)S(1)}, bf16[32,3712]{1,0:T(8,128)(2,1)S(1)}, u32[]{:S(2)}, u32[]{:S(2)}) collective-permute-start(bf16[32,3712]{1,0:T(8,128)(2,1)S(1)} %pad_maximum_fusion.2), channel_id=1, source_target_pairs={{0,1},{1,0},{2,3},{3,2},{4,12},{5,13},{6,14},{7,15},{8,9},{9,8},{1... | collective-permute-start | bytes 712712 | tf_op jit(solution)/shard_map/ppermute | solution.py:292
  16.9 6.8 %collective-permute-start.4 = (bf16[32,3584]{1,0:T(8,128)(2,1)S(1)}, bf16[32,3584]{1,0:T(8,128)(2,1)S(1)}, u32[]{:S(2)}, u32[]{:S(2)}) collective-permute-start(bf16[32,3584]{1,0:T(8,128)(2,1)S(1)} %pad_maximum_fusion.3), channel_id=1, source_target_pairs={{0,8},{1,9},{2,10},{3,11},{4,5},{5,4},{6,7},{7,6},{8,0},{9,1},{10,... | collective-permute-start | bytes 688136 | tf_op jit(solution)/shard_map/ppermute | solution.py:292
  23.8 2.6 %collective-permute-start.7 = (bf16[64,3712]{1,0:T(8,128)(2,1)S(1)}, bf16[64,3712]{1,0:T(8,128)(2,1)S(1)}, u32[]{:S(2)}, u32[]{:S(2)}) collective-permute-start(bf16[64,3712]{1,0:T(8,128)(2,1)S(1)} %pad_maximum_fusion.own1_ref), channel_id=1, source_target_pairs={{0,4},{1,5},{2,6},{3,7},{4,0},{5,1},{6,2},{7,3},{8,12},{9,13},{10,... | collective-permute-start | bytes 1425416 | tf_op jit(solution)/shard_map/ppermute | solution.py:292
  24.4 2.1 %collective-permute-start.6 = (bf16[64,3584]{1,0:T(8,128)(2,1)S(1)}, bf16[64,3584]{1,0:T(8,128)(2,1)S(1)}, u32[]{:S(2)}, u32[]{:S(2)}) collective-permute-start(bf16[64,3584]{1,0:T(8,128)(2,1)S(1)} %pad_maximum_fusion.1.own0_ref), channel_id=1, source_target_pairs={{0,4},{1,5},{2,6},{3,7},{4,0},{5,1},{6,2},{7,3},{8,12},{9,13},{10,... | collective-permute-start | bytes 1376264 | tf_op jit(solution)/shard_map/ppermute | solution.py:292
  32.4 1.9 %collective-permute-start.8 = (bf16[64,3584]{1,0:T(8,128)(2,1)S(1)}, bf16[64,3584]{1,0:T(8,128)(2,1)S(1)}, u32[]{:S(2)}, u32[]{:S(2)}) collective-permute-start(bf16[64,3584]{1,0:T(8,128)(2,1)S(1)} %get-tuple-element.26), channel_id=1, source_target_pairs={{0,4},{1,5},{2,6},{3,7},{4,0},{5,1},{6,2},{7,3},{8,12},{9,13},{10,... | collective-permute-start | bytes 1376264 | tf_op jit(solution)/shard_map/ppermute | solution.py:292
  32.9 3.3 %collective-permute-start.12 = (bf16[64,3584]{1,0:T(8,128)(2,1)S(1)}, bf16[64,3584]{1,0:T(8,128)(2,1)S(1)}, u32[]{:S(2)}, u32[]{:S(2)}) collective-permute-start(bf16[64,3584]{1,0:T(8,128)(2,1)S(1)} %get-tuple-element.28), channel_id=1, source_target_pairs={{0,4},{1,5},{2,6},{3,7},{4,0},{5,1},{6,2},{7,3},{8,12},{9,13},{10,... | collective-permute-start | bytes 1376264 | tf_op jit(solution)/shard_map/ppermute | solution.py:292
  34.4 8.0 %collective-permute-start.9 = (bf16[32,3584]{1,0:T(8,128)(2,1)S(1)}, bf16[32,3584]{1,0:T(8,128)(2,1)S(1)}, u32[]{:S(2)}, u32[]{:S(2)}) collective-permute-start(bf16[32,3584]{1,0:T(8,128)(2,1)S(1)} %get-tuple-element.29), channel_id=1, source_target_pairs={{0,8},{1,9},{2,10},{3,11},{4,5},{5,4},{6,7},{7,6},{8,0},{9,1},{10,... | collective-permute-start | bytes 688136 | tf_op jit(solution)/shard_map/ppermute | solution.py:292
  36.3 8.2 %collective-permute-start.13 = (bf16[32,3584]{1,0:T(8,128)(2,1)S(1)}, bf16[32,3584]{1,0:T(8,128)(2,1)S(1)}, u32[]{:S(2)}, u32[]{:S(2)}) collective-permute-start(bf16[32,3584]{1,0:T(8,128)(2,1)S(1)} %get-tuple-element.31), channel_id=1, source_target_pairs={{0,1},{1,0},{2,3},{3,2},{4,12},{5,13},{6,14},{7,15},{8,9},{9,8},{1... | collective-permute-start | bytes 688136 | tf_op jit(solution)/shard_map/ppermute | solution.py:292
  42.4 5.8 %collective-permute-start.10 = (bf16[16,3584]{1,0:T(8,128)(2,1)S(1)}, bf16[16,3584]{1,0:T(8,128)(2,1)S(1)}, u32[]{:S(2)}, u32[]{:S(2)}) collective-permute-start(bf16[16,3584]{1,0:T(8,128)(2,1)S(1)} %get-tuple-element.33), channel_id=1, source_target_pairs={{0,1},{1,0},{2,3},{3,2},{4,6},{5,7},{6,4},{7,5},{8,9},{9,8},{10,11... | collective-permute-start | bytes 344072 | tf_op jit(solution)/shard_map/ppermute | solution.py:292
  44.5 7.4 %collective-permute-start.14 = (bf16[16,3584]{1,0:T(8,128)(2,1)S(1)}, bf16[16,3584]{1,0:T(8,128)(2,1)S(1)}, u32[]{:S(2)}, u32[]{:S(2)}) collective-permute-start(bf16[16,3584]{1,0:T(8,128)(2,1)S(1)} %get-tuple-element.35), channel_id=1, source_target_pairs={{0,2},{1,3},{2,0},{3,1},{4,5},{5,4},{6,7},{7,6},{8,10},{9,11},{10,... | collective-permute-start | bytes 344072 | tf_op jit(solution)/shard_map/ppermute | solution.py:292
  48.2 5.9 %collective-permute-start.11 = (bf16[8,3584]{1,0:T(8,128)(2,1)S(1)}, bf16[8,3584]{1,0:T(8,128)(2,1)S(1)}, u32[]{:S(2)}, u32[]{:S(2)}) collective-permute-start(bf16[8,3584]{1,0:T(8,128)(2,1)S(1)} %fusion.5), channel_id=1, source_target_pairs={{0,2},{1,3},{2,0},{3,1},{4,12},{5,13},{6,14},{7,15},{8,10},{9,11},... | collective-permute-start | bytes 172040 | tf_op jit(solution)/shard_map/ppermute | solution.py:292
  52.0 4.2 %collective-permute-start.15 = (bf16[8,3584]{1,0:T(8,128)(2,1)S(1)}, bf16[8,3584]{1,0:T(8,128)(2,1)S(1)}, u32[]{:S(2)}, u32[]{:S(2)}) collective-permute-start(bf16[8,3584]{1,0:T(8,128)(2,1)S(1)} %fusion.2), channel_id=1, source_target_pairs={{0,8},{1,9},{2,10},{3,11},{4,6},{5,7},{6,4},{7,5},{8,0},{9,1},{10,... | collective-permute-start | bytes 172040 | tf_op jit(solution)/shard_map/ppermute | solution.py:292

commit v11 on v10

--- a/solution.py
+++ b/solution.py
@@ -124,7 +124,7 @@
     return jnp.sum(jnp.where(lane == node, dense.astype(F32), 0.0), axis=1, keepdims=True)
 
 
-DOWN_PARTS = 4
+DOWN_PARTS = 7
 
 
 def down_scratch(rows, hidden, width):
@@ -187,21 +187,9 @@
         store(at, jnp.dot(act[...], second[:, at], preferred_element_type=F32))
 
 
-def regroup(value, outer, inner):
-    rows = value.shape[0] // (outer * inner)
-    return jnp.concatenate(
-        [
-            value[(o * inner + i) * rows : (o * inner + i + 1) * rows]
-            for i in range(inner)
-            for o in range(outer)
-        ],
-        axis=0,
-    )
-
-
-def reorder(value, turn):
-    value = value.astype(F32)
-    return jnp.where(turn == 1, regroup(value, 2, 4), regroup(value, 4, 2)).astype(BF16)
+def reorder(value):
+    quarter = value.shape[0] // 4
+    return jnp.concatenate([value[i * quarter : (i + 1) * quarter] for i in (0, 2, 1, 3)], axis=0)
 
 
 def pair_kernel(
@@ -213,19 +201,19 @@
         start_group(groups, i)
     half, cut = own0_ref.shape
     x[:half, :cut] = own0_ref[...]
-    odd = place_ref[0] % 2
-    x[:half, cut:] = reorder(own1_ref[...], odd)
+    x[:half, cut:] = reorder(own1_ref[...])
     x[half:, :cut] = other0_ref[...]
-    x[half:, cut:] = reorder(other1_ref[...], 1 - odd)
+    x[half:, cut:] = reorder(other1_ref[...])
 
     def store(at, total):
+        total = total.astype(BF16)
         if at.stop <= cut:
-            own0_out_ref[:, at] = total[:half].astype(BF16)
-            other0_out_ref[:, at] = total[half:].astype(BF16)
+            own0_out_ref[:, at] = total[:half]
+            other0_out_ref[:, at] = total[half:]
         else:
             at = slice(at.start - cut, at.stop - cut)
-            own1_out_ref[:, at] = reorder(total[:half], 1 - odd)
-            other1_out_ref[:, at] = reorder(total[half:], odd)
+            own1_out_ref[:, at] = reorder(total[:half])
+            other1_out_ref[:, at] = reorder(total[half:])
 
     ffn(share, place_ref, x, first_ref, up_ref, act, second, functools.partial(wait_group, groups), store)
 
@@ -233,12 +221,12 @@
 def pair_rows(place, pieces, first, up, down, sdown, share):
     half, cut = pieces[0].shape
     hidden, width = down.shape
-    out = jax.ShapeDtypeStruct((half, cut), BF16)
+    outs = [jax.ShapeDtypeStruct((half, columns), BF16) for columns in (cut, width - cut)] * 2
     return pl.pallas_call(
         functools.partial(pair_kernel, share),
         in_specs=[SMEM_SPEC] + [VMEM_SPEC] * 6 + [ANY_SPEC] * 2,
         out_specs=[VMEM_SPEC] * 4,
-        out_shape=[out] * 4,
+        out_shape=outs,
         scratch_shapes=[pltpu.VMEM((2 * half, width + LANES), BF16)] + down_scratch(2 * half, hidden, width),
         compiler_params=pltpu.CompilerParams(vmem_limit_bytes=24 << 20),
         name="pair_rows",
@@ -283,17 +271,13 @@
     return functools.reduce(lambda a, b: a + b, (t.astype(F32) for t in terms))
 
 
-def flipped(value, even, odd):
-    pairs = []
-    for node in range(4):
-        for local in range(4):
-            node_bits, local_bits = odd if node % 2 else even
-            pairs.append((node * 4 + local, (node ^ node_bits) * 4 + (local ^ local_bits)))
-    return lax.ppermute(value, ("node", "local"), pairs)
+def flipped(value, bits):
+    axis = 0 if bits[0] else 1
+    return lax.ppermute(value, ("node", "local")[axis], [(i, i ^ bits[axis]) for i in range(4)])
 
 
 X, Z1, Z2, CORE = (2, 0), (0, 1), (0, 2), (1, 0)
-PHASES = ((Z2, X), (Z1, Z2), (X, Z1))
+PHASES = ((Z2, Z2), (Z1, X), (X, Z1))
 
 
 def stack(*values):
@@ -325,7 +309,7 @@
         part = block_rows(place, x, first, load_up(up), down, down_shared, share)
         return lax.psum_scatter(part, ("node", "local"), scatter_dimension=0, tiled=True)
 
-    cut = width // 2
+    cut = width * 4 // 7 // LANES * LANES
     own = [packed[:, :cut], packed[:, cut:]]
     loads = (
         lambda *ready: None,
@@ -334,24 +318,24 @@
     )
     loaded = []
     for phase, load in zip(PHASES, loads):
-        got = [flipped(part, *pairs) for part, pairs in zip(own, (phase, phase[::-1]))]
+        got = [flipped(part, pairs) for part, pairs in zip(own, phase)]
         weights = load(*own)
         if weights is not None:
             got, weights = lax.optimization_barrier((got, weights))
             loaded.append(weights)
         own = [stack(part, add) for part, add in zip(own, got)]
     first, up = loaded
-    other = [flipped(part, CORE, CORE) for part in own]
+    other = [flipped(part, CORE) for part in own]
 
     outs = pair_rows(place, own + other, first, up, down, down_shared, share)
 
-    totals = [[own, flipped(other, CORE, CORE)] for own, other in zip(outs[:2], outs[2:])]
+    totals = [[own, flipped(other, CORE)] for own, other in zip(outs[:2], outs[2:])]
     for phase in reversed(PHASES):
-        for i, pairs in enumerate((phase, phase[::-1])):
+        for i, pairs in enumerate(phase):
             total = totals[i]
             half = total[0].shape[0] // 2
             sent = f32_sum(*(t[half:] for t in total)).astype(BF16)
-            totals[i] = [f32_sum(*(t[:half] for t in total)), flipped(sent, *pairs)]
+            totals[i] = [f32_sum(*(t[:half] for t in total)), flipped(sent, pairs)]
     return jnp.concatenate([f32_sum(*total).astype(BF16) for total in totals], axis=1)
 
 

time: 57 us -> 58.2 us (1.021)
  waiting for transfers between devices: 16.5 us -> 20.9 us
  starting transfers between devices: 24.6 us -> 20.7 us
  Pallas kernels: 14.5 us -> 15.1 us
    ppermute x16, waiting for transfers between devices: 16.5 us -> 20.9 us  [flipped(): lax.ppermute(value, ('node', 'local')[axis], [(i, i ^ bits[axis]) for i i...]
    ppermute x16, starting transfers between devices: 24.6 us -> 20.7 us  [flipped(): lax.ppermute(value, ('node', 'local')[axis], [(i, i ^ bits[axis]) for i i...]
    pallas_call x1, Pallas kernels: 5.95 us -> 6.56 us  [pair_rows(): pl.pallas_call(functools.partial(pair_kernel, share), in_specs=[SMEM_SPEC...]
  transfers between devices with their start and end apart: 16 -> 16, of which waited for: 9 -> 10; matrix products, arithmetic and copies ran while one was open for 1% -> 1% of each run, Pallas kernels for 13% -> 13%
where the time goes in v11:
time: 58.2 us; the launch traced here: 58.1 us
  waiting for transfers between devices  20.9 us (36%)
  starting transfers between devices  20.7 us (36%)
  Pallas kernels  15.1 us (26%)
  other arithmetic  1.18 us (2%)
    ppermute x16, waiting for transfers between devices, flipped(): lax.ppermute(value, ('node', 'local')[axis], [(i, i ^ bits[axis]) for i i...  20.9 us
    ppermute x16, starting transfers between devices, flipped(): lax.ppermute(value, ('node', 'local')[axis], [(i, i ^ bits[axis]) for i i...  20.7 us
    pallas_call x1, Pallas kernels, pair_rows(): pl.pallas_call(functools.partial(pair_kernel, share), in_specs=[SMEM_SPEC...  6.56 us
    pallas_call x1, Pallas kernels, load_gate(): pl.pallas_call(functools.partial(load_gate_kernel, share), in_specs=[SMEM...  4.31 us
    pallas_call x1, Pallas kernels, load_up(): pl.pallas_call(load_up_kernel, in_specs=[ANY_SPEC], out_specs=VMEM_SPEC,...  3.17 us
  transfers between devices with their start and end apart: 16, of which 10 were waited for; matrix products, arithmetic and copies ran while one was open for 1% of the time, Pallas kernels for 13%

profile of v11, /device:TPU:0, one launch (start us, length us, event | category | flops | bytes accessed | tf_op | source)
XLA Modules:
  0.0 58.1 jit_solution(18241106354553039581)
XLA Ops:
  0.0 1.1 %pack_rows.1 = bf16[8,7296]{1,0:T(8,128)(2,1)S(1)} custom-call(bf16[8,7168]{1,0:T(8,128)(2,1)} %tokens_ref.1, s32[4,8]{1,0:T(4,128)} %bitcast.9, bf16[4,8]{1,0:T(4,128)(2,1)} %bitcast.10), custom_call_target="tpu_custom_call" | custom-call | tf_op jit(solution)/shard_map/pack_rows/pallas_call | solution.py:48
  1.1 4.1 %collective-permute-start = (bf16[8,4096]{1,0:T(8,128)(2,1)S(1)}, bf16[8,4096]{1,0:T(8,128)(2,1)S(1)}, u32[]{:S(2)}, u32[]{:S(2)}) collective-permute-start(bf16[8,4096]{1,0:T(8,128)(2,1)S(1)} %slice.104), channel_id=1, source_target_pairs={{0,2},{1,3},{2,0},{3,1},{4,6},{5,7},{6,4},{7,5},{8,10},{9,11},{10,... | collective-permute-start | bytes 196616 | tf_op jit(solution)/shard_map/ppermute | solution.py:276
  5.2 0.1 collective-permute-start.2
  5.3 3.6 %collective-permute-done = bf16[8,4096]{1,0:T(8,128)(2,1)S(1)} collective-permute-done((bf16[8,4096]{1,0:T(8,128)(2,1)S(1)}, bf16[8,4096]{1,0:T(8,128)(2,1)S(1)}, u32[]{:S(2)}, u32[]{:S(2)}) %collective-permute-start) | collective-permute-done | bytes 65568 | tf_op jit(solution)/shard_map/ppermute | solution.py:276
  8.9 1.8 %collective-permute-start.1 = (bf16[16,4096]{1,0:T(8,128)(2,1)S(1)}, bf16[16,4096]{1,0:T(8,128)(2,1)S(1)}, u32[]{:S(2)}, u32[]{:S(2)}) collective-permute-start(bf16[16,4096]{1,0:T(8,128)(2,1)S(1)} %pad_maximum_fusion.4), channel_id=1, source_target_pairs={{0,1},{1,0},{2,3},{3,2},{4,5},{5,4},{6,7},{7,6},{8,9},{9,8},{10,11... | collective-permute-start | bytes 393224 | tf_op jit(solution)/shard_map/ppermute | solution.py:276
  10.7 0.0 collective-permute-done.2
  10.7 1.6 %collective-permute-start.3 = (bf16[16,3200]{1,0:T(8,128)(2,1)S(1)}, bf16[16,3200]{1,0:T(8,128)(2,1)S(1)}, u32[]{:S(2)}, u32[]{:S(2)}) collective-permute-start(bf16[16,3200]{1,0:T(8,128)(2,1)S(1)} %pad_maximum_fusion.6), channel_id=1, source_target_pairs={{0,8},{4,12},{8,0},{12,4},{1,9},{5,13},{9,1},{13,5},{2,10},{6,14},... | collective-permute-start | bytes 307208 | tf_op jit(solution)/shard_map/ppermute | solution.py:276
  12.3 4.3 %load_gate.1.first_ref = bf16[7168,768]{1,0:T(8,128)(2,1)S(1)} custom-call(s32[1]{0:T(128)} %bitcast.place_ref, bf16[7168,512]{1,0:T(8,128)(2,1)} %bitcast.7, bf16[7168,512]{1,0:T(8,128)(2,1)} %sgate_ref.1, bf16[7168,512]{1,0:T(8,128)(2,1)} %sup_ref.1), custom_call_target="tpu_custom_call" | custom-call | bytes 22020096 | tf_op jit(solution)/shard_map/load_gate/pallas_call | solution.py:78
  16.6 0.0 collective-permute-done.3
  16.6 0.0 collective-permute-done.1
  16.6 0.6 collective-permute-start.4
  17.2 1.2 %collective-permute-start.5 = (bf16[32,3200]{1,0:T(8,128)(2,1)S(1)}, bf16[32,3200]{1,0:T(8,128)(2,1)S(1)}, u32[]{:S(2)}, u32[]{:S(2)}) collective-permute-start(bf16[32,3200]{1,0:T(8,128)(2,1)S(1)} %pad_maximum_fusion.3), channel_id=1, source_target_pairs={{0,1},{1,0},{2,3},{3,2},{4,5},{5,4},{6,7},{7,6},{8,9},{9,8},{10,11... | collective-permute-start | bytes 614408 | tf_op jit(solution)/shard_map/ppermute | solution.py:276
  18.4 3.2 %load_up.1.up_ref = bf16[7168,512]{1,0:T(8,128)(2,1)S(1)} custom-call(bf16[7168,512]{1,0:T(8,128)(2,1)} %bitcast.6), custom_call_target="tpu_custom_call" | custom-call | bytes 14680064 | tf_op jit(solution)/shard_map/load_up/pallas_call | solution.py:106
  21.6 1.8 %collective-permute-done.5 = bf16[32,3200]{1,0:T(8,128)(2,1)S(1)} collective-permute-done((bf16[32,3200]{1,0:T(8,128)(2,1)S(1)}, bf16[32,3200]{1,0:T(8,128)(2,1)S(1)}, u32[]{:S(2)}, u32[]{:S(2)}) %collective-permute-start.5) | collective-permute-done | bytes 204832 | tf_op jit(solution)/shard_map/ppermute | solution.py:276
  23.4 1.0 %collective-permute-done.4 = bf16[32,4096]{1,0:T(8,128)(2,1)S(1)} collective-permute-done((bf16[32,4096]{1,0:T(8,128)(2,1)S(1)}, bf16[32,4096]{1,0:T(8,128)(2,1)S(1)}, u32[]{:S(2)}, u32[]{:S(2)}) %collective-permute-start.4) | collective-permute-done | bytes 262176 | tf_op jit(solution)/shard_map/ppermute | solution.py:276
  24.5 0.1 collective-permute-start.6
  24.6 0.6 collective-permute-start.7
  25.2 1.9 %collective-permute-done.7.other1_ref = bf16[64,3200]{1,0:T(8,128)(2,1)S(1)} collective-permute-done((bf16[64,3200]{1,0:T(8,128)(2,1)S(1)}, bf16[64,3200]{1,0:T(8,128)(2,1)S(1)}, u32[]{:S(2)}, u32[]{:S(2)}) %collective-permute-start.7) | collective-permute-done | bytes 409632 | tf_op jit(solution)/shard_map/ppermute | solution.py:276
  27.0 0.0 collective-permute-done.6.other0_ref
  27.0 6.6 %pair_rows.1 = (bf16[64,4096]{1,0:T(8,128)(2,1)S(1)}, bf16[64,3072]{1,0:T(8,128)(2,1)S(1)}, bf16[64,4096]{1,0:T(8,128)(2,1)S(1)}, bf16[64,3072]{1,0:T(8,128)(2,1)S(1)}) custom-call(s32[1]{0:T(128)} %bitcast.place_ref, bf16[64,4096]{1,0:T(8,128)(2,1)S(1)} %pad_maximum_fusion.own0_ref, bf16[64,3200]{1,0:T(8,128)(2,1)S(1)} %pad_maximum_fusion.1.own1_ref, ...), custom_call_target="tpu_custom_call" | custom-call | tf_op jit(solution)/shard_map/pair_rows/pallas_call | solution.py:225
  33.6 0.2 collective-permute-start.12
  33.8 0.4 collective-permute-start.8
  34.2 1.2 %collective-permute-done.12 = bf16[64,3072]{1,0:T(8,128)(2,1)S(1)} collective-permute-done((bf16[64,3072]{1,0:T(8,128)(2,1)S(1)}, bf16[64,3072]{1,0:T(8,128)(2,1)S(1)}, u32[]{:S(2)}, u32[]{:S(2)}) %collective-permute-start.12) | collective-permute-done | bytes 393248 | tf_op jit(solution)/shard_map/ppermute | solution.py:276
  35.4 0.1 add_convert_fusion.1
  35.5 1.2 %collective-permute-start.13 = (bf16[32,3072]{1,0:T(8,128)(2,1)S(1)}, bf16[32,3072]{1,0:T(8,128)(2,1)S(1)}, u32[]{:S(2)}, u32[]{:S(2)}) collective-permute-start(bf16[32,3072]{1,0:T(8,128)(2,1)S(1)} %get-tuple-element.33), channel_id=1, source_target_pairs={{0,1},{1,0},{2,3},{3,2},{4,5},{5,4},{6,7},{7,6},{8,9},{9,8},{10,11... | collective-permute-start | bytes 589832 | tf_op jit(solution)/shard_map/ppermute | solution.py:276
  36.7 0.0 collective-permute-done.8
  36.7 0.1 add_convert_fusion
  36.8 0.7 %collective-permute-start.9 = (bf16[32,4096]{1,0:T(8,128)(2,1)S(1)}, bf16[32,4096]{1,0:T(8,128)(2,1)S(1)}, u32[]{:S(2)}, u32[]{:S(2)}) collective-permute-start(bf16[32,4096]{1,0:T(8,128)(2,1)S(1)} %get-tuple-element.29), channel_id=1, source_target_pairs={{0,8},{4,12},{8,0},{12,4},{1,9},{5,13},{9,1},{13,5},{2,10},{6,14},... | collective-permute-start | bytes 786440 | tf_op jit(solution)/shard_map/ppermute | solution.py:276
  37.5 5.0 %collective-permute-done.13 = bf16[32,3072]{1,0:T(8,128)(2,1)S(1)} collective-permute-done((bf16[32,3072]{1,0:T(8,128)(2,1)S(1)}, bf16[32,3072]{1,0:T(8,128)(2,1)S(1)}, u32[]{:S(2)}, u32[]{:S(2)}) %collective-permute-start.13) | collective-permute-done | bytes 196640 | tf_op jit(solution)/shard_map/ppermute | solution.py:276
  42.5 0.7 %collective-permute-start.14 = (bf16[16,3072]{1,0:T(8,128)(2,1)S(1)}, bf16[16,3072]{1,0:T(8,128)(2,1)S(1)}, u32[]{:S(2)}, u32[]{:S(2)}) collective-permute-start(bf16[16,3072]{1,0:T(8,128)(2,1)S(1)} %get-tuple-element.35), channel_id=1, source_target_pairs={{0,8},{4,12},{8,0},{12,4},{1,9},{5,13},{9,1},{13,5},{2,10},{6,14},... | collective-permute-start | bytes 294920 | tf_op jit(solution)/shard_map/ppermute | solution.py:276
  43.2 2.1 %collective-permute-done.9 = bf16[32,4096]{1,0:T(8,128)(2,1)S(1)} collective-permute-done((bf16[32,4096]{1,0:T(8,128)(2,1)S(1)}, bf16[32,4096]{1,0:T(8,128)(2,1)S(1)}, u32[]{:S(2)}, u32[]{:S(2)}) %collective-permute-start.9) | collective-permute-done | bytes 262176 | tf_op jit(solution)/shard_map/ppermute | solution.py:276
  45.3 0.1 fusion
  45.3 0.8 %collective-permute-start.10 = (bf16[16,4096]{1,0:T(8,128)(2,1)S(1)}, bf16[16,4096]{1,0:T(8,128)(2,1)S(1)}, u32[]{:S(2)}, u32[]{:S(2)}) collective-permute-start(bf16[16,4096]{1,0:T(8,128)(2,1)S(1)} %get-tuple-element.31), channel_id=1, source_target_pairs={{0,1},{1,0},{2,3},{3,2},{4,5},{5,4},{6,7},{7,6},{8,9},{9,8},{10,11... | collective-permute-start | bytes 393224 | tf_op jit(solution)/shard_map/ppermute | solution.py:276
  46.1 1.1 %collective-permute-done.14 = bf16[16,3072]{1,0:T(8,128)(2,1)S(1)} collective-permute-done((bf16[16,3072]{1,0:T(8,128)(2,1)S(1)}, bf16[16,3072]{1,0:T(8,128)(2,1)S(1)}, u32[]{:S(2)}, u32[]{:S(2)}) %collective-permute-start.14) | collective-permute-done | bytes 98336 | tf_op jit(solution)/shard_map/ppermute | solution.py:276
  47.2 3.3 %collective-permute-start.15 = (bf16[8,3072]{1,0:T(8,128)(2,1)S(1)}, bf16[8,3072]{1,0:T(8,128)(2,1)S(1)}, u32[]{:S(2)}, u32[]{:S(2)}) collective-permute-start(bf16[8,3072]{1,0:T(8,128)(2,1)S(1)} %fusion.5), channel_id=1, source_target_pairs={{0,2},{1,3},{2,0},{3,1},{4,6},{5,7},{6,4},{7,5},{8,10},{9,11},{10,... | collective-permute-start | bytes 147464 | tf_op jit(solution)/shard_map/ppermute | solution.py:276
  50.5 0.4 collective-permute-done.10
  50.9 3.6 %collective-permute-start.11 = (bf16[8,4096]{1,0:T(8,128)(2,1)S(1)}, bf16[8,4096]{1,0:T(8,128)(2,1)S(1)}, u32[]{:S(2)}, u32[]{:S(2)}) collective-permute-start(bf16[8,4096]{1,0:T(8,128)(2,1)S(1)} %fusion.2), channel_id=1, source_target_pairs={{0,2},{1,3},{2,0},{3,1},{4,6},{5,7},{6,4},{7,5},{8,10},{9,11},{10,... | collective-permute-start | bytes 196616 | tf_op jit(solution)/shard_map/ppermute | solution.py:276
  54.5 0.0 collective-permute-done.15
  54.6 2.8 %collective-permute-done.11 = bf16[8,4096]{1,0:T(8,128)(2,1)S(1)} collective-permute-done((bf16[8,4096]{1,0:T(8,128)(2,1)S(1)}, bf16[8,4096]{1,0:T(8,128)(2,1)S(1)}, u32[]{:S(2)}, u32[]{:S(2)}) %collective-permute-start.11) | collective-permute-done | bytes 65568 | tf_op jit(solution)/shard_map/ppermute | solution.py:276
  57.4 0.7 %pad_maximum_fusion.5 = bf16[8,7168]{1,0:T(8,128)(2,1)} fusion(bf16[8,3072]{1,0:T(8,128)(2,1)S(1)} %fusion.7, bf16[8,4096]{1,0:T(8,128)(2,1)S(1)} %fusion.4), kind=kLoop, calls=%fused_computation.20 | loop fusion | flops 229376 | bytes 229376 | tf_op jit(solution)/shard_map/concatenate | solution.py:339
  (13 shorter events, 0.3 us)
Async XLA Ops:
  1.1 7.8 %collective-permute-start = (bf16[8,4096]{1,0:T(8,128)(2,1)S(1)}, bf16[8,4096]{1,0:T(8,128)(2,1)S(1)}, u32[]{:S(2)}, u32[]{:S(2)}) collective-permute-start(bf16[8,4096]{1,0:T(8,128)(2,1)S(1)} %slice.104), channel_id=1, source_target_pairs={{0,2},{1,3},{2,0},{3,1},{4,6},{5,7},{6,4},{7,5},{8,10},{9,11},{10,... | collective-permute-start | bytes 196616 | tf_op jit(solution)/shard_map/ppermute | solution.py:276
  5.2 5.5 %collective-permute-start.2 = (bf16[8,3200]{1,0:T(8,128)(2,1)S(1)}, bf16[8,3200]{1,0:T(8,128)(2,1)S(1)}, u32[]{:S(2)}, u32[]{:S(2)}) collective-permute-start(bf16[8,3200]{1,0:T(8,128)(2,1)S(1)} %slice.105), channel_id=1, source_target_pairs={{0,2},{1,3},{2,0},{3,1},{4,6},{5,7},{6,4},{7,5},{8,10},{9,11},{10,... | collective-permute-start | bytes 153608 | tf_op jit(solution)/shard_map/ppermute | solution.py:276
  8.9 7.7 %collective-permute-start.1 = (bf16[16,4096]{1,0:T(8,128)(2,1)S(1)}, bf16[16,4096]{1,0:T(8,128)(2,1)S(1)}, u32[]{:S(2)}, u32[]{:S(2)}) collective-permute-start(bf16[16,4096]{1,0:T(8,128)(2,1)S(1)} %pad_maximum_fusion.4), channel_id=1, source_target_pairs={{0,1},{1,0},{2,3},{3,2},{4,5},{5,4},{6,7},{7,6},{8,9},{9,8},{10,11... | collective-permute-start | bytes 393224 | tf_op jit(solution)/shard_map/ppermute | solution.py:276
  10.7 5.9 %collective-permute-start.3 = (bf16[16,3200]{1,0:T(8,128)(2,1)S(1)}, bf16[16,3200]{1,0:T(8,128)(2,1)S(1)}, u32[]{:S(2)}, u32[]{:S(2)}) collective-permute-start(bf16[16,3200]{1,0:T(8,128)(2,1)S(1)} %pad_maximum_fusion.6), channel_id=1, source_target_pairs={{0,8},{4,12},{8,0},{12,4},{1,9},{5,13},{9,1},{13,5},{2,10},{6,14},... | collective-permute-start | bytes 307208 | tf_op jit(solution)/shard_map/ppermute | solution.py:276
  16.6 7.8 %collective-permute-start.4 = (bf16[32,4096]{1,0:T(8,128)(2,1)S(1)}, bf16[32,4096]{1,0:T(8,128)(2,1)S(1)}, u32[]{:S(2)}, u32[]{:S(2)}) collective-permute-start(bf16[32,4096]{1,0:T(8,128)(2,1)S(1)} %pad_maximum_fusion.2), channel_id=1, source_target_pairs={{0,8},{4,12},{8,0},{12,4},{1,9},{5,13},{9,1},{13,5},{2,10},{6,14},... | collective-permute-start | bytes 786440 | tf_op jit(solution)/shard_map/ppermute | solution.py:276
  17.2 6.2 %collective-permute-start.5 = (bf16[32,3200]{1,0:T(8,128)(2,1)S(1)}, bf16[32,3200]{1,0:T(8,128)(2,1)S(1)}, u32[]{:S(2)}, u32[]{:S(2)}) collective-permute-start(bf16[32,3200]{1,0:T(8,128)(2,1)S(1)} %pad_maximum_fusion.3), channel_id=1, source_target_pairs={{0,1},{1,0},{2,3},{3,2},{4,5},{5,4},{6,7},{7,6},{8,9},{9,8},{10,11... | collective-permute-start | bytes 614408 | tf_op jit(solution)/shard_map/ppermute | solution.py:276
  24.5 2.6 %collective-permute-start.6 = (bf16[64,4096]{1,0:T(8,128)(2,1)S(1)}, bf16[64,4096]{1,0:T(8,128)(2,1)S(1)}, u32[]{:S(2)}, u32[]{:S(2)}) collective-permute-start(bf16[64,4096]{1,0:T(8,128)(2,1)S(1)} %pad_maximum_fusion.own0_ref), channel_id=1, source_target_pairs={{0,4},{4,0},{8,12},{12,8},{1,5},{5,1},{9,13},{13,9},{2,6},{6,2},{1... | collective-permute-start | bytes 1572872 | tf_op jit(solution)/shard_map/ppermute | solution.py:276
  24.6 2.4 %collective-permute-start.7 = (bf16[64,3200]{1,0:T(8,128)(2,1)S(1)}, bf16[64,3200]{1,0:T(8,128)(2,1)S(1)}, u32[]{:S(2)}, u32[]{:S(2)}) collective-permute-start(bf16[64,3200]{1,0:T(8,128)(2,1)S(1)} %pad_maximum_fusion.1.own1_ref), channel_id=1, source_target_pairs={{0,4},{4,0},{8,12},{12,8},{1,5},{5,1},{9,13},{13,9},{2,6},{6,2},{1... | collective-permute-start | bytes 1228808 | tf_op jit(solution)/shard_map/ppermute | solution.py:276
  33.6 1.8 %collective-permute-start.12 = (bf16[64,3072]{1,0:T(8,128)(2,1)S(1)}, bf16[64,3072]{1,0:T(8,128)(2,1)S(1)}, u32[]{:S(2)}, u32[]{:S(2)}) collective-permute-start(bf16[64,3072]{1,0:T(8,128)(2,1)S(1)} %get-tuple-element.28), channel_id=1, source_target_pairs={{0,4},{4,0},{8,12},{12,8},{1,5},{5,1},{9,13},{13,9},{2,6},{6,2},{1... | collective-permute-start | bytes 1179656 | tf_op jit(solution)/shard_map/ppermute | solution.py:276
  33.8 2.9 %collective-permute-start.8 = (bf16[64,4096]{1,0:T(8,128)(2,1)S(1)}, bf16[64,4096]{1,0:T(8,128)(2,1)S(1)}, u32[]{:S(2)}, u32[]{:S(2)}) collective-permute-start(bf16[64,4096]{1,0:T(8,128)(2,1)S(1)} %get-tuple-element.26), channel_id=1, source_target_pairs={{0,4},{4,0},{8,12},{12,8},{1,5},{5,1},{9,13},{13,9},{2,6},{6,2},{1... | collective-permute-start | bytes 1572872 | tf_op jit(solution)/shard_map/ppermute | solution.py:276
  35.5 7.0 %collective-permute-start.13 = (bf16[32,3072]{1,0:T(8,128)(2,1)S(1)}, bf16[32,3072]{1,0:T(8,128)(2,1)S(1)}, u32[]{:S(2)}, u32[]{:S(2)}) collective-permute-start(bf16[32,3072]{1,0:T(8,128)(2,1)S(1)} %get-tuple-element.33), channel_id=1, source_target_pairs={{0,1},{1,0},{2,3},{3,2},{4,5},{5,4},{6,7},{7,6},{8,9},{9,8},{10,11... | collective-permute-start | bytes 589832 | tf_op jit(solution)/shard_map/ppermute | solution.py:276
  36.8 8.5 %collective-permute-start.9 = (bf16[32,4096]{1,0:T(8,128)(2,1)S(1)}, bf16[32,4096]{1,0:T(8,128)(2,1)S(1)}, u32[]{:S(2)}, u32[]{:S(2)}) collective-permute-start(bf16[32,4096]{1,0:T(8,128)(2,1)S(1)} %get-tuple-element.29), channel_id=1, source_target_pairs={{0,8},{4,12},{8,0},{12,4},{1,9},{5,13},{9,1},{13,5},{2,10},{6,14},... | collective-permute-start | bytes 786440 | tf_op jit(solution)/shard_map/ppermute | solution.py:276
  42.5 4.7 %collective-permute-start.14 = (bf16[16,3072]{1,0:T(8,128)(2,1)S(1)}, bf16[16,3072]{1,0:T(8,128)(2,1)S(1)}, u32[]{:S(2)}, u32[]{:S(2)}) collective-permute-start(bf16[16,3072]{1,0:T(8,128)(2,1)S(1)} %get-tuple-element.35), channel_id=1, source_target_pairs={{0,8},{4,12},{8,0},{12,4},{1,9},{5,13},{9,1},{13,5},{2,10},{6,14},... | collective-permute-start | bytes 294920 | tf_op jit(solution)/shard_map/ppermute | solution.py:276
  45.3 5.6 %collective-permute-start.10 = (bf16[16,4096]{1,0:T(8,128)(2,1)S(1)}, bf16[16,4096]{1,0:T(8,128)(2,1)S(1)}, u32[]{:S(2)}, u32[]{:S(2)}) collective-permute-start(bf16[16,4096]{1,0:T(8,128)(2,1)S(1)} %get-tuple-element.31), channel_id=1, source_target_pairs={{0,1},{1,0},{2,3},{3,2},{4,5},{5,4},{6,7},{7,6},{8,9},{9,8},{10,11... | collective-permute-start | bytes 393224 | tf_op jit(solution)/shard_map/ppermute | solution.py:276
  47.2 7.3 %collective-permute-start.15 = (bf16[8,3072]{1,0:T(8,128)(2,1)S(1)}, bf16[8,3072]{1,0:T(8,128)(2,1)S(1)}, u32[]{:S(2)}, u32[]{:S(2)}) collective-permute-start(bf16[8,3072]{1,0:T(8,128)(2,1)S(1)} %fusion.5), channel_id=1, source_target_pairs={{0,2},{1,3},{2,0},{3,1},{4,6},{5,7},{6,4},{7,5},{8,10},{9,11},{10,... | collective-permute-start | bytes 147464 | tf_op jit(solution)/shard_map/ppermute | solution.py:276
  50.9 6.5 %collective-permute-start.11 = (bf16[8,4096]{1,0:T(8,128)(2,1)S(1)}, bf16[8,4096]{1,0:T(8,128)(2,1)S(1)}, u32[]{:S(2)}, u32[]{:S(2)}) collective-permute-start(bf16[8,4096]{1,0:T(8,128)(2,1)S(1)} %fusion.2), channel_id=1, source_target_pairs={{0,2},{1,3},{2,0},{3,1},{4,6},{5,7},{6,4},{7,5},{8,10},{9,11},{10,... | collective-permute-start | bytes 196616 | tf_op jit(solution)/shard_map/ppermute | solution.py:276

commit v12 on v10

--- a/solution.py
+++ b/solution.py
@@ -165,6 +165,14 @@
         copy.wait()
 
 
+def shared_units(share, node, both):
+    shared = silu(both[:, :LANES]) * both[:, LANES:]
+    if share > 1:
+        lane = lax.broadcasted_iota(jnp.int32, shared.shape, 1)
+        shared = jnp.where(lane // (LANES // share) == node % share, shared, 0.0)
+    return shared.astype(BF16)
+
+
 def ffn(share, place_ref, x, first_ref, up_ref, act, second, take, store):
     width, hidden = up_ref.shape
     node = place_ref[0]
@@ -176,11 +184,7 @@
         up = jnp.dot(rows, up_ref[:, at : at + tile], preferred_element_type=F32)
         act[:, at : at + tile] = (silu(gate) * up * weight).astype(BF16)
     both = jnp.dot(rows, first_ref[:, hidden:], preferred_element_type=F32)
-    shared = silu(both[:, :LANES]) * both[:, LANES:]
-    if share > 1:
-        lane = lax.broadcasted_iota(jnp.int32, shared.shape, 1)
-        shared = jnp.where(lane // (LANES // share) == node % share, shared, 0.0)
-    act[:, hidden:] = shared.astype(BF16)
+    act[:, hidden:] = shared_units(share, node, both)
     for i in range(DOWN_PARTS):
         at = slice(i * piece, (i + 1) * piece)
         take(i)
@@ -204,45 +208,146 @@
     return jnp.where(turn == 1, regroup(value, 2, 4), regroup(value, 4, 2)).astype(BF16)
 
 
-def pair_kernel(
-    share, place_ref, own0_ref, own1_ref, other0_ref, other1_ref, first_ref, up_ref, down_ref, sdown_ref,
-    own0_out_ref, own1_out_ref, other0_out_ref, other1_out_ref, x, act, second, sems,
+def half_down_copies(share, place_ref, down_ref, sdown_ref, out_ref, lower, sems):
+    hidden = down_ref.shape[0]
+    column = pl.multiple_of((place_ref[0] // share) * LANES, LANES)
+    parts = 2
+    piece = out_ref.shape[1] // parts
+    copies = []
+    for i in range(parts):
+        source, target = pl.ds(lower + i * piece, piece), pl.ds(i * piece, piece)
+        copies.append(
+            pltpu.make_async_copy(
+                down_ref.at[:, source], out_ref.at[pl.ds(0, hidden), target], sems.at[2 * i]
+            )
+        )
+        copies.append(
+            pltpu.make_async_copy(
+                sdown_ref.at[pl.ds(column, LANES), source],
+                out_ref.at[pl.ds(hidden, LANES), target],
+                sems.at[2 * i + 1],
+            )
+        )
+    return copies
+
+
+def late_half_kernel(
+    share, place_ref, own_ref, other_ref, first_ref, up_ref, down_ref, sdown_ref, acc_ref, second_ref, x, sems
 ):
-    groups = down_copies(share, place_ref, down_ref, sdown_ref, second, sems)
-    for i in range(DOWN_PARTS):
-        start_group(groups, i)
-    half, cut = own0_ref.shape
-    x[:half, :cut] = own0_ref[...]
+    copies = half_down_copies(share, place_ref, down_ref, sdown_ref, second_ref, 0, sems)
+    for copy in copies:
+        copy.start()
+    width, hidden = up_ref.shape
+    half, columns = own_ref.shape
+    cut = width + LANES - columns
     odd = place_ref[0] % 2
-    x[:half, cut:] = reorder(own1_ref[...], odd)
-    x[half:, :cut] = other0_ref[...]
-    x[half:, cut:] = reorder(other1_ref[...], 1 - odd)
-
-    def store(at, total):
-        if at.stop <= cut:
-            own0_out_ref[:, at] = total[:half].astype(BF16)
-            other0_out_ref[:, at] = total[half:].astype(BF16)
-        else:
-            at = slice(at.start - cut, at.stop - cut)
-            own1_out_ref[:, at] = reorder(total[:half], 1 - odd)
-            other1_out_ref[:, at] = reorder(total[half:], odd)
-
-    ffn(share, place_ref, x, first_ref, up_ref, act, second, functools.partial(wait_group, groups), store)
-
-
-def pair_rows(place, pieces, first, up, down, sdown, share):
-    half, cut = pieces[0].shape
+    x[:half, :] = reorder(own_ref[...], odd)
+    x[half:, :] = reorder(other_ref[...], 1 - odd)
+    rows = x[:, : width - cut]
+    acc_ref[:, :hidden] = jnp.dot(rows, first_ref[cut:, :hidden], preferred_element_type=F32)
+    acc_ref[:, hidden : 2 * hidden] = jnp.dot(rows, up_ref[cut:, :], preferred_element_type=F32)
+    acc_ref[:, 2 * hidden : 2 * hidden + 2 * LANES] = jnp.dot(
+        rows, first_ref[cut:, hidden:], preferred_element_type=F32
+    )
+    weight = row_weight(place_ref[0], x[:, width - cut :])
+    acc_ref[:, 2 * hidden + 2 * LANES :] = jnp.broadcast_to(weight, (2 * half, LANES))
+    for copy in copies:
+        copy.wait()
+
+
+def early_half_kernel(
+    share, place_ref, own_ref, other_ref, first_ref, up_ref, acc_ref, second_ref, down_ref, sdown_ref,
+    own_out_ref, other_out_ref, act_ref, later_ref, x, sems,
+):
+    half, cut = own_ref.shape
+    copies = half_down_copies(share, place_ref, down_ref, sdown_ref, later_ref, cut, sems)
+    for copy in copies:
+        copy.start()
+    hidden = up_ref.shape[1]
+    x[:half, :] = own_ref[...]
+    x[half:, :] = other_ref[...]
+    rows = x[...]
+    tile = min(2 * LANES, hidden)
+    weight = acc_ref[:, 2 * hidden + 2 * LANES :][:, :1]
+    for at in range(0, hidden, tile):
+        gate = acc_ref[:, at : at + tile] + jnp.dot(
+            rows, first_ref[:cut, at : at + tile], preferred_element_type=F32
+        )
+        up = acc_ref[:, hidden + at : hidden + at + tile] + jnp.dot(
+            rows, up_ref[:cut, at : at + tile], preferred_element_type=F32
+        )
+        act_ref[:, at : at + tile] = (silu(gate) * up * weight).astype(BF16)
+    both = acc_ref[:, 2 * hidden : 2 * hidden + 2 * LANES] + jnp.dot(
+        rows, first_ref[:cut, hidden:], preferred_element_type=F32
+    )
+    act_ref[:, hidden:] = shared_units(share, place_ref[0], both)
+    piece = cut // 2
+    for i in range(2):
+        at = slice(i * piece, (i + 1) * piece)
+        total = jnp.dot(act_ref[...], second_ref[:, at], preferred_element_type=F32).astype(BF16)
+        own_out_ref[:, at] = total[:half]
+        other_out_ref[:, at] = total[half:]
+    for copy in copies:
+        copy.wait()
+
+
+def last_half_kernel(place_ref, act_ref, second_ref, own_out_ref, other_out_ref):
+    half, columns = own_out_ref.shape
+    odd = place_ref[0] % 2
+    piece = columns // 2
+    for i in range(2):
+        at = slice(i * piece, (i + 1) * piece)
+        total = jnp.dot(act_ref[...], second_ref[:, at], preferred_element_type=F32)
+        own_out_ref[:, at] = reorder(total[:half], 1 - odd)
+        other_out_ref[:, at] = reorder(total[half:], odd)
+
+
+def estimate(rows, depth, columns):
+    return pl.CostEstimate(
+        flops=2 * rows * depth * columns, bytes_accessed=2 * depth * columns, transcendentals=0
+    )
+
+
+def pair_rows(place, own, other, first, up, down, sdown, share):
+    half, cut = own[0].shape
     hidden, width = down.shape
-    out = jax.ShapeDtypeStruct((half, cut), BF16)
-    return pl.pallas_call(
-        functools.partial(pair_kernel, share),
+    down, sdown = in_hbm(down), in_hbm(sdown)
+    units = hidden + LANES
+    acc, second = pl.pallas_call(
+        functools.partial(late_half_kernel, share),
+        in_specs=[SMEM_SPEC] + [VMEM_SPEC] * 4 + [ANY_SPEC] * 2,
+        out_specs=[VMEM_SPEC] * 2,
+        out_shape=[pltpu.VMEM((2 * half, 2 * units + LANES), F32), pltpu.VMEM((units, cut), BF16)],
+        scratch_shapes=[pltpu.VMEM((2 * half, own[1].shape[1]), BF16), pltpu.SemaphoreType.DMA((4,))],
+        cost_estimate=estimate(2 * half, width - cut, 2 * units),
+        compiler_params=pltpu.CompilerParams(vmem_limit_bytes=10 << 20),
+        name="late_half",
+    )(place, own[1], other[1], first, up, down, sdown)
+    own_out, other_out, act, later = pl.pallas_call(
+        functools.partial(early_half_kernel, share),
         in_specs=[SMEM_SPEC] + [VMEM_SPEC] * 6 + [ANY_SPEC] * 2,
         out_specs=[VMEM_SPEC] * 4,
-        out_shape=[out] * 4,
-        scratch_shapes=[pltpu.VMEM((2 * half, width + LANES), BF16)] + down_scratch(2 * half, hidden, width),
-        compiler_params=pltpu.CompilerParams(vmem_limit_bytes=24 << 20),
-        name="pair_rows",
-    )(place, *pieces, first, up, in_hbm(down), in_hbm(sdown))
+        out_shape=[
+            pltpu.VMEM((half, cut), BF16),
+            pltpu.VMEM((half, cut), BF16),
+            pltpu.VMEM((2 * half, units), BF16),
+            pltpu.VMEM((units, width - cut), BF16),
+        ],
+        scratch_shapes=[pltpu.VMEM((2 * half, cut), BF16), pltpu.SemaphoreType.DMA((4,))],
+        cost_estimate=estimate(2 * half, cut, 3 * units),
+        compiler_params=pltpu.CompilerParams(vmem_limit_bytes=10 << 20),
+        name="early_half",
+    )(place, own[0], other[0], first, up, acc, second, down, sdown)
+    last = pl.pallas_call(
+        last_half_kernel,
+        in_specs=[SMEM_SPEC] + [VMEM_SPEC] * 2,
+        out_specs=[VMEM_SPEC] * 2,
+        out_shape=[pltpu.VMEM((half, width - cut), BF16)] * 2,
+        cost_estimate=estimate(2 * half, width - cut, units),
+        compiler_params=pltpu.CompilerParams(vmem_limit_bytes=10 << 20),
+        name="last_half",
+    )(place, act, later)
+    return own_out, last[0], other_out, last[1]
 
 
 def block_kernel(
@@ -343,7 +448,7 @@
     first, up = loaded
     other = [flipped(part, CORE, CORE) for part in own]
 
-    outs = pair_rows(place, own + other, first, up, down, down_shared, share)
+    outs = pair_rows(place, own, other, first, up, down, down_shared, share)
 
     totals = [[own, flipped(other, CORE, CORE)] for own, other in zip(outs[:2], outs[2:])]
     for phase in reversed(PHASES):

time: 57 us -> 57.2 us (level)
  Pallas kernels: 14.5 us -> 16.5 us
  waiting for transfers between devices: 16.5 us -> 14.8 us
    pallas_call x1 -> x3, Pallas kernels: 5.95 us -> 7.93 us  [the longest x1 3.55 us: pair_rows(): pl.pallas_call(functools.partial(late_half_kernel, share), in_specs=[SMEM...]
    ppermute x16, waiting for transfers between devices: 16.5 us -> 14.8 us  [flipped(): return lax.ppermute(value, ('node', 'local'), pairs)]
  transfers between devices with their start and end apart: 16 -> 16, of which waited for: 9 -> 9; matrix products, arithmetic and copies ran while one was open for 1% -> 1% of each run, Pallas kernels for 13% -> 21%
where the time goes in v12:
time: 57.2 us; the launch traced here: 57 us
  starting transfers between devices  24.4 us (43%)
  Pallas kernels  16.5 us (29%)
  waiting for transfers between devices  14.8 us (26%)
  other arithmetic  1.18 us (2%)
    ppermute x16, starting transfers between devices, flipped(): return lax.ppermute(value, ('node', 'local'), pairs)  24.4 us
    ppermute x16, waiting for transfers between devices, flipped(): return lax.ppermute(value, ('node', 'local'), pairs)  14.8 us
    pallas_call x1, Pallas kernels, load_gate(): pl.pallas_call(functools.partial(load_gate_kernel, share), in_specs=[SMEM...  4.31 us
    pallas_call x1, Pallas kernels, pair_rows(): pl.pallas_call(functools.partial(late_half_kernel, share), in_specs=[SMEM...  3.55 us
    pallas_call x1, Pallas kernels, pair_rows(): pl.pallas_call(functools.partial(early_half_kernel, share), in_specs=[SME...  3.49 us
    pallas_call x1, Pallas kernels, load_up(): pl.pallas_call(load_up_kernel, in_specs=[ANY_SPEC], out_specs=VMEM_SPEC,...  3.17 us
  transfers between devices with their start and end apart: 16, of which 9 were waited for; matrix products, arithmetic and copies ran while one was open for 1% of the time, Pallas kernels for 21%

profile of v12, /device:TPU:0, one launch (start us, length us, event | category | flops | bytes accessed | tf_op | source)
XLA Modules:
  0.0 57.0 jit_solution(7785903735503494454)
XLA Ops:
  0.0 1.1 %pack_rows.1 = bf16[8,7296]{1,0:T(8,128)(2,1)S(1)} custom-call(bf16[8,7168]{1,0:T(8,128)(2,1)} %tokens_ref.1, s32[4,8]{1,0:T(4,128)} %bitcast.10, bf16[4,8]{1,0:T(4,128)(2,1)} %bitcast.11), custom_call_target="tpu_custom_call" | custom-call | tf_op jit(solution)/shard_map/pack_rows/pallas_call | solution.py:48
  1.1 3.0 %collective-permute-start.2 = (bf16[8,3712]{1,0:T(8,128)(2,1)S(1)}, bf16[8,3712]{1,0:T(8,128)(2,1)S(1)}, u32[]{:S(2)}, u32[]{:S(2)}) collective-permute-start(bf16[8,3712]{1,0:T(8,128)(2,1)S(1)} %slice.105), channel_id=1, source_target_pairs={{0,8},{1,9},{2,10},{3,11},{4,6},{5,7},{6,4},{7,5},{8,0},{9,1},{10,... | collective-permute-start | bytes 178184 | tf_op jit(solution)/shard_map/ppermute | solution.py:397
  4.1 2.6 %collective-permute-start = (bf16[8,3584]{1,0:T(8,128)(2,1)S(1)}, bf16[8,3584]{1,0:T(8,128)(2,1)S(1)}, u32[]{:S(2)}, u32[]{:S(2)}) collective-permute-start(bf16[8,3584]{1,0:T(8,128)(2,1)S(1)} %slice.104), channel_id=1, source_target_pairs={{0,2},{1,3},{2,0},{3,1},{4,12},{5,13},{6,14},{7,15},{8,10},{9,11},... | collective-permute-start | bytes 172040 | tf_op jit(solution)/shard_map/ppermute | solution.py:397
  6.7 0.0 collective-permute-done.2
  6.7 2.8 %collective-permute-start.3 = (bf16[16,3712]{1,0:T(8,128)(2,1)S(1)}, bf16[16,3712]{1,0:T(8,128)(2,1)S(1)}, u32[]{:S(2)}, u32[]{:S(2)}) collective-permute-start(bf16[16,3712]{1,0:T(8,128)(2,1)S(1)} %pad_maximum_fusion.4), channel_id=1, source_target_pairs={{0,2},{1,3},{2,0},{3,1},{4,5},{5,4},{6,7},{7,6},{8,10},{9,11},{10,... | collective-permute-start | bytes 356360 | tf_op jit(solution)/shard_map/ppermute | solution.py:397
  9.5 0.0 collective-permute-done
  9.5 1.6 %collective-permute-start.1 = (bf16[16,3584]{1,0:T(8,128)(2,1)S(1)}, bf16[16,3584]{1,0:T(8,128)(2,1)S(1)}, u32[]{:S(2)}, u32[]{:S(2)}) collective-permute-start(bf16[16,3584]{1,0:T(8,128)(2,1)S(1)} %pad_maximum_fusion.5), channel_id=1, source_target_pairs={{0,1},{1,0},{2,3},{3,2},{4,6},{5,7},{6,4},{7,5},{8,9},{9,8},{10,11... | collective-permute-start | bytes 344072 | tf_op jit(solution)/shard_map/ppermute | solution.py:397
  11.1 4.3 %load_gate.1.first_ref = bf16[7168,768]{1,0:T(8,128)(2,1)S(1)} custom-call(s32[1]{0:T(128)} %bitcast.place_ref, bf16[7168,512]{1,0:T(8,128)(2,1)} %bitcast.9, bf16[7168,512]{1,0:T(8,128)(2,1)} %sgate_ref.1, bf16[7168,512]{1,0:T(8,128)(2,1)} %sup_ref.1), custom_call_target="tpu_custom_call" | custom-call | bytes 22020096 | tf_op jit(solution)/shard_map/load_gate/pallas_call | solution.py:78
  15.4 0.0 collective-permute-done.1
  15.5 0.3 collective-permute-done.3
  15.8 1.1 %collective-permute-start.5 = (bf16[32,3712]{1,0:T(8,128)(2,1)S(1)}, bf16[32,3712]{1,0:T(8,128)(2,1)S(1)}, u32[]{:S(2)}, u32[]{:S(2)}) collective-permute-start(bf16[32,3712]{1,0:T(8,128)(2,1)S(1)} %pad_maximum_fusion.2), channel_id=1, source_target_pairs={{0,1},{1,0},{2,3},{3,2},{4,12},{5,13},{6,14},{7,15},{8,9},{9,8},{1... | collective-permute-start | bytes 712712 | tf_op jit(solution)/shard_map/ppermute | solution.py:397
  16.9 1.6 %collective-permute-start.4 = (bf16[32,3584]{1,0:T(8,128)(2,1)S(1)}, bf16[32,3584]{1,0:T(8,128)(2,1)S(1)}, u32[]{:S(2)}, u32[]{:S(2)}) collective-permute-start(bf16[32,3584]{1,0:T(8,128)(2,1)S(1)} %pad_maximum_fusion.3), channel_id=1, source_target_pairs={{0,8},{1,9},{2,10},{3,11},{4,5},{5,4},{6,7},{7,6},{8,0},{9,1},{10,... | collective-permute-start | bytes 688136 | tf_op jit(solution)/shard_map/ppermute | solution.py:397
  18.5 3.2 %load_up.1.up_ref = bf16[7168,512]{1,0:T(8,128)(2,1)S(1)} custom-call(bf16[7168,512]{1,0:T(8,128)(2,1)} %bitcast.8), custom_call_target="tpu_custom_call" | custom-call | bytes 14680064 | tf_op jit(solution)/shard_map/load_up/pallas_call | solution.py:106
  21.7 2.1 %collective-permute-done.4 = bf16[32,3584]{1,0:T(8,128)(2,1)S(1)} collective-permute-done((bf16[32,3584]{1,0:T(8,128)(2,1)S(1)}, bf16[32,3584]{1,0:T(8,128)(2,1)S(1)}, u32[]{:S(2)}, u32[]{:S(2)}) %collective-permute-start.4) | collective-permute-done | bytes 229408 | tf_op jit(solution)/shard_map/ppermute | solution.py:397
  23.7 0.1 collective-permute-done.5
  23.9 0.5 collective-permute-start.7
  24.4 0.1 collective-permute-start.6
  24.5 1.3 %collective-permute-done.7.other_ref = bf16[64,3712]{1,0:T(8,128)(2,1)S(1)} collective-permute-done((bf16[64,3712]{1,0:T(8,128)(2,1)S(1)}, bf16[64,3712]{1,0:T(8,128)(2,1)S(1)}, u32[]{:S(2)}, u32[]{:S(2)}) %collective-permute-start.7) | collective-permute-done | bytes 475168 | tf_op jit(solution)/shard_map/ppermute | solution.py:397
  25.8 3.6 %late_half.1 = (f32[128,1408]{1,0:T(8,128)S(1)}, bf16[640,3584]{1,0:T(8,128)(2,1)S(1)}) custom-call(s32[1]{0:T(128)} %bitcast.place_ref, bf16[64,3712]{1,0:T(8,128)(2,1)S(1)} %pad_maximum_fusion.own_ref, bf16[64,3712]{1,0:T(8,128)(2,1)S(1)} %collective-permute-done.7.other_ref, bf16[7168,768]{1,0:T(8,128)(2,1)S(1)} %load_gate.1.first_ref, ...), custom_call_target="tpu_custom_call" | custom-call | flops 1174405120 | bytes 9175040 | tf_op jit(solution)/shard_map/late_half/pallas_call | solution.py:316
  29.4 0.0 collective-permute-done.6.other_ref
  29.4 3.5 %early_half.1 = (bf16[64,3584]{1,0:T(8,128)(2,1)S(1)}, bf16[64,3584]{1,0:T(8,128)(2,1)S(1)}, bf16[128,640]{1,0:T(8,128)(2,1)S(1)}, bf16[640,3584]{1,0:T(8,128)(2,1)S(1)}) custom-call(s32[1]{0:T(128)} %bitcast.place_ref, bf16[64,3584]{1,0:T(8,128)(2,1)S(1)} %pad_maximum_fusion.1.own_ref, bf16[64,3584]{1,0:T(8,128)(2,1)S(1)} %collective-permute-done.6.other_ref, ...), custom_call_target="tpu_custom_call" | custom-call | flops 1761607680 | bytes 13762560 | tf_op jit(solution)/shard_map/early_half/pallas_call | solution.py:326
  32.9 0.4 collective-permute-start.8
  33.3 0.9 %last_half.1 = (bf16[64,3584]{1,0:T(8,128)(2,1)S(1)}, bf16[64,3584]{1,0:T(8,128)(2,1)S(1)}) custom-call(s32[1]{0:T(128)} %bitcast.place_ref, bf16[128,640]{1,0:T(8,128)(2,1)S(1)} %get-tuple-element.33.act_ref, bf16[640,3584]{1,0:T(8,128)(2,1)S(1)} %get-tuple-element.34.second_ref), custom_call_target="tpu_custom_call" | custom-call | flops 587202560 | bytes 4587520 | tf_op jit(solution)/shard_map/last_half/pallas_call | solution.py:341
  34.2 0.2 collective-permute-start.12
  34.4 0.4 collective-permute-done.8
  34.8 0.1 add_convert_fusion.1
  34.9 1.8 %collective-permute-start.9 = (bf16[32,3584]{1,0:T(8,128)(2,1)S(1)}, bf16[32,3584]{1,0:T(8,128)(2,1)S(1)}, u32[]{:S(2)}, u32[]{:S(2)}) collective-permute-start(bf16[32,3584]{1,0:T(8,128)(2,1)S(1)} %get-tuple-element.37), channel_id=1, source_target_pairs={{0,8},{1,9},{2,10},{3,11},{4,5},{5,4},{6,7},{7,6},{8,0},{9,1},{10,... | collective-permute-start | bytes 688136 | tf_op jit(solution)/shard_map/ppermute | solution.py:397
  36.7 0.0 collective-permute-done.12
  36.7 0.1 add_convert_fusion
  36.8 0.8 %collective-permute-start.13 = (bf16[32,3584]{1,0:T(8,128)(2,1)S(1)}, bf16[32,3584]{1,0:T(8,128)(2,1)S(1)}, u32[]{:S(2)}, u32[]{:S(2)}) collective-permute-start(bf16[32,3584]{1,0:T(8,128)(2,1)S(1)} %get-tuple-element.39), channel_id=1, source_target_pairs={{0,1},{1,0},{2,3},{3,2},{4,12},{5,13},{6,14},{7,15},{8,9},{9,8},{1... | collective-permute-start | bytes 688136 | tf_op jit(solution)/shard_map/ppermute | solution.py:397
  37.6 5.2 %collective-permute-done.9 = bf16[32,3584]{1,0:T(8,128)(2,1)S(1)} collective-permute-done((bf16[32,3584]{1,0:T(8,128)(2,1)S(1)}, bf16[32,3584]{1,0:T(8,128)(2,1)S(1)}, u32[]{:S(2)}, u32[]{:S(2)}) %collective-permute-start.9) | collective-permute-done | bytes 229408 | tf_op jit(solution)/shard_map/ppermute | solution.py:397
  42.8 0.1 fusion.1
  42.9 1.8 %collective-permute-start.10 = (bf16[16,3584]{1,0:T(8,128)(2,1)S(1)}, bf16[16,3584]{1,0:T(8,128)(2,1)S(1)}, u32[]{:S(2)}, u32[]{:S(2)}) collective-permute-start(bf16[16,3584]{1,0:T(8,128)(2,1)S(1)} %get-tuple-element.41), channel_id=1, source_target_pairs={{0,1},{1,0},{2,3},{3,2},{4,6},{5,7},{6,4},{7,5},{8,9},{9,8},{10,11... | collective-permute-start | bytes 344072 | tf_op jit(solution)/shard_map/ppermute | solution.py:397
  44.7 0.0 collective-permute-done.13
  44.7 0.1 fusion
  44.8 2.7 %collective-permute-start.14 = (bf16[16,3584]{1,0:T(8,128)(2,1)S(1)}, bf16[16,3584]{1,0:T(8,128)(2,1)S(1)}, u32[]{:S(2)}, u32[]{:S(2)}) collective-permute-start(bf16[16,3584]{1,0:T(8,128)(2,1)S(1)} %get-tuple-element.43), channel_id=1, source_target_pairs={{0,2},{1,3},{2,0},{3,1},{4,5},{5,4},{6,7},{7,6},{8,10},{9,11},{10,... | collective-permute-start | bytes 344072 | tf_op jit(solution)/shard_map/ppermute | solution.py:397
  47.5 1.3 %collective-permute-done.10 = bf16[16,3584]{1,0:T(8,128)(2,1)S(1)} collective-permute-done((bf16[16,3584]{1,0:T(8,128)(2,1)S(1)}, bf16[16,3584]{1,0:T(8,128)(2,1)S(1)}, u32[]{:S(2)}, u32[]{:S(2)}) %collective-permute-start.10) | collective-permute-done | bytes 114720 | tf_op jit(solution)/shard_map/ppermute | solution.py:397
  48.8 3.2 %collective-permute-start.11 = (bf16[8,3584]{1,0:T(8,128)(2,1)S(1)}, bf16[8,3584]{1,0:T(8,128)(2,1)S(1)}, u32[]{:S(2)}, u32[]{:S(2)}) collective-permute-start(bf16[8,3584]{1,0:T(8,128)(2,1)S(1)} %fusion.5), channel_id=1, source_target_pairs={{0,2},{1,3},{2,0},{3,1},{4,12},{5,13},{6,14},{7,15},{8,10},{9,11},... | collective-permute-start | bytes 172040 | tf_op jit(solution)/shard_map/ppermute | solution.py:397
  52.1 0.0 collective-permute-done.14
  52.1 0.1 collective-permute-start.15
  52.2 2.1 %collective-permute-done.11 = bf16[8,3584]{1,0:T(8,128)(2,1)S(1)} collective-permute-done((bf16[8,3584]{1,0:T(8,128)(2,1)S(1)}, bf16[8,3584]{1,0:T(8,128)(2,1)S(1)}, u32[]{:S(2)}, u32[]{:S(2)}) %collective-permute-start.11) | collective-permute-done | bytes 57376 | tf_op jit(solution)/shard_map/ppermute | solution.py:397
  54.3 2.1 %collective-permute-done.15 = bf16[8,3584]{1,0:T(8,128)(2,1)S(1)} collective-permute-done((bf16[8,3584]{1,0:T(8,128)(2,1)S(1)}, bf16[8,3584]{1,0:T(8,128)(2,1)S(1)}, u32[]{:S(2)}, u32[]{:S(2)}) %collective-permute-start.15) | collective-permute-done | bytes 57376 | tf_op jit(solution)/shard_map/ppermute | solution.py:397
  56.4 0.7 %pad_maximum_fusion.6 = bf16[8,7168]{1,0:T(8,128)(2,1)} fusion(bf16[8,3584]{1,0:T(8,128)(2,1)S(1)} %fusion.4, bf16[8,3584]{1,0:T(8,128)(2,1)S(1)} %fusion.7), kind=kLoop, calls=%fused_computation.26 | loop fusion | flops 229376 | bytes 229376 | tf_op jit(solution)/shard_map/concatenate | solution.py:460
  (12 shorter events, 0.2 us)
Async XLA Ops:
  1.1 5.6 %collective-permute-start.2 = (bf16[8,3712]{1,0:T(8,128)(2,1)S(1)}, bf16[8,3712]{1,0:T(8,128)(2,1)S(1)}, u32[]{:S(2)}, u32[]{:S(2)}) collective-permute-start(bf16[8,3712]{1,0:T(8,128)(2,1)S(1)} %slice.105), channel_id=1, source_target_pairs={{0,8},{1,9},{2,10},{3,11},{4,6},{5,7},{6,4},{7,5},{8,0},{9,1},{10,... | collective-permute-start | bytes 178184 | tf_op jit(solution)/shard_map/ppermute | solution.py:397
  4.1 5.4 %collective-permute-start = (bf16[8,3584]{1,0:T(8,128)(2,1)S(1)}, bf16[8,3584]{1,0:T(8,128)(2,1)S(1)}, u32[]{:S(2)}, u32[]{:S(2)}) collective-permute-start(bf16[8,3584]{1,0:T(8,128)(2,1)S(1)} %slice.104), channel_id=1, source_target_pairs={{0,2},{1,3},{2,0},{3,1},{4,12},{5,13},{6,14},{7,15},{8,10},{9,11},... | collective-permute-start | bytes 172040 | tf_op jit(solution)/shard_map/ppermute | solution.py:397
  6.7 9.1 %collective-permute-start.3 = (bf16[16,3712]{1,0:T(8,128)(2,1)S(1)}, bf16[16,3712]{1,0:T(8,128)(2,1)S(1)}, u32[]{:S(2)}, u32[]{:S(2)}) collective-permute-start(bf16[16,3712]{1,0:T(8,128)(2,1)S(1)} %pad_maximum_fusion.4), channel_id=1, source_target_pairs={{0,2},{1,3},{2,0},{3,1},{4,5},{5,4},{6,7},{7,6},{8,10},{9,11},{10,... | collective-permute-start | bytes 356360 | tf_op jit(solution)/shard_map/ppermute | solution.py:397
  9.5 6.0 %collective-permute-start.1 = (bf16[16,3584]{1,0:T(8,128)(2,1)S(1)}, bf16[16,3584]{1,0:T(8,128)(2,1)S(1)}, u32[]{:S(2)}, u32[]{:S(2)}) collective-permute-start(bf16[16,3584]{1,0:T(8,128)(2,1)S(1)} %pad_maximum_fusion.5), channel_id=1, source_target_pairs={{0,1},{1,0},{2,3},{3,2},{4,6},{5,7},{6,4},{7,5},{8,9},{9,8},{10,11... | collective-permute-start | bytes 344072 | tf_op jit(solution)/shard_map/ppermute | solution.py:397
  15.8 8.0 %collective-permute-start.5 = (bf16[32,3712]{1,0:T(8,128)(2,1)S(1)}, bf16[32,3712]{1,0:T(8,128)(2,1)S(1)}, u32[]{:S(2)}, u32[]{:S(2)}) collective-permute-start(bf16[32,3712]{1,0:T(8,128)(2,1)S(1)} %pad_maximum_fusion.2), channel_id=1, source_target_pairs={{0,1},{1,0},{2,3},{3,2},{4,12},{5,13},{6,14},{7,15},{8,9},{9,8},{1... | collective-permute-start | bytes 712712 | tf_op jit(solution)/shard_map/ppermute | solution.py:397
  16.9 6.8 %collective-permute-start.4 = (bf16[32,3584]{1,0:T(8,128)(2,1)S(1)}, bf16[32,3584]{1,0:T(8,128)(2,1)S(1)}, u32[]{:S(2)}, u32[]{:S(2)}) collective-permute-start(bf16[32,3584]{1,0:T(8,128)(2,1)S(1)} %pad_maximum_fusion.3), channel_id=1, source_target_pairs={{0,8},{1,9},{2,10},{3,11},{4,5},{5,4},{6,7},{7,6},{8,0},{9,1},{10,... | collective-permute-start | bytes 688136 | tf_op jit(solution)/shard_map/ppermute | solution.py:397
  23.9 2.0 %collective-permute-start.7 = (bf16[64,3712]{1,0:T(8,128)(2,1)S(1)}, bf16[64,3712]{1,0:T(8,128)(2,1)S(1)}, u32[]{:S(2)}, u32[]{:S(2)}) collective-permute-start(bf16[64,3712]{1,0:T(8,128)(2,1)S(1)} %pad_maximum_fusion.own_ref), channel_id=1, source_target_pairs={{0,4},{1,5},{2,6},{3,7},{4,0},{5,1},{6,2},{7,3},{8,12},{9,13},{10,... | collective-permute-start | bytes 1425416 | tf_op jit(solution)/shard_map/ppermute | solution.py:397
  24.4 5.0 %collective-permute-start.6 = (bf16[64,3584]{1,0:T(8,128)(2,1)S(1)}, bf16[64,3584]{1,0:T(8,128)(2,1)S(1)}, u32[]{:S(2)}, u32[]{:S(2)}) collective-permute-start(bf16[64,3584]{1,0:T(8,128)(2,1)S(1)} %pad_maximum_fusion.1.own_ref), channel_id=1, source_target_pairs={{0,4},{1,5},{2,6},{3,7},{4,0},{5,1},{6,2},{7,3},{8,12},{9,13},{10,... | collective-permute-start | bytes 1376264 | tf_op jit(solution)/shard_map/ppermute | solution.py:397
  32.9 1.9 %collective-permute-start.8 = (bf16[64,3584]{1,0:T(8,128)(2,1)S(1)}, bf16[64,3584]{1,0:T(8,128)(2,1)S(1)}, u32[]{:S(2)}, u32[]{:S(2)}) collective-permute-start(bf16[64,3584]{1,0:T(8,128)(2,1)S(1)} %get-tuple-element.32), channel_id=1, source_target_pairs={{0,4},{1,5},{2,6},{3,7},{4,0},{5,1},{6,2},{7,3},{8,12},{9,13},{10,... | collective-permute-start | bytes 1376264 | tf_op jit(solution)/shard_map/ppermute | solution.py:397
  34.2 2.5 %collective-permute-start.12 = (bf16[64,3584]{1,0:T(8,128)(2,1)S(1)}, bf16[64,3584]{1,0:T(8,128)(2,1)S(1)}, u32[]{:S(2)}, u32[]{:S(2)}) collective-permute-start(bf16[64,3584]{1,0:T(8,128)(2,1)S(1)} %get-tuple-element.36), channel_id=1, source_target_pairs={{0,4},{1,5},{2,6},{3,7},{4,0},{5,1},{6,2},{7,3},{8,12},{9,13},{10,... | collective-permute-start | bytes 1376264 | tf_op jit(solution)/shard_map/ppermute | solution.py:397
  34.9 8.0 %collective-permute-start.9 = (bf16[32,3584]{1,0:T(8,128)(2,1)S(1)}, bf16[32,3584]{1,0:T(8,128)(2,1)S(1)}, u32[]{:S(2)}, u32[]{:S(2)}) collective-permute-start(bf16[32,3584]{1,0:T(8,128)(2,1)S(1)} %get-tuple-element.37), channel_id=1, source_target_pairs={{0,8},{1,9},{2,10},{3,11},{4,5},{5,4},{6,7},{7,6},{8,0},{9,1},{10,... | collective-permute-start | bytes 688136 | tf_op jit(solution)/shard_map/ppermute | solution.py:397
  36.8 7.9 %collective-permute-start.13 = (bf16[32,3584]{1,0:T(8,128)(2,1)S(1)}, bf16[32,3584]{1,0:T(8,128)(2,1)S(1)}, u32[]{:S(2)}, u32[]{:S(2)}) collective-permute-start(bf16[32,3584]{1,0:T(8,128)(2,1)S(1)} %get-tuple-element.39), channel_id=1, source_target_pairs={{0,1},{1,0},{2,3},{3,2},{4,12},{5,13},{6,14},{7,15},{8,9},{9,8},{1... | collective-permute-start | bytes 688136 | tf_op jit(solution)/shard_map/ppermute | solution.py:397
  42.9 5.9 %collective-permute-start.10 = (bf16[16,3584]{1,0:T(8,128)(2,1)S(1)}, bf16[16,3584]{1,0:T(8,128)(2,1)S(1)}, u32[]{:S(2)}, u32[]{:S(2)}) collective-permute-start(bf16[16,3584]{1,0:T(8,128)(2,1)S(1)} %get-tuple-element.41), channel_id=1, source_target_pairs={{0,1},{1,0},{2,3},{3,2},{4,6},{5,7},{6,4},{7,5},{8,9},{9,8},{10,11... | collective-permute-start | bytes 344072 | tf_op jit(solution)/shard_map/ppermute | solution.py:397
  44.8 7.3 %collective-permute-start.14 = (bf16[16,3584]{1,0:T(8,128)(2,1)S(1)}, bf16[16,3584]{1,0:T(8,128)(2,1)S(1)}, u32[]{:S(2)}, u32[]{:S(2)}) collective-permute-start(bf16[16,3584]{1,0:T(8,128)(2,1)S(1)} %get-tuple-element.43), channel_id=1, source_target_pairs={{0,2},{1,3},{2,0},{3,1},{4,5},{5,4},{6,7},{7,6},{8,10},{9,11},{10,... | collective-permute-start | bytes 344072 | tf_op jit(solution)/shard_map/ppermute | solution.py:397
  48.8 5.4 %collective-permute-start.11 = (bf16[8,3584]{1,0:T(8,128)(2,1)S(1)}, bf16[8,3584]{1,0:T(8,128)(2,1)S(1)}, u32[]{:S(2)}, u32[]{:S(2)}) collective-permute-start(bf16[8,3584]{1,0:T(8,128)(2,1)S(1)} %fusion.5), channel_id=1, source_target_pairs={{0,2},{1,3},{2,0},{3,1},{4,12},{5,13},{6,14},{7,15},{8,10},{9,11},... | collective-permute-start | bytes 172040 | tf_op jit(solution)/shard_map/ppermute | solution.py:397
  52.1 4.2 %collective-permute-start.15 = (bf16[8,3584]{1,0:T(8,128)(2,1)S(1)}, bf16[8,3584]{1,0:T(8,128)(2,1)S(1)}, u32[]{:S(2)}, u32[]{:S(2)}) collective-permute-start(bf16[8,3584]{1,0:T(8,128)(2,1)S(1)} %fusion.2), channel_id=1, source_target_pairs={{0,8},{1,9},{2,10},{3,11},{4,6},{5,7},{6,4},{7,5},{8,0},{9,1},{10,... | collective-permute-start | bytes 172040 | tf_op jit(solution)/shard_map/ppermute | solution.py:397

commit v13 on v12

--- a/solution.py
+++ b/solution.py
@@ -203,9 +203,9 @@
     )
 
 
-def reorder(value, turn):
-    value = value.astype(F32)
-    return jnp.where(turn == 1, regroup(value, 2, 4), regroup(value, 4, 2)).astype(BF16)
+def swap_quarters(value):
+    quarter = value.shape[0] // 4
+    return jnp.concatenate([value[i * quarter : (i + 1) * quarter] for i in (0, 2, 1, 3)], axis=0)
 
 
 def half_down_copies(share, place_ref, down_ref, sdown_ref, out_ref, lower, sems):
@@ -231,21 +231,42 @@
     return copies
 
 
+def load_down_kernel(share, place_ref, down_ref, sdown_ref, out_ref, sems):
+    run_copies(half_down_copies(share, place_ref, down_ref, sdown_ref, out_ref, 0, sems))
+
+
+def load_down(place, down, sdown, cut, share):
+    units = down.shape[0] + LANES
+    return pl.pallas_call(
+        functools.partial(load_down_kernel, share),
+        in_specs=[SMEM_SPEC] + [ANY_SPEC] * 2,
+        out_specs=VMEM_SPEC,
+        out_shape=pltpu.VMEM((units, cut), BF16),
+        scratch_shapes=[pltpu.SemaphoreType.DMA((4,))],
+        cost_estimate=pl.CostEstimate(flops=0, bytes_accessed=4 * units * cut, transcendentals=0),
+        compiler_params=pltpu.CompilerParams(vmem_limit_bytes=1 << 20),
+        name="load_down",
+    )(place, in_hbm(down), in_hbm(sdown))
+
+
 def late_half_kernel(
-    share, place_ref, own_ref, other_ref, first_ref, up_ref, down_ref, sdown_ref, acc_ref, second_ref, x, sems
+    share, place_ref, own_ref, other_ref, first_ref, up_ref, down_ref, sdown_ref, acc_ref, later_ref, x, sems
 ):
-    copies = half_down_copies(share, place_ref, down_ref, sdown_ref, second_ref, 0, sems)
-    for copy in copies:
-        copy.start()
     width, hidden = up_ref.shape
     half, columns = own_ref.shape
     cut = width + LANES - columns
-    odd = place_ref[0] % 2
-    x[:half, :] = reorder(own_ref[...], odd)
-    x[half:, :] = reorder(other_ref[...], 1 - odd)
+    copies = half_down_copies(share, place_ref, down_ref, sdown_ref, later_ref, cut, sems)
+    for copy in copies:
+        copy.start()
+    x[:half, :] = own_ref[...]
+    x[half:, :] = other_ref[...]
     rows = x[:, : width - cut]
-    acc_ref[:, :hidden] = jnp.dot(rows, first_ref[cut:, :hidden], preferred_element_type=F32)
-    acc_ref[:, hidden : 2 * hidden] = jnp.dot(rows, up_ref[cut:, :], preferred_element_type=F32)
+    tile = min(2 * LANES, hidden)
+    for at in range(0, hidden, tile):
+        acc_ref[:, at : at + tile] = jnp.dot(rows, first_ref[cut:, at : at + tile], preferred_element_type=F32)
+        acc_ref[:, hidden + at : hidden + at + tile] = jnp.dot(
+            rows, up_ref[cut:, at : at + tile], preferred_element_type=F32
+        )
     acc_ref[:, 2 * hidden : 2 * hidden + 2 * LANES] = jnp.dot(
         rows, first_ref[cut:, hidden:], preferred_element_type=F32
     )
@@ -256,13 +277,10 @@
 
 
 def early_half_kernel(
-    share, place_ref, own_ref, other_ref, first_ref, up_ref, acc_ref, second_ref, down_ref, sdown_ref,
-    own_out_ref, other_out_ref, act_ref, later_ref, x, sems,
+    share, place_ref, own_ref, other_ref, first_ref, up_ref, acc_ref, second_ref,
+    own_out_ref, other_out_ref, act_ref, x,
 ):
     half, cut = own_ref.shape
-    copies = half_down_copies(share, place_ref, down_ref, sdown_ref, later_ref, cut, sems)
-    for copy in copies:
-        copy.start()
     hidden = up_ref.shape[1]
     x[:half, :] = own_ref[...]
     x[half:, :] = other_ref[...]
@@ -287,19 +305,16 @@
         total = jnp.dot(act_ref[...], second_ref[:, at], preferred_element_type=F32).astype(BF16)
         own_out_ref[:, at] = total[:half]
         other_out_ref[:, at] = total[half:]
-    for copy in copies:
-        copy.wait()
-
-
-def last_half_kernel(place_ref, act_ref, second_ref, own_out_ref, other_out_ref):
+
+
+def last_half_kernel(act_ref, second_ref, own_out_ref, other_out_ref):
     half, columns = own_out_ref.shape
-    odd = place_ref[0] % 2
     piece = columns // 2
     for i in range(2):
         at = slice(i * piece, (i + 1) * piece)
-        total = jnp.dot(act_ref[...], second_ref[:, at], preferred_element_type=F32)
-        own_out_ref[:, at] = reorder(total[:half], 1 - odd)
-        other_out_ref[:, at] = reorder(total[half:], odd)
+        total = jnp.dot(act_ref[...], second_ref[:, at], preferred_element_type=F32).astype(BF16)
+        own_out_ref[:, at] = swap_quarters(total[:half])
+        other_out_ref[:, at] = swap_quarters(total[half:])
 
 
 def estimate(rows, depth, columns):
@@ -308,45 +323,43 @@
     )
 
 
-def pair_rows(place, own, other, first, up, down, sdown, share):
+def pair_rows(place, own, other, first, up, second, down, sdown, share):
     half, cut = own[0].shape
     hidden, width = down.shape
-    down, sdown = in_hbm(down), in_hbm(sdown)
     units = hidden + LANES
-    acc, second = pl.pallas_call(
+    acc, later = pl.pallas_call(
         functools.partial(late_half_kernel, share),
         in_specs=[SMEM_SPEC] + [VMEM_SPEC] * 4 + [ANY_SPEC] * 2,
         out_specs=[VMEM_SPEC] * 2,
-        out_shape=[pltpu.VMEM((2 * half, 2 * units + LANES), F32), pltpu.VMEM((units, cut), BF16)],
+        out_shape=[pltpu.VMEM((2 * half, 2 * units + LANES), F32), pltpu.VMEM((units, width - cut), BF16)],
         scratch_shapes=[pltpu.VMEM((2 * half, own[1].shape[1]), BF16), pltpu.SemaphoreType.DMA((4,))],
         cost_estimate=estimate(2 * half, width - cut, 2 * units),
         compiler_params=pltpu.CompilerParams(vmem_limit_bytes=10 << 20),
         name="late_half",
-    )(place, own[1], other[1], first, up, down, sdown)
-    own_out, other_out, act, later = pl.pallas_call(
+    )(place, own[1], other[1], first, up, in_hbm(down), in_hbm(sdown))
+    own_out, other_out, act = pl.pallas_call(
         functools.partial(early_half_kernel, share),
-        in_specs=[SMEM_SPEC] + [VMEM_SPEC] * 6 + [ANY_SPEC] * 2,
-        out_specs=[VMEM_SPEC] * 4,
+        in_specs=[SMEM_SPEC] + [VMEM_SPEC] * 6,
+        out_specs=[VMEM_SPEC] * 3,
         out_shape=[
             pltpu.VMEM((half, cut), BF16),
             pltpu.VMEM((half, cut), BF16),
             pltpu.VMEM((2 * half, units), BF16),
-            pltpu.VMEM((units, width - cut), BF16),
         ],
-        scratch_shapes=[pltpu.VMEM((2 * half, cut), BF16), pltpu.SemaphoreType.DMA((4,))],
+        scratch_shapes=[pltpu.VMEM((2 * half, cut), BF16)],
         cost_estimate=estimate(2 * half, cut, 3 * units),
         compiler_params=pltpu.CompilerParams(vmem_limit_bytes=10 << 20),
         name="early_half",
-    )(place, own[0], other[0], first, up, acc, second, down, sdown)
+    )(place, own[0], other[0], first, up, acc, second)
     last = pl.pallas_call(
         last_half_kernel,
-        in_specs=[SMEM_SPEC] + [VMEM_SPEC] * 2,
+        in_specs=[VMEM_SPEC] * 2,
         out_specs=[VMEM_SPEC] * 2,
         out_shape=[pltpu.VMEM((half, width - cut), BF16)] * 2,
         cost_estimate=estimate(2 * half, width - cut, units),
         compiler_params=pltpu.CompilerParams(vmem_limit_bytes=10 << 20),
         name="last_half",
-    )(place, act, later)
+    )(act, later)
     return own_out, last[0], other_out, last[1]
 
 
@@ -398,7 +411,8 @@
 
 
 X, Z1, Z2, CORE = (2, 0), (0, 1), (0, 2), (1, 0)
-PHASES = ((Z2, X), (Z1, Z2), (X, Z1))
+GATHER = ((Z2, X), (Z1, Z2), (X, Z1))
+SCATTER = ((X, Z1), (Z1, X), (Z2, Z2))
 
 
 def stack(*values):
@@ -433,30 +447,30 @@
     cut = width // 2
     own = [packed[:, :cut], packed[:, cut:]]
     loads = (
-        lambda *ready: None,
+        lambda *ready: load_down(after(place, *ready), down, down_shared, cut, share),
         lambda *ready: load_gate(after(place, *ready), gate, gate_shared, up_shared, share),
         lambda *ready: load_up(after(up, *ready)),
     )
     loaded = []
-    for phase, load in zip(PHASES, loads):
+    for phase, load in zip(GATHER, loads):
         got = [flipped(part, *pairs) for part, pairs in zip(own, (phase, phase[::-1]))]
-        weights = load(*own)
-        if weights is not None:
-            got, weights = lax.optimization_barrier((got, weights))
-            loaded.append(weights)
+        got[0], weights = lax.optimization_barrier((got[0], load(*own)))
+        loaded.append(weights)
         own = [stack(part, add) for part, add in zip(own, got)]
-    first, up = loaded
+    second, first, up = loaded
+    odd = place[0] % 2
+    own = [jnp.where(odd == i, part, regroup(part, 4, 2)) for i, part in enumerate(own)]
     other = [flipped(part, CORE, CORE) for part in own]
 
-    outs = pair_rows(place, own, other, first, up, down, down_shared, share)
+    outs = pair_rows(place, own, other, first, up, second, down, down_shared, share)
 
     totals = [[own, flipped(other, CORE, CORE)] for own, other in zip(outs[:2], outs[2:])]
-    for phase in reversed(PHASES):
-        for i, pairs in enumerate((phase, phase[::-1])):
+    for phase in SCATTER:
+        for i, bits in enumerate(phase):
             total = totals[i]
             half = total[0].shape[0] // 2
             sent = f32_sum(*(t[half:] for t in total)).astype(BF16)
-            totals[i] = [f32_sum(*(t[:half] for t in total)), flipped(sent, *pairs)]
+            totals[i] = [f32_sum(*(t[:half] for t in total)), flipped(sent, bits, bits)]
     return jnp.concatenate([f32_sum(*total).astype(BF16) for total in totals], axis=1)
 
 

time: 57.2 us -> 55.9 us (0.977)
  starting transfers between devices: 24.4 us -> 18.4 us
  waiting for transfers between devices: 14.8 us -> 18.2 us
  Pallas kernels: 16.5 us -> 17.5 us
    ppermute x16, starting transfers between devices: 24.4 us -> 18.4 us  [flipped(): return lax.ppermute(value, ('node', 'local'), pairs)]
    ppermute x16, waiting for transfers between devices: 14.8 us -> 18.2 us  [flipped(): return lax.ppermute(value, ('node', 'local'), pairs)]
    pallas_call x1 -> x2, Pallas kernels: 0.88 us -> 3.25 us  [the longest x1 2.3 us: load_down(): pl.pallas_call(functools.partial(load_down_kernel, share), in_specs=[SMEM...]
    pallas_call x1, Pallas kernels: 3.49 us -> 2.64 us  [pair_rows(): pl.pallas_call(functools.partial(early_half_kernel, share), in_specs=[SME...]
  transfers between devices with their start and end apart: 16 -> 16, of which waited for: 9 -> 9; matrix products, arithmetic and copies ran while one was open for 1% -> 1% of each run, Pallas kernels for 21% -> 25%
where the time goes in v13:
time: 55.9 us; the launch traced here: 55.7 us
  starting transfers between devices  18.4 us (33%)
  waiting for transfers between devices  18.2 us (33%)
  Pallas kernels  17.5 us (31%)
  other arithmetic  1.3 us (2%)
    ppermute x16, starting transfers between devices, flipped(): return lax.ppermute(value, ('node', 'local'), pairs)  18.4 us
    ppermute x16, waiting for transfers between devices, flipped(): return lax.ppermute(value, ('node', 'local'), pairs)  18.2 us
    pallas_call x1, Pallas kernels, load_gate(): pl.pallas_call(functools.partial(load_gate_kernel, share), in_specs=[SMEM...  4.31 us
    pallas_call x1, Pallas kernels, load_up(): pl.pallas_call(load_up_kernel, in_specs=[ANY_SPEC], out_specs=VMEM_SPEC,...  3.17 us
    pallas_call x1, Pallas kernels, pair_rows(): pl.pallas_call(functools.partial(late_half_kernel, share), in_specs=[SMEM...  3.07 us
    pallas_call x1, Pallas kernels, pair_rows(): pl.pallas_call(functools.partial(early_half_kernel, share), in_specs=[SME...  2.64 us
    pallas_call x1, Pallas kernels, load_down(): pl.pallas_call(functools.partial(load_down_kernel, share), in_specs=[SMEM...  2.3 us
  transfers between devices with their start and end apart: 16, of which 9 were waited for; matrix products, arithmetic and copies ran while one was open for 1% of the time, Pallas kernels for 25%

profile of v13, /device:TPU:0, one launch (start us, length us, event | category | flops | bytes accessed | tf_op | source)
XLA Modules:
  0.0 55.7 jit_solution(12688187302174829547)
XLA Ops:
  0.0 1.1 %pack_rows.1 = bf16[8,7296]{1,0:T(8,128)(2,1)S(1)} custom-call(bf16[8,7168]{1,0:T(8,128)(2,1)} %tokens_ref.1, s32[4,8]{1,0:T(4,128)} %bitcast.10, bf16[4,8]{1,0:T(4,128)(2,1)} %bitcast.11), custom_call_target="tpu_custom_call" | custom-call | tf_op jit(solution)/shard_map/pack_rows/pallas_call | solution.py:48
  1.1 4.1 %collective-permute-start = (bf16[8,3584]{1,0:T(8,128)(2,1)S(1)}, bf16[8,3584]{1,0:T(8,128)(2,1)S(1)}, u32[]{:S(2)}, u32[]{:S(2)}) collective-permute-start(bf16[8,3584]{1,0:T(8,128)(2,1)S(1)} %get-tuple-element.47), channel_id=1, source_target_pairs={{0,2},{1,3},{2,0},{3,1},{4,12},{5,13},{6,14},{7,15},{8,10},{9,11},... | collective-permute-start | bytes 172040 | tf_op jit(solution)/shard_map/ppermute | solution.py:410
  5.2 1.6 %collective-permute-start.2 = (bf16[8,3712]{1,0:T(8,128)(2,1)S(1)}, bf16[8,3712]{1,0:T(8,128)(2,1)S(1)}, u32[]{:S(2)}, u32[]{:S(2)}) collective-permute-start(bf16[8,3712]{1,0:T(8,128)(2,1)S(1)} %get-tuple-element.46), channel_id=1, source_target_pairs={{0,8},{1,9},{2,10},{3,11},{4,6},{5,7},{6,4},{7,5},{8,0},{9,1},{10,... | collective-permute-start | bytes 178184 | tf_op jit(solution)/shard_map/ppermute | solution.py:410
  6.8 2.3 %load_down.1.second_ref = bf16[640,3584]{1,0:T(8,128)(2,1)S(1)} custom-call(s32[1]{0:T(128)} %bitcast.place_ref, bf16[512,7168]{1,0:T(8,128)(2,1)} %bitcast.6, bf16[512,7168]{1,0:T(8,128)(2,1)} %sdown_ref.3), custom_call_target="tpu_custom_call" | custom-call | bytes 9175040 | tf_op jit(solution)/shard_map/load_down/pallas_call | solution.py:240
  9.1 0.0 collective-permute-done
  9.1 1.6 %collective-permute-start.1 = (bf16[16,3584]{1,0:T(8,128)(2,1)S(1)}, bf16[16,3584]{1,0:T(8,128)(2,1)S(1)}, u32[]{:S(2)}, u32[]{:S(2)}) collective-permute-start(bf16[16,3584]{1,0:T(8,128)(2,1)S(1)} %pad_maximum_fusion.3), channel_id=1, source_target_pairs={{0,1},{1,0},{2,3},{3,2},{4,6},{5,7},{6,4},{7,5},{8,9},{9,8},{10,11... | collective-permute-start | bytes 344072 | tf_op jit(solution)/shard_map/ppermute | solution.py:410
  10.7 0.0 collective-permute-done.2
  10.8 3.0 %collective-permute-start.4 = (bf16[16,3712]{1,0:T(8,128)(2,1)S(1)}, bf16[16,3712]{1,0:T(8,128)(2,1)S(1)}, u32[]{:S(2)}, u32[]{:S(2)}) collective-permute-start(bf16[16,3712]{1,0:T(8,128)(2,1)S(1)} %pad_maximum_fusion.2), channel_id=1, source_target_pairs={{0,2},{1,3},{2,0},{3,1},{4,5},{5,4},{6,7},{7,6},{8,10},{9,11},{10,... | collective-permute-start | bytes 356360 | tf_op jit(solution)/shard_map/ppermute | solution.py:410
  13.7 4.3 %load_gate.1.first_ref = bf16[7168,768]{1,0:T(8,128)(2,1)S(1)} custom-call(s32[1]{0:T(128)} %bitcast.place_ref, bf16[7168,512]{1,0:T(8,128)(2,1)} %bitcast.9, bf16[7168,512]{1,0:T(8,128)(2,1)} %sgate_ref.1, bf16[7168,512]{1,0:T(8,128)(2,1)} %sup_ref.1), custom_call_target="tpu_custom_call" | custom-call | bytes 22020096 | tf_op jit(solution)/shard_map/load_gate/pallas_call | solution.py:78
  18.1 0.0 collective-permute-done.1
  18.1 0.8 %collective-permute-start.3 = (bf16[32,3584]{1,0:T(8,128)(2,1)S(1)}, bf16[32,3584]{1,0:T(8,128)(2,1)S(1)}, u32[]{:S(2)}, u32[]{:S(2)}) collective-permute-start(bf16[32,3584]{1,0:T(8,128)(2,1)S(1)} %pad_maximum_fusion.1), channel_id=1, source_target_pairs={{0,8},{1,9},{2,10},{3,11},{4,5},{5,4},{6,7},{7,6},{8,0},{9,1},{10,... | collective-permute-start | bytes 688136 | tf_op jit(solution)/shard_map/ppermute | solution.py:410
  18.9 0.0 collective-permute-done.4
  18.9 0.1 collective-permute-start.6
  19.0 3.2 %load_up.1.up_ref = bf16[7168,512]{1,0:T(8,128)(2,1)S(1)} custom-call(bf16[7168,512]{1,0:T(8,128)(2,1)} %bitcast.8), custom_call_target="tpu_custom_call" | custom-call | bytes 14680064 | tf_op jit(solution)/shard_map/load_up/pallas_call | solution.py:106
  22.2 2.0 %collective-permute-done.3 = bf16[32,3584]{1,0:T(8,128)(2,1)S(1)} collective-permute-done((bf16[32,3584]{1,0:T(8,128)(2,1)S(1)}, bf16[32,3584]{1,0:T(8,128)(2,1)S(1)}, u32[]{:S(2)}, u32[]{:S(2)}) %collective-permute-start.3) | collective-permute-done | bytes 229408 | tf_op jit(solution)/shard_map/ppermute | solution.py:410
  24.3 0.8 %collective-permute-done.6 = bf16[32,3712]{1,0:T(8,128)(2,1)S(1)} collective-permute-done((bf16[32,3712]{1,0:T(8,128)(2,1)S(1)}, bf16[32,3712]{1,0:T(8,128)(2,1)S(1)}, u32[]{:S(2)}, u32[]{:S(2)}) %collective-permute-start.6) | collective-permute-done | bytes 237600 | tf_op jit(solution)/shard_map/ppermute | solution.py:410
  25.2 0.1 maximum_select_fusion.own_ref
  25.3 0.1 collective-permute-start.7
  25.4 0.1 maximum_select_fusion.1.own_ref
  25.5 0.6 %collective-permute-start.5 = (bf16[64,3584]{1,0:T(8,128)(2,1)S(1)}, bf16[64,3584]{1,0:T(8,128)(2,1)S(1)}, u32[]{:S(2)}, u32[]{:S(2)}) collective-permute-start(bf16[64,3584]{1,0:T(8,128)(2,1)S(1)} %maximum_select_fusion.1.own_ref), channel_id=1, source_target_pairs={{0,4},{1,5},{2,6},{3,7},{4,0},{5,1},{6,2},{7,3},{8,12},{9,13},{10,... | collective-permute-start | bytes 1376264 | tf_op jit(solution)/shard_map/ppermute | solution.py:410
  26.1 1.2 %collective-permute-done.7.other_ref = bf16[64,3712]{1,0:T(8,128)(2,1)S(1)} collective-permute-done((bf16[64,3712]{1,0:T(8,128)(2,1)S(1)}, bf16[64,3712]{1,0:T(8,128)(2,1)S(1)}, u32[]{:S(2)}, u32[]{:S(2)}) %collective-permute-start.7) | collective-permute-done | bytes 475168 | tf_op jit(solution)/shard_map/ppermute | solution.py:410
  27.2 3.1 %late_half.1 = (f32[128,1408]{1,0:T(8,128)S(1)}, bf16[640,3584]{1,0:T(8,128)(2,1)S(1)}) custom-call(s32[1]{0:T(128)} %bitcast.place_ref, bf16[64,3712]{1,0:T(8,128)(2,1)S(1)} %maximum_select_fusion.own_ref, bf16[64,3712]{1,0:T(8,128)(2,1)S(1)} %collective-permute-done.7.other_ref, bf16[7168,768]{1,0:T(8,128)(2,1)S(1)} %load_gate.1.first_ref, ...), custom_call_target="tpu_custom_call" | custom-call | flops 1174405120 | bytes 9175040 | tf_op jit(solution)/shard_map/late_half/pallas_call | solution.py:330
  30.3 0.0 collective-permute-done.5.other_ref
  30.3 2.6 %early_half.1 = (bf16[64,3584]{1,0:T(8,128)(2,1)S(1)}, bf16[64,3584]{1,0:T(8,128)(2,1)S(1)}, bf16[128,640]{1,0:T(8,128)(2,1)S(1)}) custom-call(s32[1]{0:T(128)} %bitcast.place_ref, bf16[64,3584]{1,0:T(8,128)(2,1)S(1)} %maximum_select_fusion.1.own_ref, bf16[64,3584]{1,0:T(8,128)(2,1)S(1)} %collective-permute-done.5.other_ref, ...), custom_call_target="tpu_custom_call" | custom-call | flops 1761607680 | bytes 13762560 | tf_op jit(solution)/shard_map/early_half/pallas_call | solution.py:340
  33.0 0.2 collective-permute-start.8
  33.1 0.9 %last_half.1 = (bf16[64,3584]{1,0:T(8,128)(2,1)S(1)}, bf16[64,3584]{1,0:T(8,128)(2,1)S(1)}) custom-call(bf16[128,640]{1,0:T(8,128)(2,1)S(1)} %get-tuple-element.33.act_ref, bf16[640,3584]{1,0:T(8,128)(2,1)S(1)} %get-tuple-element.34.second_ref), custom_call_target="tpu_custom_call" | custom-call | flops 587202560 | bytes 4587520 | tf_op jit(solution)/shard_map/last_half/pallas_call | solution.py:354
  34.1 0.5 collective-permute-start.12
  34.5 0.3 collective-permute-done.8
  34.8 0.1 add_convert_fusion.1
  34.9 1.4 %collective-permute-start.9 = (bf16[32,3584]{1,0:T(8,128)(2,1)S(1)}, bf16[32,3584]{1,0:T(8,128)(2,1)S(1)}, u32[]{:S(2)}, u32[]{:S(2)}) collective-permute-start(bf16[32,3584]{1,0:T(8,128)(2,1)S(1)} %get-tuple-element.37), channel_id=1, source_target_pairs={{0,8},{1,9},{2,10},{3,11},{4,12},{5,13},{6,14},{7,15},{8,0},{9,1},... | collective-permute-start | bytes 688136 | tf_op jit(solution)/shard_map/ppermute | solution.py:410
  36.3 0.0 collective-permute-done.12
  36.3 0.1 add_convert_fusion
  36.4 0.1 collective-permute-start.13
  36.5 6.2 %collective-permute-done.9 = bf16[32,3584]{1,0:T(8,128)(2,1)S(1)} collective-permute-done((bf16[32,3584]{1,0:T(8,128)(2,1)S(1)}, bf16[32,3584]{1,0:T(8,128)(2,1)S(1)}, u32[]{:S(2)}, u32[]{:S(2)}) %collective-permute-start.9) | collective-permute-done | bytes 229408 | tf_op jit(solution)/shard_map/ppermute | solution.py:410
  42.7 0.1 collective-permute-start.10
  42.8 1.3 %collective-permute-done.13 = bf16[32,3584]{1,0:T(8,128)(2,1)S(1)} collective-permute-done((bf16[32,3584]{1,0:T(8,128)(2,1)S(1)}, bf16[32,3584]{1,0:T(8,128)(2,1)S(1)}, u32[]{:S(2)}, u32[]{:S(2)}) %collective-permute-start.13) | collective-permute-done | bytes 229408 | tf_op jit(solution)/shard_map/ppermute | solution.py:410
  44.1 1.4 %collective-permute-start.14 = (bf16[16,3584]{1,0:T(8,128)(2,1)S(1)}, bf16[16,3584]{1,0:T(8,128)(2,1)S(1)}, u32[]{:S(2)}, u32[]{:S(2)}) collective-permute-start(bf16[16,3584]{1,0:T(8,128)(2,1)S(1)} %get-tuple-element.43), channel_id=1, source_target_pairs={{0,8},{1,9},{2,10},{3,11},{4,12},{5,13},{6,14},{7,15},{8,0},{9,1},... | collective-permute-start | bytes 344072 | tf_op jit(solution)/shard_map/ppermute | solution.py:410
  45.4 2.1 %collective-permute-done.10 = bf16[16,3584]{1,0:T(8,128)(2,1)S(1)} collective-permute-done((bf16[16,3584]{1,0:T(8,128)(2,1)S(1)}, bf16[16,3584]{1,0:T(8,128)(2,1)S(1)}, u32[]{:S(2)}, u32[]{:S(2)}) %collective-permute-start.10) | collective-permute-done | bytes 114720 | tf_op jit(solution)/shard_map/ppermute | solution.py:410
  47.6 1.7 %collective-permute-start.11 = (bf16[8,3584]{1,0:T(8,128)(2,1)S(1)}, bf16[8,3584]{1,0:T(8,128)(2,1)S(1)}, u32[]{:S(2)}, u32[]{:S(2)}) collective-permute-start(bf16[8,3584]{1,0:T(8,128)(2,1)S(1)} %fusion.5), channel_id=1, source_target_pairs={{0,2},{1,3},{2,0},{3,1},{4,6},{5,7},{6,4},{7,5},{8,10},{9,11},{10,... | collective-permute-start | bytes 172040 | tf_op jit(solution)/shard_map/ppermute | solution.py:410
  49.3 0.0 collective-permute-done.14
  49.3 1.4 %collective-permute-start.15 = (bf16[8,3584]{1,0:T(8,128)(2,1)S(1)}, bf16[8,3584]{1,0:T(8,128)(2,1)S(1)}, u32[]{:S(2)}, u32[]{:S(2)}) collective-permute-start(bf16[8,3584]{1,0:T(8,128)(2,1)S(1)} %fusion.2), channel_id=1, source_target_pairs={{0,2},{1,3},{2,0},{3,1},{4,6},{5,7},{6,4},{7,5},{8,10},{9,11},{10,... | collective-permute-start | bytes 172040 | tf_op jit(solution)/shard_map/ppermute | solution.py:410
  50.7 2.7 %collective-permute-done.11 = bf16[8,3584]{1,0:T(8,128)(2,1)S(1)} collective-permute-done((bf16[8,3584]{1,0:T(8,128)(2,1)S(1)}, bf16[8,3584]{1,0:T(8,128)(2,1)S(1)}, u32[]{:S(2)}, u32[]{:S(2)}) %collective-permute-start.11) | collective-permute-done | bytes 57376 | tf_op jit(solution)/shard_map/ppermute | solution.py:410
  53.4 1.7 %collective-permute-done.15 = bf16[8,3584]{1,0:T(8,128)(2,1)S(1)} collective-permute-done((bf16[8,3584]{1,0:T(8,128)(2,1)S(1)}, bf16[8,3584]{1,0:T(8,128)(2,1)S(1)}, u32[]{:S(2)}, u32[]{:S(2)}) %collective-permute-start.15) | collective-permute-done | bytes 57376 | tf_op jit(solution)/shard_map/ppermute | solution.py:410
  55.1 0.7 %pad_maximum_fusion.4 = bf16[8,7168]{1,0:T(8,128)(2,1)} fusion(bf16[8,3584]{1,0:T(8,128)(2,1)S(1)} %fusion.4, bf16[8,3584]{1,0:T(8,128)(2,1)S(1)} %fusion.7), kind=kLoop, calls=%fused_computation.26 | loop fusion | flops 229376 | bytes 229376 | tf_op jit(solution)/shard_map/concatenate | solution.py:474
  (26 shorter events, 0.3 us)
Async XLA Ops:
  1.1 8.0 %collective-permute-start = (bf16[8,3584]{1,0:T(8,128)(2,1)S(1)}, bf16[8,3584]{1,0:T(8,128)(2,1)S(1)}, u32[]{:S(2)}, u32[]{:S(2)}) collective-permute-start(bf16[8,3584]{1,0:T(8,128)(2,1)S(1)} %get-tuple-element.47), channel_id=1, source_target_pairs={{0,2},{1,3},{2,0},{3,1},{4,12},{5,13},{6,14},{7,15},{8,10},{9,11},... | collective-permute-start | bytes 172040 | tf_op jit(solution)/shard_map/ppermute | solution.py:410
  5.2 5.5 %collective-permute-start.2 = (bf16[8,3712]{1,0:T(8,128)(2,1)S(1)}, bf16[8,3712]{1,0:T(8,128)(2,1)S(1)}, u32[]{:S(2)}, u32[]{:S(2)}) collective-permute-start(bf16[8,3712]{1,0:T(8,128)(2,1)S(1)} %get-tuple-element.46), channel_id=1, source_target_pairs={{0,8},{1,9},{2,10},{3,11},{4,6},{5,7},{6,4},{7,5},{8,0},{9,1},{10,... | collective-permute-start | bytes 178184 | tf_op jit(solution)/shard_map/ppermute | solution.py:410
  9.1 9.0 %collective-permute-start.1 = (bf16[16,3584]{1,0:T(8,128)(2,1)S(1)}, bf16[16,3584]{1,0:T(8,128)(2,1)S(1)}, u32[]{:S(2)}, u32[]{:S(2)}) collective-permute-start(bf16[16,3584]{1,0:T(8,128)(2,1)S(1)} %pad_maximum_fusion.3), channel_id=1, source_target_pairs={{0,1},{1,0},{2,3},{3,2},{4,6},{5,7},{6,4},{7,5},{8,9},{9,8},{10,11... | collective-permute-start | bytes 344072 | tf_op jit(solution)/shard_map/ppermute | solution.py:410
  10.8 8.1 %collective-permute-start.4 = (bf16[16,3712]{1,0:T(8,128)(2,1)S(1)}, bf16[16,3712]{1,0:T(8,128)(2,1)S(1)}, u32[]{:S(2)}, u32[]{:S(2)}) collective-permute-start(bf16[16,3712]{1,0:T(8,128)(2,1)S(1)} %pad_maximum_fusion.2), channel_id=1, source_target_pairs={{0,2},{1,3},{2,0},{3,1},{4,5},{5,4},{6,7},{7,6},{8,10},{9,11},{10,... | collective-permute-start | bytes 356360 | tf_op jit(solution)/shard_map/ppermute | solution.py:410
  18.1 6.1 %collective-permute-start.3 = (bf16[32,3584]{1,0:T(8,128)(2,1)S(1)}, bf16[32,3584]{1,0:T(8,128)(2,1)S(1)}, u32[]{:S(2)}, u32[]{:S(2)}) collective-permute-start(bf16[32,3584]{1,0:T(8,128)(2,1)S(1)} %pad_maximum_fusion.1), channel_id=1, source_target_pairs={{0,8},{1,9},{2,10},{3,11},{4,5},{5,4},{6,7},{7,6},{8,0},{9,1},{10,... | collective-permute-start | bytes 688136 | tf_op jit(solution)/shard_map/ppermute | solution.py:410
  18.9 6.2 %collective-permute-start.6 = (bf16[32,3712]{1,0:T(8,128)(2,1)S(1)}, bf16[32,3712]{1,0:T(8,128)(2,1)S(1)}, u32[]{:S(2)}, u32[]{:S(2)}) collective-permute-start(bf16[32,3712]{1,0:T(8,128)(2,1)S(1)} %pad_maximum_fusion), channel_id=1, source_target_pairs={{0,1},{1,0},{2,3},{3,2},{4,12},{5,13},{6,14},{7,15},{8,9},{9,8},{1... | collective-permute-start | bytes 712712 | tf_op jit(solution)/shard_map/ppermute | solution.py:410
  25.3 1.9 %collective-permute-start.7 = (bf16[64,3712]{1,0:T(8,128)(2,1)S(1)}, bf16[64,3712]{1,0:T(8,128)(2,1)S(1)}, u32[]{:S(2)}, u32[]{:S(2)}) collective-permute-start(bf16[64,3712]{1,0:T(8,128)(2,1)S(1)} %maximum_select_fusion.own_ref), channel_id=1, source_target_pairs={{0,4},{1,5},{2,6},{3,7},{4,0},{5,1},{6,2},{7,3},{8,12},{9,13},{10,... | collective-permute-start | bytes 1425416 | tf_op jit(solution)/shard_map/ppermute | solution.py:410
  25.5 4.8 %collective-permute-start.5 = (bf16[64,3584]{1,0:T(8,128)(2,1)S(1)}, bf16[64,3584]{1,0:T(8,128)(2,1)S(1)}, u32[]{:S(2)}, u32[]{:S(2)}) collective-permute-start(bf16[64,3584]{1,0:T(8,128)(2,1)S(1)} %maximum_select_fusion.1.own_ref), channel_id=1, source_target_pairs={{0,4},{1,5},{2,6},{3,7},{4,0},{5,1},{6,2},{7,3},{8,12},{9,13},{10,... | collective-permute-start | bytes 1376264 | tf_op jit(solution)/shard_map/ppermute | solution.py:410
  33.0 1.9 %collective-permute-start.8 = (bf16[64,3584]{1,0:T(8,128)(2,1)S(1)}, bf16[64,3584]{1,0:T(8,128)(2,1)S(1)}, u32[]{:S(2)}, u32[]{:S(2)}) collective-permute-start(bf16[64,3584]{1,0:T(8,128)(2,1)S(1)} %get-tuple-element.32), channel_id=1, source_target_pairs={{0,4},{1,5},{2,6},{3,7},{4,0},{5,1},{6,2},{7,3},{8,12},{9,13},{10,... | collective-permute-start | bytes 1376264 | tf_op jit(solution)/shard_map/ppermute | solution.py:410
  34.1 2.2 %collective-permute-start.12 = (bf16[64,3584]{1,0:T(8,128)(2,1)S(1)}, bf16[64,3584]{1,0:T(8,128)(2,1)S(1)}, u32[]{:S(2)}, u32[]{:S(2)}) collective-permute-start(bf16[64,3584]{1,0:T(8,128)(2,1)S(1)} %get-tuple-element.36), channel_id=1, source_target_pairs={{0,4},{1,5},{2,6},{3,7},{4,0},{5,1},{6,2},{7,3},{8,12},{9,13},{10,... | collective-permute-start | bytes 1376264 | tf_op jit(solution)/shard_map/ppermute | solution.py:410
  34.9 7.7 %collective-permute-start.9 = (bf16[32,3584]{1,0:T(8,128)(2,1)S(1)}, bf16[32,3584]{1,0:T(8,128)(2,1)S(1)}, u32[]{:S(2)}, u32[]{:S(2)}) collective-permute-start(bf16[32,3584]{1,0:T(8,128)(2,1)S(1)} %get-tuple-element.37), channel_id=1, source_target_pairs={{0,8},{1,9},{2,10},{3,11},{4,12},{5,13},{6,14},{7,15},{8,0},{9,1},... | collective-permute-start | bytes 688136 | tf_op jit(solution)/shard_map/ppermute | solution.py:410
  36.4 7.6 %collective-permute-start.13 = (bf16[32,3584]{1,0:T(8,128)(2,1)S(1)}, bf16[32,3584]{1,0:T(8,128)(2,1)S(1)}, u32[]{:S(2)}, u32[]{:S(2)}) collective-permute-start(bf16[32,3584]{1,0:T(8,128)(2,1)S(1)} %get-tuple-element.39), channel_id=1, source_target_pairs={{0,1},{1,0},{2,3},{3,2},{4,5},{5,4},{6,7},{7,6},{8,9},{9,8},{10,11... | collective-permute-start | bytes 688136 | tf_op jit(solution)/shard_map/ppermute | solution.py:410
  42.7 4.9 %collective-permute-start.10 = (bf16[16,3584]{1,0:T(8,128)(2,1)S(1)}, bf16[16,3584]{1,0:T(8,128)(2,1)S(1)}, u32[]{:S(2)}, u32[]{:S(2)}) collective-permute-start(bf16[16,3584]{1,0:T(8,128)(2,1)S(1)} %get-tuple-element.41), channel_id=1, source_target_pairs={{0,1},{1,0},{2,3},{3,2},{4,5},{5,4},{6,7},{7,6},{8,9},{9,8},{10,11... | collective-permute-start | bytes 344072 | tf_op jit(solution)/shard_map/ppermute | solution.py:410
  44.1 5.2 %collective-permute-start.14 = (bf16[16,3584]{1,0:T(8,128)(2,1)S(1)}, bf16[16,3584]{1,0:T(8,128)(2,1)S(1)}, u32[]{:S(2)}, u32[]{:S(2)}) collective-permute-start(bf16[16,3584]{1,0:T(8,128)(2,1)S(1)} %get-tuple-element.43), channel_id=1, source_target_pairs={{0,8},{1,9},{2,10},{3,11},{4,12},{5,13},{6,14},{7,15},{8,0},{9,1},... | collective-permute-start | bytes 344072 | tf_op jit(solution)/shard_map/ppermute | solution.py:410
  47.6 5.8 %collective-permute-start.11 = (bf16[8,3584]{1,0:T(8,128)(2,1)S(1)}, bf16[8,3584]{1,0:T(8,128)(2,1)S(1)}, u32[]{:S(2)}, u32[]{:S(2)}) collective-permute-start(bf16[8,3584]{1,0:T(8,128)(2,1)S(1)} %fusion.5), channel_id=1, source_target_pairs={{0,2},{1,3},{2,0},{3,1},{4,6},{5,7},{6,4},{7,5},{8,10},{9,11},{10,... | collective-permute-start | bytes 172040 | tf_op jit(solution)/shard_map/ppermute | solution.py:410
  49.3 5.8 %collective-permute-start.15 = (bf16[8,3584]{1,0:T(8,128)(2,1)S(1)}, bf16[8,3584]{1,0:T(8,128)(2,1)S(1)}, u32[]{:S(2)}, u32[]{:S(2)}) collective-permute-start(bf16[8,3584]{1,0:T(8,128)(2,1)S(1)} %fusion.2), channel_id=1, source_target_pairs={{0,2},{1,3},{2,0},{3,1},{4,6},{5,7},{6,4},{7,5},{8,10},{9,11},{10,... | collective-permute-start | bytes 172040 | tf_op jit(solution)/shard_map/ppermute | solution.py:410

commit v14 on v13

--- a/solution.py
+++ b/solution.py
@@ -53,18 +53,17 @@
     )(tokens, group_ids.T, route_weights.T)
 
 
-def load_gate_kernel(share, place_ref, gate_ref, sgate_ref, sup_ref, out_ref, sems):
-    width, hidden = gate_ref.shape
+def load_kernel(share, place_ref, routed_ref, shared_ref, out_ref, sems):
+    width, hidden = routed_ref.shape
     column = pl.multiple_of((place_ref[0] // share) * LANES, LANES)
-    parts = 4
+    parts = sems.shape[0] // 2
     piece = width // parts
     copies = []
     for i in range(parts):
         at = pl.ds(i * piece, piece)
         for source, lower, size in (
-            (gate_ref.at[at, :], 0, hidden),
-            (sgate_ref.at[at, pl.ds(column, LANES)], hidden, LANES),
-            (sup_ref.at[at, pl.ds(column, LANES)], hidden + LANES, LANES),
+            (routed_ref.at[at, :], 0, hidden),
+            (shared_ref.at[at, pl.ds(column, LANES)], hidden, LANES),
         ):
             copies.append(
                 pltpu.make_async_copy(source, out_ref.at[at, pl.ds(lower, size)], sems.at[len(copies)])
@@ -72,47 +71,19 @@
     run_copies(copies)
 
 
-def load_gate(place, gate, sgate, sup, share):
-    width, hidden = gate.shape
-    shape = (width, hidden + 2 * LANES)
+def load_weights(place, routed, shared, share):
+    width, hidden = routed.shape
+    shape = (width, hidden + LANES)
     return pl.pallas_call(
-        functools.partial(load_gate_kernel, share),
-        in_specs=[SMEM_SPEC] + [ANY_SPEC] * 3,
+        functools.partial(load_kernel, share),
+        in_specs=[SMEM_SPEC] + [ANY_SPEC] * 2,
         out_specs=VMEM_SPEC,
         out_shape=pltpu.VMEM(shape, BF16),
-        scratch_shapes=[pltpu.SemaphoreType.DMA((12,))],
+        scratch_shapes=[pltpu.SemaphoreType.DMA((8,))],
         cost_estimate=pl.CostEstimate(flops=0, bytes_accessed=4 * shape[0] * shape[1], transcendentals=0),
         compiler_params=pltpu.CompilerParams(vmem_limit_bytes=1 << 20),
-        name="load_gate",
-    )(place, in_hbm(gate), in_hbm(sgate), in_hbm(sup))
-
-
-def load_up_kernel(up_ref, out_ref, sems):
-    width = up_ref.shape[0]
-    parts = 8
-    piece = width // parts
-    run_copies(
-        [
-            pltpu.make_async_copy(
-                up_ref.at[pl.ds(i * piece, piece), :], out_ref.at[pl.ds(i * piece, piece), :], sems.at[i]
-            )
-            for i in range(parts)
-        ]
-    )
-
-
-def load_up(up):
-    width, hidden = up.shape
-    return pl.pallas_call(
-        load_up_kernel,
-        in_specs=[ANY_SPEC],
-        out_specs=VMEM_SPEC,
-        out_shape=pltpu.VMEM((width, hidden), BF16),
-        scratch_shapes=[pltpu.SemaphoreType.DMA((8,))],
-        cost_estimate=pl.CostEstimate(flops=0, bytes_accessed=4 * width * hidden, transcendentals=0),
-        compiler_params=pltpu.CompilerParams(vmem_limit_bytes=1 << 20),
-        name="load_up",
-    )(in_hbm(up))
+        name="load_weights",
+    )(place, in_hbm(routed), in_hbm(shared))
 
 
 def silu(v):
@@ -165,26 +136,30 @@
         copy.wait()
 
 
-def shared_units(share, node, both):
-    shared = silu(both[:, :LANES]) * both[:, LANES:]
+def shared_units(share, node, gate, up):
+    shared = silu(gate) * up
     if share > 1:
         lane = lax.broadcasted_iota(jnp.int32, shared.shape, 1)
         shared = jnp.where(lane // (LANES // share) == node % share, shared, 0.0)
     return shared.astype(BF16)
 
 
-def ffn(share, place_ref, x, first_ref, up_ref, act, second, take, store):
-    width, hidden = up_ref.shape
+def tiles_of(units):
+    tile = 2 * LANES
+    return [slice(at, min(at + tile, units)) for at in range(0, units, tile)]
+
+
+def ffn(share, place_ref, x, gate_ref, up_ref, act, second, take, store):
+    width, units = gate_ref.shape
+    hidden = units - LANES
     node = place_ref[0]
     rows = x[:, :width]
     weight = row_weight(node, x[:, width:])
-    tile, piece = min(2 * LANES, hidden), width // DOWN_PARTS
-    for at in range(0, hidden, tile):
-        gate = jnp.dot(rows, first_ref[:, at : at + tile], preferred_element_type=F32)
-        up = jnp.dot(rows, up_ref[:, at : at + tile], preferred_element_type=F32)
-        act[:, at : at + tile] = (silu(gate) * up * weight).astype(BF16)
-    both = jnp.dot(rows, first_ref[:, hidden:], preferred_element_type=F32)
-    act[:, hidden:] = shared_units(share, node, both)
+    gate = jnp.dot(rows, gate_ref[...], preferred_element_type=F32)
+    up = jnp.dot(rows, up_ref[...], preferred_element_type=F32)
+    act[:, :hidden] = (silu(gate[:, :hidden]) * up[:, :hidden] * weight).astype(BF16)
+    act[:, hidden:] = shared_units(share, node, gate[:, hidden:], up[:, hidden:])
+    piece = width // DOWN_PARTS
     for i in range(DOWN_PARTS):
         at = slice(i * piece, (i + 1) * piece)
         take(i)
@@ -249,62 +224,49 @@
     )(place, in_hbm(down), in_hbm(sdown))
 
 
-def late_half_kernel(
-    share, place_ref, own_ref, other_ref, first_ref, up_ref, down_ref, sdown_ref, acc_ref, later_ref, x, sems
-):
-    width, hidden = up_ref.shape
+def late_half_kernel(place_ref, own_ref, other_ref, gate_ref, up_ref, gate_acc_ref, up_acc_ref, weight_ref, x):
+    width, units = gate_ref.shape
     half, columns = own_ref.shape
     cut = width + LANES - columns
+    x[:half, :] = own_ref[...]
+    x[half:, :] = other_ref[...]
+    rows = x[:, : width - cut]
+    for at in tiles_of(units):
+        gate_acc_ref[:, at] = jnp.dot(rows, gate_ref[cut:, at], preferred_element_type=F32)
+        up_acc_ref[:, at] = jnp.dot(rows, up_ref[cut:, at], preferred_element_type=F32)
+    weight = row_weight(place_ref[0], x[:, width - cut :])
+    weight_ref[...] = jnp.broadcast_to(weight, weight_ref.shape)
+
+
+def early_half_kernel(
+    share, place_ref, own_ref, other_ref, gate_ref, up_ref, gate_acc_ref, up_acc_ref, weight_ref, second_ref,
+    down_ref, sdown_ref, own_out_ref, other_out_ref, act_ref, later_ref, x, sems,
+):
+    half, cut = own_ref.shape
     copies = half_down_copies(share, place_ref, down_ref, sdown_ref, later_ref, cut, sems)
     for copy in copies:
         copy.start()
-    x[:half, :] = own_ref[...]
-    x[half:, :] = other_ref[...]
-    rows = x[:, : width - cut]
-    tile = min(2 * LANES, hidden)
-    for at in range(0, hidden, tile):
-        acc_ref[:, at : at + tile] = jnp.dot(rows, first_ref[cut:, at : at + tile], preferred_element_type=F32)
-        acc_ref[:, hidden + at : hidden + at + tile] = jnp.dot(
-            rows, up_ref[cut:, at : at + tile], preferred_element_type=F32
-        )
-    acc_ref[:, 2 * hidden : 2 * hidden + 2 * LANES] = jnp.dot(
-        rows, first_ref[cut:, hidden:], preferred_element_type=F32
-    )
-    weight = row_weight(place_ref[0], x[:, width - cut :])
-    acc_ref[:, 2 * hidden + 2 * LANES :] = jnp.broadcast_to(weight, (2 * half, LANES))
-    for copy in copies:
-        copy.wait()
-
-
-def early_half_kernel(
-    share, place_ref, own_ref, other_ref, first_ref, up_ref, acc_ref, second_ref,
-    own_out_ref, other_out_ref, act_ref, x,
-):
-    half, cut = own_ref.shape
-    hidden = up_ref.shape[1]
+    units = gate_ref.shape[1]
+    hidden = units - LANES
     x[:half, :] = own_ref[...]
     x[half:, :] = other_ref[...]
     rows = x[...]
-    tile = min(2 * LANES, hidden)
-    weight = acc_ref[:, 2 * hidden + 2 * LANES :][:, :1]
-    for at in range(0, hidden, tile):
-        gate = acc_ref[:, at : at + tile] + jnp.dot(
-            rows, first_ref[:cut, at : at + tile], preferred_element_type=F32
-        )
-        up = acc_ref[:, hidden + at : hidden + at + tile] + jnp.dot(
-            rows, up_ref[:cut, at : at + tile], preferred_element_type=F32
-        )
-        act_ref[:, at : at + tile] = (silu(gate) * up * weight).astype(BF16)
-    both = acc_ref[:, 2 * hidden : 2 * hidden + 2 * LANES] + jnp.dot(
-        rows, first_ref[:cut, hidden:], preferred_element_type=F32
-    )
-    act_ref[:, hidden:] = shared_units(share, place_ref[0], both)
+    weight = weight_ref[:, :1]
+    for at in tiles_of(units):
+        gate = gate_acc_ref[:, at] + jnp.dot(rows, gate_ref[:cut, at], preferred_element_type=F32)
+        up = up_acc_ref[:, at] + jnp.dot(rows, up_ref[:cut, at], preferred_element_type=F32)
+        if at.start < hidden:
+            act_ref[:, at] = (silu(gate) * up * weight).astype(BF16)
+        else:
+            act_ref[:, at] = shared_units(share, place_ref[0], gate, up)
     piece = cut // 2
     for i in range(2):
         at = slice(i * piece, (i + 1) * piece)
         total = jnp.dot(act_ref[...], second_ref[:, at], preferred_element_type=F32).astype(BF16)
         own_out_ref[:, at] = total[:half]
         other_out_ref[:, at] = total[half:]
+    for copy in copies:
+        copy.wait()
 
 
 def last_half_kernel(act_ref, second_ref, own_out_ref, other_out_ref):
@@ -323,34 +285,35 @@
     )
 
 
-def pair_rows(place, own, other, first, up, second, down, sdown, share):
+def pair_rows(place, own, other, gate, up, second, down, sdown, share):
     half, cut = own[0].shape
     hidden, width = down.shape
     units = hidden + LANES
-    acc, later = pl.pallas_call(
-        functools.partial(late_half_kernel, share),
-        in_specs=[SMEM_SPEC] + [VMEM_SPEC] * 4 + [ANY_SPEC] * 2,
-        out_specs=[VMEM_SPEC] * 2,
-        out_shape=[pltpu.VMEM((2 * half, 2 * units + LANES), F32), pltpu.VMEM((units, width - cut), BF16)],
-        scratch_shapes=[pltpu.VMEM((2 * half, own[1].shape[1]), BF16), pltpu.SemaphoreType.DMA((4,))],
+    partial = pl.pallas_call(
+        late_half_kernel,
+        in_specs=[SMEM_SPEC] + [VMEM_SPEC] * 4,
+        out_specs=[VMEM_SPEC] * 3,
+        out_shape=[pltpu.VMEM((2 * half, columns), F32) for columns in (units, units, LANES)],
+        scratch_shapes=[pltpu.VMEM((2 * half, own[1].shape[1]), BF16)],
         cost_estimate=estimate(2 * half, width - cut, 2 * units),
         compiler_params=pltpu.CompilerParams(vmem_limit_bytes=10 << 20),
         name="late_half",
-    )(place, own[1], other[1], first, up, in_hbm(down), in_hbm(sdown))
-    own_out, other_out, act = pl.pallas_call(
+    )(place, own[1], other[1], gate, up)
+    own_out, other_out, act, later = pl.pallas_call(
         functools.partial(early_half_kernel, share),
-        in_specs=[SMEM_SPEC] + [VMEM_SPEC] * 6,
-        out_specs=[VMEM_SPEC] * 3,
+        in_specs=[SMEM_SPEC] + [VMEM_SPEC] * 8 + [ANY_SPEC] * 2,
+        out_specs=[VMEM_SPEC] * 4,
         out_shape=[
             pltpu.VMEM((half, cut), BF16),
             pltpu.VMEM((half, cut), BF16),
             pltpu.VMEM((2 * half, units), BF16),
+            pltpu.VMEM((units, width - cut), BF16),
         ],
-        scratch_shapes=[pltpu.VMEM((2 * half, cut), BF16)],
+        scratch_shapes=[pltpu.VMEM((2 * half, cut), BF16), pltpu.SemaphoreType.DMA((4,))],
         cost_estimate=estimate(2 * half, cut, 3 * units),
         compiler_params=pltpu.CompilerParams(vmem_limit_bytes=10 << 20),
         name="early_half",
-    )(place, own[0], other[0], first, up, acc, second)
+    )(place, own[0], other[0], gate, up, *partial, second, in_hbm(down), in_hbm(sdown))
     last = pl.pallas_call(
         last_half_kernel,
         in_specs=[VMEM_SPEC] * 2,
@@ -364,7 +327,7 @@
 
 
 def block_kernel(
-    share, place_ref, x_ref, first_ref, up_ref, down_ref, sdown_ref, out_ref, act, second, sems
+    share, place_ref, x_ref, gate_ref, up_ref, down_ref, sdown_ref, out_ref, act, second, sems
 ):
     groups = down_copies(share, place_ref, down_ref, sdown_ref, second, sems)
 
@@ -378,10 +341,10 @@
     def store(at, total):
         out_ref[:, at] = total.astype(BF16)
 
-    ffn(share, place_ref, x_ref, first_ref, up_ref, act, second, lambda i: None, store)
-
-
-def block_rows(place, x, first, up, down, sdown, share):
+    ffn(share, place_ref, x_ref, gate_ref, up_ref, act, second, lambda i: None, store)
+
+
+def block_rows(place, x, gate, up, down, sdown, share):
     rows, packed = x.shape
     hidden, width = down.shape
     block = min(rows, ROW_BLOCK)
@@ -394,7 +357,7 @@
         scratch_shapes=down_scratch(block, hidden, width),
         compiler_params=pltpu.CompilerParams(vmem_limit_bytes=24 << 20),
         name="block_rows",
-    )(place, x, first, up, in_hbm(down), in_hbm(sdown))
+    )(place, x, gate, up, in_hbm(down), in_hbm(sdown))
 
 
 def f32_sum(*terms):
@@ -440,29 +403,30 @@
 
     if node_count != 4 or local_count != 4:
         x = lax.all_gather(packed, ("node", "local"), axis=0, tiled=True)
-        first = load_gate(place, gate, gate_shared, up_shared, share)
-        part = block_rows(place, x, first, load_up(up), down, down_shared, share)
+        gate = load_weights(place, gate, gate_shared, share)
+        up = load_weights(place, up, up_shared, share)
+        part = block_rows(place, x, gate, up, down, down_shared, share)
         return lax.psum_scatter(part, ("node", "local"), scatter_dimension=0, tiled=True)
 
     cut = width // 2
     own = [packed[:, :cut], packed[:, cut:]]
     loads = (
         lambda *ready: load_down(after(place, *ready), down, down_shared, cut, share),
-        lambda *ready: load_gate(after(place, *ready), gate, gate_shared, up_shared, share),
-        lambda *ready: load_up(after(up, *ready)),
+        lambda *ready: load_weights(after(place, *ready), gate, gate_shared, share),
+        lambda *ready: load_weights(after(place, *ready), up, up_shared, share),
     )
     loaded = []
     for phase, load in zip(GATHER, loads):
-        got = [flipped(part, *pairs) for part, pairs in zip(own, (phase, phase[::-1]))]
-        got[0], weights = lax.optimization_barrier((got[0], load(*own)))
+        got = [flipped(part, *pairs) for part, pairs in zip(own, (phase[::-1], phase))]
+        got[1], weights = lax.optimization_barrier((got[1], load(*own)))
         loaded.append(weights)
         own = [stack(part, add) for part, add in zip(own, got)]
-    second, first, up = loaded
+    second, gate, up = loaded
     odd = place[0] % 2
-    own = [jnp.where(odd == i, part, regroup(part, 4, 2)) for i, part in enumerate(own)]
+    own = [jnp.where(odd == 1 - i, part, regroup(part, 4, 2)) for i, part in enumerate(own)]
     other = [flipped(part, CORE, CORE) for part in own]
 
-    outs = pair_rows(place, own, other, first, up, second, down, down_shared, share)
+    outs = pair_rows(place, own, other, gate, up, second, down, down_shared, share)
 
     totals = [[own, flipped(other, CORE, CORE)] for own, other in zip(outs[:2], outs[2:])]
     for phase in SCATTER:

time: 55.9 us -> 56.7 us (1.014)
  waiting for transfers between devices: 18.2 us -> 23.6 us
  starting transfers between devices: 18.4 us -> 13.8 us
    ppermute x16, waiting for transfers between devices: 18.2 us -> 23.6 us  [flipped(): return lax.ppermute(value, ('node', 'local'), pairs)]
    ppermute x16, starting transfers between devices: 18.4 us -> 13.8 us  [flipped(): return lax.ppermute(value, ('node', 'local'), pairs)]
    pallas_call x1, Pallas kernels: 2.64 us -> 4.17 us  [pair_rows(): pl.pallas_call(functools.partial(early_half_kernel, share), in_specs=[SME...]
    pallas_call x3, Pallas kernels: 10.5 us -> 9.06 us  [the longest x2 7.38 us: load_weights(): pl.pallas_call(functools.partial(load_kernel, share), in_specs=[SMEM_SPEC...]
  transfers between devices with their start and end apart: 16 -> 16, of which waited for: 9 -> 11; matrix products, arithmetic and copies ran while one was open for 1% -> 1% of each run, Pallas kernels for 25% -> 22%
where the time goes in v14:
time: 56.7 us; the launch traced here: 56.5 us
  waiting for transfers between devices  23.6 us (42%)
  Pallas kernels  17.5 us (31%)
  starting transfers between devices  13.8 us (24%)
  other arithmetic  1.31 us (2%)
    ppermute x16, waiting for transfers between devices, flipped(): return lax.ppermute(value, ('node', 'local'), pairs)  23.6 us
    ppermute x16, starting transfers between devices, flipped(): return lax.ppermute(value, ('node', 'local'), pairs)  13.8 us
    pallas_call x2, Pallas kernels, load_weights(): pl.pallas_call(functools.partial(load_kernel, share), in_specs=[SMEM_SPEC...  7.38 us
    pallas_call x1, Pallas kernels, pair_rows(): pl.pallas_call(functools.partial(early_half_kernel, share), in_specs=[SME...  4.17 us
    pallas_call x1, Pallas kernels, load_down(): pl.pallas_call(functools.partial(load_down_kernel, share), in_specs=[SMEM...  2.3 us
    pallas_call x1, Pallas kernels, pair_rows(): pl.pallas_call(late_half_kernel, in_specs=[SMEM_SPEC] + [VMEM_SPEC] * 4,...  1.68 us
  transfers between devices with their start and end apart: 16, of which 11 were waited for; matrix products, arithmetic and copies ran while one was open for 1% of the time, Pallas kernels for 22%

profile of v14, /device:TPU:0, one launch (start us, length us, event | category | flops | bytes accessed | tf_op | source)
XLA Modules:
  0.0 56.5 jit_solution(7543313138785629200)
XLA Ops:
  0.0 1.1 %pack_rows.1 = bf16[8,7296]{1,0:T(8,128)(2,1)S(1)} custom-call(bf16[8,7168]{1,0:T(8,128)(2,1)} %tokens_ref.1, s32[4,8]{1,0:T(4,128)} %bitcast.10, bf16[4,8]{1,0:T(4,128)(2,1)} %bitcast.11), custom_call_target="tpu_custom_call" | custom-call | tf_op jit(solution)/shard_map/pack_rows/pallas_call | solution.py:48
  1.1 3.0 %collective-permute-start = (bf16[8,3584]{1,0:T(8,128)(2,1)S(1)}, bf16[8,3584]{1,0:T(8,128)(2,1)S(1)}, u32[]{:S(2)}, u32[]{:S(2)}) collective-permute-start(bf16[8,3584]{1,0:T(8,128)(2,1)S(1)} %get-tuple-element.51), channel_id=1, source_target_pairs={{0,8},{1,9},{2,10},{3,11},{4,6},{5,7},{6,4},{7,5},{8,0},{9,1},{10,... | collective-permute-start | bytes 172040 | tf_op jit(solution)/shard_map/ppermute | solution.py:373
  4.1 2.7 %collective-permute-start.4 = (bf16[8,3712]{1,0:T(8,128)(2,1)S(1)}, bf16[8,3712]{1,0:T(8,128)(2,1)S(1)}, u32[]{:S(2)}, u32[]{:S(2)}) collective-permute-start(bf16[8,3712]{1,0:T(8,128)(2,1)S(1)} %get-tuple-element.50), channel_id=1, source_target_pairs={{0,2},{1,3},{2,0},{3,1},{4,12},{5,13},{6,14},{7,15},{8,10},{9,11},... | collective-permute-start | bytes 178184 | tf_op jit(solution)/shard_map/ppermute | solution.py:373
  6.8 2.3 %load_down.1.second_ref = bf16[640,3584]{1,0:T(8,128)(2,1)S(1)} custom-call(s32[1]{0:T(128)} %bitcast.place_ref, bf16[512,7168]{1,0:T(8,128)(2,1)} %bitcast.6, bf16[512,7168]{1,0:T(8,128)(2,1)} %sdown_ref.3), custom_call_target="tpu_custom_call" | custom-call | bytes 9175040 | tf_op jit(solution)/shard_map/load_down/pallas_call | solution.py:215
  9.1 0.0 collective-permute-done
  9.1 0.4 collective-permute-start.1
  9.5 0.0 collective-permute-done.4
  9.5 1.6 %collective-permute-start.5 = (bf16[16,3712]{1,0:T(8,128)(2,1)S(1)}, bf16[16,3712]{1,0:T(8,128)(2,1)S(1)}, u32[]{:S(2)}, u32[]{:S(2)}) collective-permute-start(bf16[16,3712]{1,0:T(8,128)(2,1)S(1)} %pad_maximum_fusion.2), channel_id=1, source_target_pairs={{0,1},{1,0},{2,3},{3,2},{4,6},{5,7},{6,4},{7,5},{8,9},{9,8},{10,11... | collective-permute-start | bytes 356360 | tf_op jit(solution)/shard_map/ppermute | solution.py:373
  11.2 3.7 %load_weights.2.gate_ref = bf16[7168,640]{1,0:T(8,128)(2,1)S(1)} custom-call(s32[1]{0:T(128)} %bitcast.place_ref, bf16[7168,512]{1,0:T(8,128)(2,1)} %bitcast.8, bf16[7168,512]{1,0:T(8,128)(2,1)} %shared_ref.2), custom_call_target="tpu_custom_call" | custom-call | bytes 18350080 | tf_op jit(solution)/shard_map/load_weights/pallas_call | solution.py:77
  14.9 3.3 %collective-permute-done.1 = bf16[16,3584]{1,0:T(8,128)(2,1)S(1)} collective-permute-done((bf16[16,3584]{1,0:T(8,128)(2,1)S(1)}, bf16[16,3584]{1,0:T(8,128)(2,1)S(1)}, u32[]{:S(2)}, u32[]{:S(2)}) %collective-permute-start.1) | collective-permute-done | bytes 114720 | tf_op jit(solution)/shard_map/ppermute | solution.py:373
  18.2 0.1 collective-permute-start.2
  18.3 0.0 collective-permute-done.5
  18.3 0.7 %collective-permute-start.6 = (bf16[32,3712]{1,0:T(8,128)(2,1)S(1)}, bf16[32,3712]{1,0:T(8,128)(2,1)S(1)}, u32[]{:S(2)}, u32[]{:S(2)}) collective-permute-start(bf16[32,3712]{1,0:T(8,128)(2,1)S(1)} %pad_maximum_fusion), channel_id=1, source_target_pairs={{0,8},{1,9},{2,10},{3,11},{4,5},{5,4},{6,7},{7,6},{8,0},{9,1},{10,... | collective-permute-start | bytes 712712 | tf_op jit(solution)/shard_map/ppermute | solution.py:373
  19.1 3.7 %load_weights.3.up_ref = bf16[7168,640]{1,0:T(8,128)(2,1)S(1)} custom-call(s32[1]{0:T(128)} %bitcast.place_ref, bf16[7168,512]{1,0:T(8,128)(2,1)} %bitcast.9, bf16[7168,512]{1,0:T(8,128)(2,1)} %shared_ref.3), custom_call_target="tpu_custom_call" | custom-call | bytes 18350080 | tf_op jit(solution)/shard_map/load_weights/pallas_call | solution.py:77
  22.8 3.2 %collective-permute-done.2 = bf16[32,3584]{1,0:T(8,128)(2,1)S(1)} collective-permute-done((bf16[32,3584]{1,0:T(8,128)(2,1)S(1)}, bf16[32,3584]{1,0:T(8,128)(2,1)S(1)}, u32[]{:S(2)}, u32[]{:S(2)}) %collective-permute-start.2) | collective-permute-done | bytes 229408 | tf_op jit(solution)/shard_map/ppermute | solution.py:373
  26.1 0.0 collective-permute-done.6
  26.2 0.1 maximum_select_fusion.own_ref
  26.3 0.1 collective-permute-start.7
  26.4 0.1 maximum_select_fusion.1.own_ref
  26.5 0.6 collective-permute-start.3
  27.0 1.2 %collective-permute-done.7.other_ref = bf16[64,3712]{1,0:T(8,128)(2,1)S(1)} collective-permute-done((bf16[64,3712]{1,0:T(8,128)(2,1)S(1)}, bf16[64,3712]{1,0:T(8,128)(2,1)S(1)}, u32[]{:S(2)}, u32[]{:S(2)}) %collective-permute-start.7) | collective-permute-done | bytes 475168 | tf_op jit(solution)/shard_map/ppermute | solution.py:373
  28.2 1.7 %late_half.1 = (f32[128,640]{1,0:T(8,128)S(1)}, f32[128,640]{1,0:T(8,128)S(1)}, f32[128,128]{1,0:T(8,128)S(1)}) custom-call(s32[1]{0:T(128)} %bitcast.place_ref, bf16[64,3712]{1,0:T(8,128)(2,1)S(1)} %maximum_select_fusion.own_ref, bf16[64,3712]{1,0:T(8,128)(2,1)S(1)} %collective-permute-done.7.other_ref, bf16[7168,640]{1,0:T(8,128)(2,1)S(1)} %load_weights.2.gate_ref, ...), custom_call_target="tpu_custom_call" | custom-call | flops 1174405120 | bytes 9175040 | tf_op jit(solution)/shard_map/late_half/pallas_call | solution.py:292
  29.9 0.0 collective-permute-done.3.other_ref
  29.9 4.2 %early_half.1 = (bf16[64,3584]{1,0:T(8,128)(2,1)S(1)}, bf16[64,3584]{1,0:T(8,128)(2,1)S(1)}, bf16[128,640]{1,0:T(8,128)(2,1)S(1)}, bf16[640,3584]{1,0:T(8,128)(2,1)S(1)}) custom-call(s32[1]{0:T(128)} %bitcast.place_ref, bf16[64,3584]{1,0:T(8,128)(2,1)S(1)} %maximum_select_fusion.1.own_ref, bf16[64,3584]{1,0:T(8,128)(2,1)S(1)} %collective-permute-done.3.other_ref, ...), custom_call_target="tpu_custom_call" | custom-call | flops 1761607680 | bytes 13762560 | tf_op jit(solution)/shard_map/early_half/pallas_call | solution.py:302
  34.1 0.2 collective-permute-start.8
  34.3 0.9 %last_half.1 = (bf16[64,3584]{1,0:T(8,128)(2,1)S(1)}, bf16[64,3584]{1,0:T(8,128)(2,1)S(1)}) custom-call(bf16[128,640]{1,0:T(8,128)(2,1)S(1)} %get-tuple-element.37.act_ref, bf16[640,3584]{1,0:T(8,128)(2,1)S(1)} %get-tuple-element.38.second_ref), custom_call_target="tpu_custom_call" | custom-call | flops 587202560 | bytes 4587520 | tf_op jit(solution)/shard_map/last_half/pallas_call | solution.py:317
  35.2 0.4 collective-permute-start.12
  35.6 0.4 collective-permute-done.8
  36.0 0.1 add_convert_fusion.1
  36.1 0.5 collective-permute-start.9
  36.5 0.5 collective-permute-done.12
  37.0 0.1 add_convert_fusion
  37.1 0.5 collective-permute-start.13
  37.7 6.1 %collective-permute-done.9 = bf16[32,3584]{1,0:T(8,128)(2,1)S(1)} collective-permute-done((bf16[32,3584]{1,0:T(8,128)(2,1)S(1)}, bf16[32,3584]{1,0:T(8,128)(2,1)S(1)}, u32[]{:S(2)}, u32[]{:S(2)}) %collective-permute-start.9) | collective-permute-done | bytes 229408 | tf_op jit(solution)/shard_map/ppermute | solution.py:373
  43.8 0.5 collective-permute-start.10
  44.3 0.8 %collective-permute-done.13 = bf16[32,3584]{1,0:T(8,128)(2,1)S(1)} collective-permute-done((bf16[32,3584]{1,0:T(8,128)(2,1)S(1)}, bf16[32,3584]{1,0:T(8,128)(2,1)S(1)}, u32[]{:S(2)}, u32[]{:S(2)}) %collective-permute-start.13) | collective-permute-done | bytes 229408 | tf_op jit(solution)/shard_map/ppermute | solution.py:373
  45.1 0.1 fusion
  45.1 0.7 %collective-permute-start.14 = (bf16[16,3584]{1,0:T(8,128)(2,1)S(1)}, bf16[16,3584]{1,0:T(8,128)(2,1)S(1)}, u32[]{:S(2)}, u32[]{:S(2)}) collective-permute-start(bf16[16,3584]{1,0:T(8,128)(2,1)S(1)} %get-tuple-element.47), channel_id=1, source_target_pairs={{0,8},{1,9},{2,10},{3,11},{4,12},{5,13},{6,14},{7,15},{8,0},{9,1},... | collective-permute-start | bytes 344072 | tf_op jit(solution)/shard_map/ppermute | solution.py:373
  45.8 2.9 %collective-permute-done.10 = bf16[16,3584]{1,0:T(8,128)(2,1)S(1)} collective-permute-done((bf16[16,3584]{1,0:T(8,128)(2,1)S(1)}, bf16[16,3584]{1,0:T(8,128)(2,1)S(1)}, u32[]{:S(2)}, u32[]{:S(2)}) %collective-permute-start.10) | collective-permute-done | bytes 114720 | tf_op jit(solution)/shard_map/ppermute | solution.py:373
  48.7 0.1 collective-permute-start.11
  48.8 1.2 %collective-permute-done.14 = bf16[16,3584]{1,0:T(8,128)(2,1)S(1)} collective-permute-done((bf16[16,3584]{1,0:T(8,128)(2,1)S(1)}, bf16[16,3584]{1,0:T(8,128)(2,1)S(1)}, u32[]{:S(2)}, u32[]{:S(2)}) %collective-permute-start.14) | collective-permute-done | bytes 114720 | tf_op jit(solution)/shard_map/ppermute | solution.py:373
  50.0 1.7 %collective-permute-start.15 = (bf16[8,3584]{1,0:T(8,128)(2,1)S(1)}, bf16[8,3584]{1,0:T(8,128)(2,1)S(1)}, u32[]{:S(2)}, u32[]{:S(2)}) collective-permute-start(bf16[8,3584]{1,0:T(8,128)(2,1)S(1)} %fusion.2), channel_id=1, source_target_pairs={{0,2},{1,3},{2,0},{3,1},{4,6},{5,7},{6,4},{7,5},{8,10},{9,11},{10,... | collective-permute-start | bytes 172040 | tf_op jit(solution)/shard_map/ppermute | solution.py:373
  51.8 2.8 %collective-permute-done.11 = bf16[8,3584]{1,0:T(8,128)(2,1)S(1)} collective-permute-done((bf16[8,3584]{1,0:T(8,128)(2,1)S(1)}, bf16[8,3584]{1,0:T(8,128)(2,1)S(1)}, u32[]{:S(2)}, u32[]{:S(2)}) %collective-permute-start.11) | collective-permute-done | bytes 57376 | tf_op jit(solution)/shard_map/ppermute | solution.py:373
  54.6 1.2 %collective-permute-done.15 = bf16[8,3584]{1,0:T(8,128)(2,1)S(1)} collective-permute-done((bf16[8,3584]{1,0:T(8,128)(2,1)S(1)}, bf16[8,3584]{1,0:T(8,128)(2,1)S(1)}, u32[]{:S(2)}, u32[]{:S(2)}) %collective-permute-start.15) | collective-permute-done | bytes 57376 | tf_op jit(solution)/shard_map/ppermute | solution.py:373
  55.9 0.7 %pad_maximum_fusion.4 = bf16[8,7168]{1,0:T(8,128)(2,1)} fusion(bf16[8,3584]{1,0:T(8,128)(2,1)S(1)} %fusion.4, bf16[8,3584]{1,0:T(8,128)(2,1)S(1)} %fusion.7), kind=kLoop, calls=%fused_computation.26 | loop fusion | flops 229376 | bytes 229376 | tf_op jit(solution)/shard_map/concatenate | solution.py:438
  (25 shorter events, 0.3 us)
Async XLA Ops:
  1.1 8.0 %collective-permute-start = (bf16[8,3584]{1,0:T(8,128)(2,1)S(1)}, bf16[8,3584]{1,0:T(8,128)(2,1)S(1)}, u32[]{:S(2)}, u32[]{:S(2)}) collective-permute-start(bf16[8,3584]{1,0:T(8,128)(2,1)S(1)} %get-tuple-element.51), channel_id=1, source_target_pairs={{0,8},{1,9},{2,10},{3,11},{4,6},{5,7},{6,4},{7,5},{8,0},{9,1},{10,... | collective-permute-start | bytes 172040 | tf_op jit(solution)/shard_map/ppermute | solution.py:373
  4.1 5.4 %collective-permute-start.4 = (bf16[8,3712]{1,0:T(8,128)(2,1)S(1)}, bf16[8,3712]{1,0:T(8,128)(2,1)S(1)}, u32[]{:S(2)}, u32[]{:S(2)}) collective-permute-start(bf16[8,3712]{1,0:T(8,128)(2,1)S(1)} %get-tuple-element.50), channel_id=1, source_target_pairs={{0,2},{1,3},{2,0},{3,1},{4,12},{5,13},{6,14},{7,15},{8,10},{9,11},... | collective-permute-start | bytes 178184 | tf_op jit(solution)/shard_map/ppermute | solution.py:373
  9.1 9.1 %collective-permute-start.1 = (bf16[16,3584]{1,0:T(8,128)(2,1)S(1)}, bf16[16,3584]{1,0:T(8,128)(2,1)S(1)}, u32[]{:S(2)}, u32[]{:S(2)}) collective-permute-start(bf16[16,3584]{1,0:T(8,128)(2,1)S(1)} %pad_maximum_fusion.3), channel_id=1, source_target_pairs={{0,2},{1,3},{2,0},{3,1},{4,5},{5,4},{6,7},{7,6},{8,10},{9,11},{10,... | collective-permute-start | bytes 344072 | tf_op jit(solution)/shard_map/ppermute | solution.py:373
  9.5 8.8 %collective-permute-start.5 = (bf16[16,3712]{1,0:T(8,128)(2,1)S(1)}, bf16[16,3712]{1,0:T(8,128)(2,1)S(1)}, u32[]{:S(2)}, u32[]{:S(2)}) collective-permute-start(bf16[16,3712]{1,0:T(8,128)(2,1)S(1)} %pad_maximum_fusion.2), channel_id=1, source_target_pairs={{0,1},{1,0},{2,3},{3,2},{4,6},{5,7},{6,4},{7,5},{8,9},{9,8},{10,11... | collective-permute-start | bytes 356360 | tf_op jit(solution)/shard_map/ppermute | solution.py:373
  18.2 7.8 %collective-permute-start.2 = (bf16[32,3584]{1,0:T(8,128)(2,1)S(1)}, bf16[32,3584]{1,0:T(8,128)(2,1)S(1)}, u32[]{:S(2)}, u32[]{:S(2)}) collective-permute-start(bf16[32,3584]{1,0:T(8,128)(2,1)S(1)} %pad_maximum_fusion.1), channel_id=1, source_target_pairs={{0,1},{1,0},{2,3},{3,2},{4,12},{5,13},{6,14},{7,15},{8,9},{9,8},{1... | collective-permute-start | bytes 688136 | tf_op jit(solution)/shard_map/ppermute | solution.py:373
  18.3 7.7 %collective-permute-start.6 = (bf16[32,3712]{1,0:T(8,128)(2,1)S(1)}, bf16[32,3712]{1,0:T(8,128)(2,1)S(1)}, u32[]{:S(2)}, u32[]{:S(2)}) collective-permute-start(bf16[32,3712]{1,0:T(8,128)(2,1)S(1)} %pad_maximum_fusion), channel_id=1, source_target_pairs={{0,8},{1,9},{2,10},{3,11},{4,5},{5,4},{6,7},{7,6},{8,0},{9,1},{10,... | collective-permute-start | bytes 712712 | tf_op jit(solution)/shard_map/ppermute | solution.py:373
  26.3 1.9 %collective-permute-start.7 = (bf16[64,3712]{1,0:T(8,128)(2,1)S(1)}, bf16[64,3712]{1,0:T(8,128)(2,1)S(1)}, u32[]{:S(2)}, u32[]{:S(2)}) collective-permute-start(bf16[64,3712]{1,0:T(8,128)(2,1)S(1)} %maximum_select_fusion.own_ref), channel_id=1, source_target_pairs={{0,4},{1,5},{2,6},{3,7},{4,0},{5,1},{6,2},{7,3},{8,12},{9,13},{10,... | collective-permute-start | bytes 1425416 | tf_op jit(solution)/shard_map/ppermute | solution.py:373
  26.5 3.4 %collective-permute-start.3 = (bf16[64,3584]{1,0:T(8,128)(2,1)S(1)}, bf16[64,3584]{1,0:T(8,128)(2,1)S(1)}, u32[]{:S(2)}, u32[]{:S(2)}) collective-permute-start(bf16[64,3584]{1,0:T(8,128)(2,1)S(1)} %maximum_select_fusion.1.own_ref), channel_id=1, source_target_pairs={{0,4},{1,5},{2,6},{3,7},{4,0},{5,1},{6,2},{7,3},{8,12},{9,13},{10,... | collective-permute-start | bytes 1376264 | tf_op jit(solution)/shard_map/ppermute | solution.py:373
  34.1 1.9 %collective-permute-start.8 = (bf16[64,3584]{1,0:T(8,128)(2,1)S(1)}, bf16[64,3584]{1,0:T(8,128)(2,1)S(1)}, u32[]{:S(2)}, u32[]{:S(2)}) collective-permute-start(bf16[64,3584]{1,0:T(8,128)(2,1)S(1)} %get-tuple-element.36), channel_id=1, source_target_pairs={{0,4},{1,5},{2,6},{3,7},{4,0},{5,1},{6,2},{7,3},{8,12},{9,13},{10,... | collective-permute-start | bytes 1376264 | tf_op jit(solution)/shard_map/ppermute | solution.py:373
  35.2 1.9 %collective-permute-start.12 = (bf16[64,3584]{1,0:T(8,128)(2,1)S(1)}, bf16[64,3584]{1,0:T(8,128)(2,1)S(1)}, u32[]{:S(2)}, u32[]{:S(2)}) collective-permute-start(bf16[64,3584]{1,0:T(8,128)(2,1)S(1)} %get-tuple-element.40), channel_id=1, source_target_pairs={{0,4},{1,5},{2,6},{3,7},{4,0},{5,1},{6,2},{7,3},{8,12},{9,13},{10,... | collective-permute-start | bytes 1376264 | tf_op jit(solution)/shard_map/ppermute | solution.py:373
  36.1 7.7 %collective-permute-start.9 = (bf16[32,3584]{1,0:T(8,128)(2,1)S(1)}, bf16[32,3584]{1,0:T(8,128)(2,1)S(1)}, u32[]{:S(2)}, u32[]{:S(2)}) collective-permute-start(bf16[32,3584]{1,0:T(8,128)(2,1)S(1)} %get-tuple-element.41), channel_id=1, source_target_pairs={{0,8},{1,9},{2,10},{3,11},{4,12},{5,13},{6,14},{7,15},{8,0},{9,1},... | collective-permute-start | bytes 688136 | tf_op jit(solution)/shard_map/ppermute | solution.py:373
  37.1 7.9 %collective-permute-start.13 = (bf16[32,3584]{1,0:T(8,128)(2,1)S(1)}, bf16[32,3584]{1,0:T(8,128)(2,1)S(1)}, u32[]{:S(2)}, u32[]{:S(2)}) collective-permute-start(bf16[32,3584]{1,0:T(8,128)(2,1)S(1)} %get-tuple-element.43), channel_id=1, source_target_pairs={{0,1},{1,0},{2,3},{3,2},{4,5},{5,4},{6,7},{7,6},{8,9},{9,8},{10,11... | collective-permute-start | bytes 688136 | tf_op jit(solution)/shard_map/ppermute | solution.py:373
  43.8 4.9 %collective-permute-start.10 = (bf16[16,3584]{1,0:T(8,128)(2,1)S(1)}, bf16[16,3584]{1,0:T(8,128)(2,1)S(1)}, u32[]{:S(2)}, u32[]{:S(2)}) collective-permute-start(bf16[16,3584]{1,0:T(8,128)(2,1)S(1)} %get-tuple-element.45), channel_id=1, source_target_pairs={{0,1},{1,0},{2,3},{3,2},{4,5},{5,4},{6,7},{7,6},{8,9},{9,8},{10,11... | collective-permute-start | bytes 344072 | tf_op jit(solution)/shard_map/ppermute | solution.py:373
  45.1 4.9 %collective-permute-start.14 = (bf16[16,3584]{1,0:T(8,128)(2,1)S(1)}, bf16[16,3584]{1,0:T(8,128)(2,1)S(1)}, u32[]{:S(2)}, u32[]{:S(2)}) collective-permute-start(bf16[16,3584]{1,0:T(8,128)(2,1)S(1)} %get-tuple-element.47), channel_id=1, source_target_pairs={{0,8},{1,9},{2,10},{3,11},{4,12},{5,13},{6,14},{7,15},{8,0},{9,1},... | collective-permute-start | bytes 344072 | tf_op jit(solution)/shard_map/ppermute | solution.py:373
  48.7 5.9 %collective-permute-start.11 = (bf16[8,3584]{1,0:T(8,128)(2,1)S(1)}, bf16[8,3584]{1,0:T(8,128)(2,1)S(1)}, u32[]{:S(2)}, u32[]{:S(2)}) collective-permute-start(bf16[8,3584]{1,0:T(8,128)(2,1)S(1)} %fusion.5), channel_id=1, source_target_pairs={{0,2},{1,3},{2,0},{3,1},{4,6},{5,7},{6,4},{7,5},{8,10},{9,11},{10,... | collective-permute-start | bytes 172040 | tf_op jit(solution)/shard_map/ppermute | solution.py:373
  50.0 5.8 %collective-permute-start.15 = (bf16[8,3584]{1,0:T(8,128)(2,1)S(1)}, bf16[8,3584]{1,0:T(8,128)(2,1)S(1)}, u32[]{:S(2)}, u32[]{:S(2)}) collective-permute-start(bf16[8,3584]{1,0:T(8,128)(2,1)S(1)} %fusion.2), channel_id=1, source_target_pairs={{0,2},{1,3},{2,0},{3,1},{4,6},{5,7},{6,4},{7,5},{8,10},{9,11},{10,... | collective-permute-start | bytes 172040 | tf_op jit(solution)/shard_map/ppermute | solution.py:373

commit v15 on v14

--- a/solution.py
+++ b/solution.py
@@ -53,10 +53,9 @@
     )(tokens, group_ids.T, route_weights.T)
 
 
-def load_kernel(share, place_ref, routed_ref, shared_ref, out_ref, sems):
+def weight_copies(share, place_ref, routed_ref, shared_ref, out_ref, sems, parts):
     width, hidden = routed_ref.shape
     column = pl.multiple_of((place_ref[0] // share) * LANES, LANES)
-    parts = sems.shape[0] // 2
     piece = width // parts
     copies = []
     for i in range(parts):
@@ -68,7 +67,11 @@
             copies.append(
                 pltpu.make_async_copy(source, out_ref.at[at, pl.ds(lower, size)], sems.at[len(copies)])
             )
-    run_copies(copies)
+    return copies
+
+
+def load_kernel(share, place_ref, routed_ref, shared_ref, out_ref, sems):
+    run_copies(weight_copies(share, place_ref, routed_ref, shared_ref, out_ref, sems, sems.shape[0] // 2))
 
 
 def load_weights(place, routed, shared, share):
@@ -183,10 +186,9 @@
     return jnp.concatenate([value[i * quarter : (i + 1) * quarter] for i in (0, 2, 1, 3)], axis=0)
 
 
-def half_down_copies(share, place_ref, down_ref, sdown_ref, out_ref, lower, sems):
+def down_range_copies(share, place_ref, down_ref, sdown_ref, out_ref, lower, sems, parts):
     hidden = down_ref.shape[0]
     column = pl.multiple_of((place_ref[0] // share) * LANES, LANES)
-    parts = 2
     piece = out_ref.shape[1] // parts
     copies = []
     for i in range(parts):
@@ -206,28 +208,39 @@
     return copies
 
 
-def load_down_kernel(share, place_ref, down_ref, sdown_ref, out_ref, sems):
-    run_copies(half_down_copies(share, place_ref, down_ref, sdown_ref, out_ref, 0, sems))
-
-
-def load_down(place, down, sdown, cut, share):
-    units = down.shape[0] + LANES
+def load_late_kernel(share, place_ref, up_ref, sup_ref, down_ref, sdown_ref, up_out_ref, down_out_ref, sems):
+    parts = (sems.shape[0] - 4) // 2
+    run_copies(
+        weight_copies(share, place_ref, up_ref, sup_ref, up_out_ref, sems, parts)
+        + down_range_copies(share, place_ref, down_ref, sdown_ref, down_out_ref, 0, sems.at[2 * parts :], 2)
+    )
+
+
+def load_late(place, up, sup, down, sdown, cut, share):
+    width, hidden = up.shape
+    units = hidden + LANES
     return pl.pallas_call(
-        functools.partial(load_down_kernel, share),
-        in_specs=[SMEM_SPEC] + [ANY_SPEC] * 2,
-        out_specs=VMEM_SPEC,
-        out_shape=pltpu.VMEM((units, cut), BF16),
-        scratch_shapes=[pltpu.SemaphoreType.DMA((4,))],
-        cost_estimate=pl.CostEstimate(flops=0, bytes_accessed=4 * units * cut, transcendentals=0),
+        functools.partial(load_late_kernel, share),
+        in_specs=[SMEM_SPEC] + [ANY_SPEC] * 4,
+        out_specs=[VMEM_SPEC] * 2,
+        out_shape=[pltpu.VMEM((width, units), BF16), pltpu.VMEM((units, cut), BF16)],
+        scratch_shapes=[pltpu.SemaphoreType.DMA((12,))],
+        cost_estimate=pl.CostEstimate(flops=0, bytes_accessed=4 * units * (width + cut), transcendentals=0),
         compiler_params=pltpu.CompilerParams(vmem_limit_bytes=1 << 20),
-        name="load_down",
-    )(place, in_hbm(down), in_hbm(sdown))
-
-
-def late_half_kernel(place_ref, own_ref, other_ref, gate_ref, up_ref, gate_acc_ref, up_acc_ref, weight_ref, x):
+        name="load_late",
+    )(place, *(in_hbm(w) for w in (up, sup, down, sdown)))
+
+
+def late_half_kernel(
+    share, place_ref, own_ref, other_ref, gate_ref, up_ref, down_ref, sdown_ref,
+    gate_acc_ref, up_acc_ref, weight_ref, later_ref, x, sems,
+):
     width, units = gate_ref.shape
     half, columns = own_ref.shape
     cut = width + LANES - columns
+    copies = down_range_copies(share, place_ref, down_ref, sdown_ref, later_ref, cut, sems, 1)
+    for copy in copies:
+        copy.start()
     x[:half, :] = own_ref[...]
     x[half:, :] = other_ref[...]
     rows = x[:, : width - cut]
@@ -236,6 +249,8 @@
         up_acc_ref[:, at] = jnp.dot(rows, up_ref[cut:, at], preferred_element_type=F32)
     weight = row_weight(place_ref[0], x[:, width - cut :])
     weight_ref[...] = jnp.broadcast_to(weight, weight_ref.shape)
+    for copy in copies:
+        copy.wait()
 
 
 def early_half_kernel(
@@ -243,7 +258,8 @@
     down_ref, sdown_ref, own_out_ref, other_out_ref, act_ref, later_ref, x, sems,
 ):
     half, cut = own_ref.shape
-    copies = half_down_copies(share, place_ref, down_ref, sdown_ref, later_ref, cut, sems)
+    lower = down_ref.shape[1] - later_ref.shape[1]
+    copies = down_range_copies(share, place_ref, down_ref, sdown_ref, later_ref, lower, sems, 1)
     for copy in copies:
         copy.start()
     units = gate_ref.shape[1]
@@ -269,12 +285,12 @@
         copy.wait()
 
 
-def last_half_kernel(act_ref, second_ref, own_out_ref, other_out_ref):
+def last_half_kernel(act_ref, third_ref, fourth_ref, own_out_ref, other_out_ref):
     half, columns = own_out_ref.shape
     piece = columns // 2
-    for i in range(2):
+    for i, later_ref in enumerate((third_ref, fourth_ref)):
         at = slice(i * piece, (i + 1) * piece)
-        total = jnp.dot(act_ref[...], second_ref[:, at], preferred_element_type=F32).astype(BF16)
+        total = jnp.dot(act_ref[...], later_ref[...], preferred_element_type=F32).astype(BF16)
         own_out_ref[:, at] = swap_quarters(total[:half])
         other_out_ref[:, at] = swap_quarters(total[half:])
 
@@ -289,17 +305,19 @@
     half, cut = own[0].shape
     hidden, width = down.shape
     units = hidden + LANES
-    partial = pl.pallas_call(
-        late_half_kernel,
-        in_specs=[SMEM_SPEC] + [VMEM_SPEC] * 4,
-        out_specs=[VMEM_SPEC] * 3,
-        out_shape=[pltpu.VMEM((2 * half, columns), F32) for columns in (units, units, LANES)],
-        scratch_shapes=[pltpu.VMEM((2 * half, own[1].shape[1]), BF16)],
+    down, sdown = in_hbm(down), in_hbm(sdown)
+    quarter = pltpu.VMEM((units, (width - cut) // 2), BF16)
+    *partial, third = pl.pallas_call(
+        functools.partial(late_half_kernel, share),
+        in_specs=[SMEM_SPEC] + [VMEM_SPEC] * 4 + [ANY_SPEC] * 2,
+        out_specs=[VMEM_SPEC] * 4,
+        out_shape=[pltpu.VMEM((2 * half, columns), F32) for columns in (units, units, LANES)] + [quarter],
+        scratch_shapes=[pltpu.VMEM((2 * half, own[1].shape[1]), BF16), pltpu.SemaphoreType.DMA((2,))],
         cost_estimate=estimate(2 * half, width - cut, 2 * units),
         compiler_params=pltpu.CompilerParams(vmem_limit_bytes=10 << 20),
         name="late_half",
-    )(place, own[1], other[1], gate, up)
-    own_out, other_out, act, later = pl.pallas_call(
+    )(place, own[1], other[1], gate, up, down, sdown)
+    own_out, other_out, act, fourth = pl.pallas_call(
         functools.partial(early_half_kernel, share),
         in_specs=[SMEM_SPEC] + [VMEM_SPEC] * 8 + [ANY_SPEC] * 2,
         out_specs=[VMEM_SPEC] * 4,
@@ -307,22 +325,22 @@
             pltpu.VMEM((half, cut), BF16),
             pltpu.VMEM((half, cut), BF16),
             pltpu.VMEM((2 * half, units), BF16),
-            pltpu.VMEM((units, width - cut), BF16),
+            quarter,
         ],
-        scratch_shapes=[pltpu.VMEM((2 * half, cut), BF16), pltpu.SemaphoreType.DMA((4,))],
+        scratch_shapes=[pltpu.VMEM((2 * half, cut), BF16), pltpu.SemaphoreType.DMA((2,))],
         cost_estimate=estimate(2 * half, cut, 3 * units),
         compiler_params=pltpu.CompilerParams(vmem_limit_bytes=10 << 20),
         name="early_half",
-    )(place, own[0], other[0], gate, up, *partial, second, in_hbm(down), in_hbm(sdown))
+    )(place, own[0], other[0], gate, up, *partial, second, down, sdown)
     last = pl.pallas_call(
         last_half_kernel,
-        in_specs=[VMEM_SPEC] * 2,
+        in_specs=[VMEM_SPEC] * 3,
         out_specs=[VMEM_SPEC] * 2,
         out_shape=[pltpu.VMEM((half, width - cut), BF16)] * 2,
         cost_estimate=estimate(2 * half, width - cut, units),
         compiler_params=pltpu.CompilerParams(vmem_limit_bytes=10 << 20),
         name="last_half",
-    )(act, later)
+    )(act, third, fourth)
     return own_out, last[0], other_out, last[1]
 
 
@@ -411,19 +429,21 @@
     cut = width // 2
     own = [packed[:, :cut], packed[:, cut:]]
     loads = (
-        lambda *ready: load_down(after(place, *ready), down, down_shared, cut, share),
-        lambda *ready: load_weights(after(place, *ready), gate, gate_shared, share),
-        lambda *ready: load_weights(after(place, *ready), up, up_shared, share),
-    )
-    loaded = []
+        lambda *ready: (),
+        lambda *ready: (load_weights(after(place, *ready), gate, gate_shared, share),),
+        lambda *ready: load_late(after(place, *ready), up, up_shared, down, down_shared, cut, share),
+    )
+    loaded = ()
     for phase, load in zip(GATHER, loads):
-        got = [flipped(part, *pairs) for part, pairs in zip(own, (phase[::-1], phase))]
-        got[1], weights = lax.optimization_barrier((got[1], load(*own)))
-        loaded.append(weights)
+        got = [flipped(part, *pairs) for part, pairs in zip(own, (phase, phase[::-1]))]
+        weights = tuple(load(*own))
+        if weights:
+            got, weights = lax.optimization_barrier((got, weights))
+        loaded += weights
         own = [stack(part, add) for part, add in zip(own, got)]
-    second, gate, up = loaded
+    gate, up, second = loaded
     odd = place[0] % 2
-    own = [jnp.where(odd == 1 - i, part, regroup(part, 4, 2)) for i, part in enumerate(own)]
+    own = [jnp.where(odd == i, part, regroup(part, 4, 2)) for i, part in enumerate(own)]
     other = [flipped(part, CORE, CORE) for part in own]
 
     outs = pair_rows(place, own, other, gate, up, second, down, down_shared, share)

time: 56.7 us -> 56.9 us (level)
  starting transfers between devices: 13.8 us -> 23.5 us
  waiting for transfers between devices: 23.6 us -> 14.1 us
    ppermute x16, starting transfers between devices: 13.8 us -> 23.5 us  [flipped(): return lax.ppermute(value, ('node', 'local'), pairs)]
    ppermute x16, waiting for transfers between devices: 23.6 us -> 14.1 us  [flipped(): return lax.ppermute(value, ('node', 'local'), pairs)]
    pallas_call x3, Pallas kernels: 4.85 us -> 9.04 us  [the longest x1 5.05 us: load_late(): pl.pallas_call(functools.partial(load_late_kernel, share), in_specs=[SMEM...]
    pallas_call x2 -> x1, Pallas kernels: 7.38 us -> 3.69 us  [load_weights(): pl.pallas_call(functools.partial(load_kernel, share), in_specs=[SMEM_SPEC...]
    pallas_call x1, Pallas kernels: 4.17 us -> 3.55 us  [pair_rows(): pl.pallas_call(functools.partial(early_half_kernel, share), in_specs=[SME...]
  transfers between devices with their start and end apart: 16 -> 16, of which waited for: 11 -> 8; matrix products, arithmetic and copies ran while one was open for 1% -> 1% of each run, Pallas kernels for 22% -> 22%
where the time goes in v15:
time: 56.9 us; the launch traced here: 56.7 us
  starting transfers between devices  23.5 us (41%)
  Pallas kernels  17.3 us (30%)
  waiting for transfers between devices  14.1 us (25%)
  other arithmetic  1.35 us (2%)
    ppermute x16, starting transfers between devices, flipped(): return lax.ppermute(value, ('node', 'local'), pairs)  23.5 us
    ppermute x16, waiting for transfers between devices, flipped(): return lax.ppermute(value, ('node', 'local'), pairs)  14.1 us
    pallas_call x1, Pallas kernels, load_late(): pl.pallas_call(functools.partial(load_late_kernel, share), in_specs=[SMEM...  5.05 us
    pallas_call x1, Pallas kernels, load_weights(): pl.pallas_call(functools.partial(load_kernel, share), in_specs=[SMEM_SPEC...  3.69 us
    pallas_call x1, Pallas kernels, pair_rows(): pl.pallas_call(functools.partial(early_half_kernel, share), in_specs=[SME...  3.55 us
    pallas_call x1, Pallas kernels, pair_rows(): pl.pallas_call(functools.partial(late_half_kernel, share), in_specs=[SMEM...  3.1 us
  transfers between devices with their start and end apart: 16, of which 8 were waited for; matrix products, arithmetic and copies ran while one was open for 1% of the time, Pallas kernels for 22%

profile of v15, /device:TPU:0, one launch (start us, length us, event | category | flops | bytes accessed | tf_op | source)
XLA Modules:
  0.0 56.7 jit_solution(7300527764041518868)
XLA Ops:
  0.0 1.1 %pack_rows.1 = bf16[8,7296]{1,0:T(8,128)(2,1)S(1)} custom-call(bf16[8,7168]{1,0:T(8,128)(2,1)} %tokens_ref.1, s32[4,8]{1,0:T(4,128)} %bitcast.11, bf16[4,8]{1,0:T(4,128)(2,1)} %bitcast.12), custom_call_target="tpu_custom_call" | custom-call | tf_op jit(solution)/shard_map/pack_rows/pallas_call | solution.py:48
  1.1 3.0 %collective-permute-start.2 = (bf16[8,3712]{1,0:T(8,128)(2,1)S(1)}, bf16[8,3712]{1,0:T(8,128)(2,1)S(1)}, u32[]{:S(2)}, u32[]{:S(2)}) collective-permute-start(bf16[8,3712]{1,0:T(8,128)(2,1)S(1)} %get-tuple-element.56), channel_id=1, source_target_pairs={{0,8},{1,9},{2,10},{3,11},{4,6},{5,7},{6,4},{7,5},{8,0},{9,1},{10,... | collective-permute-start | bytes 178184 | tf_op jit(solution)/shard_map/ppermute | solution.py:391
  4.1 2.7 %collective-permute-start = (bf16[8,3584]{1,0:T(8,128)(2,1)S(1)}, bf16[8,3584]{1,0:T(8,128)(2,1)S(1)}, u32[]{:S(2)}, u32[]{:S(2)}) collective-permute-start(bf16[8,3584]{1,0:T(8,128)(2,1)S(1)} %get-tuple-element.57), channel_id=1, source_target_pairs={{0,2},{1,3},{2,0},{3,1},{4,12},{5,13},{6,14},{7,15},{8,10},{9,11},... | collective-permute-start | bytes 172040 | tf_op jit(solution)/shard_map/ppermute | solution.py:391
  6.8 0.0 collective-permute-done.2
  6.8 2.7 %collective-permute-start.3 = (bf16[16,3712]{1,0:T(8,128)(2,1)S(1)}, bf16[16,3712]{1,0:T(8,128)(2,1)S(1)}, u32[]{:S(2)}, u32[]{:S(2)}) collective-permute-start(bf16[16,3712]{1,0:T(8,128)(2,1)S(1)} %pad_maximum_fusion.2), channel_id=1, source_target_pairs={{0,2},{1,3},{2,0},{3,1},{4,5},{5,4},{6,7},{7,6},{8,10},{9,11},{10,... | collective-permute-start | bytes 356360 | tf_op jit(solution)/shard_map/ppermute | solution.py:391
  9.5 0.0 collective-permute-done
  9.5 1.6 %collective-permute-start.1 = (bf16[16,3584]{1,0:T(8,128)(2,1)S(1)}, bf16[16,3584]{1,0:T(8,128)(2,1)S(1)}, u32[]{:S(2)}, u32[]{:S(2)}) collective-permute-start(bf16[16,3584]{1,0:T(8,128)(2,1)S(1)} %pad_maximum_fusion.3), channel_id=1, source_target_pairs={{0,1},{1,0},{2,3},{3,2},{4,6},{5,7},{6,4},{7,5},{8,9},{9,8},{10,11... | collective-permute-start | bytes 344072 | tf_op jit(solution)/shard_map/ppermute | solution.py:391
  11.1 3.7 %load_weights.1.gate_ref = bf16[7168,640]{1,0:T(8,128)(2,1)S(1)} custom-call(s32[1]{0:T(128)} %bitcast.place_ref, bf16[7168,512]{1,0:T(8,128)(2,1)} %bitcast.9, bf16[7168,512]{1,0:T(8,128)(2,1)} %shared_ref.1), custom_call_target="tpu_custom_call" | custom-call | bytes 18350080 | tf_op jit(solution)/shard_map/load_weights/pallas_call | solution.py:80
  14.8 0.0 collective-permute-done.1
  14.8 1.1 %collective-permute-done.3 = bf16[16,3712]{1,0:T(8,128)(2,1)S(1)} collective-permute-done((bf16[16,3712]{1,0:T(8,128)(2,1)S(1)}, bf16[16,3712]{1,0:T(8,128)(2,1)S(1)}, u32[]{:S(2)}, u32[]{:S(2)}) %collective-permute-start.3) | collective-permute-done | bytes 118816 | tf_op jit(solution)/shard_map/ppermute | solution.py:391
  15.9 1.6 %collective-permute-start.4 = (bf16[32,3584]{1,0:T(8,128)(2,1)S(1)}, bf16[32,3584]{1,0:T(8,128)(2,1)S(1)}, u32[]{:S(2)}, u32[]{:S(2)}) collective-permute-start(bf16[32,3584]{1,0:T(8,128)(2,1)S(1)} %pad_maximum_fusion.1), channel_id=1, source_target_pairs={{0,8},{1,9},{2,10},{3,11},{4,5},{5,4},{6,7},{7,6},{8,0},{9,1},{10,... | collective-permute-start | bytes 688136 | tf_op jit(solution)/shard_map/ppermute | solution.py:391
  17.6 0.9 %collective-permute-start.5 = (bf16[32,3712]{1,0:T(8,128)(2,1)S(1)}, bf16[32,3712]{1,0:T(8,128)(2,1)S(1)}, u32[]{:S(2)}, u32[]{:S(2)}) collective-permute-start(bf16[32,3712]{1,0:T(8,128)(2,1)S(1)} %pad_maximum_fusion), channel_id=1, source_target_pairs={{0,1},{1,0},{2,3},{3,2},{4,12},{5,13},{6,14},{7,15},{8,9},{9,8},{1... | collective-permute-start | bytes 712712 | tf_op jit(solution)/shard_map/ppermute | solution.py:391
  18.5 5.1 %load_late.1 = (bf16[7168,640]{1,0:T(8,128)(2,1)S(1)}, bf16[640,3584]{1,0:T(8,128)(2,1)S(1)}) custom-call(s32[1]{0:T(128)} %bitcast.place_ref, bf16[7168,512]{1,0:T(8,128)(2,1)} %bitcast.10, bf16[7168,512]{1,0:T(8,128)(2,1)} %sup_ref.1, bf16[512,7168]{1,0:T(8,128)(2,1)} %bitcast.6, bf16[512,7168]{1,0:T(8,128)(2,1)} %sdown_ref.5), custom_call_target="tpu_custom_call" | custom-call | bytes 27525120 | tf_op jit(solution)/shard_map/load_late/pallas_call | solution.py:222
  23.6 0.4 collective-permute-done.4
  23.9 0.0 collective-permute-done.5
  24.1 0.1 maximum_select_fusion.own_ref
  24.3 0.1 collective-permute-start.7
  24.3 0.1 maximum_select_fusion.1.own_ref
  24.5 0.6 collective-permute-start.6
  25.0 1.1 %collective-permute-done.7.other_ref = bf16[64,3712]{1,0:T(8,128)(2,1)S(1)} collective-permute-done((bf16[64,3712]{1,0:T(8,128)(2,1)S(1)}, bf16[64,3712]{1,0:T(8,128)(2,1)S(1)}, u32[]{:S(2)}, u32[]{:S(2)}) %collective-permute-start.7) | collective-permute-done | bytes 475168 | tf_op jit(solution)/shard_map/ppermute | solution.py:391
  26.2 3.1 %late_half.1 = (f32[128,640]{1,0:T(8,128)S(1)}, f32[128,640]{1,0:T(8,128)S(1)}, f32[128,128]{1,0:T(8,128)S(1)}, bf16[640,1792]{1,0:T(8,128)(2,1)S(1)}) custom-call(s32[1]{0:T(128)} %bitcast.place_ref, bf16[64,3712]{1,0:T(8,128)(2,1)S(1)} %maximum_select_fusion.own_ref, bf16[64,3712]{1,0:T(8,128)(2,1)S(1)} %collective-permute-done.7.other_ref, ...), custom_call_target="tpu_custom_call" | custom-call | flops 1174405120 | bytes 9175040 | tf_op jit(solution)/shard_map/late_half/pallas_call | solution.py:310
  29.3 0.0 collective-permute-done.6.other_ref
  29.3 3.5 %early_half.1 = (bf16[64,3584]{1,0:T(8,128)(2,1)S(1)}, bf16[64,3584]{1,0:T(8,128)(2,1)S(1)}, bf16[128,640]{1,0:T(8,128)(2,1)S(1)}, bf16[640,1792]{1,0:T(8,128)(2,1)S(1)}) custom-call(s32[1]{0:T(128)} %bitcast.place_ref, bf16[64,3584]{1,0:T(8,128)(2,1)S(1)} %maximum_select_fusion.1.own_ref, bf16[64,3584]{1,0:T(8,128)(2,1)S(1)} %collective-permute-done.6.other_ref, ...), custom_call_target="tpu_custom_call" | custom-call | flops 1761607680 | bytes 13762560 | tf_op jit(solution)/shard_map/early_half/pallas_call | solution.py:320
  32.8 0.2 collective-permute-start.8
  33.0 0.9 %last_half.1 = (bf16[64,3584]{1,0:T(8,128)(2,1)S(1)}, bf16[64,3584]{1,0:T(8,128)(2,1)S(1)}) custom-call(bf16[128,640]{1,0:T(8,128)(2,1)S(1)} %get-tuple-element.42.act_ref, bf16[640,1792]{1,0:T(8,128)(2,1)S(1)} %get-tuple-element.43.third_ref, bf16[640,1792]{1,0:T(8,128)(2,1)S(1)} %get-tuple-element.44.fourth_ref), custom_call_target="tpu_custom_call" | custom-call | flops 587202560 | bytes 4587520 | tf_op jit(solution)/shard_map/last_half/pallas_call | solution.py:335
  33.9 0.4 collective-permute-start.12
  34.4 0.4 collective-permute-done.8
  34.7 0.1 add_convert_fusion.1
  34.8 1.6 %collective-permute-start.9 = (bf16[32,3584]{1,0:T(8,128)(2,1)S(1)}, bf16[32,3584]{1,0:T(8,128)(2,1)S(1)}, u32[]{:S(2)}, u32[]{:S(2)}) collective-permute-start(bf16[32,3584]{1,0:T(8,128)(2,1)S(1)} %get-tuple-element.47), channel_id=1, source_target_pairs={{0,8},{1,9},{2,10},{3,11},{4,12},{5,13},{6,14},{7,15},{8,0},{9,1},... | collective-permute-start | bytes 688136 | tf_op jit(solution)/shard_map/ppermute | solution.py:391
  36.4 0.0 collective-permute-done.12
  36.4 0.1 add_convert_fusion
  36.5 1.3 %collective-permute-start.13 = (bf16[32,3584]{1,0:T(8,128)(2,1)S(1)}, bf16[32,3584]{1,0:T(8,128)(2,1)S(1)}, u32[]{:S(2)}, u32[]{:S(2)}) collective-permute-start(bf16[32,3584]{1,0:T(8,128)(2,1)S(1)} %get-tuple-element.49), channel_id=1, source_target_pairs={{0,1},{1,0},{2,3},{3,2},{4,5},{5,4},{6,7},{7,6},{8,9},{9,8},{10,11... | collective-permute-start | bytes 688136 | tf_op jit(solution)/shard_map/ppermute | solution.py:391
  37.8 4.7 %collective-permute-done.9 = bf16[32,3584]{1,0:T(8,128)(2,1)S(1)} collective-permute-done((bf16[32,3584]{1,0:T(8,128)(2,1)S(1)}, bf16[32,3584]{1,0:T(8,128)(2,1)S(1)}, u32[]{:S(2)}, u32[]{:S(2)}) %collective-permute-start.9) | collective-permute-done | bytes 229408 | tf_op jit(solution)/shard_map/ppermute | solution.py:391
  42.5 0.1 fusion.1
  42.6 1.3 %collective-permute-start.10 = (bf16[16,3584]{1,0:T(8,128)(2,1)S(1)}, bf16[16,3584]{1,0:T(8,128)(2,1)S(1)}, u32[]{:S(2)}, u32[]{:S(2)}) collective-permute-start(bf16[16,3584]{1,0:T(8,128)(2,1)S(1)} %get-tuple-element.51), channel_id=1, source_target_pairs={{0,1},{1,0},{2,3},{3,2},{4,5},{5,4},{6,7},{7,6},{8,9},{9,8},{10,11... | collective-permute-start | bytes 344072 | tf_op jit(solution)/shard_map/ppermute | solution.py:391
  43.9 0.0 collective-permute-done.13
  44.0 0.1 fusion
  44.0 1.5 %collective-permute-start.14 = (bf16[16,3584]{1,0:T(8,128)(2,1)S(1)}, bf16[16,3584]{1,0:T(8,128)(2,1)S(1)}, u32[]{:S(2)}, u32[]{:S(2)}) collective-permute-start(bf16[16,3584]{1,0:T(8,128)(2,1)S(1)} %get-tuple-element.53), channel_id=1, source_target_pairs={{0,8},{1,9},{2,10},{3,11},{4,12},{5,13},{6,14},{7,15},{8,0},{9,1},... | collective-permute-start | bytes 344072 | tf_op jit(solution)/shard_map/ppermute | solution.py:391
  45.5 1.9 %collective-permute-done.10 = bf16[16,3584]{1,0:T(8,128)(2,1)S(1)} collective-permute-done((bf16[16,3584]{1,0:T(8,128)(2,1)S(1)}, bf16[16,3584]{1,0:T(8,128)(2,1)S(1)}, u32[]{:S(2)}, u32[]{:S(2)}) %collective-permute-start.10) | collective-permute-done | bytes 114720 | tf_op jit(solution)/shard_map/ppermute | solution.py:391
  47.5 2.8 %collective-permute-start.11 = (bf16[8,3584]{1,0:T(8,128)(2,1)S(1)}, bf16[8,3584]{1,0:T(8,128)(2,1)S(1)}, u32[]{:S(2)}, u32[]{:S(2)}) collective-permute-start(bf16[8,3584]{1,0:T(8,128)(2,1)S(1)} %fusion.5), channel_id=1, source_target_pairs={{0,2},{1,3},{2,0},{3,1},{4,6},{5,7},{6,4},{7,5},{8,10},{9,11},{10,... | collective-permute-start | bytes 172040 | tf_op jit(solution)/shard_map/ppermute | solution.py:391
  50.2 0.0 collective-permute-done.14
  50.2 1.3 %collective-permute-start.15 = (bf16[8,3584]{1,0:T(8,128)(2,1)S(1)}, bf16[8,3584]{1,0:T(8,128)(2,1)S(1)}, u32[]{:S(2)}, u32[]{:S(2)}) collective-permute-start(bf16[8,3584]{1,0:T(8,128)(2,1)S(1)} %fusion.2), channel_id=1, source_target_pairs={{0,2},{1,3},{2,0},{3,1},{4,6},{5,7},{6,4},{7,5},{8,10},{9,11},{10,... | collective-permute-start | bytes 172040 | tf_op jit(solution)/shard_map/ppermute | solution.py:391
  51.5 2.6 %collective-permute-done.11 = bf16[8,3584]{1,0:T(8,128)(2,1)S(1)} collective-permute-done((bf16[8,3584]{1,0:T(8,128)(2,1)S(1)}, bf16[8,3584]{1,0:T(8,128)(2,1)S(1)}, u32[]{:S(2)}, u32[]{:S(2)}) %collective-permute-start.11) | collective-permute-done | bytes 57376 | tf_op jit(solution)/shard_map/ppermute | solution.py:391
  54.2 1.8 %collective-permute-done.15 = bf16[8,3584]{1,0:T(8,128)(2,1)S(1)} collective-permute-done((bf16[8,3584]{1,0:T(8,128)(2,1)S(1)}, bf16[8,3584]{1,0:T(8,128)(2,1)S(1)}, u32[]{:S(2)}, u32[]{:S(2)}) %collective-permute-start.15) | collective-permute-done | bytes 57376 | tf_op jit(solution)/shard_map/ppermute | solution.py:391
  56.0 0.7 %pad_maximum_fusion.4 = bf16[8,7168]{1,0:T(8,128)(2,1)} fusion(bf16[8,3584]{1,0:T(8,128)(2,1)S(1)} %fusion.4, bf16[8,3584]{1,0:T(8,128)(2,1)S(1)} %fusion.7), kind=kLoop, calls=%fused_computation.26 | loop fusion | flops 229376 | bytes 229376 | tf_op jit(solution)/shard_map/concatenate | solution.py:458
  (24 shorter events, 0.3 us)
Async XLA Ops:
  1.1 5.7 %collective-permute-start.2 = (bf16[8,3712]{1,0:T(8,128)(2,1)S(1)}, bf16[8,3712]{1,0:T(8,128)(2,1)S(1)}, u32[]{:S(2)}, u32[]{:S(2)}) collective-permute-start(bf16[8,3712]{1,0:T(8,128)(2,1)S(1)} %get-tuple-element.56), channel_id=1, source_target_pairs={{0,8},{1,9},{2,10},{3,11},{4,6},{5,7},{6,4},{7,5},{8,0},{9,1},{10,... | collective-permute-start | bytes 178184 | tf_op jit(solution)/shard_map/ppermute | solution.py:391
  4.1 5.4 %collective-permute-start = (bf16[8,3584]{1,0:T(8,128)(2,1)S(1)}, bf16[8,3584]{1,0:T(8,128)(2,1)S(1)}, u32[]{:S(2)}, u32[]{:S(2)}) collective-permute-start(bf16[8,3584]{1,0:T(8,128)(2,1)S(1)} %get-tuple-element.57), channel_id=1, source_target_pairs={{0,2},{1,3},{2,0},{3,1},{4,12},{5,13},{6,14},{7,15},{8,10},{9,11},... | collective-permute-start | bytes 172040 | tf_op jit(solution)/shard_map/ppermute | solution.py:391
  6.8 9.1 %collective-permute-start.3 = (bf16[16,3712]{1,0:T(8,128)(2,1)S(1)}, bf16[16,3712]{1,0:T(8,128)(2,1)S(1)}, u32[]{:S(2)}, u32[]{:S(2)}) collective-permute-start(bf16[16,3712]{1,0:T(8,128)(2,1)S(1)} %pad_maximum_fusion.2), channel_id=1, source_target_pairs={{0,2},{1,3},{2,0},{3,1},{4,5},{5,4},{6,7},{7,6},{8,10},{9,11},{10,... | collective-permute-start | bytes 356360 | tf_op jit(solution)/shard_map/ppermute | solution.py:391
  9.5 5.3 %collective-permute-start.1 = (bf16[16,3584]{1,0:T(8,128)(2,1)S(1)}, bf16[16,3584]{1,0:T(8,128)(2,1)S(1)}, u32[]{:S(2)}, u32[]{:S(2)}) collective-permute-start(bf16[16,3584]{1,0:T(8,128)(2,1)S(1)} %pad_maximum_fusion.3), channel_id=1, source_target_pairs={{0,1},{1,0},{2,3},{3,2},{4,6},{5,7},{6,4},{7,5},{8,9},{9,8},{10,11... | collective-permute-start | bytes 344072 | tf_op jit(solution)/shard_map/ppermute | solution.py:391
  15.9 8.0 %collective-permute-start.4 = (bf16[32,3584]{1,0:T(8,128)(2,1)S(1)}, bf16[32,3584]{1,0:T(8,128)(2,1)S(1)}, u32[]{:S(2)}, u32[]{:S(2)}) collective-permute-start(bf16[32,3584]{1,0:T(8,128)(2,1)S(1)} %pad_maximum_fusion.1), channel_id=1, source_target_pairs={{0,8},{1,9},{2,10},{3,11},{4,5},{5,4},{6,7},{7,6},{8,0},{9,1},{10,... | collective-permute-start | bytes 688136 | tf_op jit(solution)/shard_map/ppermute | solution.py:391
  17.6 6.3 %collective-permute-start.5 = (bf16[32,3712]{1,0:T(8,128)(2,1)S(1)}, bf16[32,3712]{1,0:T(8,128)(2,1)S(1)}, u32[]{:S(2)}, u32[]{:S(2)}) collective-permute-start(bf16[32,3712]{1,0:T(8,128)(2,1)S(1)} %pad_maximum_fusion), channel_id=1, source_target_pairs={{0,1},{1,0},{2,3},{3,2},{4,12},{5,13},{6,14},{7,15},{8,9},{9,8},{1... | collective-permute-start | bytes 712712 | tf_op jit(solution)/shard_map/ppermute | solution.py:391
  24.3 1.9 %collective-permute-start.7 = (bf16[64,3712]{1,0:T(8,128)(2,1)S(1)}, bf16[64,3712]{1,0:T(8,128)(2,1)S(1)}, u32[]{:S(2)}, u32[]{:S(2)}) collective-permute-start(bf16[64,3712]{1,0:T(8,128)(2,1)S(1)} %maximum_select_fusion.own_ref), channel_id=1, source_target_pairs={{0,4},{1,5},{2,6},{3,7},{4,0},{5,1},{6,2},{7,3},{8,12},{9,13},{10,... | collective-permute-start | bytes 1425416 | tf_op jit(solution)/shard_map/ppermute | solution.py:391
  24.5 4.8 %collective-permute-start.6 = (bf16[64,3584]{1,0:T(8,128)(2,1)S(1)}, bf16[64,3584]{1,0:T(8,128)(2,1)S(1)}, u32[]{:S(2)}, u32[]{:S(2)}) collective-permute-start(bf16[64,3584]{1,0:T(8,128)(2,1)S(1)} %maximum_select_fusion.1.own_ref), channel_id=1, source_target_pairs={{0,4},{1,5},{2,6},{3,7},{4,0},{5,1},{6,2},{7,3},{8,12},{9,13},{10,... | collective-permute-start | bytes 1376264 | tf_op jit(solution)/shard_map/ppermute | solution.py:391
  32.8 1.9 %collective-permute-start.8 = (bf16[64,3584]{1,0:T(8,128)(2,1)S(1)}, bf16[64,3584]{1,0:T(8,128)(2,1)S(1)}, u32[]{:S(2)}, u32[]{:S(2)}) collective-permute-start(bf16[64,3584]{1,0:T(8,128)(2,1)S(1)} %get-tuple-element.41), channel_id=1, source_target_pairs={{0,4},{1,5},{2,6},{3,7},{4,0},{5,1},{6,2},{7,3},{8,12},{9,13},{10,... | collective-permute-start | bytes 1376264 | tf_op jit(solution)/shard_map/ppermute | solution.py:391
  33.9 2.5 %collective-permute-start.12 = (bf16[64,3584]{1,0:T(8,128)(2,1)S(1)}, bf16[64,3584]{1,0:T(8,128)(2,1)S(1)}, u32[]{:S(2)}, u32[]{:S(2)}) collective-permute-start(bf16[64,3584]{1,0:T(8,128)(2,1)S(1)} %get-tuple-element.46), channel_id=1, source_target_pairs={{0,4},{1,5},{2,6},{3,7},{4,0},{5,1},{6,2},{7,3},{8,12},{9,13},{10,... | collective-permute-start | bytes 1376264 | tf_op jit(solution)/shard_map/ppermute | solution.py:391
  34.8 7.7 %collective-permute-start.9 = (bf16[32,3584]{1,0:T(8,128)(2,1)S(1)}, bf16[32,3584]{1,0:T(8,128)(2,1)S(1)}, u32[]{:S(2)}, u32[]{:S(2)}) collective-permute-start(bf16[32,3584]{1,0:T(8,128)(2,1)S(1)} %get-tuple-element.47), channel_id=1, source_target_pairs={{0,8},{1,9},{2,10},{3,11},{4,12},{5,13},{6,14},{7,15},{8,0},{9,1},... | collective-permute-start | bytes 688136 | tf_op jit(solution)/shard_map/ppermute | solution.py:391
  36.5 7.4 %collective-permute-start.13 = (bf16[32,3584]{1,0:T(8,128)(2,1)S(1)}, bf16[32,3584]{1,0:T(8,128)(2,1)S(1)}, u32[]{:S(2)}, u32[]{:S(2)}) collective-permute-start(bf16[32,3584]{1,0:T(8,128)(2,1)S(1)} %get-tuple-element.49), channel_id=1, source_target_pairs={{0,1},{1,0},{2,3},{3,2},{4,5},{5,4},{6,7},{7,6},{8,9},{9,8},{10,11... | collective-permute-start | bytes 688136 | tf_op jit(solution)/shard_map/ppermute | solution.py:391
  42.6 4.9 %collective-permute-start.10 = (bf16[16,3584]{1,0:T(8,128)(2,1)S(1)}, bf16[16,3584]{1,0:T(8,128)(2,1)S(1)}, u32[]{:S(2)}, u32[]{:S(2)}) collective-permute-start(bf16[16,3584]{1,0:T(8,128)(2,1)S(1)} %get-tuple-element.51), channel_id=1, source_target_pairs={{0,1},{1,0},{2,3},{3,2},{4,5},{5,4},{6,7},{7,6},{8,9},{9,8},{10,11... | collective-permute-start | bytes 344072 | tf_op jit(solution)/shard_map/ppermute | solution.py:391
  44.0 6.2 %collective-permute-start.14 = (bf16[16,3584]{1,0:T(8,128)(2,1)S(1)}, bf16[16,3584]{1,0:T(8,128)(2,1)S(1)}, u32[]{:S(2)}, u32[]{:S(2)}) collective-permute-start(bf16[16,3584]{1,0:T(8,128)(2,1)S(1)} %get-tuple-element.53), channel_id=1, source_target_pairs={{0,8},{1,9},{2,10},{3,11},{4,12},{5,13},{6,14},{7,15},{8,0},{9,1},... | collective-permute-start | bytes 344072 | tf_op jit(solution)/shard_map/ppermute | solution.py:391
  47.5 6.7 %collective-permute-start.11 = (bf16[8,3584]{1,0:T(8,128)(2,1)S(1)}, bf16[8,3584]{1,0:T(8,128)(2,1)S(1)}, u32[]{:S(2)}, u32[]{:S(2)}) collective-permute-start(bf16[8,3584]{1,0:T(8,128)(2,1)S(1)} %fusion.5), channel_id=1, source_target_pairs={{0,2},{1,3},{2,0},{3,1},{4,6},{5,7},{6,4},{7,5},{8,10},{9,11},{10,... | collective-permute-start | bytes 172040 | tf_op jit(solution)/shard_map/ppermute | solution.py:391
  50.2 5.8 %collective-permute-start.15 = (bf16[8,3584]{1,0:T(8,128)(2,1)S(1)}, bf16[8,3584]{1,0:T(8,128)(2,1)S(1)}, u32[]{:S(2)}, u32[]{:S(2)}) collective-permute-start(bf16[8,3584]{1,0:T(8,128)(2,1)S(1)} %fusion.2), channel_id=1, source_target_pairs={{0,2},{1,3},{2,0},{3,1},{4,6},{5,7},{6,4},{7,5},{8,10},{9,11},{10,... | collective-permute-start | bytes 172040 | tf_op jit(solution)/shard_map/ppermute | solution.py:391

commit v16 on v15

--- a/solution.py
+++ b/solution.py
@@ -186,33 +186,30 @@
     return jnp.concatenate([value[i * quarter : (i + 1) * quarter] for i in (0, 2, 1, 3)], axis=0)
 
 
-def down_range_copies(share, place_ref, down_ref, sdown_ref, out_ref, lower, sems, parts):
+DOWN_ROWS = 64
+
+
+def down_range_copies(share, place_ref, down_ref, sdown_ref, out_ref, lower, sems):
     hidden = down_ref.shape[0]
     column = pl.multiple_of((place_ref[0] // share) * LANES, LANES)
-    piece = out_ref.shape[1] // parts
+    columns = pl.ds(lower, out_ref.shape[1])
     copies = []
-    for i in range(parts):
-        source, target = pl.ds(lower + i * piece, piece), pl.ds(i * piece, piece)
+    for at in range(0, hidden + LANES, DOWN_ROWS):
+        if at < hidden:
+            source = down_ref.at[pl.ds(at, DOWN_ROWS), columns]
+        else:
+            source = sdown_ref.at[pl.ds(column + (at - hidden), DOWN_ROWS), columns]
         copies.append(
-            pltpu.make_async_copy(
-                down_ref.at[:, source], out_ref.at[pl.ds(0, hidden), target], sems.at[2 * i]
-            )
-        )
-        copies.append(
-            pltpu.make_async_copy(
-                sdown_ref.at[pl.ds(column, LANES), source],
-                out_ref.at[pl.ds(hidden, LANES), target],
-                sems.at[2 * i + 1],
-            )
+            pltpu.make_async_copy(source, out_ref.at[pl.ds(at, DOWN_ROWS), :], sems.at[len(copies)])
         )
     return copies
 
 
 def load_late_kernel(share, place_ref, up_ref, sup_ref, down_ref, sdown_ref, up_out_ref, down_out_ref, sems):
-    parts = (sems.shape[0] - 4) // 2
+    parts = 4
     run_copies(
         weight_copies(share, place_ref, up_ref, sup_ref, up_out_ref, sems, parts)
-        + down_range_copies(share, place_ref, down_ref, sdown_ref, down_out_ref, 0, sems.at[2 * parts :], 2)
+        + down_range_copies(share, place_ref, down_ref, sdown_ref, down_out_ref, 0, sems.at[2 * parts :])
     )
 
 
@@ -224,7 +221,7 @@
         in_specs=[SMEM_SPEC] + [ANY_SPEC] * 4,
         out_specs=[VMEM_SPEC] * 2,
         out_shape=[pltpu.VMEM((width, units), BF16), pltpu.VMEM((units, cut), BF16)],
-        scratch_shapes=[pltpu.SemaphoreType.DMA((12,))],
+        scratch_shapes=[pltpu.SemaphoreType.DMA((8 + units // DOWN_ROWS,))],
         cost_estimate=pl.CostEstimate(flops=0, bytes_accessed=4 * units * (width + cut), transcendentals=0),
         compiler_params=pltpu.CompilerParams(vmem_limit_bytes=1 << 20),
         name="load_late",
@@ -238,7 +235,7 @@
     width, units = gate_ref.shape
     half, columns = own_ref.shape
     cut = width + LANES - columns
-    copies = down_range_copies(share, place_ref, down_ref, sdown_ref, later_ref, cut, sems, 1)
+    copies = down_range_copies(share, place_ref, down_ref, sdown_ref, later_ref, cut, sems)
     for copy in copies:
         copy.start()
     x[:half, :] = own_ref[...]
@@ -259,7 +256,7 @@
 ):
     half, cut = own_ref.shape
     lower = down_ref.shape[1] - later_ref.shape[1]
-    copies = down_range_copies(share, place_ref, down_ref, sdown_ref, later_ref, lower, sems, 1)
+    copies = down_range_copies(share, place_ref, down_ref, sdown_ref, later_ref, lower, sems)
     for copy in copies:
         copy.start()
     units = gate_ref.shape[1]
@@ -312,7 +309,7 @@
         in_specs=[SMEM_SPEC] + [VMEM_SPEC] * 4 + [ANY_SPEC] * 2,
         out_specs=[VMEM_SPEC] * 4,
         out_shape=[pltpu.VMEM((2 * half, columns), F32) for columns in (units, units, LANES)] + [quarter],
-        scratch_shapes=[pltpu.VMEM((2 * half, own[1].shape[1]), BF16), pltpu.SemaphoreType.DMA((2,))],
+        scratch_shapes=[pltpu.VMEM((2 * half, own[1].shape[1]), BF16), pltpu.SemaphoreType.DMA((units // DOWN_ROWS,))],
         cost_estimate=estimate(2 * half, width - cut, 2 * units),
         compiler_params=pltpu.CompilerParams(vmem_limit_bytes=10 << 20),
         name="late_half",
@@ -327,7 +324,7 @@
             pltpu.VMEM((2 * half, units), BF16),
             quarter,
         ],
-        scratch_shapes=[pltpu.VMEM((2 * half, cut), BF16), pltpu.SemaphoreType.DMA((2,))],
+        scratch_shapes=[pltpu.VMEM((2 * half, cut), BF16), pltpu.SemaphoreType.DMA((units // DOWN_ROWS,))],
         cost_estimate=estimate(2 * half, cut, 3 * units),
         compiler_params=pltpu.CompilerParams(vmem_limit_bytes=10 << 20),
         name="early_half",

time: 56.9 us -> 57.6 us (1.012)
  Pallas kernels: 17.3 us -> 18.1 us
  transfers between devices with their start and end apart: 16 -> 16, of which waited for: 8 -> 8; matrix products, arithmetic and copies ran while one was open for 1% -> 1% of each run, Pallas kernels for 22% -> 23%
where the time goes in v16:
time: 57.6 us; the launch traced here: 57.4 us
  starting transfers between devices  23.6 us (41%)
  Pallas kernels  18.1 us (31%)
  waiting for transfers between devices  14 us (24%)
  other arithmetic  1.35 us (2%)
    ppermute x16, starting transfers between devices, flipped(): return lax.ppermute(value, ('node', 'local'), pairs)  23.6 us
    ppermute x16, waiting for transfers between devices, flipped(): return lax.ppermute(value, ('node', 'local'), pairs)  14 us
    pallas_call x1, Pallas kernels, load_late(): pl.pallas_call(functools.partial(load_late_kernel, share), in_specs=[SMEM...  5.09 us
    pallas_call x1, Pallas kernels, pair_rows(): pl.pallas_call(functools.partial(early_half_kernel, share), in_specs=[SME...  4.07 us
    pallas_call x1, Pallas kernels, load_weights(): pl.pallas_call(functools.partial(load_kernel, share), in_specs=[SMEM_SPEC...  3.69 us
    pallas_call x1, Pallas kernels, pair_rows(): pl.pallas_call(functools.partial(late_half_kernel, share), in_specs=[SMEM...  3.3 us
  transfers between devices with their start and end apart: 16, of which 8 were waited for; matrix products, arithmetic and copies ran while one was open for 1% of the time, Pallas kernels for 23%

profile of v16, /device:TPU:0, one launch (start us, length us, event | category | flops | bytes accessed | tf_op | source)
XLA Modules:
  0.0 57.4 jit_solution(7097294635267422954)
XLA Ops:
  0.0 1.1 %pack_rows.1 = bf16[8,7296]{1,0:T(8,128)(2,1)S(1)} custom-call(bf16[8,7168]{1,0:T(8,128)(2,1)} %tokens_ref.1, s32[4,8]{1,0:T(4,128)} %bitcast.11, bf16[4,8]{1,0:T(4,128)(2,1)} %bitcast.12), custom_call_target="tpu_custom_call" | custom-call | tf_op jit(solution)/shard_map/pack_rows/pallas_call | solution.py:48
  1.1 3.0 %collective-permute-start.2 = (bf16[8,3712]{1,0:T(8,128)(2,1)S(1)}, bf16[8,3712]{1,0:T(8,128)(2,1)S(1)}, u32[]{:S(2)}, u32[]{:S(2)}) collective-permute-start(bf16[8,3712]{1,0:T(8,128)(2,1)S(1)} %get-tuple-element.56), channel_id=1, source_target_pairs={{0,8},{1,9},{2,10},{3,11},{4,6},{5,7},{6,4},{7,5},{8,0},{9,1},{10,... | collective-permute-start | bytes 178184 | tf_op jit(solution)/shard_map/ppermute | solution.py:388
  4.1 2.7 %collective-permute-start = (bf16[8,3584]{1,0:T(8,128)(2,1)S(1)}, bf16[8,3584]{1,0:T(8,128)(2,1)S(1)}, u32[]{:S(2)}, u32[]{:S(2)}) collective-permute-start(bf16[8,3584]{1,0:T(8,128)(2,1)S(1)} %get-tuple-element.57), channel_id=1, source_target_pairs={{0,2},{1,3},{2,0},{3,1},{4,12},{5,13},{6,14},{7,15},{8,10},{9,11},... | collective-permute-start | bytes 172040 | tf_op jit(solution)/shard_map/ppermute | solution.py:388
  6.8 0.0 collective-permute-done.2
  6.8 2.7 %collective-permute-start.3 = (bf16[16,3712]{1,0:T(8,128)(2,1)S(1)}, bf16[16,3712]{1,0:T(8,128)(2,1)S(1)}, u32[]{:S(2)}, u32[]{:S(2)}) collective-permute-start(bf16[16,3712]{1,0:T(8,128)(2,1)S(1)} %pad_maximum_fusion.2), channel_id=1, source_target_pairs={{0,2},{1,3},{2,0},{3,1},{4,5},{5,4},{6,7},{7,6},{8,10},{9,11},{10,... | collective-permute-start | bytes 356360 | tf_op jit(solution)/shard_map/ppermute | solution.py:388
  9.5 0.0 collective-permute-done
  9.5 1.6 %collective-permute-start.1 = (bf16[16,3584]{1,0:T(8,128)(2,1)S(1)}, bf16[16,3584]{1,0:T(8,128)(2,1)S(1)}, u32[]{:S(2)}, u32[]{:S(2)}) collective-permute-start(bf16[16,3584]{1,0:T(8,128)(2,1)S(1)} %pad_maximum_fusion.3), channel_id=1, source_target_pairs={{0,1},{1,0},{2,3},{3,2},{4,6},{5,7},{6,4},{7,5},{8,9},{9,8},{10,11... | collective-permute-start | bytes 344072 | tf_op jit(solution)/shard_map/ppermute | solution.py:388
  11.1 3.7 %load_weights.1.gate_ref = bf16[7168,640]{1,0:T(8,128)(2,1)S(1)} custom-call(s32[1]{0:T(128)} %bitcast.place_ref, bf16[7168,512]{1,0:T(8,128)(2,1)} %bitcast.9, bf16[7168,512]{1,0:T(8,128)(2,1)} %shared_ref.1), custom_call_target="tpu_custom_call" | custom-call | bytes 18350080 | tf_op jit(solution)/shard_map/load_weights/pallas_call | solution.py:80
  14.8 0.0 collective-permute-done.1
  14.8 1.1 %collective-permute-done.3 = bf16[16,3712]{1,0:T(8,128)(2,1)S(1)} collective-permute-done((bf16[16,3712]{1,0:T(8,128)(2,1)S(1)}, bf16[16,3712]{1,0:T(8,128)(2,1)S(1)}, u32[]{:S(2)}, u32[]{:S(2)}) %collective-permute-start.3) | collective-permute-done | bytes 118816 | tf_op jit(solution)/shard_map/ppermute | solution.py:388
  15.9 1.6 %collective-permute-start.4 = (bf16[32,3584]{1,0:T(8,128)(2,1)S(1)}, bf16[32,3584]{1,0:T(8,128)(2,1)S(1)}, u32[]{:S(2)}, u32[]{:S(2)}) collective-permute-start(bf16[32,3584]{1,0:T(8,128)(2,1)S(1)} %pad_maximum_fusion.1), channel_id=1, source_target_pairs={{0,8},{1,9},{2,10},{3,11},{4,5},{5,4},{6,7},{7,6},{8,0},{9,1},{10,... | collective-permute-start | bytes 688136 | tf_op jit(solution)/shard_map/ppermute | solution.py:388
  17.6 0.9 %collective-permute-start.5 = (bf16[32,3712]{1,0:T(8,128)(2,1)S(1)}, bf16[32,3712]{1,0:T(8,128)(2,1)S(1)}, u32[]{:S(2)}, u32[]{:S(2)}) collective-permute-start(bf16[32,3712]{1,0:T(8,128)(2,1)S(1)} %pad_maximum_fusion), channel_id=1, source_target_pairs={{0,1},{1,0},{2,3},{3,2},{4,12},{5,13},{6,14},{7,15},{8,9},{9,8},{1... | collective-permute-start | bytes 712712 | tf_op jit(solution)/shard_map/ppermute | solution.py:388
  18.5 5.1 %load_late.1 = (bf16[7168,640]{1,0:T(8,128)(2,1)S(1)}, bf16[640,3584]{1,0:T(8,128)(2,1)S(1)}) custom-call(s32[1]{0:T(128)} %bitcast.place_ref, bf16[7168,512]{1,0:T(8,128)(2,1)} %bitcast.10, bf16[7168,512]{1,0:T(8,128)(2,1)} %sup_ref.1, bf16[512,7168]{1,0:T(8,128)(2,1)} %bitcast.6, bf16[512,7168]{1,0:T(8,128)(2,1)} %sdown_ref.5), custom_call_target="tpu_custom_call" | custom-call | bytes 27525120 | tf_op jit(solution)/shard_map/load_late/pallas_call | solution.py:219
  23.6 0.3 collective-permute-done.4
  23.9 0.0 collective-permute-done.5
  24.1 0.1 maximum_select_fusion.own_ref
  24.3 0.1 collective-permute-start.7
  24.3 0.1 maximum_select_fusion.1.own_ref
  24.5 0.6 collective-permute-start.6
  25.0 1.1 %collective-permute-done.7.other_ref = bf16[64,3712]{1,0:T(8,128)(2,1)S(1)} collective-permute-done((bf16[64,3712]{1,0:T(8,128)(2,1)S(1)}, bf16[64,3712]{1,0:T(8,128)(2,1)S(1)}, u32[]{:S(2)}, u32[]{:S(2)}) %collective-permute-start.7) | collective-permute-done | bytes 475168 | tf_op jit(solution)/shard_map/ppermute | solution.py:388
  26.2 3.3 %late_half.1 = (f32[128,640]{1,0:T(8,128)S(1)}, f32[128,640]{1,0:T(8,128)S(1)}, f32[128,128]{1,0:T(8,128)S(1)}, bf16[640,1792]{1,0:T(8,128)(2,1)S(1)}) custom-call(s32[1]{0:T(128)} %bitcast.place_ref, bf16[64,3712]{1,0:T(8,128)(2,1)S(1)} %maximum_select_fusion.own_ref, bf16[64,3712]{1,0:T(8,128)(2,1)S(1)} %collective-permute-done.7.other_ref, ...), custom_call_target="tpu_custom_call" | custom-call | flops 1174405120 | bytes 9175040 | tf_op jit(solution)/shard_map/late_half/pallas_call | solution.py:307
  29.5 0.0 collective-permute-done.6.other_ref
  29.5 4.1 %early_half.1 = (bf16[64,3584]{1,0:T(8,128)(2,1)S(1)}, bf16[64,3584]{1,0:T(8,128)(2,1)S(1)}, bf16[128,640]{1,0:T(8,128)(2,1)S(1)}, bf16[640,1792]{1,0:T(8,128)(2,1)S(1)}) custom-call(s32[1]{0:T(128)} %bitcast.place_ref, bf16[64,3584]{1,0:T(8,128)(2,1)S(1)} %maximum_select_fusion.1.own_ref, bf16[64,3584]{1,0:T(8,128)(2,1)S(1)} %collective-permute-done.6.other_ref, ...), custom_call_target="tpu_custom_call" | custom-call | flops 1761607680 | bytes 13762560 | tf_op jit(solution)/shard_map/early_half/pallas_call | solution.py:317
  33.5 0.2 collective-permute-start.8
  33.8 0.9 %last_half.1 = (bf16[64,3584]{1,0:T(8,128)(2,1)S(1)}, bf16[64,3584]{1,0:T(8,128)(2,1)S(1)}) custom-call(bf16[128,640]{1,0:T(8,128)(2,1)S(1)} %get-tuple-element.42.act_ref, bf16[640,1792]{1,0:T(8,128)(2,1)S(1)} %get-tuple-element.43.third_ref, bf16[640,1792]{1,0:T(8,128)(2,1)S(1)} %get-tuple-element.44.fourth_ref), custom_call_target="tpu_custom_call" | custom-call | flops 587202560 | bytes 4587520 | tf_op jit(solution)/shard_map/last_half/pallas_call | solution.py:332
  34.6 0.4 collective-permute-start.12
  35.1 0.4 collective-permute-done.8
  35.4 0.1 add_convert_fusion.1
  35.5 1.6 %collective-permute-start.9 = (bf16[32,3584]{1,0:T(8,128)(2,1)S(1)}, bf16[32,3584]{1,0:T(8,128)(2,1)S(1)}, u32[]{:S(2)}, u32[]{:S(2)}) collective-permute-start(bf16[32,3584]{1,0:T(8,128)(2,1)S(1)} %get-tuple-element.47), channel_id=1, source_target_pairs={{0,8},{1,9},{2,10},{3,11},{4,12},{5,13},{6,14},{7,15},{8,0},{9,1},... | collective-permute-start | bytes 688136 | tf_op jit(solution)/shard_map/ppermute | solution.py:388
  37.1 0.0 collective-permute-done.12
  37.1 0.1 add_convert_fusion
  37.2 1.3 %collective-permute-start.13 = (bf16[32,3584]{1,0:T(8,128)(2,1)S(1)}, bf16[32,3584]{1,0:T(8,128)(2,1)S(1)}, u32[]{:S(2)}, u32[]{:S(2)}) collective-permute-start(bf16[32,3584]{1,0:T(8,128)(2,1)S(1)} %get-tuple-element.49), channel_id=1, source_target_pairs={{0,1},{1,0},{2,3},{3,2},{4,5},{5,4},{6,7},{7,6},{8,9},{9,8},{10,11... | collective-permute-start | bytes 688136 | tf_op jit(solution)/shard_map/ppermute | solution.py:388
  38.5 4.7 %collective-permute-done.9 = bf16[32,3584]{1,0:T(8,128)(2,1)S(1)} collective-permute-done((bf16[32,3584]{1,0:T(8,128)(2,1)S(1)}, bf16[32,3584]{1,0:T(8,128)(2,1)S(1)}, u32[]{:S(2)}, u32[]{:S(2)}) %collective-permute-start.9) | collective-permute-done | bytes 229408 | tf_op jit(solution)/shard_map/ppermute | solution.py:388
  43.2 0.1 fusion.1
  43.3 1.3 %collective-permute-start.10 = (bf16[16,3584]{1,0:T(8,128)(2,1)S(1)}, bf16[16,3584]{1,0:T(8,128)(2,1)S(1)}, u32[]{:S(2)}, u32[]{:S(2)}) collective-permute-start(bf16[16,3584]{1,0:T(8,128)(2,1)S(1)} %get-tuple-element.51), channel_id=1, source_target_pairs={{0,1},{1,0},{2,3},{3,2},{4,5},{5,4},{6,7},{7,6},{8,9},{9,8},{10,11... | collective-permute-start | bytes 344072 | tf_op jit(solution)/shard_map/ppermute | solution.py:388
  44.6 0.0 collective-permute-done.13
  44.7 0.1 fusion
  44.7 1.5 %collective-permute-start.14 = (bf16[16,3584]{1,0:T(8,128)(2,1)S(1)}, bf16[16,3584]{1,0:T(8,128)(2,1)S(1)}, u32[]{:S(2)}, u32[]{:S(2)}) collective-permute-start(bf16[16,3584]{1,0:T(8,128)(2,1)S(1)} %get-tuple-element.53), channel_id=1, source_target_pairs={{0,8},{1,9},{2,10},{3,11},{4,12},{5,13},{6,14},{7,15},{8,0},{9,1},... | collective-permute-start | bytes 344072 | tf_op jit(solution)/shard_map/ppermute | solution.py:388
  46.2 1.9 %collective-permute-done.10 = bf16[16,3584]{1,0:T(8,128)(2,1)S(1)} collective-permute-done((bf16[16,3584]{1,0:T(8,128)(2,1)S(1)}, bf16[16,3584]{1,0:T(8,128)(2,1)S(1)}, u32[]{:S(2)}, u32[]{:S(2)}) %collective-permute-start.10) | collective-permute-done | bytes 114720 | tf_op jit(solution)/shard_map/ppermute | solution.py:388
  48.2 2.8 %collective-permute-start.11 = (bf16[8,3584]{1,0:T(8,128)(2,1)S(1)}, bf16[8,3584]{1,0:T(8,128)(2,1)S(1)}, u32[]{:S(2)}, u32[]{:S(2)}) collective-permute-start(bf16[8,3584]{1,0:T(8,128)(2,1)S(1)} %fusion.5), channel_id=1, source_target_pairs={{0,2},{1,3},{2,0},{3,1},{4,6},{5,7},{6,4},{7,5},{8,10},{9,11},{10,... | collective-permute-start | bytes 172040 | tf_op jit(solution)/shard_map/ppermute | solution.py:388
  50.9 0.0 collective-permute-done.14
  51.0 1.3 %collective-permute-start.15 = (bf16[8,3584]{1,0:T(8,128)(2,1)S(1)}, bf16[8,3584]{1,0:T(8,128)(2,1)S(1)}, u32[]{:S(2)}, u32[]{:S(2)}) collective-permute-start(bf16[8,3584]{1,0:T(8,128)(2,1)S(1)} %fusion.2), channel_id=1, source_target_pairs={{0,2},{1,3},{2,0},{3,1},{4,6},{5,7},{6,4},{7,5},{8,10},{9,11},{10,... | collective-permute-start | bytes 172040 | tf_op jit(solution)/shard_map/ppermute | solution.py:388
  52.3 2.6 %collective-permute-done.11 = bf16[8,3584]{1,0:T(8,128)(2,1)S(1)} collective-permute-done((bf16[8,3584]{1,0:T(8,128)(2,1)S(1)}, bf16[8,3584]{1,0:T(8,128)(2,1)S(1)}, u32[]{:S(2)}, u32[]{:S(2)}) %collective-permute-start.11) | collective-permute-done | bytes 57376 | tf_op jit(solution)/shard_map/ppermute | solution.py:388
  54.9 1.8 %collective-permute-done.15 = bf16[8,3584]{1,0:T(8,128)(2,1)S(1)} collective-permute-done((bf16[8,3584]{1,0:T(8,128)(2,1)S(1)}, bf16[8,3584]{1,0:T(8,128)(2,1)S(1)}, u32[]{:S(2)}, u32[]{:S(2)}) %collective-permute-start.15) | collective-permute-done | bytes 57376 | tf_op jit(solution)/shard_map/ppermute | solution.py:388
  56.7 0.7 %pad_maximum_fusion.4 = bf16[8,7168]{1,0:T(8,128)(2,1)} fusion(bf16[8,3584]{1,0:T(8,128)(2,1)S(1)} %fusion.4, bf16[8,3584]{1,0:T(8,128)(2,1)S(1)} %fusion.7), kind=kLoop, calls=%fused_computation.26 | loop fusion | flops 229376 | bytes 229376 | tf_op jit(solution)/shard_map/concatenate | solution.py:455
  (24 shorter events, 0.3 us)
Async XLA Ops:
  1.1 5.7 %collective-permute-start.2 = (bf16[8,3712]{1,0:T(8,128)(2,1)S(1)}, bf16[8,3712]{1,0:T(8,128)(2,1)S(1)}, u32[]{:S(2)}, u32[]{:S(2)}) collective-permute-start(bf16[8,3712]{1,0:T(8,128)(2,1)S(1)} %get-tuple-element.56), channel_id=1, source_target_pairs={{0,8},{1,9},{2,10},{3,11},{4,6},{5,7},{6,4},{7,5},{8,0},{9,1},{10,... | collective-permute-start | bytes 178184 | tf_op jit(solution)/shard_map/ppermute | solution.py:388
  4.1 5.4 %collective-permute-start = (bf16[8,3584]{1,0:T(8,128)(2,1)S(1)}, bf16[8,3584]{1,0:T(8,128)(2,1)S(1)}, u32[]{:S(2)}, u32[]{:S(2)}) collective-permute-start(bf16[8,3584]{1,0:T(8,128)(2,1)S(1)} %get-tuple-element.57), channel_id=1, source_target_pairs={{0,2},{1,3},{2,0},{3,1},{4,12},{5,13},{6,14},{7,15},{8,10},{9,11},... | collective-permute-start | bytes 172040 | tf_op jit(solution)/shard_map/ppermute | solution.py:388
  6.8 9.1 %collective-permute-start.3 = (bf16[16,3712]{1,0:T(8,128)(2,1)S(1)}, bf16[16,3712]{1,0:T(8,128)(2,1)S(1)}, u32[]{:S(2)}, u32[]{:S(2)}) collective-permute-start(bf16[16,3712]{1,0:T(8,128)(2,1)S(1)} %pad_maximum_fusion.2), channel_id=1, source_target_pairs={{0,2},{1,3},{2,0},{3,1},{4,5},{5,4},{6,7},{7,6},{8,10},{9,11},{10,... | collective-permute-start | bytes 356360 | tf_op jit(solution)/shard_map/ppermute | solution.py:388
  9.5 5.3 %collective-permute-start.1 = (bf16[16,3584]{1,0:T(8,128)(2,1)S(1)}, bf16[16,3584]{1,0:T(8,128)(2,1)S(1)}, u32[]{:S(2)}, u32[]{:S(2)}) collective-permute-start(bf16[16,3584]{1,0:T(8,128)(2,1)S(1)} %pad_maximum_fusion.3), channel_id=1, source_target_pairs={{0,1},{1,0},{2,3},{3,2},{4,6},{5,7},{6,4},{7,5},{8,9},{9,8},{10,11... | collective-permute-start | bytes 344072 | tf_op jit(solution)/shard_map/ppermute | solution.py:388
  15.9 8.0 %collective-permute-start.4 = (bf16[32,3584]{1,0:T(8,128)(2,1)S(1)}, bf16[32,3584]{1,0:T(8,128)(2,1)S(1)}, u32[]{:S(2)}, u32[]{:S(2)}) collective-permute-start(bf16[32,3584]{1,0:T(8,128)(2,1)S(1)} %pad_maximum_fusion.1), channel_id=1, source_target_pairs={{0,8},{1,9},{2,10},{3,11},{4,5},{5,4},{6,7},{7,6},{8,0},{9,1},{10,... | collective-permute-start | bytes 688136 | tf_op jit(solution)/shard_map/ppermute | solution.py:388
  17.6 6.3 %collective-permute-start.5 = (bf16[32,3712]{1,0:T(8,128)(2,1)S(1)}, bf16[32,3712]{1,0:T(8,128)(2,1)S(1)}, u32[]{:S(2)}, u32[]{:S(2)}) collective-permute-start(bf16[32,3712]{1,0:T(8,128)(2,1)S(1)} %pad_maximum_fusion), channel_id=1, source_target_pairs={{0,1},{1,0},{2,3},{3,2},{4,12},{5,13},{6,14},{7,15},{8,9},{9,8},{1... | collective-permute-start | bytes 712712 | tf_op jit(solution)/shard_map/ppermute | solution.py:388
  24.3 1.9 %collective-permute-start.7 = (bf16[64,3712]{1,0:T(8,128)(2,1)S(1)}, bf16[64,3712]{1,0:T(8,128)(2,1)S(1)}, u32[]{:S(2)}, u32[]{:S(2)}) collective-permute-start(bf16[64,3712]{1,0:T(8,128)(2,1)S(1)} %maximum_select_fusion.own_ref), channel_id=1, source_target_pairs={{0,4},{1,5},{2,6},{3,7},{4,0},{5,1},{6,2},{7,3},{8,12},{9,13},{10,... | collective-permute-start | bytes 1425416 | tf_op jit(solution)/shard_map/ppermute | solution.py:388
  24.5 5.0 %collective-permute-start.6 = (bf16[64,3584]{1,0:T(8,128)(2,1)S(1)}, bf16[64,3584]{1,0:T(8,128)(2,1)S(1)}, u32[]{:S(2)}, u32[]{:S(2)}) collective-permute-start(bf16[64,3584]{1,0:T(8,128)(2,1)S(1)} %maximum_select_fusion.1.own_ref), channel_id=1, source_target_pairs={{0,4},{1,5},{2,6},{3,7},{4,0},{5,1},{6,2},{7,3},{8,12},{9,13},{10,... | collective-permute-start | bytes 1376264 | tf_op jit(solution)/shard_map/ppermute | solution.py:388
  33.5 1.9 %collective-permute-start.8 = (bf16[64,3584]{1,0:T(8,128)(2,1)S(1)}, bf16[64,3584]{1,0:T(8,128)(2,1)S(1)}, u32[]{:S(2)}, u32[]{:S(2)}) collective-permute-start(bf16[64,3584]{1,0:T(8,128)(2,1)S(1)} %get-tuple-element.41), channel_id=1, source_target_pairs={{0,4},{1,5},{2,6},{3,7},{4,0},{5,1},{6,2},{7,3},{8,12},{9,13},{10,... | collective-permute-start | bytes 1376264 | tf_op jit(solution)/shard_map/ppermute | solution.py:388
  34.6 2.5 %collective-permute-start.12 = (bf16[64,3584]{1,0:T(8,128)(2,1)S(1)}, bf16[64,3584]{1,0:T(8,128)(2,1)S(1)}, u32[]{:S(2)}, u32[]{:S(2)}) collective-permute-start(bf16[64,3584]{1,0:T(8,128)(2,1)S(1)} %get-tuple-element.46), channel_id=1, source_target_pairs={{0,4},{1,5},{2,6},{3,7},{4,0},{5,1},{6,2},{7,3},{8,12},{9,13},{10,... | collective-permute-start | bytes 1376264 | tf_op jit(solution)/shard_map/ppermute | solution.py:388
  35.5 7.7 %collective-permute-start.9 = (bf16[32,3584]{1,0:T(8,128)(2,1)S(1)}, bf16[32,3584]{1,0:T(8,128)(2,1)S(1)}, u32[]{:S(2)}, u32[]{:S(2)}) collective-permute-start(bf16[32,3584]{1,0:T(8,128)(2,1)S(1)} %get-tuple-element.47), channel_id=1, source_target_pairs={{0,8},{1,9},{2,10},{3,11},{4,12},{5,13},{6,14},{7,15},{8,0},{9,1},... | collective-permute-start | bytes 688136 | tf_op jit(solution)/shard_map/ppermute | solution.py:388
  37.2 7.4 %collective-permute-start.13 = (bf16[32,3584]{1,0:T(8,128)(2,1)S(1)}, bf16[32,3584]{1,0:T(8,128)(2,1)S(1)}, u32[]{:S(2)}, u32[]{:S(2)}) collective-permute-start(bf16[32,3584]{1,0:T(8,128)(2,1)S(1)} %get-tuple-element.49), channel_id=1, source_target_pairs={{0,1},{1,0},{2,3},{3,2},{4,5},{5,4},{6,7},{7,6},{8,9},{9,8},{10,11... | collective-permute-start | bytes 688136 | tf_op jit(solution)/shard_map/ppermute | solution.py:388
  43.3 4.9 %collective-permute-start.10 = (bf16[16,3584]{1,0:T(8,128)(2,1)S(1)}, bf16[16,3584]{1,0:T(8,128)(2,1)S(1)}, u32[]{:S(2)}, u32[]{:S(2)}) collective-permute-start(bf16[16,3584]{1,0:T(8,128)(2,1)S(1)} %get-tuple-element.51), channel_id=1, source_target_pairs={{0,1},{1,0},{2,3},{3,2},{4,5},{5,4},{6,7},{7,6},{8,9},{9,8},{10,11... | collective-permute-start | bytes 344072 | tf_op jit(solution)/shard_map/ppermute | solution.py:388
  44.7 6.2 %collective-permute-start.14 = (bf16[16,3584]{1,0:T(8,128)(2,1)S(1)}, bf16[16,3584]{1,0:T(8,128)(2,1)S(1)}, u32[]{:S(2)}, u32[]{:S(2)}) collective-permute-start(bf16[16,3584]{1,0:T(8,128)(2,1)S(1)} %get-tuple-element.53), channel_id=1, source_target_pairs={{0,8},{1,9},{2,10},{3,11},{4,12},{5,13},{6,14},{7,15},{8,0},{9,1},... | collective-permute-start | bytes 344072 | tf_op jit(solution)/shard_map/ppermute | solution.py:388
  48.2 6.7 %collective-permute-start.11 = (bf16[8,3584]{1,0:T(8,128)(2,1)S(1)}, bf16[8,3584]{1,0:T(8,128)(2,1)S(1)}, u32[]{:S(2)}, u32[]{:S(2)}) collective-permute-start(bf16[8,3584]{1,0:T(8,128)(2,1)S(1)} %fusion.5), channel_id=1, source_target_pairs={{0,2},{1,3},{2,0},{3,1},{4,6},{5,7},{6,4},{7,5},{8,10},{9,11},{10,... | collective-permute-start | bytes 172040 | tf_op jit(solution)/shard_map/ppermute | solution.py:388
  51.0 5.8 %collective-permute-start.15 = (bf16[8,3584]{1,0:T(8,128)(2,1)S(1)}, bf16[8,3584]{1,0:T(8,128)(2,1)S(1)}, u32[]{:S(2)}, u32[]{:S(2)}) collective-permute-start(bf16[8,3584]{1,0:T(8,128)(2,1)S(1)} %fusion.2), channel_id=1, source_target_pairs={{0,2},{1,3},{2,0},{3,1},{4,6},{5,7},{6,4},{7,5},{8,10},{9,11},{10,... | collective-permute-start | bytes 172040 | tf_op jit(solution)/shard_map/ppermute | solution.py:388

commit v17 on v16

--- a/solution.py
+++ b/solution.py
@@ -186,7 +186,7 @@
     return jnp.concatenate([value[i * quarter : (i + 1) * quarter] for i in (0, 2, 1, 3)], axis=0)
 
 
-DOWN_ROWS = 64
+DOWN_ROWS = 128
 
 
 def down_range_copies(share, place_ref, down_ref, sdown_ref, out_ref, lower, sems):
@@ -205,39 +205,57 @@
     return copies
 
 
-def load_late_kernel(share, place_ref, up_ref, sup_ref, down_ref, sdown_ref, up_out_ref, down_out_ref, sems):
+def load_both_kernel(
+    share, lower, place_ref, routed_ref, shared_ref, down_ref, sdown_ref, out_ref, down_out_ref, sems
+):
     parts = 4
     run_copies(
-        weight_copies(share, place_ref, up_ref, sup_ref, up_out_ref, sems, parts)
-        + down_range_copies(share, place_ref, down_ref, sdown_ref, down_out_ref, 0, sems.at[2 * parts :])
-    )
-
-
-def load_late(place, up, sup, down, sdown, cut, share):
-    width, hidden = up.shape
+        weight_copies(share, place_ref, routed_ref, shared_ref, out_ref, sems, parts)
+        + down_range_copies(
+            share, place_ref, down_ref, sdown_ref, down_out_ref, lower, sems.at[2 * parts :]
+        )
+    )
+
+
+def load_both(place, routed, shared, down, sdown, lower, columns, share):
+    width, hidden = routed.shape
     units = hidden + LANES
     return pl.pallas_call(
-        functools.partial(load_late_kernel, share),
+        functools.partial(load_both_kernel, share, lower),
         in_specs=[SMEM_SPEC] + [ANY_SPEC] * 4,
         out_specs=[VMEM_SPEC] * 2,
-        out_shape=[pltpu.VMEM((width, units), BF16), pltpu.VMEM((units, cut), BF16)],
+        out_shape=[pltpu.VMEM((width, units), BF16), pltpu.VMEM((units, columns), BF16)],
         scratch_shapes=[pltpu.SemaphoreType.DMA((8 + units // DOWN_ROWS,))],
-        cost_estimate=pl.CostEstimate(flops=0, bytes_accessed=4 * units * (width + cut), transcendentals=0),
+        cost_estimate=pl.CostEstimate(
+            flops=0, bytes_accessed=4 * units * (width + columns), transcendentals=0
+        ),
         compiler_params=pltpu.CompilerParams(vmem_limit_bytes=1 << 20),
-        name="load_late",
-    )(place, *(in_hbm(w) for w in (up, sup, down, sdown)))
-
-
-def late_half_kernel(
-    share, place_ref, own_ref, other_ref, gate_ref, up_ref, down_ref, sdown_ref,
-    gate_acc_ref, up_acc_ref, weight_ref, later_ref, x, sems,
-):
+        name="load_both",
+    )(place, *(in_hbm(w) for w in (routed, shared, down, sdown)))
+
+
+def load_down_kernel(share, lower, place_ref, down_ref, sdown_ref, out_ref, sems):
+    run_copies(down_range_copies(share, place_ref, down_ref, sdown_ref, out_ref, lower, sems))
+
+
+def load_down(place, down, sdown, lower, columns, share):
+    units = down.shape[0] + LANES
+    return pl.pallas_call(
+        functools.partial(load_down_kernel, share, lower),
+        in_specs=[SMEM_SPEC] + [ANY_SPEC] * 2,
+        out_specs=VMEM_SPEC,
+        out_shape=pltpu.VMEM((units, columns), BF16),
+        scratch_shapes=[pltpu.SemaphoreType.DMA((units // DOWN_ROWS,))],
+        cost_estimate=pl.CostEstimate(flops=0, bytes_accessed=4 * units * columns, transcendentals=0),
+        compiler_params=pltpu.CompilerParams(vmem_limit_bytes=1 << 20),
+        name="load_down",
+    )(place, in_hbm(down), in_hbm(sdown))
+
+
+def late_half_kernel(place_ref, own_ref, other_ref, gate_ref, up_ref, gate_acc_ref, up_acc_ref, weight_ref, x):
     width, units = gate_ref.shape
     half, columns = own_ref.shape
     cut = width + LANES - columns
-    copies = down_range_copies(share, place_ref, down_ref, sdown_ref, later_ref, cut, sems)
-    for copy in copies:
-        copy.start()
     x[:half, :] = own_ref[...]
     x[half:, :] = other_ref[...]
     rows = x[:, : width - cut]
@@ -246,19 +264,13 @@
         up_acc_ref[:, at] = jnp.dot(rows, up_ref[cut:, at], preferred_element_type=F32)
     weight = row_weight(place_ref[0], x[:, width - cut :])
     weight_ref[...] = jnp.broadcast_to(weight, weight_ref.shape)
-    for copy in copies:
-        copy.wait()
 
 
 def early_half_kernel(
     share, place_ref, own_ref, other_ref, gate_ref, up_ref, gate_acc_ref, up_acc_ref, weight_ref, second_ref,
-    down_ref, sdown_ref, own_out_ref, other_out_ref, act_ref, later_ref, x, sems,
+    own_out_ref, other_out_ref, act_ref, x,
 ):
     half, cut = own_ref.shape
-    lower = down_ref.shape[1] - later_ref.shape[1]
-    copies = down_range_copies(share, place_ref, down_ref, sdown_ref, later_ref, lower, sems)
-    for copy in copies:
-        copy.start()
     units = gate_ref.shape[1]
     hidden = units - LANES
     x[:half, :] = own_ref[...]
@@ -278,8 +290,6 @@
         total = jnp.dot(act_ref[...], second_ref[:, at], preferred_element_type=F32).astype(BF16)
         own_out_ref[:, at] = total[:half]
         other_out_ref[:, at] = total[half:]
-    for copy in copies:
-        copy.wait()
 
 
 def last_half_kernel(act_ref, third_ref, fourth_ref, own_out_ref, other_out_ref):
@@ -298,37 +308,33 @@
     )
 
 
-def pair_rows(place, own, other, gate, up, second, down, sdown, share):
+def pair_rows(place, own, other, gate, up, second, third, fourth, share):
     half, cut = own[0].shape
-    hidden, width = down.shape
-    units = hidden + LANES
-    down, sdown = in_hbm(down), in_hbm(sdown)
-    quarter = pltpu.VMEM((units, (width - cut) // 2), BF16)
-    *partial, third = pl.pallas_call(
-        functools.partial(late_half_kernel, share),
-        in_specs=[SMEM_SPEC] + [VMEM_SPEC] * 4 + [ANY_SPEC] * 2,
-        out_specs=[VMEM_SPEC] * 4,
-        out_shape=[pltpu.VMEM((2 * half, columns), F32) for columns in (units, units, LANES)] + [quarter],
-        scratch_shapes=[pltpu.VMEM((2 * half, own[1].shape[1]), BF16), pltpu.SemaphoreType.DMA((units // DOWN_ROWS,))],
+    width, units = gate.shape
+    partial = pl.pallas_call(
+        late_half_kernel,
+        in_specs=[SMEM_SPEC] + [VMEM_SPEC] * 4,
+        out_specs=[VMEM_SPEC] * 3,
+        out_shape=[pltpu.VMEM((2 * half, columns), F32) for columns in (units, units, LANES)],
+        scratch_shapes=[pltpu.VMEM((2 * half, own[1].shape[1]), BF16)],
         cost_estimate=estimate(2 * half, width - cut, 2 * units),
         compiler_params=pltpu.CompilerParams(vmem_limit_bytes=10 << 20),
         name="late_half",
-    )(place, own[1], other[1], gate, up, down, sdown)
-    own_out, other_out, act, fourth = pl.pallas_call(
+    )(place, own[1], other[1], gate, up)
+    own_out, other_out, act = pl.pallas_call(
         functools.partial(early_half_kernel, share),
-        in_specs=[SMEM_SPEC] + [VMEM_SPEC] * 8 + [ANY_SPEC] * 2,
-        out_specs=[VMEM_SPEC] * 4,
+        in_specs=[SMEM_SPEC] + [VMEM_SPEC] * 8,
+        out_specs=[VMEM_SPEC] * 3,
         out_shape=[
             pltpu.VMEM((half, cut), BF16),
             pltpu.VMEM((half, cut), BF16),
             pltpu.VMEM((2 * half, units), BF16),
-            quarter,
         ],
-        scratch_shapes=[pltpu.VMEM((2 * half, cut), BF16), pltpu.SemaphoreType.DMA((units // DOWN_ROWS,))],
+        scratch_shapes=[pltpu.VMEM((2 * half, cut), BF16)],
         cost_estimate=estimate(2 * half, cut, 3 * units),
         compiler_params=pltpu.CompilerParams(vmem_limit_bytes=10 << 20),
         name="early_half",
-    )(place, own[0], other[0], gate, up, *partial, second, down, sdown)
+    )(place, own[0], other[0], gate, up, *partial, second)
     last = pl.pallas_call(
         last_half_kernel,
         in_specs=[VMEM_SPEC] * 3,
@@ -425,10 +431,13 @@
 
     cut = width // 2
     own = [packed[:, :cut], packed[:, cut:]]
+    quarter = (width - cut) // 2
     loads = (
         lambda *ready: (),
-        lambda *ready: (load_weights(after(place, *ready), gate, gate_shared, share),),
-        lambda *ready: load_late(after(place, *ready), up, up_shared, down, down_shared, cut, share),
+        lambda *ready: load_both(
+            after(place, *ready), gate, gate_shared, down, down_shared, cut, quarter, share
+        ),
+        lambda *ready: load_both(after(place, *ready), up, up_shared, down, down_shared, 0, cut, share),
     )
     loaded = ()
     for phase, load in zip(GATHER, loads):
@@ -438,12 +447,15 @@
             got, weights = lax.optimization_barrier((got, weights))
         loaded += weights
         own = [stack(part, add) for part, add in zip(own, got)]
-    gate, up, second = loaded
+    gate, third, up, second = loaded
     odd = place[0] % 2
     own = [jnp.where(odd == i, part, regroup(part, 4, 2)) for i, part in enumerate(own)]
     other = [flipped(part, CORE, CORE) for part in own]
 
-    outs = pair_rows(place, own, other, gate, up, second, down, down_shared, share)
+    fourth = load_down(after(place, *own), down, down_shared, cut + quarter, quarter, share)
+    other[1], fourth = lax.optimization_barrier((other[1], fourth))
+
+    outs = pair_rows(place, own, other, gate, up, second, third, fourth, share)
 
     totals = [[own, flipped(other, CORE, CORE)] for own, other in zip(outs[:2], outs[2:])]
     for phase in SCATTER:

time: 57.6 us -> 54.9 us (0.953)
  waiting for transfers between devices: 14 us -> 12.1 us
  Pallas kernels: 18.1 us -> 17.3 us
    ppermute x16, waiting for transfers between devices: 14 us -> 12.1 us  [flipped(): return lax.ppermute(value, ('node', 'local'), pairs)]
    pallas_call x1, Pallas kernels: 4.07 us -> 2.55 us  [pair_rows(): pl.pallas_call(functools.partial(early_half_kernel, share), in_specs=[SME...]
    pallas_call x3 -> x4, Pallas kernels: 12.1 us -> 12.8 us  [the longest x2 9.49 us: load_both(): pl.pallas_call(functools.partial(load_both_kernel, share, lower), in_spec...]
  transfers between devices with their start and end apart: 16 -> 16, of which waited for: 8 -> 7; matrix products, arithmetic and copies ran while one was open for 1% -> 1% of each run, Pallas kernels for 23% -> 25%
where the time goes in v17:
time: 54.9 us; the launch traced here: 54.7 us
  starting transfers between devices  23.6 us (43%)
  Pallas kernels  17.3 us (32%)
  waiting for transfers between devices  12.1 us (22%)
  other arithmetic  1.33 us (2%)
    ppermute x16, starting transfers between devices, flipped(): return lax.ppermute(value, ('node', 'local'), pairs)  23.6 us
    ppermute x16, waiting for transfers between devices, flipped(): return lax.ppermute(value, ('node', 'local'), pairs)  12.1 us
    pallas_call x2, Pallas kernels, load_both(): pl.pallas_call(functools.partial(load_both_kernel, share, lower), in_spec...  9.49 us
    pallas_call x1, Pallas kernels, pair_rows(): pl.pallas_call(functools.partial(early_half_kernel, share), in_specs=[SME...  2.55 us
    pallas_call x1, Pallas kernels, pair_rows(): pl.pallas_call(late_half_kernel, in_specs=[SMEM_SPEC] + [VMEM_SPEC] * 4,...  1.66 us
    pallas_call x1, Pallas kernels, load_down(): pl.pallas_call(functools.partial(load_down_kernel, share, lower), in_spec...  1.62 us
  transfers between devices with their start and end apart: 16, of which 7 were waited for; matrix products, arithmetic and copies ran while one was open for 1% of the time, Pallas kernels for 25%

profile of v17, /device:TPU:0, one launch (start us, length us, event | category | flops | bytes accessed | tf_op | source)
XLA Modules:
  0.0 54.7 jit_solution(9962680920918830255)
XLA Ops:
  0.0 1.1 %pack_rows.1 = bf16[8,7296]{1,0:T(8,128)(2,1)S(1)} custom-call(bf16[8,7168]{1,0:T(8,128)(2,1)} %tokens_ref.1, s32[4,8]{1,0:T(4,128)} %bitcast.11, bf16[4,8]{1,0:T(4,128)(2,1)} %bitcast.12), custom_call_target="tpu_custom_call" | custom-call | tf_op jit(solution)/shard_map/pack_rows/pallas_call | solution.py:48
  1.1 3.0 %collective-permute-start.2 = (bf16[8,3712]{1,0:T(8,128)(2,1)S(1)}, bf16[8,3712]{1,0:T(8,128)(2,1)S(1)}, u32[]{:S(2)}, u32[]{:S(2)}) collective-permute-start(bf16[8,3712]{1,0:T(8,128)(2,1)S(1)} %get-tuple-element.64), channel_id=1, source_target_pairs={{0,8},{1,9},{2,10},{3,11},{4,6},{5,7},{6,4},{7,5},{8,0},{9,1},{10,... | collective-permute-start | bytes 178184 | tf_op jit(solution)/shard_map/ppermute | solution.py:394
  4.1 2.7 %collective-permute-start = (bf16[8,3584]{1,0:T(8,128)(2,1)S(1)}, bf16[8,3584]{1,0:T(8,128)(2,1)S(1)}, u32[]{:S(2)}, u32[]{:S(2)}) collective-permute-start(bf16[8,3584]{1,0:T(8,128)(2,1)S(1)} %get-tuple-element.65), channel_id=1, source_target_pairs={{0,2},{1,3},{2,0},{3,1},{4,12},{5,13},{6,14},{7,15},{8,10},{9,11},... | collective-permute-start | bytes 172040 | tf_op jit(solution)/shard_map/ppermute | solution.py:394
  6.8 0.0 collective-permute-done.2
  6.8 2.7 %collective-permute-start.3 = (bf16[16,3712]{1,0:T(8,128)(2,1)S(1)}, bf16[16,3712]{1,0:T(8,128)(2,1)S(1)}, u32[]{:S(2)}, u32[]{:S(2)}) collective-permute-start(bf16[16,3712]{1,0:T(8,128)(2,1)S(1)} %pad_maximum_fusion.2), channel_id=1, source_target_pairs={{0,2},{1,3},{2,0},{3,1},{4,5},{5,4},{6,7},{7,6},{8,10},{9,11},{10,... | collective-permute-start | bytes 356360 | tf_op jit(solution)/shard_map/ppermute | solution.py:394
  9.5 0.0 collective-permute-done
  9.5 1.6 %collective-permute-start.1 = (bf16[16,3584]{1,0:T(8,128)(2,1)S(1)}, bf16[16,3584]{1,0:T(8,128)(2,1)S(1)}, u32[]{:S(2)}, u32[]{:S(2)}) collective-permute-start(bf16[16,3584]{1,0:T(8,128)(2,1)S(1)} %pad_maximum_fusion.3), channel_id=1, source_target_pairs={{0,1},{1,0},{2,3},{3,2},{4,6},{5,7},{6,4},{7,5},{8,9},{9,8},{10,11... | collective-permute-start | bytes 344072 | tf_op jit(solution)/shard_map/ppermute | solution.py:394
  11.1 4.4 %load_both.2 = (bf16[7168,640]{1,0:T(8,128)(2,1)S(1)}, bf16[640,1792]{1,0:T(8,128)(2,1)S(1)}) custom-call(s32[1]{0:T(128)} %bitcast.place_ref, bf16[7168,512]{1,0:T(8,128)(2,1)} %bitcast.9, bf16[7168,512]{1,0:T(8,128)(2,1)} %shared_ref.2, bf16[512,7168]{1,0:T(8,128)(2,1)} %bitcast.6, bf16[512,7168]{1,0:T(8,128)(2,1)} %sdown_ref.5), custom_call_target="tpu_custom_call" | custom-call | bytes 22937600 | tf_op jit(solution)/shard_map/load_both/pallas_call | solution.py:223
  15.5 0.0 collective-permute-done.1
  15.6 0.4 collective-permute-done.3
  15.9 1.6 %collective-permute-start.4 = (bf16[32,3584]{1,0:T(8,128)(2,1)S(1)}, bf16[32,3584]{1,0:T(8,128)(2,1)S(1)}, u32[]{:S(2)}, u32[]{:S(2)}) collective-permute-start(bf16[32,3584]{1,0:T(8,128)(2,1)S(1)} %pad_maximum_fusion.1), channel_id=1, source_target_pairs={{0,8},{1,9},{2,10},{3,11},{4,5},{5,4},{6,7},{7,6},{8,0},{9,1},{10,... | collective-permute-start | bytes 688136 | tf_op jit(solution)/shard_map/ppermute | solution.py:394
  17.6 0.9 %collective-permute-start.5 = (bf16[32,3712]{1,0:T(8,128)(2,1)S(1)}, bf16[32,3712]{1,0:T(8,128)(2,1)S(1)}, u32[]{:S(2)}, u32[]{:S(2)}) collective-permute-start(bf16[32,3712]{1,0:T(8,128)(2,1)S(1)} %pad_maximum_fusion), channel_id=1, source_target_pairs={{0,1},{1,0},{2,3},{3,2},{4,12},{5,13},{6,14},{7,15},{8,9},{9,8},{1... | collective-permute-start | bytes 712712 | tf_op jit(solution)/shard_map/ppermute | solution.py:394
  18.5 5.1 %load_both.3 = (bf16[7168,640]{1,0:T(8,128)(2,1)S(1)}, bf16[640,3584]{1,0:T(8,128)(2,1)S(1)}) custom-call(s32[1]{0:T(128)} %bitcast.place_ref, bf16[7168,512]{1,0:T(8,128)(2,1)} %bitcast.10, bf16[7168,512]{1,0:T(8,128)(2,1)} %shared_ref.3, bf16[512,7168]{1,0:T(8,128)(2,1)} %bitcast.7, bf16[512,7168]{1,0:T(8,128)(2,1)} %sdown_ref.5), custom_call_target="tpu_custom_call" | custom-call | bytes 27525120 | tf_op jit(solution)/shard_map/load_both/pallas_call | solution.py:223
  23.6 0.3 collective-permute-done.4
  23.9 0.0 collective-permute-done.5
  24.1 0.1 maximum_select_fusion.own_ref
  24.2 0.1 collective-permute-start.7
  24.3 0.1 maximum_select_fusion.1.own_ref
  24.4 0.6 %collective-permute-start.6 = (bf16[64,3584]{1,0:T(8,128)(2,1)S(1)}, bf16[64,3584]{1,0:T(8,128)(2,1)S(1)}, u32[]{:S(2)}, u32[]{:S(2)}) collective-permute-start(bf16[64,3584]{1,0:T(8,128)(2,1)S(1)} %maximum_select_fusion.1.own_ref), channel_id=1, source_target_pairs={{0,4},{1,5},{2,6},{3,7},{4,0},{5,1},{6,2},{7,3},{8,12},{9,13},{10,... | collective-permute-start | bytes 1376264 | tf_op jit(solution)/shard_map/ppermute | solution.py:394
  25.0 1.6 %load_down.1.fourth_ref = bf16[640,1792]{1,0:T(8,128)(2,1)S(1)} custom-call(s32[1]{0:T(128)} %bitcast.place_ref, bf16[512,7168]{1,0:T(8,128)(2,1)} %bitcast.8, bf16[512,7168]{1,0:T(8,128)(2,1)} %sdown_ref.5), custom_call_target="tpu_custom_call" | custom-call | bytes 4587520 | tf_op jit(solution)/shard_map/load_down/pallas_call | solution.py:243
  26.6 0.0 collective-permute-done.7.other_ref
  26.6 1.7 %late_half.1 = (f32[128,640]{1,0:T(8,128)S(1)}, f32[128,640]{1,0:T(8,128)S(1)}, f32[128,128]{1,0:T(8,128)S(1)}) custom-call(s32[1]{0:T(128)} %bitcast.place_ref, bf16[64,3712]{1,0:T(8,128)(2,1)S(1)} %maximum_select_fusion.own_ref, bf16[64,3712]{1,0:T(8,128)(2,1)S(1)} %collective-permute-done.7.other_ref, bf16[7168,640]{1,0:T(8,128)(2,1)S(1)} %get-tuple-element.39.gate_ref, ...), custom_call_target="tpu_custom_call" | custom-call | flops 1174405120 | bytes 9175040 | tf_op jit(solution)/shard_map/late_half/pallas_call | solution.py:314
  28.3 0.0 collective-permute-done.6.other_ref
  28.3 2.5 %early_half.1 = (bf16[64,3584]{1,0:T(8,128)(2,1)S(1)}, bf16[64,3584]{1,0:T(8,128)(2,1)S(1)}, bf16[128,640]{1,0:T(8,128)(2,1)S(1)}) custom-call(s32[1]{0:T(128)} %bitcast.place_ref, bf16[64,3584]{1,0:T(8,128)(2,1)S(1)} %maximum_select_fusion.1.own_ref, bf16[64,3584]{1,0:T(8,128)(2,1)S(1)} %collective-permute-done.6.other_ref, ...), custom_call_target="tpu_custom_call" | custom-call | flops 1761607680 | bytes 13762560 | tf_op jit(solution)/shard_map/early_half/pallas_call | solution.py:324
  30.9 0.1 collective-permute-start.8
  31.0 0.9 %last_half.1 = (bf16[64,3584]{1,0:T(8,128)(2,1)S(1)}, bf16[64,3584]{1,0:T(8,128)(2,1)S(1)}) custom-call(bf16[128,640]{1,0:T(8,128)(2,1)S(1)} %get-tuple-element.50.act_ref, bf16[640,1792]{1,0:T(8,128)(2,1)S(1)} %get-tuple-element.51.third_ref, bf16[640,1792]{1,0:T(8,128)(2,1)S(1)} %load_down.1.fourth_ref), custom_call_target="tpu_custom_call" | custom-call | flops 587202560 | bytes 4587520 | tf_op jit(solution)/shard_map/last_half/pallas_call | solution.py:338
  31.9 0.6 %collective-permute-start.12 = (bf16[64,3584]{1,0:T(8,128)(2,1)S(1)}, bf16[64,3584]{1,0:T(8,128)(2,1)S(1)}, u32[]{:S(2)}, u32[]{:S(2)}) collective-permute-start(bf16[64,3584]{1,0:T(8,128)(2,1)S(1)} %get-tuple-element.54), channel_id=1, source_target_pairs={{0,4},{1,5},{2,6},{3,7},{4,0},{5,1},{6,2},{7,3},{8,12},{9,13},{10,... | collective-permute-start | bytes 1376264 | tf_op jit(solution)/shard_map/ppermute | solution.py:394
  32.4 0.3 collective-permute-done.8
  32.8 0.1 add_convert_fusion.1
  32.9 1.6 %collective-permute-start.9 = (bf16[32,3584]{1,0:T(8,128)(2,1)S(1)}, bf16[32,3584]{1,0:T(8,128)(2,1)S(1)}, u32[]{:S(2)}, u32[]{:S(2)}) collective-permute-start(bf16[32,3584]{1,0:T(8,128)(2,1)S(1)} %get-tuple-element.55), channel_id=1, source_target_pairs={{0,8},{1,9},{2,10},{3,11},{4,12},{5,13},{6,14},{7,15},{8,0},{9,1},... | collective-permute-start | bytes 688136 | tf_op jit(solution)/shard_map/ppermute | solution.py:394
  34.5 0.0 collective-permute-done.12
  34.5 0.1 add_convert_fusion
  34.6 1.3 %collective-permute-start.13 = (bf16[32,3584]{1,0:T(8,128)(2,1)S(1)}, bf16[32,3584]{1,0:T(8,128)(2,1)S(1)}, u32[]{:S(2)}, u32[]{:S(2)}) collective-permute-start(bf16[32,3584]{1,0:T(8,128)(2,1)S(1)} %get-tuple-element.57), channel_id=1, source_target_pairs={{0,1},{1,0},{2,3},{3,2},{4,5},{5,4},{6,7},{7,6},{8,9},{9,8},{10,11... | collective-permute-start | bytes 688136 | tf_op jit(solution)/shard_map/ppermute | solution.py:394
  35.8 4.7 %collective-permute-done.9 = bf16[32,3584]{1,0:T(8,128)(2,1)S(1)} collective-permute-done((bf16[32,3584]{1,0:T(8,128)(2,1)S(1)}, bf16[32,3584]{1,0:T(8,128)(2,1)S(1)}, u32[]{:S(2)}, u32[]{:S(2)}) %collective-permute-start.9) | collective-permute-done | bytes 229408 | tf_op jit(solution)/shard_map/ppermute | solution.py:394
  40.6 0.1 fusion.1
  40.6 1.3 %collective-permute-start.10 = (bf16[16,3584]{1,0:T(8,128)(2,1)S(1)}, bf16[16,3584]{1,0:T(8,128)(2,1)S(1)}, u32[]{:S(2)}, u32[]{:S(2)}) collective-permute-start(bf16[16,3584]{1,0:T(8,128)(2,1)S(1)} %get-tuple-element.59), channel_id=1, source_target_pairs={{0,1},{1,0},{2,3},{3,2},{4,5},{5,4},{6,7},{7,6},{8,9},{9,8},{10,11... | collective-permute-start | bytes 344072 | tf_op jit(solution)/shard_map/ppermute | solution.py:394
  42.0 0.0 collective-permute-done.13
  42.0 0.1 fusion
  42.0 1.5 %collective-permute-start.14 = (bf16[16,3584]{1,0:T(8,128)(2,1)S(1)}, bf16[16,3584]{1,0:T(8,128)(2,1)S(1)}, u32[]{:S(2)}, u32[]{:S(2)}) collective-permute-start(bf16[16,3584]{1,0:T(8,128)(2,1)S(1)} %get-tuple-element.61), channel_id=1, source_target_pairs={{0,8},{1,9},{2,10},{3,11},{4,12},{5,13},{6,14},{7,15},{8,0},{9,1},... | collective-permute-start | bytes 344072 | tf_op jit(solution)/shard_map/ppermute | solution.py:394
  43.6 1.9 %collective-permute-done.10 = bf16[16,3584]{1,0:T(8,128)(2,1)S(1)} collective-permute-done((bf16[16,3584]{1,0:T(8,128)(2,1)S(1)}, bf16[16,3584]{1,0:T(8,128)(2,1)S(1)}, u32[]{:S(2)}, u32[]{:S(2)}) %collective-permute-start.10) | collective-permute-done | bytes 114720 | tf_op jit(solution)/shard_map/ppermute | solution.py:394
  45.5 2.8 %collective-permute-start.11 = (bf16[8,3584]{1,0:T(8,128)(2,1)S(1)}, bf16[8,3584]{1,0:T(8,128)(2,1)S(1)}, u32[]{:S(2)}, u32[]{:S(2)}) collective-permute-start(bf16[8,3584]{1,0:T(8,128)(2,1)S(1)} %fusion.5), channel_id=1, source_target_pairs={{0,2},{1,3},{2,0},{3,1},{4,6},{5,7},{6,4},{7,5},{8,10},{9,11},{10,... | collective-permute-start | bytes 172040 | tf_op jit(solution)/shard_map/ppermute | solution.py:394
  48.3 0.0 collective-permute-done.14
  48.3 1.3 %collective-permute-start.15 = (bf16[8,3584]{1,0:T(8,128)(2,1)S(1)}, bf16[8,3584]{1,0:T(8,128)(2,1)S(1)}, u32[]{:S(2)}, u32[]{:S(2)}) collective-permute-start(bf16[8,3584]{1,0:T(8,128)(2,1)S(1)} %fusion.2), channel_id=1, source_target_pairs={{0,2},{1,3},{2,0},{3,1},{4,6},{5,7},{6,4},{7,5},{8,10},{9,11},{10,... | collective-permute-start | bytes 172040 | tf_op jit(solution)/shard_map/ppermute | solution.py:394
  49.6 2.6 %collective-permute-done.11 = bf16[8,3584]{1,0:T(8,128)(2,1)S(1)} collective-permute-done((bf16[8,3584]{1,0:T(8,128)(2,1)S(1)}, bf16[8,3584]{1,0:T(8,128)(2,1)S(1)}, u32[]{:S(2)}, u32[]{:S(2)}) %collective-permute-start.11) | collective-permute-done | bytes 57376 | tf_op jit(solution)/shard_map/ppermute | solution.py:394
  52.2 1.8 %collective-permute-done.15 = bf16[8,3584]{1,0:T(8,128)(2,1)S(1)} collective-permute-done((bf16[8,3584]{1,0:T(8,128)(2,1)S(1)}, bf16[8,3584]{1,0:T(8,128)(2,1)S(1)}, u32[]{:S(2)}, u32[]{:S(2)}) %collective-permute-start.15) | collective-permute-done | bytes 57376 | tf_op jit(solution)/shard_map/ppermute | solution.py:394
  54.1 0.7 %pad_maximum_fusion.4 = bf16[8,7168]{1,0:T(8,128)(2,1)} fusion(bf16[8,3584]{1,0:T(8,128)(2,1)S(1)} %fusion.4, bf16[8,3584]{1,0:T(8,128)(2,1)S(1)} %fusion.7), kind=kLoop, calls=%fused_computation.26 | loop fusion | flops 229376 | bytes 229376 | tf_op jit(solution)/shard_map/concatenate | solution.py:467
  (24 shorter events, 0.3 us)
Async XLA Ops:
  1.1 5.7 %collective-permute-start.2 = (bf16[8,3712]{1,0:T(8,128)(2,1)S(1)}, bf16[8,3712]{1,0:T(8,128)(2,1)S(1)}, u32[]{:S(2)}, u32[]{:S(2)}) collective-permute-start(bf16[8,3712]{1,0:T(8,128)(2,1)S(1)} %get-tuple-element.64), channel_id=1, source_target_pairs={{0,8},{1,9},{2,10},{3,11},{4,6},{5,7},{6,4},{7,5},{8,0},{9,1},{10,... | collective-permute-start | bytes 178184 | tf_op jit(solution)/shard_map/ppermute | solution.py:394
  4.1 5.4 %collective-permute-start = (bf16[8,3584]{1,0:T(8,128)(2,1)S(1)}, bf16[8,3584]{1,0:T(8,128)(2,1)S(1)}, u32[]{:S(2)}, u32[]{:S(2)}) collective-permute-start(bf16[8,3584]{1,0:T(8,128)(2,1)S(1)} %get-tuple-element.65), channel_id=1, source_target_pairs={{0,2},{1,3},{2,0},{3,1},{4,12},{5,13},{6,14},{7,15},{8,10},{9,11},... | collective-permute-start | bytes 172040 | tf_op jit(solution)/shard_map/ppermute | solution.py:394
  6.8 9.1 %collective-permute-start.3 = (bf16[16,3712]{1,0:T(8,128)(2,1)S(1)}, bf16[16,3712]{1,0:T(8,128)(2,1)S(1)}, u32[]{:S(2)}, u32[]{:S(2)}) collective-permute-start(bf16[16,3712]{1,0:T(8,128)(2,1)S(1)} %pad_maximum_fusion.2), channel_id=1, source_target_pairs={{0,2},{1,3},{2,0},{3,1},{4,5},{5,4},{6,7},{7,6},{8,10},{9,11},{10,... | collective-permute-start | bytes 356360 | tf_op jit(solution)/shard_map/ppermute | solution.py:394
  9.5 6.1 %collective-permute-start.1 = (bf16[16,3584]{1,0:T(8,128)(2,1)S(1)}, bf16[16,3584]{1,0:T(8,128)(2,1)S(1)}, u32[]{:S(2)}, u32[]{:S(2)}) collective-permute-start(bf16[16,3584]{1,0:T(8,128)(2,1)S(1)} %pad_maximum_fusion.3), channel_id=1, source_target_pairs={{0,1},{1,0},{2,3},{3,2},{4,6},{5,7},{6,4},{7,5},{8,9},{9,8},{10,11... | collective-permute-start | bytes 344072 | tf_op jit(solution)/shard_map/ppermute | solution.py:394
  15.9 8.0 %collective-permute-start.4 = (bf16[32,3584]{1,0:T(8,128)(2,1)S(1)}, bf16[32,3584]{1,0:T(8,128)(2,1)S(1)}, u32[]{:S(2)}, u32[]{:S(2)}) collective-permute-start(bf16[32,3584]{1,0:T(8,128)(2,1)S(1)} %pad_maximum_fusion.1), channel_id=1, source_target_pairs={{0,8},{1,9},{2,10},{3,11},{4,5},{5,4},{6,7},{7,6},{8,0},{9,1},{10,... | collective-permute-start | bytes 688136 | tf_op jit(solution)/shard_map/ppermute | solution.py:394
  17.6 6.3 %collective-permute-start.5 = (bf16[32,3712]{1,0:T(8,128)(2,1)S(1)}, bf16[32,3712]{1,0:T(8,128)(2,1)S(1)}, u32[]{:S(2)}, u32[]{:S(2)}) collective-permute-start(bf16[32,3712]{1,0:T(8,128)(2,1)S(1)} %pad_maximum_fusion), channel_id=1, source_target_pairs={{0,1},{1,0},{2,3},{3,2},{4,12},{5,13},{6,14},{7,15},{8,9},{9,8},{1... | collective-permute-start | bytes 712712 | tf_op jit(solution)/shard_map/ppermute | solution.py:394
  24.2 2.4 %collective-permute-start.7 = (bf16[64,3712]{1,0:T(8,128)(2,1)S(1)}, bf16[64,3712]{1,0:T(8,128)(2,1)S(1)}, u32[]{:S(2)}, u32[]{:S(2)}) collective-permute-start(bf16[64,3712]{1,0:T(8,128)(2,1)S(1)} %maximum_select_fusion.own_ref), channel_id=1, source_target_pairs={{0,4},{1,5},{2,6},{3,7},{4,0},{5,1},{6,2},{7,3},{8,12},{9,13},{10,... | collective-permute-start | bytes 1425416 | tf_op jit(solution)/shard_map/ppermute | solution.py:394
  24.4 3.9 %collective-permute-start.6 = (bf16[64,3584]{1,0:T(8,128)(2,1)S(1)}, bf16[64,3584]{1,0:T(8,128)(2,1)S(1)}, u32[]{:S(2)}, u32[]{:S(2)}) collective-permute-start(bf16[64,3584]{1,0:T(8,128)(2,1)S(1)} %maximum_select_fusion.1.own_ref), channel_id=1, source_target_pairs={{0,4},{1,5},{2,6},{3,7},{4,0},{5,1},{6,2},{7,3},{8,12},{9,13},{10,... | collective-permute-start | bytes 1376264 | tf_op jit(solution)/shard_map/ppermute | solution.py:394
  30.9 1.9 %collective-permute-start.8 = (bf16[64,3584]{1,0:T(8,128)(2,1)S(1)}, bf16[64,3584]{1,0:T(8,128)(2,1)S(1)}, u32[]{:S(2)}, u32[]{:S(2)}) collective-permute-start(bf16[64,3584]{1,0:T(8,128)(2,1)S(1)} %get-tuple-element.49), channel_id=1, source_target_pairs={{0,4},{1,5},{2,6},{3,7},{4,0},{5,1},{6,2},{7,3},{8,12},{9,13},{10,... | collective-permute-start | bytes 1376264 | tf_op jit(solution)/shard_map/ppermute | solution.py:394
  31.9 2.6 %collective-permute-start.12 = (bf16[64,3584]{1,0:T(8,128)(2,1)S(1)}, bf16[64,3584]{1,0:T(8,128)(2,1)S(1)}, u32[]{:S(2)}, u32[]{:S(2)}) collective-permute-start(bf16[64,3584]{1,0:T(8,128)(2,1)S(1)} %get-tuple-element.54), channel_id=1, source_target_pairs={{0,4},{1,5},{2,6},{3,7},{4,0},{5,1},{6,2},{7,3},{8,12},{9,13},{10,... | collective-permute-start | bytes 1376264 | tf_op jit(solution)/shard_map/ppermute | solution.py:394
  32.9 7.7 %collective-permute-start.9 = (bf16[32,3584]{1,0:T(8,128)(2,1)S(1)}, bf16[32,3584]{1,0:T(8,128)(2,1)S(1)}, u32[]{:S(2)}, u32[]{:S(2)}) collective-permute-start(bf16[32,3584]{1,0:T(8,128)(2,1)S(1)} %get-tuple-element.55), channel_id=1, source_target_pairs={{0,8},{1,9},{2,10},{3,11},{4,12},{5,13},{6,14},{7,15},{8,0},{9,1},... | collective-permute-start | bytes 688136 | tf_op jit(solution)/shard_map/ppermute | solution.py:394
  34.6 7.4 %collective-permute-start.13 = (bf16[32,3584]{1,0:T(8,128)(2,1)S(1)}, bf16[32,3584]{1,0:T(8,128)(2,1)S(1)}, u32[]{:S(2)}, u32[]{:S(2)}) collective-permute-start(bf16[32,3584]{1,0:T(8,128)(2,1)S(1)} %get-tuple-element.57), channel_id=1, source_target_pairs={{0,1},{1,0},{2,3},{3,2},{4,5},{5,4},{6,7},{7,6},{8,9},{9,8},{10,11... | collective-permute-start | bytes 688136 | tf_op jit(solution)/shard_map/ppermute | solution.py:394
  40.6 4.9 %collective-permute-start.10 = (bf16[16,3584]{1,0:T(8,128)(2,1)S(1)}, bf16[16,3584]{1,0:T(8,128)(2,1)S(1)}, u32[]{:S(2)}, u32[]{:S(2)}) collective-permute-start(bf16[16,3584]{1,0:T(8,128)(2,1)S(1)} %get-tuple-element.59), channel_id=1, source_target_pairs={{0,1},{1,0},{2,3},{3,2},{4,5},{5,4},{6,7},{7,6},{8,9},{9,8},{10,11... | collective-permute-start | bytes 344072 | tf_op jit(solution)/shard_map/ppermute | solution.py:394
  42.0 6.2 %collective-permute-start.14 = (bf16[16,3584]{1,0:T(8,128)(2,1)S(1)}, bf16[16,3584]{1,0:T(8,128)(2,1)S(1)}, u32[]{:S(2)}, u32[]{:S(2)}) collective-permute-start(bf16[16,3584]{1,0:T(8,128)(2,1)S(1)} %get-tuple-element.61), channel_id=1, source_target_pairs={{0,8},{1,9},{2,10},{3,11},{4,12},{5,13},{6,14},{7,15},{8,0},{9,1},... | collective-permute-start | bytes 344072 | tf_op jit(solution)/shard_map/ppermute | solution.py:394
  45.5 6.7 %collective-permute-start.11 = (bf16[8,3584]{1,0:T(8,128)(2,1)S(1)}, bf16[8,3584]{1,0:T(8,128)(2,1)S(1)}, u32[]{:S(2)}, u32[]{:S(2)}) collective-permute-start(bf16[8,3584]{1,0:T(8,128)(2,1)S(1)} %fusion.5), channel_id=1, source_target_pairs={{0,2},{1,3},{2,0},{3,1},{4,6},{5,7},{6,4},{7,5},{8,10},{9,11},{10,... | collective-permute-start | bytes 172040 | tf_op jit(solution)/shard_map/ppermute | solution.py:394
  48.3 5.8 %collective-permute-start.15 = (bf16[8,3584]{1,0:T(8,128)(2,1)S(1)}, bf16[8,3584]{1,0:T(8,128)(2,1)S(1)}, u32[]{:S(2)}, u32[]{:S(2)}) collective-permute-start(bf16[8,3584]{1,0:T(8,128)(2,1)S(1)} %fusion.2), channel_id=1, source_target_pairs={{0,2},{1,3},{2,0},{3,1},{4,6},{5,7},{6,4},{7,5},{8,10},{9,11},{10,... | collective-permute-start | bytes 172040 | tf_op jit(solution)/shard_map/ppermute | solution.py:394

commit v18 on v17

--- a/solution.py
+++ b/solution.py
@@ -292,12 +292,12 @@
         other_out_ref[:, at] = total[half:]
 
 
-def last_half_kernel(act_ref, third_ref, fourth_ref, own_out_ref, other_out_ref):
+def last_half_kernel(act_ref, later_ref, own_out_ref, other_out_ref):
     half, columns = own_out_ref.shape
     piece = columns // 2
-    for i, later_ref in enumerate((third_ref, fourth_ref)):
+    for i in range(2):
         at = slice(i * piece, (i + 1) * piece)
-        total = jnp.dot(act_ref[...], later_ref[...], preferred_element_type=F32).astype(BF16)
+        total = jnp.dot(act_ref[...], later_ref[:, at], preferred_element_type=F32).astype(BF16)
         own_out_ref[:, at] = swap_quarters(total[:half])
         other_out_ref[:, at] = swap_quarters(total[half:])
 
@@ -308,7 +308,7 @@
     )
 
 
-def pair_rows(place, own, other, gate, up, second, third, fourth, share):
+def pair_rows(place, own, other, gate, up, second, later, share):
     half, cut = own[0].shape
     width, units = gate.shape
     partial = pl.pallas_call(
@@ -337,13 +337,13 @@
     )(place, own[0], other[0], gate, up, *partial, second)
     last = pl.pallas_call(
         last_half_kernel,
-        in_specs=[VMEM_SPEC] * 3,
+        in_specs=[VMEM_SPEC] * 2,
         out_specs=[VMEM_SPEC] * 2,
         out_shape=[pltpu.VMEM((half, width - cut), BF16)] * 2,
         cost_estimate=estimate(2 * half, width - cut, units),
         compiler_params=pltpu.CompilerParams(vmem_limit_bytes=10 << 20),
         name="last_half",
-    )(act, third, fourth)
+    )(act, later)
     return own_out, last[0], other_out, last[1]
 
 
@@ -431,31 +431,28 @@
 
     cut = width // 2
     own = [packed[:, :cut], packed[:, cut:]]
-    quarter = (width - cut) // 2
     loads = (
-        lambda *ready: (),
-        lambda *ready: load_both(
-            after(place, *ready), gate, gate_shared, down, down_shared, cut, quarter, share
-        ),
+        lambda *ready: (load_down(after(place, *ready), down, down_shared, cut, width - cut, share),),
+        lambda *ready: (load_weights(after(place, *ready), gate, gate_shared, share),),
         lambda *ready: load_both(after(place, *ready), up, up_shared, down, down_shared, 0, cut, share),
     )
     loaded = ()
-    for phase, load in zip(GATHER, loads):
-        got = [flipped(part, *pairs) for part, pairs in zip(own, (phase, phase[::-1]))]
+    for number, (phase, load) in enumerate(zip(GATHER, loads)):
+        got = [flipped(part, *pairs) for part, pairs in zip(own, (phase[::-1], phase))]
         weights = tuple(load(*own))
-        if weights:
+        if number == 0:
+            got[1], weights = lax.optimization_barrier((got[1], weights))
+        else:
             got, weights = lax.optimization_barrier((got, weights))
         loaded += weights
         own = [stack(part, add) for part, add in zip(own, got)]
-    gate, third, up, second = loaded
+    later, gate, up, second = loaded
     odd = place[0] % 2
-    own = [jnp.where(odd == i, part, regroup(part, 4, 2)) for i, part in enumerate(own)]
+    own = [jnp.where(odd == 1 - i, part, regroup(part, 4, 2)) for i, part in enumerate(own)]
     other = [flipped(part, CORE, CORE) for part in own]
 
-    fourth = load_down(after(place, *own), down, down_shared, cut + quarter, quarter, share)
-    other[1], fourth = lax.optimization_barrier((other[1], fourth))
-
-    outs = pair_rows(place, own, other, gate, up, second, third, fourth, share)
+
+    outs = pair_rows(place, own, other, gate, up, second, later, share)
 
     totals = [[own, flipped(other, CORE, CORE)] for own, other in zip(outs[:2], outs[2:])]
     for phase in SCATTER:

time: 54.9 us -> 55.5 us (1.011)
  starting transfers between devices: 23.6 us -> 20.1 us
  local copies, waits for them, and re-layouts: 0.15 us -> 2.25 us
  waiting for transfers between devices: 12.1 us -> 14.1 us
    pallas_call x2 -> x1, Pallas kernels: 9.49 us -> 5.08 us  [load_both(): pl.pallas_call(functools.partial(load_both_kernel, share, lower), in_spec...]
    pallas_call x1 -> x2, Pallas kernels: 0.91 us -> 4.64 us  [the longest x1 3.69 us: load_weights(): pl.pallas_call(functools.partial(load_kernel, share), in_specs=[SMEM_SPEC...]
    ppermute x16, starting transfers between devices: 23.6 us -> 20.1 us  [flipped(): return lax.ppermute(value, ('node', 'local'), pairs)]
    unnamed x13 -> x19, local copies, waits for them, and re-layouts: 0.12 us -> 2.23 us
    ppermute x16, waiting for transfers between devices: 12.1 us -> 14.1 us  [flipped(): return lax.ppermute(value, ('node', 'local'), pairs)]
    pallas_call x1, Pallas kernels: 1.62 us -> 2.33 us  [load_down(): pl.pallas_call(functools.partial(load_down_kernel, share, lower), in_spec...]
  transfers between devices with their start and end apart: 16 -> 16, of which waited for: 7 -> 8; matrix products, arithmetic and copies ran while one was open for 1% -> 1% of each run, Pallas kernels for 25% -> 25%
where the time goes in v18:
time: 55.5 us; the launch traced here: 55.3 us
  starting transfers between devices  20.1 us (36%)
  Pallas kernels  17.2 us (31%)
  waiting for transfers between devices  14.1 us (25%)
  local copies, waits for them, and re-layouts  2.25 us (4%)
  other arithmetic  1.31 us (2%)
    ppermute x16, starting transfers between devices, flipped(): return lax.ppermute(value, ('node', 'local'), pairs)  20.1 us
    ppermute x16, waiting for transfers between devices, flipped(): return lax.ppermute(value, ('node', 'local'), pairs)  14.1 us
    pallas_call x1, Pallas kernels, load_both(): pl.pallas_call(functools.partial(load_both_kernel, share, lower), in_spec...  5.08 us
    pallas_call x1, Pallas kernels, load_weights(): pl.pallas_call(functools.partial(load_kernel, share), in_specs=[SMEM_SPEC...  3.69 us
    pallas_call x1, Pallas kernels, pair_rows(): pl.pallas_call(functools.partial(early_half_kernel, share), in_specs=[SME...  2.47 us
    pallas_call x1, Pallas kernels, load_down(): pl.pallas_call(functools.partial(load_down_kernel, share, lower), in_spec...  2.33 us
    unnamed x19, local copies, waits for them, and re-layouts  2.23 us
    pallas_call x1, Pallas kernels, pair_rows(): pl.pallas_call(late_half_kernel, in_specs=[SMEM_SPEC] + [VMEM_SPEC] * 4,...  1.66 us
  transfers between devices with their start and end apart: 16, of which 8 were waited for; matrix products, arithmetic and copies ran while one was open for 1% of the time, Pallas kernels for 25%

profile of v18, /device:TPU:0, one launch (start us, length us, event | category | flops | bytes accessed | tf_op | source)
XLA Modules:
  0.0 55.3 jit_solution(13692936846801428809)
XLA Ops:
  0.0 1.1 %pack_rows.1 = bf16[8,7296]{1,0:T(8,128)(2,1)S(1)} custom-call(bf16[8,7168]{1,0:T(8,128)(2,1)} %tokens_ref.1, s32[4,8]{1,0:T(4,128)} %bitcast.12, bf16[4,8]{1,0:T(4,128)(2,1)} %bitcast.13), custom_call_target="tpu_custom_call" | custom-call | tf_op jit(solution)/shard_map/pack_rows/pallas_call | solution.py:48
  1.1 4.1 %collective-permute-start.2 = (bf16[8,3712]{1,0:T(8,128)(2,1)S(1)}, bf16[8,3712]{1,0:T(8,128)(2,1)S(1)}, u32[]{:S(2)}, u32[]{:S(2)}) collective-permute-start(bf16[8,3712]{1,0:T(8,128)(2,1)S(1)} %get-tuple-element.58), channel_id=1, source_target_pairs={{0,2},{1,3},{2,0},{3,1},{4,12},{5,13},{6,14},{7,15},{8,10},{9,11},... | collective-permute-start | bytes 178184 | tf_op jit(solution)/shard_map/ppermute | solution.py:394
  5.2 1.6 %collective-permute-start = (bf16[8,3584]{1,0:T(8,128)(2,1)S(1)}, bf16[8,3584]{1,0:T(8,128)(2,1)S(1)}, u32[]{:S(2)}, u32[]{:S(2)}) collective-permute-start(bf16[8,3584]{1,0:T(8,128)(2,1)S(1)} %get-tuple-element.59), channel_id=1, source_target_pairs={{0,8},{1,9},{2,10},{3,11},{4,6},{5,7},{6,4},{7,5},{8,0},{9,1},{10,... | collective-permute-start | bytes 172040 | tf_op jit(solution)/shard_map/ppermute | solution.py:394
  6.8 2.3 %load_down.1.later_ref = bf16[640,3584]{1,0:T(8,128)(2,1)S(1)} custom-call(s32[1]{0:T(128)} %bitcast.place_ref, bf16[512,7168]{1,0:T(8,128)(2,1)} %bitcast.8, bf16[512,7168]{1,0:T(8,128)(2,1)} %sdown_ref.3), custom_call_target="tpu_custom_call" | custom-call | bytes 9175040 | tf_op jit(solution)/shard_map/load_down/pallas_call | solution.py:243
  9.1 0.0 copy-start
  9.1 2.1 %copy-done = bf16[640,3584]{1,0:T(8,128)(2,1)} copy-done((bf16[640,3584]{1,0:T(8,128)(2,1)}, bf16[640,3584]{1,0:T(8,128)(2,1)S(1)}, u32[]{:S(2)}) %copy-start) | copy-done | bytes 4587544
  11.2 0.0 collective-permute-done.2
  11.2 1.6 %collective-permute-start.3 = (bf16[16,3712]{1,0:T(8,128)(2,1)S(1)}, bf16[16,3712]{1,0:T(8,128)(2,1)S(1)}, u32[]{:S(2)}, u32[]{:S(2)}) collective-permute-start(bf16[16,3712]{1,0:T(8,128)(2,1)S(1)} %pad_maximum_fusion.2), channel_id=1, source_target_pairs={{0,1},{1,0},{2,3},{3,2},{4,6},{5,7},{6,4},{7,5},{8,9},{9,8},{10,11... | collective-permute-start | bytes 356360 | tf_op jit(solution)/shard_map/ppermute | solution.py:394
  12.9 0.0 collective-permute-done
  12.9 0.9 %collective-permute-start.1 = (bf16[16,3584]{1,0:T(8,128)(2,1)S(1)}, bf16[16,3584]{1,0:T(8,128)(2,1)S(1)}, u32[]{:S(2)}, u32[]{:S(2)}) collective-permute-start(bf16[16,3584]{1,0:T(8,128)(2,1)S(1)} %pad_maximum_fusion.3), channel_id=1, source_target_pairs={{0,2},{1,3},{2,0},{3,1},{4,5},{5,4},{6,7},{7,6},{8,10},{9,11},{10,... | collective-permute-start | bytes 344072 | tf_op jit(solution)/shard_map/ppermute | solution.py:394
  13.8 3.7 %load_weights.1.gate_ref = bf16[7168,640]{1,0:T(8,128)(2,1)S(1)} custom-call(s32[1]{0:T(128)} %bitcast.place_ref, bf16[7168,512]{1,0:T(8,128)(2,1)} %bitcast.10, bf16[7168,512]{1,0:T(8,128)(2,1)} %shared_ref.2), custom_call_target="tpu_custom_call" | custom-call | bytes 18350080 | tf_op jit(solution)/shard_map/load_weights/pallas_call | solution.py:80
  17.5 2.5 %collective-permute-done.1 = bf16[16,3584]{1,0:T(8,128)(2,1)S(1)} collective-permute-done((bf16[16,3584]{1,0:T(8,128)(2,1)S(1)}, bf16[16,3584]{1,0:T(8,128)(2,1)S(1)}, u32[]{:S(2)}, u32[]{:S(2)}) %collective-permute-start.1) | collective-permute-done | bytes 114720 | tf_op jit(solution)/shard_map/ppermute | solution.py:394
  19.9 0.0 collective-permute-done.3
  20.0 0.4 collective-permute-start.4
  20.4 0.7 %collective-permute-start.5 = (bf16[32,3712]{1,0:T(8,128)(2,1)S(1)}, bf16[32,3712]{1,0:T(8,128)(2,1)S(1)}, u32[]{:S(2)}, u32[]{:S(2)}) collective-permute-start(bf16[32,3712]{1,0:T(8,128)(2,1)S(1)} %pad_maximum_fusion), channel_id=1, source_target_pairs={{0,8},{1,9},{2,10},{3,11},{4,5},{5,4},{6,7},{7,6},{8,0},{9,1},{10,... | collective-permute-start | bytes 712712 | tf_op jit(solution)/shard_map/ppermute | solution.py:394
  21.1 5.1 %load_both.1 = (bf16[7168,640]{1,0:T(8,128)(2,1)S(1)}, bf16[640,3584]{1,0:T(8,128)(2,1)S(1)}) custom-call(s32[1]{0:T(128)} %bitcast.place_ref, bf16[7168,512]{1,0:T(8,128)(2,1)} %bitcast.11, bf16[7168,512]{1,0:T(8,128)(2,1)} %shared_ref.3, bf16[512,7168]{1,0:T(8,128)(2,1)} %bitcast.9, bf16[512,7168]{1,0:T(8,128)(2,1)} %sdown_ref.3), custom_call_target="tpu_custom_call" | custom-call | bytes 27525120 | tf_op jit(solution)/shard_map/load_both/pallas_call | solution.py:223
  26.1 0.0 collective-permute-done.4
  26.2 0.3 collective-permute-done.5
  26.7 0.1 maximum_select_fusion.own_ref
  26.8 0.1 collective-permute-start.7
  26.9 0.1 maximum_select_fusion.1.own_ref
  27.0 0.6 %collective-permute-start.6 = (bf16[64,3584]{1,0:T(8,128)(2,1)S(1)}, bf16[64,3584]{1,0:T(8,128)(2,1)S(1)}, u32[]{:S(2)}, u32[]{:S(2)}) collective-permute-start(bf16[64,3584]{1,0:T(8,128)(2,1)S(1)} %maximum_select_fusion.1.own_ref), channel_id=1, source_target_pairs={{0,4},{1,5},{2,6},{3,7},{4,0},{5,1},{6,2},{7,3},{8,12},{9,13},{10,... | collective-permute-start | bytes 1376264 | tf_op jit(solution)/shard_map/ppermute | solution.py:394
  27.5 1.1 %collective-permute-done.7.other_ref = bf16[64,3712]{1,0:T(8,128)(2,1)S(1)} collective-permute-done((bf16[64,3712]{1,0:T(8,128)(2,1)S(1)}, bf16[64,3712]{1,0:T(8,128)(2,1)S(1)}, u32[]{:S(2)}, u32[]{:S(2)}) %collective-permute-start.7) | collective-permute-done | bytes 475168 | tf_op jit(solution)/shard_map/ppermute | solution.py:394
  28.7 1.7 %late_half.1 = (f32[128,640]{1,0:T(8,128)S(1)}, f32[128,640]{1,0:T(8,128)S(1)}, f32[128,128]{1,0:T(8,128)S(1)}) custom-call(s32[1]{0:T(128)} %bitcast.place_ref, bf16[64,3712]{1,0:T(8,128)(2,1)S(1)} %maximum_select_fusion.own_ref, bf16[64,3712]{1,0:T(8,128)(2,1)S(1)} %collective-permute-done.7.other_ref, bf16[7168,640]{1,0:T(8,128)(2,1)S(1)} %load_weights.1.gate_ref, ...), custom_call_target="tpu_custom_call" | custom-call | flops 1174405120 | bytes 9175040 | tf_op jit(solution)/shard_map/late_half/pallas_call | solution.py:314
  30.4 0.0 collective-permute-done.6.other_ref
  30.4 0.0 slice-start.1
  30.4 2.5 %early_half.1 = (bf16[64,3584]{1,0:T(8,128)(2,1)S(1)}, bf16[64,3584]{1,0:T(8,128)(2,1)S(1)}, bf16[128,640]{1,0:T(8,128)(2,1)S(1)}) custom-call(s32[1]{0:T(128)} %bitcast.place_ref, bf16[64,3584]{1,0:T(8,128)(2,1)S(1)} %maximum_select_fusion.1.own_ref, bf16[64,3584]{1,0:T(8,128)(2,1)S(1)} %collective-permute-done.6.other_ref, ...), custom_call_target="tpu_custom_call" | custom-call | flops 1761607680 | bytes 13762560 | tf_op jit(solution)/shard_map/early_half/pallas_call | solution.py:324
  32.9 0.2 collective-permute-start.8
  33.1 0.0 slice-done
  33.1 0.9 %last_half.1 = (bf16[64,3584]{1,0:T(8,128)(2,1)S(1)}, bf16[64,3584]{1,0:T(8,128)(2,1)S(1)}) custom-call(bf16[128,640]{1,0:T(8,128)(2,1)S(1)} %get-tuple-element.45.act_ref, bf16[640,3584]{1,0:T(8,128)(2,1)S(1)} %bitcast.7), custom_call_target="tpu_custom_call" | custom-call | flops 587202560 | bytes 4587520 | tf_op jit(solution)/shard_map/last_half/pallas_call | solution.py:338
  34.0 0.4 collective-permute-start.12
  34.5 0.3 collective-permute-done.8
  34.7 0.1 add_convert_fusion.1
  34.8 1.1 %collective-permute-start.9 = (bf16[32,3584]{1,0:T(8,128)(2,1)S(1)}, bf16[32,3584]{1,0:T(8,128)(2,1)S(1)}, u32[]{:S(2)}, u32[]{:S(2)}) collective-permute-start(bf16[32,3584]{1,0:T(8,128)(2,1)S(1)} %get-tuple-element.49), channel_id=1, source_target_pairs={{0,8},{1,9},{2,10},{3,11},{4,12},{5,13},{6,14},{7,15},{8,0},{9,1},... | collective-permute-start | bytes 688136 | tf_op jit(solution)/shard_map/ppermute | solution.py:394
  36.0 0.0 collective-permute-done.12
  36.0 0.1 add_convert_fusion
  36.1 1.8 %collective-permute-start.13 = (bf16[32,3584]{1,0:T(8,128)(2,1)S(1)}, bf16[32,3584]{1,0:T(8,128)(2,1)S(1)}, u32[]{:S(2)}, u32[]{:S(2)}) collective-permute-start(bf16[32,3584]{1,0:T(8,128)(2,1)S(1)} %get-tuple-element.51), channel_id=1, source_target_pairs={{0,1},{1,0},{2,3},{3,2},{4,5},{5,4},{6,7},{7,6},{8,9},{9,8},{10,11... | collective-permute-start | bytes 688136 | tf_op jit(solution)/shard_map/ppermute | solution.py:394
  37.9 4.7 %collective-permute-done.9 = bf16[32,3584]{1,0:T(8,128)(2,1)S(1)} collective-permute-done((bf16[32,3584]{1,0:T(8,128)(2,1)S(1)}, bf16[32,3584]{1,0:T(8,128)(2,1)S(1)}, u32[]{:S(2)}, u32[]{:S(2)}) %collective-permute-start.9) | collective-permute-done | bytes 229408 | tf_op jit(solution)/shard_map/ppermute | solution.py:394
  42.6 1.8 %collective-permute-start.10 = (bf16[16,3584]{1,0:T(8,128)(2,1)S(1)}, bf16[16,3584]{1,0:T(8,128)(2,1)S(1)}, u32[]{:S(2)}, u32[]{:S(2)}) collective-permute-start(bf16[16,3584]{1,0:T(8,128)(2,1)S(1)} %get-tuple-element.53), channel_id=1, source_target_pairs={{0,1},{1,0},{2,3},{3,2},{4,5},{5,4},{6,7},{7,6},{8,9},{9,8},{10,11... | collective-permute-start | bytes 344072 | tf_op jit(solution)/shard_map/ppermute | solution.py:394
  44.4 0.0 collective-permute-done.13
  44.4 1.1 %collective-permute-start.14 = (bf16[16,3584]{1,0:T(8,128)(2,1)S(1)}, bf16[16,3584]{1,0:T(8,128)(2,1)S(1)}, u32[]{:S(2)}, u32[]{:S(2)}) collective-permute-start(bf16[16,3584]{1,0:T(8,128)(2,1)S(1)} %get-tuple-element.55), channel_id=1, source_target_pairs={{0,8},{1,9},{2,10},{3,11},{4,12},{5,13},{6,14},{7,15},{8,0},{9,1},... | collective-permute-start | bytes 344072 | tf_op jit(solution)/shard_map/ppermute | solution.py:394
  45.5 1.9 %collective-permute-done.10 = bf16[16,3584]{1,0:T(8,128)(2,1)S(1)} collective-permute-done((bf16[16,3584]{1,0:T(8,128)(2,1)S(1)}, bf16[16,3584]{1,0:T(8,128)(2,1)S(1)}, u32[]{:S(2)}, u32[]{:S(2)}) %collective-permute-start.10) | collective-permute-done | bytes 114720 | tf_op jit(solution)/shard_map/ppermute | solution.py:394
  47.5 2.0 %collective-permute-start.11 = (bf16[8,3584]{1,0:T(8,128)(2,1)S(1)}, bf16[8,3584]{1,0:T(8,128)(2,1)S(1)}, u32[]{:S(2)}, u32[]{:S(2)}) collective-permute-start(bf16[8,3584]{1,0:T(8,128)(2,1)S(1)} %fusion.5), channel_id=1, source_target_pairs={{0,2},{1,3},{2,0},{3,1},{4,6},{5,7},{6,4},{7,5},{8,10},{9,11},{10,... | collective-permute-start | bytes 172040 | tf_op jit(solution)/shard_map/ppermute | solution.py:394
  49.5 0.0 collective-permute-done.14
  49.5 1.8 %collective-permute-start.15 = (bf16[8,3584]{1,0:T(8,128)(2,1)S(1)}, bf16[8,3584]{1,0:T(8,128)(2,1)S(1)}, u32[]{:S(2)}, u32[]{:S(2)}) collective-permute-start(bf16[8,3584]{1,0:T(8,128)(2,1)S(1)} %fusion.2), channel_id=1, source_target_pairs={{0,2},{1,3},{2,0},{3,1},{4,6},{5,7},{6,4},{7,5},{8,10},{9,11},{10,... | collective-permute-start | bytes 172040 | tf_op jit(solution)/shard_map/ppermute | solution.py:394
  51.3 2.5 %collective-permute-done.11 = bf16[8,3584]{1,0:T(8,128)(2,1)S(1)} collective-permute-done((bf16[8,3584]{1,0:T(8,128)(2,1)S(1)}, bf16[8,3584]{1,0:T(8,128)(2,1)S(1)}, u32[]{:S(2)}, u32[]{:S(2)}) %collective-permute-start.11) | collective-permute-done | bytes 57376 | tf_op jit(solution)/shard_map/ppermute | solution.py:394
  53.9 0.8 %collective-permute-done.15 = bf16[8,3584]{1,0:T(8,128)(2,1)S(1)} collective-permute-done((bf16[8,3584]{1,0:T(8,128)(2,1)S(1)}, bf16[8,3584]{1,0:T(8,128)(2,1)S(1)}, u32[]{:S(2)}, u32[]{:S(2)}) %collective-permute-start.15) | collective-permute-done | bytes 57376 | tf_op jit(solution)/shard_map/ppermute | solution.py:394
  54.7 0.7 %pad_maximum_fusion.4 = bf16[8,7168]{1,0:T(8,128)(2,1)} fusion(bf16[8,3584]{1,0:T(8,128)(2,1)S(1)} %fusion.4, bf16[8,3584]{1,0:T(8,128)(2,1)S(1)} %fusion.7), kind=kLoop, calls=%fused_computation.26 | loop fusion | flops 229376 | bytes 229376 | tf_op jit(solution)/shard_map/concatenate | solution.py:464
  (29 shorter events, 0.4 us)
Async XLA Ops:
  1.1 10.1 %collective-permute-start.2 = (bf16[8,3712]{1,0:T(8,128)(2,1)S(1)}, bf16[8,3712]{1,0:T(8,128)(2,1)S(1)}, u32[]{:S(2)}, u32[]{:S(2)}) collective-permute-start(bf16[8,3712]{1,0:T(8,128)(2,1)S(1)} %get-tuple-element.58), channel_id=1, source_target_pairs={{0,2},{1,3},{2,0},{3,1},{4,12},{5,13},{6,14},{7,15},{8,10},{9,11},... | collective-permute-start | bytes 178184 | tf_op jit(solution)/shard_map/ppermute | solution.py:394
  5.2 7.7 %collective-permute-start = (bf16[8,3584]{1,0:T(8,128)(2,1)S(1)}, bf16[8,3584]{1,0:T(8,128)(2,1)S(1)}, u32[]{:S(2)}, u32[]{:S(2)}) collective-permute-start(bf16[8,3584]{1,0:T(8,128)(2,1)S(1)} %get-tuple-element.59), channel_id=1, source_target_pairs={{0,8},{1,9},{2,10},{3,11},{4,6},{5,7},{6,4},{7,5},{8,0},{9,1},{10,... | collective-permute-start | bytes 172040 | tf_op jit(solution)/shard_map/ppermute | solution.py:394
  9.1 2.1 %copy-start = (bf16[640,3584]{1,0:T(8,128)(2,1)}, bf16[640,3584]{1,0:T(8,128)(2,1)S(1)}, u32[]{:S(2)}) copy-start(bf16[640,3584]{1,0:T(8,128)(2,1)S(1)} %load_down.1.later_ref) | copy-start | bytes 13762564
  11.2 8.7 %collective-permute-start.3 = (bf16[16,3712]{1,0:T(8,128)(2,1)S(1)}, bf16[16,3712]{1,0:T(8,128)(2,1)S(1)}, u32[]{:S(2)}, u32[]{:S(2)}) collective-permute-start(bf16[16,3712]{1,0:T(8,128)(2,1)S(1)} %pad_maximum_fusion.2), channel_id=1, source_target_pairs={{0,1},{1,0},{2,3},{3,2},{4,6},{5,7},{6,4},{7,5},{8,9},{9,8},{10,11... | collective-permute-start | bytes 356360 | tf_op jit(solution)/shard_map/ppermute | solution.py:394
  12.9 7.1 %collective-permute-start.1 = (bf16[16,3584]{1,0:T(8,128)(2,1)S(1)}, bf16[16,3584]{1,0:T(8,128)(2,1)S(1)}, u32[]{:S(2)}, u32[]{:S(2)}) collective-permute-start(bf16[16,3584]{1,0:T(8,128)(2,1)S(1)} %pad_maximum_fusion.3), channel_id=1, source_target_pairs={{0,2},{1,3},{2,0},{3,1},{4,5},{5,4},{6,7},{7,6},{8,10},{9,11},{10,... | collective-permute-start | bytes 344072 | tf_op jit(solution)/shard_map/ppermute | solution.py:394
  20.0 6.1 %collective-permute-start.4 = (bf16[32,3584]{1,0:T(8,128)(2,1)S(1)}, bf16[32,3584]{1,0:T(8,128)(2,1)S(1)}, u32[]{:S(2)}, u32[]{:S(2)}) collective-permute-start(bf16[32,3584]{1,0:T(8,128)(2,1)S(1)} %pad_maximum_fusion.1), channel_id=1, source_target_pairs={{0,1},{1,0},{2,3},{3,2},{4,12},{5,13},{6,14},{7,15},{8,9},{9,8},{1... | collective-permute-start | bytes 688136 | tf_op jit(solution)/shard_map/ppermute | solution.py:394
  20.4 6.1 %collective-permute-start.5 = (bf16[32,3712]{1,0:T(8,128)(2,1)S(1)}, bf16[32,3712]{1,0:T(8,128)(2,1)S(1)}, u32[]{:S(2)}, u32[]{:S(2)}) collective-permute-start(bf16[32,3712]{1,0:T(8,128)(2,1)S(1)} %pad_maximum_fusion), channel_id=1, source_target_pairs={{0,8},{1,9},{2,10},{3,11},{4,5},{5,4},{6,7},{7,6},{8,0},{9,1},{10,... | collective-permute-start | bytes 712712 | tf_op jit(solution)/shard_map/ppermute | solution.py:394
  26.8 1.9 %collective-permute-start.7 = (bf16[64,3712]{1,0:T(8,128)(2,1)S(1)}, bf16[64,3712]{1,0:T(8,128)(2,1)S(1)}, u32[]{:S(2)}, u32[]{:S(2)}) collective-permute-start(bf16[64,3712]{1,0:T(8,128)(2,1)S(1)} %maximum_select_fusion.own_ref), channel_id=1, source_target_pairs={{0,4},{1,5},{2,6},{3,7},{4,0},{5,1},{6,2},{7,3},{8,12},{9,13},{10,... | collective-permute-start | bytes 1425416 | tf_op jit(solution)/shard_map/ppermute | solution.py:394
  27.0 3.4 %collective-permute-start.6 = (bf16[64,3584]{1,0:T(8,128)(2,1)S(1)}, bf16[64,3584]{1,0:T(8,128)(2,1)S(1)}, u32[]{:S(2)}, u32[]{:S(2)}) collective-permute-start(bf16[64,3584]{1,0:T(8,128)(2,1)S(1)} %maximum_select_fusion.1.own_ref), channel_id=1, source_target_pairs={{0,4},{1,5},{2,6},{3,7},{4,0},{5,1},{6,2},{7,3},{8,12},{9,13},{10,... | collective-permute-start | bytes 1376264 | tf_op jit(solution)/shard_map/ppermute | solution.py:394
  28.7 4.4 %slice-start = ((s8[4587520]{0:T(1024)(128)(4,1)}), s8[4194304]{0:T(1024)(128)(4,1)S(1)}, s32[]{:S(2)}) async-start(s8[4587520]{0:T(1024)(128)(4,1)} %bitcast.6), calls=%async_computation | async-start | bytes 8388608
  30.4 2.7 %slice-start.1 = ((s8[4587520]{0:T(1024)(128)(4,1)}), s8[393216]{0:T(1024)(128)(4,1)S(1)}, s32[]{:S(2)}) async-start(s8[4587520]{0:T(1024)(128)(4,1)} %bitcast.6), calls=%async_computation.1 | async-start | bytes 786432
  32.9 1.9 %collective-permute-start.8 = (bf16[64,3584]{1,0:T(8,128)(2,1)S(1)}, bf16[64,3584]{1,0:T(8,128)(2,1)S(1)}, u32[]{:S(2)}, u32[]{:S(2)}) collective-permute-start(bf16[64,3584]{1,0:T(8,128)(2,1)S(1)} %get-tuple-element.44), channel_id=1, source_target_pairs={{0,4},{1,5},{2,6},{3,7},{4,0},{5,1},{6,2},{7,3},{8,12},{9,13},{10,... | collective-permute-start | bytes 1376264 | tf_op jit(solution)/shard_map/ppermute | solution.py:394
  34.0 1.9 %collective-permute-start.12 = (bf16[64,3584]{1,0:T(8,128)(2,1)S(1)}, bf16[64,3584]{1,0:T(8,128)(2,1)S(1)}, u32[]{:S(2)}, u32[]{:S(2)}) collective-permute-start(bf16[64,3584]{1,0:T(8,128)(2,1)S(1)} %get-tuple-element.48), channel_id=1, source_target_pairs={{0,4},{1,5},{2,6},{3,7},{4,0},{5,1},{6,2},{7,3},{8,12},{9,13},{10,... | collective-permute-start | bytes 1376264 | tf_op jit(solution)/shard_map/ppermute | solution.py:394
  34.8 7.7 %collective-permute-start.9 = (bf16[32,3584]{1,0:T(8,128)(2,1)S(1)}, bf16[32,3584]{1,0:T(8,128)(2,1)S(1)}, u32[]{:S(2)}, u32[]{:S(2)}) collective-permute-start(bf16[32,3584]{1,0:T(8,128)(2,1)S(1)} %get-tuple-element.49), channel_id=1, source_target_pairs={{0,8},{1,9},{2,10},{3,11},{4,12},{5,13},{6,14},{7,15},{8,0},{9,1},... | collective-permute-start | bytes 688136 | tf_op jit(solution)/shard_map/ppermute | solution.py:394
  36.1 8.3 %collective-permute-start.13 = (bf16[32,3584]{1,0:T(8,128)(2,1)S(1)}, bf16[32,3584]{1,0:T(8,128)(2,1)S(1)}, u32[]{:S(2)}, u32[]{:S(2)}) collective-permute-start(bf16[32,3584]{1,0:T(8,128)(2,1)S(1)} %get-tuple-element.51), channel_id=1, source_target_pairs={{0,1},{1,0},{2,3},{3,2},{4,5},{5,4},{6,7},{7,6},{8,9},{9,8},{10,11... | collective-permute-start | bytes 688136 | tf_op jit(solution)/shard_map/ppermute | solution.py:394
  42.6 4.9 %collective-permute-start.10 = (bf16[16,3584]{1,0:T(8,128)(2,1)S(1)}, bf16[16,3584]{1,0:T(8,128)(2,1)S(1)}, u32[]{:S(2)}, u32[]{:S(2)}) collective-permute-start(bf16[16,3584]{1,0:T(8,128)(2,1)S(1)} %get-tuple-element.53), channel_id=1, source_target_pairs={{0,1},{1,0},{2,3},{3,2},{4,5},{5,4},{6,7},{7,6},{8,9},{9,8},{10,11... | collective-permute-start | bytes 344072 | tf_op jit(solution)/shard_map/ppermute | solution.py:394
  44.4 5.0 %collective-permute-start.14 = (bf16[16,3584]{1,0:T(8,128)(2,1)S(1)}, bf16[16,3584]{1,0:T(8,128)(2,1)S(1)}, u32[]{:S(2)}, u32[]{:S(2)}) collective-permute-start(bf16[16,3584]{1,0:T(8,128)(2,1)S(1)} %get-tuple-element.55), channel_id=1, source_target_pairs={{0,8},{1,9},{2,10},{3,11},{4,12},{5,13},{6,14},{7,15},{8,0},{9,1},... | collective-permute-start | bytes 344072 | tf_op jit(solution)/shard_map/ppermute | solution.py:394
  47.5 6.4 %collective-permute-start.11 = (bf16[8,3584]{1,0:T(8,128)(2,1)S(1)}, bf16[8,3584]{1,0:T(8,128)(2,1)S(1)}, u32[]{:S(2)}, u32[]{:S(2)}) collective-permute-start(bf16[8,3584]{1,0:T(8,128)(2,1)S(1)} %fusion.5), channel_id=1, source_target_pairs={{0,2},{1,3},{2,0},{3,1},{4,6},{5,7},{6,4},{7,5},{8,10},{9,11},{10,... | collective-permute-start | bytes 172040 | tf_op jit(solution)/shard_map/ppermute | solution.py:394
  49.5 5.1 %collective-permute-start.15 = (bf16[8,3584]{1,0:T(8,128)(2,1)S(1)}, bf16[8,3584]{1,0:T(8,128)(2,1)S(1)}, u32[]{:S(2)}, u32[]{:S(2)}) collective-permute-start(bf16[8,3584]{1,0:T(8,128)(2,1)S(1)} %fusion.2), channel_id=1, source_target_pairs={{0,2},{1,3},{2,0},{3,1},{4,6},{5,7},{6,4},{7,5},{8,10},{9,11},{10,... | collective-permute-start | bytes 172040 | tf_op jit(solution)/shard_map/ppermute | solution.py:394

commit v19 on v18

--- a/solution.py
+++ b/solution.py
@@ -432,13 +432,15 @@
     cut = width // 2
     own = [packed[:, :cut], packed[:, cut:]]
     loads = (
-        lambda *ready: (load_down(after(place, *ready), down, down_shared, cut, width - cut, share),),
+        lambda *ready: (load_down(after(place, *ready), down, down_shared, 0, cut, share),),
         lambda *ready: (load_weights(after(place, *ready), gate, gate_shared, share),),
-        lambda *ready: load_both(after(place, *ready), up, up_shared, down, down_shared, 0, cut, share),
+        lambda *ready: load_both(
+            after(place, *ready), up, up_shared, down, down_shared, cut, width - cut, share
+        ),
     )
     loaded = ()
     for number, (phase, load) in enumerate(zip(GATHER, loads)):
-        got = [flipped(part, *pairs) for part, pairs in zip(own, (phase[::-1], phase))]
+        got = [flipped(part, *pairs) for part, pairs in zip(own, (phase, phase[::-1]))]
         weights = tuple(load(*own))
         if number == 0:
             got[1], weights = lax.optimization_barrier((got[1], weights))
@@ -446,9 +448,9 @@
             got, weights = lax.optimization_barrier((got, weights))
         loaded += weights
         own = [stack(part, add) for part, add in zip(own, got)]
-    later, gate, up, second = loaded
+    second, gate, up, later = loaded
     odd = place[0] % 2
-    own = [jnp.where(odd == 1 - i, part, regroup(part, 4, 2)) for i, part in enumerate(own)]
+    own = [jnp.where(odd == i, part, regroup(part, 4, 2)) for i, part in enumerate(own)]
     other = [flipped(part, CORE, CORE) for part in own]
 
 

time: 55.5 us -> 57.1 us (1.029)
  waiting for transfers between devices: 14.1 us -> 22.6 us
  starting transfers between devices: 20.1 us -> 13.3 us
    ppermute x16, waiting for transfers between devices: 14.1 us -> 22.6 us  [flipped(): return lax.ppermute(value, ('node', 'local'), pairs)]
    ppermute x16, starting transfers between devices: 20.1 us -> 13.3 us  [flipped(): return lax.ppermute(value, ('node', 'local'), pairs)]
  transfers between devices with their start and end apart: 16 -> 16, of which waited for: 8 -> 12; matrix products, arithmetic and copies ran while one was open for 1% -> 1% of each run, Pallas kernels for 25% -> 24%
where the time goes in v19:
time: 57.1 us; the launch traced here: 56.9 us
  waiting for transfers between devices  22.6 us (40%)
  Pallas kernels  17.2 us (30%)
  starting transfers between devices  13.3 us (23%)
  local copies, waits for them, and re-layouts  2.26 us (4%)
  other arithmetic  1.32 us (2%)
    ppermute x16, waiting for transfers between devices, flipped(): return lax.ppermute(value, ('node', 'local'), pairs)  22.6 us
    ppermute x16, starting transfers between devices, flipped(): return lax.ppermute(value, ('node', 'local'), pairs)  13.3 us
    pallas_call x1, Pallas kernels, load_both(): pl.pallas_call(functools.partial(load_both_kernel, share, lower), in_spec...  5.09 us
    pallas_call x1, Pallas kernels, load_weights(): pl.pallas_call(functools.partial(load_kernel, share), in_specs=[SMEM_SPEC...  3.69 us
    pallas_call x1, Pallas kernels, pair_rows(): pl.pallas_call(functools.partial(early_half_kernel, share), in_specs=[SME...  2.38 us
    pallas_call x1, Pallas kernels, load_down(): pl.pallas_call(functools.partial(load_down_kernel, share, lower), in_spec...  2.33 us
    unnamed x19, local copies, waits for them, and re-layouts  2.23 us
    pallas_call x1, Pallas kernels, pair_rows(): pl.pallas_call(late_half_kernel, in_specs=[SMEM_SPEC] + [VMEM_SPEC] * 4,...  1.66 us
  transfers between devices with their start and end apart: 16, of which 12 were waited for; matrix products, arithmetic and copies ran while one was open for 1% of the time, Pallas kernels for 24%

profile of v19, /device:TPU:0, one launch (start us, length us, event | category | flops | bytes accessed | tf_op | source)
XLA Modules:
  0.0 56.9 jit_solution(10843099517142044858)
XLA Ops:
  0.0 1.1 %pack_rows.1 = bf16[8,7296]{1,0:T(8,128)(2,1)S(1)} custom-call(bf16[8,7168]{1,0:T(8,128)(2,1)} %tokens_ref.1, s32[4,8]{1,0:T(4,128)} %bitcast.12, bf16[4,8]{1,0:T(4,128)(2,1)} %bitcast.13), custom_call_target="tpu_custom_call" | custom-call | tf_op jit(solution)/shard_map/pack_rows/pallas_call | solution.py:48
  1.1 3.0 %collective-permute-start.2 = (bf16[8,3712]{1,0:T(8,128)(2,1)S(1)}, bf16[8,3712]{1,0:T(8,128)(2,1)S(1)}, u32[]{:S(2)}, u32[]{:S(2)}) collective-permute-start(bf16[8,3712]{1,0:T(8,128)(2,1)S(1)} %get-tuple-element.58), channel_id=1, source_target_pairs={{0,8},{1,9},{2,10},{3,11},{4,6},{5,7},{6,4},{7,5},{8,0},{9,1},{10,... | collective-permute-start | bytes 178184 | tf_op jit(solution)/shard_map/ppermute | solution.py:394
  4.1 2.7 %collective-permute-start = (bf16[8,3584]{1,0:T(8,128)(2,1)S(1)}, bf16[8,3584]{1,0:T(8,128)(2,1)S(1)}, u32[]{:S(2)}, u32[]{:S(2)}) collective-permute-start(bf16[8,3584]{1,0:T(8,128)(2,1)S(1)} %get-tuple-element.59), channel_id=1, source_target_pairs={{0,2},{1,3},{2,0},{3,1},{4,12},{5,13},{6,14},{7,15},{8,10},{9,11},... | collective-permute-start | bytes 172040 | tf_op jit(solution)/shard_map/ppermute | solution.py:394
  6.8 2.3 %load_down.1.second_ref = bf16[640,3584]{1,0:T(8,128)(2,1)S(1)} custom-call(s32[1]{0:T(128)} %bitcast.place_ref, bf16[512,7168]{1,0:T(8,128)(2,1)} %bitcast.8, bf16[512,7168]{1,0:T(8,128)(2,1)} %sdown_ref.3), custom_call_target="tpu_custom_call" | custom-call | bytes 9175040 | tf_op jit(solution)/shard_map/load_down/pallas_call | solution.py:243
  9.1 2.1 %copy-done = bf16[640,3584]{1,0:T(8,128)(2,1)} copy-done((bf16[640,3584]{1,0:T(8,128)(2,1)}, bf16[640,3584]{1,0:T(8,128)(2,1)S(1)}, u32[]{:S(2)}) %copy-start) | copy-done | bytes 4587544
  11.2 0.0 collective-permute-done.2
  11.2 0.4 collective-permute-start.3
  11.6 0.0 collective-permute-done
  11.6 1.6 %collective-permute-start.1 = (bf16[16,3584]{1,0:T(8,128)(2,1)S(1)}, bf16[16,3584]{1,0:T(8,128)(2,1)S(1)}, u32[]{:S(2)}, u32[]{:S(2)}) collective-permute-start(bf16[16,3584]{1,0:T(8,128)(2,1)S(1)} %pad_maximum_fusion.3), channel_id=1, source_target_pairs={{0,1},{1,0},{2,3},{3,2},{4,6},{5,7},{6,4},{7,5},{8,9},{9,8},{10,11... | collective-permute-start | bytes 344072 | tf_op jit(solution)/shard_map/ppermute | solution.py:394
  13.3 3.7 %load_weights.1.gate_ref = bf16[7168,640]{1,0:T(8,128)(2,1)S(1)} custom-call(s32[1]{0:T(128)} %bitcast.place_ref, bf16[7168,512]{1,0:T(8,128)(2,1)} %bitcast.10, bf16[7168,512]{1,0:T(8,128)(2,1)} %shared_ref.2), custom_call_target="tpu_custom_call" | custom-call | bytes 18350080 | tf_op jit(solution)/shard_map/load_weights/pallas_call | solution.py:80
  17.0 0.3 collective-permute-done.1
  17.3 3.1 %collective-permute-done.3 = bf16[16,3712]{1,0:T(8,128)(2,1)S(1)} collective-permute-done((bf16[16,3712]{1,0:T(8,128)(2,1)S(1)}, bf16[16,3712]{1,0:T(8,128)(2,1)S(1)}, u32[]{:S(2)}, u32[]{:S(2)}) %collective-permute-start.3) | collective-permute-done | bytes 118816 | tf_op jit(solution)/shard_map/ppermute | solution.py:394
  20.4 0.6 %collective-permute-start.4 = (bf16[32,3584]{1,0:T(8,128)(2,1)S(1)}, bf16[32,3584]{1,0:T(8,128)(2,1)S(1)}, u32[]{:S(2)}, u32[]{:S(2)}) collective-permute-start(bf16[32,3584]{1,0:T(8,128)(2,1)S(1)} %pad_maximum_fusion.1), channel_id=1, source_target_pairs={{0,8},{1,9},{2,10},{3,11},{4,5},{5,4},{6,7},{7,6},{8,0},{9,1},{10,... | collective-permute-start | bytes 688136 | tf_op jit(solution)/shard_map/ppermute | solution.py:394
  21.0 0.0 collective-permute-start.5
  21.0 5.1 %load_both.1 = (bf16[7168,640]{1,0:T(8,128)(2,1)S(1)}, bf16[640,3584]{1,0:T(8,128)(2,1)S(1)}) custom-call(s32[1]{0:T(128)} %bitcast.place_ref, bf16[7168,512]{1,0:T(8,128)(2,1)} %bitcast.11, bf16[7168,512]{1,0:T(8,128)(2,1)} %shared_ref.3, bf16[512,7168]{1,0:T(8,128)(2,1)} %bitcast.9, bf16[512,7168]{1,0:T(8,128)(2,1)} %sdown_ref.3), custom_call_target="tpu_custom_call" | custom-call | bytes 27525120 | tf_op jit(solution)/shard_map/load_both/pallas_call | solution.py:223
  26.1 2.1 %collective-permute-done.4 = bf16[32,3584]{1,0:T(8,128)(2,1)S(1)} collective-permute-done((bf16[32,3584]{1,0:T(8,128)(2,1)S(1)}, bf16[32,3584]{1,0:T(8,128)(2,1)S(1)}, u32[]{:S(2)}, u32[]{:S(2)}) %collective-permute-start.4) | collective-permute-done | bytes 229408 | tf_op jit(solution)/shard_map/ppermute | solution.py:394
  28.2 0.0 collective-permute-done.5
  28.3 0.1 maximum_select_fusion.own_ref
  28.5 0.1 collective-permute-start.7
  28.6 0.0 slice-start
  28.6 0.1 maximum_select_fusion.1.own_ref
  28.7 0.0 slice-start.1
  28.7 0.6 collective-permute-start.6
  29.3 1.1 %collective-permute-done.7.other_ref = bf16[64,3712]{1,0:T(8,128)(2,1)S(1)} collective-permute-done((bf16[64,3712]{1,0:T(8,128)(2,1)S(1)}, bf16[64,3712]{1,0:T(8,128)(2,1)S(1)}, u32[]{:S(2)}, u32[]{:S(2)}) %collective-permute-start.7) | collective-permute-done | bytes 475168 | tf_op jit(solution)/shard_map/ppermute | solution.py:394
  30.4 1.7 %late_half.1 = (f32[128,640]{1,0:T(8,128)S(1)}, f32[128,640]{1,0:T(8,128)S(1)}, f32[128,128]{1,0:T(8,128)S(1)}) custom-call(s32[1]{0:T(128)} %bitcast.place_ref, bf16[64,3712]{1,0:T(8,128)(2,1)S(1)} %maximum_select_fusion.own_ref, bf16[64,3712]{1,0:T(8,128)(2,1)S(1)} %collective-permute-done.7.other_ref, bf16[7168,640]{1,0:T(8,128)(2,1)S(1)} %load_weights.1.gate_ref, ...), custom_call_target="tpu_custom_call" | custom-call | flops 1174405120 | bytes 9175040 | tf_op jit(solution)/shard_map/late_half/pallas_call | solution.py:314
  32.1 0.0 collective-permute-done.6.other_ref
  32.1 0.0 slice-done
  32.1 2.4 %early_half.1 = (bf16[64,3584]{1,0:T(8,128)(2,1)S(1)}, bf16[64,3584]{1,0:T(8,128)(2,1)S(1)}, bf16[128,640]{1,0:T(8,128)(2,1)S(1)}) custom-call(s32[1]{0:T(128)} %bitcast.place_ref, bf16[64,3584]{1,0:T(8,128)(2,1)S(1)} %maximum_select_fusion.1.own_ref, bf16[64,3584]{1,0:T(8,128)(2,1)S(1)} %collective-permute-done.6.other_ref, ...), custom_call_target="tpu_custom_call" | custom-call | flops 1761607680 | bytes 13762560 | tf_op jit(solution)/shard_map/early_half/pallas_call | solution.py:324
  34.5 0.2 collective-permute-start.8
  34.7 0.9 %last_half.1 = (bf16[64,3584]{1,0:T(8,128)(2,1)S(1)}, bf16[64,3584]{1,0:T(8,128)(2,1)S(1)}) custom-call(bf16[128,640]{1,0:T(8,128)(2,1)S(1)} %get-tuple-element.45.act_ref, bf16[640,3584]{1,0:T(8,128)(2,1)S(1)} %get-tuple-element.46.later_ref), custom_call_target="tpu_custom_call" | custom-call | flops 587202560 | bytes 4587520 | tf_op jit(solution)/shard_map/last_half/pallas_call | solution.py:338
  35.6 0.4 collective-permute-start.12
  36.1 0.3 collective-permute-done.8
  36.4 0.1 add_convert_fusion.1
  36.5 0.6 %collective-permute-start.9 = (bf16[32,3584]{1,0:T(8,128)(2,1)S(1)}, bf16[32,3584]{1,0:T(8,128)(2,1)S(1)}, u32[]{:S(2)}, u32[]{:S(2)}) collective-permute-start(bf16[32,3584]{1,0:T(8,128)(2,1)S(1)} %get-tuple-element.49), channel_id=1, source_target_pairs={{0,8},{1,9},{2,10},{3,11},{4,12},{5,13},{6,14},{7,15},{8,0},{9,1},... | collective-permute-start | bytes 688136 | tf_op jit(solution)/shard_map/ppermute | solution.py:394
  37.1 0.5 collective-permute-done.12
  37.5 0.1 add_convert_fusion
  37.6 0.5 collective-permute-start.13
  38.2 6.0 %collective-permute-done.9 = bf16[32,3584]{1,0:T(8,128)(2,1)S(1)} collective-permute-done((bf16[32,3584]{1,0:T(8,128)(2,1)S(1)}, bf16[32,3584]{1,0:T(8,128)(2,1)S(1)}, u32[]{:S(2)}, u32[]{:S(2)}) %collective-permute-start.9) | collective-permute-done | bytes 229408 | tf_op jit(solution)/shard_map/ppermute | solution.py:394
  44.2 0.3 collective-permute-start.10
  44.5 1.1 %collective-permute-done.13 = bf16[32,3584]{1,0:T(8,128)(2,1)S(1)} collective-permute-done((bf16[32,3584]{1,0:T(8,128)(2,1)S(1)}, bf16[32,3584]{1,0:T(8,128)(2,1)S(1)}, u32[]{:S(2)}, u32[]{:S(2)}) %collective-permute-start.13) | collective-permute-done | bytes 229408 | tf_op jit(solution)/shard_map/ppermute | solution.py:394
  45.6 0.6 %collective-permute-start.14 = (bf16[16,3584]{1,0:T(8,128)(2,1)S(1)}, bf16[16,3584]{1,0:T(8,128)(2,1)S(1)}, u32[]{:S(2)}, u32[]{:S(2)}) collective-permute-start(bf16[16,3584]{1,0:T(8,128)(2,1)S(1)} %get-tuple-element.55), channel_id=1, source_target_pairs={{0,8},{1,9},{2,10},{3,11},{4,12},{5,13},{6,14},{7,15},{8,0},{9,1},... | collective-permute-start | bytes 344072 | tf_op jit(solution)/shard_map/ppermute | solution.py:394
  46.2 2.9 %collective-permute-done.10 = bf16[16,3584]{1,0:T(8,128)(2,1)S(1)} collective-permute-done((bf16[16,3584]{1,0:T(8,128)(2,1)S(1)}, bf16[16,3584]{1,0:T(8,128)(2,1)S(1)}, u32[]{:S(2)}, u32[]{:S(2)}) %collective-permute-start.10) | collective-permute-done | bytes 114720 | tf_op jit(solution)/shard_map/ppermute | solution.py:394
  49.1 0.1 collective-permute-start.11
  49.2 1.3 %collective-permute-done.14 = bf16[16,3584]{1,0:T(8,128)(2,1)S(1)} collective-permute-done((bf16[16,3584]{1,0:T(8,128)(2,1)S(1)}, bf16[16,3584]{1,0:T(8,128)(2,1)S(1)}, u32[]{:S(2)}, u32[]{:S(2)}) %collective-permute-start.14) | collective-permute-done | bytes 114720 | tf_op jit(solution)/shard_map/ppermute | solution.py:394
  50.5 1.7 %collective-permute-start.15 = (bf16[8,3584]{1,0:T(8,128)(2,1)S(1)}, bf16[8,3584]{1,0:T(8,128)(2,1)S(1)}, u32[]{:S(2)}, u32[]{:S(2)}) collective-permute-start(bf16[8,3584]{1,0:T(8,128)(2,1)S(1)} %fusion.2), channel_id=1, source_target_pairs={{0,2},{1,3},{2,0},{3,1},{4,6},{5,7},{6,4},{7,5},{8,10},{9,11},{10,... | collective-permute-start | bytes 172040 | tf_op jit(solution)/shard_map/ppermute | solution.py:394
  52.2 2.7 %collective-permute-done.11 = bf16[8,3584]{1,0:T(8,128)(2,1)S(1)} collective-permute-done((bf16[8,3584]{1,0:T(8,128)(2,1)S(1)}, bf16[8,3584]{1,0:T(8,128)(2,1)S(1)}, u32[]{:S(2)}, u32[]{:S(2)}) %collective-permute-start.11) | collective-permute-done | bytes 57376 | tf_op jit(solution)/shard_map/ppermute | solution.py:394
  54.9 1.4 %collective-permute-done.15 = bf16[8,3584]{1,0:T(8,128)(2,1)S(1)} collective-permute-done((bf16[8,3584]{1,0:T(8,128)(2,1)S(1)}, bf16[8,3584]{1,0:T(8,128)(2,1)S(1)}, u32[]{:S(2)}, u32[]{:S(2)}) %collective-permute-start.15) | collective-permute-done | bytes 57376 | tf_op jit(solution)/shard_map/ppermute | solution.py:394
  56.3 0.7 %pad_maximum_fusion.4 = bf16[8,7168]{1,0:T(8,128)(2,1)} fusion(bf16[8,3584]{1,0:T(8,128)(2,1)S(1)} %fusion.4, bf16[8,3584]{1,0:T(8,128)(2,1)S(1)} %fusion.7), kind=kLoop, calls=%fused_computation.26 | loop fusion | flops 229376 | bytes 229376 | tf_op jit(solution)/shard_map/concatenate | solution.py:466
  (29 shorter events, 0.4 us)
Async XLA Ops:
  1.1 10.1 %collective-permute-start.2 = (bf16[8,3712]{1,0:T(8,128)(2,1)S(1)}, bf16[8,3712]{1,0:T(8,128)(2,1)S(1)}, u32[]{:S(2)}, u32[]{:S(2)}) collective-permute-start(bf16[8,3712]{1,0:T(8,128)(2,1)S(1)} %get-tuple-element.58), channel_id=1, source_target_pairs={{0,8},{1,9},{2,10},{3,11},{4,6},{5,7},{6,4},{7,5},{8,0},{9,1},{10,... | collective-permute-start | bytes 178184 | tf_op jit(solution)/shard_map/ppermute | solution.py:394
  4.1 7.5 %collective-permute-start = (bf16[8,3584]{1,0:T(8,128)(2,1)S(1)}, bf16[8,3584]{1,0:T(8,128)(2,1)S(1)}, u32[]{:S(2)}, u32[]{:S(2)}) collective-permute-start(bf16[8,3584]{1,0:T(8,128)(2,1)S(1)} %get-tuple-element.59), channel_id=1, source_target_pairs={{0,2},{1,3},{2,0},{3,1},{4,12},{5,13},{6,14},{7,15},{8,10},{9,11},... | collective-permute-start | bytes 172040 | tf_op jit(solution)/shard_map/ppermute | solution.py:394
  9.1 2.1 %copy-start = (bf16[640,3584]{1,0:T(8,128)(2,1)}, bf16[640,3584]{1,0:T(8,128)(2,1)S(1)}, u32[]{:S(2)}) copy-start(bf16[640,3584]{1,0:T(8,128)(2,1)S(1)} %load_down.1.second_ref) | copy-start | bytes 13762564
  11.2 9.1 %collective-permute-start.3 = (bf16[16,3712]{1,0:T(8,128)(2,1)S(1)}, bf16[16,3712]{1,0:T(8,128)(2,1)S(1)}, u32[]{:S(2)}, u32[]{:S(2)}) collective-permute-start(bf16[16,3712]{1,0:T(8,128)(2,1)S(1)} %pad_maximum_fusion.2), channel_id=1, source_target_pairs={{0,2},{1,3},{2,0},{3,1},{4,5},{5,4},{6,7},{7,6},{8,10},{9,11},{10,... | collective-permute-start | bytes 356360 | tf_op jit(solution)/shard_map/ppermute | solution.py:394
  11.6 5.6 %collective-permute-start.1 = (bf16[16,3584]{1,0:T(8,128)(2,1)S(1)}, bf16[16,3584]{1,0:T(8,128)(2,1)S(1)}, u32[]{:S(2)}, u32[]{:S(2)}) collective-permute-start(bf16[16,3584]{1,0:T(8,128)(2,1)S(1)} %pad_maximum_fusion.3), channel_id=1, source_target_pairs={{0,1},{1,0},{2,3},{3,2},{4,6},{5,7},{6,4},{7,5},{8,9},{9,8},{10,11... | collective-permute-start | bytes 344072 | tf_op jit(solution)/shard_map/ppermute | solution.py:394
  20.4 7.8 %collective-permute-start.4 = (bf16[32,3584]{1,0:T(8,128)(2,1)S(1)}, bf16[32,3584]{1,0:T(8,128)(2,1)S(1)}, u32[]{:S(2)}, u32[]{:S(2)}) collective-permute-start(bf16[32,3584]{1,0:T(8,128)(2,1)S(1)} %pad_maximum_fusion.1), channel_id=1, source_target_pairs={{0,8},{1,9},{2,10},{3,11},{4,5},{5,4},{6,7},{7,6},{8,0},{9,1},{10,... | collective-permute-start | bytes 688136 | tf_op jit(solution)/shard_map/ppermute | solution.py:394
  21.0 7.2 %collective-permute-start.5 = (bf16[32,3712]{1,0:T(8,128)(2,1)S(1)}, bf16[32,3712]{1,0:T(8,128)(2,1)S(1)}, u32[]{:S(2)}, u32[]{:S(2)}) collective-permute-start(bf16[32,3712]{1,0:T(8,128)(2,1)S(1)} %pad_maximum_fusion), channel_id=1, source_target_pairs={{0,1},{1,0},{2,3},{3,2},{4,12},{5,13},{6,14},{7,15},{8,9},{9,8},{1... | collective-permute-start | bytes 712712 | tf_op jit(solution)/shard_map/ppermute | solution.py:394
  28.5 1.9 %collective-permute-start.7 = (bf16[64,3712]{1,0:T(8,128)(2,1)S(1)}, bf16[64,3712]{1,0:T(8,128)(2,1)S(1)}, u32[]{:S(2)}, u32[]{:S(2)}) collective-permute-start(bf16[64,3712]{1,0:T(8,128)(2,1)S(1)} %maximum_select_fusion.own_ref), channel_id=1, source_target_pairs={{0,4},{1,5},{2,6},{3,7},{4,0},{5,1},{6,2},{7,3},{8,12},{9,13},{10,... | collective-permute-start | bytes 1425416 | tf_op jit(solution)/shard_map/ppermute | solution.py:394
  28.6 3.5 %slice-start = ((s8[4587520]{0:T(1024)(128)(4,1)}), s8[393216]{0:T(1024)(128)(4,1)S(1)}, s32[]{:S(2)}) async-start(s8[4587520]{0:T(1024)(128)(4,1)} %bitcast.6), calls=%async_computation | async-start | bytes 786432
  28.7 3.4 %slice-start.1 = ((s8[4587520]{0:T(1024)(128)(4,1)}), s8[4194304]{0:T(1024)(128)(4,1)S(1)}, s32[]{:S(2)}) async-start(s8[4587520]{0:T(1024)(128)(4,1)} %bitcast.6), calls=%async_computation.1 | async-start | bytes 8388608
  28.7 3.4 %collective-permute-start.6 = (bf16[64,3584]{1,0:T(8,128)(2,1)S(1)}, bf16[64,3584]{1,0:T(8,128)(2,1)S(1)}, u32[]{:S(2)}, u32[]{:S(2)}) collective-permute-start(bf16[64,3584]{1,0:T(8,128)(2,1)S(1)} %maximum_select_fusion.1.own_ref), channel_id=1, source_target_pairs={{0,4},{1,5},{2,6},{3,7},{4,0},{5,1},{6,2},{7,3},{8,12},{9,13},{10,... | collective-permute-start | bytes 1376264 | tf_op jit(solution)/shard_map/ppermute | solution.py:394
  34.5 1.9 %collective-permute-start.8 = (bf16[64,3584]{1,0:T(8,128)(2,1)S(1)}, bf16[64,3584]{1,0:T(8,128)(2,1)S(1)}, u32[]{:S(2)}, u32[]{:S(2)}) collective-permute-start(bf16[64,3584]{1,0:T(8,128)(2,1)S(1)} %get-tuple-element.44), channel_id=1, source_target_pairs={{0,4},{1,5},{2,6},{3,7},{4,0},{5,1},{6,2},{7,3},{8,12},{9,13},{10,... | collective-permute-start | bytes 1376264 | tf_op jit(solution)/shard_map/ppermute | solution.py:394
  35.6 1.9 %collective-permute-start.12 = (bf16[64,3584]{1,0:T(8,128)(2,1)S(1)}, bf16[64,3584]{1,0:T(8,128)(2,1)S(1)}, u32[]{:S(2)}, u32[]{:S(2)}) collective-permute-start(bf16[64,3584]{1,0:T(8,128)(2,1)S(1)} %get-tuple-element.48), channel_id=1, source_target_pairs={{0,4},{1,5},{2,6},{3,7},{4,0},{5,1},{6,2},{7,3},{8,12},{9,13},{10,... | collective-permute-start | bytes 1376264 | tf_op jit(solution)/shard_map/ppermute | solution.py:394
  36.5 7.7 %collective-permute-start.9 = (bf16[32,3584]{1,0:T(8,128)(2,1)S(1)}, bf16[32,3584]{1,0:T(8,128)(2,1)S(1)}, u32[]{:S(2)}, u32[]{:S(2)}) collective-permute-start(bf16[32,3584]{1,0:T(8,128)(2,1)S(1)} %get-tuple-element.49), channel_id=1, source_target_pairs={{0,8},{1,9},{2,10},{3,11},{4,12},{5,13},{6,14},{7,15},{8,0},{9,1},... | collective-permute-start | bytes 688136 | tf_op jit(solution)/shard_map/ppermute | solution.py:394
  37.6 7.9 %collective-permute-start.13 = (bf16[32,3584]{1,0:T(8,128)(2,1)S(1)}, bf16[32,3584]{1,0:T(8,128)(2,1)S(1)}, u32[]{:S(2)}, u32[]{:S(2)}) collective-permute-start(bf16[32,3584]{1,0:T(8,128)(2,1)S(1)} %get-tuple-element.51), channel_id=1, source_target_pairs={{0,1},{1,0},{2,3},{3,2},{4,5},{5,4},{6,7},{7,6},{8,9},{9,8},{10,11... | collective-permute-start | bytes 688136 | tf_op jit(solution)/shard_map/ppermute | solution.py:394
  44.2 4.9 %collective-permute-start.10 = (bf16[16,3584]{1,0:T(8,128)(2,1)S(1)}, bf16[16,3584]{1,0:T(8,128)(2,1)S(1)}, u32[]{:S(2)}, u32[]{:S(2)}) collective-permute-start(bf16[16,3584]{1,0:T(8,128)(2,1)S(1)} %get-tuple-element.53), channel_id=1, source_target_pairs={{0,1},{1,0},{2,3},{3,2},{4,5},{5,4},{6,7},{7,6},{8,9},{9,8},{10,11... | collective-permute-start | bytes 344072 | tf_op jit(solution)/shard_map/ppermute | solution.py:394
  45.6 4.9 %collective-permute-start.14 = (bf16[16,3584]{1,0:T(8,128)(2,1)S(1)}, bf16[16,3584]{1,0:T(8,128)(2,1)S(1)}, u32[]{:S(2)}, u32[]{:S(2)}) collective-permute-start(bf16[16,3584]{1,0:T(8,128)(2,1)S(1)} %get-tuple-element.55), channel_id=1, source_target_pairs={{0,8},{1,9},{2,10},{3,11},{4,12},{5,13},{6,14},{7,15},{8,0},{9,1},... | collective-permute-start | bytes 344072 | tf_op jit(solution)/shard_map/ppermute | solution.py:394
  49.1 5.8 %collective-permute-start.11 = (bf16[8,3584]{1,0:T(8,128)(2,1)S(1)}, bf16[8,3584]{1,0:T(8,128)(2,1)S(1)}, u32[]{:S(2)}, u32[]{:S(2)}) collective-permute-start(bf16[8,3584]{1,0:T(8,128)(2,1)S(1)} %fusion.5), channel_id=1, source_target_pairs={{0,2},{1,3},{2,0},{3,1},{4,6},{5,7},{6,4},{7,5},{8,10},{9,11},{10,... | collective-permute-start | bytes 172040 | tf_op jit(solution)/shard_map/ppermute | solution.py:394
  50.5 5.8 %collective-permute-start.15 = (bf16[8,3584]{1,0:T(8,128)(2,1)S(1)}, bf16[8,3584]{1,0:T(8,128)(2,1)S(1)}, u32[]{:S(2)}, u32[]{:S(2)}) collective-permute-start(bf16[8,3584]{1,0:T(8,128)(2,1)S(1)} %fusion.2), channel_id=1, source_target_pairs={{0,2},{1,3},{2,0},{3,1},{4,6},{5,7},{6,4},{7,5},{8,10},{9,11},{10,... | collective-permute-start | bytes 172040 | tf_op jit(solution)/shard_map/ppermute | solution.py:394

commit v20 on v17

--- a/solution.py
+++ b/solution.py
@@ -234,22 +234,28 @@
     )(place, *(in_hbm(w) for w in (routed, shared, down, sdown)))
 
 
-def load_down_kernel(share, lower, place_ref, down_ref, sdown_ref, out_ref, sems):
-    run_copies(down_range_copies(share, place_ref, down_ref, sdown_ref, out_ref, lower, sems))
-
-
-def load_down(place, down, sdown, lower, columns, share):
-    units = down.shape[0] + LANES
+def load_first_kernel(share, lower, place_ref, routed_ref, shared_ref, sdown_ref, out_ref, rows_ref, sems):
+    parts = 4
+    column = pl.multiple_of((place_ref[0] // share) * LANES, LANES)
+    rows = pltpu.make_async_copy(
+        sdown_ref.at[pl.ds(column, LANES), pl.ds(lower, rows_ref.shape[1])], rows_ref, sems.at[2 * parts]
+    )
+    run_copies(weight_copies(share, place_ref, routed_ref, shared_ref, out_ref, sems, parts) + [rows])
+
+
+def load_first(place, routed, shared, sdown, lower, share):
+    width, hidden = routed.shape
+    units = hidden + LANES
     return pl.pallas_call(
-        functools.partial(load_down_kernel, share, lower),
-        in_specs=[SMEM_SPEC] + [ANY_SPEC] * 2,
-        out_specs=VMEM_SPEC,
-        out_shape=pltpu.VMEM((units, columns), BF16),
-        scratch_shapes=[pltpu.SemaphoreType.DMA((units // DOWN_ROWS,))],
-        cost_estimate=pl.CostEstimate(flops=0, bytes_accessed=4 * units * columns, transcendentals=0),
+        functools.partial(load_first_kernel, share, lower),
+        in_specs=[SMEM_SPEC] + [ANY_SPEC] * 3,
+        out_specs=[VMEM_SPEC] * 2,
+        out_shape=[pltpu.VMEM((width, units), BF16), pltpu.VMEM((LANES, sdown.shape[1] - lower), BF16)],
+        scratch_shapes=[pltpu.SemaphoreType.DMA((9,))],
+        cost_estimate=pl.CostEstimate(flops=0, bytes_accessed=4 * units * width, transcendentals=0),
         compiler_params=pltpu.CompilerParams(vmem_limit_bytes=1 << 20),
-        name="load_down",
-    )(place, in_hbm(down), in_hbm(sdown))
+        name="load_first",
+    )(place, *(in_hbm(w) for w in (routed, shared, sdown)))
 
 
 def late_half_kernel(place_ref, own_ref, other_ref, gate_ref, up_ref, gate_acc_ref, up_acc_ref, weight_ref, x):
@@ -292,12 +298,16 @@
         other_out_ref[:, at] = total[half:]
 
 
-def last_half_kernel(act_ref, third_ref, fourth_ref, own_out_ref, other_out_ref):
+def last_half_kernel(act_ref, down_ref, rows_ref, own_out_ref, other_out_ref):
     half, columns = own_out_ref.shape
+    hidden, width = down_ref.shape
     piece = columns // 2
-    for i, later_ref in enumerate((third_ref, fourth_ref)):
+    for i in range(2):
         at = slice(i * piece, (i + 1) * piece)
-        total = jnp.dot(act_ref[...], later_ref[...], preferred_element_type=F32).astype(BF16)
+        whole = slice(width - columns + i * piece, width - columns + (i + 1) * piece)
+        total = jnp.dot(act_ref[:, :hidden], down_ref[:, whole], preferred_element_type=F32)
+        total += jnp.dot(act_ref[:, hidden:], rows_ref[:, at], preferred_element_type=F32)
+        total = total.astype(BF16)
         own_out_ref[:, at] = swap_quarters(total[:half])
         other_out_ref[:, at] = swap_quarters(total[half:])
 
@@ -308,7 +318,7 @@
     )
 
 
-def pair_rows(place, own, other, gate, up, second, third, fourth, share):
+def pair_rows(place, own, other, gate, up, second, down, rows, share):
     half, cut = own[0].shape
     width, units = gate.shape
     partial = pl.pallas_call(
@@ -343,7 +353,7 @@
         cost_estimate=estimate(2 * half, width - cut, units),
         compiler_params=pltpu.CompilerParams(vmem_limit_bytes=10 << 20),
         name="last_half",
-    )(act, third, fourth)
+    )(act, pltpu.with_memory_space_constraint(down, pltpu.VMEM), rows)
     return own_out, last[0], other_out, last[1]
 
 
@@ -431,12 +441,9 @@
 
     cut = width // 2
     own = [packed[:, :cut], packed[:, cut:]]
-    quarter = (width - cut) // 2
     loads = (
         lambda *ready: (),
-        lambda *ready: load_both(
-            after(place, *ready), gate, gate_shared, down, down_shared, cut, quarter, share
-        ),
+        lambda *ready: load_first(after(place, *ready), gate, gate_shared, down_shared, cut, share),
         lambda *ready: load_both(after(place, *ready), up, up_shared, down, down_shared, 0, cut, share),
     )
     loaded = ()
@@ -447,15 +454,12 @@
             got, weights = lax.optimization_barrier((got, weights))
         loaded += weights
         own = [stack(part, add) for part, add in zip(own, got)]
-    gate, third, up, second = loaded
+    gate, late_rows, up, second = loaded
     odd = place[0] % 2
     own = [jnp.where(odd == i, part, regroup(part, 4, 2)) for i, part in enumerate(own)]
     other = [flipped(part, CORE, CORE) for part in own]
 
-    fourth = load_down(after(place, *own), down, down_shared, cut + quarter, quarter, share)
-    other[1], fourth = lax.optimization_barrier((other[1], fourth))
-
-    outs = pair_rows(place, own, other, gate, up, second, third, fourth, share)
+    outs = pair_rows(place, own, other, gate, up, second, down, late_rows, share)
 
     totals = [[own, flipped(other, CORE, CORE)] for own, other in zip(outs[:2], outs[2:])]
     for phase in SCATTER:

time: 54.9 us -> 55.3 us (level)
  Pallas kernels: 17.3 us -> 15.2 us
  waiting for transfers between devices: 12.1 us -> 14 us
  starting transfers between devices: 23.6 us -> 24.2 us
    pallas_call x2 -> x1, Pallas kernels: 9.49 us -> 5.08 us  [load_both(): pl.pallas_call(functools.partial(load_both_kernel, share, lower), in_spec...]
    pallas_call x1, Pallas kernels: 1.62 us -> 4 us  [load_first(): pl.pallas_call(functools.partial(load_first_kernel, share, lower), in_spe...]
    ppermute x16, waiting for transfers between devices: 12.1 us -> 14 us  [flipped(): return lax.ppermute(value, ('node', 'local'), pairs)]
    ppermute x16, starting transfers between devices: 23.6 us -> 24.2 us  [flipped(): return lax.ppermute(value, ('node', 'local'), pairs)]
  transfers between devices with their start and end apart: 16 -> 16, of which waited for: 7 -> 8; matrix products, arithmetic and copies ran while one was open for 1% -> 1% of each run, Pallas kernels for 25% -> 20%
where the time goes in v20:
time: 55.3 us; the launch traced here: 55.2 us
  starting transfers between devices  24.2 us (44%)
  Pallas kernels  15.2 us (27%)
  waiting for transfers between devices  14 us (25%)
  other arithmetic  1.33 us (2%)
    ppermute x16, starting transfers between devices, flipped(): return lax.ppermute(value, ('node', 'local'), pairs)  24.2 us
    ppermute x16, waiting for transfers between devices, flipped(): return lax.ppermute(value, ('node', 'local'), pairs)  14 us
    pallas_call x1, Pallas kernels, load_both(): pl.pallas_call(functools.partial(load_both_kernel, share, lower), in_spec...  5.08 us
    pallas_call x1, Pallas kernels, load_first(): pl.pallas_call(functools.partial(load_first_kernel, share, lower), in_spe...  4 us
    pallas_call x1, Pallas kernels, pair_rows(): pl.pallas_call(functools.partial(early_half_kernel, share), in_specs=[SME...  2.47 us
    pallas_call x1, Pallas kernels, pair_rows(): pl.pallas_call(late_half_kernel, in_specs=[SMEM_SPEC] + [VMEM_SPEC] * 4,...  1.68 us
  transfers between devices with their start and end apart: 16, of which 8 were waited for; matrix products, arithmetic and copies ran while one was open for 1% of the time, Pallas kernels for 20%

profile of v20, /device:TPU:0, one launch (start us, length us, event | category | flops | bytes accessed | tf_op | source)
XLA Modules:
  0.0 55.2 jit_solution(5278554062671843128)
XLA Ops:
  0.0 1.1 %pack_rows.1 = bf16[8,7296]{1,0:T(8,128)(2,1)S(1)} custom-call(bf16[8,7168]{1,0:T(8,128)(2,1)} %tokens_ref.1, s32[4,8]{1,0:T(4,128)} %bitcast.12, bf16[4,8]{1,0:T(4,128)(2,1)} %bitcast.13), custom_call_target="tpu_custom_call" | custom-call | tf_op jit(solution)/shard_map/pack_rows/pallas_call | solution.py:48
  1.1 3.0 %collective-permute-start.2 = (bf16[8,3712]{1,0:T(8,128)(2,1)S(1)}, bf16[8,3712]{1,0:T(8,128)(2,1)S(1)}, u32[]{:S(2)}, u32[]{:S(2)}) collective-permute-start(bf16[8,3712]{1,0:T(8,128)(2,1)S(1)} %get-tuple-element.58), channel_id=1, source_target_pairs={{0,8},{1,9},{2,10},{3,11},{4,6},{5,7},{6,4},{7,5},{8,0},{9,1},{10,... | collective-permute-start | bytes 178184 | tf_op jit(solution)/shard_map/ppermute | solution.py:404
  4.1 2.7 %collective-permute-start = (bf16[8,3584]{1,0:T(8,128)(2,1)S(1)}, bf16[8,3584]{1,0:T(8,128)(2,1)S(1)}, u32[]{:S(2)}, u32[]{:S(2)}) collective-permute-start(bf16[8,3584]{1,0:T(8,128)(2,1)S(1)} %get-tuple-element.59), channel_id=1, source_target_pairs={{0,2},{1,3},{2,0},{3,1},{4,12},{5,13},{6,14},{7,15},{8,10},{9,11},... | collective-permute-start | bytes 172040 | tf_op jit(solution)/shard_map/ppermute | solution.py:404
  6.8 0.0 collective-permute-done.2
  6.8 2.7 %collective-permute-start.3 = (bf16[16,3712]{1,0:T(8,128)(2,1)S(1)}, bf16[16,3712]{1,0:T(8,128)(2,1)S(1)}, u32[]{:S(2)}, u32[]{:S(2)}) collective-permute-start(bf16[16,3712]{1,0:T(8,128)(2,1)S(1)} %pad_maximum_fusion.2), channel_id=1, source_target_pairs={{0,2},{1,3},{2,0},{3,1},{4,5},{5,4},{6,7},{7,6},{8,10},{9,11},{10,... | collective-permute-start | bytes 356360 | tf_op jit(solution)/shard_map/ppermute | solution.py:404
  9.5 0.0 collective-permute-done
  9.5 1.6 %collective-permute-start.1 = (bf16[16,3584]{1,0:T(8,128)(2,1)S(1)}, bf16[16,3584]{1,0:T(8,128)(2,1)S(1)}, u32[]{:S(2)}, u32[]{:S(2)}) collective-permute-start(bf16[16,3584]{1,0:T(8,128)(2,1)S(1)} %pad_maximum_fusion.3), channel_id=1, source_target_pairs={{0,1},{1,0},{2,3},{3,2},{4,6},{5,7},{6,4},{7,5},{8,9},{9,8},{10,11... | collective-permute-start | bytes 344072 | tf_op jit(solution)/shard_map/ppermute | solution.py:404
  11.1 4.0 %load_first.1 = (bf16[7168,640]{1,0:T(8,128)(2,1)S(1)}, bf16[128,3584]{1,0:T(8,128)(2,1)S(1)}) custom-call(s32[1]{0:T(128)} %bitcast.place_ref, bf16[7168,512]{1,0:T(8,128)(2,1)} %bitcast.10, bf16[7168,512]{1,0:T(8,128)(2,1)} %shared_ref.2, bf16[512,7168]{1,0:T(8,128)(2,1)} %sdown_ref.3), custom_call_target="tpu_custom_call" | custom-call | bytes 18350080 | tf_op jit(solution)/shard_map/load_first/pallas_call | solution.py:249
  15.1 0.0 collective-permute-done.1
  15.2 0.8 %collective-permute-done.3 = bf16[16,3712]{1,0:T(8,128)(2,1)S(1)} collective-permute-done((bf16[16,3712]{1,0:T(8,128)(2,1)S(1)}, bf16[16,3712]{1,0:T(8,128)(2,1)S(1)}, u32[]{:S(2)}, u32[]{:S(2)}) %collective-permute-start.3) | collective-permute-done | bytes 118816 | tf_op jit(solution)/shard_map/ppermute | solution.py:404
  15.9 1.6 %collective-permute-start.4 = (bf16[32,3584]{1,0:T(8,128)(2,1)S(1)}, bf16[32,3584]{1,0:T(8,128)(2,1)S(1)}, u32[]{:S(2)}, u32[]{:S(2)}) collective-permute-start(bf16[32,3584]{1,0:T(8,128)(2,1)S(1)} %pad_maximum_fusion.1), channel_id=1, source_target_pairs={{0,8},{1,9},{2,10},{3,11},{4,5},{5,4},{6,7},{7,6},{8,0},{9,1},{10,... | collective-permute-start | bytes 688136 | tf_op jit(solution)/shard_map/ppermute | solution.py:404
  17.6 0.9 %collective-permute-start.5 = (bf16[32,3712]{1,0:T(8,128)(2,1)S(1)}, bf16[32,3712]{1,0:T(8,128)(2,1)S(1)}, u32[]{:S(2)}, u32[]{:S(2)}) collective-permute-start(bf16[32,3712]{1,0:T(8,128)(2,1)S(1)} %pad_maximum_fusion), channel_id=1, source_target_pairs={{0,1},{1,0},{2,3},{3,2},{4,12},{5,13},{6,14},{7,15},{8,9},{9,8},{1... | collective-permute-start | bytes 712712 | tf_op jit(solution)/shard_map/ppermute | solution.py:404
  18.5 5.1 %load_both.1 = (bf16[7168,640]{1,0:T(8,128)(2,1)S(1)}, bf16[640,3584]{1,0:T(8,128)(2,1)S(1)}) custom-call(s32[1]{0:T(128)} %bitcast.place_ref, bf16[7168,512]{1,0:T(8,128)(2,1)} %bitcast.11, bf16[7168,512]{1,0:T(8,128)(2,1)} %shared_ref.3, bf16[512,7168]{1,0:T(8,128)(2,1)} %bitcast.6, bf16[512,7168]{1,0:T(8,128)(2,1)} %sdown_ref.3), custom_call_target="tpu_custom_call" | custom-call | bytes 27525120 | tf_op jit(solution)/shard_map/load_both/pallas_call | solution.py:223
  23.6 0.3 collective-permute-done.4
  23.9 0.0 collective-permute-done.5
  24.1 0.1 maximum_select_fusion.own_ref
  24.2 0.1 collective-permute-start.7
  24.3 0.1 maximum_select_fusion.1.own_ref
  24.4 0.6 %collective-permute-start.6 = (bf16[64,3584]{1,0:T(8,128)(2,1)S(1)}, bf16[64,3584]{1,0:T(8,128)(2,1)S(1)}, u32[]{:S(2)}, u32[]{:S(2)}) collective-permute-start(bf16[64,3584]{1,0:T(8,128)(2,1)S(1)} %maximum_select_fusion.1.own_ref), channel_id=1, source_target_pairs={{0,4},{1,5},{2,6},{3,7},{4,0},{5,1},{6,2},{7,3},{8,12},{9,13},{10,... | collective-permute-start | bytes 1376264 | tf_op jit(solution)/shard_map/ppermute | solution.py:404
  25.0 1.1 %collective-permute-done.7.other_ref = bf16[64,3712]{1,0:T(8,128)(2,1)S(1)} collective-permute-done((bf16[64,3712]{1,0:T(8,128)(2,1)S(1)}, bf16[64,3712]{1,0:T(8,128)(2,1)S(1)}, u32[]{:S(2)}, u32[]{:S(2)}) %collective-permute-start.7) | collective-permute-done | bytes 475168 | tf_op jit(solution)/shard_map/ppermute | solution.py:404
  26.1 0.0 slice-start
  26.2 1.7 %late_half.1 = (f32[128,640]{1,0:T(8,128)S(1)}, f32[128,640]{1,0:T(8,128)S(1)}, f32[128,128]{1,0:T(8,128)S(1)}) custom-call(s32[1]{0:T(128)} %bitcast.place_ref, bf16[64,3712]{1,0:T(8,128)(2,1)S(1)} %maximum_select_fusion.own_ref, bf16[64,3712]{1,0:T(8,128)(2,1)S(1)} %collective-permute-done.7.other_ref, bf16[7168,640]{1,0:T(8,128)(2,1)S(1)} %get-tuple-element.36.gate_ref, ...), custom_call_target="tpu_custom_call" | custom-call | flops 1174405120 | bytes 9175040 | tf_op jit(solution)/shard_map/late_half/pallas_call | solution.py:324
  27.8 0.0 collective-permute-done.6.other_ref
  27.9 0.0 slice-start.1
  27.9 2.5 %early_half.1 = (bf16[64,3584]{1,0:T(8,128)(2,1)S(1)}, bf16[64,3584]{1,0:T(8,128)(2,1)S(1)}, bf16[128,640]{1,0:T(8,128)(2,1)S(1)}) custom-call(s32[1]{0:T(128)} %bitcast.place_ref, bf16[64,3584]{1,0:T(8,128)(2,1)S(1)} %maximum_select_fusion.1.own_ref, bf16[64,3584]{1,0:T(8,128)(2,1)S(1)} %collective-permute-done.6.other_ref, ...), custom_call_target="tpu_custom_call" | custom-call | flops 1761607680 | bytes 13762560 | tf_op jit(solution)/shard_map/early_half/pallas_call | solution.py:334
  30.3 0.0 slice-done
  30.3 0.0 slice-done.1
  30.4 0.9 %last_half.1 = (bf16[64,3584]{1,0:T(8,128)(2,1)S(1)}, bf16[64,3584]{1,0:T(8,128)(2,1)S(1)}) custom-call(bf16[128,640]{1,0:T(8,128)(2,1)S(1)} %get-tuple-element.45.act_ref, bf16[512,7168]{1,0:T(8,128)(2,1)S(1)} %bitcast.9, bf16[128,3584]{1,0:T(8,128)(2,1)S(1)} %get-tuple-element.46.rows_ref), custom_call_target="tpu_custom_call" | custom-call | flops 587202560 | bytes 4587520 | tf_op jit(solution)/shard_map/last_half/pallas_call | solution.py:348
  31.3 0.2 collective-permute-start.12
  31.5 0.4 collective-permute-start.8
  31.9 1.3 %collective-permute-done.12 = bf16[64,3584]{1,0:T(8,128)(2,1)S(1)} collective-permute-done((bf16[64,3584]{1,0:T(8,128)(2,1)S(1)}, bf16[64,3584]{1,0:T(8,128)(2,1)S(1)}, u32[]{:S(2)}, u32[]{:S(2)}) %collective-permute-start.12) | collective-permute-done | bytes 458784 | tf_op jit(solution)/shard_map/ppermute | solution.py:404
  33.2 0.1 add_convert_fusion
  33.3 1.4 %collective-permute-start.13 = (bf16[32,3584]{1,0:T(8,128)(2,1)S(1)}, bf16[32,3584]{1,0:T(8,128)(2,1)S(1)}, u32[]{:S(2)}, u32[]{:S(2)}) collective-permute-start(bf16[32,3584]{1,0:T(8,128)(2,1)S(1)} %get-tuple-element.51), channel_id=1, source_target_pairs={{0,1},{1,0},{2,3},{3,2},{4,5},{5,4},{6,7},{7,6},{8,9},{9,8},{10,11... | collective-permute-start | bytes 688136 | tf_op jit(solution)/shard_map/ppermute | solution.py:404
  34.7 0.0 collective-permute-done.8
  34.7 0.1 add_convert_fusion.1
  34.8 1.5 %collective-permute-start.9 = (bf16[32,3584]{1,0:T(8,128)(2,1)S(1)}, bf16[32,3584]{1,0:T(8,128)(2,1)S(1)}, u32[]{:S(2)}, u32[]{:S(2)}) collective-permute-start(bf16[32,3584]{1,0:T(8,128)(2,1)S(1)} %get-tuple-element.49), channel_id=1, source_target_pairs={{0,8},{1,9},{2,10},{3,11},{4,12},{5,13},{6,14},{7,15},{8,0},{9,1},... | collective-permute-start | bytes 688136 | tf_op jit(solution)/shard_map/ppermute | solution.py:404
  36.3 4.7 %collective-permute-done.13 = bf16[32,3584]{1,0:T(8,128)(2,1)S(1)} collective-permute-done((bf16[32,3584]{1,0:T(8,128)(2,1)S(1)}, bf16[32,3584]{1,0:T(8,128)(2,1)S(1)}, u32[]{:S(2)}, u32[]{:S(2)}) %collective-permute-start.13) | collective-permute-done | bytes 229408 | tf_op jit(solution)/shard_map/ppermute | solution.py:404
  41.1 1.6 %collective-permute-start.14 = (bf16[16,3584]{1,0:T(8,128)(2,1)S(1)}, bf16[16,3584]{1,0:T(8,128)(2,1)S(1)}, u32[]{:S(2)}, u32[]{:S(2)}) collective-permute-start(bf16[16,3584]{1,0:T(8,128)(2,1)S(1)} %get-tuple-element.55), channel_id=1, source_target_pairs={{0,8},{1,9},{2,10},{3,11},{4,12},{5,13},{6,14},{7,15},{8,0},{9,1},... | collective-permute-start | bytes 344072 | tf_op jit(solution)/shard_map/ppermute | solution.py:404
  42.7 0.0 collective-permute-done.9
  42.7 0.1 fusion.1
  42.7 1.3 %collective-permute-start.10 = (bf16[16,3584]{1,0:T(8,128)(2,1)S(1)}, bf16[16,3584]{1,0:T(8,128)(2,1)S(1)}, u32[]{:S(2)}, u32[]{:S(2)}) collective-permute-start(bf16[16,3584]{1,0:T(8,128)(2,1)S(1)} %get-tuple-element.53), channel_id=1, source_target_pairs={{0,1},{1,0},{2,3},{3,2},{4,5},{5,4},{6,7},{7,6},{8,9},{9,8},{10,11... | collective-permute-start | bytes 344072 | tf_op jit(solution)/shard_map/ppermute | solution.py:404
  44.0 1.9 %collective-permute-done.14 = bf16[16,3584]{1,0:T(8,128)(2,1)S(1)} collective-permute-done((bf16[16,3584]{1,0:T(8,128)(2,1)S(1)}, bf16[16,3584]{1,0:T(8,128)(2,1)S(1)}, u32[]{:S(2)}, u32[]{:S(2)}) %collective-permute-start.14) | collective-permute-done | bytes 114720 | tf_op jit(solution)/shard_map/ppermute | solution.py:404
  46.0 2.8 %collective-permute-start.15 = (bf16[8,3584]{1,0:T(8,128)(2,1)S(1)}, bf16[8,3584]{1,0:T(8,128)(2,1)S(1)}, u32[]{:S(2)}, u32[]{:S(2)}) collective-permute-start(bf16[8,3584]{1,0:T(8,128)(2,1)S(1)} %fusion.2), channel_id=1, source_target_pairs={{0,2},{1,3},{2,0},{3,1},{4,6},{5,7},{6,4},{7,5},{8,10},{9,11},{10,... | collective-permute-start | bytes 172040 | tf_op jit(solution)/shard_map/ppermute | solution.py:404
  48.7 0.0 collective-permute-done.10
  48.7 2.0 %collective-permute-start.11 = (bf16[8,3584]{1,0:T(8,128)(2,1)S(1)}, bf16[8,3584]{1,0:T(8,128)(2,1)S(1)}, u32[]{:S(2)}, u32[]{:S(2)}) collective-permute-start(bf16[8,3584]{1,0:T(8,128)(2,1)S(1)} %fusion.5), channel_id=1, source_target_pairs={{0,2},{1,3},{2,0},{3,1},{4,6},{5,7},{6,4},{7,5},{8,10},{9,11},{10,... | collective-permute-start | bytes 172040 | tf_op jit(solution)/shard_map/ppermute | solution.py:404
  50.7 1.9 %collective-permute-done.15 = bf16[8,3584]{1,0:T(8,128)(2,1)S(1)} collective-permute-done((bf16[8,3584]{1,0:T(8,128)(2,1)S(1)}, bf16[8,3584]{1,0:T(8,128)(2,1)S(1)}, u32[]{:S(2)}, u32[]{:S(2)}) %collective-permute-start.15) | collective-permute-done | bytes 57376 | tf_op jit(solution)/shard_map/ppermute | solution.py:404
  52.7 1.8 %collective-permute-done.11 = bf16[8,3584]{1,0:T(8,128)(2,1)S(1)} collective-permute-done((bf16[8,3584]{1,0:T(8,128)(2,1)S(1)}, bf16[8,3584]{1,0:T(8,128)(2,1)S(1)}, u32[]{:S(2)}, u32[]{:S(2)}) %collective-permute-start.11) | collective-permute-done | bytes 57376 | tf_op jit(solution)/shard_map/ppermute | solution.py:404
  54.5 0.7 %pad_maximum_fusion.4 = bf16[8,7168]{1,0:T(8,128)(2,1)} fusion(bf16[8,3584]{1,0:T(8,128)(2,1)S(1)} %fusion.4, bf16[8,3584]{1,0:T(8,128)(2,1)S(1)} %fusion.7), kind=kLoop, calls=%fused_computation.26 | loop fusion | flops 229376 | bytes 229376 | tf_op jit(solution)/shard_map/concatenate | solution.py:471
  (26 shorter events, 0.3 us)
Async XLA Ops:
  1.1 5.7 %collective-permute-start.2 = (bf16[8,3712]{1,0:T(8,128)(2,1)S(1)}, bf16[8,3712]{1,0:T(8,128)(2,1)S(1)}, u32[]{:S(2)}, u32[]{:S(2)}) collective-permute-start(bf16[8,3712]{1,0:T(8,128)(2,1)S(1)} %get-tuple-element.58), channel_id=1, source_target_pairs={{0,8},{1,9},{2,10},{3,11},{4,6},{5,7},{6,4},{7,5},{8,0},{9,1},{10,... | collective-permute-start | bytes 178184 | tf_op jit(solution)/shard_map/ppermute | solution.py:404
  4.1 5.4 %collective-permute-start = (bf16[8,3584]{1,0:T(8,128)(2,1)S(1)}, bf16[8,3584]{1,0:T(8,128)(2,1)S(1)}, u32[]{:S(2)}, u32[]{:S(2)}) collective-permute-start(bf16[8,3584]{1,0:T(8,128)(2,1)S(1)} %get-tuple-element.59), channel_id=1, source_target_pairs={{0,2},{1,3},{2,0},{3,1},{4,12},{5,13},{6,14},{7,15},{8,10},{9,11},... | collective-permute-start | bytes 172040 | tf_op jit(solution)/shard_map/ppermute | solution.py:404
  6.8 9.1 %collective-permute-start.3 = (bf16[16,3712]{1,0:T(8,128)(2,1)S(1)}, bf16[16,3712]{1,0:T(8,128)(2,1)S(1)}, u32[]{:S(2)}, u32[]{:S(2)}) collective-permute-start(bf16[16,3712]{1,0:T(8,128)(2,1)S(1)} %pad_maximum_fusion.2), channel_id=1, source_target_pairs={{0,2},{1,3},{2,0},{3,1},{4,5},{5,4},{6,7},{7,6},{8,10},{9,11},{10,... | collective-permute-start | bytes 356360 | tf_op jit(solution)/shard_map/ppermute | solution.py:404
  9.5 5.7 %collective-permute-start.1 = (bf16[16,3584]{1,0:T(8,128)(2,1)S(1)}, bf16[16,3584]{1,0:T(8,128)(2,1)S(1)}, u32[]{:S(2)}, u32[]{:S(2)}) collective-permute-start(bf16[16,3584]{1,0:T(8,128)(2,1)S(1)} %pad_maximum_fusion.3), channel_id=1, source_target_pairs={{0,1},{1,0},{2,3},{3,2},{4,6},{5,7},{6,4},{7,5},{8,9},{9,8},{10,11... | collective-permute-start | bytes 344072 | tf_op jit(solution)/shard_map/ppermute | solution.py:404
  15.9 8.0 %collective-permute-start.4 = (bf16[32,3584]{1,0:T(8,128)(2,1)S(1)}, bf16[32,3584]{1,0:T(8,128)(2,1)S(1)}, u32[]{:S(2)}, u32[]{:S(2)}) collective-permute-start(bf16[32,3584]{1,0:T(8,128)(2,1)S(1)} %pad_maximum_fusion.1), channel_id=1, source_target_pairs={{0,8},{1,9},{2,10},{3,11},{4,5},{5,4},{6,7},{7,6},{8,0},{9,1},{10,... | collective-permute-start | bytes 688136 | tf_op jit(solution)/shard_map/ppermute | solution.py:404
  17.6 6.3 %collective-permute-start.5 = (bf16[32,3712]{1,0:T(8,128)(2,1)S(1)}, bf16[32,3712]{1,0:T(8,128)(2,1)S(1)}, u32[]{:S(2)}, u32[]{:S(2)}) collective-permute-start(bf16[32,3712]{1,0:T(8,128)(2,1)S(1)} %pad_maximum_fusion), channel_id=1, source_target_pairs={{0,1},{1,0},{2,3},{3,2},{4,12},{5,13},{6,14},{7,15},{8,9},{9,8},{1... | collective-permute-start | bytes 712712 | tf_op jit(solution)/shard_map/ppermute | solution.py:404
  24.2 1.9 %collective-permute-start.7 = (bf16[64,3712]{1,0:T(8,128)(2,1)S(1)}, bf16[64,3712]{1,0:T(8,128)(2,1)S(1)}, u32[]{:S(2)}, u32[]{:S(2)}) collective-permute-start(bf16[64,3712]{1,0:T(8,128)(2,1)S(1)} %maximum_select_fusion.own_ref), channel_id=1, source_target_pairs={{0,4},{1,5},{2,6},{3,7},{4,0},{5,1},{6,2},{7,3},{8,12},{9,13},{10,... | collective-permute-start | bytes 1425416 | tf_op jit(solution)/shard_map/ppermute | solution.py:404
  24.4 3.4 %collective-permute-start.6 = (bf16[64,3584]{1,0:T(8,128)(2,1)S(1)}, bf16[64,3584]{1,0:T(8,128)(2,1)S(1)}, u32[]{:S(2)}, u32[]{:S(2)}) collective-permute-start(bf16[64,3584]{1,0:T(8,128)(2,1)S(1)} %maximum_select_fusion.1.own_ref), channel_id=1, source_target_pairs={{0,4},{1,5},{2,6},{3,7},{4,0},{5,1},{6,2},{7,3},{8,12},{9,13},{10,... | collective-permute-start | bytes 1376264 | tf_op jit(solution)/shard_map/ppermute | solution.py:404
  26.1 4.2 %slice-start = ((s8[7340032]{0:T(1024)(128)(4,1)}), s8[4194304]{0:T(1024)(128)(4,1)S(1)}, s32[]{:S(2)}) async-start(s8[7340032]{0:T(1024)(128)(4,1)} %bitcast.7), calls=%async_computation | async-start | bytes 8388608
  27.9 2.5 %slice-start.1 = ((s8[7340032]{0:T(1024)(128)(4,1)}), s8[3145728]{0:T(1024)(128)(4,1)S(1)}, s32[]{:S(2)}) async-start(s8[7340032]{0:T(1024)(128)(4,1)} %bitcast.7), calls=%async_computation.1 | async-start | bytes 6291456
  31.3 1.9 %collective-permute-start.12 = (bf16[64,3584]{1,0:T(8,128)(2,1)S(1)}, bf16[64,3584]{1,0:T(8,128)(2,1)S(1)}, u32[]{:S(2)}, u32[]{:S(2)}) collective-permute-start(bf16[64,3584]{1,0:T(8,128)(2,1)S(1)} %get-tuple-element.48), channel_id=1, source_target_pairs={{0,4},{1,5},{2,6},{3,7},{4,0},{5,1},{6,2},{7,3},{8,12},{9,13},{10,... | collective-permute-start | bytes 1376264 | tf_op jit(solution)/shard_map/ppermute | solution.py:404
  31.5 3.1 %collective-permute-start.8 = (bf16[64,3584]{1,0:T(8,128)(2,1)S(1)}, bf16[64,3584]{1,0:T(8,128)(2,1)S(1)}, u32[]{:S(2)}, u32[]{:S(2)}) collective-permute-start(bf16[64,3584]{1,0:T(8,128)(2,1)S(1)} %get-tuple-element.44), channel_id=1, source_target_pairs={{0,4},{1,5},{2,6},{3,7},{4,0},{5,1},{6,2},{7,3},{8,12},{9,13},{10,... | collective-permute-start | bytes 1376264 | tf_op jit(solution)/shard_map/ppermute | solution.py:404
  33.3 7.7 %collective-permute-start.13 = (bf16[32,3584]{1,0:T(8,128)(2,1)S(1)}, bf16[32,3584]{1,0:T(8,128)(2,1)S(1)}, u32[]{:S(2)}, u32[]{:S(2)}) collective-permute-start(bf16[32,3584]{1,0:T(8,128)(2,1)S(1)} %get-tuple-element.51), channel_id=1, source_target_pairs={{0,1},{1,0},{2,3},{3,2},{4,5},{5,4},{6,7},{7,6},{8,9},{9,8},{10,11... | collective-permute-start | bytes 688136 | tf_op jit(solution)/shard_map/ppermute | solution.py:404
  34.8 7.9 %collective-permute-start.9 = (bf16[32,3584]{1,0:T(8,128)(2,1)S(1)}, bf16[32,3584]{1,0:T(8,128)(2,1)S(1)}, u32[]{:S(2)}, u32[]{:S(2)}) collective-permute-start(bf16[32,3584]{1,0:T(8,128)(2,1)S(1)} %get-tuple-element.49), channel_id=1, source_target_pairs={{0,8},{1,9},{2,10},{3,11},{4,12},{5,13},{6,14},{7,15},{8,0},{9,1},... | collective-permute-start | bytes 688136 | tf_op jit(solution)/shard_map/ppermute | solution.py:404
  41.1 4.9 %collective-permute-start.14 = (bf16[16,3584]{1,0:T(8,128)(2,1)S(1)}, bf16[16,3584]{1,0:T(8,128)(2,1)S(1)}, u32[]{:S(2)}, u32[]{:S(2)}) collective-permute-start(bf16[16,3584]{1,0:T(8,128)(2,1)S(1)} %get-tuple-element.55), channel_id=1, source_target_pairs={{0,8},{1,9},{2,10},{3,11},{4,12},{5,13},{6,14},{7,15},{8,0},{9,1},... | collective-permute-start | bytes 344072 | tf_op jit(solution)/shard_map/ppermute | solution.py:404
  42.7 6.0 %collective-permute-start.10 = (bf16[16,3584]{1,0:T(8,128)(2,1)S(1)}, bf16[16,3584]{1,0:T(8,128)(2,1)S(1)}, u32[]{:S(2)}, u32[]{:S(2)}) collective-permute-start(bf16[16,3584]{1,0:T(8,128)(2,1)S(1)} %get-tuple-element.53), channel_id=1, source_target_pairs={{0,1},{1,0},{2,3},{3,2},{4,5},{5,4},{6,7},{7,6},{8,9},{9,8},{10,11... | collective-permute-start | bytes 344072 | tf_op jit(solution)/shard_map/ppermute | solution.py:404
  46.0 6.7 %collective-permute-start.15 = (bf16[8,3584]{1,0:T(8,128)(2,1)S(1)}, bf16[8,3584]{1,0:T(8,128)(2,1)S(1)}, u32[]{:S(2)}, u32[]{:S(2)}) collective-permute-start(bf16[8,3584]{1,0:T(8,128)(2,1)S(1)} %fusion.2), channel_id=1, source_target_pairs={{0,2},{1,3},{2,0},{3,1},{4,6},{5,7},{6,4},{7,5},{8,10},{9,11},{10,... | collective-permute-start | bytes 172040 | tf_op jit(solution)/shard_map/ppermute | solution.py:404
  48.7 5.8 %collective-permute-start.11 = (bf16[8,3584]{1,0:T(8,128)(2,1)S(1)}, bf16[8,3584]{1,0:T(8,128)(2,1)S(1)}, u32[]{:S(2)}, u32[]{:S(2)}) collective-permute-start(bf16[8,3584]{1,0:T(8,128)(2,1)S(1)} %fusion.5), channel_id=1, source_target_pairs={{0,2},{1,3},{2,0},{3,1},{4,6},{5,7},{6,4},{7,5},{8,10},{9,11},{10,... | collective-permute-start | bytes 172040 | tf_op jit(solution)/shard_map/ppermute | solution.py:404

commit v21 on v20

--- a/solution.py
+++ b/solution.py
@@ -461,7 +461,8 @@
 
     outs = pair_rows(place, own, other, gate, up, second, down, late_rows, share)
 
-    totals = [[own, flipped(other, CORE, CORE)] for own, other in zip(outs[:2], outs[2:])]
+    swapped = flipped(outs[2], CORE, CORE)
+    totals = [[outs[0], swapped], [outs[1], flipped(after(outs[3], swapped), CORE, CORE)]]
     for phase in SCATTER:
         for i, bits in enumerate(phase):
             total = totals[i]

time: 55.3 us -> 54.7 us (0.989)
  starting transfers between devices: 24.2 us -> 23.6 us
    ppermute x16, starting transfers between devices: 24.2 us -> 23.6 us  [flipped(): return lax.ppermute(value, ('node', 'local'), pairs)]
  transfers between devices with their start and end apart: 16 -> 16, of which waited for: 8 -> 9; matrix products, arithmetic and copies ran while one was open for 1% -> 1% of each run, Pallas kernels for 20% -> 21%
where the time goes in v21:
time: 54.7 us; the launch traced here: 54.5 us
  starting transfers between devices  23.6 us (43%)
  Pallas kernels  15.2 us (28%)
  waiting for transfers between devices  14.1 us (26%)
  other arithmetic  1.31 us (2%)
    ppermute x16, starting transfers between devices, flipped(): return lax.ppermute(value, ('node', 'local'), pairs)  23.6 us
    ppermute x16, waiting for transfers between devices, flipped(): return lax.ppermute(value, ('node', 'local'), pairs)  14.1 us
    pallas_call x1, Pallas kernels, load_both(): pl.pallas_call(functools.partial(load_both_kernel, share, lower), in_spec...  5.08 us
    pallas_call x1, Pallas kernels, load_first(): pl.pallas_call(functools.partial(load_first_kernel, share, lower), in_spe...  4 us
    pallas_call x1, Pallas kernels, pair_rows(): pl.pallas_call(functools.partial(early_half_kernel, share), in_specs=[SME...  2.47 us
    pallas_call x1, Pallas kernels, pair_rows(): pl.pallas_call(late_half_kernel, in_specs=[SMEM_SPEC] + [VMEM_SPEC] * 4,...  1.68 us
  transfers between devices with their start and end apart: 16, of which 9 were waited for; matrix products, arithmetic and copies ran while one was open for 1% of the time, Pallas kernels for 21%

profile of v21, /device:TPU:0, one launch (start us, length us, event | category | flops | bytes accessed | tf_op | source)
XLA Modules:
  0.0 54.5 jit_solution(15578811957972069718)
XLA Ops:
  0.0 1.1 %pack_rows.1 = bf16[8,7296]{1,0:T(8,128)(2,1)S(1)} custom-call(bf16[8,7168]{1,0:T(8,128)(2,1)} %tokens_ref.1, s32[4,8]{1,0:T(4,128)} %bitcast.12, bf16[4,8]{1,0:T(4,128)(2,1)} %bitcast.13), custom_call_target="tpu_custom_call" | custom-call | tf_op jit(solution)/shard_map/pack_rows/pallas_call | solution.py:48
  1.1 3.0 %collective-permute-start.2 = (bf16[8,3712]{1,0:T(8,128)(2,1)S(1)}, bf16[8,3712]{1,0:T(8,128)(2,1)S(1)}, u32[]{:S(2)}, u32[]{:S(2)}) collective-permute-start(bf16[8,3712]{1,0:T(8,128)(2,1)S(1)} %get-tuple-element.60), channel_id=1, source_target_pairs={{0,8},{1,9},{2,10},{3,11},{4,6},{5,7},{6,4},{7,5},{8,0},{9,1},{10,... | collective-permute-start | bytes 178184 | tf_op jit(solution)/shard_map/ppermute | solution.py:404
  4.1 2.7 %collective-permute-start = (bf16[8,3584]{1,0:T(8,128)(2,1)S(1)}, bf16[8,3584]{1,0:T(8,128)(2,1)S(1)}, u32[]{:S(2)}, u32[]{:S(2)}) collective-permute-start(bf16[8,3584]{1,0:T(8,128)(2,1)S(1)} %get-tuple-element.61), channel_id=1, source_target_pairs={{0,2},{1,3},{2,0},{3,1},{4,12},{5,13},{6,14},{7,15},{8,10},{9,11},... | collective-permute-start | bytes 172040 | tf_op jit(solution)/shard_map/ppermute | solution.py:404
  6.8 0.0 collective-permute-done.2
  6.8 2.7 %collective-permute-start.3 = (bf16[16,3712]{1,0:T(8,128)(2,1)S(1)}, bf16[16,3712]{1,0:T(8,128)(2,1)S(1)}, u32[]{:S(2)}, u32[]{:S(2)}) collective-permute-start(bf16[16,3712]{1,0:T(8,128)(2,1)S(1)} %pad_maximum_fusion.2), channel_id=1, source_target_pairs={{0,2},{1,3},{2,0},{3,1},{4,5},{5,4},{6,7},{7,6},{8,10},{9,11},{10,... | collective-permute-start | bytes 356360 | tf_op jit(solution)/shard_map/ppermute | solution.py:404
  9.5 0.0 collective-permute-done
  9.5 1.6 %collective-permute-start.1 = (bf16[16,3584]{1,0:T(8,128)(2,1)S(1)}, bf16[16,3584]{1,0:T(8,128)(2,1)S(1)}, u32[]{:S(2)}, u32[]{:S(2)}) collective-permute-start(bf16[16,3584]{1,0:T(8,128)(2,1)S(1)} %pad_maximum_fusion.3), channel_id=1, source_target_pairs={{0,1},{1,0},{2,3},{3,2},{4,6},{5,7},{6,4},{7,5},{8,9},{9,8},{10,11... | collective-permute-start | bytes 344072 | tf_op jit(solution)/shard_map/ppermute | solution.py:404
  11.1 4.0 %load_first.1 = (bf16[7168,640]{1,0:T(8,128)(2,1)S(1)}, bf16[128,3584]{1,0:T(8,128)(2,1)S(1)}) custom-call(s32[1]{0:T(128)} %bitcast.place_ref, bf16[7168,512]{1,0:T(8,128)(2,1)} %bitcast.10, bf16[7168,512]{1,0:T(8,128)(2,1)} %shared_ref.2, bf16[512,7168]{1,0:T(8,128)(2,1)} %sdown_ref.3), custom_call_target="tpu_custom_call" | custom-call | bytes 18350080 | tf_op jit(solution)/shard_map/load_first/pallas_call | solution.py:249
  15.1 0.0 collective-permute-done.1
  15.2 0.8 %collective-permute-done.3 = bf16[16,3712]{1,0:T(8,128)(2,1)S(1)} collective-permute-done((bf16[16,3712]{1,0:T(8,128)(2,1)S(1)}, bf16[16,3712]{1,0:T(8,128)(2,1)S(1)}, u32[]{:S(2)}, u32[]{:S(2)}) %collective-permute-start.3) | collective-permute-done | bytes 118816 | tf_op jit(solution)/shard_map/ppermute | solution.py:404
  15.9 1.6 %collective-permute-start.4 = (bf16[32,3584]{1,0:T(8,128)(2,1)S(1)}, bf16[32,3584]{1,0:T(8,128)(2,1)S(1)}, u32[]{:S(2)}, u32[]{:S(2)}) collective-permute-start(bf16[32,3584]{1,0:T(8,128)(2,1)S(1)} %pad_maximum_fusion.1), channel_id=1, source_target_pairs={{0,8},{1,9},{2,10},{3,11},{4,5},{5,4},{6,7},{7,6},{8,0},{9,1},{10,... | collective-permute-start | bytes 688136 | tf_op jit(solution)/shard_map/ppermute | solution.py:404
  17.6 0.9 %collective-permute-start.5 = (bf16[32,3712]{1,0:T(8,128)(2,1)S(1)}, bf16[32,3712]{1,0:T(8,128)(2,1)S(1)}, u32[]{:S(2)}, u32[]{:S(2)}) collective-permute-start(bf16[32,3712]{1,0:T(8,128)(2,1)S(1)} %pad_maximum_fusion), channel_id=1, source_target_pairs={{0,1},{1,0},{2,3},{3,2},{4,12},{5,13},{6,14},{7,15},{8,9},{9,8},{1... | collective-permute-start | bytes 712712 | tf_op jit(solution)/shard_map/ppermute | solution.py:404
  18.5 5.1 %load_both.1 = (bf16[7168,640]{1,0:T(8,128)(2,1)S(1)}, bf16[640,3584]{1,0:T(8,128)(2,1)S(1)}) custom-call(s32[1]{0:T(128)} %bitcast.place_ref, bf16[7168,512]{1,0:T(8,128)(2,1)} %bitcast.11, bf16[7168,512]{1,0:T(8,128)(2,1)} %shared_ref.3, bf16[512,7168]{1,0:T(8,128)(2,1)} %bitcast.6, bf16[512,7168]{1,0:T(8,128)(2,1)} %sdown_ref.3), custom_call_target="tpu_custom_call" | custom-call | bytes 27525120 | tf_op jit(solution)/shard_map/load_both/pallas_call | solution.py:223
  23.6 0.3 collective-permute-done.4
  23.9 0.0 collective-permute-done.5
  24.1 0.1 maximum_select_fusion.own_ref
  24.2 0.1 collective-permute-start.7
  24.3 0.1 maximum_select_fusion.1.own_ref
  24.4 0.6 %collective-permute-start.6 = (bf16[64,3584]{1,0:T(8,128)(2,1)S(1)}, bf16[64,3584]{1,0:T(8,128)(2,1)S(1)}, u32[]{:S(2)}, u32[]{:S(2)}) collective-permute-start(bf16[64,3584]{1,0:T(8,128)(2,1)S(1)} %maximum_select_fusion.1.own_ref), channel_id=1, source_target_pairs={{0,4},{1,5},{2,6},{3,7},{4,0},{5,1},{6,2},{7,3},{8,12},{9,13},{10,... | collective-permute-start | bytes 1376264 | tf_op jit(solution)/shard_map/ppermute | solution.py:404
  25.0 1.1 %collective-permute-done.7.other_ref = bf16[64,3712]{1,0:T(8,128)(2,1)S(1)} collective-permute-done((bf16[64,3712]{1,0:T(8,128)(2,1)S(1)}, bf16[64,3712]{1,0:T(8,128)(2,1)S(1)}, u32[]{:S(2)}, u32[]{:S(2)}) %collective-permute-start.7) | collective-permute-done | bytes 475168 | tf_op jit(solution)/shard_map/ppermute | solution.py:404
  26.1 0.0 slice-start
  26.2 1.7 %late_half.1 = (f32[128,640]{1,0:T(8,128)S(1)}, f32[128,640]{1,0:T(8,128)S(1)}, f32[128,128]{1,0:T(8,128)S(1)}) custom-call(s32[1]{0:T(128)} %bitcast.place_ref, bf16[64,3712]{1,0:T(8,128)(2,1)S(1)} %maximum_select_fusion.own_ref, bf16[64,3712]{1,0:T(8,128)(2,1)S(1)} %collective-permute-done.7.other_ref, bf16[7168,640]{1,0:T(8,128)(2,1)S(1)} %get-tuple-element.37.gate_ref, ...), custom_call_target="tpu_custom_call" | custom-call | flops 1174405120 | bytes 9175040 | tf_op jit(solution)/shard_map/late_half/pallas_call | solution.py:324
  27.8 0.0 collective-permute-done.6.other_ref
  27.9 0.0 slice-start.1
  27.9 2.5 %early_half.1 = (bf16[64,3584]{1,0:T(8,128)(2,1)S(1)}, bf16[64,3584]{1,0:T(8,128)(2,1)S(1)}, bf16[128,640]{1,0:T(8,128)(2,1)S(1)}) custom-call(s32[1]{0:T(128)} %bitcast.place_ref, bf16[64,3584]{1,0:T(8,128)(2,1)S(1)} %maximum_select_fusion.1.own_ref, bf16[64,3584]{1,0:T(8,128)(2,1)S(1)} %collective-permute-done.6.other_ref, ...), custom_call_target="tpu_custom_call" | custom-call | flops 1761607680 | bytes 13762560 | tf_op jit(solution)/shard_map/early_half/pallas_call | solution.py:334
  30.3 0.2 collective-permute-start.8
  30.6 0.0 slice-done
  30.6 0.0 slice-done.1
  30.6 0.9 %last_half.1 = (bf16[64,3584]{1,0:T(8,128)(2,1)S(1)}, bf16[64,3584]{1,0:T(8,128)(2,1)S(1)}) custom-call(bf16[128,640]{1,0:T(8,128)(2,1)S(1)} %get-tuple-element.46.act_ref, bf16[512,7168]{1,0:T(8,128)(2,1)S(1)} %bitcast.9, bf16[128,3584]{1,0:T(8,128)(2,1)S(1)} %get-tuple-element.47.rows_ref), custom_call_target="tpu_custom_call" | custom-call | flops 587202560 | bytes 4587520 | tf_op jit(solution)/shard_map/last_half/pallas_call | solution.py:348
  31.5 0.7 %collective-permute-done.8 = bf16[64,3584]{1,0:T(8,128)(2,1)S(1)} collective-permute-done((bf16[64,3584]{1,0:T(8,128)(2,1)S(1)}, bf16[64,3584]{1,0:T(8,128)(2,1)S(1)}, u32[]{:S(2)}, u32[]{:S(2)}) %collective-permute-start.8) | collective-permute-done | bytes 458784 | tf_op jit(solution)/shard_map/ppermute | solution.py:404
  32.2 0.1 collective-permute-start.12
  32.4 0.1 add_convert_fusion.1
  32.5 1.6 %collective-permute-start.9 = (bf16[32,3584]{1,0:T(8,128)(2,1)S(1)}, bf16[32,3584]{1,0:T(8,128)(2,1)S(1)}, u32[]{:S(2)}, u32[]{:S(2)}) collective-permute-start(bf16[32,3584]{1,0:T(8,128)(2,1)S(1)} %get-tuple-element.51), channel_id=1, source_target_pairs={{0,8},{1,9},{2,10},{3,11},{4,12},{5,13},{6,14},{7,15},{8,0},{9,1},... | collective-permute-start | bytes 688136 | tf_op jit(solution)/shard_map/ppermute | solution.py:404
  34.1 0.0 collective-permute-done.12
  34.1 0.1 add_convert_fusion
  34.2 1.3 %collective-permute-start.13 = (bf16[32,3584]{1,0:T(8,128)(2,1)S(1)}, bf16[32,3584]{1,0:T(8,128)(2,1)S(1)}, u32[]{:S(2)}, u32[]{:S(2)}) collective-permute-start(bf16[32,3584]{1,0:T(8,128)(2,1)S(1)} %get-tuple-element.53), channel_id=1, source_target_pairs={{0,1},{1,0},{2,3},{3,2},{4,5},{5,4},{6,7},{7,6},{8,9},{9,8},{10,11... | collective-permute-start | bytes 688136 | tf_op jit(solution)/shard_map/ppermute | solution.py:404
  35.5 4.9 %collective-permute-done.9 = bf16[32,3584]{1,0:T(8,128)(2,1)S(1)} collective-permute-done((bf16[32,3584]{1,0:T(8,128)(2,1)S(1)}, bf16[32,3584]{1,0:T(8,128)(2,1)S(1)}, u32[]{:S(2)}, u32[]{:S(2)}) %collective-permute-start.9) | collective-permute-done | bytes 229408 | tf_op jit(solution)/shard_map/ppermute | solution.py:404
  40.4 1.4 %collective-permute-start.10 = (bf16[16,3584]{1,0:T(8,128)(2,1)S(1)}, bf16[16,3584]{1,0:T(8,128)(2,1)S(1)}, u32[]{:S(2)}, u32[]{:S(2)}) collective-permute-start(bf16[16,3584]{1,0:T(8,128)(2,1)S(1)} %get-tuple-element.55), channel_id=1, source_target_pairs={{0,1},{1,0},{2,3},{3,2},{4,5},{5,4},{6,7},{7,6},{8,9},{9,8},{10,11... | collective-permute-start | bytes 344072 | tf_op jit(solution)/shard_map/ppermute | solution.py:404
  41.8 0.1 collective-permute-done.13
  41.9 1.6 %collective-permute-start.14 = (bf16[16,3584]{1,0:T(8,128)(2,1)S(1)}, bf16[16,3584]{1,0:T(8,128)(2,1)S(1)}, u32[]{:S(2)}, u32[]{:S(2)}) collective-permute-start(bf16[16,3584]{1,0:T(8,128)(2,1)S(1)} %get-tuple-element.57), channel_id=1, source_target_pairs={{0,8},{1,9},{2,10},{3,11},{4,12},{5,13},{6,14},{7,15},{8,0},{9,1},... | collective-permute-start | bytes 344072 | tf_op jit(solution)/shard_map/ppermute | solution.py:404
  43.5 1.8 %collective-permute-done.10 = bf16[16,3584]{1,0:T(8,128)(2,1)S(1)} collective-permute-done((bf16[16,3584]{1,0:T(8,128)(2,1)S(1)}, bf16[16,3584]{1,0:T(8,128)(2,1)S(1)}, u32[]{:S(2)}, u32[]{:S(2)}) %collective-permute-start.10) | collective-permute-done | bytes 114720 | tf_op jit(solution)/shard_map/ppermute | solution.py:404
  45.3 2.8 %collective-permute-start.11 = (bf16[8,3584]{1,0:T(8,128)(2,1)S(1)}, bf16[8,3584]{1,0:T(8,128)(2,1)S(1)}, u32[]{:S(2)}, u32[]{:S(2)}) collective-permute-start(bf16[8,3584]{1,0:T(8,128)(2,1)S(1)} %fusion.5), channel_id=1, source_target_pairs={{0,2},{1,3},{2,0},{3,1},{4,6},{5,7},{6,4},{7,5},{8,10},{9,11},{10,... | collective-permute-start | bytes 172040 | tf_op jit(solution)/shard_map/ppermute | solution.py:404
  48.1 0.0 collective-permute-done.14
  48.1 1.4 %collective-permute-start.15 = (bf16[8,3584]{1,0:T(8,128)(2,1)S(1)}, bf16[8,3584]{1,0:T(8,128)(2,1)S(1)}, u32[]{:S(2)}, u32[]{:S(2)}) collective-permute-start(bf16[8,3584]{1,0:T(8,128)(2,1)S(1)} %fusion.2), channel_id=1, source_target_pairs={{0,2},{1,3},{2,0},{3,1},{4,6},{5,7},{6,4},{7,5},{8,10},{9,11},{10,... | collective-permute-start | bytes 172040 | tf_op jit(solution)/shard_map/ppermute | solution.py:404
  49.5 2.7 %collective-permute-done.11 = bf16[8,3584]{1,0:T(8,128)(2,1)S(1)} collective-permute-done((bf16[8,3584]{1,0:T(8,128)(2,1)S(1)}, bf16[8,3584]{1,0:T(8,128)(2,1)S(1)}, u32[]{:S(2)}, u32[]{:S(2)}) %collective-permute-start.11) | collective-permute-done | bytes 57376 | tf_op jit(solution)/shard_map/ppermute | solution.py:404
  52.3 1.6 %collective-permute-done.15 = bf16[8,3584]{1,0:T(8,128)(2,1)S(1)} collective-permute-done((bf16[8,3584]{1,0:T(8,128)(2,1)S(1)}, bf16[8,3584]{1,0:T(8,128)(2,1)S(1)}, u32[]{:S(2)}, u32[]{:S(2)}) %collective-permute-start.15) | collective-permute-done | bytes 57376 | tf_op jit(solution)/shard_map/ppermute | solution.py:404
  53.9 0.7 %pad_maximum_fusion.4 = bf16[8,7168]{1,0:T(8,128)(2,1)} fusion(bf16[8,3584]{1,0:T(8,128)(2,1)S(1)} %fusion.4, bf16[8,3584]{1,0:T(8,128)(2,1)S(1)} %fusion.7), kind=kLoop, calls=%fused_computation.26 | loop fusion | flops 229376 | bytes 229376 | tf_op jit(solution)/shard_map/concatenate | solution.py:472
  (27 shorter events, 0.4 us)
Async XLA Ops:
  1.1 5.7 %collective-permute-start.2 = (bf16[8,3712]{1,0:T(8,128)(2,1)S(1)}, bf16[8,3712]{1,0:T(8,128)(2,1)S(1)}, u32[]{:S(2)}, u32[]{:S(2)}) collective-permute-start(bf16[8,3712]{1,0:T(8,128)(2,1)S(1)} %get-tuple-element.60), channel_id=1, source_target_pairs={{0,8},{1,9},{2,10},{3,11},{4,6},{5,7},{6,4},{7,5},{8,0},{9,1},{10,... | collective-permute-start | bytes 178184 | tf_op jit(solution)/shard_map/ppermute | solution.py:404
  4.1 5.4 %collective-permute-start = (bf16[8,3584]{1,0:T(8,128)(2,1)S(1)}, bf16[8,3584]{1,0:T(8,128)(2,1)S(1)}, u32[]{:S(2)}, u32[]{:S(2)}) collective-permute-start(bf16[8,3584]{1,0:T(8,128)(2,1)S(1)} %get-tuple-element.61), channel_id=1, source_target_pairs={{0,2},{1,3},{2,0},{3,1},{4,12},{5,13},{6,14},{7,15},{8,10},{9,11},... | collective-permute-start | bytes 172040 | tf_op jit(solution)/shard_map/ppermute | solution.py:404
  6.8 9.1 %collective-permute-start.3 = (bf16[16,3712]{1,0:T(8,128)(2,1)S(1)}, bf16[16,3712]{1,0:T(8,128)(2,1)S(1)}, u32[]{:S(2)}, u32[]{:S(2)}) collective-permute-start(bf16[16,3712]{1,0:T(8,128)(2,1)S(1)} %pad_maximum_fusion.2), channel_id=1, source_target_pairs={{0,2},{1,3},{2,0},{3,1},{4,5},{5,4},{6,7},{7,6},{8,10},{9,11},{10,... | collective-permute-start | bytes 356360 | tf_op jit(solution)/shard_map/ppermute | solution.py:404
  9.5 5.7 %collective-permute-start.1 = (bf16[16,3584]{1,0:T(8,128)(2,1)S(1)}, bf16[16,3584]{1,0:T(8,128)(2,1)S(1)}, u32[]{:S(2)}, u32[]{:S(2)}) collective-permute-start(bf16[16,3584]{1,0:T(8,128)(2,1)S(1)} %pad_maximum_fusion.3), channel_id=1, source_target_pairs={{0,1},{1,0},{2,3},{3,2},{4,6},{5,7},{6,4},{7,5},{8,9},{9,8},{10,11... | collective-permute-start | bytes 344072 | tf_op jit(solution)/shard_map/ppermute | solution.py:404
  15.9 8.0 %collective-permute-start.4 = (bf16[32,3584]{1,0:T(8,128)(2,1)S(1)}, bf16[32,3584]{1,0:T(8,128)(2,1)S(1)}, u32[]{:S(2)}, u32[]{:S(2)}) collective-permute-start(bf16[32,3584]{1,0:T(8,128)(2,1)S(1)} %pad_maximum_fusion.1), channel_id=1, source_target_pairs={{0,8},{1,9},{2,10},{3,11},{4,5},{5,4},{6,7},{7,6},{8,0},{9,1},{10,... | collective-permute-start | bytes 688136 | tf_op jit(solution)/shard_map/ppermute | solution.py:404
  17.6 6.3 %collective-permute-start.5 = (bf16[32,3712]{1,0:T(8,128)(2,1)S(1)}, bf16[32,3712]{1,0:T(8,128)(2,1)S(1)}, u32[]{:S(2)}, u32[]{:S(2)}) collective-permute-start(bf16[32,3712]{1,0:T(8,128)(2,1)S(1)} %pad_maximum_fusion), channel_id=1, source_target_pairs={{0,1},{1,0},{2,3},{3,2},{4,12},{5,13},{6,14},{7,15},{8,9},{9,8},{1... | collective-permute-start | bytes 712712 | tf_op jit(solution)/shard_map/ppermute | solution.py:404
  24.2 1.9 %collective-permute-start.7 = (bf16[64,3712]{1,0:T(8,128)(2,1)S(1)}, bf16[64,3712]{1,0:T(8,128)(2,1)S(1)}, u32[]{:S(2)}, u32[]{:S(2)}) collective-permute-start(bf16[64,3712]{1,0:T(8,128)(2,1)S(1)} %maximum_select_fusion.own_ref), channel_id=1, source_target_pairs={{0,4},{1,5},{2,6},{3,7},{4,0},{5,1},{6,2},{7,3},{8,12},{9,13},{10,... | collective-permute-start | bytes 1425416 | tf_op jit(solution)/shard_map/ppermute | solution.py:404
  24.4 3.4 %collective-permute-start.6 = (bf16[64,3584]{1,0:T(8,128)(2,1)S(1)}, bf16[64,3584]{1,0:T(8,128)(2,1)S(1)}, u32[]{:S(2)}, u32[]{:S(2)}) collective-permute-start(bf16[64,3584]{1,0:T(8,128)(2,1)S(1)} %maximum_select_fusion.1.own_ref), channel_id=1, source_target_pairs={{0,4},{1,5},{2,6},{3,7},{4,0},{5,1},{6,2},{7,3},{8,12},{9,13},{10,... | collective-permute-start | bytes 1376264 | tf_op jit(solution)/shard_map/ppermute | solution.py:404
  26.1 4.4 %slice-start = ((s8[7340032]{0:T(1024)(128)(4,1)}), s8[4194304]{0:T(1024)(128)(4,1)S(1)}, s32[]{:S(2)}) async-start(s8[7340032]{0:T(1024)(128)(4,1)} %bitcast.7), calls=%async_computation | async-start | bytes 8388608
  27.9 2.7 %slice-start.1 = ((s8[7340032]{0:T(1024)(128)(4,1)}), s8[3145728]{0:T(1024)(128)(4,1)S(1)}, s32[]{:S(2)}) async-start(s8[7340032]{0:T(1024)(128)(4,1)} %bitcast.7), calls=%async_computation.1 | async-start | bytes 6291456
  30.3 1.9 %collective-permute-start.8 = (bf16[64,3584]{1,0:T(8,128)(2,1)S(1)}, bf16[64,3584]{1,0:T(8,128)(2,1)S(1)}, u32[]{:S(2)}, u32[]{:S(2)}) collective-permute-start(bf16[64,3584]{1,0:T(8,128)(2,1)S(1)} %get-tuple-element.45), channel_id=1, source_target_pairs={{0,4},{1,5},{2,6},{3,7},{4,0},{5,1},{6,2},{7,3},{8,12},{9,13},{10,... | collective-permute-start | bytes 1376264 | tf_op jit(solution)/shard_map/ppermute | solution.py:404
  32.2 1.9 %collective-permute-start.12 = (bf16[64,3584]{1,0:T(8,128)(2,1)S(1)}, bf16[64,3584]{1,0:T(8,128)(2,1)S(1)}, u32[]{:S(2)}, u32[]{:S(2)}) collective-permute-start(bf16[64,3584]{1,0:T(8,128)(2,1)S(1)} %get-tuple-element.50), channel_id=1, source_target_pairs={{0,4},{1,5},{2,6},{3,7},{4,0},{5,1},{6,2},{7,3},{8,12},{9,13},{10,... | collective-permute-start | bytes 1376264 | tf_op jit(solution)/shard_map/ppermute | solution.py:404
  32.5 7.9 %collective-permute-start.9 = (bf16[32,3584]{1,0:T(8,128)(2,1)S(1)}, bf16[32,3584]{1,0:T(8,128)(2,1)S(1)}, u32[]{:S(2)}, u32[]{:S(2)}) collective-permute-start(bf16[32,3584]{1,0:T(8,128)(2,1)S(1)} %get-tuple-element.51), channel_id=1, source_target_pairs={{0,8},{1,9},{2,10},{3,11},{4,12},{5,13},{6,14},{7,15},{8,0},{9,1},... | collective-permute-start | bytes 688136 | tf_op jit(solution)/shard_map/ppermute | solution.py:404
  34.2 7.7 %collective-permute-start.13 = (bf16[32,3584]{1,0:T(8,128)(2,1)S(1)}, bf16[32,3584]{1,0:T(8,128)(2,1)S(1)}, u32[]{:S(2)}, u32[]{:S(2)}) collective-permute-start(bf16[32,3584]{1,0:T(8,128)(2,1)S(1)} %get-tuple-element.53), channel_id=1, source_target_pairs={{0,1},{1,0},{2,3},{3,2},{4,5},{5,4},{6,7},{7,6},{8,9},{9,8},{10,11... | collective-permute-start | bytes 688136 | tf_op jit(solution)/shard_map/ppermute | solution.py:404
  40.4 4.9 %collective-permute-start.10 = (bf16[16,3584]{1,0:T(8,128)(2,1)S(1)}, bf16[16,3584]{1,0:T(8,128)(2,1)S(1)}, u32[]{:S(2)}, u32[]{:S(2)}) collective-permute-start(bf16[16,3584]{1,0:T(8,128)(2,1)S(1)} %get-tuple-element.55), channel_id=1, source_target_pairs={{0,1},{1,0},{2,3},{3,2},{4,5},{5,4},{6,7},{7,6},{8,9},{9,8},{10,11... | collective-permute-start | bytes 344072 | tf_op jit(solution)/shard_map/ppermute | solution.py:404
  41.9 6.2 %collective-permute-start.14 = (bf16[16,3584]{1,0:T(8,128)(2,1)S(1)}, bf16[16,3584]{1,0:T(8,128)(2,1)S(1)}, u32[]{:S(2)}, u32[]{:S(2)}) collective-permute-start(bf16[16,3584]{1,0:T(8,128)(2,1)S(1)} %get-tuple-element.57), channel_id=1, source_target_pairs={{0,8},{1,9},{2,10},{3,11},{4,12},{5,13},{6,14},{7,15},{8,0},{9,1},... | collective-permute-start | bytes 344072 | tf_op jit(solution)/shard_map/ppermute | solution.py:404
  45.3 6.9 %collective-permute-start.11 = (bf16[8,3584]{1,0:T(8,128)(2,1)S(1)}, bf16[8,3584]{1,0:T(8,128)(2,1)S(1)}, u32[]{:S(2)}, u32[]{:S(2)}) collective-permute-start(bf16[8,3584]{1,0:T(8,128)(2,1)S(1)} %fusion.5), channel_id=1, source_target_pairs={{0,2},{1,3},{2,0},{3,1},{4,6},{5,7},{6,4},{7,5},{8,10},{9,11},{10,... | collective-permute-start | bytes 172040 | tf_op jit(solution)/shard_map/ppermute | solution.py:404
  48.1 5.8 %collective-permute-start.15 = (bf16[8,3584]{1,0:T(8,128)(2,1)S(1)}, bf16[8,3584]{1,0:T(8,128)(2,1)S(1)}, u32[]{:S(2)}, u32[]{:S(2)}) collective-permute-start(bf16[8,3584]{1,0:T(8,128)(2,1)S(1)} %fusion.2), channel_id=1, source_target_pairs={{0,2},{1,3},{2,0},{3,1},{4,6},{5,7},{6,4},{7,5},{8,10},{9,11},{10,... | collective-permute-start | bytes 172040 | tf_op jit(solution)/shard_map/ppermute | solution.py:404

commit v22 on v20

--- a/solution.py
+++ b/solution.py
@@ -53,16 +53,17 @@
     )(tokens, group_ids.T, route_weights.T)
 
 
-def weight_copies(share, place_ref, routed_ref, shared_ref, out_ref, sems, parts):
-    width, hidden = routed_ref.shape
+def weight_copies(share, place_ref, routed_ref, shared_ref, out_ref, sems, parts, first_row=0):
+    hidden = routed_ref.shape[1]
     column = pl.multiple_of((place_ref[0] // share) * LANES, LANES)
-    piece = width // parts
+    piece = out_ref.shape[0] // parts
     copies = []
     for i in range(parts):
         at = pl.ds(i * piece, piece)
+        rows = pl.ds(first_row + i * piece, piece)
         for source, lower, size in (
-            (routed_ref.at[at, :], 0, hidden),
-            (shared_ref.at[at, pl.ds(column, LANES)], hidden, LANES),
+            (routed_ref.at[rows, :], 0, hidden),
+            (shared_ref.at[rows, pl.ds(column, LANES)], hidden, LANES),
         ):
             copies.append(
                 pltpu.make_async_copy(source, out_ref.at[at, pl.ds(lower, size)], sems.at[len(copies)])
@@ -70,15 +71,19 @@
     return copies
 
 
-def load_kernel(share, place_ref, routed_ref, shared_ref, out_ref, sems):
-    run_copies(weight_copies(share, place_ref, routed_ref, shared_ref, out_ref, sems, sems.shape[0] // 2))
-
-
-def load_weights(place, routed, shared, share):
+def load_kernel(share, first_row, place_ref, routed_ref, shared_ref, out_ref, sems):
+    run_copies(
+        weight_copies(
+            share, place_ref, routed_ref, shared_ref, out_ref, sems, sems.shape[0] // 2, first_row
+        )
+    )
+
+
+def load_weights(place, routed, shared, share, first_row=0, rows=None):
     width, hidden = routed.shape
-    shape = (width, hidden + LANES)
+    shape = (width if rows is None else rows, hidden + LANES)
     return pl.pallas_call(
-        functools.partial(load_kernel, share),
+        functools.partial(load_kernel, share, first_row),
         in_specs=[SMEM_SPEC] + [ANY_SPEC] * 2,
         out_specs=VMEM_SPEC,
         out_shape=pltpu.VMEM(shape, BF16),
@@ -169,18 +174,6 @@
         store(at, jnp.dot(act[...], second[:, at], preferred_element_type=F32))
 
 
-def regroup(value, outer, inner):
-    rows = value.shape[0] // (outer * inner)
-    return jnp.concatenate(
-        [
-            value[(o * inner + i) * rows : (o * inner + i + 1) * rows]
-            for i in range(inner)
-            for o in range(outer)
-        ],
-        axis=0,
-    )
-
-
 def swap_quarters(value):
     quarter = value.shape[0] // 4
     return jnp.concatenate([value[i * quarter : (i + 1) * quarter] for i in (0, 2, 1, 3)], axis=0)
@@ -244,8 +237,7 @@
 
 
 def load_first(place, routed, shared, sdown, lower, share):
-    width, hidden = routed.shape
-    units = hidden + LANES
+    width, units = lower, routed.shape[1] + LANES
     return pl.pallas_call(
         functools.partial(load_first_kernel, share, lower),
         in_specs=[SMEM_SPEC] + [ANY_SPEC] * 3,
@@ -259,14 +251,14 @@
 
 
 def late_half_kernel(place_ref, own_ref, other_ref, gate_ref, up_ref, gate_acc_ref, up_acc_ref, weight_ref, x):
-    width, units = gate_ref.shape
+    width, units = up_ref.shape
     half, columns = own_ref.shape
     cut = width + LANES - columns
     x[:half, :] = own_ref[...]
     x[half:, :] = other_ref[...]
     rows = x[:, : width - cut]
     for at in tiles_of(units):
-        gate_acc_ref[:, at] = jnp.dot(rows, gate_ref[cut:, at], preferred_element_type=F32)
+        gate_acc_ref[:, at] = jnp.dot(rows, gate_ref[:, at], preferred_element_type=F32)
         up_acc_ref[:, at] = jnp.dot(rows, up_ref[cut:, at], preferred_element_type=F32)
     weight = row_weight(place_ref[0], x[:, width - cut :])
     weight_ref[...] = jnp.broadcast_to(weight, weight_ref.shape)
@@ -284,7 +276,7 @@
     rows = x[...]
     weight = weight_ref[:, :1]
     for at in tiles_of(units):
-        gate = gate_acc_ref[:, at] + jnp.dot(rows, gate_ref[:cut, at], preferred_element_type=F32)
+        gate = gate_acc_ref[:, at] + jnp.dot(rows, gate_ref[:, at], preferred_element_type=F32)
         up = up_acc_ref[:, at] + jnp.dot(rows, up_ref[:cut, at], preferred_element_type=F32)
         if at.start < hidden:
             act_ref[:, at] = (silu(gate) * up * weight).astype(BF16)
@@ -318,9 +310,9 @@
     )
 
 
-def pair_rows(place, own, other, gate, up, second, down, rows, share):
+def pair_rows(place, own, other, gate, late_gate, up, second, down, rows, share):
     half, cut = own[0].shape
-    width, units = gate.shape
+    width, units = up.shape
     partial = pl.pallas_call(
         late_half_kernel,
         in_specs=[SMEM_SPEC] + [VMEM_SPEC] * 4,
@@ -330,7 +322,7 @@
         cost_estimate=estimate(2 * half, width - cut, 2 * units),
         compiler_params=pltpu.CompilerParams(vmem_limit_bytes=10 << 20),
         name="late_half",
-    )(place, own[1], other[1], gate, up)
+    )(place, own[1], other[1], late_gate, up)
     own_out, other_out, act = pl.pallas_call(
         functools.partial(early_half_kernel, share),
         in_specs=[SMEM_SPEC] + [VMEM_SPEC] * 8,
@@ -395,18 +387,14 @@
     return functools.reduce(lambda a, b: a + b, (t.astype(F32) for t in terms))
 
 
-def flipped(value, even, odd):
-    pairs = []
-    for node in range(4):
-        for local in range(4):
-            node_bits, local_bits = odd if node % 2 else even
-            pairs.append((node * 4 + local, (node ^ node_bits) * 4 + (local ^ local_bits)))
-    return lax.ppermute(value, ("node", "local"), pairs)
+def flipped(value, bits):
+    axis = 0 if bits[0] else 1
+    return lax.ppermute(value, ("node", "local")[axis], [(i, i ^ bits[axis]) for i in range(4)])
 
 
 X, Z1, Z2, CORE = (2, 0), (0, 1), (0, 2), (1, 0)
-GATHER = ((Z2, X), (Z1, Z2), (X, Z1))
-SCATTER = ((X, Z1), (Z1, X), (Z2, Z2))
+GATHER = ((Z2, Z2), (Z1, X), (X, Z1))
+SCATTER = GATHER[::-1]
 
 
 def stack(*values):
@@ -442,32 +430,34 @@
     cut = width // 2
     own = [packed[:, :cut], packed[:, cut:]]
     loads = (
-        lambda *ready: (),
+        lambda *ready: (load_weights(after(place, *ready), gate, gate_shared, share, cut, width - cut),),
         lambda *ready: load_first(after(place, *ready), gate, gate_shared, down_shared, cut, share),
         lambda *ready: load_both(after(place, *ready), up, up_shared, down, down_shared, 0, cut, share),
     )
     loaded = ()
-    for phase, load in zip(GATHER, loads):
-        got = [flipped(part, *pairs) for part, pairs in zip(own, (phase, phase[::-1]))]
+    for number, (phase, load) in enumerate(zip(GATHER, loads)):
+        got = [flipped(part, bits) for part, bits in zip(own, phase)]
         weights = tuple(load(*own))
-        if weights:
+        if number == 0:
+            got[1], weights = lax.optimization_barrier((got[1], weights))
+        else:
             got, weights = lax.optimization_barrier((got, weights))
         loaded += weights
         own = [stack(part, add) for part, add in zip(own, got)]
-    gate, late_rows, up, second = loaded
-    odd = place[0] % 2
-    own = [jnp.where(odd == i, part, regroup(part, 4, 2)) for i, part in enumerate(own)]
-    other = [flipped(part, CORE, CORE) for part in own]
-
-    outs = pair_rows(place, own, other, gate, up, second, down, late_rows, share)
-
-    totals = [[own, flipped(other, CORE, CORE)] for own, other in zip(outs[:2], outs[2:])]
+    late_gate, gate, late_rows, up, second = loaded
+    own[1] = swap_quarters(own[1])
+    other = [flipped(part, CORE) for part in own]
+
+    outs = pair_rows(place, own, other, gate, late_gate, up, second, down, late_rows, share)
+
+    swapped = flipped(outs[2], CORE)
+    totals = [[outs[0], swapped], [outs[1], flipped(after(outs[3], swapped), CORE)]]
     for phase in SCATTER:
         for i, bits in enumerate(phase):
             total = totals[i]
             half = total[0].shape[0] // 2
             sent = f32_sum(*(t[half:] for t in total)).astype(BF16)
-            totals[i] = [f32_sum(*(t[:half] for t in total)), flipped(sent, bits, bits)]
+            totals[i] = [f32_sum(*(t[:half] for t in total)), flipped(sent, bits)]
     return jnp.concatenate([f32_sum(*total).astype(BF16) for total in totals], axis=1)
 
 

time: 55.3 us -> 54.5 us (0.986)
  starting transfers between devices: 24.2 us -> 20.9 us
  waiting for transfers between devices: 14 us -> 15.9 us
  Pallas kernels: 15.2 us -> 16.2 us
    ppermute x16, starting transfers between devices: 24.2 us -> 20.9 us  [flipped(): lax.ppermute(value, ('node', 'local')[axis], [(i, i ^ bits[axis]) for i i...]
    pallas_call x0 -> x1, Pallas kernels: none -> 2.34 us  [load_weights(): pl.pallas_call(functools.partial(load_kernel, share, first_row), in_specs...]
    ppermute x16, waiting for transfers between devices: 14 us -> 15.9 us  [flipped(): lax.ppermute(value, ('node', 'local')[axis], [(i, i ^ bits[axis]) for i i...]
    pallas_call x1, Pallas kernels: 4 us -> 2.67 us  [load_first(): pl.pallas_call(functools.partial(load_first_kernel, share, lower), in_spe...]
  transfers between devices with their start and end apart: 16 -> 16, of which waited for: 8 -> 11; matrix products, arithmetic and copies ran while one was open for 1% -> 1% of each run, Pallas kernels for 20% -> 23%
where the time goes in v22:
time: 54.5 us; the launch traced here: 54.4 us
  starting transfers between devices  20.9 us (38%)
  Pallas kernels  16.2 us (30%)
  waiting for transfers between devices  15.9 us (29%)
  other arithmetic  1.12 us (2%)
    ppermute x16, starting transfers between devices, flipped(): lax.ppermute(value, ('node', 'local')[axis], [(i, i ^ bits[axis]) for i i...  20.9 us
    ppermute x16, waiting for transfers between devices, flipped(): lax.ppermute(value, ('node', 'local')[axis], [(i, i ^ bits[axis]) for i i...  15.9 us
    pallas_call x1, Pallas kernels, load_both(): pl.pallas_call(functools.partial(load_both_kernel, share, lower), in_spec...  5.08 us
    pallas_call x1, Pallas kernels, load_first(): pl.pallas_call(functools.partial(load_first_kernel, share, lower), in_spe...  2.67 us
    pallas_call x1, Pallas kernels, pair_rows(): pl.pallas_call(functools.partial(early_half_kernel, share), in_specs=[SME...  2.47 us
    pallas_call x1, Pallas kernels, load_weights(): pl.pallas_call(functools.partial(load_kernel, share, first_row), in_specs...  2.34 us
    pallas_call x1, Pallas kernels, pair_rows(): pl.pallas_call(late_half_kernel, in_specs=[SMEM_SPEC] + [VMEM_SPEC] * 4,...  1.68 us
  transfers between devices with their start and end apart: 16, of which 11 were waited for; matrix products, arithmetic and copies ran while one was open for 1% of the time, Pallas kernels for 23%

profile of v22, /device:TPU:0, one launch (start us, length us, event | category | flops | bytes accessed | tf_op | source)
XLA Modules:
  0.0 54.4 jit_solution(14391412803449868754)
XLA Ops:
  0.0 1.1 %pack_rows.1 = bf16[8,7296]{1,0:T(8,128)(2,1)S(1)} custom-call(bf16[8,7168]{1,0:T(8,128)(2,1)} %tokens_ref.1, s32[4,8]{1,0:T(4,128)} %bitcast.13, bf16[4,8]{1,0:T(4,128)(2,1)} %bitcast.14), custom_call_target="tpu_custom_call" | custom-call | tf_op jit(solution)/shard_map/pack_rows/pallas_call | solution.py:48
  1.1 4.1 %collective-permute-start.2 = (bf16[8,3712]{1,0:T(8,128)(2,1)S(1)}, bf16[8,3712]{1,0:T(8,128)(2,1)S(1)}, u32[]{:S(2)}, u32[]{:S(2)}) collective-permute-start(bf16[8,3712]{1,0:T(8,128)(2,1)S(1)} %get-tuple-element.66), channel_id=1, source_target_pairs={{0,2},{1,3},{2,0},{3,1},{4,6},{5,7},{6,4},{7,5},{8,10},{9,11},{10,... | collective-permute-start | bytes 178184 | tf_op jit(solution)/shard_map/ppermute | solution.py:392
  5.2 0.1 collective-permute-start
  5.3 2.3 %load_weights.1.gate_ref = bf16[3584,640]{1,0:T(8,128)(2,1)S(1)} custom-call(s32[1]{0:T(128)} %bitcast.place_ref, bf16[7168,512]{1,0:T(8,128)(2,1)} %bitcast.10, bf16[7168,512]{1,0:T(8,128)(2,1)} %shared_ref.4), custom_call_target="tpu_custom_call" | custom-call | bytes 9175040 | tf_op jit(solution)/shard_map/load_weights/pallas_call | solution.py:85
  7.6 0.4 collective-permute-done.2
  8.0 2.4 %collective-permute-start.3 = (bf16[16,3712]{1,0:T(8,128)(2,1)S(1)}, bf16[16,3712]{1,0:T(8,128)(2,1)S(1)}, u32[]{:S(2)}, u32[]{:S(2)}) collective-permute-start(bf16[16,3712]{1,0:T(8,128)(2,1)S(1)} %pad_maximum_fusion.3), channel_id=1, source_target_pairs={{0,8},{4,12},{8,0},{12,4},{1,9},{5,13},{9,1},{13,5},{2,10},{6,14},... | collective-permute-start | bytes 356360 | tf_op jit(solution)/shard_map/ppermute | solution.py:392
  10.4 0.1 collective-permute-done
  10.6 1.5 %collective-permute-start.1 = (bf16[16,3584]{1,0:T(8,128)(2,1)S(1)}, bf16[16,3584]{1,0:T(8,128)(2,1)S(1)}, u32[]{:S(2)}, u32[]{:S(2)}) collective-permute-start(bf16[16,3584]{1,0:T(8,128)(2,1)S(1)} %pad_maximum_fusion.4), channel_id=1, source_target_pairs={{0,1},{1,0},{2,3},{3,2},{4,5},{5,4},{6,7},{7,6},{8,9},{9,8},{10,11... | collective-permute-start | bytes 344072 | tf_op jit(solution)/shard_map/ppermute | solution.py:392
  12.1 2.7 %load_first.1 = (bf16[3584,640]{1,0:T(8,128)(2,1)S(1)}, bf16[128,3584]{1,0:T(8,128)(2,1)S(1)}) custom-call(s32[1]{0:T(128)} %bitcast.place_ref, bf16[7168,512]{1,0:T(8,128)(2,1)} %bitcast.11, bf16[7168,512]{1,0:T(8,128)(2,1)} %shared_ref.4, bf16[512,7168]{1,0:T(8,128)(2,1)} %sdown_ref.3), custom_call_target="tpu_custom_call" | custom-call | bytes 9175040 | tf_op jit(solution)/shard_map/load_first/pallas_call | solution.py:241
  14.8 0.6 %collective-permute-done.1 = bf16[16,3584]{1,0:T(8,128)(2,1)S(1)} collective-permute-done((bf16[16,3584]{1,0:T(8,128)(2,1)S(1)}, bf16[16,3584]{1,0:T(8,128)(2,1)S(1)}, u32[]{:S(2)}, u32[]{:S(2)}) %collective-permute-start.1) | collective-permute-done | bytes 114720 | tf_op jit(solution)/shard_map/ppermute | solution.py:392
  15.4 0.0 collective-permute-done.3
  15.5 1.5 %collective-permute-start.5 = (bf16[32,3712]{1,0:T(8,128)(2,1)S(1)}, bf16[32,3712]{1,0:T(8,128)(2,1)S(1)}, u32[]{:S(2)}, u32[]{:S(2)}) collective-permute-start(bf16[32,3712]{1,0:T(8,128)(2,1)S(1)} %pad_maximum_fusion.1), channel_id=1, source_target_pairs={{0,1},{1,0},{2,3},{3,2},{4,5},{5,4},{6,7},{7,6},{8,9},{9,8},{10,11... | collective-permute-start | bytes 712712 | tf_op jit(solution)/shard_map/ppermute | solution.py:392
  17.0 1.4 %collective-permute-start.4 = (bf16[32,3584]{1,0:T(8,128)(2,1)S(1)}, bf16[32,3584]{1,0:T(8,128)(2,1)S(1)}, u32[]{:S(2)}, u32[]{:S(2)}) collective-permute-start(bf16[32,3584]{1,0:T(8,128)(2,1)S(1)} %pad_maximum_fusion.2), channel_id=1, source_target_pairs={{0,8},{4,12},{8,0},{12,4},{1,9},{5,13},{9,1},{13,5},{2,10},{6,14},... | collective-permute-start | bytes 688136 | tf_op jit(solution)/shard_map/ppermute | solution.py:392
  18.4 5.1 %load_both.1 = (bf16[7168,640]{1,0:T(8,128)(2,1)S(1)}, bf16[640,3584]{1,0:T(8,128)(2,1)S(1)}) custom-call(s32[1]{0:T(128)} %bitcast.place_ref, bf16[7168,512]{1,0:T(8,128)(2,1)} %bitcast.12, bf16[7168,512]{1,0:T(8,128)(2,1)} %shared_ref.5, bf16[512,7168]{1,0:T(8,128)(2,1)} %bitcast.6, bf16[512,7168]{1,0:T(8,128)(2,1)} %sdown_ref.3), custom_call_target="tpu_custom_call" | custom-call | bytes 27525120 | tf_op jit(solution)/shard_map/load_both/pallas_call | solution.py:216
  23.5 0.0 collective-permute-done.4
  23.5 0.0 collective-permute-done.5
  23.6 0.1 collective-permute-start.7
  23.7 0.6 %collective-permute-start.6 = (bf16[64,3584]{1,0:T(8,128)(2,1)S(1)}, bf16[64,3584]{1,0:T(8,128)(2,1)S(1)}, u32[]{:S(2)}, u32[]{:S(2)}) collective-permute-start(bf16[64,3584]{1,0:T(8,128)(2,1)S(1)} %pad_maximum_fusion.own_ref), channel_id=1, source_target_pairs={{0,4},{4,0},{8,12},{12,8},{1,5},{5,1},{9,13},{13,9},{2,6},{6,2},{1... | collective-permute-start | bytes 1376264 | tf_op jit(solution)/shard_map/ppermute | solution.py:392
  24.3 1.2 %collective-permute-done.7.other_ref = bf16[64,3712]{1,0:T(8,128)(2,1)S(1)} collective-permute-done((bf16[64,3712]{1,0:T(8,128)(2,1)S(1)}, bf16[64,3712]{1,0:T(8,128)(2,1)S(1)}, u32[]{:S(2)}, u32[]{:S(2)}) %collective-permute-start.7) | collective-permute-done | bytes 475168 | tf_op jit(solution)/shard_map/ppermute | solution.py:392
  25.5 0.0 slice-start
  25.5 1.7 %late_half.1 = (f32[128,640]{1,0:T(8,128)S(1)}, f32[128,640]{1,0:T(8,128)S(1)}, f32[128,128]{1,0:T(8,128)S(1)}) custom-call(s32[1]{0:T(128)} %bitcast.place_ref, bf16[64,3712]{1,0:T(8,128)(2,1)S(1)} %slice_dynamic-update-slice_fusion.own_ref, bf16[64,3712]{1,0:T(8,128)(2,1)S(1)} %collective-permute-done.7.other_ref, ...), custom_call_target="tpu_custom_call" | custom-call | flops 1174405120 | bytes 9175040 | tf_op jit(solution)/shard_map/late_half/pallas_call | solution.py:316
  27.2 0.0 collective-permute-done.6.other_ref
  27.2 0.0 slice-start.1
  27.2 2.5 %early_half.1 = (bf16[64,3584]{1,0:T(8,128)(2,1)S(1)}, bf16[64,3584]{1,0:T(8,128)(2,1)S(1)}, bf16[128,640]{1,0:T(8,128)(2,1)S(1)}) custom-call(s32[1]{0:T(128)} %bitcast.place_ref, bf16[64,3584]{1,0:T(8,128)(2,1)S(1)} %pad_maximum_fusion.own_ref, bf16[64,3584]{1,0:T(8,128)(2,1)S(1)} %collective-permute-done.6.other_ref, ...), custom_call_target="tpu_custom_call" | custom-call | flops 1761607680 | bytes 13762560 | tf_op jit(solution)/shard_map/early_half/pallas_call | solution.py:326
  29.7 0.2 collective-permute-start.8
  29.9 0.0 slice-done
  29.9 0.0 slice-done.1
  29.9 0.9 %last_half.1 = (bf16[64,3584]{1,0:T(8,128)(2,1)S(1)}, bf16[64,3584]{1,0:T(8,128)(2,1)S(1)}) custom-call(bf16[128,640]{1,0:T(8,128)(2,1)S(1)} %get-tuple-element.52.act_ref, bf16[512,7168]{1,0:T(8,128)(2,1)S(1)} %bitcast.9, bf16[128,3584]{1,0:T(8,128)(2,1)S(1)} %get-tuple-element.53.rows_ref), custom_call_target="tpu_custom_call" | custom-call | flops 587202560 | bytes 4587520 | tf_op jit(solution)/shard_map/last_half/pallas_call | solution.py:340
  30.8 0.8 %collective-permute-done.8 = bf16[64,3584]{1,0:T(8,128)(2,1)S(1)} collective-permute-done((bf16[64,3584]{1,0:T(8,128)(2,1)S(1)}, bf16[64,3584]{1,0:T(8,128)(2,1)S(1)}, u32[]{:S(2)}, u32[]{:S(2)}) %collective-permute-start.8) | collective-permute-done | bytes 458784 | tf_op jit(solution)/shard_map/ppermute | solution.py:392
  31.6 0.1 collective-permute-start.12
  31.7 0.1 add_convert_fusion.1
  31.8 1.1 %collective-permute-start.9 = (bf16[32,3584]{1,0:T(8,128)(2,1)S(1)}, bf16[32,3584]{1,0:T(8,128)(2,1)S(1)}, u32[]{:S(2)}, u32[]{:S(2)}) collective-permute-start(bf16[32,3584]{1,0:T(8,128)(2,1)S(1)} %get-tuple-element.57), channel_id=1, source_target_pairs={{0,8},{4,12},{8,0},{12,4},{1,9},{5,13},{9,1},{13,5},{2,10},{6,14},... | collective-permute-start | bytes 688136 | tf_op jit(solution)/shard_map/ppermute | solution.py:392
  32.9 0.5 collective-permute-done.12
  33.4 0.1 add_convert_fusion
  33.5 0.9 %collective-permute-start.13 = (bf16[32,3584]{1,0:T(8,128)(2,1)S(1)}, bf16[32,3584]{1,0:T(8,128)(2,1)S(1)}, u32[]{:S(2)}, u32[]{:S(2)}) collective-permute-start(bf16[32,3584]{1,0:T(8,128)(2,1)S(1)} %get-tuple-element.59), channel_id=1, source_target_pairs={{0,1},{1,0},{2,3},{3,2},{4,5},{5,4},{6,7},{7,6},{8,9},{9,8},{10,11... | collective-permute-start | bytes 688136 | tf_op jit(solution)/shard_map/ppermute | solution.py:392
  34.4 5.4 %collective-permute-done.9 = bf16[32,3584]{1,0:T(8,128)(2,1)S(1)} collective-permute-done((bf16[32,3584]{1,0:T(8,128)(2,1)S(1)}, bf16[32,3584]{1,0:T(8,128)(2,1)S(1)}, u32[]{:S(2)}, u32[]{:S(2)}) %collective-permute-start.9) | collective-permute-done | bytes 229408 | tf_op jit(solution)/shard_map/ppermute | solution.py:392
  39.8 0.9 %collective-permute-start.10 = (bf16[16,3584]{1,0:T(8,128)(2,1)S(1)}, bf16[16,3584]{1,0:T(8,128)(2,1)S(1)}, u32[]{:S(2)}, u32[]{:S(2)}) collective-permute-start(bf16[16,3584]{1,0:T(8,128)(2,1)S(1)} %get-tuple-element.61), channel_id=1, source_target_pairs={{0,1},{1,0},{2,3},{3,2},{4,5},{5,4},{6,7},{7,6},{8,9},{9,8},{10,11... | collective-permute-start | bytes 344072 | tf_op jit(solution)/shard_map/ppermute | solution.py:392
  40.7 0.5 collective-permute-done.13
  41.3 1.1 %collective-permute-start.14 = (bf16[16,3584]{1,0:T(8,128)(2,1)S(1)}, bf16[16,3584]{1,0:T(8,128)(2,1)S(1)}, u32[]{:S(2)}, u32[]{:S(2)}) collective-permute-start(bf16[16,3584]{1,0:T(8,128)(2,1)S(1)} %get-tuple-element.63), channel_id=1, source_target_pairs={{0,8},{4,12},{8,0},{12,4},{1,9},{5,13},{9,1},{13,5},{2,10},{6,14},... | collective-permute-start | bytes 344072 | tf_op jit(solution)/shard_map/ppermute | solution.py:392
  42.3 2.4 %collective-permute-done.10 = bf16[16,3584]{1,0:T(8,128)(2,1)S(1)} collective-permute-done((bf16[16,3584]{1,0:T(8,128)(2,1)S(1)}, bf16[16,3584]{1,0:T(8,128)(2,1)S(1)}, u32[]{:S(2)}, u32[]{:S(2)}) %collective-permute-start.10) | collective-permute-done | bytes 114720 | tf_op jit(solution)/shard_map/ppermute | solution.py:392
  44.7 3.8 %collective-permute-start.11 = (bf16[8,3584]{1,0:T(8,128)(2,1)S(1)}, bf16[8,3584]{1,0:T(8,128)(2,1)S(1)}, u32[]{:S(2)}, u32[]{:S(2)}) collective-permute-start(bf16[8,3584]{1,0:T(8,128)(2,1)S(1)} %fusion.5), channel_id=1, source_target_pairs={{0,2},{1,3},{2,0},{3,1},{4,6},{5,7},{6,4},{7,5},{8,10},{9,11},{10,... | collective-permute-start | bytes 172040 | tf_op jit(solution)/shard_map/ppermute | solution.py:392
  48.5 0.0 collective-permute-done.14
  48.5 1.0 %collective-permute-start.15 = (bf16[8,3584]{1,0:T(8,128)(2,1)S(1)}, bf16[8,3584]{1,0:T(8,128)(2,1)S(1)}, u32[]{:S(2)}, u32[]{:S(2)}) collective-permute-start(bf16[8,3584]{1,0:T(8,128)(2,1)S(1)} %fusion.2), channel_id=1, source_target_pairs={{0,2},{1,3},{2,0},{3,1},{4,6},{5,7},{6,4},{7,5},{8,10},{9,11},{10,... | collective-permute-start | bytes 172040 | tf_op jit(solution)/shard_map/ppermute | solution.py:392
  49.6 2.4 %collective-permute-done.11 = bf16[8,3584]{1,0:T(8,128)(2,1)S(1)} collective-permute-done((bf16[8,3584]{1,0:T(8,128)(2,1)S(1)}, bf16[8,3584]{1,0:T(8,128)(2,1)S(1)}, u32[]{:S(2)}, u32[]{:S(2)}) %collective-permute-start.11) | collective-permute-done | bytes 57376 | tf_op jit(solution)/shard_map/ppermute | solution.py:392
  52.0 1.7 %collective-permute-done.15 = bf16[8,3584]{1,0:T(8,128)(2,1)S(1)} collective-permute-done((bf16[8,3584]{1,0:T(8,128)(2,1)S(1)}, bf16[8,3584]{1,0:T(8,128)(2,1)S(1)}, u32[]{:S(2)}, u32[]{:S(2)}) %collective-permute-start.15) | collective-permute-done | bytes 57376 | tf_op jit(solution)/shard_map/ppermute | solution.py:392
  53.7 0.7 %pad_maximum_fusion.5 = bf16[8,7168]{1,0:T(8,128)(2,1)} fusion(bf16[8,3584]{1,0:T(8,128)(2,1)S(1)} %fusion.4, bf16[8,3584]{1,0:T(8,128)(2,1)S(1)} %fusion.7), kind=kLoop, calls=%fused_computation.27 | loop fusion | flops 229376 | bytes 229376 | tf_op jit(solution)/shard_map/concatenate | solution.py:461
  (18 shorter events, 0.3 us)
Async XLA Ops:
  1.1 6.9 %collective-permute-start.2 = (bf16[8,3712]{1,0:T(8,128)(2,1)S(1)}, bf16[8,3712]{1,0:T(8,128)(2,1)S(1)}, u32[]{:S(2)}, u32[]{:S(2)}) collective-permute-start(bf16[8,3712]{1,0:T(8,128)(2,1)S(1)} %get-tuple-element.66), channel_id=1, source_target_pairs={{0,2},{1,3},{2,0},{3,1},{4,6},{5,7},{6,4},{7,5},{8,10},{9,11},{10,... | collective-permute-start | bytes 178184 | tf_op jit(solution)/shard_map/ppermute | solution.py:392
  5.2 5.4 %collective-permute-start = (bf16[8,3584]{1,0:T(8,128)(2,1)S(1)}, bf16[8,3584]{1,0:T(8,128)(2,1)S(1)}, u32[]{:S(2)}, u32[]{:S(2)}) collective-permute-start(bf16[8,3584]{1,0:T(8,128)(2,1)S(1)} %slice.112), channel_id=1, source_target_pairs={{0,2},{1,3},{2,0},{3,1},{4,6},{5,7},{6,4},{7,5},{8,10},{9,11},{10,... | collective-permute-start | bytes 172040 | tf_op jit(solution)/shard_map/ppermute | solution.py:392
  8.0 7.4 %collective-permute-start.3 = (bf16[16,3712]{1,0:T(8,128)(2,1)S(1)}, bf16[16,3712]{1,0:T(8,128)(2,1)S(1)}, u32[]{:S(2)}, u32[]{:S(2)}) collective-permute-start(bf16[16,3712]{1,0:T(8,128)(2,1)S(1)} %pad_maximum_fusion.3), channel_id=1, source_target_pairs={{0,8},{4,12},{8,0},{12,4},{1,9},{5,13},{9,1},{13,5},{2,10},{6,14},... | collective-permute-start | bytes 356360 | tf_op jit(solution)/shard_map/ppermute | solution.py:392
  10.6 4.9 %collective-permute-start.1 = (bf16[16,3584]{1,0:T(8,128)(2,1)S(1)}, bf16[16,3584]{1,0:T(8,128)(2,1)S(1)}, u32[]{:S(2)}, u32[]{:S(2)}) collective-permute-start(bf16[16,3584]{1,0:T(8,128)(2,1)S(1)} %pad_maximum_fusion.4), channel_id=1, source_target_pairs={{0,1},{1,0},{2,3},{3,2},{4,5},{5,4},{6,7},{7,6},{8,9},{9,8},{10,11... | collective-permute-start | bytes 344072 | tf_op jit(solution)/shard_map/ppermute | solution.py:392
  15.5 8.1 %collective-permute-start.5 = (bf16[32,3712]{1,0:T(8,128)(2,1)S(1)}, bf16[32,3712]{1,0:T(8,128)(2,1)S(1)}, u32[]{:S(2)}, u32[]{:S(2)}) collective-permute-start(bf16[32,3712]{1,0:T(8,128)(2,1)S(1)} %pad_maximum_fusion.1), channel_id=1, source_target_pairs={{0,1},{1,0},{2,3},{3,2},{4,5},{5,4},{6,7},{7,6},{8,9},{9,8},{10,11... | collective-permute-start | bytes 712712 | tf_op jit(solution)/shard_map/ppermute | solution.py:392
  17.0 6.5 %collective-permute-start.4 = (bf16[32,3584]{1,0:T(8,128)(2,1)S(1)}, bf16[32,3584]{1,0:T(8,128)(2,1)S(1)}, u32[]{:S(2)}, u32[]{:S(2)}) collective-permute-start(bf16[32,3584]{1,0:T(8,128)(2,1)S(1)} %pad_maximum_fusion.2), channel_id=1, source_target_pairs={{0,8},{4,12},{8,0},{12,4},{1,9},{5,13},{9,1},{13,5},{2,10},{6,14},... | collective-permute-start | bytes 688136 | tf_op jit(solution)/shard_map/ppermute | solution.py:392
  23.6 1.9 %collective-permute-start.7 = (bf16[64,3712]{1,0:T(8,128)(2,1)S(1)}, bf16[64,3712]{1,0:T(8,128)(2,1)S(1)}, u32[]{:S(2)}, u32[]{:S(2)}) collective-permute-start(bf16[64,3712]{1,0:T(8,128)(2,1)S(1)} %slice_dynamic-update-slice_fusion.own_ref), channel_id=1, source_target_pairs={{0,4},{4,0},{8,12},{12,8},{1,5},{5,1},{9,13},{13,9},{2,6},{6,2},{1... | collective-permute-start | bytes 1425416 | tf_op jit(solution)/shard_map/ppermute | solution.py:392
  23.7 3.5 %collective-permute-start.6 = (bf16[64,3584]{1,0:T(8,128)(2,1)S(1)}, bf16[64,3584]{1,0:T(8,128)(2,1)S(1)}, u32[]{:S(2)}, u32[]{:S(2)}) collective-permute-start(bf16[64,3584]{1,0:T(8,128)(2,1)S(1)} %pad_maximum_fusion.own_ref), channel_id=1, source_target_pairs={{0,4},{4,0},{8,12},{12,8},{1,5},{5,1},{9,13},{13,9},{2,6},{6,2},{1... | collective-permute-start | bytes 1376264 | tf_op jit(solution)/shard_map/ppermute | solution.py:392
  25.5 4.4 %slice-start = ((s8[7340032]{0:T(1024)(128)(4,1)}), s8[4194304]{0:T(1024)(128)(4,1)S(1)}, s32[]{:S(2)}) async-start(s8[7340032]{0:T(1024)(128)(4,1)} %bitcast.7), calls=%async_computation | async-start | bytes 8388608
  27.2 2.7 %slice-start.1 = ((s8[7340032]{0:T(1024)(128)(4,1)}), s8[3145728]{0:T(1024)(128)(4,1)S(1)}, s32[]{:S(2)}) async-start(s8[7340032]{0:T(1024)(128)(4,1)} %bitcast.7), calls=%async_computation.1 | async-start | bytes 6291456
  29.7 1.9 %collective-permute-start.8 = (bf16[64,3584]{1,0:T(8,128)(2,1)S(1)}, bf16[64,3584]{1,0:T(8,128)(2,1)S(1)}, u32[]{:S(2)}, u32[]{:S(2)}) collective-permute-start(bf16[64,3584]{1,0:T(8,128)(2,1)S(1)} %get-tuple-element.51), channel_id=1, source_target_pairs={{0,4},{4,0},{8,12},{12,8},{1,5},{5,1},{9,13},{13,9},{2,6},{6,2},{1... | collective-permute-start | bytes 1376264 | tf_op jit(solution)/shard_map/ppermute | solution.py:392
  31.6 1.8 %collective-permute-start.12 = (bf16[64,3584]{1,0:T(8,128)(2,1)S(1)}, bf16[64,3584]{1,0:T(8,128)(2,1)S(1)}, u32[]{:S(2)}, u32[]{:S(2)}) collective-permute-start(bf16[64,3584]{1,0:T(8,128)(2,1)S(1)} %get-tuple-element.56), channel_id=1, source_target_pairs={{0,4},{4,0},{8,12},{12,8},{1,5},{5,1},{9,13},{13,9},{2,6},{6,2},{1... | collective-permute-start | bytes 1376264 | tf_op jit(solution)/shard_map/ppermute | solution.py:392
  31.8 7.9 %collective-permute-start.9 = (bf16[32,3584]{1,0:T(8,128)(2,1)S(1)}, bf16[32,3584]{1,0:T(8,128)(2,1)S(1)}, u32[]{:S(2)}, u32[]{:S(2)}) collective-permute-start(bf16[32,3584]{1,0:T(8,128)(2,1)S(1)} %get-tuple-element.57), channel_id=1, source_target_pairs={{0,8},{4,12},{8,0},{12,4},{1,9},{5,13},{9,1},{13,5},{2,10},{6,14},... | collective-permute-start | bytes 688136 | tf_op jit(solution)/shard_map/ppermute | solution.py:392
  33.5 7.7 %collective-permute-start.13 = (bf16[32,3584]{1,0:T(8,128)(2,1)S(1)}, bf16[32,3584]{1,0:T(8,128)(2,1)S(1)}, u32[]{:S(2)}, u32[]{:S(2)}) collective-permute-start(bf16[32,3584]{1,0:T(8,128)(2,1)S(1)} %get-tuple-element.59), channel_id=1, source_target_pairs={{0,1},{1,0},{2,3},{3,2},{4,5},{5,4},{6,7},{7,6},{8,9},{9,8},{10,11... | collective-permute-start | bytes 688136 | tf_op jit(solution)/shard_map/ppermute | solution.py:392
  39.8 4.9 %collective-permute-start.10 = (bf16[16,3584]{1,0:T(8,128)(2,1)S(1)}, bf16[16,3584]{1,0:T(8,128)(2,1)S(1)}, u32[]{:S(2)}, u32[]{:S(2)}) collective-permute-start(bf16[16,3584]{1,0:T(8,128)(2,1)S(1)} %get-tuple-element.61), channel_id=1, source_target_pairs={{0,1},{1,0},{2,3},{3,2},{4,5},{5,4},{6,7},{7,6},{8,9},{9,8},{10,11... | collective-permute-start | bytes 344072 | tf_op jit(solution)/shard_map/ppermute | solution.py:392
  41.3 7.3 %collective-permute-start.14 = (bf16[16,3584]{1,0:T(8,128)(2,1)S(1)}, bf16[16,3584]{1,0:T(8,128)(2,1)S(1)}, u32[]{:S(2)}, u32[]{:S(2)}) collective-permute-start(bf16[16,3584]{1,0:T(8,128)(2,1)S(1)} %get-tuple-element.63), channel_id=1, source_target_pairs={{0,8},{4,12},{8,0},{12,4},{1,9},{5,13},{9,1},{13,5},{2,10},{6,14},... | collective-permute-start | bytes 344072 | tf_op jit(solution)/shard_map/ppermute | solution.py:392
  44.7 7.3 %collective-permute-start.11 = (bf16[8,3584]{1,0:T(8,128)(2,1)S(1)}, bf16[8,3584]{1,0:T(8,128)(2,1)S(1)}, u32[]{:S(2)}, u32[]{:S(2)}) collective-permute-start(bf16[8,3584]{1,0:T(8,128)(2,1)S(1)} %fusion.5), channel_id=1, source_target_pairs={{0,2},{1,3},{2,0},{3,1},{4,6},{5,7},{6,4},{7,5},{8,10},{9,11},{10,... | collective-permute-start | bytes 172040 | tf_op jit(solution)/shard_map/ppermute | solution.py:392
  48.5 5.1 %collective-permute-start.15 = (bf16[8,3584]{1,0:T(8,128)(2,1)S(1)}, bf16[8,3584]{1,0:T(8,128)(2,1)S(1)}, u32[]{:S(2)}, u32[]{:S(2)}) collective-permute-start(bf16[8,3584]{1,0:T(8,128)(2,1)S(1)} %fusion.2), channel_id=1, source_target_pairs={{0,2},{1,3},{2,0},{3,1},{4,6},{5,7},{6,4},{7,5},{8,10},{9,11},{10,... | collective-permute-start | bytes 172040 | tf_op jit(solution)/shard_map/ppermute | solution.py:392

commit v23 on v22

--- a/solution.py
+++ b/solution.py
@@ -198,33 +198,39 @@
     return copies
 
 
-def load_both_kernel(
-    share, lower, place_ref, routed_ref, shared_ref, down_ref, sdown_ref, out_ref, down_out_ref, sems
-):
+def load_late_kernel(share, place_ref, shared_ref, down_ref, sdown_ref, out_ref, down_out_ref, sems):
     parts = 4
+    column = pl.multiple_of((place_ref[0] // share) * LANES, LANES)
+    piece = shared_ref.shape[0] // parts
+    copies = [
+        pltpu.make_async_copy(
+            shared_ref.at[pl.ds(i * piece, piece), pl.ds(column, LANES)],
+            out_ref.at[pl.ds(i * piece, piece), :],
+            sems.at[i],
+        )
+        for i in range(parts)
+    ]
     run_copies(
-        weight_copies(share, place_ref, routed_ref, shared_ref, out_ref, sems, parts)
-        + down_range_copies(
-            share, place_ref, down_ref, sdown_ref, down_out_ref, lower, sems.at[2 * parts :]
-        )
-    )
-
-
-def load_both(place, routed, shared, down, sdown, lower, columns, share):
-    width, hidden = routed.shape
-    units = hidden + LANES
+        copies
+        + down_range_copies(share, place_ref, down_ref, sdown_ref, down_out_ref, 0, sems.at[parts:])
+    )
+
+
+def load_late(place, shared, down, sdown, columns, share):
+    width = shared.shape[0]
+    units = down.shape[0] + LANES
     return pl.pallas_call(
-        functools.partial(load_both_kernel, share, lower),
-        in_specs=[SMEM_SPEC] + [ANY_SPEC] * 4,
+        functools.partial(load_late_kernel, share),
+        in_specs=[SMEM_SPEC] + [ANY_SPEC] * 3,
         out_specs=[VMEM_SPEC] * 2,
-        out_shape=[pltpu.VMEM((width, units), BF16), pltpu.VMEM((units, columns), BF16)],
-        scratch_shapes=[pltpu.SemaphoreType.DMA((8 + units // DOWN_ROWS,))],
+        out_shape=[pltpu.VMEM((width, LANES), BF16), pltpu.VMEM((units, columns), BF16)],
+        scratch_shapes=[pltpu.SemaphoreType.DMA((4 + units // DOWN_ROWS,))],
         cost_estimate=pl.CostEstimate(
-            flops=0, bytes_accessed=4 * units * (width + columns), transcendentals=0
+            flops=0, bytes_accessed=4 * (units * columns + width * LANES), transcendentals=0
         ),
         compiler_params=pltpu.CompilerParams(vmem_limit_bytes=1 << 20),
-        name="load_both",
-    )(place, *(in_hbm(w) for w in (routed, shared, down, sdown)))
+        name="load_late",
+    )(place, *(in_hbm(w) for w in (shared, down, sdown)))
 
 
 def load_first_kernel(share, lower, place_ref, routed_ref, shared_ref, sdown_ref, out_ref, rows_ref, sems):
@@ -250,8 +256,11 @@
     )(place, *(in_hbm(w) for w in (routed, shared, sdown)))
 
 
-def late_half_kernel(place_ref, own_ref, other_ref, gate_ref, up_ref, gate_acc_ref, up_acc_ref, weight_ref, x):
-    width, units = up_ref.shape
+def late_half_kernel(
+    place_ref, own_ref, other_ref, gate_ref, up_ref, sup_ref, gate_acc_ref, up_acc_ref, weight_ref, x
+):
+    width, hidden = up_ref.shape
+    units = hidden + LANES
     half, columns = own_ref.shape
     cut = width + LANES - columns
     x[:half, :] = own_ref[...]
@@ -259,13 +268,14 @@
     rows = x[:, : width - cut]
     for at in tiles_of(units):
         gate_acc_ref[:, at] = jnp.dot(rows, gate_ref[:, at], preferred_element_type=F32)
-        up_acc_ref[:, at] = jnp.dot(rows, up_ref[cut:, at], preferred_element_type=F32)
+        up = up_ref[cut:, at] if at.start < hidden else sup_ref[cut:, :]
+        up_acc_ref[:, at] = jnp.dot(rows, up, preferred_element_type=F32)
     weight = row_weight(place_ref[0], x[:, width - cut :])
     weight_ref[...] = jnp.broadcast_to(weight, weight_ref.shape)
 
 
 def early_half_kernel(
-    share, place_ref, own_ref, other_ref, gate_ref, up_ref, gate_acc_ref, up_acc_ref, weight_ref, second_ref,
+    share, place_ref, own_ref, other_ref, gate_ref, up_ref, sup_ref, gate_acc_ref, up_acc_ref, weight_ref, second_ref,
     own_out_ref, other_out_ref, act_ref, x,
 ):
     half, cut = own_ref.shape
@@ -277,7 +287,8 @@
     weight = weight_ref[:, :1]
     for at in tiles_of(units):
         gate = gate_acc_ref[:, at] + jnp.dot(rows, gate_ref[:, at], preferred_element_type=F32)
-        up = up_acc_ref[:, at] + jnp.dot(rows, up_ref[:cut, at], preferred_element_type=F32)
+        up = up_ref[:cut, at] if at.start < hidden else sup_ref[:cut, :]
+        up = up_acc_ref[:, at] + jnp.dot(rows, up, preferred_element_type=F32)
         if at.start < hidden:
             act_ref[:, at] = (silu(gate) * up * weight).astype(BF16)
         else:
@@ -310,22 +321,24 @@
     )
 
 
-def pair_rows(place, own, other, gate, late_gate, up, second, down, rows, share):
+def pair_rows(place, own, other, gate, late_gate, up, sup, second, down, rows, share):
     half, cut = own[0].shape
-    width, units = up.shape
+    width, hidden = up.shape
+    units = hidden + LANES
+    up = pltpu.with_memory_space_constraint(up, pltpu.VMEM)
     partial = pl.pallas_call(
         late_half_kernel,
-        in_specs=[SMEM_SPEC] + [VMEM_SPEC] * 4,
+        in_specs=[SMEM_SPEC] + [VMEM_SPEC] * 5,
         out_specs=[VMEM_SPEC] * 3,
         out_shape=[pltpu.VMEM((2 * half, columns), F32) for columns in (units, units, LANES)],
         scratch_shapes=[pltpu.VMEM((2 * half, own[1].shape[1]), BF16)],
         cost_estimate=estimate(2 * half, width - cut, 2 * units),
         compiler_params=pltpu.CompilerParams(vmem_limit_bytes=10 << 20),
         name="late_half",
-    )(place, own[1], other[1], late_gate, up)
+    )(place, own[1], other[1], late_gate, up, sup)
     own_out, other_out, act = pl.pallas_call(
         functools.partial(early_half_kernel, share),
-        in_specs=[SMEM_SPEC] + [VMEM_SPEC] * 8,
+        in_specs=[SMEM_SPEC] + [VMEM_SPEC] * 9,
         out_specs=[VMEM_SPEC] * 3,
         out_shape=[
             pltpu.VMEM((half, cut), BF16),
@@ -336,7 +349,7 @@
         cost_estimate=estimate(2 * half, cut, 3 * units),
         compiler_params=pltpu.CompilerParams(vmem_limit_bytes=10 << 20),
         name="early_half",
-    )(place, own[0], other[0], gate, up, *partial, second)
+    )(place, own[0], other[0], gate, up, sup, *partial, second)
     last = pl.pallas_call(
         last_half_kernel,
         in_specs=[VMEM_SPEC] * 3,
@@ -432,7 +445,7 @@
     loads = (
         lambda *ready: (load_weights(after(place, *ready), gate, gate_shared, share, cut, width - cut),),
         lambda *ready: load_first(after(place, *ready), gate, gate_shared, down_shared, cut, share),
-        lambda *ready: load_both(after(place, *ready), up, up_shared, down, down_shared, 0, cut, share),
+        lambda *ready: load_late(after(place, *ready), up_shared, down, down_shared, cut, share),
     )
     loaded = ()
     for number, (phase, load) in enumerate(zip(GATHER, loads)):
@@ -444,11 +457,11 @@
             got, weights = lax.optimization_barrier((got, weights))
         loaded += weights
         own = [stack(part, add) for part, add in zip(own, got)]
-    late_gate, gate, late_rows, up, second = loaded
+    late_gate, gate, late_rows, sup, second = loaded
     own[1] = swap_quarters(own[1])
     other = [flipped(part, CORE) for part in own]
 
-    outs = pair_rows(place, own, other, gate, late_gate, up, second, down, late_rows, share)
+    outs = pair_rows(place, own, other, gate, late_gate, up, sup, second, down, late_rows, share)
 
     swapped = flipped(outs[2], CORE)
     totals = [[outs[0], swapped], [outs[1], flipped(after(outs[3], swapped), CORE)]]

time: 54.5 us -> 54.2 us (level)
  Pallas kernels: 16.2 us -> 14.1 us
  waiting for transfers between devices: 15.9 us -> 17.2 us
    pallas_call x2, Pallas kernels: 6.76 us -> 4.8 us  [the longest x1 3.12 us: load_late(): pl.pallas_call(functools.partial(load_late_kernel, share), in_specs=[SMEM...]
    ppermute x16, waiting for transfers between devices: 15.9 us -> 17.2 us  [flipped(): lax.ppermute(value, ('node', 'local')[axis], [(i, i ^ bits[axis]) for i i...]
    ppermute x16, starting transfers between devices: 20.9 us -> 21.4 us  [flipped(): lax.ppermute(value, ('node', 'local')[axis], [(i, i ^ bits[axis]) for i i...]
  transfers between devices with their start and end apart: 16 -> 16, of which waited for: 11 -> 12; matrix products, arithmetic and copies ran while one was open for 1% -> 1% of each run, Pallas kernels for 23% -> 20%
where the time goes in v23:
time: 54.2 us; the launch traced here: 54.1 us
  starting transfers between devices  21.4 us (39%)
  waiting for transfers between devices  17.2 us (32%)
  Pallas kernels  14.1 us (26%)
  other arithmetic  1.09 us (2%)
    ppermute x16, starting transfers between devices, flipped(): lax.ppermute(value, ('node', 'local')[axis], [(i, i ^ bits[axis]) for i i...  21.4 us
    ppermute x16, waiting for transfers between devices, flipped(): lax.ppermute(value, ('node', 'local')[axis], [(i, i ^ bits[axis]) for i i...  17.2 us
    pallas_call x1, Pallas kernels, load_late(): pl.pallas_call(functools.partial(load_late_kernel, share), in_specs=[SMEM...  3.12 us
    pallas_call x1, Pallas kernels, load_first(): pl.pallas_call(functools.partial(load_first_kernel, share, lower), in_spe...  2.67 us
    pallas_call x1, Pallas kernels, pair_rows(): pl.pallas_call(functools.partial(early_half_kernel, share), in_specs=[SME...  2.38 us
    pallas_call x1, Pallas kernels, load_weights(): pl.pallas_call(functools.partial(load_kernel, share, first_row), in_specs...  2.34 us
    pallas_call x1, Pallas kernels, pair_rows(): pl.pallas_call(late_half_kernel, in_specs=[SMEM_SPEC] + [VMEM_SPEC] * 5,...  1.67 us
  transfers between devices with their start and end apart: 16, of which 12 were waited for; matrix products, arithmetic and copies ran while one was open for 1% of the time, Pallas kernels for 20%

profile of v23, /device:TPU:0, one launch (start us, length us, event | category | flops | bytes accessed | tf_op | source)
XLA Modules:
  0.0 54.1 jit_solution(7602853981883826428)
XLA Ops:
  0.0 1.1 %pack_rows.1 = bf16[8,7296]{1,0:T(8,128)(2,1)S(1)} custom-call(bf16[8,7168]{1,0:T(8,128)(2,1)} %tokens_ref.1, s32[4,8]{1,0:T(4,128)} %bitcast.16, bf16[4,8]{1,0:T(4,128)(2,1)} %bitcast.17), custom_call_target="tpu_custom_call" | custom-call | tf_op jit(solution)/shard_map/pack_rows/pallas_call | solution.py:48
  1.1 4.1 %collective-permute-start.2 = (bf16[8,3712]{1,0:T(8,128)(2,1)S(1)}, bf16[8,3712]{1,0:T(8,128)(2,1)S(1)}, u32[]{:S(2)}, u32[]{:S(2)}) collective-permute-start(bf16[8,3712]{1,0:T(8,128)(2,1)S(1)} %get-tuple-element.66), channel_id=1, source_target_pairs={{0,2},{1,3},{2,0},{3,1},{4,6},{5,7},{6,4},{7,5},{8,10},{9,11},{10,... | collective-permute-start | bytes 178184 | tf_op jit(solution)/shard_map/ppermute | solution.py:405
  5.2 0.1 collective-permute-start
  5.3 2.3 %load_weights.1.gate_ref = bf16[3584,640]{1,0:T(8,128)(2,1)S(1)} custom-call(s32[1]{0:T(128)} %bitcast.place_ref, bf16[7168,512]{1,0:T(8,128)(2,1)} %bitcast.14, bf16[7168,512]{1,0:T(8,128)(2,1)} %shared_ref.4), custom_call_target="tpu_custom_call" | custom-call | bytes 9175040 | tf_op jit(solution)/shard_map/load_weights/pallas_call | solution.py:85
  7.6 0.4 collective-permute-done.2
  8.0 2.4 %collective-permute-start.3 = (bf16[16,3712]{1,0:T(8,128)(2,1)S(1)}, bf16[16,3712]{1,0:T(8,128)(2,1)S(1)}, u32[]{:S(2)}, u32[]{:S(2)}) collective-permute-start(bf16[16,3712]{1,0:T(8,128)(2,1)S(1)} %pad_maximum_fusion.3), channel_id=1, source_target_pairs={{0,8},{4,12},{8,0},{12,4},{1,9},{5,13},{9,1},{13,5},{2,10},{6,14},... | collective-permute-start | bytes 356360 | tf_op jit(solution)/shard_map/ppermute | solution.py:405
  10.4 0.1 collective-permute-done
  10.6 1.5 %collective-permute-start.1 = (bf16[16,3584]{1,0:T(8,128)(2,1)S(1)}, bf16[16,3584]{1,0:T(8,128)(2,1)S(1)}, u32[]{:S(2)}, u32[]{:S(2)}) collective-permute-start(bf16[16,3584]{1,0:T(8,128)(2,1)S(1)} %pad_maximum_fusion.4), channel_id=1, source_target_pairs={{0,1},{1,0},{2,3},{3,2},{4,5},{5,4},{6,7},{7,6},{8,9},{9,8},{10,11... | collective-permute-start | bytes 344072 | tf_op jit(solution)/shard_map/ppermute | solution.py:405
  12.1 2.7 %load_first.1 = (bf16[3584,640]{1,0:T(8,128)(2,1)S(1)}, bf16[128,3584]{1,0:T(8,128)(2,1)S(1)}) custom-call(s32[1]{0:T(128)} %bitcast.place_ref, bf16[7168,512]{1,0:T(8,128)(2,1)} %bitcast.15, bf16[7168,512]{1,0:T(8,128)(2,1)} %shared_ref.4, bf16[512,7168]{1,0:T(8,128)(2,1)} %sdown_ref.3), custom_call_target="tpu_custom_call" | custom-call | bytes 9175040 | tf_op jit(solution)/shard_map/load_first/pallas_call | solution.py:247
  14.8 0.6 %collective-permute-done.1 = bf16[16,3584]{1,0:T(8,128)(2,1)S(1)} collective-permute-done((bf16[16,3584]{1,0:T(8,128)(2,1)S(1)}, bf16[16,3584]{1,0:T(8,128)(2,1)S(1)}, u32[]{:S(2)}, u32[]{:S(2)}) %collective-permute-start.1) | collective-permute-done | bytes 114720 | tf_op jit(solution)/shard_map/ppermute | solution.py:405
  15.4 0.0 collective-permute-done.3
  15.4 0.0 slice-start
  15.5 1.5 %collective-permute-start.5 = (bf16[32,3712]{1,0:T(8,128)(2,1)S(1)}, bf16[32,3712]{1,0:T(8,128)(2,1)S(1)}, u32[]{:S(2)}, u32[]{:S(2)}) collective-permute-start(bf16[32,3712]{1,0:T(8,128)(2,1)S(1)} %pad_maximum_fusion.1), channel_id=1, source_target_pairs={{0,1},{1,0},{2,3},{3,2},{4,5},{5,4},{6,7},{7,6},{8,9},{9,8},{10,11... | collective-permute-start | bytes 712712 | tf_op jit(solution)/shard_map/ppermute | solution.py:405
  17.0 1.4 %collective-permute-start.4 = (bf16[32,3584]{1,0:T(8,128)(2,1)S(1)}, bf16[32,3584]{1,0:T(8,128)(2,1)S(1)}, u32[]{:S(2)}, u32[]{:S(2)}) collective-permute-start(bf16[32,3584]{1,0:T(8,128)(2,1)S(1)} %pad_maximum_fusion.2), channel_id=1, source_target_pairs={{0,8},{4,12},{8,0},{12,4},{1,9},{5,13},{9,1},{13,5},{2,10},{6,14},... | collective-permute-start | bytes 688136 | tf_op jit(solution)/shard_map/ppermute | solution.py:405
  18.4 3.1 %load_late.1 = (bf16[7168,128]{1,0:T(8,128)(2,1)S(1)}, bf16[640,3584]{1,0:T(8,128)(2,1)S(1)}) custom-call(s32[1]{0:T(128)} %bitcast.place_ref, bf16[7168,512]{1,0:T(8,128)(2,1)} %shared_ref.5, bf16[512,7168]{1,0:T(8,128)(2,1)} %bitcast.10, bf16[512,7168]{1,0:T(8,128)(2,1)} %sdown_ref.3), custom_call_target="tpu_custom_call" | custom-call | bytes 12845056 | tf_op jit(solution)/shard_map/load_late/pallas_call | solution.py:222
  21.6 1.5 %collective-permute-done.4 = bf16[32,3584]{1,0:T(8,128)(2,1)S(1)} collective-permute-done((bf16[32,3584]{1,0:T(8,128)(2,1)S(1)}, bf16[32,3584]{1,0:T(8,128)(2,1)S(1)}, u32[]{:S(2)}, u32[]{:S(2)}) %collective-permute-start.4) | collective-permute-done | bytes 229408 | tf_op jit(solution)/shard_map/ppermute | solution.py:405
  23.1 0.0 collective-permute-done.5
  23.2 0.1 collective-permute-start.7
  23.3 0.6 %collective-permute-start.6 = (bf16[64,3584]{1,0:T(8,128)(2,1)S(1)}, bf16[64,3584]{1,0:T(8,128)(2,1)S(1)}, u32[]{:S(2)}, u32[]{:S(2)}) collective-permute-start(bf16[64,3584]{1,0:T(8,128)(2,1)S(1)} %pad_maximum_fusion.own_ref), channel_id=1, source_target_pairs={{0,4},{4,0},{8,12},{12,8},{1,5},{5,1},{9,13},{13,9},{2,6},{6,2},{1... | collective-permute-start | bytes 1376264 | tf_op jit(solution)/shard_map/ppermute | solution.py:405
  23.8 1.2 %collective-permute-done.7.other_ref = bf16[64,3712]{1,0:T(8,128)(2,1)S(1)} collective-permute-done((bf16[64,3712]{1,0:T(8,128)(2,1)S(1)}, bf16[64,3712]{1,0:T(8,128)(2,1)S(1)}, u32[]{:S(2)}, u32[]{:S(2)}) %collective-permute-start.7) | collective-permute-done | bytes 475168 | tf_op jit(solution)/shard_map/ppermute | solution.py:405
  25.1 0.0 slice-done
  25.1 0.0 slice-done.1
  25.1 1.7 %late_half.1 = (f32[128,640]{1,0:T(8,128)S(1)}, f32[128,640]{1,0:T(8,128)S(1)}, f32[128,128]{1,0:T(8,128)S(1)}) custom-call(s32[1]{0:T(128)} %bitcast.place_ref, bf16[64,3712]{1,0:T(8,128)(2,1)S(1)} %slice_dynamic-update-slice_fusion.own_ref, bf16[64,3712]{1,0:T(8,128)(2,1)S(1)} %collective-permute-done.7.other_ref, ...), custom_call_target="tpu_custom_call" | custom-call | flops 1174405120 | bytes 9175040 | tf_op jit(solution)/shard_map/late_half/pallas_call | solution.py:329
  26.8 0.0 collective-permute-done.6.other_ref
  26.8 0.0 slice-start.3
  26.8 2.4 %early_half.1 = (bf16[64,3584]{1,0:T(8,128)(2,1)S(1)}, bf16[64,3584]{1,0:T(8,128)(2,1)S(1)}, bf16[128,640]{1,0:T(8,128)(2,1)S(1)}) custom-call(s32[1]{0:T(128)} %bitcast.place_ref, bf16[64,3584]{1,0:T(8,128)(2,1)S(1)} %pad_maximum_fusion.own_ref, bf16[64,3584]{1,0:T(8,128)(2,1)S(1)} %collective-permute-done.6.other_ref, ...), custom_call_target="tpu_custom_call" | custom-call | flops 1761607680 | bytes 13762560 | tf_op jit(solution)/shard_map/early_half/pallas_call | solution.py:339
  29.2 0.2 collective-permute-start.8
  29.4 0.0 slice-done.2
  29.4 0.0 slice-done.3
  29.4 0.9 %last_half.1 = (bf16[64,3584]{1,0:T(8,128)(2,1)S(1)}, bf16[64,3584]{1,0:T(8,128)(2,1)S(1)}) custom-call(bf16[128,640]{1,0:T(8,128)(2,1)S(1)} %get-tuple-element.52.act_ref, bf16[512,7168]{1,0:T(8,128)(2,1)S(1)} %bitcast.13, bf16[128,3584]{1,0:T(8,128)(2,1)S(1)} %get-tuple-element.53.rows_ref), custom_call_target="tpu_custom_call" | custom-call | flops 587202560 | bytes 4587520 | tf_op jit(solution)/shard_map/last_half/pallas_call | solution.py:353
  30.3 0.8 %collective-permute-done.8 = bf16[64,3584]{1,0:T(8,128)(2,1)S(1)} collective-permute-done((bf16[64,3584]{1,0:T(8,128)(2,1)S(1)}, bf16[64,3584]{1,0:T(8,128)(2,1)S(1)}, u32[]{:S(2)}, u32[]{:S(2)}) %collective-permute-start.8) | collective-permute-done | bytes 458784 | tf_op jit(solution)/shard_map/ppermute | solution.py:405
  31.1 0.1 collective-permute-start.12
  31.2 0.1 add_convert_fusion.1
  31.3 1.5 %collective-permute-start.9 = (bf16[32,3584]{1,0:T(8,128)(2,1)S(1)}, bf16[32,3584]{1,0:T(8,128)(2,1)S(1)}, u32[]{:S(2)}, u32[]{:S(2)}) collective-permute-start(bf16[32,3584]{1,0:T(8,128)(2,1)S(1)} %get-tuple-element.57), channel_id=1, source_target_pairs={{0,8},{4,12},{8,0},{12,4},{1,9},{5,13},{9,1},{13,5},{2,10},{6,14},... | collective-permute-start | bytes 688136 | tf_op jit(solution)/shard_map/ppermute | solution.py:405
  32.8 0.1 collective-permute-done.12
  32.9 0.1 add_convert_fusion
  33.0 0.8 %collective-permute-start.13 = (bf16[32,3584]{1,0:T(8,128)(2,1)S(1)}, bf16[32,3584]{1,0:T(8,128)(2,1)S(1)}, u32[]{:S(2)}, u32[]{:S(2)}) collective-permute-start(bf16[32,3584]{1,0:T(8,128)(2,1)S(1)} %get-tuple-element.59), channel_id=1, source_target_pairs={{0,1},{1,0},{2,3},{3,2},{4,5},{5,4},{6,7},{7,6},{8,9},{9,8},{10,11... | collective-permute-start | bytes 688136 | tf_op jit(solution)/shard_map/ppermute | solution.py:405
  33.7 5.5 %collective-permute-done.9 = bf16[32,3584]{1,0:T(8,128)(2,1)S(1)} collective-permute-done((bf16[32,3584]{1,0:T(8,128)(2,1)S(1)}, bf16[32,3584]{1,0:T(8,128)(2,1)S(1)}, u32[]{:S(2)}, u32[]{:S(2)}) %collective-permute-start.9) | collective-permute-done | bytes 229408 | tf_op jit(solution)/shard_map/ppermute | solution.py:405
  39.3 0.6 %collective-permute-start.10 = (bf16[16,3584]{1,0:T(8,128)(2,1)S(1)}, bf16[16,3584]{1,0:T(8,128)(2,1)S(1)}, u32[]{:S(2)}, u32[]{:S(2)}) collective-permute-start(bf16[16,3584]{1,0:T(8,128)(2,1)S(1)} %get-tuple-element.61), channel_id=1, source_target_pairs={{0,1},{1,0},{2,3},{3,2},{4,5},{5,4},{6,7},{7,6},{8,9},{9,8},{10,11... | collective-permute-start | bytes 344072 | tf_op jit(solution)/shard_map/ppermute | solution.py:405
  39.9 0.8 %collective-permute-done.13 = bf16[32,3584]{1,0:T(8,128)(2,1)S(1)} collective-permute-done((bf16[32,3584]{1,0:T(8,128)(2,1)S(1)}, bf16[32,3584]{1,0:T(8,128)(2,1)S(1)}, u32[]{:S(2)}, u32[]{:S(2)}) %collective-permute-start.13) | collective-permute-done | bytes 229408 | tf_op jit(solution)/shard_map/ppermute | solution.py:405
  40.7 1.5 %collective-permute-start.14 = (bf16[16,3584]{1,0:T(8,128)(2,1)S(1)}, bf16[16,3584]{1,0:T(8,128)(2,1)S(1)}, u32[]{:S(2)}, u32[]{:S(2)}) collective-permute-start(bf16[16,3584]{1,0:T(8,128)(2,1)S(1)} %get-tuple-element.63), channel_id=1, source_target_pairs={{0,8},{4,12},{8,0},{12,4},{1,9},{5,13},{9,1},{13,5},{2,10},{6,14},... | collective-permute-start | bytes 344072 | tf_op jit(solution)/shard_map/ppermute | solution.py:405
  42.2 1.9 %collective-permute-done.10 = bf16[16,3584]{1,0:T(8,128)(2,1)S(1)} collective-permute-done((bf16[16,3584]{1,0:T(8,128)(2,1)S(1)}, bf16[16,3584]{1,0:T(8,128)(2,1)S(1)}, u32[]{:S(2)}, u32[]{:S(2)}) %collective-permute-start.10) | collective-permute-done | bytes 114720 | tf_op jit(solution)/shard_map/ppermute | solution.py:405
  44.2 3.5 %collective-permute-start.11 = (bf16[8,3584]{1,0:T(8,128)(2,1)S(1)}, bf16[8,3584]{1,0:T(8,128)(2,1)S(1)}, u32[]{:S(2)}, u32[]{:S(2)}) collective-permute-start(bf16[8,3584]{1,0:T(8,128)(2,1)S(1)} %fusion.5), channel_id=1, source_target_pairs={{0,2},{1,3},{2,0},{3,1},{4,6},{5,7},{6,4},{7,5},{8,10},{9,11},{10,... | collective-permute-start | bytes 172040 | tf_op jit(solution)/shard_map/ppermute | solution.py:405
  47.7 0.0 collective-permute-done.14
  47.7 1.5 %collective-permute-start.15 = (bf16[8,3584]{1,0:T(8,128)(2,1)S(1)}, bf16[8,3584]{1,0:T(8,128)(2,1)S(1)}, u32[]{:S(2)}, u32[]{:S(2)}) collective-permute-start(bf16[8,3584]{1,0:T(8,128)(2,1)S(1)} %fusion.2), channel_id=1, source_target_pairs={{0,2},{1,3},{2,0},{3,1},{4,6},{5,7},{6,4},{7,5},{8,10},{9,11},{10,... | collective-permute-start | bytes 172040 | tf_op jit(solution)/shard_map/ppermute | solution.py:405
  49.2 2.4 %collective-permute-done.11 = bf16[8,3584]{1,0:T(8,128)(2,1)S(1)} collective-permute-done((bf16[8,3584]{1,0:T(8,128)(2,1)S(1)}, bf16[8,3584]{1,0:T(8,128)(2,1)S(1)}, u32[]{:S(2)}, u32[]{:S(2)}) %collective-permute-start.11) | collective-permute-done | bytes 57376 | tf_op jit(solution)/shard_map/ppermute | solution.py:405
  51.6 1.8 %collective-permute-done.15 = bf16[8,3584]{1,0:T(8,128)(2,1)S(1)} collective-permute-done((bf16[8,3584]{1,0:T(8,128)(2,1)S(1)}, bf16[8,3584]{1,0:T(8,128)(2,1)S(1)}, u32[]{:S(2)}, u32[]{:S(2)}) %collective-permute-start.15) | collective-permute-done | bytes 57376 | tf_op jit(solution)/shard_map/ppermute | solution.py:405
  53.4 0.7 %pad_maximum_fusion.5 = bf16[8,7168]{1,0:T(8,128)(2,1)} fusion(bf16[8,3584]{1,0:T(8,128)(2,1)S(1)} %fusion.4, bf16[8,3584]{1,0:T(8,128)(2,1)S(1)} %fusion.7), kind=kLoop, calls=%fused_computation.27 | loop fusion | flops 229376 | bytes 229376 | tf_op jit(solution)/shard_map/concatenate | solution.py:474
  (21 shorter events, 0.3 us)
Async XLA Ops:
  1.1 6.9 %collective-permute-start.2 = (bf16[8,3712]{1,0:T(8,128)(2,1)S(1)}, bf16[8,3712]{1,0:T(8,128)(2,1)S(1)}, u32[]{:S(2)}, u32[]{:S(2)}) collective-permute-start(bf16[8,3712]{1,0:T(8,128)(2,1)S(1)} %get-tuple-element.66), channel_id=1, source_target_pairs={{0,2},{1,3},{2,0},{3,1},{4,6},{5,7},{6,4},{7,5},{8,10},{9,11},{10,... | collective-permute-start | bytes 178184 | tf_op jit(solution)/shard_map/ppermute | solution.py:405
  5.2 5.4 %collective-permute-start = (bf16[8,3584]{1,0:T(8,128)(2,1)S(1)}, bf16[8,3584]{1,0:T(8,128)(2,1)S(1)}, u32[]{:S(2)}, u32[]{:S(2)}) collective-permute-start(bf16[8,3584]{1,0:T(8,128)(2,1)S(1)} %slice.112), channel_id=1, source_target_pairs={{0,2},{1,3},{2,0},{3,1},{4,6},{5,7},{6,4},{7,5},{8,10},{9,11},{10,... | collective-permute-start | bytes 172040 | tf_op jit(solution)/shard_map/ppermute | solution.py:405
  8.0 7.4 %collective-permute-start.3 = (bf16[16,3712]{1,0:T(8,128)(2,1)S(1)}, bf16[16,3712]{1,0:T(8,128)(2,1)S(1)}, u32[]{:S(2)}, u32[]{:S(2)}) collective-permute-start(bf16[16,3712]{1,0:T(8,128)(2,1)S(1)} %pad_maximum_fusion.3), channel_id=1, source_target_pairs={{0,8},{4,12},{8,0},{12,4},{1,9},{5,13},{9,1},{13,5},{2,10},{6,14},... | collective-permute-start | bytes 356360 | tf_op jit(solution)/shard_map/ppermute | solution.py:405
  10.6 4.9 %collective-permute-start.1 = (bf16[16,3584]{1,0:T(8,128)(2,1)S(1)}, bf16[16,3584]{1,0:T(8,128)(2,1)S(1)}, u32[]{:S(2)}, u32[]{:S(2)}) collective-permute-start(bf16[16,3584]{1,0:T(8,128)(2,1)S(1)} %pad_maximum_fusion.4), channel_id=1, source_target_pairs={{0,1},{1,0},{2,3},{3,2},{4,5},{5,4},{6,7},{7,6},{8,9},{9,8},{10,11... | collective-permute-start | bytes 344072 | tf_op jit(solution)/shard_map/ppermute | solution.py:405
  15.4 9.6 %slice-start = ((s8[7340032]{0:T(1024)(128)(4,1)}), s8[4194304]{0:T(1024)(128)(4,1)S(1)}, s32[]{:S(2)}) async-start(s8[7340032]{0:T(1024)(128)(4,1)} %bitcast.6), calls=%async_computation | async-start | bytes 8388608
  15.5 7.7 %collective-permute-start.5 = (bf16[32,3712]{1,0:T(8,128)(2,1)S(1)}, bf16[32,3712]{1,0:T(8,128)(2,1)S(1)}, u32[]{:S(2)}, u32[]{:S(2)}) collective-permute-start(bf16[32,3712]{1,0:T(8,128)(2,1)S(1)} %pad_maximum_fusion.1), channel_id=1, source_target_pairs={{0,1},{1,0},{2,3},{3,2},{4,5},{5,4},{6,7},{7,6},{8,9},{9,8},{10,11... | collective-permute-start | bytes 712712 | tf_op jit(solution)/shard_map/ppermute | solution.py:405
  17.0 6.1 %collective-permute-start.4 = (bf16[32,3584]{1,0:T(8,128)(2,1)S(1)}, bf16[32,3584]{1,0:T(8,128)(2,1)S(1)}, u32[]{:S(2)}, u32[]{:S(2)}) collective-permute-start(bf16[32,3584]{1,0:T(8,128)(2,1)S(1)} %pad_maximum_fusion.2), channel_id=1, source_target_pairs={{0,8},{4,12},{8,0},{12,4},{1,9},{5,13},{9,1},{13,5},{2,10},{6,14},... | collective-permute-start | bytes 688136 | tf_op jit(solution)/shard_map/ppermute | solution.py:405
  18.4 6.6 %slice-start.1 = ((s8[7340032]{0:T(1024)(128)(4,1)}), s8[3145728]{0:T(1024)(128)(4,1)S(1)}, s32[]{:S(2)}) async-start(s8[7340032]{0:T(1024)(128)(4,1)} %bitcast.6), calls=%async_computation.1 | async-start | bytes 6291456
  23.2 1.9 %collective-permute-start.7 = (bf16[64,3712]{1,0:T(8,128)(2,1)S(1)}, bf16[64,3712]{1,0:T(8,128)(2,1)S(1)}, u32[]{:S(2)}, u32[]{:S(2)}) collective-permute-start(bf16[64,3712]{1,0:T(8,128)(2,1)S(1)} %slice_dynamic-update-slice_fusion.own_ref), channel_id=1, source_target_pairs={{0,4},{4,0},{8,12},{12,8},{1,5},{5,1},{9,13},{13,9},{2,6},{6,2},{1... | collective-permute-start | bytes 1425416 | tf_op jit(solution)/shard_map/ppermute | solution.py:405
  23.3 3.5 %collective-permute-start.6 = (bf16[64,3584]{1,0:T(8,128)(2,1)S(1)}, bf16[64,3584]{1,0:T(8,128)(2,1)S(1)}, u32[]{:S(2)}, u32[]{:S(2)}) collective-permute-start(bf16[64,3584]{1,0:T(8,128)(2,1)S(1)} %pad_maximum_fusion.own_ref), channel_id=1, source_target_pairs={{0,4},{4,0},{8,12},{12,8},{1,5},{5,1},{9,13},{13,9},{2,6},{6,2},{1... | collective-permute-start | bytes 1376264 | tf_op jit(solution)/shard_map/ppermute | solution.py:405
  25.1 4.3 %slice-start.2 = ((s8[7340032]{0:T(1024)(128)(4,1)}), s8[4194304]{0:T(1024)(128)(4,1)S(1)}, s32[]{:S(2)}) async-start(s8[7340032]{0:T(1024)(128)(4,1)} %bitcast.11), calls=%async_computation.2 | async-start | bytes 8388608
  26.8 2.6 %slice-start.3 = ((s8[7340032]{0:T(1024)(128)(4,1)}), s8[3145728]{0:T(1024)(128)(4,1)S(1)}, s32[]{:S(2)}) async-start(s8[7340032]{0:T(1024)(128)(4,1)} %bitcast.11), calls=%async_computation.3 | async-start | bytes 6291456
  29.2 1.9 %collective-permute-start.8 = (bf16[64,3584]{1,0:T(8,128)(2,1)S(1)}, bf16[64,3584]{1,0:T(8,128)(2,1)S(1)}, u32[]{:S(2)}, u32[]{:S(2)}) collective-permute-start(bf16[64,3584]{1,0:T(8,128)(2,1)S(1)} %get-tuple-element.51), channel_id=1, source_target_pairs={{0,4},{4,0},{8,12},{12,8},{1,5},{5,1},{9,13},{13,9},{2,6},{6,2},{1... | collective-permute-start | bytes 1376264 | tf_op jit(solution)/shard_map/ppermute | solution.py:405
  31.1 1.8 %collective-permute-start.12 = (bf16[64,3584]{1,0:T(8,128)(2,1)S(1)}, bf16[64,3584]{1,0:T(8,128)(2,1)S(1)}, u32[]{:S(2)}, u32[]{:S(2)}) collective-permute-start(bf16[64,3584]{1,0:T(8,128)(2,1)S(1)} %get-tuple-element.56), channel_id=1, source_target_pairs={{0,4},{4,0},{8,12},{12,8},{1,5},{5,1},{9,13},{13,9},{2,6},{6,2},{1... | collective-permute-start | bytes 1376264 | tf_op jit(solution)/shard_map/ppermute | solution.py:405
  31.3 7.9 %collective-permute-start.9 = (bf16[32,3584]{1,0:T(8,128)(2,1)S(1)}, bf16[32,3584]{1,0:T(8,128)(2,1)S(1)}, u32[]{:S(2)}, u32[]{:S(2)}) collective-permute-start(bf16[32,3584]{1,0:T(8,128)(2,1)S(1)} %get-tuple-element.57), channel_id=1, source_target_pairs={{0,8},{4,12},{8,0},{12,4},{1,9},{5,13},{9,1},{13,5},{2,10},{6,14},... | collective-permute-start | bytes 688136 | tf_op jit(solution)/shard_map/ppermute | solution.py:405
  33.0 7.7 %collective-permute-start.13 = (bf16[32,3584]{1,0:T(8,128)(2,1)S(1)}, bf16[32,3584]{1,0:T(8,128)(2,1)S(1)}, u32[]{:S(2)}, u32[]{:S(2)}) collective-permute-start(bf16[32,3584]{1,0:T(8,128)(2,1)S(1)} %get-tuple-element.59), channel_id=1, source_target_pairs={{0,1},{1,0},{2,3},{3,2},{4,5},{5,4},{6,7},{7,6},{8,9},{9,8},{10,11... | collective-permute-start | bytes 688136 | tf_op jit(solution)/shard_map/ppermute | solution.py:405
  39.3 4.9 %collective-permute-start.10 = (bf16[16,3584]{1,0:T(8,128)(2,1)S(1)}, bf16[16,3584]{1,0:T(8,128)(2,1)S(1)}, u32[]{:S(2)}, u32[]{:S(2)}) collective-permute-start(bf16[16,3584]{1,0:T(8,128)(2,1)S(1)} %get-tuple-element.61), channel_id=1, source_target_pairs={{0,1},{1,0},{2,3},{3,2},{4,5},{5,4},{6,7},{7,6},{8,9},{9,8},{10,11... | collective-permute-start | bytes 344072 | tf_op jit(solution)/shard_map/ppermute | solution.py:405
  40.7 7.0 %collective-permute-start.14 = (bf16[16,3584]{1,0:T(8,128)(2,1)S(1)}, bf16[16,3584]{1,0:T(8,128)(2,1)S(1)}, u32[]{:S(2)}, u32[]{:S(2)}) collective-permute-start(bf16[16,3584]{1,0:T(8,128)(2,1)S(1)} %get-tuple-element.63), channel_id=1, source_target_pairs={{0,8},{4,12},{8,0},{12,4},{1,9},{5,13},{9,1},{13,5},{2,10},{6,14},... | collective-permute-start | bytes 344072 | tf_op jit(solution)/shard_map/ppermute | solution.py:405
  44.2 7.4 %collective-permute-start.11 = (bf16[8,3584]{1,0:T(8,128)(2,1)S(1)}, bf16[8,3584]{1,0:T(8,128)(2,1)S(1)}, u32[]{:S(2)}, u32[]{:S(2)}) collective-permute-start(bf16[8,3584]{1,0:T(8,128)(2,1)S(1)} %fusion.5), channel_id=1, source_target_pairs={{0,2},{1,3},{2,0},{3,1},{4,6},{5,7},{6,4},{7,5},{8,10},{9,11},{10,... | collective-permute-start | bytes 172040 | tf_op jit(solution)/shard_map/ppermute | solution.py:405
  47.7 5.7 %collective-permute-start.15 = (bf16[8,3584]{1,0:T(8,128)(2,1)S(1)}, bf16[8,3584]{1,0:T(8,128)(2,1)S(1)}, u32[]{:S(2)}, u32[]{:S(2)}) collective-permute-start(bf16[8,3584]{1,0:T(8,128)(2,1)S(1)} %fusion.2), channel_id=1, source_target_pairs={{0,2},{1,3},{2,0},{3,1},{4,6},{5,7},{6,4},{7,5},{8,10},{9,11},{10,... | collective-permute-start | bytes 172040 | tf_op jit(solution)/shard_map/ppermute | solution.py:405

commit v24 on v23

--- a/solution.py
+++ b/solution.py
@@ -406,8 +406,8 @@
 
 
 X, Z1, Z2, CORE = (2, 0), (0, 1), (0, 2), (1, 0)
-GATHER = ((Z2, Z2), (Z1, X), (X, Z1))
-SCATTER = GATHER[::-1]
+GATHER = ((Z1, X), (X, Z1))
+SCATTER = ((X, Z1), (Z1, X), (Z2, Z2))
 
 
 def stack(*values):
@@ -441,23 +441,22 @@
         return lax.psum_scatter(part, ("node", "local"), scatter_dimension=0, tiled=True)
 
     cut = width // 2
+    got = flipped(packed, Z2)
+    late_gate = load_weights(after(place, packed), gate, gate_shared, share, cut, width - cut)
+    got, late_gate = lax.optimization_barrier((got, late_gate))
+    packed = stack(packed, got)
     own = [packed[:, :cut], packed[:, cut:]]
     loads = (
-        lambda *ready: (load_weights(after(place, *ready), gate, gate_shared, share, cut, width - cut),),
         lambda *ready: load_first(after(place, *ready), gate, gate_shared, down_shared, cut, share),
         lambda *ready: load_late(after(place, *ready), up_shared, down, down_shared, cut, share),
     )
     loaded = ()
-    for number, (phase, load) in enumerate(zip(GATHER, loads)):
+    for phase, load in zip(GATHER, loads):
         got = [flipped(part, bits) for part, bits in zip(own, phase)]
-        weights = tuple(load(*own))
-        if number == 0:
-            got[1], weights = lax.optimization_barrier((got[1], weights))
-        else:
-            got, weights = lax.optimization_barrier((got, weights))
+        got, weights = lax.optimization_barrier((got, tuple(load(*own))))
         loaded += weights
         own = [stack(part, add) for part, add in zip(own, got)]
-    late_gate, gate, late_rows, sup, second = loaded
+    gate, late_rows, sup, second = loaded
     own[1] = swap_quarters(own[1])
     other = [flipped(part, CORE) for part in own]
 

time: 54.2 us -> 55.4 us (1.022)
  waiting for transfers between devices: 17.2 us -> 22.3 us
  starting transfers between devices: 21.4 us -> 17.5 us
    ppermute x16 -> x15, waiting for transfers between devices: 17.2 us -> 22.3 us  [flipped(): lax.ppermute(value, ('node', 'local')[axis], [(i, i ^ bits[axis]) for i i...]
    ppermute x16 -> x15, starting transfers between devices: 21.4 us -> 17.5 us  [flipped(): lax.ppermute(value, ('node', 'local')[axis], [(i, i ^ bits[axis]) for i i...]
  transfers between devices with their start and end apart: 16 -> 15, of which waited for: 12 -> 11; matrix products, arithmetic and copies ran while one was open for 1% -> 1% of each run, Pallas kernels for 20% -> 19%
where the time goes in v24:
time: 55.4 us; the launch traced here: 55.3 us
  waiting for transfers between devices  22.3 us (40%)
  starting transfers between devices  17.5 us (32%)
  Pallas kernels  14.1 us (25%)
  other arithmetic  1.16 us (2%)
    ppermute x15, waiting for transfers between devices, flipped(): lax.ppermute(value, ('node', 'local')[axis], [(i, i ^ bits[axis]) for i i...  22.3 us
    ppermute x15, starting transfers between devices, flipped(): lax.ppermute(value, ('node', 'local')[axis], [(i, i ^ bits[axis]) for i i...  17.5 us
    pallas_call x1, Pallas kernels, load_late(): pl.pallas_call(functools.partial(load_late_kernel, share), in_specs=[SMEM...  3.12 us
    pallas_call x1, Pallas kernels, load_first(): pl.pallas_call(functools.partial(load_first_kernel, share, lower), in_spe...  2.67 us
    pallas_call x1, Pallas kernels, pair_rows(): pl.pallas_call(functools.partial(early_half_kernel, share), in_specs=[SME...  2.38 us
    pallas_call x1, Pallas kernels, load_weights(): pl.pallas_call(functools.partial(load_kernel, share, first_row), in_specs...  2.34 us
    pallas_call x1, Pallas kernels, pair_rows(): pl.pallas_call(late_half_kernel, in_specs=[SMEM_SPEC] + [VMEM_SPEC] * 5,...  1.65 us
  transfers between devices with their start and end apart: 15, of which 11 were waited for; matrix products, arithmetic and copies ran while one was open for 1% of the time, Pallas kernels for 19%

profile of v24, /device:TPU:0, one launch (start us, length us, event | category | flops | bytes accessed | tf_op | source)
XLA Modules:
  0.0 55.3 jit_solution(4731825393551432974)
XLA Ops:
  0.0 1.1 %pack_rows.1 = bf16[8,7296]{1,0:T(8,128)(2,1)S(1)} custom-call(bf16[8,7168]{1,0:T(8,128)(2,1)} %tokens_ref.1, s32[4,8]{1,0:T(4,128)} %bitcast.16, bf16[4,8]{1,0:T(4,128)(2,1)} %bitcast.17), custom_call_target="tpu_custom_call" | custom-call | tf_op jit(solution)/shard_map/pack_rows/pallas_call | solution.py:48
  1.1 4.1 %collective-permute-start = (bf16[8,7296]{1,0:T(8,128)(2,1)S(1)}, bf16[8,7296]{1,0:T(8,128)(2,1)S(1)}, u32[]{:S(2)}, u32[]{:S(2)}) collective-permute-start(bf16[8,7296]{1,0:T(8,128)(2,1)S(1)} %pack_rows.1), channel_id=1, source_target_pairs={{0,2},{1,3},{2,0},{3,1},{4,6},{5,7},{6,4},{7,5},{8,10},{9,11},{10,... | collective-permute-start | bytes 350216 | tf_op jit(solution)/shard_map/ppermute | solution.py:405
  5.2 2.3 %load_weights.1.gate_ref = bf16[3584,640]{1,0:T(8,128)(2,1)S(1)} custom-call(s32[1]{0:T(128)} %bitcast.place_ref, bf16[7168,512]{1,0:T(8,128)(2,1)} %bitcast.14, bf16[7168,512]{1,0:T(8,128)(2,1)} %shared_ref.4), custom_call_target="tpu_custom_call" | custom-call | bytes 9175040 | tf_op jit(solution)/shard_map/load_weights/pallas_call | solution.py:85
  7.5 3.3 %collective-permute-done = bf16[8,7296]{1,0:T(8,128)(2,1)S(1)} collective-permute-done((bf16[8,7296]{1,0:T(8,128)(2,1)S(1)}, bf16[8,7296]{1,0:T(8,128)(2,1)S(1)}, u32[]{:S(2)}, u32[]{:S(2)}) %collective-permute-start) | collective-permute-done | bytes 116768 | tf_op jit(solution)/shard_map/ppermute | solution.py:405
  10.9 1.6 %collective-permute-start.2 = (bf16[16,3712]{1,0:T(8,128)(2,1)S(1)}, bf16[16,3712]{1,0:T(8,128)(2,1)S(1)}, u32[]{:S(2)}, u32[]{:S(2)}) collective-permute-start(bf16[16,3712]{1,0:T(8,128)(2,1)S(1)} %pad_maximum_fusion.4), channel_id=1, source_target_pairs={{0,8},{4,12},{8,0},{12,4},{1,9},{5,13},{9,1},{13,5},{2,10},{6,14},... | collective-permute-start | bytes 356360 | tf_op jit(solution)/shard_map/ppermute | solution.py:405
  12.5 0.7 %collective-permute-start.1 = (bf16[16,3584]{1,0:T(8,128)(2,1)S(1)}, bf16[16,3584]{1,0:T(8,128)(2,1)S(1)}, u32[]{:S(2)}, u32[]{:S(2)}) collective-permute-start(bf16[16,3584]{1,0:T(8,128)(2,1)S(1)} %pad_maximum_fusion.5), channel_id=1, source_target_pairs={{0,1},{1,0},{2,3},{3,2},{4,5},{5,4},{6,7},{7,6},{8,9},{9,8},{10,11... | collective-permute-start | bytes 344072 | tf_op jit(solution)/shard_map/ppermute | solution.py:405
  13.2 2.7 %load_first.1 = (bf16[3584,640]{1,0:T(8,128)(2,1)S(1)}, bf16[128,3584]{1,0:T(8,128)(2,1)S(1)}) custom-call(s32[1]{0:T(128)} %bitcast.place_ref, bf16[7168,512]{1,0:T(8,128)(2,1)} %bitcast.15, bf16[7168,512]{1,0:T(8,128)(2,1)} %shared_ref.4, bf16[512,7168]{1,0:T(8,128)(2,1)} %sdown_ref.3), custom_call_target="tpu_custom_call" | custom-call | bytes 9175040 | tf_op jit(solution)/shard_map/load_first/pallas_call | solution.py:247
  15.9 1.4 %collective-permute-done.1 = bf16[16,3584]{1,0:T(8,128)(2,1)S(1)} collective-permute-done((bf16[16,3584]{1,0:T(8,128)(2,1)S(1)}, bf16[16,3584]{1,0:T(8,128)(2,1)S(1)}, u32[]{:S(2)}, u32[]{:S(2)}) %collective-permute-start.1) | collective-permute-done | bytes 114720 | tf_op jit(solution)/shard_map/ppermute | solution.py:405
  17.4 0.0 collective-permute-done.2
  17.4 0.7 %collective-permute-start.4 = (bf16[32,3712]{1,0:T(8,128)(2,1)S(1)}, bf16[32,3712]{1,0:T(8,128)(2,1)S(1)}, u32[]{:S(2)}, u32[]{:S(2)}) collective-permute-start(bf16[32,3712]{1,0:T(8,128)(2,1)S(1)} %pad_maximum_fusion.2), channel_id=1, source_target_pairs={{0,1},{1,0},{2,3},{3,2},{4,5},{5,4},{6,7},{7,6},{8,9},{9,8},{10,11... | collective-permute-start | bytes 712712 | tf_op jit(solution)/shard_map/ppermute | solution.py:405
  18.1 0.6 %collective-permute-start.3 = (bf16[32,3584]{1,0:T(8,128)(2,1)S(1)}, bf16[32,3584]{1,0:T(8,128)(2,1)S(1)}, u32[]{:S(2)}, u32[]{:S(2)}) collective-permute-start(bf16[32,3584]{1,0:T(8,128)(2,1)S(1)} %pad_maximum_fusion.3), channel_id=1, source_target_pairs={{0,8},{4,12},{8,0},{12,4},{1,9},{5,13},{9,1},{13,5},{2,10},{6,14},... | collective-permute-start | bytes 688136 | tf_op jit(solution)/shard_map/ppermute | solution.py:405
  18.7 0.0 slice-start
  18.7 0.0 slice-start.1
  18.7 3.1 %load_late.1 = (bf16[7168,128]{1,0:T(8,128)(2,1)S(1)}, bf16[640,3584]{1,0:T(8,128)(2,1)S(1)}) custom-call(s32[1]{0:T(128)} %bitcast.place_ref, bf16[7168,512]{1,0:T(8,128)(2,1)} %shared_ref.5, bf16[512,7168]{1,0:T(8,128)(2,1)} %bitcast.10, bf16[512,7168]{1,0:T(8,128)(2,1)} %sdown_ref.3), custom_call_target="tpu_custom_call" | custom-call | bytes 12845056 | tf_op jit(solution)/shard_map/load_late/pallas_call | solution.py:222
  21.9 2.4 %collective-permute-done.3 = bf16[32,3584]{1,0:T(8,128)(2,1)S(1)} collective-permute-done((bf16[32,3584]{1,0:T(8,128)(2,1)S(1)}, bf16[32,3584]{1,0:T(8,128)(2,1)S(1)}, u32[]{:S(2)}, u32[]{:S(2)}) %collective-permute-start.3) | collective-permute-done | bytes 229408 | tf_op jit(solution)/shard_map/ppermute | solution.py:405
  24.3 0.0 collective-permute-done.4
  24.3 0.1 pad_maximum_fusion.own_ref
  24.4 0.1 collective-permute-start.6
  24.5 0.6 %collective-permute-start.5 = (bf16[64,3584]{1,0:T(8,128)(2,1)S(1)}, bf16[64,3584]{1,0:T(8,128)(2,1)S(1)}, u32[]{:S(2)}, u32[]{:S(2)}) collective-permute-start(bf16[64,3584]{1,0:T(8,128)(2,1)S(1)} %pad_maximum_fusion.1.own_ref), channel_id=1, source_target_pairs={{0,4},{4,0},{8,12},{12,8},{1,5},{5,1},{9,13},{13,9},{2,6},{6,2},{1... | collective-permute-start | bytes 1376264 | tf_op jit(solution)/shard_map/ppermute | solution.py:405
  25.1 1.2 %collective-permute-done.6.other_ref = bf16[64,3712]{1,0:T(8,128)(2,1)S(1)} collective-permute-done((bf16[64,3712]{1,0:T(8,128)(2,1)S(1)}, bf16[64,3712]{1,0:T(8,128)(2,1)S(1)}, u32[]{:S(2)}, u32[]{:S(2)}) %collective-permute-start.6) | collective-permute-done | bytes 475168 | tf_op jit(solution)/shard_map/ppermute | solution.py:405
  26.3 0.0 slice-done
  26.3 0.0 slice-done.1
  26.3 1.6 %late_half.1 = (f32[128,640]{1,0:T(8,128)S(1)}, f32[128,640]{1,0:T(8,128)S(1)}, f32[128,128]{1,0:T(8,128)S(1)}) custom-call(s32[1]{0:T(128)} %bitcast.place_ref, bf16[64,3712]{1,0:T(8,128)(2,1)S(1)} %pad_maximum_fusion.own_ref, bf16[64,3712]{1,0:T(8,128)(2,1)S(1)} %collective-permute-done.6.other_ref, bf16[3584,640]{1,0:T(8,128)(2,1)S(1)} %load_weights.1.gate_ref, ...), custom_call_target="tpu_custom_call" | custom-call | flops 1174405120 | bytes 9175040 | tf_op jit(solution)/shard_map/late_half/pallas_call | solution.py:329
  28.0 0.0 collective-permute-done.5.other_ref
  28.0 0.0 slice-start.3
  28.0 2.4 %early_half.1 = (bf16[64,3584]{1,0:T(8,128)(2,1)S(1)}, bf16[64,3584]{1,0:T(8,128)(2,1)S(1)}, bf16[128,640]{1,0:T(8,128)(2,1)S(1)}) custom-call(s32[1]{0:T(128)} %bitcast.place_ref, bf16[64,3584]{1,0:T(8,128)(2,1)S(1)} %pad_maximum_fusion.1.own_ref, bf16[64,3584]{1,0:T(8,128)(2,1)S(1)} %collective-permute-done.5.other_ref, ...), custom_call_target="tpu_custom_call" | custom-call | flops 1761607680 | bytes 13762560 | tf_op jit(solution)/shard_map/early_half/pallas_call | solution.py:339
  30.4 0.2 collective-permute-start.7
  30.6 0.0 slice-done.2
  30.6 0.0 slice-done.3
  30.6 0.9 %last_half.1 = (bf16[64,3584]{1,0:T(8,128)(2,1)S(1)}, bf16[64,3584]{1,0:T(8,128)(2,1)S(1)}) custom-call(bf16[128,640]{1,0:T(8,128)(2,1)S(1)} %get-tuple-element.52.act_ref, bf16[512,7168]{1,0:T(8,128)(2,1)S(1)} %bitcast.13, bf16[128,3584]{1,0:T(8,128)(2,1)S(1)} %get-tuple-element.53.rows_ref), custom_call_target="tpu_custom_call" | custom-call | flops 587202560 | bytes 4587520 | tf_op jit(solution)/shard_map/last_half/pallas_call | solution.py:353
  31.5 0.8 %collective-permute-done.7 = bf16[64,3584]{1,0:T(8,128)(2,1)S(1)} collective-permute-done((bf16[64,3584]{1,0:T(8,128)(2,1)S(1)}, bf16[64,3584]{1,0:T(8,128)(2,1)S(1)}, u32[]{:S(2)}, u32[]{:S(2)}) %collective-permute-start.7) | collective-permute-done | bytes 458784 | tf_op jit(solution)/shard_map/ppermute | solution.py:405
  32.3 0.1 collective-permute-start.11
  32.4 0.1 add_convert_fusion.1
  32.5 0.6 %collective-permute-start.8 = (bf16[32,3584]{1,0:T(8,128)(2,1)S(1)}, bf16[32,3584]{1,0:T(8,128)(2,1)S(1)}, u32[]{:S(2)}, u32[]{:S(2)}) collective-permute-start(bf16[32,3584]{1,0:T(8,128)(2,1)S(1)} %get-tuple-element.57), channel_id=1, source_target_pairs={{0,8},{4,12},{8,0},{12,4},{1,9},{5,13},{9,1},{13,5},{2,10},{6,14},... | collective-permute-start | bytes 688136 | tf_op jit(solution)/shard_map/ppermute | solution.py:405
  33.2 0.9 %collective-permute-done.11 = bf16[64,3584]{1,0:T(8,128)(2,1)S(1)} collective-permute-done((bf16[64,3584]{1,0:T(8,128)(2,1)S(1)}, bf16[64,3584]{1,0:T(8,128)(2,1)S(1)}, u32[]{:S(2)}, u32[]{:S(2)}) %collective-permute-start.11) | collective-permute-done | bytes 458784 | tf_op jit(solution)/shard_map/ppermute | solution.py:405
  34.1 0.1 add_convert_fusion
  34.2 1.3 %collective-permute-start.12 = (bf16[32,3584]{1,0:T(8,128)(2,1)S(1)}, bf16[32,3584]{1,0:T(8,128)(2,1)S(1)}, u32[]{:S(2)}, u32[]{:S(2)}) collective-permute-start(bf16[32,3584]{1,0:T(8,128)(2,1)S(1)} %get-tuple-element.59), channel_id=1, source_target_pairs={{0,1},{1,0},{2,3},{3,2},{4,5},{5,4},{6,7},{7,6},{8,9},{9,8},{10,11... | collective-permute-start | bytes 688136 | tf_op jit(solution)/shard_map/ppermute | solution.py:405
  35.5 4.9 %collective-permute-done.8 = bf16[32,3584]{1,0:T(8,128)(2,1)S(1)} collective-permute-done((bf16[32,3584]{1,0:T(8,128)(2,1)S(1)}, bf16[32,3584]{1,0:T(8,128)(2,1)S(1)}, u32[]{:S(2)}, u32[]{:S(2)}) %collective-permute-start.8) | collective-permute-done | bytes 229408 | tf_op jit(solution)/shard_map/ppermute | solution.py:405
  40.5 1.3 %collective-permute-start.9 = (bf16[16,3584]{1,0:T(8,128)(2,1)S(1)}, bf16[16,3584]{1,0:T(8,128)(2,1)S(1)}, u32[]{:S(2)}, u32[]{:S(2)}) collective-permute-start(bf16[16,3584]{1,0:T(8,128)(2,1)S(1)} %get-tuple-element.61), channel_id=1, source_target_pairs={{0,1},{1,0},{2,3},{3,2},{4,5},{5,4},{6,7},{7,6},{8,9},{9,8},{10,11... | collective-permute-start | bytes 344072 | tf_op jit(solution)/shard_map/ppermute | solution.py:405
  41.8 0.1 collective-permute-done.12
  41.9 0.6 %collective-permute-start.13 = (bf16[16,3584]{1,0:T(8,128)(2,1)S(1)}, bf16[16,3584]{1,0:T(8,128)(2,1)S(1)}, u32[]{:S(2)}, u32[]{:S(2)}) collective-permute-start(bf16[16,3584]{1,0:T(8,128)(2,1)S(1)} %get-tuple-element.63), channel_id=1, source_target_pairs={{0,8},{4,12},{8,0},{12,4},{1,9},{5,13},{9,1},{13,5},{2,10},{6,14},... | collective-permute-start | bytes 344072 | tf_op jit(solution)/shard_map/ppermute | solution.py:405
  42.6 2.8 %collective-permute-done.9 = bf16[16,3584]{1,0:T(8,128)(2,1)S(1)} collective-permute-done((bf16[16,3584]{1,0:T(8,128)(2,1)S(1)}, bf16[16,3584]{1,0:T(8,128)(2,1)S(1)}, u32[]{:S(2)}, u32[]{:S(2)}) %collective-permute-start.9) | collective-permute-done | bytes 114720 | tf_op jit(solution)/shard_map/ppermute | solution.py:405
  45.4 3.5 %collective-permute-start.10 = (bf16[8,3584]{1,0:T(8,128)(2,1)S(1)}, bf16[8,3584]{1,0:T(8,128)(2,1)S(1)}, u32[]{:S(2)}, u32[]{:S(2)}) collective-permute-start(bf16[8,3584]{1,0:T(8,128)(2,1)S(1)} %fusion.5), channel_id=1, source_target_pairs={{0,2},{1,3},{2,0},{3,1},{4,6},{5,7},{6,4},{7,5},{8,10},{9,11},{10,... | collective-permute-start | bytes 172040 | tf_op jit(solution)/shard_map/ppermute | solution.py:405
  48.9 0.0 collective-permute-done.13
  48.9 1.3 %collective-permute-start.14 = (bf16[8,3584]{1,0:T(8,128)(2,1)S(1)}, bf16[8,3584]{1,0:T(8,128)(2,1)S(1)}, u32[]{:S(2)}, u32[]{:S(2)}) collective-permute-start(bf16[8,3584]{1,0:T(8,128)(2,1)S(1)} %fusion.2), channel_id=1, source_target_pairs={{0,2},{1,3},{2,0},{3,1},{4,6},{5,7},{6,4},{7,5},{8,10},{9,11},{10,... | collective-permute-start | bytes 172040 | tf_op jit(solution)/shard_map/ppermute | solution.py:405
  50.3 2.5 %collective-permute-done.10 = bf16[8,3584]{1,0:T(8,128)(2,1)S(1)} collective-permute-done((bf16[8,3584]{1,0:T(8,128)(2,1)S(1)}, bf16[8,3584]{1,0:T(8,128)(2,1)S(1)}, u32[]{:S(2)}, u32[]{:S(2)}) %collective-permute-start.10) | collective-permute-done | bytes 57376 | tf_op jit(solution)/shard_map/ppermute | solution.py:405
  52.8 1.8 %collective-permute-done.14 = bf16[8,3584]{1,0:T(8,128)(2,1)S(1)} collective-permute-done((bf16[8,3584]{1,0:T(8,128)(2,1)S(1)}, bf16[8,3584]{1,0:T(8,128)(2,1)S(1)}, u32[]{:S(2)}, u32[]{:S(2)}) %collective-permute-start.14) | collective-permute-done | bytes 57376 | tf_op jit(solution)/shard_map/ppermute | solution.py:405
  54.6 0.7 %pad_maximum_fusion.6 = bf16[8,7168]{1,0:T(8,128)(2,1)} fusion(bf16[8,3584]{1,0:T(8,128)(2,1)S(1)} %fusion.4, bf16[8,3584]{1,0:T(8,128)(2,1)S(1)} %fusion.7), kind=kLoop, calls=%fused_computation.26 | loop fusion | flops 229376 | bytes 229376 | tf_op jit(solution)/shard_map/concatenate | solution.py:473
  (15 shorter events, 0.3 us)
Async XLA Ops:
  1.1 9.8 %collective-permute-start = (bf16[8,7296]{1,0:T(8,128)(2,1)S(1)}, bf16[8,7296]{1,0:T(8,128)(2,1)S(1)}, u32[]{:S(2)}, u32[]{:S(2)}) collective-permute-start(bf16[8,7296]{1,0:T(8,128)(2,1)S(1)} %pack_rows.1), channel_id=1, source_target_pairs={{0,2},{1,3},{2,0},{3,1},{4,6},{5,7},{6,4},{7,5},{8,10},{9,11},{10,... | collective-permute-start | bytes 350216 | tf_op jit(solution)/shard_map/ppermute | solution.py:405
  10.9 6.5 %collective-permute-start.2 = (bf16[16,3712]{1,0:T(8,128)(2,1)S(1)}, bf16[16,3712]{1,0:T(8,128)(2,1)S(1)}, u32[]{:S(2)}, u32[]{:S(2)}) collective-permute-start(bf16[16,3712]{1,0:T(8,128)(2,1)S(1)} %pad_maximum_fusion.4), channel_id=1, source_target_pairs={{0,8},{4,12},{8,0},{12,4},{1,9},{5,13},{9,1},{13,5},{2,10},{6,14},... | collective-permute-start | bytes 356360 | tf_op jit(solution)/shard_map/ppermute | solution.py:405
  12.5 4.9 %collective-permute-start.1 = (bf16[16,3584]{1,0:T(8,128)(2,1)S(1)}, bf16[16,3584]{1,0:T(8,128)(2,1)S(1)}, u32[]{:S(2)}, u32[]{:S(2)}) collective-permute-start(bf16[16,3584]{1,0:T(8,128)(2,1)S(1)} %pad_maximum_fusion.5), channel_id=1, source_target_pairs={{0,1},{1,0},{2,3},{3,2},{4,5},{5,4},{6,7},{7,6},{8,9},{9,8},{10,11... | collective-permute-start | bytes 344072 | tf_op jit(solution)/shard_map/ppermute | solution.py:405
  17.4 6.9 %collective-permute-start.4 = (bf16[32,3712]{1,0:T(8,128)(2,1)S(1)}, bf16[32,3712]{1,0:T(8,128)(2,1)S(1)}, u32[]{:S(2)}, u32[]{:S(2)}) collective-permute-start(bf16[32,3712]{1,0:T(8,128)(2,1)S(1)} %pad_maximum_fusion.2), channel_id=1, source_target_pairs={{0,1},{1,0},{2,3},{3,2},{4,5},{5,4},{6,7},{7,6},{8,9},{9,8},{10,11... | collective-permute-start | bytes 712712 | tf_op jit(solution)/shard_map/ppermute | solution.py:405
  18.1 6.2 %collective-permute-start.3 = (bf16[32,3584]{1,0:T(8,128)(2,1)S(1)}, bf16[32,3584]{1,0:T(8,128)(2,1)S(1)}, u32[]{:S(2)}, u32[]{:S(2)}) collective-permute-start(bf16[32,3584]{1,0:T(8,128)(2,1)S(1)} %pad_maximum_fusion.3), channel_id=1, source_target_pairs={{0,8},{4,12},{8,0},{12,4},{1,9},{5,13},{9,1},{13,5},{2,10},{6,14},... | collective-permute-start | bytes 688136 | tf_op jit(solution)/shard_map/ppermute | solution.py:405
  18.7 7.6 %slice-start = ((s8[7340032]{0:T(1024)(128)(4,1)}), s8[4194304]{0:T(1024)(128)(4,1)S(1)}, s32[]{:S(2)}) async-start(s8[7340032]{0:T(1024)(128)(4,1)} %bitcast.6), calls=%async_computation | async-start | bytes 8388608
  18.7 7.6 %slice-start.1 = ((s8[7340032]{0:T(1024)(128)(4,1)}), s8[3145728]{0:T(1024)(128)(4,1)S(1)}, s32[]{:S(2)}) async-start(s8[7340032]{0:T(1024)(128)(4,1)} %bitcast.6), calls=%async_computation.1 | async-start | bytes 6291456
  24.4 1.9 %collective-permute-start.6 = (bf16[64,3712]{1,0:T(8,128)(2,1)S(1)}, bf16[64,3712]{1,0:T(8,128)(2,1)S(1)}, u32[]{:S(2)}, u32[]{:S(2)}) collective-permute-start(bf16[64,3712]{1,0:T(8,128)(2,1)S(1)} %pad_maximum_fusion.own_ref), channel_id=1, source_target_pairs={{0,4},{4,0},{8,12},{12,8},{1,5},{5,1},{9,13},{13,9},{2,6},{6,2},{1... | collective-permute-start | bytes 1425416 | tf_op jit(solution)/shard_map/ppermute | solution.py:405
  24.5 3.5 %collective-permute-start.5 = (bf16[64,3584]{1,0:T(8,128)(2,1)S(1)}, bf16[64,3584]{1,0:T(8,128)(2,1)S(1)}, u32[]{:S(2)}, u32[]{:S(2)}) collective-permute-start(bf16[64,3584]{1,0:T(8,128)(2,1)S(1)} %pad_maximum_fusion.1.own_ref), channel_id=1, source_target_pairs={{0,4},{4,0},{8,12},{12,8},{1,5},{5,1},{9,13},{13,9},{2,6},{6,2},{1... | collective-permute-start | bytes 1376264 | tf_op jit(solution)/shard_map/ppermute | solution.py:405
  26.3 4.3 %slice-start.2 = ((s8[7340032]{0:T(1024)(128)(4,1)}), s8[4194304]{0:T(1024)(128)(4,1)S(1)}, s32[]{:S(2)}) async-start(s8[7340032]{0:T(1024)(128)(4,1)} %bitcast.11), calls=%async_computation.2 | async-start | bytes 8388608
  28.0 2.6 %slice-start.3 = ((s8[7340032]{0:T(1024)(128)(4,1)}), s8[3145728]{0:T(1024)(128)(4,1)S(1)}, s32[]{:S(2)}) async-start(s8[7340032]{0:T(1024)(128)(4,1)} %bitcast.11), calls=%async_computation.3 | async-start | bytes 6291456
  30.4 1.9 %collective-permute-start.7 = (bf16[64,3584]{1,0:T(8,128)(2,1)S(1)}, bf16[64,3584]{1,0:T(8,128)(2,1)S(1)}, u32[]{:S(2)}, u32[]{:S(2)}) collective-permute-start(bf16[64,3584]{1,0:T(8,128)(2,1)S(1)} %get-tuple-element.51), channel_id=1, source_target_pairs={{0,4},{4,0},{8,12},{12,8},{1,5},{5,1},{9,13},{13,9},{2,6},{6,2},{1... | collective-permute-start | bytes 1376264 | tf_op jit(solution)/shard_map/ppermute | solution.py:405
  32.3 1.8 %collective-permute-start.11 = (bf16[64,3584]{1,0:T(8,128)(2,1)S(1)}, bf16[64,3584]{1,0:T(8,128)(2,1)S(1)}, u32[]{:S(2)}, u32[]{:S(2)}) collective-permute-start(bf16[64,3584]{1,0:T(8,128)(2,1)S(1)} %get-tuple-element.56), channel_id=1, source_target_pairs={{0,4},{4,0},{8,12},{12,8},{1,5},{5,1},{9,13},{13,9},{2,6},{6,2},{1... | collective-permute-start | bytes 1376264 | tf_op jit(solution)/shard_map/ppermute | solution.py:405
  32.5 7.9 %collective-permute-start.8 = (bf16[32,3584]{1,0:T(8,128)(2,1)S(1)}, bf16[32,3584]{1,0:T(8,128)(2,1)S(1)}, u32[]{:S(2)}, u32[]{:S(2)}) collective-permute-start(bf16[32,3584]{1,0:T(8,128)(2,1)S(1)} %get-tuple-element.57), channel_id=1, source_target_pairs={{0,8},{4,12},{8,0},{12,4},{1,9},{5,13},{9,1},{13,5},{2,10},{6,14},... | collective-permute-start | bytes 688136 | tf_op jit(solution)/shard_map/ppermute | solution.py:405
  34.2 7.7 %collective-permute-start.12 = (bf16[32,3584]{1,0:T(8,128)(2,1)S(1)}, bf16[32,3584]{1,0:T(8,128)(2,1)S(1)}, u32[]{:S(2)}, u32[]{:S(2)}) collective-permute-start(bf16[32,3584]{1,0:T(8,128)(2,1)S(1)} %get-tuple-element.59), channel_id=1, source_target_pairs={{0,1},{1,0},{2,3},{3,2},{4,5},{5,4},{6,7},{7,6},{8,9},{9,8},{10,11... | collective-permute-start | bytes 688136 | tf_op jit(solution)/shard_map/ppermute | solution.py:405
  40.5 4.9 %collective-permute-start.9 = (bf16[16,3584]{1,0:T(8,128)(2,1)S(1)}, bf16[16,3584]{1,0:T(8,128)(2,1)S(1)}, u32[]{:S(2)}, u32[]{:S(2)}) collective-permute-start(bf16[16,3584]{1,0:T(8,128)(2,1)S(1)} %get-tuple-element.61), channel_id=1, source_target_pairs={{0,1},{1,0},{2,3},{3,2},{4,5},{5,4},{6,7},{7,6},{8,9},{9,8},{10,11... | collective-permute-start | bytes 344072 | tf_op jit(solution)/shard_map/ppermute | solution.py:405
  41.9 7.0 %collective-permute-start.13 = (bf16[16,3584]{1,0:T(8,128)(2,1)S(1)}, bf16[16,3584]{1,0:T(8,128)(2,1)S(1)}, u32[]{:S(2)}, u32[]{:S(2)}) collective-permute-start(bf16[16,3584]{1,0:T(8,128)(2,1)S(1)} %get-tuple-element.63), channel_id=1, source_target_pairs={{0,8},{4,12},{8,0},{12,4},{1,9},{5,13},{9,1},{13,5},{2,10},{6,14},... | collective-permute-start | bytes 344072 | tf_op jit(solution)/shard_map/ppermute | solution.py:405
  45.4 7.4 %collective-permute-start.10 = (bf16[8,3584]{1,0:T(8,128)(2,1)S(1)}, bf16[8,3584]{1,0:T(8,128)(2,1)S(1)}, u32[]{:S(2)}, u32[]{:S(2)}) collective-permute-start(bf16[8,3584]{1,0:T(8,128)(2,1)S(1)} %fusion.5), channel_id=1, source_target_pairs={{0,2},{1,3},{2,0},{3,1},{4,6},{5,7},{6,4},{7,5},{8,10},{9,11},{10,... | collective-permute-start | bytes 172040 | tf_op jit(solution)/shard_map/ppermute | solution.py:405
  48.9 5.7 %collective-permute-start.14 = (bf16[8,3584]{1,0:T(8,128)(2,1)S(1)}, bf16[8,3584]{1,0:T(8,128)(2,1)S(1)}, u32[]{:S(2)}, u32[]{:S(2)}) collective-permute-start(bf16[8,3584]{1,0:T(8,128)(2,1)S(1)} %fusion.2), channel_id=1, source_target_pairs={{0,2},{1,3},{2,0},{3,1},{4,6},{5,7},{6,4},{7,5},{8,10},{9,11},{10,... | collective-permute-start | bytes 172040 | tf_op jit(solution)/shard_map/ppermute | solution.py:405

commit v25 on v23

--- a/solution.py
+++ b/solution.py
@@ -198,7 +198,9 @@
     return copies
 
 
-def load_late_kernel(share, place_ref, shared_ref, down_ref, sdown_ref, out_ref, down_out_ref, sems):
+def load_late_kernel(
+    share, place_ref, shared_ref, down_ref, sdown_ref, out_ref, down_out_ref, rows_ref, sems
+):
     parts = 4
     column = pl.multiple_of((place_ref[0] // share) * LANES, LANES)
     piece = shared_ref.shape[0] // parts
@@ -210,9 +212,15 @@
         )
         for i in range(parts)
     ]
+    rows = pltpu.make_async_copy(
+        sdown_ref.at[pl.ds(column, LANES), pl.ds(down_out_ref.shape[1], rows_ref.shape[1])],
+        rows_ref,
+        sems.at[parts],
+    )
     run_copies(
         copies
-        + down_range_copies(share, place_ref, down_ref, sdown_ref, down_out_ref, 0, sems.at[parts:])
+        + [rows]
+        + down_range_copies(share, place_ref, down_ref, sdown_ref, down_out_ref, 0, sems.at[parts + 1 :])
     )
 
 
@@ -222,38 +230,19 @@
     return pl.pallas_call(
         functools.partial(load_late_kernel, share),
         in_specs=[SMEM_SPEC] + [ANY_SPEC] * 3,
-        out_specs=[VMEM_SPEC] * 2,
-        out_shape=[pltpu.VMEM((width, LANES), BF16), pltpu.VMEM((units, columns), BF16)],
-        scratch_shapes=[pltpu.SemaphoreType.DMA((4 + units // DOWN_ROWS,))],
+        out_specs=[VMEM_SPEC] * 3,
+        out_shape=[
+            pltpu.VMEM((width, LANES), BF16),
+            pltpu.VMEM((units, columns), BF16),
+            pltpu.VMEM((LANES, sdown.shape[1] - columns), BF16),
+        ],
+        scratch_shapes=[pltpu.SemaphoreType.DMA((5 + units // DOWN_ROWS,))],
         cost_estimate=pl.CostEstimate(
             flops=0, bytes_accessed=4 * (units * columns + width * LANES), transcendentals=0
         ),
         compiler_params=pltpu.CompilerParams(vmem_limit_bytes=1 << 20),
         name="load_late",
     )(place, *(in_hbm(w) for w in (shared, down, sdown)))
-
-
-def load_first_kernel(share, lower, place_ref, routed_ref, shared_ref, sdown_ref, out_ref, rows_ref, sems):
-    parts = 4
-    column = pl.multiple_of((place_ref[0] // share) * LANES, LANES)
-    rows = pltpu.make_async_copy(
-        sdown_ref.at[pl.ds(column, LANES), pl.ds(lower, rows_ref.shape[1])], rows_ref, sems.at[2 * parts]
-    )
-    run_copies(weight_copies(share, place_ref, routed_ref, shared_ref, out_ref, sems, parts) + [rows])
-
-
-def load_first(place, routed, shared, sdown, lower, share):
-    width, units = lower, routed.shape[1] + LANES
-    return pl.pallas_call(
-        functools.partial(load_first_kernel, share, lower),
-        in_specs=[SMEM_SPEC] + [ANY_SPEC] * 3,
-        out_specs=[VMEM_SPEC] * 2,
-        out_shape=[pltpu.VMEM((width, units), BF16), pltpu.VMEM((LANES, sdown.shape[1] - lower), BF16)],
-        scratch_shapes=[pltpu.SemaphoreType.DMA((9,))],
-        cost_estimate=pl.CostEstimate(flops=0, bytes_accessed=4 * units * width, transcendentals=0),
-        compiler_params=pltpu.CompilerParams(vmem_limit_bytes=1 << 20),
-        name="load_first",
-    )(place, *(in_hbm(w) for w in (routed, shared, sdown)))
 
 
 def late_half_kernel(
@@ -444,7 +433,7 @@
     own = [packed[:, :cut], packed[:, cut:]]
     loads = (
         lambda *ready: (load_weights(after(place, *ready), gate, gate_shared, share, cut, width - cut),),
-        lambda *ready: load_first(after(place, *ready), gate, gate_shared, down_shared, cut, share),
+        lambda *ready: (load_weights(after(place, *ready), gate, gate_shared, share, 0, cut),),
         lambda *ready: load_late(after(place, *ready), up_shared, down, down_shared, cut, share),
     )
     loaded = ()
@@ -457,7 +446,7 @@
             got, weights = lax.optimization_barrier((got, weights))
         loaded += weights
         own = [stack(part, add) for part, add in zip(own, got)]
-    late_gate, gate, late_rows, sup, second = loaded
+    late_gate, gate, sup, second, late_rows = loaded
     own[1] = swap_quarters(own[1])
     other = [flipped(part, CORE) for part in own]
 

time: 54.2 us -> 54.2 us (level)
    pallas_call x1 -> x0, Pallas kernels: 2.67 us -> none  [load_first(): pl.pallas_call(functools.partial(load_first_kernel, share, lower), in_spe...]
    pallas_call x1 -> x2, Pallas kernels: 2.34 us -> 4.68 us  [load_weights(): pl.pallas_call(functools.partial(load_kernel, share, first_row), in_specs...]
where the time goes in v25:
time: 54.2 us; the launch traced here: 54.1 us
  starting transfers between devices  21.4 us (39%)
  waiting for transfers between devices  17.2 us (32%)
  Pallas kernels  14.1 us (26%)
  other arithmetic  1.09 us (2%)
    ppermute x16, starting transfers between devices, flipped(): lax.ppermute(value, ('node', 'local')[axis], [(i, i ^ bits[axis]) for i i...  21.4 us
    ppermute x16, waiting for transfers between devices, flipped(): lax.ppermute(value, ('node', 'local')[axis], [(i, i ^ bits[axis]) for i i...  17.2 us
    pallas_call x2, Pallas kernels, load_weights(): pl.pallas_call(functools.partial(load_kernel, share, first_row), in_specs...  4.68 us
    pallas_call x1, Pallas kernels, load_late(): pl.pallas_call(functools.partial(load_late_kernel, share), in_specs=[SMEM...  3.39 us
    pallas_call x1, Pallas kernels, pair_rows(): pl.pallas_call(functools.partial(early_half_kernel, share), in_specs=[SME...  2.38 us
    pallas_call x1, Pallas kernels, pair_rows(): pl.pallas_call(late_half_kernel, in_specs=[SMEM_SPEC] + [VMEM_SPEC] * 5,...  1.67 us
  transfers between devices with their start and end apart: 16, of which 12 were waited for; matrix products, arithmetic and copies ran while one was open for 1% of the time, Pallas kernels for 20%

profile of v25, /device:TPU:0, one launch (start us, length us, event | category | flops | bytes accessed | tf_op | source)
XLA Modules:
  0.0 54.1 jit_solution(18061019423903274281)
XLA Ops:
  0.0 1.1 %pack_rows.1 = bf16[8,7296]{1,0:T(8,128)(2,1)S(1)} custom-call(bf16[8,7168]{1,0:T(8,128)(2,1)} %tokens_ref.1, s32[4,8]{1,0:T(4,128)} %bitcast.16, bf16[4,8]{1,0:T(4,128)(2,1)} %bitcast.17), custom_call_target="tpu_custom_call" | custom-call | tf_op jit(solution)/shard_map/pack_rows/pallas_call | solution.py:48
  1.1 4.1 %collective-permute-start.2 = (bf16[8,3712]{1,0:T(8,128)(2,1)S(1)}, bf16[8,3712]{1,0:T(8,128)(2,1)S(1)}, u32[]{:S(2)}, u32[]{:S(2)}) collective-permute-start(bf16[8,3712]{1,0:T(8,128)(2,1)S(1)} %get-tuple-element.64), channel_id=1, source_target_pairs={{0,2},{1,3},{2,0},{3,1},{4,6},{5,7},{6,4},{7,5},{8,10},{9,11},{10,... | collective-permute-start | bytes 178184 | tf_op jit(solution)/shard_map/ppermute | solution.py:394
  5.2 0.1 collective-permute-start
  5.3 2.3 %load_weights.2.gate_ref = bf16[3584,640]{1,0:T(8,128)(2,1)S(1)} custom-call(s32[1]{0:T(128)} %bitcast.place_ref, bf16[7168,512]{1,0:T(8,128)(2,1)} %bitcast.14, bf16[7168,512]{1,0:T(8,128)(2,1)} %shared_ref.4), custom_call_target="tpu_custom_call" | custom-call | bytes 9175040 | tf_op jit(solution)/shard_map/load_weights/pallas_call | solution.py:85
  7.6 0.4 collective-permute-done.2
  8.0 2.4 %collective-permute-start.3 = (bf16[16,3712]{1,0:T(8,128)(2,1)S(1)}, bf16[16,3712]{1,0:T(8,128)(2,1)S(1)}, u32[]{:S(2)}, u32[]{:S(2)}) collective-permute-start(bf16[16,3712]{1,0:T(8,128)(2,1)S(1)} %pad_maximum_fusion.3), channel_id=1, source_target_pairs={{0,8},{4,12},{8,0},{12,4},{1,9},{5,13},{9,1},{13,5},{2,10},{6,14},... | collective-permute-start | bytes 356360 | tf_op jit(solution)/shard_map/ppermute | solution.py:394
  10.4 0.1 collective-permute-done
  10.6 1.5 %collective-permute-start.1 = (bf16[16,3584]{1,0:T(8,128)(2,1)S(1)}, bf16[16,3584]{1,0:T(8,128)(2,1)S(1)}, u32[]{:S(2)}, u32[]{:S(2)}) collective-permute-start(bf16[16,3584]{1,0:T(8,128)(2,1)S(1)} %pad_maximum_fusion.4), channel_id=1, source_target_pairs={{0,1},{1,0},{2,3},{3,2},{4,5},{5,4},{6,7},{7,6},{8,9},{9,8},{10,11... | collective-permute-start | bytes 344072 | tf_op jit(solution)/shard_map/ppermute | solution.py:394
  12.1 2.3 %load_weights.3.gate_ref = bf16[3584,640]{1,0:T(8,128)(2,1)S(1)} custom-call(s32[1]{0:T(128)} %bitcast.place_ref, bf16[7168,512]{1,0:T(8,128)(2,1)} %bitcast.15, bf16[7168,512]{1,0:T(8,128)(2,1)} %shared_ref.4), custom_call_target="tpu_custom_call" | custom-call | bytes 9175040 | tf_op jit(solution)/shard_map/load_weights/pallas_call | solution.py:85
  14.5 1.0 %collective-permute-done.1 = bf16[16,3584]{1,0:T(8,128)(2,1)S(1)} collective-permute-done((bf16[16,3584]{1,0:T(8,128)(2,1)S(1)}, bf16[16,3584]{1,0:T(8,128)(2,1)S(1)}, u32[]{:S(2)}, u32[]{:S(2)}) %collective-permute-start.1) | collective-permute-done | bytes 114720 | tf_op jit(solution)/shard_map/ppermute | solution.py:394
  15.4 0.0 collective-permute-done.3
  15.4 0.0 slice-start
  15.5 1.5 %collective-permute-start.5 = (bf16[32,3712]{1,0:T(8,128)(2,1)S(1)}, bf16[32,3712]{1,0:T(8,128)(2,1)S(1)}, u32[]{:S(2)}, u32[]{:S(2)}) collective-permute-start(bf16[32,3712]{1,0:T(8,128)(2,1)S(1)} %pad_maximum_fusion.1), channel_id=1, source_target_pairs={{0,1},{1,0},{2,3},{3,2},{4,5},{5,4},{6,7},{7,6},{8,9},{9,8},{10,11... | collective-permute-start | bytes 712712 | tf_op jit(solution)/shard_map/ppermute | solution.py:394
  17.0 1.4 %collective-permute-start.4 = (bf16[32,3584]{1,0:T(8,128)(2,1)S(1)}, bf16[32,3584]{1,0:T(8,128)(2,1)S(1)}, u32[]{:S(2)}, u32[]{:S(2)}) collective-permute-start(bf16[32,3584]{1,0:T(8,128)(2,1)S(1)} %pad_maximum_fusion.2), channel_id=1, source_target_pairs={{0,8},{4,12},{8,0},{12,4},{1,9},{5,13},{9,1},{13,5},{2,10},{6,14},... | collective-permute-start | bytes 688136 | tf_op jit(solution)/shard_map/ppermute | solution.py:394
  18.4 3.4 %load_late.1 = (bf16[7168,128]{1,0:T(8,128)(2,1)S(1)}, bf16[640,3584]{1,0:T(8,128)(2,1)S(1)}, bf16[128,3584]{1,0:T(8,128)(2,1)S(1)}) custom-call(s32[1]{0:T(128)} %bitcast.place_ref, bf16[7168,512]{1,0:T(8,128)(2,1)} %shared_ref.5, bf16[512,7168]{1,0:T(8,128)(2,1)} %bitcast.10, bf16[512,7168]{1,0:T(8,128)(2,1)} %sdown_ref.1), custom_call_target="tpu_custom_call" | custom-call | bytes 12845056 | tf_op jit(solution)/shard_map/load_late/pallas_call | solution.py:230
  21.8 1.3 %collective-permute-done.4 = bf16[32,3584]{1,0:T(8,128)(2,1)S(1)} collective-permute-done((bf16[32,3584]{1,0:T(8,128)(2,1)S(1)}, bf16[32,3584]{1,0:T(8,128)(2,1)S(1)}, u32[]{:S(2)}, u32[]{:S(2)}) %collective-permute-start.4) | collective-permute-done | bytes 229408 | tf_op jit(solution)/shard_map/ppermute | solution.py:394
  23.1 0.0 collective-permute-done.5
  23.2 0.1 collective-permute-start.7
  23.3 0.6 %collective-permute-start.6 = (bf16[64,3584]{1,0:T(8,128)(2,1)S(1)}, bf16[64,3584]{1,0:T(8,128)(2,1)S(1)}, u32[]{:S(2)}, u32[]{:S(2)}) collective-permute-start(bf16[64,3584]{1,0:T(8,128)(2,1)S(1)} %pad_maximum_fusion.own_ref), channel_id=1, source_target_pairs={{0,4},{4,0},{8,12},{12,8},{1,5},{5,1},{9,13},{13,9},{2,6},{6,2},{1... | collective-permute-start | bytes 1376264 | tf_op jit(solution)/shard_map/ppermute | solution.py:394
  23.8 1.2 %collective-permute-done.7.other_ref = bf16[64,3712]{1,0:T(8,128)(2,1)S(1)} collective-permute-done((bf16[64,3712]{1,0:T(8,128)(2,1)S(1)}, bf16[64,3712]{1,0:T(8,128)(2,1)S(1)}, u32[]{:S(2)}, u32[]{:S(2)}) %collective-permute-start.7) | collective-permute-done | bytes 475168 | tf_op jit(solution)/shard_map/ppermute | solution.py:394
  25.1 0.0 slice-done
  25.1 0.0 slice-done.1
  25.1 1.7 %late_half.1 = (f32[128,640]{1,0:T(8,128)S(1)}, f32[128,640]{1,0:T(8,128)S(1)}, f32[128,128]{1,0:T(8,128)S(1)}) custom-call(s32[1]{0:T(128)} %bitcast.place_ref, bf16[64,3712]{1,0:T(8,128)(2,1)S(1)} %slice_dynamic-update-slice_fusion.own_ref, bf16[64,3712]{1,0:T(8,128)(2,1)S(1)} %collective-permute-done.7.other_ref, ...), custom_call_target="tpu_custom_call" | custom-call | flops 1174405120 | bytes 9175040 | tf_op jit(solution)/shard_map/late_half/pallas_call | solution.py:318
  26.8 0.0 collective-permute-done.6.other_ref
  26.8 0.0 slice-start.3
  26.8 2.4 %early_half.1 = (bf16[64,3584]{1,0:T(8,128)(2,1)S(1)}, bf16[64,3584]{1,0:T(8,128)(2,1)S(1)}, bf16[128,640]{1,0:T(8,128)(2,1)S(1)}) custom-call(s32[1]{0:T(128)} %bitcast.place_ref, bf16[64,3584]{1,0:T(8,128)(2,1)S(1)} %pad_maximum_fusion.own_ref, bf16[64,3584]{1,0:T(8,128)(2,1)S(1)} %collective-permute-done.6.other_ref, ...), custom_call_target="tpu_custom_call" | custom-call | flops 1761607680 | bytes 13762560 | tf_op jit(solution)/shard_map/early_half/pallas_call | solution.py:328
  29.2 0.2 collective-permute-start.8
  29.4 0.0 slice-done.2
  29.4 0.0 slice-done.3
  29.4 0.9 %last_half.1 = (bf16[64,3584]{1,0:T(8,128)(2,1)S(1)}, bf16[64,3584]{1,0:T(8,128)(2,1)S(1)}) custom-call(bf16[128,640]{1,0:T(8,128)(2,1)S(1)} %get-tuple-element.50.act_ref, bf16[512,7168]{1,0:T(8,128)(2,1)S(1)} %bitcast.13, bf16[128,3584]{1,0:T(8,128)(2,1)S(1)} %get-tuple-element.51.rows_ref), custom_call_target="tpu_custom_call" | custom-call | flops 587202560 | bytes 4587520 | tf_op jit(solution)/shard_map/last_half/pallas_call | solution.py:342
  30.3 0.8 %collective-permute-done.8 = bf16[64,3584]{1,0:T(8,128)(2,1)S(1)} collective-permute-done((bf16[64,3584]{1,0:T(8,128)(2,1)S(1)}, bf16[64,3584]{1,0:T(8,128)(2,1)S(1)}, u32[]{:S(2)}, u32[]{:S(2)}) %collective-permute-start.8) | collective-permute-done | bytes 458784 | tf_op jit(solution)/shard_map/ppermute | solution.py:394
  31.1 0.1 collective-permute-start.12
  31.2 0.1 add_convert_fusion.1
  31.3 1.5 %collective-permute-start.9 = (bf16[32,3584]{1,0:T(8,128)(2,1)S(1)}, bf16[32,3584]{1,0:T(8,128)(2,1)S(1)}, u32[]{:S(2)}, u32[]{:S(2)}) collective-permute-start(bf16[32,3584]{1,0:T(8,128)(2,1)S(1)} %get-tuple-element.55), channel_id=1, source_target_pairs={{0,8},{4,12},{8,0},{12,4},{1,9},{5,13},{9,1},{13,5},{2,10},{6,14},... | collective-permute-start | bytes 688136 | tf_op jit(solution)/shard_map/ppermute | solution.py:394
  32.8 0.1 collective-permute-done.12
  32.9 0.1 add_convert_fusion
  33.0 0.8 %collective-permute-start.13 = (bf16[32,3584]{1,0:T(8,128)(2,1)S(1)}, bf16[32,3584]{1,0:T(8,128)(2,1)S(1)}, u32[]{:S(2)}, u32[]{:S(2)}) collective-permute-start(bf16[32,3584]{1,0:T(8,128)(2,1)S(1)} %get-tuple-element.57), channel_id=1, source_target_pairs={{0,1},{1,0},{2,3},{3,2},{4,5},{5,4},{6,7},{7,6},{8,9},{9,8},{10,11... | collective-permute-start | bytes 688136 | tf_op jit(solution)/shard_map/ppermute | solution.py:394
  33.7 5.5 %collective-permute-done.9 = bf16[32,3584]{1,0:T(8,128)(2,1)S(1)} collective-permute-done((bf16[32,3584]{1,0:T(8,128)(2,1)S(1)}, bf16[32,3584]{1,0:T(8,128)(2,1)S(1)}, u32[]{:S(2)}, u32[]{:S(2)}) %collective-permute-start.9) | collective-permute-done | bytes 229408 | tf_op jit(solution)/shard_map/ppermute | solution.py:394
  39.3 0.6 %collective-permute-start.10 = (bf16[16,3584]{1,0:T(8,128)(2,1)S(1)}, bf16[16,3584]{1,0:T(8,128)(2,1)S(1)}, u32[]{:S(2)}, u32[]{:S(2)}) collective-permute-start(bf16[16,3584]{1,0:T(8,128)(2,1)S(1)} %get-tuple-element.59), channel_id=1, source_target_pairs={{0,1},{1,0},{2,3},{3,2},{4,5},{5,4},{6,7},{7,6},{8,9},{9,8},{10,11... | collective-permute-start | bytes 344072 | tf_op jit(solution)/shard_map/ppermute | solution.py:394
  39.9 0.8 %collective-permute-done.13 = bf16[32,3584]{1,0:T(8,128)(2,1)S(1)} collective-permute-done((bf16[32,3584]{1,0:T(8,128)(2,1)S(1)}, bf16[32,3584]{1,0:T(8,128)(2,1)S(1)}, u32[]{:S(2)}, u32[]{:S(2)}) %collective-permute-start.13) | collective-permute-done | bytes 229408 | tf_op jit(solution)/shard_map/ppermute | solution.py:394
  40.7 1.5 %collective-permute-start.14 = (bf16[16,3584]{1,0:T(8,128)(2,1)S(1)}, bf16[16,3584]{1,0:T(8,128)(2,1)S(1)}, u32[]{:S(2)}, u32[]{:S(2)}) collective-permute-start(bf16[16,3584]{1,0:T(8,128)(2,1)S(1)} %get-tuple-element.61), channel_id=1, source_target_pairs={{0,8},{4,12},{8,0},{12,4},{1,9},{5,13},{9,1},{13,5},{2,10},{6,14},... | collective-permute-start | bytes 344072 | tf_op jit(solution)/shard_map/ppermute | solution.py:394
  42.2 1.9 %collective-permute-done.10 = bf16[16,3584]{1,0:T(8,128)(2,1)S(1)} collective-permute-done((bf16[16,3584]{1,0:T(8,128)(2,1)S(1)}, bf16[16,3584]{1,0:T(8,128)(2,1)S(1)}, u32[]{:S(2)}, u32[]{:S(2)}) %collective-permute-start.10) | collective-permute-done | bytes 114720 | tf_op jit(solution)/shard_map/ppermute | solution.py:394
  44.2 3.5 %collective-permute-start.11 = (bf16[8,3584]{1,0:T(8,128)(2,1)S(1)}, bf16[8,3584]{1,0:T(8,128)(2,1)S(1)}, u32[]{:S(2)}, u32[]{:S(2)}) collective-permute-start(bf16[8,3584]{1,0:T(8,128)(2,1)S(1)} %fusion.5), channel_id=1, source_target_pairs={{0,2},{1,3},{2,0},{3,1},{4,6},{5,7},{6,4},{7,5},{8,10},{9,11},{10,... | collective-permute-start | bytes 172040 | tf_op jit(solution)/shard_map/ppermute | solution.py:394
  47.7 0.0 collective-permute-done.14
  47.7 1.5 %collective-permute-start.15 = (bf16[8,3584]{1,0:T(8,128)(2,1)S(1)}, bf16[8,3584]{1,0:T(8,128)(2,1)S(1)}, u32[]{:S(2)}, u32[]{:S(2)}) collective-permute-start(bf16[8,3584]{1,0:T(8,128)(2,1)S(1)} %fusion.2), channel_id=1, source_target_pairs={{0,2},{1,3},{2,0},{3,1},{4,6},{5,7},{6,4},{7,5},{8,10},{9,11},{10,... | collective-permute-start | bytes 172040 | tf_op jit(solution)/shard_map/ppermute | solution.py:394
  49.2 2.4 %collective-permute-done.11 = bf16[8,3584]{1,0:T(8,128)(2,1)S(1)} collective-permute-done((bf16[8,3584]{1,0:T(8,128)(2,1)S(1)}, bf16[8,3584]{1,0:T(8,128)(2,1)S(1)}, u32[]{:S(2)}, u32[]{:S(2)}) %collective-permute-start.11) | collective-permute-done | bytes 57376 | tf_op jit(solution)/shard_map/ppermute | solution.py:394
  51.6 1.8 %collective-permute-done.15 = bf16[8,3584]{1,0:T(8,128)(2,1)S(1)} collective-permute-done((bf16[8,3584]{1,0:T(8,128)(2,1)S(1)}, bf16[8,3584]{1,0:T(8,128)(2,1)S(1)}, u32[]{:S(2)}, u32[]{:S(2)}) %collective-permute-start.15) | collective-permute-done | bytes 57376 | tf_op jit(solution)/shard_map/ppermute | solution.py:394
  53.4 0.7 %pad_maximum_fusion.5 = bf16[8,7168]{1,0:T(8,128)(2,1)} fusion(bf16[8,3584]{1,0:T(8,128)(2,1)S(1)} %fusion.4, bf16[8,3584]{1,0:T(8,128)(2,1)S(1)} %fusion.7), kind=kLoop, calls=%fused_computation.27 | loop fusion | flops 229376 | bytes 229376 | tf_op jit(solution)/shard_map/concatenate | solution.py:463
  (21 shorter events, 0.3 us)
Async XLA Ops:
  1.1 6.9 %collective-permute-start.2 = (bf16[8,3712]{1,0:T(8,128)(2,1)S(1)}, bf16[8,3712]{1,0:T(8,128)(2,1)S(1)}, u32[]{:S(2)}, u32[]{:S(2)}) collective-permute-start(bf16[8,3712]{1,0:T(8,128)(2,1)S(1)} %get-tuple-element.64), channel_id=1, source_target_pairs={{0,2},{1,3},{2,0},{3,1},{4,6},{5,7},{6,4},{7,5},{8,10},{9,11},{10,... | collective-permute-start | bytes 178184 | tf_op jit(solution)/shard_map/ppermute | solution.py:394
  5.2 5.4 %collective-permute-start = (bf16[8,3584]{1,0:T(8,128)(2,1)S(1)}, bf16[8,3584]{1,0:T(8,128)(2,1)S(1)}, u32[]{:S(2)}, u32[]{:S(2)}) collective-permute-start(bf16[8,3584]{1,0:T(8,128)(2,1)S(1)} %slice.112), channel_id=1, source_target_pairs={{0,2},{1,3},{2,0},{3,1},{4,6},{5,7},{6,4},{7,5},{8,10},{9,11},{10,... | collective-permute-start | bytes 172040 | tf_op jit(solution)/shard_map/ppermute | solution.py:394
  8.0 7.4 %collective-permute-start.3 = (bf16[16,3712]{1,0:T(8,128)(2,1)S(1)}, bf16[16,3712]{1,0:T(8,128)(2,1)S(1)}, u32[]{:S(2)}, u32[]{:S(2)}) collective-permute-start(bf16[16,3712]{1,0:T(8,128)(2,1)S(1)} %pad_maximum_fusion.3), channel_id=1, source_target_pairs={{0,8},{4,12},{8,0},{12,4},{1,9},{5,13},{9,1},{13,5},{2,10},{6,14},... | collective-permute-start | bytes 356360 | tf_op jit(solution)/shard_map/ppermute | solution.py:394
  10.6 4.9 %collective-permute-start.1 = (bf16[16,3584]{1,0:T(8,128)(2,1)S(1)}, bf16[16,3584]{1,0:T(8,128)(2,1)S(1)}, u32[]{:S(2)}, u32[]{:S(2)}) collective-permute-start(bf16[16,3584]{1,0:T(8,128)(2,1)S(1)} %pad_maximum_fusion.4), channel_id=1, source_target_pairs={{0,1},{1,0},{2,3},{3,2},{4,5},{5,4},{6,7},{7,6},{8,9},{9,8},{10,11... | collective-permute-start | bytes 344072 | tf_op jit(solution)/shard_map/ppermute | solution.py:394
  15.4 9.6 %slice-start = ((s8[7340032]{0:T(1024)(128)(4,1)}), s8[4194304]{0:T(1024)(128)(4,1)S(1)}, s32[]{:S(2)}) async-start(s8[7340032]{0:T(1024)(128)(4,1)} %bitcast.6), calls=%async_computation | async-start | bytes 8388608
  15.5 7.7 %collective-permute-start.5 = (bf16[32,3712]{1,0:T(8,128)(2,1)S(1)}, bf16[32,3712]{1,0:T(8,128)(2,1)S(1)}, u32[]{:S(2)}, u32[]{:S(2)}) collective-permute-start(bf16[32,3712]{1,0:T(8,128)(2,1)S(1)} %pad_maximum_fusion.1), channel_id=1, source_target_pairs={{0,1},{1,0},{2,3},{3,2},{4,5},{5,4},{6,7},{7,6},{8,9},{9,8},{10,11... | collective-permute-start | bytes 712712 | tf_op jit(solution)/shard_map/ppermute | solution.py:394
  17.0 6.1 %collective-permute-start.4 = (bf16[32,3584]{1,0:T(8,128)(2,1)S(1)}, bf16[32,3584]{1,0:T(8,128)(2,1)S(1)}, u32[]{:S(2)}, u32[]{:S(2)}) collective-permute-start(bf16[32,3584]{1,0:T(8,128)(2,1)S(1)} %pad_maximum_fusion.2), channel_id=1, source_target_pairs={{0,8},{4,12},{8,0},{12,4},{1,9},{5,13},{9,1},{13,5},{2,10},{6,14},... | collective-permute-start | bytes 688136 | tf_op jit(solution)/shard_map/ppermute | solution.py:394
  18.4 6.6 %slice-start.1 = ((s8[7340032]{0:T(1024)(128)(4,1)}), s8[3145728]{0:T(1024)(128)(4,1)S(1)}, s32[]{:S(2)}) async-start(s8[7340032]{0:T(1024)(128)(4,1)} %bitcast.6), calls=%async_computation.1 | async-start | bytes 6291456
  23.2 1.9 %collective-permute-start.7 = (bf16[64,3712]{1,0:T(8,128)(2,1)S(1)}, bf16[64,3712]{1,0:T(8,128)(2,1)S(1)}, u32[]{:S(2)}, u32[]{:S(2)}) collective-permute-start(bf16[64,3712]{1,0:T(8,128)(2,1)S(1)} %slice_dynamic-update-slice_fusion.own_ref), channel_id=1, source_target_pairs={{0,4},{4,0},{8,12},{12,8},{1,5},{5,1},{9,13},{13,9},{2,6},{6,2},{1... | collective-permute-start | bytes 1425416 | tf_op jit(solution)/shard_map/ppermute | solution.py:394
  23.3 3.5 %collective-permute-start.6 = (bf16[64,3584]{1,0:T(8,128)(2,1)S(1)}, bf16[64,3584]{1,0:T(8,128)(2,1)S(1)}, u32[]{:S(2)}, u32[]{:S(2)}) collective-permute-start(bf16[64,3584]{1,0:T(8,128)(2,1)S(1)} %pad_maximum_fusion.own_ref), channel_id=1, source_target_pairs={{0,4},{4,0},{8,12},{12,8},{1,5},{5,1},{9,13},{13,9},{2,6},{6,2},{1... | collective-permute-start | bytes 1376264 | tf_op jit(solution)/shard_map/ppermute | solution.py:394
  25.1 4.3 %slice-start.2 = ((s8[7340032]{0:T(1024)(128)(4,1)}), s8[4194304]{0:T(1024)(128)(4,1)S(1)}, s32[]{:S(2)}) async-start(s8[7340032]{0:T(1024)(128)(4,1)} %bitcast.11), calls=%async_computation.2 | async-start | bytes 8388608
  26.8 2.6 %slice-start.3 = ((s8[7340032]{0:T(1024)(128)(4,1)}), s8[3145728]{0:T(1024)(128)(4,1)S(1)}, s32[]{:S(2)}) async-start(s8[7340032]{0:T(1024)(128)(4,1)} %bitcast.11), calls=%async_computation.3 | async-start | bytes 6291456
  29.2 1.9 %collective-permute-start.8 = (bf16[64,3584]{1,0:T(8,128)(2,1)S(1)}, bf16[64,3584]{1,0:T(8,128)(2,1)S(1)}, u32[]{:S(2)}, u32[]{:S(2)}) collective-permute-start(bf16[64,3584]{1,0:T(8,128)(2,1)S(1)} %get-tuple-element.49), channel_id=1, source_target_pairs={{0,4},{4,0},{8,12},{12,8},{1,5},{5,1},{9,13},{13,9},{2,6},{6,2},{1... | collective-permute-start | bytes 1376264 | tf_op jit(solution)/shard_map/ppermute | solution.py:394
  31.1 1.8 %collective-permute-start.12 = (bf16[64,3584]{1,0:T(8,128)(2,1)S(1)}, bf16[64,3584]{1,0:T(8,128)(2,1)S(1)}, u32[]{:S(2)}, u32[]{:S(2)}) collective-permute-start(bf16[64,3584]{1,0:T(8,128)(2,1)S(1)} %get-tuple-element.54), channel_id=1, source_target_pairs={{0,4},{4,0},{8,12},{12,8},{1,5},{5,1},{9,13},{13,9},{2,6},{6,2},{1... | collective-permute-start | bytes 1376264 | tf_op jit(solution)/shard_map/ppermute | solution.py:394
  31.3 7.9 %collective-permute-start.9 = (bf16[32,3584]{1,0:T(8,128)(2,1)S(1)}, bf16[32,3584]{1,0:T(8,128)(2,1)S(1)}, u32[]{:S(2)}, u32[]{:S(2)}) collective-permute-start(bf16[32,3584]{1,0:T(8,128)(2,1)S(1)} %get-tuple-element.55), channel_id=1, source_target_pairs={{0,8},{4,12},{8,0},{12,4},{1,9},{5,13},{9,1},{13,5},{2,10},{6,14},... | collective-permute-start | bytes 688136 | tf_op jit(solution)/shard_map/ppermute | solution.py:394
  33.0 7.7 %collective-permute-start.13 = (bf16[32,3584]{1,0:T(8,128)(2,1)S(1)}, bf16[32,3584]{1,0:T(8,128)(2,1)S(1)}, u32[]{:S(2)}, u32[]{:S(2)}) collective-permute-start(bf16[32,3584]{1,0:T(8,128)(2,1)S(1)} %get-tuple-element.57), channel_id=1, source_target_pairs={{0,1},{1,0},{2,3},{3,2},{4,5},{5,4},{6,7},{7,6},{8,9},{9,8},{10,11... | collective-permute-start | bytes 688136 | tf_op jit(solution)/shard_map/ppermute | solution.py:394
  39.3 4.9 %collective-permute-start.10 = (bf16[16,3584]{1,0:T(8,128)(2,1)S(1)}, bf16[16,3584]{1,0:T(8,128)(2,1)S(1)}, u32[]{:S(2)}, u32[]{:S(2)}) collective-permute-start(bf16[16,3584]{1,0:T(8,128)(2,1)S(1)} %get-tuple-element.59), channel_id=1, source_target_pairs={{0,1},{1,0},{2,3},{3,2},{4,5},{5,4},{6,7},{7,6},{8,9},{9,8},{10,11... | collective-permute-start | bytes 344072 | tf_op jit(solution)/shard_map/ppermute | solution.py:394
  40.7 7.0 %collective-permute-start.14 = (bf16[16,3584]{1,0:T(8,128)(2,1)S(1)}, bf16[16,3584]{1,0:T(8,128)(2,1)S(1)}, u32[]{:S(2)}, u32[]{:S(2)}) collective-permute-start(bf16[16,3584]{1,0:T(8,128)(2,1)S(1)} %get-tuple-element.61), channel_id=1, source_target_pairs={{0,8},{4,12},{8,0},{12,4},{1,9},{5,13},{9,1},{13,5},{2,10},{6,14},... | collective-permute-start | bytes 344072 | tf_op jit(solution)/shard_map/ppermute | solution.py:394
  44.2 7.4 %collective-permute-start.11 = (bf16[8,3584]{1,0:T(8,128)(2,1)S(1)}, bf16[8,3584]{1,0:T(8,128)(2,1)S(1)}, u32[]{:S(2)}, u32[]{:S(2)}) collective-permute-start(bf16[8,3584]{1,0:T(8,128)(2,1)S(1)} %fusion.5), channel_id=1, source_target_pairs={{0,2},{1,3},{2,0},{3,1},{4,6},{5,7},{6,4},{7,5},{8,10},{9,11},{10,... | collective-permute-start | bytes 172040 | tf_op jit(solution)/shard_map/ppermute | solution.py:394
  47.7 5.7 %collective-permute-start.15 = (bf16[8,3584]{1,0:T(8,128)(2,1)S(1)}, bf16[8,3584]{1,0:T(8,128)(2,1)S(1)}, u32[]{:S(2)}, u32[]{:S(2)}) collective-permute-start(bf16[8,3584]{1,0:T(8,128)(2,1)S(1)} %fusion.2), channel_id=1, source_target_pairs={{0,2},{1,3},{2,0},{3,1},{4,6},{5,7},{6,4},{7,5},{8,10},{9,11},{10,... | collective-permute-start | bytes 172040 | tf_op jit(solution)/shard_map/ppermute | solution.py:394

commit v26 on v25

--- a/solution.py
+++ b/solution.py
@@ -286,8 +286,8 @@
     for i in range(2):
         at = slice(i * piece, (i + 1) * piece)
         total = jnp.dot(act_ref[...], second_ref[:, at], preferred_element_type=F32).astype(BF16)
-        own_out_ref[:, at] = total[:half]
-        other_out_ref[:, at] = total[half:]
+        own_out_ref[:, at] = swap_quarters(total[:half])
+        other_out_ref[:, at] = swap_quarters(total[half:])
 
 
 def last_half_kernel(act_ref, down_ref, rows_ref, own_out_ref, other_out_ref):
@@ -300,8 +300,8 @@
         total = jnp.dot(act_ref[:, :hidden], down_ref[:, whole], preferred_element_type=F32)
         total += jnp.dot(act_ref[:, hidden:], rows_ref[:, at], preferred_element_type=F32)
         total = total.astype(BF16)
-        own_out_ref[:, at] = swap_quarters(total[:half])
-        other_out_ref[:, at] = swap_quarters(total[half:])
+        own_out_ref[:, at] = total[:half]
+        other_out_ref[:, at] = total[half:]
 
 
 def estimate(rows, depth, columns):
@@ -395,8 +395,8 @@
 
 
 X, Z1, Z2, CORE = (2, 0), (0, 1), (0, 2), (1, 0)
-GATHER = ((Z2, Z2), (Z1, X), (X, Z1))
-SCATTER = GATHER[::-1]
+GATHER = ((Z2, Z2), (X, Z1), (Z1, X))
+SCATTER = ((X, Z1), (Z1, X), (Z2, Z2))
 
 
 def stack(*values):

time: 54.2 us -> 53.6 us (0.989)
  transfers between devices with their start and end apart: 16 -> 16, of which waited for: 12 -> 11; matrix products, arithmetic and copies ran while one was open for 1% -> 1% of each run, Pallas kernels for 20% -> 20%
where the time goes in v26:
time: 53.6 us; the launch traced here: 53.5 us
  starting transfers between devices  21.1 us (39%)
  waiting for transfers between devices  16.9 us (32%)
  Pallas kernels  14.1 us (26%)
  other arithmetic  1.09 us (2%)
    ppermute x16, starting transfers between devices, flipped(): lax.ppermute(value, ('node', 'local')[axis], [(i, i ^ bits[axis]) for i i...  21.1 us
    ppermute x16, waiting for transfers between devices, flipped(): lax.ppermute(value, ('node', 'local')[axis], [(i, i ^ bits[axis]) for i i...  16.9 us
    pallas_call x2, Pallas kernels, load_weights(): pl.pallas_call(functools.partial(load_kernel, share, first_row), in_specs...  4.68 us
    pallas_call x1, Pallas kernels, load_late(): pl.pallas_call(functools.partial(load_late_kernel, share), in_specs=[SMEM...  3.39 us
    pallas_call x1, Pallas kernels, pair_rows(): pl.pallas_call(functools.partial(early_half_kernel, share), in_specs=[SME...  2.38 us
    pallas_call x1, Pallas kernels, pair_rows(): pl.pallas_call(late_half_kernel, in_specs=[SMEM_SPEC] + [VMEM_SPEC] * 5,...  1.67 us
  transfers between devices with their start and end apart: 16, of which 11 were waited for; matrix products, arithmetic and copies ran while one was open for 1% of the time, Pallas kernels for 20%

profile of v26, /device:TPU:0, one launch (start us, length us, event | category | flops | bytes accessed | tf_op | source)
XLA Modules:
  0.0 53.5 jit_solution(2381926287204441428)
XLA Ops:
  0.0 1.1 %pack_rows.1 = bf16[8,7296]{1,0:T(8,128)(2,1)S(1)} custom-call(bf16[8,7168]{1,0:T(8,128)(2,1)} %tokens_ref.1, s32[4,8]{1,0:T(4,128)} %bitcast.16, bf16[4,8]{1,0:T(4,128)(2,1)} %bitcast.17), custom_call_target="tpu_custom_call" | custom-call | tf_op jit(solution)/shard_map/pack_rows/pallas_call | solution.py:48
  1.1 4.1 %collective-permute-start.2 = (bf16[8,3712]{1,0:T(8,128)(2,1)S(1)}, bf16[8,3712]{1,0:T(8,128)(2,1)S(1)}, u32[]{:S(2)}, u32[]{:S(2)}) collective-permute-start(bf16[8,3712]{1,0:T(8,128)(2,1)S(1)} %get-tuple-element.64), channel_id=1, source_target_pairs={{0,2},{1,3},{2,0},{3,1},{4,6},{5,7},{6,4},{7,5},{8,10},{9,11},{10,... | collective-permute-start | bytes 178184 | tf_op jit(solution)/shard_map/ppermute | solution.py:394
  5.2 0.1 collective-permute-start
  5.3 2.3 %load_weights.2.gate_ref = bf16[3584,640]{1,0:T(8,128)(2,1)S(1)} custom-call(s32[1]{0:T(128)} %bitcast.place_ref, bf16[7168,512]{1,0:T(8,128)(2,1)} %bitcast.14, bf16[7168,512]{1,0:T(8,128)(2,1)} %shared_ref.4), custom_call_target="tpu_custom_call" | custom-call | bytes 9175040 | tf_op jit(solution)/shard_map/load_weights/pallas_call | solution.py:85
  7.6 0.4 collective-permute-done.2
  8.0 2.5 %collective-permute-start.3 = (bf16[16,3712]{1,0:T(8,128)(2,1)S(1)}, bf16[16,3712]{1,0:T(8,128)(2,1)S(1)}, u32[]{:S(2)}, u32[]{:S(2)}) collective-permute-start(bf16[16,3712]{1,0:T(8,128)(2,1)S(1)} %pad_maximum_fusion.3), channel_id=1, source_target_pairs={{0,1},{1,0},{2,3},{3,2},{4,5},{5,4},{6,7},{7,6},{8,9},{9,8},{10,11... | collective-permute-start | bytes 356360 | tf_op jit(solution)/shard_map/ppermute | solution.py:394
  10.5 0.0 collective-permute-done
  10.6 1.7 %collective-permute-start.1 = (bf16[16,3584]{1,0:T(8,128)(2,1)S(1)}, bf16[16,3584]{1,0:T(8,128)(2,1)S(1)}, u32[]{:S(2)}, u32[]{:S(2)}) collective-permute-start(bf16[16,3584]{1,0:T(8,128)(2,1)S(1)} %pad_maximum_fusion.4), channel_id=1, source_target_pairs={{0,8},{4,12},{8,0},{12,4},{1,9},{5,13},{9,1},{13,5},{2,10},{6,14},... | collective-permute-start | bytes 344072 | tf_op jit(solution)/shard_map/ppermute | solution.py:394
  12.3 2.3 %load_weights.3.gate_ref = bf16[3584,640]{1,0:T(8,128)(2,1)S(1)} custom-call(s32[1]{0:T(128)} %bitcast.place_ref, bf16[7168,512]{1,0:T(8,128)(2,1)} %bitcast.15, bf16[7168,512]{1,0:T(8,128)(2,1)} %shared_ref.4), custom_call_target="tpu_custom_call" | custom-call | bytes 9175040 | tf_op jit(solution)/shard_map/load_weights/pallas_call | solution.py:85
  14.6 0.8 %collective-permute-done.1 = bf16[16,3584]{1,0:T(8,128)(2,1)S(1)} collective-permute-done((bf16[16,3584]{1,0:T(8,128)(2,1)S(1)}, bf16[16,3584]{1,0:T(8,128)(2,1)S(1)}, u32[]{:S(2)}, u32[]{:S(2)}) %collective-permute-start.1) | collective-permute-done | bytes 114720 | tf_op jit(solution)/shard_map/ppermute | solution.py:394
  15.4 0.0 collective-permute-done.3
  15.4 0.0 slice-start
  15.5 1.7 %collective-permute-start.5 = (bf16[32,3712]{1,0:T(8,128)(2,1)S(1)}, bf16[32,3712]{1,0:T(8,128)(2,1)S(1)}, u32[]{:S(2)}, u32[]{:S(2)}) collective-permute-start(bf16[32,3712]{1,0:T(8,128)(2,1)S(1)} %pad_maximum_fusion.1), channel_id=1, source_target_pairs={{0,8},{4,12},{8,0},{12,4},{1,9},{5,13},{9,1},{13,5},{2,10},{6,14},... | collective-permute-start | bytes 712712 | tf_op jit(solution)/shard_map/ppermute | solution.py:394
  17.2 1.2 %collective-permute-start.4 = (bf16[32,3584]{1,0:T(8,128)(2,1)S(1)}, bf16[32,3584]{1,0:T(8,128)(2,1)S(1)}, u32[]{:S(2)}, u32[]{:S(2)}) collective-permute-start(bf16[32,3584]{1,0:T(8,128)(2,1)S(1)} %pad_maximum_fusion.2), channel_id=1, source_target_pairs={{0,1},{1,0},{2,3},{3,2},{4,5},{5,4},{6,7},{7,6},{8,9},{9,8},{10,11... | collective-permute-start | bytes 688136 | tf_op jit(solution)/shard_map/ppermute | solution.py:394
  18.4 3.4 %load_late.1 = (bf16[7168,128]{1,0:T(8,128)(2,1)S(1)}, bf16[640,3584]{1,0:T(8,128)(2,1)S(1)}, bf16[128,3584]{1,0:T(8,128)(2,1)S(1)}) custom-call(s32[1]{0:T(128)} %bitcast.place_ref, bf16[7168,512]{1,0:T(8,128)(2,1)} %shared_ref.5, bf16[512,7168]{1,0:T(8,128)(2,1)} %bitcast.10, bf16[512,7168]{1,0:T(8,128)(2,1)} %sdown_ref.1), custom_call_target="tpu_custom_call" | custom-call | bytes 12845056 | tf_op jit(solution)/shard_map/load_late/pallas_call | solution.py:230
  21.8 1.4 %collective-permute-done.4 = bf16[32,3584]{1,0:T(8,128)(2,1)S(1)} collective-permute-done((bf16[32,3584]{1,0:T(8,128)(2,1)S(1)}, bf16[32,3584]{1,0:T(8,128)(2,1)S(1)}, u32[]{:S(2)}, u32[]{:S(2)}) %collective-permute-start.4) | collective-permute-done | bytes 229408 | tf_op jit(solution)/shard_map/ppermute | solution.py:394
  23.3 0.0 collective-permute-done.5
  23.3 0.1 collective-permute-start.7
  23.4 0.6 %collective-permute-start.6 = (bf16[64,3584]{1,0:T(8,128)(2,1)S(1)}, bf16[64,3584]{1,0:T(8,128)(2,1)S(1)}, u32[]{:S(2)}, u32[]{:S(2)}) collective-permute-start(bf16[64,3584]{1,0:T(8,128)(2,1)S(1)} %pad_maximum_fusion.own_ref), channel_id=1, source_target_pairs={{0,4},{4,0},{8,12},{12,8},{1,5},{5,1},{9,13},{13,9},{2,6},{6,2},{1... | collective-permute-start | bytes 1376264 | tf_op jit(solution)/shard_map/ppermute | solution.py:394
  24.0 1.2 %collective-permute-done.7.other_ref = bf16[64,3712]{1,0:T(8,128)(2,1)S(1)} collective-permute-done((bf16[64,3712]{1,0:T(8,128)(2,1)S(1)}, bf16[64,3712]{1,0:T(8,128)(2,1)S(1)}, u32[]{:S(2)}, u32[]{:S(2)}) %collective-permute-start.7) | collective-permute-done | bytes 475168 | tf_op jit(solution)/shard_map/ppermute | solution.py:394
  25.2 0.0 slice-done
  25.2 0.0 slice-done.1
  25.2 1.7 %late_half.1 = (f32[128,640]{1,0:T(8,128)S(1)}, f32[128,640]{1,0:T(8,128)S(1)}, f32[128,128]{1,0:T(8,128)S(1)}) custom-call(s32[1]{0:T(128)} %bitcast.place_ref, bf16[64,3712]{1,0:T(8,128)(2,1)S(1)} %slice_dynamic-update-slice_fusion.own_ref, bf16[64,3712]{1,0:T(8,128)(2,1)S(1)} %collective-permute-done.7.other_ref, ...), custom_call_target="tpu_custom_call" | custom-call | flops 1174405120 | bytes 9175040 | tf_op jit(solution)/shard_map/late_half/pallas_call | solution.py:318
  26.9 0.0 collective-permute-done.6.other_ref
  26.9 0.0 slice-start.3
  26.9 2.4 %early_half.1 = (bf16[64,3584]{1,0:T(8,128)(2,1)S(1)}, bf16[64,3584]{1,0:T(8,128)(2,1)S(1)}, bf16[128,640]{1,0:T(8,128)(2,1)S(1)}) custom-call(s32[1]{0:T(128)} %bitcast.place_ref, bf16[64,3584]{1,0:T(8,128)(2,1)S(1)} %pad_maximum_fusion.own_ref, bf16[64,3584]{1,0:T(8,128)(2,1)S(1)} %collective-permute-done.6.other_ref, ...), custom_call_target="tpu_custom_call" | custom-call | flops 1761607680 | bytes 13762560 | tf_op jit(solution)/shard_map/early_half/pallas_call | solution.py:328
  29.3 0.2 collective-permute-start.8
  29.5 0.0 slice-done.2
  29.5 0.0 slice-done.3
  29.5 0.9 %last_half.1 = (bf16[64,3584]{1,0:T(8,128)(2,1)S(1)}, bf16[64,3584]{1,0:T(8,128)(2,1)S(1)}) custom-call(bf16[128,640]{1,0:T(8,128)(2,1)S(1)} %get-tuple-element.50.act_ref, bf16[512,7168]{1,0:T(8,128)(2,1)S(1)} %bitcast.13, bf16[128,3584]{1,0:T(8,128)(2,1)S(1)} %get-tuple-element.51.rows_ref), custom_call_target="tpu_custom_call" | custom-call | flops 587202560 | bytes 4587520 | tf_op jit(solution)/shard_map/last_half/pallas_call | solution.py:342
  30.4 0.8 %collective-permute-done.8 = bf16[64,3584]{1,0:T(8,128)(2,1)S(1)} collective-permute-done((bf16[64,3584]{1,0:T(8,128)(2,1)S(1)}, bf16[64,3584]{1,0:T(8,128)(2,1)S(1)}, u32[]{:S(2)}, u32[]{:S(2)}) %collective-permute-start.8) | collective-permute-done | bytes 458784 | tf_op jit(solution)/shard_map/ppermute | solution.py:394
  31.2 0.1 collective-permute-start.12
  31.3 0.1 add_convert_fusion.1
  31.5 0.5 collective-permute-start.9
  31.9 1.1 %collective-permute-done.12 = bf16[64,3584]{1,0:T(8,128)(2,1)S(1)} collective-permute-done((bf16[64,3584]{1,0:T(8,128)(2,1)S(1)}, bf16[64,3584]{1,0:T(8,128)(2,1)S(1)}, u32[]{:S(2)}, u32[]{:S(2)}) %collective-permute-start.12) | collective-permute-done | bytes 458784 | tf_op jit(solution)/shard_map/ppermute | solution.py:394
  33.0 0.1 add_convert_fusion
  33.1 1.3 %collective-permute-start.13 = (bf16[32,3584]{1,0:T(8,128)(2,1)S(1)}, bf16[32,3584]{1,0:T(8,128)(2,1)S(1)}, u32[]{:S(2)}, u32[]{:S(2)}) collective-permute-start(bf16[32,3584]{1,0:T(8,128)(2,1)S(1)} %get-tuple-element.57), channel_id=1, source_target_pairs={{0,1},{1,0},{2,3},{3,2},{4,5},{5,4},{6,7},{7,6},{8,9},{9,8},{10,11... | collective-permute-start | bytes 688136 | tf_op jit(solution)/shard_map/ppermute | solution.py:394
  34.5 4.9 %collective-permute-done.9 = bf16[32,3584]{1,0:T(8,128)(2,1)S(1)} collective-permute-done((bf16[32,3584]{1,0:T(8,128)(2,1)S(1)}, bf16[32,3584]{1,0:T(8,128)(2,1)S(1)}, u32[]{:S(2)}, u32[]{:S(2)}) %collective-permute-start.9) | collective-permute-done | bytes 229408 | tf_op jit(solution)/shard_map/ppermute | solution.py:394
  39.4 1.3 %collective-permute-start.10 = (bf16[16,3584]{1,0:T(8,128)(2,1)S(1)}, bf16[16,3584]{1,0:T(8,128)(2,1)S(1)}, u32[]{:S(2)}, u32[]{:S(2)}) collective-permute-start(bf16[16,3584]{1,0:T(8,128)(2,1)S(1)} %get-tuple-element.59), channel_id=1, source_target_pairs={{0,1},{1,0},{2,3},{3,2},{4,5},{5,4},{6,7},{7,6},{8,9},{9,8},{10,11... | collective-permute-start | bytes 344072 | tf_op jit(solution)/shard_map/ppermute | solution.py:394
  40.8 0.1 collective-permute-done.13
  40.9 0.5 %collective-permute-start.14 = (bf16[16,3584]{1,0:T(8,128)(2,1)S(1)}, bf16[16,3584]{1,0:T(8,128)(2,1)S(1)}, u32[]{:S(2)}, u32[]{:S(2)}) collective-permute-start(bf16[16,3584]{1,0:T(8,128)(2,1)S(1)} %get-tuple-element.61), channel_id=1, source_target_pairs={{0,8},{4,12},{8,0},{12,4},{1,9},{5,13},{9,1},{13,5},{2,10},{6,14},... | collective-permute-start | bytes 344072 | tf_op jit(solution)/shard_map/ppermute | solution.py:394
  41.4 2.9 %collective-permute-done.10 = bf16[16,3584]{1,0:T(8,128)(2,1)S(1)} collective-permute-done((bf16[16,3584]{1,0:T(8,128)(2,1)S(1)}, bf16[16,3584]{1,0:T(8,128)(2,1)S(1)}, u32[]{:S(2)}, u32[]{:S(2)}) %collective-permute-start.10) | collective-permute-done | bytes 114720 | tf_op jit(solution)/shard_map/ppermute | solution.py:394
  44.3 3.3 %collective-permute-start.11 = (bf16[8,3584]{1,0:T(8,128)(2,1)S(1)}, bf16[8,3584]{1,0:T(8,128)(2,1)S(1)}, u32[]{:S(2)}, u32[]{:S(2)}) collective-permute-start(bf16[8,3584]{1,0:T(8,128)(2,1)S(1)} %fusion.5), channel_id=1, source_target_pairs={{0,2},{1,3},{2,0},{3,1},{4,6},{5,7},{6,4},{7,5},{8,10},{9,11},{10,... | collective-permute-start | bytes 172040 | tf_op jit(solution)/shard_map/ppermute | solution.py:394
  47.6 0.0 collective-permute-done.14
  47.6 1.8 %collective-permute-start.15 = (bf16[8,3584]{1,0:T(8,128)(2,1)S(1)}, bf16[8,3584]{1,0:T(8,128)(2,1)S(1)}, u32[]{:S(2)}, u32[]{:S(2)}) collective-permute-start(bf16[8,3584]{1,0:T(8,128)(2,1)S(1)} %fusion.2), channel_id=1, source_target_pairs={{0,2},{1,3},{2,0},{3,1},{4,6},{5,7},{6,4},{7,5},{8,10},{9,11},{10,... | collective-permute-start | bytes 172040 | tf_op jit(solution)/shard_map/ppermute | solution.py:394
  49.4 0.8 %collective-permute-done.11 = bf16[8,3584]{1,0:T(8,128)(2,1)S(1)} collective-permute-done((bf16[8,3584]{1,0:T(8,128)(2,1)S(1)}, bf16[8,3584]{1,0:T(8,128)(2,1)S(1)}, u32[]{:S(2)}, u32[]{:S(2)}) %collective-permute-start.11) | collective-permute-done | bytes 57376 | tf_op jit(solution)/shard_map/ppermute | solution.py:394
  50.3 2.5 %collective-permute-done.15 = bf16[8,3584]{1,0:T(8,128)(2,1)S(1)} collective-permute-done((bf16[8,3584]{1,0:T(8,128)(2,1)S(1)}, bf16[8,3584]{1,0:T(8,128)(2,1)S(1)}, u32[]{:S(2)}, u32[]{:S(2)}) %collective-permute-start.15) | collective-permute-done | bytes 57376 | tf_op jit(solution)/shard_map/ppermute | solution.py:394
  52.8 0.7 %pad_maximum_fusion.5 = bf16[8,7168]{1,0:T(8,128)(2,1)} fusion(bf16[8,3584]{1,0:T(8,128)(2,1)S(1)} %fusion.4, bf16[8,3584]{1,0:T(8,128)(2,1)S(1)} %fusion.7), kind=kLoop, calls=%fused_computation.27 | loop fusion | flops 229376 | bytes 229376 | tf_op jit(solution)/shard_map/concatenate | solution.py:463
  (21 shorter events, 0.3 us)
Async XLA Ops:
  1.1 6.9 %collective-permute-start.2 = (bf16[8,3712]{1,0:T(8,128)(2,1)S(1)}, bf16[8,3712]{1,0:T(8,128)(2,1)S(1)}, u32[]{:S(2)}, u32[]{:S(2)}) collective-permute-start(bf16[8,3712]{1,0:T(8,128)(2,1)S(1)} %get-tuple-element.64), channel_id=1, source_target_pairs={{0,2},{1,3},{2,0},{3,1},{4,6},{5,7},{6,4},{7,5},{8,10},{9,11},{10,... | collective-permute-start | bytes 178184 | tf_op jit(solution)/shard_map/ppermute | solution.py:394
  5.2 5.4 %collective-permute-start = (bf16[8,3584]{1,0:T(8,128)(2,1)S(1)}, bf16[8,3584]{1,0:T(8,128)(2,1)S(1)}, u32[]{:S(2)}, u32[]{:S(2)}) collective-permute-start(bf16[8,3584]{1,0:T(8,128)(2,1)S(1)} %slice.112), channel_id=1, source_target_pairs={{0,2},{1,3},{2,0},{3,1},{4,6},{5,7},{6,4},{7,5},{8,10},{9,11},{10,... | collective-permute-start | bytes 172040 | tf_op jit(solution)/shard_map/ppermute | solution.py:394
  8.0 7.4 %collective-permute-start.3 = (bf16[16,3712]{1,0:T(8,128)(2,1)S(1)}, bf16[16,3712]{1,0:T(8,128)(2,1)S(1)}, u32[]{:S(2)}, u32[]{:S(2)}) collective-permute-start(bf16[16,3712]{1,0:T(8,128)(2,1)S(1)} %pad_maximum_fusion.3), channel_id=1, source_target_pairs={{0,1},{1,0},{2,3},{3,2},{4,5},{5,4},{6,7},{7,6},{8,9},{9,8},{10,11... | collective-permute-start | bytes 356360 | tf_op jit(solution)/shard_map/ppermute | solution.py:394
  10.6 4.9 %collective-permute-start.1 = (bf16[16,3584]{1,0:T(8,128)(2,1)S(1)}, bf16[16,3584]{1,0:T(8,128)(2,1)S(1)}, u32[]{:S(2)}, u32[]{:S(2)}) collective-permute-start(bf16[16,3584]{1,0:T(8,128)(2,1)S(1)} %pad_maximum_fusion.4), channel_id=1, source_target_pairs={{0,8},{4,12},{8,0},{12,4},{1,9},{5,13},{9,1},{13,5},{2,10},{6,14},... | collective-permute-start | bytes 344072 | tf_op jit(solution)/shard_map/ppermute | solution.py:394
  15.4 9.8 %slice-start = ((s8[7340032]{0:T(1024)(128)(4,1)}), s8[4194304]{0:T(1024)(128)(4,1)S(1)}, s32[]{:S(2)}) async-start(s8[7340032]{0:T(1024)(128)(4,1)} %bitcast.6), calls=%async_computation | async-start | bytes 8388608
  15.5 7.8 %collective-permute-start.5 = (bf16[32,3712]{1,0:T(8,128)(2,1)S(1)}, bf16[32,3712]{1,0:T(8,128)(2,1)S(1)}, u32[]{:S(2)}, u32[]{:S(2)}) collective-permute-start(bf16[32,3712]{1,0:T(8,128)(2,1)S(1)} %pad_maximum_fusion.1), channel_id=1, source_target_pairs={{0,8},{4,12},{8,0},{12,4},{1,9},{5,13},{9,1},{13,5},{2,10},{6,14},... | collective-permute-start | bytes 712712 | tf_op jit(solution)/shard_map/ppermute | solution.py:394
  17.2 6.1 %collective-permute-start.4 = (bf16[32,3584]{1,0:T(8,128)(2,1)S(1)}, bf16[32,3584]{1,0:T(8,128)(2,1)S(1)}, u32[]{:S(2)}, u32[]{:S(2)}) collective-permute-start(bf16[32,3584]{1,0:T(8,128)(2,1)S(1)} %pad_maximum_fusion.2), channel_id=1, source_target_pairs={{0,1},{1,0},{2,3},{3,2},{4,5},{5,4},{6,7},{7,6},{8,9},{9,8},{10,11... | collective-permute-start | bytes 688136 | tf_op jit(solution)/shard_map/ppermute | solution.py:394
  18.4 6.8 %slice-start.1 = ((s8[7340032]{0:T(1024)(128)(4,1)}), s8[3145728]{0:T(1024)(128)(4,1)S(1)}, s32[]{:S(2)}) async-start(s8[7340032]{0:T(1024)(128)(4,1)} %bitcast.6), calls=%async_computation.1 | async-start | bytes 6291456
  23.3 1.9 %collective-permute-start.7 = (bf16[64,3712]{1,0:T(8,128)(2,1)S(1)}, bf16[64,3712]{1,0:T(8,128)(2,1)S(1)}, u32[]{:S(2)}, u32[]{:S(2)}) collective-permute-start(bf16[64,3712]{1,0:T(8,128)(2,1)S(1)} %slice_dynamic-update-slice_fusion.own_ref), channel_id=1, source_target_pairs={{0,4},{4,0},{8,12},{12,8},{1,5},{5,1},{9,13},{13,9},{2,6},{6,2},{1... | collective-permute-start | bytes 1425416 | tf_op jit(solution)/shard_map/ppermute | solution.py:394
  23.4 3.5 %collective-permute-start.6 = (bf16[64,3584]{1,0:T(8,128)(2,1)S(1)}, bf16[64,3584]{1,0:T(8,128)(2,1)S(1)}, u32[]{:S(2)}, u32[]{:S(2)}) collective-permute-start(bf16[64,3584]{1,0:T(8,128)(2,1)S(1)} %pad_maximum_fusion.own_ref), channel_id=1, source_target_pairs={{0,4},{4,0},{8,12},{12,8},{1,5},{5,1},{9,13},{13,9},{2,6},{6,2},{1... | collective-permute-start | bytes 1376264 | tf_op jit(solution)/shard_map/ppermute | solution.py:394
  25.2 4.3 %slice-start.2 = ((s8[7340032]{0:T(1024)(128)(4,1)}), s8[4194304]{0:T(1024)(128)(4,1)S(1)}, s32[]{:S(2)}) async-start(s8[7340032]{0:T(1024)(128)(4,1)} %bitcast.11), calls=%async_computation.2 | async-start | bytes 8388608
  26.9 2.6 %slice-start.3 = ((s8[7340032]{0:T(1024)(128)(4,1)}), s8[3145728]{0:T(1024)(128)(4,1)S(1)}, s32[]{:S(2)}) async-start(s8[7340032]{0:T(1024)(128)(4,1)} %bitcast.11), calls=%async_computation.3 | async-start | bytes 6291456
  29.3 1.9 %collective-permute-start.8 = (bf16[64,3584]{1,0:T(8,128)(2,1)S(1)}, bf16[64,3584]{1,0:T(8,128)(2,1)S(1)}, u32[]{:S(2)}, u32[]{:S(2)}) collective-permute-start(bf16[64,3584]{1,0:T(8,128)(2,1)S(1)} %get-tuple-element.49), channel_id=1, source_target_pairs={{0,4},{4,0},{8,12},{12,8},{1,5},{5,1},{9,13},{13,9},{2,6},{6,2},{1... | collective-permute-start | bytes 1376264 | tf_op jit(solution)/shard_map/ppermute | solution.py:394
  31.2 1.8 %collective-permute-start.12 = (bf16[64,3584]{1,0:T(8,128)(2,1)S(1)}, bf16[64,3584]{1,0:T(8,128)(2,1)S(1)}, u32[]{:S(2)}, u32[]{:S(2)}) collective-permute-start(bf16[64,3584]{1,0:T(8,128)(2,1)S(1)} %get-tuple-element.54), channel_id=1, source_target_pairs={{0,4},{4,0},{8,12},{12,8},{1,5},{5,1},{9,13},{13,9},{2,6},{6,2},{1... | collective-permute-start | bytes 1376264 | tf_op jit(solution)/shard_map/ppermute | solution.py:394
  31.5 7.9 %collective-permute-start.9 = (bf16[32,3584]{1,0:T(8,128)(2,1)S(1)}, bf16[32,3584]{1,0:T(8,128)(2,1)S(1)}, u32[]{:S(2)}, u32[]{:S(2)}) collective-permute-start(bf16[32,3584]{1,0:T(8,128)(2,1)S(1)} %get-tuple-element.55), channel_id=1, source_target_pairs={{0,8},{4,12},{8,0},{12,4},{1,9},{5,13},{9,1},{13,5},{2,10},{6,14},... | collective-permute-start | bytes 688136 | tf_op jit(solution)/shard_map/ppermute | solution.py:394
  33.1 7.7 %collective-permute-start.13 = (bf16[32,3584]{1,0:T(8,128)(2,1)S(1)}, bf16[32,3584]{1,0:T(8,128)(2,1)S(1)}, u32[]{:S(2)}, u32[]{:S(2)}) collective-permute-start(bf16[32,3584]{1,0:T(8,128)(2,1)S(1)} %get-tuple-element.57), channel_id=1, source_target_pairs={{0,1},{1,0},{2,3},{3,2},{4,5},{5,4},{6,7},{7,6},{8,9},{9,8},{10,11... | collective-permute-start | bytes 688136 | tf_op jit(solution)/shard_map/ppermute | solution.py:394
  39.4 4.9 %collective-permute-start.10 = (bf16[16,3584]{1,0:T(8,128)(2,1)S(1)}, bf16[16,3584]{1,0:T(8,128)(2,1)S(1)}, u32[]{:S(2)}, u32[]{:S(2)}) collective-permute-start(bf16[16,3584]{1,0:T(8,128)(2,1)S(1)} %get-tuple-element.59), channel_id=1, source_target_pairs={{0,1},{1,0},{2,3},{3,2},{4,5},{5,4},{6,7},{7,6},{8,9},{9,8},{10,11... | collective-permute-start | bytes 344072 | tf_op jit(solution)/shard_map/ppermute | solution.py:394
  40.9 6.7 %collective-permute-start.14 = (bf16[16,3584]{1,0:T(8,128)(2,1)S(1)}, bf16[16,3584]{1,0:T(8,128)(2,1)S(1)}, u32[]{:S(2)}, u32[]{:S(2)}) collective-permute-start(bf16[16,3584]{1,0:T(8,128)(2,1)S(1)} %get-tuple-element.61), channel_id=1, source_target_pairs={{0,8},{4,12},{8,0},{12,4},{1,9},{5,13},{9,1},{13,5},{2,10},{6,14},... | collective-permute-start | bytes 344072 | tf_op jit(solution)/shard_map/ppermute | solution.py:394
  44.3 5.9 %collective-permute-start.11 = (bf16[8,3584]{1,0:T(8,128)(2,1)S(1)}, bf16[8,3584]{1,0:T(8,128)(2,1)S(1)}, u32[]{:S(2)}, u32[]{:S(2)}) collective-permute-start(bf16[8,3584]{1,0:T(8,128)(2,1)S(1)} %fusion.5), channel_id=1, source_target_pairs={{0,2},{1,3},{2,0},{3,1},{4,6},{5,7},{6,4},{7,5},{8,10},{9,11},{10,... | collective-permute-start | bytes 172040 | tf_op jit(solution)/shard_map/ppermute | solution.py:394
  47.6 5.1 %collective-permute-start.15 = (bf16[8,3584]{1,0:T(8,128)(2,1)S(1)}, bf16[8,3584]{1,0:T(8,128)(2,1)S(1)}, u32[]{:S(2)}, u32[]{:S(2)}) collective-permute-start(bf16[8,3584]{1,0:T(8,128)(2,1)S(1)} %fusion.2), channel_id=1, source_target_pairs={{0,2},{1,3},{2,0},{3,1},{4,6},{5,7},{6,4},{7,5},{8,10},{9,11},{10,... | collective-permute-start | bytes 172040 | tf_op jit(solution)/shard_map/ppermute | solution.py:394
